TPU v7x, 32 devices: a whole 2x2x4 slice. The times are simulated.
32 devices in a mesh: mic: 4 (over y, core), tm: 8 (over z, x).
Axes of the slice: x: 2, y: 2, z: 4, core: 2. Of those that a mesh axis runs over, the one named last changes fastest.
Arguments:
- frames: bfloat16 [8, 1024, 512], P('mic', 'tm'), may hold values from -6 to 6
- cotangent: bfloat16 [8, 1024, 512], P('mic', 'tm'), may hold values from -6 to 6
- kernel: float32 [31, 512], replicated, may hold values from -1 to 1
- w_query: bfloat16 [512, 512], replicated, may hold values from -0.25 to 0.25
- w_key: bfloat16 [512, 512], replicated, may hold values from -0.25 to 0.25
- w_value: bfloat16 [512, 512], replicated, may hold values from -0.25 to 0.25
- w_out: bfloat16 [512, 512], replicated, may hold values from -0.25 to 0.25
Outputs:
- layer_out: bfloat16 [8, 1024, 512], P('mic', 'tm')
- frame_grad: bfloat16 [8, 1024, 512], P('mic', 'tm')
- kernel_grad: float32 [31, 512], replicated
- query_grad: float32 [512, 512], replicated
- key_grad: float32 [512, 512], replicated
- value_grad: float32 [512, 512], replicated
- out_grad: float32 [512, 512], replicated
All inputs are finite; a program needn't handle non-finite values.
Results may differ from a plain program's by a relative error of at most 0.013.
Values may be sent and summed in bfloat16 or wider, within the bound.
No kernel may reach another device: no remote copies, remote signals or barrier semaphores. Data moves between devices by JAX's collectives and lax.ppermute only.
A program may use at most 128 MiB of HBM per device.

v0:
```python
import math

import jax
import jax.numpy as jnp
from jax import lax
from jax.sharding import PartitionSpec as P

HEADS = 8


def extended(array, sides, width):
    for axis, dim in sides:
        size, length = (lax.axis_size(axis), array.shape[dim])
        up = [(i, (i + 1) % size) for i in range(size - 1)]
        down = [(j, i) for i, j in up]
        last = lax.slice_in_dim(array, length - width, length, axis=dim)
        first = lax.slice_in_dim(array, 0, width, axis=dim)
        before = lax.ppermute(last, axis, up)
        after = lax.ppermute(first, axis, down)
        array = jnp.concatenate([before, array, after], axis=dim)
    return array


def depthwise(padded, kernel, length):
    summed = jnp.zeros((padded.shape[0], length, padded.shape[2]), jnp.float32)
    for offset in range(kernel.shape[0]):
        summed = (
            summed + padded[:, offset : offset + length, :].astype(jnp.float32) * kernel[offset]
        )
    return summed


def transposed(padded, kernel, length):
    reach = kernel.shape[0] - 1
    summed = jnp.zeros((padded.shape[0], length, padded.shape[2]), jnp.float32)
    for offset in range(kernel.shape[0]):
        start = reach - offset
        summed = summed + padded[:, start : start + length, :] * kernel[offset]
    return summed


def kernel_terms(padded, gradient, taps):
    length = gradient.shape[1]
    rows_out = []
    for offset in range(taps):
        rows_out.append(
            jnp.sum(
                padded[:, offset : offset + length, :].astype(jnp.float32) * gradient, axis=(0, 1)
            )
        )
    return jnp.stack(rows_out)


def split_heads(rows, head_count):
    first, length, width = rows.shape
    return rows.astype(jnp.float32).reshape(first, length, head_count, width // head_count)


def attend(queries, key_rows, value_rows, head_count):
    first, length, width = queries.shape
    factor = 1.0 / math.sqrt(width // head_count)
    query_heads = split_heads(queries, head_count)
    key_heads = split_heads(key_rows, head_count)
    value_heads = split_heads(value_rows, head_count)
    scores = jnp.einsum("athe,bthe->abth", query_heads, key_heads) * factor
    weights = jnp.exp(scores)
    weights = weights / jnp.sum(weights, axis=1, keepdims=True)
    mixed = jnp.einsum("abth,bthe->athe", weights, value_heads).reshape(first, length, width)
    return (mixed, weights)


def attend_back(queries, key_rows, value_rows, weights, upstream, head_count):
    first, length, width = queries.shape
    others = key_rows.shape[0]
    factor = 1.0 / math.sqrt(width // head_count)
    query_heads = split_heads(queries, head_count)
    key_heads = split_heads(key_rows, head_count)
    value_heads = split_heads(value_rows, head_count)
    up_heads = split_heads(upstream, head_count)
    products = jnp.einsum("athe,bthe->abth", up_heads, value_heads)
    inner = weights * (products - jnp.sum(weights * products, axis=1, keepdims=True)) * factor
    dquery = jnp.einsum("abth,bthe->athe", inner, key_heads).reshape(first, length, width)
    key_terms = jnp.einsum("abth,athe->bthe", inner, query_heads).reshape(others, length, width)
    value_terms = jnp.einsum("abth,athe->bthe", weights, up_heads).reshape(others, length, width)
    return (dquery, key_terms, value_terms)


def project(inputs, matrix):
    width = inputs.shape[-1]
    return jnp.dot(inputs.reshape(-1, width), matrix, preferred_element_type=jnp.float32).reshape(
        inputs.shape[:-1] + (matrix.shape[1],)
    )


def outer(left, right):
    width = left.shape[-1]
    return jnp.dot(
        left.reshape(-1, width).T,
        right.reshape(-1, right.shape[-1]),
        preferred_element_type=jnp.float32,
    )


def shards(frames, cotangent, kernel, w_query, w_key, w_value, w_out):
    reach = kernel.shape[0] // 2
    length = frames.shape[1]
    count = frames.shape[0]
    padded = extended(frames, (("tm", 1),), reach)
    conv = depthwise(padded, kernel, length)
    acted = jax.nn.silu(conv).astype(jnp.bfloat16)
    queries = project(acted, w_query).astype(jnp.bfloat16)
    key_rows = project(acted, w_key).astype(jnp.bfloat16)
    value_rows = project(acted, w_value).astype(jnp.bfloat16)
    key_all, value_all = (
        lax.all_gather(key_rows, "mic", axis=0, tiled=True),
        lax.all_gather(value_rows, "mic", axis=0, tiled=True),
    )
    mixed, weights = attend(queries, key_all, value_all, HEADS)
    mixed = mixed.astype(jnp.bfloat16)
    upstream = project(cotangent, w_out.T).astype(jnp.bfloat16)
    dquery, key_terms, value_terms = attend_back(
        queries, key_all, value_all, weights, upstream, HEADS
    )
    key_sum, value_sum = (
        lax.psum_scatter(key_terms, "mic", scatter_dimension=0, tiled=True),
        lax.psum_scatter(value_terms, "mic", scatter_dimension=0, tiled=True),
    )
    layer_out = (frames.astype(jnp.float32) + project(mixed, w_out)).astype(jnp.bfloat16)
    out_term = outer(mixed, cotangent)
    dquery = dquery.astype(jnp.bfloat16)
    dkey = key_sum.astype(jnp.bfloat16)
    dvalue = value_sum.astype(jnp.bfloat16)
    query_term = outer(acted, dquery)
    key_term = outer(acted, dkey)
    value_term = outer(acted, dvalue)
    dacted = project(dquery, w_query.T) + project(dkey, w_key.T) + project(dvalue, w_value.T)
    sig = jax.nn.sigmoid(conv)
    dconv = dacted * sig * (1.0 + conv * (1.0 - sig))
    grad_pad = extended(dconv.astype(jnp.bfloat16), (("tm", 1),), reach).astype(dconv.dtype)
    frame_grad = (cotangent.astype(jnp.float32) + transposed(grad_pad, kernel, length)).astype(
        jnp.bfloat16
    )
    tap_term = kernel_terms(padded, dconv, kernel.shape[0])
    norm_factor = 1.0 / math.sqrt(lax.axis_size("mic") * count * lax.axis_size("tm") * length)
    summed = lax.psum((tap_term, query_term, key_term, value_term, out_term), ("mic", "tm"))
    kernel_grad = summed[0] * norm_factor
    query_grad = summed[1] * norm_factor
    key_grad = summed[2] * norm_factor
    value_grad = summed[3] * norm_factor
    out_grad = summed[4] * norm_factor
    return (layer_out, frame_grad, kernel_grad, query_grad, key_grad, value_grad, out_grad)


def solution(mesh):
    in_specs = (P("mic", "tm", None), P("mic", "tm", None), P(), P(), P(), P(), P())
    out_specs = (P("mic", "tm", None), P("mic", "tm", None), P(), P(), P(), P(), P())
    return jax.shard_map(shards, mesh=mesh, in_specs=in_specs, out_specs=out_specs, check_vma=False)
```

profile of v0, /device:TPU:0, one launch (start us, length us, event | category | flops | bytes accessed | tf_op | source)
XLA Modules:
  0.0 314.8 jit_solution(14763579049120905425)
XLA Ops:
  7.2 0.8 fusion.131
  8.1 1.3 collective-permute-start.1
  9.4 5.5 %collective-permute-start = (bf16[2,15,512]{2,1,0:T(8,128)(2,1)S(1)}, bf16[2,15,512]{2,1,0:T(8,128)(2,1)S(1)}, u32[]{:S(2)}, u32[]{:S(2)}) collective-permute-start(bf16[2,15,512]{2,1,0:T(8,128)(2,1)S(1)} %get-tuple-element.47), channel_id=1, source_target_pairs={{0,1},{1,2},{2,3},{3,4},{4,5},{5,6},{6,7},{8,9},{9,10},{10,11},{11... | collective-permute-start | bytes 92168 | tf_op jit(solution)/shard_map/ppermute | solution.py:18
  14.9 1.0 fusion.133
  15.9 1.2 fusion.132
  17.1 1.0 constant_dynamic-update-slice_fusion.1
  18.3 6.6 %multiply_convert_fusion = (bf16[2,128,512]{2,1,0:T(8,128)(2,1)S(1)}, f32[2,128,512]{2,1,0:T(8,128)}) fusion(f32[512]{0:T(512)S(1)} %bitcast.166, bf16[2,143,512]{2,1,0:T(8,128)(2,1)S(1)} %constant_dynamic-update-slice_fusion, f32[512]{0:T(512)S(1)} %bitcast.168, f32[512]{0:T(512)S(1)} %bitcast.172, f32[512]{0:T(512)S(1)} %bitcast.174, ...), kind=kLoop, calls=%fused_computation.241 | loop fusion | flops 18612224 | bytes 5074944 | tf_op jit(solution)/shard_map/convert_element_type | solution.py:110
  24.9 1.0 convolution_convert_fusion.5
  26.0 1.0 convolution_convert_fusion.4
  27.8 1.1 copy.62
  29.3 1.1 copy.56
  30.4 14.0 %all-gather.3.cloned.1.call-done = bf16[8,128,512]{2,1,0:T(8,128)(2,1)} async-done(((bf16[2,128,512]{2,1,0:T(8,128)(2,1)}), bf16[8,128,512]{2,1,0:T(8,128)(2,1)}) %all-gather.3.cloned.1.call-update) | async-done | bytes 1048592 | tf_op jit(solution)/shard_map/all_gather | solution.py:116
  44.5 1.6 copy.52
  46.1 3.8 %copy.57 = bf16[8,128,8,64]{3,0,2,1:T(8,128)(2,1)} copy(bf16[8,128,8,64]{1,3,2,0:T(8,128)(2,1)S(1)} %bitcast.138) | data formatting | bytes 2097152 | tf_op jit(solution)/shard_map/reshape | solution.py:56
  49.9 13.5 %all-gather.5.cloned.1.call-done = bf16[8,128,512]{2,1,0:T(8,128)(2,1)} async-done(((bf16[2,128,512]{2,1,0:T(8,128)(2,1)}), bf16[8,128,512]{2,1,0:T(8,128)(2,1)}) %all-gather.5.cloned.1.call-update) | async-done | bytes 1048592 | tf_op jit(solution)/shard_map/all_gather | solution.py:115
  63.4 1.6 copy.53
  65.0 3.7 %copy.55 = bf16[8,128,8,64]{3,0,2,1:T(8,128)(2,1)} copy(bf16[8,128,8,64]{1,3,2,0:T(8,128)(2,1)S(1)} %bitcast.139) | data formatting | bytes 2097152 | tf_op jit(solution)/shard_map/reshape | solution.py:56
  68.7 4.0 %convolution_bitcast_fusion.6 = f32[2,8,128,8]{1,0,3,2:T(2,128)} fusion(bf16[8,128,8,64]{3,0,2,1:T(8,128)(2,1)} %copy.57, bf16[2,128,8,64]{3,0,2,1:T(2,128)(2,1)} %copy.62), kind=kOutput, calls=%fused_computation.20 | convolution fusion | flops 2097152 | bytes 1376256 | tf_op jit(solution)/shard_map/athe,bthe->abth/dot_general | solution.py:80
  72.8 5.1 %multiply_reduce_fusion = (f32[2,128,8]{0,2,1:T(8,128)}, f32[2,8,128,8]{1,0,3,2:T(2,128)}) fusion(f32[2,8,128,8]{1,0,3,2:T(2,128)} %convolution_bitcast_fusion.6, bf16[8,128,8,64]{3,0,2,1:T(8,128)(2,1)S(1)} %copy-done.4, bf16[2,128,8,64]{3,0,2,1:T(2,128)(2,1)} %copy.56), kind=kOutput, calls=%fused_computation.39 | convolution fusion | flops 2162695 | bytes 1449984 | tf_op jit(solution)/shard_map/div | solution.py:67
  77.8 5.7 %convolution_bitcast_fusion.1 = f32[8,128,8,64]{3,0,2,1:T(8,128)} fusion(bf16[2,128,8,64]{3,0,2,1:T(2,128)(2,1)} %copy.56, f32[2,8,128,8]{1,0,3,2:T(2,128)} %get-tuple-element.81, f32[2,8,128,8]{1,0,3,2:T(2,128)} %convolution_bitcast_fusion.6, f32[2,128,8]{0,2,1:T(8,128)} %get-tuple-element.80), kind=kOutput, calls=%fused_computation.1 | convolution fusion | flops 2146304 | bytes 2498560 | tf_op jit(solution)/shard_map/abth,athe->bthe/dot_general | solution.py:83
  83.5 4.8 %copy.67 = f32[8,128,8,64]{1,3,2,0:T(8,128)} copy(f32[8,128,8,64]{3,0,2,1:T(8,128)} %convolution_bitcast_fusion.1) | data formatting | bytes 4194304 | tf_op jit(solution)/shard_map/abth,athe->bthe/transpose | solution.py:83
  88.5 0.7 copy-done.12
  89.6 2.9 convolution_bitcast_fusion
  92.6 5.1 %copy.70 = f32[8,128,8,64]{1,3,2,0:T(8,128)} copy(f32[8,128,8,64]{3,0,2,1:T(8,128)} %convolution_bitcast_fusion) | data formatting | bytes 4194304 | tf_op jit(solution)/shard_map/abth,athe->bthe/transpose | solution.py:84
  97.7 1.6 copy-done.3
  99.3 3.2 %fusion.2 = bf16[2,128,8,64]{3,0,2,1:T(2,128)(2,1)} fusion(bf16[8,128,8,64]{3,0,2,1:T(8,128)(2,1)S(1)} %copy-done.3, f32[2,8,128,8]{1,0,3,2:T(2,128)} %get-tuple-element.81), kind=kOutput, calls=%fused_computation.26 | convolution fusion | flops 2097152 | bytes 1376256 | tf_op jit(solution)/shard_map/abth,bthe->athe/dot_general | solution.py:68
  102.5 1.3 copy.58
  103.8 4.2 %fusion.3 = bf16[2,128,8,64]{3,0,2,1:T(2,128)(2,1)S(1)} fusion(bf16[8,128,8,64]{3,0,2,1:T(8,128)(2,1)} %copy.55, f32[2,8,128,8]{1,0,3,2:T(2,128)} %get-tuple-element.81, f32[2,8,128,8]{1,0,3,2:T(2,128)} %convolution_bitcast_fusion.6, f32[2,128,8]{0,2,1:T(8,128)} %get-tuple-element.80), kind=kOutput, calls=%fused_computation.27 | convolution fusion | flops 2277376 | bytes 1449984 | tf_op jit(solution)/shard_map/abth,bthe->athe/dot_general | solution.py:82
  108.6 1.3 convolution_bitcast_fusion.5
  109.9 1.3 convolution_bitcast_fusion.2
  111.2 1.0 fusion.6
  112.6 7.3 %reduce-scatter.3.cloned.1.call-done = f32[2,128,512]{1,2,0:T(8,128)} async-done(((f32[8,128,512]{1,2,0:T(8,128)}), f32[2,128,512]{1,2,0:T(8,128)}) %reduce-scatter.3.cloned.1.call-update) | async-done | bytes 524304 | tf_op jit(solution)/shard_map/reduce_scatter | solution.py:125
  119.9 2.4 convolution_bitcast_fusion.4
  122.2 31.6 %reduce-scatter.5.cloned.1.call-done = f32[2,128,512]{1,2,0:T(8,128)} async-done(((f32[8,128,512]{1,2,0:T(8,128)}), f32[2,128,512]{1,2,0:T(8,128)}) %reduce-scatter.5.cloned.1.call-update) | async-done | bytes 524304 | tf_op jit(solution)/shard_map/reduce_scatter | solution.py:126
  153.8 2.4 convolution_bitcast_fusion.3
  156.2 1.0 copy-done.9
  157.8 0.7 copy-done.16
  158.6 1.6 fusion.66
  160.3 1.3 collective-permute-start.3
  161.6 4.5 %collective-permute-start.2 = (bf16[2,15,512]{2,1,0:T(8,128)(2,1)S(1)}, bf16[2,15,512]{2,1,0:T(8,128)(2,1)S(1)}, u32[]{:S(2)}, u32[]{:S(2)}) collective-permute-start(bf16[2,15,512]{2,1,0:T(8,128)(2,1)S(1)} %get-tuple-element.45), channel_id=1, source_target_pairs={{0,1},{1,2},{2,3},{3,4},{4,5},{5,6},{6,7},{8,9},{9,10},{10,11},{11... | collective-permute-start | bytes 92168 | tf_op jit(solution)/shard_map/ppermute | solution.py:18
  166.2 0.5 fusion.37
  166.7 0.6 fusion.46
  167.5 41.1 %psum.35 = f32[31,512]{1,0:T(8,128)S(1)} all-reduce(f32[31,512]{1,0:T(8,128)S(1)} %stack.127), channel_id=1, replica_groups=mesh['mic'=4,'tm'=8] {'mic','tm'}, use_global_device_ids=true, to_apply=%region_35.36 | all-reduce | flops 15872 | bytes 126976 | tf_op jit(solution)/shard_map/psum | solution.py:145
  208.7 0.6 broadcast_multiply_fusion.4
  209.5 2.8 fusion.70
  212.3 91.2 %all-reduce.3.cloned.1.call-done = (f32[512,512]{1,0:T(8,128)}, f32[512,512]{1,0:T(8,128)}, f32[512,512]{1,0:T(8,128)}, f32[512,512]{1,0:T(8,128)}) async-done(((f32[512,512]{1,0:T(8,128)}, f32[512,512]{1,0:T(8,128)}, f32[512,512]{1,0:T(8,128)}, f32[512,512]{1,0:T(8,128)}), (f32[512,512]{1,0:T(8,128)}, f32[512,512]{1,0:T(8,128)}, f32[512,512]{1,0:T(8,128)}, ...) | async-done | bytes 4194320 | tf_op jit(solution)/shard_map/psum | solution.py:145
  303.4 3.2 %broadcast_multiply_fusion.2 = (f32[512,512]{1,0:T(8,128)}, f32[512,512]{1,0:T(8,128)}) fusion(f32[512,512]{1,0:T(8,128)} %get-tuple-element.39, f32[512,512]{1,0:T(8,128)} %get-tuple-element.38), kind=kLoop, calls=%fused_computation.237 | loop fusion | flops 524288 | bytes 4194304 | tf_op jit(solution)/shard_map/mul | solution.py:148
  306.7 1.6 broadcast_multiply_fusion
  (101 shorter events, 3.9 us)
Async XLA Ops:
  7.2 17.7 %copy-start = (bf16[512,512]{1,0:T(8,128)(2,1)S(1)}, bf16[512,512]{1,0:T(8,128)(2,1)}, u32[]{:S(2)}) copy-start(bf16[512,512]{1,0:T(8,128)(2,1)} %param.12) | copy-start | bytes 1572868
  7.2 37.3 %all-gather.3.cloned.1.call-start = ((), (), s32[]{:S(2)}) async-start(), calls=%async_computation.2 | async-start | bytes 1310720 | tf_op jit(solution)/shard_map/all_gather | solution.py:116
  8.1 10.0 %collective-permute-start.1 = (bf16[2,15,512]{2,1,0:T(8,128)(2,1)S(1)}, bf16[2,15,512]{2,1,0:T(8,128)(2,1)S(1)}, u32[]{:S(2)}, u32[]{:S(2)}) collective-permute-start(bf16[2,15,512]{2,1,0:T(8,128)(2,1)S(1)} %get-tuple-element.48), channel_id=1, source_target_pairs={{1,0},{2,1},{3,2},{4,3},{5,4},{6,5},{7,6},{9,8},{10,9},{11,10},{12... | collective-permute-start | bytes 92168 | tf_op jit(solution)/shard_map/ppermute | solution.py:19
  9.4 8.8 %collective-permute-start = (bf16[2,15,512]{2,1,0:T(8,128)(2,1)S(1)}, bf16[2,15,512]{2,1,0:T(8,128)(2,1)S(1)}, u32[]{:S(2)}, u32[]{:S(2)}) collective-permute-start(bf16[2,15,512]{2,1,0:T(8,128)(2,1)S(1)} %get-tuple-element.47), channel_id=1, source_target_pairs={{0,1},{1,2},{2,3},{3,4},{4,5},{5,6},{6,7},{8,9},{9,10},{10,11},{11... | collective-permute-start | bytes 92168 | tf_op jit(solution)/shard_map/ppermute | solution.py:18
  17.0 1.1 copy-start.18
  17.0 1.1 copy-start.20
  17.0 1.1 copy-start.22
  17.1 1.1 copy-start.24
  17.1 1.1 copy-start.26
  17.1 1.1 copy-start.28
  17.1 1.1 copy-start.30
  17.1 1.1 copy-start.32
  17.1 1.1 copy-start.34
  17.1 1.1 copy-start.36
  17.1 1.1 copy-start.38
  18.3 7.7 %copy-start.10 = (bf16[512,512]{1,0:T(8,128)(2,1)S(1)}, bf16[512,512]{1,0:T(8,128)(2,1)}, u32[]{:S(2)}) copy-start(bf16[512,512]{1,0:T(8,128)(2,1)} %param.11) | copy-start | bytes 1572868
  24.8 2.4 copy-start.2
  24.8 2.4 copy-start.5
  25.9 3.0 copy-start.7
  25.9 37.5 %all-gather.5.cloned.1.call-start = ((), (), s32[]{:S(2)}) async-start(), calls=%async_computation.3 | async-start | bytes 1310720 | tf_op jit(solution)/shard_map/all_gather | solution.py:115
  27.0 92.9 %reduce-scatter.3.cloned.1.call-start = ((), (), s32[]{:S(2)}) async-start(), calls=%async_computation.4 | async-start | bytes 2621440 | tf_op jit(solution)/shard_map/reduce_scatter | solution.py:125
  68.7 4.0 %copy-start.4 = (bf16[8,128,8,64]{3,0,2,1:T(8,128)(2,1)S(1)}, bf16[8,128,8,64]{3,0,2,1:T(8,128)(2,1)}, u32[]{:S(2)}) copy-start(bf16[8,128,8,64]{3,0,2,1:T(8,128)(2,1)} %copy.55) | copy-start | bytes 3145732
  88.2 1.0 copy-start.12
  88.3 1.4 copy-start.15
  88.3 65.6 %reduce-scatter.5.cloned.1.call-start = ((), (), s32[]{:S(2)}) async-start(), calls=%async_computation.5 | async-start | bytes 2621440 | tf_op jit(solution)/shard_map/reduce_scatter | solution.py:126
  97.6 1.6 copy-start.3
  97.7 205.8 %all-reduce.3.cloned.1.call-start = ((), (), s32[]{:S(2)}) async-start(), calls=%async_computation.6 | async-start | bytes 8388608 | tf_op jit(solution)/shard_map/psum | solution.py:145
  108.0 3.1 copy-start.1
  108.1 3.1 copy-start.6
  108.5 3.6 %copy-start.8 = (bf16[512,512]{1,0:T(8,128)(2,1)S(1)}, bf16[512,512]{1,0:T(8,128)(2,1)}, u32[]{:S(2)}) copy-start(bf16[512,512]{1,0:T(8,128)(2,1)} %param.10) | copy-start | bytes 1572868
  156.2 1.0 copy-start.9
  156.2 1.2 copy-start.11
  157.4 1.2 copy-start.17
  160.2 49.2 %copy-start.19 = (f32[1,512]{1,0:T(1,128)S(1)}, f32[1,512]{1,0:T(1,128)}, u32[]{:S(2)}) copy-start(f32[1,512]{1,0:T(1,128)} %copy-done.18) | copy-start | bytes 6148
  160.2 49.2 %copy-start.21 = (f32[1,512]{1,0:T(1,128)S(1)}, f32[1,512]{1,0:T(1,128)}, u32[]{:S(2)}) copy-start(f32[1,512]{1,0:T(1,128)} %copy-done.20) | copy-start | bytes 6148
  160.2 49.2 %copy-start.23 = (f32[1,512]{1,0:T(1,128)S(1)}, f32[1,512]{1,0:T(1,128)}, u32[]{:S(2)}) copy-start(f32[1,512]{1,0:T(1,128)} %copy-done.22) | copy-start | bytes 6148
  160.2 49.2 %copy-start.25 = (f32[1,512]{1,0:T(1,128)S(1)}, f32[1,512]{1,0:T(1,128)}, u32[]{:S(2)}) copy-start(f32[1,512]{1,0:T(1,128)} %copy-done.24) | copy-start | bytes 6148
  160.2 49.2 %copy-start.27 = (f32[1,512]{1,0:T(1,128)S(1)}, f32[1,512]{1,0:T(1,128)}, u32[]{:S(2)}) copy-start(f32[1,512]{1,0:T(1,128)} %copy-done.26) | copy-start | bytes 6148
  160.3 49.2 %copy-start.29 = (f32[1,512]{1,0:T(1,128)S(1)}, f32[1,512]{1,0:T(1,128)}, u32[]{:S(2)}) copy-start(f32[1,512]{1,0:T(1,128)} %copy-done.28) | copy-start | bytes 6148
  160.3 49.2 %copy-start.31 = (f32[1,512]{1,0:T(1,128)S(1)}, f32[1,512]{1,0:T(1,128)}, u32[]{:S(2)}) copy-start(f32[1,512]{1,0:T(1,128)} %copy-done.30) | copy-start | bytes 6148
  160.3 49.2 %copy-start.33 = (f32[1,512]{1,0:T(1,128)S(1)}, f32[1,512]{1,0:T(1,128)}, u32[]{:S(2)}) copy-start(f32[1,512]{1,0:T(1,128)} %copy-done.32) | copy-start | bytes 6148
  160.3 49.2 %copy-start.35 = (f32[1,512]{1,0:T(1,128)S(1)}, f32[1,512]{1,0:T(1,128)}, u32[]{:S(2)}) copy-start(f32[1,512]{1,0:T(1,128)} %copy-done.34) | copy-start | bytes 6148
  160.3 49.2 %copy-start.37 = (f32[1,512]{1,0:T(1,128)S(1)}, f32[1,512]{1,0:T(1,128)}, u32[]{:S(2)}) copy-start(f32[1,512]{1,0:T(1,128)} %copy-done.36) | copy-start | bytes 6148
  160.3 49.2 %copy-start.39 = (f32[1,512]{1,0:T(1,128)S(1)}, f32[1,512]{1,0:T(1,128)}, u32[]{:S(2)}) copy-start(f32[1,512]{1,0:T(1,128)} %copy-done.38) | copy-start | bytes 6148
  160.3 49.0 %collective-permute-start.3 = (bf16[2,15,512]{2,1,0:T(8,128)(2,1)S(1)}, bf16[2,15,512]{2,1,0:T(8,128)(2,1)S(1)}, u32[]{:S(2)}, u32[]{:S(2)}) collective-permute-start(bf16[2,15,512]{2,1,0:T(8,128)(2,1)S(1)} %get-tuple-element.46), channel_id=1, source_target_pairs={{1,0},{2,1},{3,2},{4,3},{5,4},{6,5},{7,6},{9,8},{10,9},{11,10},{12... | collective-permute-start | bytes 92168 | tf_op jit(solution)/shard_map/ppermute | solution.py:19
  161.6 47.7 %collective-permute-start.2 = (bf16[2,15,512]{2,1,0:T(8,128)(2,1)S(1)}, bf16[2,15,512]{2,1,0:T(8,128)(2,1)S(1)}, u32[]{:S(2)}, u32[]{:S(2)}) collective-permute-start(bf16[2,15,512]{2,1,0:T(8,128)(2,1)S(1)} %get-tuple-element.45), channel_id=1, source_target_pairs={{0,1},{1,2},{2,3},{3,4},{4,5},{5,6},{6,7},{8,9},{9,10},{10,11},{11... | collective-permute-start | bytes 92168 | tf_op jit(solution)/shard_map/ppermute | solution.py:18
  303.4 3.3 %copy-start.13 = (f32[512,512]{1,0:T(8,128)S(1)}, f32[512,512]{1,0:T(8,128)}, u32[]{:S(2)}) copy-start(f32[512,512]{1,0:T(8,128)} %get-tuple-element.40) | copy-start | bytes 3145732
  303.4 3.3 %copy-start.14 = (f32[512,512]{1,0:T(8,128)S(1)}, f32[512,512]{1,0:T(8,128)}, u32[]{:S(2)}) copy-start(f32[512,512]{1,0:T(8,128)} %get-tuple-element.41) | copy-start | bytes 3145732
  (1 other events, 1.0 us)
Sparse Core Ops, SparseCore 0:
  26.0 18.3 all-gather.2
  46.6 16.7 all-gather.4
  88.4 31.4 reduce-scatter.2
  122.4 31.3 reduce-scatter.4
  160.1 143.2 all-reduce.2
where the time goes:
time: 316 us; the launch traced here: 315 us
  waiting for transfers between devices  158 us (50%)
  blocking collectives  41.1 us (13%)
  matrix products  38.4 us (12%)
  local copies, waits for them, and re-layouts  33.9 us (11%)
  other arithmetic  16.1 us (5%)
  between operations  14.4 us (5%)
  starting transfers between devices  13.2 us (4%)
    psum x1, waiting for transfers between devices, shards(): lax.psum((tap_term, query_term, key_term, value_term, out_term), ('mic',...  91.2 us
    psum x1, blocking collectives, shards(): lax.psum((tap_term, query_term, key_term, value_term, out_term), ('mic',...  41.1 us
    reduce_scatter x1, waiting for transfers between devices, shards(): lax.psum_scatter(value_terms, 'mic', scatter_dimension=0, tiled=True)  31.6 us
    all_gather x1, waiting for transfers between devices, shards(): lax.all_gather(value_rows, 'mic', axis=0, tiled=True)  14 us
    all_gather x1, waiting for transfers between devices, shards(): lax.all_gather(key_rows, 'mic', axis=0, tiled=True)  13.5 us
    ppermute x2, starting transfers between devices, extended(): before = lax.ppermute(last, axis, up)  10 us
    reshape x4, local copies, waits for them, and re-layouts, split_heads(): rows.astype(jnp.float32)  9.76 us
    dot_general x4, matrix products, outer(): jnp.dot(left.reshape(-1, width).T, right.reshape(-1, right.shape[-1]), pr...  7.31 us
  transfers between devices with their start and end apart: 9, of which 5 were waited for; matrix products, arithmetic and copies ran while one was open for 14% of the time, Pallas kernels for 0%

commit v1 on v0

v1 whole, which is shorter than its diff:
```python
import functools
import math

import jax
import jax.numpy as jnp
from jax import lax
from jax.experimental import pallas as pl
from jax.experimental.pallas import tpu as pltpu
from jax.sharding import PartitionSpec as P

HEADS = 8
LANES = 128
HALO = 16
NT = (((1,), (1,)), ((), ()))
TN = (((0,), (0,)), ((), ()))
BF = jnp.bfloat16
F32 = jnp.float32
VMEM_LIMIT = 56 * 1024 * 1024


def mm(left, right, dims=(((1,), (0,)), ((), ()))):
    return lax.dot_general(left, right, dims, preferred_element_type=F32)


def rolled(x, shift):
    return x if shift == 0 else pltpu.roll(x, x.shape[0] - shift, axis=0)


def window(x, taps, rows):
    acc = None
    for r in range(8):
        xr = rolled(x, r)
        for k in range(4):
            o = 8 * k + r
            if o == 0:
                continue
            term = xr[8 * k : 8 * k + rows] * taps(o)
            acc = term if acc is None else acc + term
    return acc


def main_kernel(
    plan, got, before, after, kern, wq, wk, wv, wo, back, packed,
    conv_s, act_s, cot_s, q_s, k_s, v_s, u_s, mix_s, dq_s, dk_s, dv_s, dconv_s, tap_s,
):
    groups, count, sub, width, chunks, factor = plan
    mics = groups * count
    cuts = sub // HALO
    block = mics * HALO
    cols = width // LANES

    def frames_window(a, m, lanes):
        return jnp.concatenate(
            [before[a, m, :, lanes], got[a, 0, m, :, lanes], after[a, m, :, lanes]], axis=0
        ).astype(F32)

    def conv_step(n, _):
        a, m = n // count, n % count
        for lc in range(cols):
            lanes = slice(lc * LANES, (lc + 1) * LANES)
            conv = window(
                frames_window(a, m, lanes), lambda o: kern[o - 1 : o, lanes], sub
            )
            acted = (conv * jax.nn.sigmoid(conv)).astype(BF)
            for c in range(cuts):
                at = pl.multiple_of(c * block + n * HALO, HALO)
                conv_s[pl.ds(at, HALO), lanes] = conv[c * HALO : (c + 1) * HALO]
                act_s[pl.ds(at, HALO), lanes] = acted[c * HALO : (c + 1) * HALO]
        for c in range(cuts):
            at = pl.multiple_of(c * block + n * HALO, HALO)
            cot_s[pl.ds(at, HALO), :] = got[a, 1, m, c * HALO : (c + 1) * HALO, :]
        return 0

    lax.fori_loop(0, mics, conv_step, 0)
    acted = act_s[...]
    cot = cot_s[...]
    q_s[...] = mm(acted, wq[...]).astype(BF)
    k_s[...] = mm(acted, wk[...]).astype(BF)
    v_s[...] = mm(acted, wv[...]).astype(BF)
    u_s[...] = mm(cot, wo[...], NT).astype(BF)

    depth = width // HEADS
    per = LANES // depth
    lane = lax.broadcasted_iota(jnp.int32, (block, LANES), 1)
    row_i = lax.broadcasted_iota(jnp.int32, (block, per * block), 0)
    col_i = lax.broadcasted_iota(jnp.int32, (block, per * block), 1)
    same = (row_i % HALO) == (col_i % HALO)

    def by_head(x):
        return jnp.concatenate(
            [jnp.where(lane // depth == h, x, jnp.zeros_like(x)) for h in range(per)], axis=0
        )

    def sums(x):
        return [
            jnp.sum(x[:, h * block : (h + 1) * block], axis=1, keepdims=True) for h in range(per)
        ]

    def each(x, values, op):
        return jnp.concatenate(
            [op(x[:, h * block : (h + 1) * block], values[h]) for h in range(per)], axis=1
        )

    def pick(x):
        out = x[:block]
        for h in range(1, per):
            out = jnp.where(lane // depth == h, x[h * block : (h + 1) * block], out)
        return out

    for c in range(cuts):
        rows = slice(c * block, (c + 1) * block)
        for p in range(cols):
            lanes = slice(p * LANES, (p + 1) * LANES)
            q, u = q_s[rows, lanes], u_s[rows, lanes]
            kc, vc = by_head(k_s[rows, lanes]), by_head(v_s[rows, lanes])
            e = jnp.where(same, jnp.exp(mm(q, kc, NT) * factor), 0.0)
            w = each(e, sums(e), lambda x, s: x / s)
            up = mm(u, vc, NT)
            wup = w * up
            inner = each(up, sums(wup), lambda x, s: x - s) * w * factor
            wb, ib = w.astype(BF), inner.astype(BF)
            mix_s[rows, lanes] = mm(wb, vc).astype(BF)
            dq_s[rows, lanes] = mm(ib, kc).astype(BF)
            dk_s[rows, lanes] = pick(mm(ib, q, TN)).astype(BF)
            dv_s[rows, lanes] = pick(mm(wb, u, TN)).astype(BF)

    dacted = mm(dq_s[...], wq[...], NT) + mm(dk_s[...], wk[...], NT) + mm(dv_s[...], wv[...], NT)
    conv = conv_s[...]
    sig = jax.nn.sigmoid(conv)
    dconv_s[...] = dacted * sig * (1.0 + conv * (1.0 - sig))
    proj = mm(mix_s[...], wo[...])
    for n in range(mics):
        a, m = n // count, n % count
        for c in range(cuts):
            at = c * block + n * HALO
            part = slice(c * HALO, (c + 1) * HALO)
            back[a, 0, m, part, :] = (
                got[a, 0, m, part, :].astype(F32) + proj[at : at + HALO]
            ).astype(BF)
            back[a, 1, m, part, :] = dconv_s[at : at + HALO, :].astype(BF)

    per_chunk = 4 * cols * width // chunks
    act_t = acted.T
    mix_t = mix_s[...].T
    for i, (left, right) in enumerate(
        ((act_t, dq_s), (act_t, dk_s), (act_t, dv_s), (mix_t, cot_s))
    ):
        grad = mm(left, right[...]).astype(BF)
        for cb in range(cols):
            for at in range(0, width, per_chunk):
                g = ((i * cols + cb) * width + at) // per_chunk
                packed[g, 0:per_chunk, :] = grad[at : at + per_chunk, cb * LANES : (cb + 1) * LANES]

    for lc in range(cols):
        lanes = slice(lc * LANES, (lc + 1) * LANES)

        def tap_step(n, accs):
            a, m = n // count, n % count
            x = frames_window(a, m, lanes)
            d = jnp.concatenate(
                [
                    dconv_s[pl.ds(pl.multiple_of(c * block + n * HALO, HALO), HALO), lanes]
                    for c in range(cuts)
                ],
                axis=0,
            )
            out = list(accs)
            for r in range(8):
                xr = rolled(x, r)
                for k in range(4):
                    o = 8 * k + r
                    if o == 0:
                        continue
                    prod = xr[8 * k : 8 * k + sub] * d
                    out[o - 1] = out[o - 1] + jnp.sum(prod.reshape(sub // 8, 8, LANES), axis=0)
            return tuple(out)

        accs = lax.fori_loop(0, mics, tap_step, tuple(jnp.zeros((8, LANES), F32) for _ in range(31)))
        tap_s[lc * 32 : lc * 32 + 32, :] = jnp.concatenate(
            [jnp.sum(x, axis=0, keepdims=True) for x in accs] + [jnp.zeros((1, LANES), F32)], axis=0
        )

    tap_rows = max(1, cols * 32 // chunks)
    for g in range(chunks):
        tail = jnp.zeros((HALO, LANES), F32)
        if g * tap_rows < cols * 32:
            tail = jnp.concatenate(
                [tap_s[g * tap_rows : (g + 1) * tap_rows, :], tail[tap_rows:]], axis=0
            )
        packed[g, per_chunk : per_chunk + HALO, :] = tail.astype(BF)


def final_kernel(plan, got, taps, *outs):
    chunks, width, norm, order = plan
    cols = width // LANES
    per_chunk = 4 * cols * width // chunks
    tap_rows = max(1, cols * 32 // chunks)
    for f in range(chunks):
        g = order[f]
        flat = g * per_chunk
        i, cb, at = flat // (cols * width), (flat // width) % cols, flat % width
        outs[i][at : at + per_chunk, cb * LANES : (cb + 1) * LANES] = (
            got[f, 0:per_chunk, :].astype(F32) * norm
        )
        row = g * tap_rows
        if row < cols * 32:
            lc, j = row // 32, row % 32
            kept = min(tap_rows, 31 - j)
            if kept > 0:
                tail = got[f, per_chunk : per_chunk + HALO, :].astype(F32) * norm
                taps[j : j + kept, lc * LANES : (lc + 1) * LANES] = tail[0:kept]


def frame_kernel(plan, got, before, after, cot, kern, layer_out, frame_grad):
    groups, count, sub, width = plan
    cols = width // LANES

    def edge(a, m, lanes):
        first = before[m, :, lanes] if a == 0 else got[a - 1, 1, m, sub - HALO :, lanes]
        last = after[m, :, lanes] if a == groups - 1 else got[a + 1, 1, m, :HALO, lanes]
        return jnp.concatenate([first, got[a, 1, m, :, lanes], last], axis=0).astype(F32)

    def step(m, _):
        for a in range(groups):
            part = slice(a * sub, (a + 1) * sub)
            layer_out[m, part, :] = got[a, 0, m, :, :]
            for lc in range(cols):
                lanes = slice(lc * LANES, (lc + 1) * LANES)
                total = window(edge(a, m, lanes), lambda o: kern[31 - o : 32 - o, lanes], sub)
                frame_grad[m, part, lanes] = (cot[m, part, lanes].astype(F32) + total).astype(BF)
        return 0

    lax.fori_loop(0, count, step, 0)


def call(body, outs, scratch, *args):
    return pl.pallas_call(
        body,
        out_shape=outs,
        in_specs=[pl.BlockSpec(memory_space=pltpu.VMEM)] * len(args),
        out_specs=jax.tree.map(lambda _: pl.BlockSpec(memory_space=pltpu.VMEM), outs),
        scratch_shapes=scratch,
        compiler_params=pltpu.CompilerParams(vmem_limit_bytes=VMEM_LIMIT),
    )(*args)


def neighbours(groups, blocks):
    def flat(s):
        return (s % groups) * blocks + s // groups

    return [(flat(s), flat(s + 1)) for s in range(groups * blocks - 1)]


def summed_over(x, groups, size):
    got = lax.all_to_all(
        x.reshape(size, x.shape[0] // size, *x.shape[1:]),
        ("mic", "tm"), 0, 0, tiled=True, axis_index_groups=groups,
    )
    return jnp.sum(got.astype(F32), axis=0).astype(BF)


def shards(frames, cotangent, kernel, w_query, w_key, w_value, w_out):
    groups, blocks = lax.axis_size("mic"), lax.axis_size("tm")
    count, length, width = frames.shape
    sub = length // groups
    chunks = groups * blocks
    rows = groups * count * sub
    shape = jax.ShapeDtypeStruct

    send = jnp.stack([frames, cotangent]).reshape(2, count, groups, sub, width)
    got = lax.all_to_all(send.transpose(2, 0, 1, 3, 4), "mic", 0, 0, tiled=True)
    up = neighbours(groups, blocks)
    down = [(j, i) for i, j in up]
    before = lax.ppermute(got[:, 0, :, sub - HALO :, :], ("mic", "tm"), up)
    after = lax.ppermute(got[:, 0, :, :HALO, :], ("mic", "tm"), down)

    factor = 1.0 / math.sqrt(width // HEADS)
    per_chunk = 4 * width * width // LANES // chunks
    big = pltpu.VMEM((rows, width), BF)
    wide = pltpu.VMEM((rows, width), F32)
    back, packed = call(
        functools.partial(main_kernel, (groups, count, sub, width, chunks, factor)),
        (
            shape((groups, 2, count, sub, width), BF),
            shape((chunks, per_chunk + HALO, LANES), BF),
        ),
        [wide] + [big] * 10 + [wide, pltpu.VMEM((32 * width // LANES, LANES), F32)],
        got, before, after, kernel, w_query, w_key, w_value, w_out,
    )

    cores, xs = 2, 2
    ys, zs = groups // cores, blocks // xs

    def device(y, core, z, x):
        return ((y * cores + core) * zs + z) * xs + x

    over_core = [
        [device(y, core, z, x) for core in range(cores)]
        for y in range(ys) for z in range(zs) for x in range(xs)
    ]
    over_plane = [
        [device(y, core, z, x) for y in range(ys) for x in range(xs)]
        for core in range(cores) for z in range(zs)
    ]
    over_line = [
        [device(y, core, z, x) for z in range(zs)]
        for y in range(ys) for core in range(cores) for x in range(xs)
    ]
    order = [0] * chunks
    for y in range(ys):
        for core in range(cores):
            for z in range(zs):
                for x in range(xs):
                    order[device(y, core, z, x)] = ((core * ys + y) * xs + x) * zs + z
    part = summed_over(packed, over_core, cores)
    part = summed_over(part, over_plane, ys * xs)
    part = summed_over(part, over_line, zs)
    whole = lax.all_gather(part[0], ("mic", "tm"), axis=0, tiled=False)

    home = lax.all_to_all(back, "mic", 0, 0, tiled=True)
    up = [(i, i + 1) for i in range(blocks - 1)]
    down = [(j, i) for i, j in up]
    before = lax.ppermute(home[groups - 1, 1, :, sub - HALO :, :], "tm", up)
    after = lax.ppermute(home[0, 1, :, :HALO, :], "tm", down)
    layer_out, frame_grad = call(
        functools.partial(frame_kernel, (groups, count, sub, width)),
        (shape((count, length, width), BF), shape((count, length, width), BF)),
        [], home, before, after, cotangent, kernel,
    )
    norm = 1.0 / math.sqrt(groups * count * blocks * length)
    square = shape((width, width), F32)
    grads = call(
        functools.partial(final_kernel, (chunks, width, norm, order)),
        (shape((31, width), F32), square, square, square, square),
        [], whole,
    )
    return (layer_out, frame_grad, *grads)


def solution(mesh):
    in_specs = (P("mic", "tm", None), P("mic", "tm", None), P(), P(), P(), P(), P())
    out_specs = (P("mic", "tm", None), P("mic", "tm", None), P(), P(), P(), P(), P())
    return jax.shard_map(shards, mesh=mesh, in_specs=in_specs, out_specs=out_specs, check_vma=False)
```

time: 316 us -> 151 us (0.48)
  waiting for transfers between devices: 158 us -> 34 us
  matrix products: 38.4 us -> 0 us
  local copies, waits for them, and re-layouts: 33.9 us -> 1.36 us
  blocking collectives: 41.1 us -> 68.1 us
  Pallas kernels: 0 us -> 20.2 us
  other arithmetic: 16.1 us -> 2.69 us
    psum x1 -> x0, waiting for transfers between devices: 91.2 us -> none  [shards(): lax.psum((tap_term, query_term, key_term, value_term, out_term), ('mic',...]
    all_to_all x0 -> x5, blocking collectives: none -> 68.1 us  [the longest x3 43.5 us: summed_over(): lax.all_to_all(x.reshape(size, x.shape[0] // size, *x.shape[1:]), ('mic',...]
    psum x1 -> x0, blocking collectives: 41.1 us -> none  [shards(): lax.psum((tap_term, query_term, key_term, value_term, out_term), ('mic',...]
    reduce_scatter x2 -> x0, waiting for transfers between devices: 38.9 us -> none  [the longest x1 31.6 us: shards(): lax.psum_scatter(value_terms, 'mic', scatter_dimension=0, tiled=True)]
    dot_general x17 -> x0, matrix products: 33.3 us -> none  [the longest x4 7.31 us: outer(): jnp.dot(left.reshape(-1, width).T, right.reshape(-1, right.shape[-1]), pr...]
    pallas_call x0 -> x3, Pallas kernels: none -> 20.2 us  [call(): pl.pallas_call(body, out_shape=outs, in_specs=[pl.BlockSpec(memory_space=...]
    transpose x2 -> x1, local copies, waits for them, and re-layouts: 9.85 us -> 0.04 us  [shards(): got = lax.all_to_all(send.transpose(2, 0, 1, 3, 4), 'mic', 0, 0, tiled=True)]
    reshape x4 -> x0, local copies, waits for them, and re-layouts: 9.76 us -> none  [split_heads(): rows.astype(jnp.float32)]
  transfers between devices with their start and end apart: 9 -> 5, of which waited for: 5 -> 3; matrix products, arithmetic and copies ran while one was open for 14% -> 0% of each run, Pallas kernels for 0% -> 2%
where the time goes in v1:
time: 151 us
  blocking collectives  68.1 us (45%)
  waiting for transfers between devices  34 us (23%)
  Pallas kernels  20.2 us (13%)
  between operations  14.1 us (9%)
  starting transfers between devices  10.2 us (7%)
  other arithmetic  2.69 us (2%)
    all_to_all x3, blocking collectives, summed_over(): lax.all_to_all(x.reshape(size, x.shape[0] // size, *x.shape[1:]), ('mic',...  43.5 us
    all_gather x1, waiting for transfers between devices, shards(): whole = lax.all_gather(part[0], ('mic', 'tm'), axis=0, tiled=False)  31.5 us
    pallas_call x3, Pallas kernels, call(): pl.pallas_call(body, out_shape=outs, in_specs=[pl.BlockSpec(memory_space=...  20.2 us
    all_to_all x1, blocking collectives, shards(): got = lax.all_to_all(send.transpose(2, 0, 1, 3, 4), 'mic', 0, 0, tiled=True)  12.9 us
    all_to_all x1, blocking collectives, shards(): home = lax.all_to_all(back, 'mic', 0, 0, tiled=True)  11.7 us
    ppermute x1, starting transfers between devices, shards(): before = lax.ppermute(home[groups - 1, 1, :, sub - HALO:, :], 'tm', up)  4.55 us
    ppermute x1, starting transfers between devices, shards(): before = lax.ppermute(got[:, 0, :, sub - HALO:, :], ('mic', 'tm'), up)  3.04 us
  transfers between devices with their start and end apart: 5, of which 3 were waited for; matrix products, arithmetic and copies ran while one was open for 0% of the time, Pallas kernels for 2%

profile of v1, /device:TPU:0, one launch (start us, length us, event | category | flops | bytes accessed | tf_op | source)
XLA Modules:
  0.0 150.6 jit_solution(2768409096402055817)
XLA Ops:
  7.2 0.0 all-gather.3.cloned.1.call-start
  7.2 1.1 maximum_bitcast_fusion
  8.3 12.9 %all_to_all.25.got = bf16[4,2,2,32,512]{4,3,2,1,0:T(8,128)(2,1)S(1)} all-to-all(bf16[4,2,2,32,512]{4,3,2,1,0:T(8,128)(2,1)S(1)} %copy.21), channel_id=1, replica_groups=mesh['mic'=4,'tm'=8] {'mic'}, dimensions={0} | all-to-all | bytes 1048576 | tf_op jit(solution)/shard_map/all_to_all | solution.py:271
  21.2 0.0 copy-start
  21.3 1.3 collective-permute-start.1
  22.6 3.0 %collective-permute-start = (bf16[4,2,16,512]{3,2,1,0:T(8,128)(2,1)S(1)}, bf16[4,2,16,512]{3,2,1,0:T(8,128)(2,1)S(1)}, u32[]{:S(2)}, u32[]{:S(2)}) collective-permute-start(bf16[4,2,16,512]{3,2,1,0:T(8,128)(2,1)S(1)} %get-tuple-element.28), channel_id=1, source_target_pairs={{0,8},{8,16},{16,24},{24,1},{1,9},{9,17},{17,25},{25,2},{2,10},{10... | collective-permute-start | bytes 393224 | tf_op jit(solution)/shard_map/ppermute | solution.py:274
  25.6 0.0 collective-permute-done.1.after
  25.6 0.0 copy-start.3
  25.6 0.9 collective-permute-done.before
  26.6 0.0 copy-done
  26.6 0.0 copy-done.3
  26.6 0.0 copy-start.4
  26.6 0.7 copy-done.4
  27.2 12.6 %shard_map.126 = (bf16[4,2,2,32,512]{4,3,2,1,0:T(8,128)(2,1)}, bf16[32,272,128]{2,1,0:T(8,128)(2,1)}) custom-call(bf16[4,2,2,32,512]{4,3,2,1,0:T(8,128)(2,1)} %copy-done, bf16[4,2,16,512]{3,2,1,0:T(8,128)(2,1)} %copy-done.4, bf16[4,2,16,512]{3,2,1,0:T(8,128)(2,1)} %copy-done.3, f32[31,512]{1,0:T(8,128)} %kern.3, bf16[512,512]{1,0:T(8,128)(2,1)} %wq.1, ...), custom_call_target="tpu_custom_call" | custom-call | tf_op jit(solution)/shard_map/pallas_call | solution.py:237
  39.8 7.9 %all_to_all.26 = bf16[2,16,272,128]{3,2,1,0:T(8,128)(2,1)S(1)} all-to-all(bf16[2,16,272,128]{3,2,1,0:T(8,128)(2,1)} %bitcast.24), channel_id=1, replica_groups={{0,8},{1,9},{2,10},{3,11},{4,12},{5,13},{6,14},{7,15},{16,24},{17,25},{..., dimensions={0} | all-to-all | bytes 4456448 | tf_op jit(solution)/shard_map/all_to_all | solution.py:255
  47.7 0.7 reduce_sum.38
  48.4 0.0 copy-start.2
  48.4 20.9 %all_to_all.27 = bf16[4,4,272,128]{3,2,1,0:T(8,128)(2,1)S(1)} all-to-all(bf16[4,4,272,128]{3,2,1,0:T(8,128)(2,1)S(1)} %bitcast.22), channel_id=1, replica_groups={{0,1,16,17},{2,3,18,19},{4,5,20,21},{6,7,22,23},{8,9,24,25},{10,11,26,2..., dimensions={0} | all-to-all | bytes 2228224 | tf_op jit(solution)/shard_map/all_to_all | solution.py:255
  69.3 0.2 reduce_sum.39
  69.6 14.6 %all_to_all.28 = bf16[4,1,272,128]{3,2,1,0:T(8,128)(2,1)S(1)} all-to-all(bf16[4,1,272,128]{3,2,1,0:T(8,128)(2,1)S(1)} %bitcast.25), channel_id=1, replica_groups={{0,2,4,6},{1,3,5,7},{8,10,12,14},{9,11,13,15},{16,18,20,22},{17,19,21,2..., dimensions={0} | all-to-all | bytes 557056 | tf_op jit(solution)/shard_map/all_to_all | solution.py:255
  84.2 0.7 reduce_sum.40
  84.9 0.0 all-gather.3.cloned.1.call-update
  84.9 0.0 copy-done.2
  84.9 11.7 %all_to_all.29.got = bf16[4,2,2,32,512]{4,3,2,1,0:T(8,128)(2,1)S(1)} all-to-all(bf16[4,2,2,32,512]{4,3,2,1,0:T(8,128)(2,1)S(1)} %copy-done.2), channel_id=1, replica_groups=mesh['mic'=4,'tm'=8] {'mic'}, dimensions={0} | all-to-all | bytes 1048576 | tf_op jit(solution)/shard_map/all_to_all | solution.py:320
  96.7 0.0 copy-start.1
  96.7 1.3 collective-permute-start.3
  98.0 4.5 %collective-permute-start.2 = (bf16[2,16,512]{2,1,0:T(8,128)(2,1)S(1)}, bf16[2,16,512]{2,1,0:T(8,128)(2,1)S(1)}, u32[]{:S(2)}, u32[]{:S(2)}) collective-permute-start(bf16[2,16,512]{2,1,0:T(8,128)(2,1)S(1)} %get-tuple-element.26), channel_id=1, source_target_pairs={{0,1},{1,2},{2,3},{3,4},{4,5},{5,6},{6,7},{8,9},{9,10},{10,11},{11... | collective-permute-start | bytes 98312 | tf_op jit(solution)/shard_map/ppermute | solution.py:323
  102.6 0.0 collective-permute-done.3.after
  102.6 0.0 copy-start.5
  102.6 1.6 %collective-permute-done.2.before = bf16[2,16,512]{2,1,0:T(8,128)(2,1)S(1)} collective-permute-done((bf16[2,16,512]{2,1,0:T(8,128)(2,1)S(1)}, bf16[2,16,512]{2,1,0:T(8,128)(2,1)S(1)}, u32[]{:S(2)}, u32[]{:S(2)}) %collective-permute-start.2) | collective-permute-done | bytes 32800 | tf_op jit(solution)/shard_map/ppermute | solution.py:323
  104.1 0.0 copy-done.1
  104.1 0.0 copy-done.5
  104.1 0.0 copy-start.6
  104.1 0.6 copy-done.6
  104.8 3.5 %shard_map.127 = (bf16[2,128,512]{2,1,0:T(8,128)(2,1)}, bf16[2,128,512]{2,1,0:T(8,128)(2,1)}) custom-call(bf16[4,2,2,32,512]{4,3,2,1,0:T(8,128)(2,1)} %copy-done.1, bf16[2,16,512]{2,1,0:T(8,128)(2,1)} %copy-done.6, bf16[2,16,512]{2,1,0:T(8,128)(2,1)} %copy-done.5, bf16[2,128,512]{2,1,0:T(8,128)(2,1)} %cot.1, f32[31,512]{1,0:T(8,128)} %kern.3), custom_call_target="tpu_custom_call" | custom-call | tf_op jit(solution)/shard_map/pallas_call | solution.py:237
  108.3 31.5 %all-gather.3.cloned.1.call-done = bf16[8704,128]{1,0:T(8,128)(2,1)} async-done(((bf16[272,128]{1,0:T(8,128)(2,1)}), bf16[8704,128]{1,0:T(8,128)(2,1)}) %all-gather.3.cloned.1.call-update) | async-done | bytes 2228240 | tf_op jit(solution)/shard_map/all_gather | solution.py:318
  139.7 4.1 %shard_map.128 = (f32[31,512]{1,0:T(8,128)}, f32[512,512]{1,0:T(8,128)}, f32[512,512]{1,0:T(8,128)}, f32[512,512]{1,0:T(8,128)}, f32[512,512]{1,0:T(8,128)}) custom-call(bf16[32,272,128]{2,1,0:T(8,128)(2,1)} %bitcast.23), custom_call_target="tpu_custom_call" | custom-call | tf_op jit(solution)/shard_map/pallas_call | solution.py:237
  (3 shorter events, 0.1 us)
Async XLA Ops:
  7.2 132.6 %all-gather.3.cloned.1.call-start = ((), (), s32[]{:S(2)}) async-start(), calls=%async_computation.5 | async-start | bytes 2297856 | tf_op jit(solution)/shard_map/all_gather | solution.py:318
  21.2 5.3 %copy-start = (bf16[4,2,2,32,512]{4,3,2,1,0:T(8,128)(2,1)}, bf16[4,2,2,32,512]{4,3,2,1,0:T(8,128)(2,1)S(1)}, u32[]{:S(2)}) copy-start(bf16[4,2,2,32,512]{4,3,2,1,0:T(8,128)(2,1)S(1)} %all_to_all.25.got) | copy-start | bytes 1572868
  21.3 4.3 %collective-permute-start.1 = (bf16[4,2,16,512]{3,2,1,0:T(8,128)(2,1)S(1)}, bf16[4,2,16,512]{3,2,1,0:T(8,128)(2,1)S(1)}, u32[]{:S(2)}, u32[]{:S(2)}) collective-permute-start(bf16[4,2,16,512]{3,2,1,0:T(8,128)(2,1)S(1)} %get-tuple-element.27), channel_id=1, source_target_pairs={{8,0},{16,8},{24,16},{1,24},{9,1},{17,9},{25,17},{2,25},{10,2},{18... | collective-permute-start | bytes 393224 | tf_op jit(solution)/shard_map/ppermute | solution.py:275
  22.6 4.0 %collective-permute-start = (bf16[4,2,16,512]{3,2,1,0:T(8,128)(2,1)S(1)}, bf16[4,2,16,512]{3,2,1,0:T(8,128)(2,1)S(1)}, u32[]{:S(2)}, u32[]{:S(2)}) collective-permute-start(bf16[4,2,16,512]{3,2,1,0:T(8,128)(2,1)S(1)} %get-tuple-element.28), channel_id=1, source_target_pairs={{0,8},{8,16},{16,24},{24,1},{1,9},{9,17},{17,25},{25,2},{2,10},{10... | collective-permute-start | bytes 393224 | tf_op jit(solution)/shard_map/ppermute | solution.py:274
  25.6 1.0 copy-start.3
  26.6 0.7 copy-start.4
  48.4 36.5 %copy-start.2 = (bf16[4,2,2,32,512]{4,3,2,1,0:T(8,128)(2,1)S(1)}, bf16[4,2,2,32,512]{4,3,2,1,0:T(8,128)(2,1)}, u32[]{:S(2)}) copy-start(bf16[4,2,2,32,512]{4,3,2,1,0:T(8,128)(2,1)} %get-tuple-element.16) | copy-start | bytes 1572868
  96.7 7.4 %copy-start.1 = (bf16[4,2,2,32,512]{4,3,2,1,0:T(8,128)(2,1)}, bf16[4,2,2,32,512]{4,3,2,1,0:T(8,128)(2,1)S(1)}, u32[]{:S(2)}) copy-start(bf16[4,2,2,32,512]{4,3,2,1,0:T(8,128)(2,1)S(1)} %all_to_all.29.got) | copy-start | bytes 1572868
  96.7 5.9 %collective-permute-start.3 = (bf16[2,16,512]{2,1,0:T(8,128)(2,1)S(1)}, bf16[2,16,512]{2,1,0:T(8,128)(2,1)S(1)}, u32[]{:S(2)}, u32[]{:S(2)}) collective-permute-start(bf16[2,16,512]{2,1,0:T(8,128)(2,1)S(1)} %get-tuple-element.25), channel_id=1, source_target_pairs={{1,0},{2,1},{3,2},{4,3},{5,4},{6,5},{7,6},{9,8},{10,9},{11,10},{12... | collective-permute-start | bytes 98312 | tf_op jit(solution)/shard_map/ppermute | solution.py:324
  98.0 6.1 %collective-permute-start.2 = (bf16[2,16,512]{2,1,0:T(8,128)(2,1)S(1)}, bf16[2,16,512]{2,1,0:T(8,128)(2,1)S(1)}, u32[]{:S(2)}, u32[]{:S(2)}) collective-permute-start(bf16[2,16,512]{2,1,0:T(8,128)(2,1)S(1)} %get-tuple-element.26), channel_id=1, source_target_pairs={{0,1},{1,2},{2,3},{3,4},{4,5},{5,6},{6,7},{8,9},{9,10},{10,11},{11... | collective-permute-start | bytes 98312 | tf_op jit(solution)/shard_map/ppermute | solution.py:323
  102.6 1.6 %copy-start.5 = (bf16[2,16,512]{2,1,0:T(8,128)(2,1)}, bf16[2,16,512]{2,1,0:T(8,128)(2,1)S(1)}, u32[]{:S(2)}) copy-start(bf16[2,16,512]{2,1,0:T(8,128)(2,1)S(1)} %collective-permute-done.3.after) | copy-start | bytes 98308
  104.1 0.6 copy-start.6
Sparse Core Ops, SparseCore 0:
  85.1 54.6 all-gather.2

commit v2 on v1

--- a/solution.py
+++ b/solution.py
@@ -40,10 +40,12 @@
 
 
 def main_kernel(
-    plan, got, before, after, kern, wq, wk, wv, wo, back, packed,
-    conv_s, act_s, cot_s, q_s, k_s, v_s, u_s, mix_s, dq_s, dk_s, dv_s, dconv_s, tap_s,
+    plan, bits, got, before, after, kern, wq, wk, wv, wo, back, keep, send,
+    conv_s, left_s, right_s, q_s, k_s, v_s, u_s, dconv_s, tap_s,
 ):
-    groups, count, sub, width, chunks, factor = plan
+    groups, count, sub, width, factor = plan
+    act_s, mix_s = left_s.at[0], left_s.at[1]
+    dq_s, dk_s, dv_s, cot_s = (right_s.at[i] for i in range(4))
     mics = groups * count
     cuts = sub // HALO
     block = mics * HALO
@@ -138,18 +140,6 @@
                 got[a, 0, m, part, :].astype(F32) + proj[at : at + HALO]
             ).astype(BF)
             back[a, 1, m, part, :] = dconv_s[at : at + HALO, :].astype(BF)
-
-    per_chunk = 4 * cols * width // chunks
-    act_t = acted.T
-    mix_t = mix_s[...].T
-    for i, (left, right) in enumerate(
-        ((act_t, dq_s), (act_t, dk_s), (act_t, dv_s), (mix_t, cot_s))
-    ):
-        grad = mm(left, right[...]).astype(BF)
-        for cb in range(cols):
-            for at in range(0, width, per_chunk):
-                g = ((i * cols + cb) * width + at) // per_chunk
-                packed[g, 0:per_chunk, :] = grad[at : at + per_chunk, cb * LANES : (cb + 1) * LANES]
 
     for lc in range(cols):
         lanes = slice(lc * LANES, (lc + 1) * LANES)
@@ -180,35 +170,83 @@
             [jnp.sum(x, axis=0, keepdims=True) for x in accs] + [jnp.zeros((1, LANES), F32)], axis=0
         )
 
-    tap_rows = max(1, cols * 32 // chunks)
-    for g in range(chunks):
-        tail = jnp.zeros((HALO, LANES), F32)
-        if g * tap_rows < cols * 32:
-            tail = jnp.concatenate(
-                [tap_s[g * tap_rows : (g + 1) * tap_rows, :], tail[tap_rows:]], axis=0
-            )
-        packed[g, per_chunk : per_chunk + HALO, :] = tail.astype(BF)
-
-
-def final_kernel(plan, got, taps, *outs):
-    chunks, width, norm, order = plan
+    tap_s[cols * 32 :, :] = jnp.zeros((HALO, LANES), F32)
+    core = bits[0]
+    size = cols * width // 8
+    tap_rows = cols
+    for out, owner in ((keep, core), (send, 1 - core)):
+        for h in range(2):
+            i = owner * 2 + h
+            grad = mm(left_s[i // 3], right_s[i], TN).astype(BF)
+            for piece in range(8):
+                flat = piece * size
+                cb, at = flat // width, flat % width
+                tail = tap_s[pl.ds(pl.multiple_of((i * 8 + piece) * tap_rows, tap_rows), HALO), :]
+                out[h, piece // 4, piece // 2 % 2, piece % 2, 0:size, :] = grad[
+                    at : at + size, cb * LANES : (cb + 1) * LANES
+                ]
+                out[h, piece // 4, piece // 2 % 2, piece % 2, size : size + HALO, :] = tail.astype(BF)
+
+
+def add(left, right):
+    return (left.astype(F32) + right.astype(F32)).astype(BF)
+
+
+def split_core(bits, keep, got, a_keep, a_send, b_keep, b_send):
+    y, x = bits[1], bits[2]
+    for h, bit, mine, theirs in ((0, x, a_keep, a_send), (1, y, b_keep, b_send)):
+        theirs[...] = add(keep[h, 1 - bit], got[h, 1 - bit])
+        mine[...] = add(keep[h, bit], got[h, bit])
+
+
+def split_plane(which, bits, keep, got, mine, theirs):
+    bit = bits[which]
+    theirs[...] = add(keep[1 - bit], got[1 - bit])
+    mine[...] = add(keep[bit], got[bit])
+
+
+def split_line(bits, a_keep, a_got, b_keep, b_got, mine, theirs):
+    bit = bits[3]
+    for h, keep, got in ((0, a_keep, a_got), (1, b_keep, b_got)):
+        theirs[h] = add(keep[1 - bit], got[1 - bit])
+        mine[h] = add(keep[bit], got[bit])
+
+
+def final_kernel(plan, bits, own, far, other_own, other_far, taps, *refs):
+    width, norm = plan
+    outs, tap_s = refs[:4], refs[4]
     cols = width // LANES
-    per_chunk = 4 * cols * width // chunks
-    tap_rows = max(1, cols * 32 // chunks)
-    for f in range(chunks):
-        g = order[f]
-        flat = g * per_chunk
-        i, cb, at = flat // (cols * width), (flat // width) % cols, flat % width
-        outs[i][at : at + per_chunk, cb * LANES : (cb + 1) * LANES] = (
-            got[f, 0:per_chunk, :].astype(F32) * norm
-        )
-        row = g * tap_rows
-        if row < cols * 32:
-            lc, j = row // 32, row % 32
-            kept = min(tap_rows, 31 - j)
-            if kept > 0:
-                tail = got[f, per_chunk : per_chunk + HALO, :].astype(F32) * norm
-                taps[j : j + kept, lc * LANES : (lc + 1) * LANES] = tail[0:kept]
+    size = cols * width // 8
+    core, y, x, z = bits[0], bits[1], bits[2], bits[3]
+
+    def emit(which, near, across):
+        for h in range(2):
+            i = 2 * which + h
+            first, second = (x, y) if h == 0 else (y, x)
+            for b1 in range(2):
+                for b2 in range(2):
+                    for b3 in range(2):
+                        part = (near, across)[b1]
+                        piece = (first ^ b1) * 4 + (second ^ b2) * 2 + (z ^ b3)
+                        flat = piece * size
+                        cb, at = flat // width, flat % width
+                        outs[i][
+                            pl.ds(pl.multiple_of(at, size), size),
+                            pl.ds(pl.multiple_of(cb * LANES, LANES), LANES),
+                        ] = part[h, b2, b3, 0:size, :].astype(F32) * norm
+                        tap_s[i * 8 + piece] = part[h, b2, b3, size : size + HALO, :].astype(F32) * norm
+
+    for which in range(2):
+        @pl.when(core == which)
+        def _():
+            emit(which, own, far)
+            emit(1 - which, other_own, other_far)
+
+    for g in range(32):
+        row = g * cols
+        lc, j = row // 32, row % 32
+        kept = min(cols, 31 - j)
+        taps[j : j + kept, lc * LANES : (lc + 1) * LANES] = tap_s[g, 0:kept]
 
 
 def frame_kernel(plan, got, before, after, cot, kern, layer_out, frame_grad):
@@ -237,7 +275,10 @@
     return pl.pallas_call(
         body,
         out_shape=outs,
-        in_specs=[pl.BlockSpec(memory_space=pltpu.VMEM)] * len(args),
+        in_specs=[
+            pl.BlockSpec(memory_space=pltpu.SMEM if x.dtype == jnp.int32 else pltpu.VMEM)
+            for x in args
+        ],
         out_specs=jax.tree.map(lambda _: pl.BlockSpec(memory_space=pltpu.VMEM), outs),
         scratch_shapes=scratch,
         compiler_params=pltpu.CompilerParams(vmem_limit_bytes=VMEM_LIMIT),
@@ -251,19 +292,10 @@
     return [(flat(s), flat(s + 1)) for s in range(groups * blocks - 1)]
 
 
-def summed_over(x, groups, size):
-    got = lax.all_to_all(
-        x.reshape(size, x.shape[0] // size, *x.shape[1:]),
-        ("mic", "tm"), 0, 0, tiled=True, axis_index_groups=groups,
-    )
-    return jnp.sum(got.astype(F32), axis=0).astype(BF)
-
-
 def shards(frames, cotangent, kernel, w_query, w_key, w_value, w_out):
     groups, blocks = lax.axis_size("mic"), lax.axis_size("tm")
     count, length, width = frames.shape
     sub = length // groups
-    chunks = groups * blocks
     rows = groups * count * sub
     shape = jax.ShapeDtypeStruct
 
@@ -274,48 +306,51 @@
     before = lax.ppermute(got[:, 0, :, sub - HALO :, :], ("mic", "tm"), up)
     after = lax.ppermute(got[:, 0, :, :HALO, :], ("mic", "tm"), down)
 
+    mic, tm = lax.axis_index("mic"), lax.axis_index("tm")
+    bits = jnp.stack([mic % 2, mic // 2, tm % 2, tm // 2 % 2]).astype(jnp.int32)
+    over_core, over_y, over_x, over_z = blocks, 2 * blocks, 1, 2
+
+    def swap(x, mask):
+        return lax.ppermute(x, ("mic", "tm"), [(f, f ^ mask) for f in range(groups * blocks)])
+
     factor = 1.0 / math.sqrt(width // HEADS)
-    per_chunk = 4 * width * width // LANES // chunks
+    piece = (width * width // LANES // 8 + HALO, LANES)
     big = pltpu.VMEM((rows, width), BF)
     wide = pltpu.VMEM((rows, width), F32)
-    back, packed = call(
-        functools.partial(main_kernel, (groups, count, sub, width, chunks, factor)),
-        (
-            shape((groups, 2, count, sub, width), BF),
-            shape((chunks, per_chunk + HALO, LANES), BF),
-        ),
-        [wide] + [big] * 10 + [wide, pltpu.VMEM((32 * width // LANES, LANES), F32)],
-        got, before, after, kernel, w_query, w_key, w_value, w_out,
-    )
-
-    cores, xs = 2, 2
-    ys, zs = groups // cores, blocks // xs
-
-    def device(y, core, z, x):
-        return ((y * cores + core) * zs + z) * xs + x
-
-    over_core = [
-        [device(y, core, z, x) for core in range(cores)]
-        for y in range(ys) for z in range(zs) for x in range(xs)
-    ]
-    over_plane = [
-        [device(y, core, z, x) for y in range(ys) for x in range(xs)]
-        for core in range(cores) for z in range(zs)
-    ]
-    over_line = [
-        [device(y, core, z, x) for z in range(zs)]
-        for y in range(ys) for core in range(cores) for x in range(xs)
-    ]
-    order = [0] * chunks
-    for y in range(ys):
-        for core in range(cores):
-            for z in range(zs):
-                for x in range(xs):
-                    order[device(y, core, z, x)] = ((core * ys + y) * xs + x) * zs + z
-    part = summed_over(packed, over_core, cores)
-    part = summed_over(part, over_plane, ys * xs)
-    part = summed_over(part, over_line, zs)
-    whole = lax.all_gather(part[0], ("mic", "tm"), axis=0, tiled=False)
+    halves = shape((2, 2, 2, 2, *piece), BF)
+    back, keep, send = call(
+        functools.partial(main_kernel, (groups, count, sub, width, factor)),
+        (shape((groups, 2, count, sub, width), BF), halves, halves),
+        [
+            wide, pltpu.VMEM((2, rows, width), BF), pltpu.VMEM((4, rows, width), BF),
+            big, big, big, big, wide, pltpu.VMEM((32 * width // LANES + HALO, LANES), F32),
+        ],
+        bits, got, before, after, kernel, w_query, w_key, w_value, w_out,
+    )
+
+    quarter, eighth, pair = (shape((*lead, *piece), BF) for lead in ((2, 2), (2,), (2,)))
+    a_keep, a_send, b_keep, b_send = call(
+        split_core, (quarter,) * 4, [], bits, keep, swap(send, over_core)
+    )
+    a_got, b_got = swap(a_send, over_x), swap(b_send, over_y)
+    a_keep, a_send = call(
+        functools.partial(split_plane, 1), (eighth,) * 2, [], bits, a_keep, a_got
+    )
+    b_keep, b_send = call(
+        functools.partial(split_plane, 2), (eighth,) * 2, [], bits, b_keep, b_got
+    )
+    a_got, b_got = swap(a_send, over_y), swap(b_send, over_x)
+    mine, theirs = call(split_line, (pair,) * 2, [], bits, a_keep, a_got, b_keep, b_got)
+    mine = add(mine, swap(theirs, over_z))
+    mask = 2 * over_z
+    while mask < blocks:
+        mine = add(mine, swap(mine, mask))
+        mask *= 2
+    line = jnp.stack([mine, swap(mine, over_z)], axis=1)
+    plane = jnp.stack([line, jnp.stack([swap(line[0], over_y), swap(line[1], over_x)])], axis=1)
+    other_plane = swap(plane, over_core)
+    far = jnp.stack([swap(plane[0], over_x), swap(plane[1], over_y)])
+    other_far = swap(far, over_core)
 
     home = lax.all_to_all(back, "mic", 0, 0, tiled=True)
     up = [(i, i + 1) for i in range(blocks - 1)]
@@ -330,9 +365,10 @@
     norm = 1.0 / math.sqrt(groups * count * blocks * length)
     square = shape((width, width), F32)
     grads = call(
-        functools.partial(final_kernel, (chunks, width, norm, order)),
+        functools.partial(final_kernel, (width, norm)),
         (shape((31, width), F32), square, square, square, square),
-        [], whole,
+        [pltpu.VMEM((32, HALO, LANES), F32)],
+        bits, plane, far, other_plane, other_far,
     )
     return (layer_out, frame_grad, *grads)
 

time: 151 us -> 126 us (0.83)
  blocking collectives: 68.1 us -> 12.9 us
  starting transfers between devices: 10.2 us -> 33.7 us
  between operations: 14.1 us -> 0.86 us
  Pallas kernels: 20.2 us -> 28.5 us
  waiting for transfers between devices: 34 us -> 39.8 us
  local copies, waits for them, and re-layouts: 1.36 us -> 6.37 us
    all_to_all x4 -> x0, blocking collectives: 55.2 us -> none  [the longest x3 43.5 us: summed_over(): lax.all_to_all(x.reshape(size, x.shape[0] // size, *x.shape[1:]), ('mic',...]
    all_gather x1 -> x0, waiting for transfers between devices: 31.5 us -> none  [shards(): whole = lax.all_gather(part[0], ('mic', 'tm'), axis=0, tiled=False)]
    ppermute x0 -> x14, waiting for transfers between devices: none -> 31.3 us  [swap(): lax.ppermute(x, ('mic', 'tm'), [(f, f ^ mask) for f in range(groups * blo...]
    ppermute x0 -> x14, starting transfers between devices: none -> 20 us  [swap(): lax.ppermute(x, ('mic', 'tm'), [(f, f ^ mask) for f in range(groups * blo...]
    pallas_call x3 -> x7, Pallas kernels: 20.2 us -> 28.5 us  [call(): pl.pallas_call(body, out_shape=outs, in_specs=[pl.BlockSpec(memory_space=...]
    all_to_all x0 -> x1, waiting for transfers between devices: none -> 6.56 us  [shards(): home = lax.all_to_all(back, 'mic', 0, 0, tiled=True)]
    unnamed x14 -> x30, local copies, waits for them, and re-layouts: 1.3 us -> 6.31 us
    all_to_all x0 -> x1, starting transfers between devices: none -> 3.47 us  [shards(): home = lax.all_to_all(back, 'mic', 0, 0, tiled=True)]
  transfers between devices with their start and end apart: 5 -> 19, of which waited for: 3 -> 14; matrix products, arithmetic and copies ran while one was open for 0% -> 1% of each run, Pallas kernels for 2% -> 6%
where the time goes in v2:
time: 126 us; the launch traced here: 125 us
  waiting for transfers between devices  39.8 us (32%)
  starting transfers between devices  33.7 us (27%)
  Pallas kernels  28.5 us (23%)
  blocking collectives  12.9 us (10%)
  local copies, waits for them, and re-layouts  6.37 us (5%)
  other arithmetic  2.9 us (2%)
    ppermute x14, waiting for transfers between devices, swap(): lax.ppermute(x, ('mic', 'tm'), [(f, f ^ mask) for f in range(groups * blo...  31.3 us
    pallas_call x7, Pallas kernels, call(): pl.pallas_call(body, out_shape=outs, in_specs=[pl.BlockSpec(memory_space=...  28.5 us
    ppermute x14, starting transfers between devices, swap(): lax.ppermute(x, ('mic', 'tm'), [(f, f ^ mask) for f in range(groups * blo...  20 us
    all_to_all x1, blocking collectives, shards(): got = lax.all_to_all(send.transpose(2, 0, 1, 3, 4), 'mic', 0, 0, tiled=True)  12.9 us
    all_to_all x1, waiting for transfers between devices, shards(): home = lax.all_to_all(back, 'mic', 0, 0, tiled=True)  6.56 us
    unnamed x30, local copies, waits for them, and re-layouts  6.31 us
    ppermute x1, starting transfers between devices, shards(): before = lax.ppermute(home[groups - 1, 1, :, sub - HALO:, :], 'tm', up)  4.55 us
    all_to_all x1, starting transfers between devices, shards(): home = lax.all_to_all(back, 'mic', 0, 0, tiled=True)  3.47 us
  transfers between devices with their start and end apart: 19, of which 14 were waited for; matrix products, arithmetic and copies ran while one was open for 1% of the time, Pallas kernels for 6%

profile of v2, /device:TPU:0, one launch (start us, length us, event | category | flops | bytes accessed | tf_op | source)
XLA Modules:
  0.0 125.0 jit_solution(4709030061845080975)
XLA Ops:
  0.6 1.1 maximum_bitcast_fusion
  1.8 12.9 %all_to_all.10.got = bf16[4,2,2,32,512]{4,3,2,1,0:T(8,128)(2,1)S(1)} all-to-all(bf16[4,2,2,32,512]{4,3,2,1,0:T(8,128)(2,1)S(1)} %copy.22), channel_id=1, replica_groups=mesh['mic'=4,'tm'=8] {'mic'}, dimensions={0} | all-to-all | bytes 1048576 | tf_op jit(solution)/shard_map/all_to_all | solution.py:303
  14.7 1.3 %collective-permute-start.1 = (bf16[4,2,16,512]{3,2,1,0:T(8,128)(2,1)S(1)}, bf16[4,2,16,512]{3,2,1,0:T(8,128)(2,1)S(1)}, u32[]{:S(2)}, u32[]{:S(2)}) collective-permute-start(bf16[4,2,16,512]{3,2,1,0:T(8,128)(2,1)S(1)} %get-tuple-element.51), channel_id=1, source_target_pairs={{8,0},{16,8},{24,16},{1,24},{9,1},{17,9},{25,17},{2,25},{10,2},{18... | collective-permute-start | bytes 393224 | tf_op jit(solution)/shard_map/ppermute | solution.py:307
  16.0 3.0 %collective-permute-start = (bf16[4,2,16,512]{3,2,1,0:T(8,128)(2,1)S(1)}, bf16[4,2,16,512]{3,2,1,0:T(8,128)(2,1)S(1)}, u32[]{:S(2)}, u32[]{:S(2)}) collective-permute-start(bf16[4,2,16,512]{3,2,1,0:T(8,128)(2,1)S(1)} %get-tuple-element.52), channel_id=1, source_target_pairs={{0,8},{8,16},{16,24},{24,1},{1,9},{9,17},{17,25},{25,2},{2,10},{10... | collective-permute-start | bytes 393224 | tf_op jit(solution)/shard_map/ppermute | solution.py:306
  19.1 0.6 pad_add_fusion.bits
  20.3 0.7 copy-done.12
  21.0 12.6 %shard_map.126 = (bf16[4,2,2,32,512]{4,3,2,1,0:T(8,128)(2,1)}, bf16[2,2,2,2,272,128]{5,4,3,2,1,0:T(8,128)(2,1)}, bf16[2,2,2,2,272,128]{5,4,3,2,1,0:T(8,128)(2,1)}) custom-call(s32[4]{0:T(128)} %pad_add_fusion.bits, bf16[4,2,2,32,512]{4,3,2,1,0:T(8,128)(2,1)} %copy-done, bf16[4,2,16,512]{3,2,1,0:T(8,128)(2,1)} %copy-done.12, ...), custom_call_target="tpu_custom_call" | custom-call | tf_op jit(solution)/shard_map/pallas_call | solution.py:275
  33.6 1.3 %collective-permute-start.4 = (bf16[2,2,2,2,272,128]{5,4,3,2,1,0:T(8,128)(2,1)}, bf16[2,2,2,2,272,128]{5,4,3,2,1,0:T(8,128)(2,1)S(1)}, u32[]{:S(2)}, u32[]{:S(2)}) collective-permute-start(bf16[2,2,2,2,272,128]{5,4,3,2,1,0:T(8,128)(2,1)} %get-tuple-element.31), channel_id=1, source_target_pairs={{0,8},{1,9},{2,10},{3,11},{4,12},{5,13},{6,14},{7,15},{8,0},{9,1},... | collective-permute-start | bytes 3342344 | tf_op jit(solution)/shard_map/ppermute | solution.py:314
  34.9 2.6 %collective-permute-done.4.got = bf16[2,2,2,2,272,128]{5,4,3,2,1,0:T(8,128)(2,1)S(1)} collective-permute-done((bf16[2,2,2,2,272,128]{5,4,3,2,1,0:T(8,128)(2,1)}, bf16[2,2,2,2,272,128]{5,4,3,2,1,0:T(8,128)(2,1)S(1)}, u32[]{:S(2)}, u32[]{:S(2)}) %collective-permute-start.4) | collective-permute-done | bytes 1114144 | tf_op jit(solution)/shard_map/ppermute | solution.py:314
  37.5 1.0 copy-done.4
  38.5 2.7 %shard_map.128 = (bf16[2,2,272,128]{3,2,1,0:T(8,128)(2,1)}, bf16[2,2,272,128]{3,2,1,0:T(8,128)(2,1)}, bf16[2,2,272,128]{3,2,1,0:T(8,128)(2,1)}, bf16[2,2,272,128]{3,2,1,0:T(8,128)(2,1)}) custom-call(s32[4]{0:T(128)} %pad_add_fusion.bits, bf16[2,2,2,2,272,128]{5,4,3,2,1,0:T(8,128)(2,1)} %get-tuple-element.30.keep, bf16[2,2,2,2,272,128]{5,4,3,2,1,0:T(8,128)(2,1)} %copy-done.4), custom_call_target="tpu_custom_call" | custom-call | tf_op jit(solution)/shard_map/pallas_call | solution.py:275
  41.2 4.0 %collective-permute-start.5 = (bf16[2,2,272,128]{3,2,1,0:T(8,128)(2,1)}, bf16[2,2,272,128]{3,2,1,0:T(8,128)(2,1)S(1)}, u32[]{:S(2)}, u32[]{:S(2)}) collective-permute-start(bf16[2,2,272,128]{3,2,1,0:T(8,128)(2,1)} %get-tuple-element.33), channel_id=1, source_target_pairs={{0,1},{1,0},{2,3},{3,2},{4,5},{5,4},{6,7},{7,6},{8,9},{9,8},{10,11... | collective-permute-start | bytes 835592 | tf_op jit(solution)/shard_map/ppermute | solution.py:314
  45.2 0.9 collective-permute-start.7
  46.0 6.3 %collective-permute-done.5.got = bf16[2,2,272,128]{3,2,1,0:T(8,128)(2,1)S(1)} collective-permute-done((bf16[2,2,272,128]{3,2,1,0:T(8,128)(2,1)}, bf16[2,2,272,128]{3,2,1,0:T(8,128)(2,1)S(1)}, u32[]{:S(2)}, u32[]{:S(2)}) %collective-permute-start.5) | collective-permute-done | bytes 278560 | tf_op jit(solution)/shard_map/ppermute | solution.py:314
  52.4 0.7 copy-done.8
  53.1 1.8 %shard_map.129 = (bf16[2,272,128]{2,1,0:T(8,128)(2,1)}, bf16[2,272,128]{2,1,0:T(8,128)(2,1)}) custom-call(s32[4]{0:T(128)} %pad_add_fusion.bits, bf16[2,2,272,128]{3,2,1,0:T(8,128)(2,1)} %get-tuple-element.32.keep, bf16[2,2,272,128]{3,2,1,0:T(8,128)(2,1)} %copy-done.8), custom_call_target="tpu_custom_call" | custom-call | tf_op jit(solution)/shard_map/pallas_call | solution.py:275
  54.9 0.9 collective-permute-start.6
  55.7 0.7 copy-done.7
  56.4 1.8 %shard_map.130 = (bf16[2,272,128]{2,1,0:T(8,128)(2,1)}, bf16[2,272,128]{2,1,0:T(8,128)(2,1)}) custom-call(s32[4]{0:T(128)} %pad_add_fusion.bits, bf16[2,2,272,128]{3,2,1,0:T(8,128)(2,1)} %get-tuple-element.36.keep, bf16[2,2,272,128]{3,2,1,0:T(8,128)(2,1)} %copy-done.7), custom_call_target="tpu_custom_call" | custom-call | tf_op jit(solution)/shard_map/pallas_call | solution.py:275
  58.2 1.7 %collective-permute-start.8 = (bf16[2,272,128]{2,1,0:T(8,128)(2,1)}, bf16[2,272,128]{2,1,0:T(8,128)(2,1)S(1)}, u32[]{:S(2)}, u32[]{:S(2)}) collective-permute-start(bf16[2,272,128]{2,1,0:T(8,128)(2,1)} %get-tuple-element.39), channel_id=1, source_target_pairs={{0,1},{1,0},{2,3},{3,2},{4,5},{5,4},{6,7},{7,6},{8,9},{9,8},{10,11... | collective-permute-start | bytes 417800 | tf_op jit(solution)/shard_map/ppermute | solution.py:314
  60.3 3.2 %collective-permute-done.8.b_got = bf16[2,272,128]{2,1,0:T(8,128)(2,1)S(1)} collective-permute-done((bf16[2,272,128]{2,1,0:T(8,128)(2,1)}, bf16[2,272,128]{2,1,0:T(8,128)(2,1)S(1)}, u32[]{:S(2)}, u32[]{:S(2)}) %collective-permute-start.8) | collective-permute-done | bytes 139296 | tf_op jit(solution)/shard_map/ppermute | solution.py:314
  63.5 0.7 copy-done.10
  64.1 1.9 %shard_map.131 = (bf16[2,272,128]{2,1,0:T(8,128)(2,1)}, bf16[2,272,128]{2,1,0:T(8,128)(2,1)}) custom-call(s32[4]{0:T(128)} %pad_add_fusion.bits, bf16[2,272,128]{2,1,0:T(8,128)(2,1)} %get-tuple-element.34.a_keep, bf16[2,272,128]{2,1,0:T(8,128)(2,1)} %copy-done.9, bf16[2,272,128]{2,1,0:T(8,128)(2,1)} %get-tuple-element.38.b_keep, bf16[2,272,128]{2,1,0:T(8,128)(2,1)} %copy-done.10), custom_call_target="tpu_custom_call" | custom-call | tf_op jit(solution)/shard_map/pallas_call | solution.py:275
  66.0 2.6 %collective-permute-start.9 = (bf16[2,272,128]{2,1,0:T(8,128)(2,1)}, bf16[2,272,128]{2,1,0:T(8,128)(2,1)S(1)}, u32[]{:S(2)}, u32[]{:S(2)}) collective-permute-start(bf16[2,272,128]{2,1,0:T(8,128)(2,1)} %get-tuple-element.41), channel_id=1, source_target_pairs={{0,2},{1,3},{2,0},{3,1},{4,6},{5,7},{6,4},{7,5},{8,10},{9,11},{10,... | collective-permute-start | bytes 417800 | tf_op jit(solution)/shard_map/ppermute | solution.py:314
  68.6 3.2 %collective-permute-done.9 = bf16[2,272,128]{2,1,0:T(8,128)(2,1)S(1)} collective-permute-done((bf16[2,272,128]{2,1,0:T(8,128)(2,1)}, bf16[2,272,128]{2,1,0:T(8,128)(2,1)S(1)}, u32[]{:S(2)}, u32[]{:S(2)}) %collective-permute-start.9) | collective-permute-done | bytes 139296 | tf_op jit(solution)/shard_map/ppermute | solution.py:314
  71.9 0.9 add_convert_fusion.1
  72.8 3.1 %collective-permute-start.10 = (bf16[2,272,128]{2,1,0:T(8,128)(2,1)S(1)}, bf16[2,272,128]{2,1,0:T(8,128)(2,1)S(1)}, u32[]{:S(2)}, u32[]{:S(2)}) collective-permute-start(bf16[2,272,128]{2,1,0:T(8,128)(2,1)S(1)} %add_convert_fusion.1), channel_id=1, source_target_pairs={{0,4},{1,5},{2,6},{3,7},{4,0},{5,1},{6,2},{7,3},{8,12},{9,13},{10,... | collective-permute-start | bytes 417800 | tf_op jit(solution)/shard_map/ppermute | solution.py:314
  75.9 4.6 %collective-permute-done.10 = bf16[2,272,128]{2,1,0:T(8,128)(2,1)S(1)} collective-permute-done((bf16[2,272,128]{2,1,0:T(8,128)(2,1)S(1)}, bf16[2,272,128]{2,1,0:T(8,128)(2,1)S(1)}, u32[]{:S(2)}, u32[]{:S(2)}) %collective-permute-start.10) | collective-permute-done | bytes 139296 | tf_op jit(solution)/shard_map/ppermute | solution.py:314
  80.6 1.0 collective-permute-start.11
  81.5 4.2 %collective-permute-done.11 = bf16[2,272,128]{2,1,0:T(8,128)(2,1)S(1)} collective-permute-done((bf16[2,272,128]{2,1,0:T(8,128)(2,1)S(1)}, bf16[2,272,128]{2,1,0:T(8,128)(2,1)S(1)}, u32[]{:S(2)}, u32[]{:S(2)}) %collective-permute-start.11) | collective-permute-done | bytes 139296 | tf_op jit(solution)/shard_map/ppermute | solution.py:314
  85.7 2.1 %collective-permute-start.12 = (bf16[2,272,128]{2,1,0:T(8,128)(2,1)S(1)}, bf16[2,272,128]{2,1,0:T(8,128)(2,1)S(1)}, u32[]{:S(2)}, u32[]{:S(2)}) collective-permute-start(bf16[2,272,128]{2,1,0:T(8,128)(2,1)S(1)} %get-tuple-element.53), channel_id=1, source_target_pairs={{0,16},{1,17},{2,18},{3,19},{4,20},{5,21},{6,22},{7,23},{8,24},{9,... | collective-permute-start | bytes 417800 | tf_op jit(solution)/shard_map/ppermute | solution.py:314
  88.1 4.2 %collective-permute-done.12 = bf16[2,272,128]{2,1,0:T(8,128)(2,1)S(1)} collective-permute-done((bf16[2,272,128]{2,1,0:T(8,128)(2,1)S(1)}, bf16[2,272,128]{2,1,0:T(8,128)(2,1)S(1)}, u32[]{:S(2)}, u32[]{:S(2)}) %collective-permute-start.12) | collective-permute-done | bytes 139296 | tf_op jit(solution)/shard_map/ppermute | solution.py:314
  92.3 1.2 collective-permute-done.13
  93.6 0.7 collective-permute-start.14
  94.3 1.0 collective-permute-start.15
  95.2 3.5 %all-to-all-start.1 = ((bf16[4,2,2,32,512]{4,3,2,1,0:T(8,128)(2,1)}), bf16[4,2,2,32,512]{4,3,2,1,0:T(8,128)(2,1)S(1)}, u32[]{:S(2)}, u32[]{:S(2)}) async-start(bf16[4,2,2,32,512]{4,3,2,1,0:T(8,128)(2,1)} %get-tuple-element.27), calls=%async_computation.1 | async-start | bytes 1048576 | tf_op jit(solution)/shard_map/all_to_all | solution.py:355
  98.8 0.5 collective-permute-start.16
  99.3 0.9 collective-permute-done.14
  100.2 0.6 collective-permute-done.15
  101.0 6.6 %all-to-all-done.1.got = bf16[4,2,2,32,512]{4,3,2,1,0:T(8,128)(2,1)S(1)} async-done(((bf16[4,2,2,32,512]{4,3,2,1,0:T(8,128)(2,1)}), bf16[4,2,2,32,512]{4,3,2,1,0:T(8,128)(2,1)S(1)}, u32[]{:S(2)}, u32[]{:S(2)}) %all-to-all-start.1) | async-done | bytes 524320 | tf_op jit(solution)/shard_map/all_to_all | solution.py:355
  107.5 1.3 %collective-permute-start.3 = (bf16[2,16,512]{2,1,0:T(8,128)(2,1)S(1)}, bf16[2,16,512]{2,1,0:T(8,128)(2,1)S(1)}, u32[]{:S(2)}, u32[]{:S(2)}) collective-permute-start(bf16[2,16,512]{2,1,0:T(8,128)(2,1)S(1)} %get-tuple-element.49), channel_id=1, source_target_pairs={{1,0},{2,1},{3,2},{4,3},{5,4},{6,5},{7,6},{9,8},{10,9},{11,10},{12... | collective-permute-start | bytes 98312 | tf_op jit(solution)/shard_map/ppermute | solution.py:359
  108.8 4.5 %collective-permute-start.2 = (bf16[2,16,512]{2,1,0:T(8,128)(2,1)S(1)}, bf16[2,16,512]{2,1,0:T(8,128)(2,1)S(1)}, u32[]{:S(2)}, u32[]{:S(2)}) collective-permute-start(bf16[2,16,512]{2,1,0:T(8,128)(2,1)S(1)} %get-tuple-element.50), channel_id=1, source_target_pairs={{0,1},{1,2},{2,3},{3,4},{4,5},{5,6},{6,7},{8,9},{9,10},{10,11},{11... | collective-permute-start | bytes 98312 | tf_op jit(solution)/shard_map/ppermute | solution.py:358
  113.4 1.6 %collective-permute-done.2.before = bf16[2,16,512]{2,1,0:T(8,128)(2,1)S(1)} collective-permute-done((bf16[2,16,512]{2,1,0:T(8,128)(2,1)S(1)}, bf16[2,16,512]{2,1,0:T(8,128)(2,1)S(1)}, u32[]{:S(2)}, u32[]{:S(2)}) %collective-permute-start.2) | collective-permute-done | bytes 32800 | tf_op jit(solution)/shard_map/ppermute | solution.py:358
  115.0 0.6 copy-done.14
  115.6 3.5 %shard_map.127 = (bf16[2,128,512]{2,1,0:T(8,128)(2,1)}, bf16[2,128,512]{2,1,0:T(8,128)(2,1)}) custom-call(bf16[4,2,2,32,512]{4,3,2,1,0:T(8,128)(2,1)} %copy-done.1, bf16[2,16,512]{2,1,0:T(8,128)(2,1)} %copy-done.14, bf16[2,16,512]{2,1,0:T(8,128)(2,1)} %copy-done.13, bf16[2,128,512]{2,1,0:T(8,128)(2,1)} %cot.1, f32[31,512]{1,0:T(8,128)} %kern.3), custom_call_target="tpu_custom_call" | custom-call | tf_op jit(solution)/shard_map/pallas_call | solution.py:275
  119.2 0.8 copy-done.5
  120.0 0.8 copy-done.6
  120.8 4.2 %shard_map.132 = (f32[31,512]{1,0:T(8,128)}, f32[512,512]{1,0:T(8,128)}, f32[512,512]{1,0:T(8,128)}, f32[512,512]{1,0:T(8,128)}, f32[512,512]{1,0:T(8,128)}) custom-call(s32[4]{0:T(128)} %pad_add_fusion.bits, bf16[2,2,2,272,128]{4,3,2,1,0:T(8,128)(2,1)} %copy-done.2, bf16[2,2,2,272,128]{4,3,2,1,0:T(8,128)(2,1)} %copy-done.3, ...), custom_call_target="tpu_custom_call" | custom-call | tf_op jit(solution)/shard_map/pallas_call | solution.py:275
  (41 shorter events, 1.7 us)
Async XLA Ops:
  14.6 5.3 %copy-start = (bf16[4,2,2,32,512]{4,3,2,1,0:T(8,128)(2,1)}, bf16[4,2,2,32,512]{4,3,2,1,0:T(8,128)(2,1)S(1)}, u32[]{:S(2)}) copy-start(bf16[4,2,2,32,512]{4,3,2,1,0:T(8,128)(2,1)S(1)} %all_to_all.10.got) | copy-start | bytes 1572868
  14.7 5.0 %collective-permute-start.1 = (bf16[4,2,16,512]{3,2,1,0:T(8,128)(2,1)S(1)}, bf16[4,2,16,512]{3,2,1,0:T(8,128)(2,1)S(1)}, u32[]{:S(2)}, u32[]{:S(2)}) collective-permute-start(bf16[4,2,16,512]{3,2,1,0:T(8,128)(2,1)S(1)} %get-tuple-element.51), channel_id=1, source_target_pairs={{8,0},{16,8},{24,16},{1,24},{9,1},{17,9},{25,17},{2,25},{10,2},{18... | collective-permute-start | bytes 393224 | tf_op jit(solution)/shard_map/ppermute | solution.py:307
  16.0 4.0 %collective-permute-start = (bf16[4,2,16,512]{3,2,1,0:T(8,128)(2,1)S(1)}, bf16[4,2,16,512]{3,2,1,0:T(8,128)(2,1)S(1)}, u32[]{:S(2)}, u32[]{:S(2)}) collective-permute-start(bf16[4,2,16,512]{3,2,1,0:T(8,128)(2,1)S(1)} %get-tuple-element.52), channel_id=1, source_target_pairs={{0,8},{8,16},{16,24},{24,1},{1,9},{9,17},{17,25},{25,2},{2,10},{10... | collective-permute-start | bytes 393224 | tf_op jit(solution)/shard_map/ppermute | solution.py:306
  19.7 0.7 copy-start.11
  20.3 0.7 copy-start.12
  33.6 3.9 %collective-permute-start.4 = (bf16[2,2,2,2,272,128]{5,4,3,2,1,0:T(8,128)(2,1)}, bf16[2,2,2,2,272,128]{5,4,3,2,1,0:T(8,128)(2,1)S(1)}, u32[]{:S(2)}, u32[]{:S(2)}) collective-permute-start(bf16[2,2,2,2,272,128]{5,4,3,2,1,0:T(8,128)(2,1)} %get-tuple-element.31), channel_id=1, source_target_pairs={{0,8},{1,9},{2,10},{3,11},{4,12},{5,13},{6,14},{7,15},{8,0},{9,1},... | collective-permute-start | bytes 3342344 | tf_op jit(solution)/shard_map/ppermute | solution.py:314
  37.5 1.0 copy-start.4
  41.2 11.2 %collective-permute-start.5 = (bf16[2,2,272,128]{3,2,1,0:T(8,128)(2,1)}, bf16[2,2,272,128]{3,2,1,0:T(8,128)(2,1)S(1)}, u32[]{:S(2)}, u32[]{:S(2)}) collective-permute-start(bf16[2,2,272,128]{3,2,1,0:T(8,128)(2,1)} %get-tuple-element.33), channel_id=1, source_target_pairs={{0,1},{1,0},{2,3},{3,2},{4,5},{5,4},{6,7},{7,6},{8,9},{9,8},{10,11... | collective-permute-start | bytes 835592 | tf_op jit(solution)/shard_map/ppermute | solution.py:314
  45.2 10.5 %collective-permute-start.7 = (bf16[2,2,272,128]{3,2,1,0:T(8,128)(2,1)}, bf16[2,2,272,128]{3,2,1,0:T(8,128)(2,1)S(1)}, u32[]{:S(2)}, u32[]{:S(2)}) collective-permute-start(bf16[2,2,272,128]{3,2,1,0:T(8,128)(2,1)} %get-tuple-element.37), channel_id=1, source_target_pairs={{0,16},{1,17},{2,18},{3,19},{4,20},{5,21},{6,22},{7,23},{8,24},{9,... | collective-permute-start | bytes 835592 | tf_op jit(solution)/shard_map/ppermute | solution.py:314
  52.4 0.7 copy-start.8
  54.9 5.4 %collective-permute-start.6 = (bf16[2,272,128]{2,1,0:T(8,128)(2,1)}, bf16[2,272,128]{2,1,0:T(8,128)(2,1)S(1)}, u32[]{:S(2)}, u32[]{:S(2)}) collective-permute-start(bf16[2,272,128]{2,1,0:T(8,128)(2,1)} %get-tuple-element.35), channel_id=1, source_target_pairs={{0,16},{1,17},{2,18},{3,19},{4,20},{5,21},{6,22},{7,23},{8,24},{9,... | collective-permute-start | bytes 417800 | tf_op jit(solution)/shard_map/ppermute | solution.py:314
  55.7 0.7 copy-start.7
  58.2 5.3 %collective-permute-start.8 = (bf16[2,272,128]{2,1,0:T(8,128)(2,1)}, bf16[2,272,128]{2,1,0:T(8,128)(2,1)S(1)}, u32[]{:S(2)}, u32[]{:S(2)}) collective-permute-start(bf16[2,272,128]{2,1,0:T(8,128)(2,1)} %get-tuple-element.39), channel_id=1, source_target_pairs={{0,1},{1,0},{2,3},{3,2},{4,5},{5,4},{6,7},{7,6},{8,9},{9,8},{10,11... | collective-permute-start | bytes 417800 | tf_op jit(solution)/shard_map/ppermute | solution.py:314
  60.3 3.2 %copy-start.9 = (bf16[2,272,128]{2,1,0:T(8,128)(2,1)}, bf16[2,272,128]{2,1,0:T(8,128)(2,1)S(1)}, u32[]{:S(2)}) copy-start(bf16[2,272,128]{2,1,0:T(8,128)(2,1)S(1)} %collective-permute-done.6.a_got) | copy-start | bytes 417796
  63.5 0.7 copy-start.10
  66.0 5.8 %collective-permute-start.9 = (bf16[2,272,128]{2,1,0:T(8,128)(2,1)}, bf16[2,272,128]{2,1,0:T(8,128)(2,1)S(1)}, u32[]{:S(2)}, u32[]{:S(2)}) collective-permute-start(bf16[2,272,128]{2,1,0:T(8,128)(2,1)} %get-tuple-element.41), channel_id=1, source_target_pairs={{0,2},{1,3},{2,0},{3,1},{4,6},{5,7},{6,4},{7,5},{8,10},{9,11},{10,... | collective-permute-start | bytes 417800 | tf_op jit(solution)/shard_map/ppermute | solution.py:314
  72.8 7.7 %collective-permute-start.10 = (bf16[2,272,128]{2,1,0:T(8,128)(2,1)S(1)}, bf16[2,272,128]{2,1,0:T(8,128)(2,1)S(1)}, u32[]{:S(2)}, u32[]{:S(2)}) collective-permute-start(bf16[2,272,128]{2,1,0:T(8,128)(2,1)S(1)} %add_convert_fusion.1), channel_id=1, source_target_pairs={{0,4},{1,5},{2,6},{3,7},{4,0},{5,1},{6,2},{7,3},{8,12},{9,13},{10,... | collective-permute-start | bytes 417800 | tf_op jit(solution)/shard_map/ppermute | solution.py:314
  80.6 5.1 %collective-permute-start.11 = (bf16[2,272,128]{2,1,0:T(8,128)(2,1)S(1)}, bf16[2,272,128]{2,1,0:T(8,128)(2,1)S(1)}, u32[]{:S(2)}, u32[]{:S(2)}) collective-permute-start(bf16[2,272,128]{2,1,0:T(8,128)(2,1)S(1)} %add_convert_fusion), channel_id=1, source_target_pairs={{0,2},{1,3},{2,0},{3,1},{4,6},{5,7},{6,4},{7,5},{8,10},{9,11},{10,... | collective-permute-start | bytes 417800 | tf_op jit(solution)/shard_map/ppermute | solution.py:314
  85.7 6.6 %collective-permute-start.12 = (bf16[2,272,128]{2,1,0:T(8,128)(2,1)S(1)}, bf16[2,272,128]{2,1,0:T(8,128)(2,1)S(1)}, u32[]{:S(2)}, u32[]{:S(2)}) collective-permute-start(bf16[2,272,128]{2,1,0:T(8,128)(2,1)S(1)} %get-tuple-element.53), channel_id=1, source_target_pairs={{0,16},{1,17},{2,18},{3,19},{4,20},{5,21},{6,22},{7,23},{8,24},{9,... | collective-permute-start | bytes 417800 | tf_op jit(solution)/shard_map/ppermute | solution.py:314
  87.8 5.7 %collective-permute-start.13 = (bf16[2,272,128]{2,1,0:T(8,128)(2,1)S(1)}, bf16[2,272,128]{2,1,0:T(8,128)(2,1)S(1)}, u32[]{:S(2)}, u32[]{:S(2)}) collective-permute-start(bf16[2,272,128]{2,1,0:T(8,128)(2,1)S(1)} %get-tuple-element.54), channel_id=1, source_target_pairs={{0,1},{1,0},{2,3},{3,2},{4,5},{5,4},{6,7},{7,6},{8,9},{9,8},{10,11... | collective-permute-start | bytes 417800 | tf_op jit(solution)/shard_map/ppermute | solution.py:314
  93.6 6.6 %collective-permute-start.14 = (bf16[2,2,272,128]{3,2,1,0:T(8,128)(2,1)S(1)}, bf16[2,2,272,128]{3,2,1,0:T(8,128)(2,1)S(1)}, u32[]{:S(2)}, u32[]{:S(2)}) collective-permute-start(bf16[2,2,272,128]{3,2,1,0:T(8,128)(2,1)S(1)} %get-tuple-element.47), channel_id=1, source_target_pairs={{0,1},{1,0},{2,3},{3,2},{4,5},{5,4},{6,7},{7,6},{8,9},{9,8},{10,11... | collective-permute-start | bytes 835592 | tf_op jit(solution)/shard_map/ppermute | solution.py:314
  94.3 6.5 %collective-permute-start.15 = (bf16[2,2,272,128]{3,2,1,0:T(8,128)(2,1)S(1)}, bf16[2,2,272,128]{3,2,1,0:T(8,128)(2,1)S(1)}, u32[]{:S(2)}, u32[]{:S(2)}) collective-permute-start(bf16[2,2,272,128]{3,2,1,0:T(8,128)(2,1)S(1)} %get-tuple-element.48), channel_id=1, source_target_pairs={{0,16},{1,17},{2,18},{3,19},{4,20},{5,21},{6,22},{7,23},{8,24},{9,... | collective-permute-start | bytes 835592 | tf_op jit(solution)/shard_map/ppermute | solution.py:314
  95.2 12.3 %all-to-all-start.1 = ((bf16[4,2,2,32,512]{4,3,2,1,0:T(8,128)(2,1)}), bf16[4,2,2,32,512]{4,3,2,1,0:T(8,128)(2,1)S(1)}, u32[]{:S(2)}, u32[]{:S(2)}) async-start(bf16[4,2,2,32,512]{4,3,2,1,0:T(8,128)(2,1)} %get-tuple-element.27), calls=%async_computation.1 | async-start | bytes 1048576 | tf_op jit(solution)/shard_map/all_to_all | solution.py:355
  98.8 20.4 %copy-start.2 = (bf16[2,2,2,272,128]{4,3,2,1,0:T(8,128)(2,1)}, bf16[2,2,2,272,128]{4,3,2,1,0:T(8,128)(2,1)S(1)}, u32[]{:S(2)}) copy-start(bf16[2,2,2,272,128]{4,3,2,1,0:T(8,128)(2,1)S(1)} %pad_maximum_fusion.own) | copy-start | bytes 1671172
  98.8 20.3 %collective-permute-start.16 = (bf16[2,2,2,272,128]{4,3,2,1,0:T(8,128)(2,1)S(1)}, bf16[2,2,2,272,128]{4,3,2,1,0:T(8,128)(2,1)S(1)}, u32[]{:S(2)}, u32[]{:S(2)}) collective-permute-start(bf16[2,2,2,272,128]{4,3,2,1,0:T(8,128)(2,1)S(1)} %pad_maximum_fusion.own), channel_id=1, source_target_pairs={{0,8},{1,9},{2,10},{3,11},{4,12},{5,13},{6,14},{7,15},{8,0},{9,1},... | collective-permute-start | bytes 1671176 | tf_op jit(solution)/shard_map/ppermute | solution.py:314
  100.9 18.3 %copy-start.3 = (bf16[2,2,2,272,128]{4,3,2,1,0:T(8,128)(2,1)}, bf16[2,2,2,272,128]{4,3,2,1,0:T(8,128)(2,1)S(1)}, u32[]{:S(2)}) copy-start(bf16[2,2,2,272,128]{4,3,2,1,0:T(8,128)(2,1)S(1)} %pad_maximum_fusion.1.far) | copy-start | bytes 1671172
  100.9 18.2 %collective-permute-start.17 = (bf16[2,2,2,272,128]{4,3,2,1,0:T(8,128)(2,1)S(1)}, bf16[2,2,2,272,128]{4,3,2,1,0:T(8,128)(2,1)S(1)}, u32[]{:S(2)}, u32[]{:S(2)}) collective-permute-start(bf16[2,2,2,272,128]{4,3,2,1,0:T(8,128)(2,1)S(1)} %pad_maximum_fusion.1.far), channel_id=1, source_target_pairs={{0,8},{1,9},{2,10},{3,11},{4,12},{5,13},{6,14},{7,15},{8,0},{9,1},... | collective-permute-start | bytes 1671176 | tf_op jit(solution)/shard_map/ppermute | solution.py:314
  107.5 7.4 %copy-start.1 = (bf16[4,2,2,32,512]{4,3,2,1,0:T(8,128)(2,1)}, bf16[4,2,2,32,512]{4,3,2,1,0:T(8,128)(2,1)S(1)}, u32[]{:S(2)}) copy-start(bf16[4,2,2,32,512]{4,3,2,1,0:T(8,128)(2,1)S(1)} %all-to-all-done.1.got) | copy-start | bytes 1572868
  107.5 5.9 %collective-permute-start.3 = (bf16[2,16,512]{2,1,0:T(8,128)(2,1)S(1)}, bf16[2,16,512]{2,1,0:T(8,128)(2,1)S(1)}, u32[]{:S(2)}, u32[]{:S(2)}) collective-permute-start(bf16[2,16,512]{2,1,0:T(8,128)(2,1)S(1)} %get-tuple-element.49), channel_id=1, source_target_pairs={{1,0},{2,1},{3,2},{4,3},{5,4},{6,5},{7,6},{9,8},{10,9},{11,10},{12... | collective-permute-start | bytes 98312 | tf_op jit(solution)/shard_map/ppermute | solution.py:359
  108.8 6.1 %collective-permute-start.2 = (bf16[2,16,512]{2,1,0:T(8,128)(2,1)S(1)}, bf16[2,16,512]{2,1,0:T(8,128)(2,1)S(1)}, u32[]{:S(2)}, u32[]{:S(2)}) collective-permute-start(bf16[2,16,512]{2,1,0:T(8,128)(2,1)S(1)} %get-tuple-element.50), channel_id=1, source_target_pairs={{0,1},{1,2},{2,3},{3,4},{4,5},{5,6},{6,7},{8,9},{9,10},{10,11},{11... | collective-permute-start | bytes 98312 | tf_op jit(solution)/shard_map/ppermute | solution.py:358
  113.4 1.6 %copy-start.13 = (bf16[2,16,512]{2,1,0:T(8,128)(2,1)}, bf16[2,16,512]{2,1,0:T(8,128)(2,1)S(1)}, u32[]{:S(2)}) copy-start(bf16[2,16,512]{2,1,0:T(8,128)(2,1)S(1)} %collective-permute-done.3.after) | copy-start | bytes 98308
  115.0 0.6 copy-start.14
  119.1 0.8 copy-start.5
  120.0 0.8 copy-start.6

commit v3 on v2

--- a/solution.py
+++ b/solution.py
@@ -15,7 +15,7 @@
 TN = (((0,), (0,)), ((), ()))
 BF = jnp.bfloat16
 F32 = jnp.float32
-VMEM_LIMIT = 56 * 1024 * 1024
+MIB = 1024 * 1024
 
 
 def mm(left, right, dims=(((1,), (0,)), ((), ()))):
@@ -188,28 +188,14 @@
                 out[h, piece // 4, piece // 2 % 2, piece % 2, size : size + HALO, :] = tail.astype(BF)
 
 
-def add(left, right):
-    return (left.astype(F32) + right.astype(F32)).astype(BF)
-
-
-def split_core(bits, keep, got, a_keep, a_send, b_keep, b_send):
-    y, x = bits[1], bits[2]
-    for h, bit, mine, theirs in ((0, x, a_keep, a_send), (1, y, b_keep, b_send)):
-        theirs[...] = add(keep[h, 1 - bit], got[h, 1 - bit])
-        mine[...] = add(keep[h, bit], got[h, bit])
-
-
-def split_plane(which, bits, keep, got, mine, theirs):
-    bit = bits[which]
-    theirs[...] = add(keep[1 - bit], got[1 - bit])
-    mine[...] = add(keep[bit], got[bit])
-
-
-def split_line(bits, a_keep, a_got, b_keep, b_got, mine, theirs):
-    bit = bits[3]
-    for h, keep, got in ((0, a_keep, a_got), (1, b_keep, b_got)):
-        theirs[h] = add(keep[1 - bit], got[1 - bit])
-        mine[h] = add(keep[bit], got[bit])
+def at(x, *where):
+    for i in where:
+        x = lax.dynamic_index_in_dim(x, i, 0, keepdims=False)
+    return x
+
+
+def total(*parts):
+    return functools.reduce(lambda x, y: x + y, [x.astype(F32) for x in parts]).astype(BF)
 
 
 def final_kernel(plan, bits, own, far, other_own, other_far, taps, *refs):
@@ -271,7 +257,7 @@
     lax.fori_loop(0, count, step, 0)
 
 
-def call(body, outs, scratch, *args):
+def call(body, outs, scratch, limit, *args):
     return pl.pallas_call(
         body,
         out_shape=outs,
@@ -281,7 +267,7 @@
         ],
         out_specs=jax.tree.map(lambda _: pl.BlockSpec(memory_space=pltpu.VMEM), outs),
         scratch_shapes=scratch,
-        compiler_params=pltpu.CompilerParams(vmem_limit_bytes=VMEM_LIMIT),
+        compiler_params=pltpu.CompilerParams(vmem_limit_bytes=limit * MIB),
     )(*args)
 
 
@@ -325,50 +311,55 @@
             wide, pltpu.VMEM((2, rows, width), BF), pltpu.VMEM((4, rows, width), BF),
             big, big, big, big, wide, pltpu.VMEM((32 * width // LANES + HALO, LANES), F32),
         ],
-        bits, got, before, after, kernel, w_query, w_key, w_value, w_out,
+        24, bits, got, before, after, kernel, w_query, w_key, w_value, w_out,
     )
 
-    quarter, eighth, pair = (shape((*lead, *piece), BF) for lead in ((2, 2), (2,), (2,)))
-    a_keep, a_send, b_keep, b_send = call(
-        split_core, (quarter,) * 4, [], bits, keep, swap(send, over_core)
+    core_got = swap(send, over_core)
+    home = lax.all_to_all(back, "mic", 0, 0, tiled=True)
+    y, x, z = bits[1], bits[2], bits[3]
+    a, b = [keep[0], core_got[0]], [keep[1], core_got[1]]
+    a_got = swap(total(*(at(t, 1 - x) for t in a)), over_x)
+    b_got = swap(total(*(at(t, 1 - y) for t in b)), over_y)
+    a, b = [at(t, x) for t in a] + [a_got], [at(t, y) for t in b] + [b_got]
+    a_got = swap(total(*(at(t, 1 - y) for t in a)), over_y)
+    b_got = swap(total(*(at(t, 1 - x) for t in b)), over_x)
+    a, b = [at(t, y) for t in a] + [a_got], [at(t, x) for t in b] + [b_got]
+    theirs = jnp.stack([total(*(at(t, 1 - z) for t in h)) for h in (a, b)])
+    theirs, home = lax.optimization_barrier((theirs, home))
+    z_got = swap(theirs, over_z)
+    mine = jnp.stack(
+        [total(*(at(t, z) for t in h), z_got[i]) for i, h in enumerate((a, b))]
     )
-    a_got, b_got = swap(a_send, over_x), swap(b_send, over_y)
-    a_keep, a_send = call(
-        functools.partial(split_plane, 1), (eighth,) * 2, [], bits, a_keep, a_got
-    )
-    b_keep, b_send = call(
-        functools.partial(split_plane, 2), (eighth,) * 2, [], bits, b_keep, b_got
-    )
-    a_got, b_got = swap(a_send, over_y), swap(b_send, over_x)
-    mine, theirs = call(split_line, (pair,) * 2, [], bits, a_keep, a_got, b_keep, b_got)
-    mine = add(mine, swap(theirs, over_z))
     mask = 2 * over_z
     while mask < blocks:
-        mine = add(mine, swap(mine, mask))
+        mine = total(mine, swap(mine, mask))
         mask *= 2
-    line = jnp.stack([mine, swap(mine, over_z)], axis=1)
-    plane = jnp.stack([line, jnp.stack([swap(line[0], over_y), swap(line[1], over_x)])], axis=1)
-    other_plane = swap(plane, over_core)
-    far = jnp.stack([swap(plane[0], over_x), swap(plane[1], over_y)])
-    other_far = swap(far, over_core)
-
-    home = lax.all_to_all(back, "mic", 0, 0, tiled=True)
+
     up = [(i, i + 1) for i in range(blocks - 1)]
     down = [(j, i) for i, j in up]
     before = lax.ppermute(home[groups - 1, 1, :, sub - HALO :, :], "tm", up)
     after = lax.ppermute(home[0, 1, :, :HALO, :], "tm", down)
+
+    line = jnp.stack([mine, swap(mine, over_z)], axis=1)
+    line, before, after = lax.optimization_barrier((line, before, after))
     layer_out, frame_grad = call(
         functools.partial(frame_kernel, (groups, count, sub, width)),
         (shape((count, length, width), BF), shape((count, length, width), BF)),
-        [], home, before, after, cotangent, kernel,
+        [], 12, home, before, after, cotangent, kernel,
     )
+    plane = jnp.stack([line, jnp.stack([swap(line[0], over_y), swap(line[1], over_x)])], axis=1)
+    other_plane = swap(plane, over_core)
+    far = jnp.stack([swap(plane[0], over_x), swap(plane[1], over_y)])
+    far, layer_out, frame_grad = lax.optimization_barrier((far, layer_out, frame_grad))
+    other_far = swap(far, over_core)
+
     norm = 1.0 / math.sqrt(groups * count * blocks * length)
     square = shape((width, width), F32)
     grads = call(
         functools.partial(final_kernel, (width, norm)),
         (shape((31, width), F32), square, square, square, square),
         [pltpu.VMEM((32, HALO, LANES), F32)],
-        bits, plane, far, other_plane, other_far,
+        16, bits, plane, far, other_plane, other_far,
     )
     return (layer_out, frame_grad, *grads)
 

time: 126 us -> 102 us (0.81)
  waiting for transfers between devices: 39.8 us -> 25 us
  Pallas kernels: 28.5 us -> 16.8 us
  local copies, waits for them, and re-layouts: 6.37 us -> 2.53 us
  starting transfers between devices: 33.7 us -> 37.5 us
  other arithmetic: 2.9 us -> 6.1 us
    pallas_call x7 -> x3, Pallas kernels: 28.5 us -> 16.8 us  [call(): pl.pallas_call(body, out_shape=outs, in_specs=[pl.BlockSpec(memory_space=...]
    ppermute x14, waiting for transfers between devices: 31.3 us -> 24.1 us  [swap(): lax.ppermute(x, ('mic', 'tm'), [(f, f ^ mask) for f in range(groups * blo...]
    all_to_all x1, waiting for transfers between devices: 6.56 us -> 0.01 us  [shards(): home = lax.all_to_all(back, 'mic', 0, 0, tiled=True)]
    unnamed x30 -> x12, local copies, waits for them, and re-layouts: 6.31 us -> 1.07 us
    ppermute x14, starting transfers between devices: 20 us -> 23.8 us  [swap(): lax.ppermute(x, ('mic', 'tm'), [(f, f ^ mask) for f in range(groups * blo...]
    convert_element_type x2 -> x8, other arithmetic: 0.99 us -> 4.66 us  [total(): functools.reduce(lambda x, y: x + y, [x.astype(F32) for x in parts])]
    ppermute x1, waiting for transfers between devices: 1.56 us -> 0.01 us  [shards(): before = lax.ppermute(home[groups - 1, 1, :, sub - HALO:, :], 'tm', up)]
    slice x0 -> x2, local copies, waits for them, and re-layouts: none -> 1.38 us  [shards(): a, b = ([keep[0], core_got[0]], [keep[1], core_got[1]])]
  transfers between devices with their start and end apart: 19 -> 19, of which waited for: 14 -> 13; matrix products, arithmetic and copies ran while one was open for 1% -> 3% of each run, Pallas kernels for 6% -> 2%
where the time goes in v3:
time: 102 us
  starting transfers between devices  37.5 us (37%)
  waiting for transfers between devices  25 us (25%)
  Pallas kernels  16.8 us (16%)
  blocking collectives  13 us (13%)
  other arithmetic  6.1 us (6%)
  local copies, waits for them, and re-layouts  2.53 us (2%)
    ppermute x14, waiting for transfers between devices, swap(): lax.ppermute(x, ('mic', 'tm'), [(f, f ^ mask) for f in range(groups * blo...  24.1 us
    ppermute x14, starting transfers between devices, swap(): lax.ppermute(x, ('mic', 'tm'), [(f, f ^ mask) for f in range(groups * blo...  23.8 us
    pallas_call x3, Pallas kernels, call(): pl.pallas_call(body, out_shape=outs, in_specs=[pl.BlockSpec(memory_space=...  16.8 us
    all_to_all x1, blocking collectives, shards(): got = lax.all_to_all(send.transpose(2, 0, 1, 3, 4), 'mic', 0, 0, tiled=True)  13 us
    convert_element_type x8, other arithmetic, total(): functools.reduce(lambda x, y: x + y, [x.astype(F32) for x in parts])  4.66 us
    ppermute x1, starting transfers between devices, shards(): before = lax.ppermute(home[groups - 1, 1, :, sub - HALO:, :], 'tm', up)  4.55 us
    all_to_all x1, starting transfers between devices, shards(): home = lax.all_to_all(back, 'mic', 0, 0, tiled=True)  3.47 us
    ppermute x1, starting transfers between devices, shards(): before = lax.ppermute(got[:, 0, :, sub - HALO:, :], ('mic', 'tm'), up)  3.04 us
  transfers between devices with their start and end apart: 19, of which 13 were waited for; matrix products, arithmetic and copies ran while one was open for 3% of the time, Pallas kernels for 2%

profile of v3, /device:TPU:0, one launch (start us, length us, event | category | flops | bytes accessed | tf_op | source)
XLA Modules:
  0.0 101.8 jit_solution(1243270846583157727)
XLA Ops:
  0.6 1.1 %maximum_bitcast_fusion = bf16[4,2,2,32,512]{4,3,0,2,1:T(8,128)(2,1)S(1)} fusion(bf16[1,2,4,32,512]{4,3,2,1,0:T(8,128)(2,1)} %bitcast.76, bf16[1,2,4,32,512]{4,3,2,1,0:T(8,128)(2,1)} %bitcast.81), kind=kLoop, calls=%fused_computation.8 | loop fusion | flops 262144 | bytes 1048576 | tf_op jit(solution)/shard_map/transpose | solution.py:289
  1.8 13.0 %all_to_all.10.got = bf16[4,2,2,32,512]{4,3,2,1,0:T(8,128)(2,1)S(1)} all-to-all(bf16[4,2,2,32,512]{4,3,2,1,0:T(8,128)(2,1)S(1)} %copy.22), channel_id=1, replica_groups=mesh['mic'=4,'tm'=8] {'mic'}, dimensions={0} | all-to-all | bytes 1048576 | tf_op jit(solution)/shard_map/all_to_all | solution.py:289
  14.8 1.3 %collective-permute-start.1 = (bf16[4,2,16,512]{3,2,1,0:T(8,128)(2,1)S(1)}, bf16[4,2,16,512]{3,2,1,0:T(8,128)(2,1)S(1)}, u32[]{:S(2)}, u32[]{:S(2)}) collective-permute-start(bf16[4,2,16,512]{3,2,1,0:T(8,128)(2,1)S(1)} %get-tuple-element.51), channel_id=1, source_target_pairs={{8,0},{16,8},{24,16},{1,24},{9,1},{17,9},{25,17},{2,25},{10,2},{18... | collective-permute-start | bytes 393224 | tf_op jit(solution)/shard_map/ppermute | solution.py:293
  16.1 3.0 %collective-permute-start = (bf16[4,2,16,512]{3,2,1,0:T(8,128)(2,1)S(1)}, bf16[4,2,16,512]{3,2,1,0:T(8,128)(2,1)S(1)}, u32[]{:S(2)}, u32[]{:S(2)}) collective-permute-start(bf16[4,2,16,512]{3,2,1,0:T(8,128)(2,1)S(1)} %get-tuple-element.52), channel_id=1, source_target_pairs={{0,8},{8,16},{16,24},{24,1},{1,9},{9,17},{17,25},{25,2},{2,10},{10... | collective-permute-start | bytes 393224 | tf_op jit(solution)/shard_map/ppermute | solution.py:292
  19.2 0.1 pad_add_fusion.bits
  19.3 0.8 collective-permute-done.before
  20.2 1.0 %copy-done.4 = bf16[512,512]{1,0:T(8,128)(2,1)S(1)} copy-done((bf16[512,512]{1,0:T(8,128)(2,1)S(1)}, bf16[512,512]{1,0:T(8,128)(2,1)}, u32[]{:S(2)}) %copy-start.4) | copy-done | bytes 524312
  21.2 11.1 %shard_map.126 = (bf16[4,2,2,32,512]{4,3,2,1,0:T(8,128)(2,1)}, bf16[2,2,2,2,272,128]{5,4,3,2,1,0:T(8,128)(2,1)S(1)}, bf16[2,2,2,2,272,128]{5,4,3,2,1,0:T(8,128)(2,1)}) custom-call(s32[4]{0:T(128)S(1)} %pad_add_fusion.bits, bf16[4,2,2,32,512]{4,3,2,1,0:T(8,128)(2,1)S(1)} %all_to_all.10.got, bf16[4,2,16,512]{3,2,1,0:T(8,128)(2,1)S(1)} %collective-permute-done.before, ...), custom_call_target="tpu_custom_call" | custom-call | tf_op jit(solution)/shard_map/pallas_call | solution.py:261
  32.3 1.7 %collective-permute-start.2 = (bf16[2,2,2,2,272,128]{5,4,3,2,1,0:T(8,128)(2,1)}, bf16[2,2,2,2,272,128]{5,4,3,2,1,0:T(8,128)(2,1)}, u32[]{:S(2)}, u32[]{:S(2)}) collective-permute-start(bf16[2,2,2,2,272,128]{5,4,3,2,1,0:T(8,128)(2,1)} %get-tuple-element.26), channel_id=1, source_target_pairs={{0,8},{1,9},{2,10},{3,11},{4,12},{5,13},{6,14},{7,15},{8,0},{9,1},... | collective-permute-start | bytes 3342344 | tf_op jit(solution)/shard_map/ppermute | solution.py:300
  33.9 0.1 fusion.18
  34.0 2.6 %collective-permute-done.2 = bf16[2,2,2,2,272,128]{5,4,3,2,1,0:T(8,128)(2,1)} collective-permute-done((bf16[2,2,2,2,272,128]{5,4,3,2,1,0:T(8,128)(2,1)}, bf16[2,2,2,2,272,128]{5,4,3,2,1,0:T(8,128)(2,1)}, u32[]{:S(2)}, u32[]{:S(2)}) %collective-permute-start.2) | collective-permute-done | bytes 1114144 | tf_op jit(solution)/shard_map/ppermute | solution.py:300
  36.7 1.3 %fusion.19 = (bf16[1,2,2,2,272,128]{5,4,3,2,1,0:T(8,128)(2,1)S(1)}, bf16[1,2,2,2,272,128]{5,4,3,2,1,0:T(8,128)(2,1)S(1)}) fusion(bf16[2,2,2,2,272,128]{5,4,3,2,1,0:T(8,128)(2,1)} %collective-permute-done.2), kind=kLoop, calls=%fused_computation.46 | loop fusion | bytes 2228224 | tf_op jit(solution)/shard_map/slice | solution.py:320
  38.0 0.8 fusion.1
  38.8 2.7 %collective-permute-start.5 = (bf16[2,2,272,128]{3,2,1,0:T(8,128)(2,1)}, bf16[2,2,272,128]{3,2,1,0:T(8,128)(2,1)S(1)}, u32[]{:S(2)}, u32[]{:S(2)}) collective-permute-start(bf16[2,2,272,128]{3,2,1,0:T(8,128)(2,1)} %fusion.1), channel_id=1, source_target_pairs={{0,16},{1,17},{2,18},{3,19},{4,20},{5,21},{6,22},{7,23},{8,24},{9,... | collective-permute-start | bytes 835592 | tf_op jit(solution)/shard_map/ppermute | solution.py:300
  41.5 0.8 fusion
  42.3 2.1 %collective-permute-start.3 = (bf16[2,2,272,128]{3,2,1,0:T(8,128)(2,1)}, bf16[2,2,272,128]{3,2,1,0:T(8,128)(2,1)}, u32[]{:S(2)}, u32[]{:S(2)}) collective-permute-start(bf16[2,2,272,128]{3,2,1,0:T(8,128)(2,1)} %fusion), channel_id=1, source_target_pairs={{0,1},{1,0},{2,3},{3,2},{4,5},{5,4},{6,7},{7,6},{8,9},{9,8},{10,11... | collective-permute-start | bytes 835592 | tf_op jit(solution)/shard_map/ppermute | solution.py:300
  44.4 3.5 %all-to-all-start.1 = ((bf16[4,2,2,32,512]{4,3,2,1,0:T(8,128)(2,1)}), bf16[4,2,2,32,512]{4,3,2,1,0:T(8,128)(2,1)S(1)}, u32[]{:S(2)}, u32[]{:S(2)}) async-start(bf16[4,2,2,32,512]{4,3,2,1,0:T(8,128)(2,1)} %get-tuple-element.27), calls=%async_computation.1 | async-start | bytes 1048576 | tf_op jit(solution)/shard_map/all_to_all | solution.py:318
  47.9 0.8 collective-permute-done.5
  48.7 0.1 fusion.6
  48.7 3.7 %collective-permute-start.6 = (bf16[2,272,128]{2,1,0:T(8,128)(2,1)S(1)}, bf16[2,272,128]{2,1,0:T(8,128)(2,1)S(1)}, u32[]{:S(2)}, u32[]{:S(2)}) collective-permute-start(bf16[2,272,128]{2,1,0:T(8,128)(2,1)S(1)} %fusion.6), channel_id=1, source_target_pairs={{0,1},{1,0},{2,3},{3,2},{4,5},{5,4},{6,7},{7,6},{8,9},{9,8},{10,11... | collective-permute-start | bytes 417800 | tf_op jit(solution)/shard_map/ppermute | solution.py:300
  52.4 1.0 fusion.7
  53.3 1.2 %collective-permute-start.4 = (bf16[2,272,128]{2,1,0:T(8,128)(2,1)S(1)}, bf16[2,272,128]{2,1,0:T(8,128)(2,1)}, u32[]{:S(2)}, u32[]{:S(2)}) collective-permute-start(bf16[2,272,128]{2,1,0:T(8,128)(2,1)S(1)} %fusion.7), channel_id=1, source_target_pairs={{0,16},{1,17},{2,18},{3,19},{4,20},{5,21},{6,22},{7,23},{8,24},{9,... | collective-permute-start | bytes 417800 | tf_op jit(solution)/shard_map/ppermute | solution.py:300
  54.5 0.9 collective-permute-done.6
  55.4 4.3 %collective-permute-done.4 = bf16[2,272,128]{2,1,0:T(8,128)(2,1)} collective-permute-done((bf16[2,272,128]{2,1,0:T(8,128)(2,1)S(1)}, bf16[2,272,128]{2,1,0:T(8,128)(2,1)}, u32[]{:S(2)}, u32[]{:S(2)}) %collective-permute-start.4) | collective-permute-done | bytes 139296 | tf_op jit(solution)/shard_map/ppermute | solution.py:300
  59.8 1.0 fusion.14
  60.8 2.4 %collective-permute-start.7 = (bf16[2,272,128]{2,1,0:T(8,128)(2,1)S(1)}, bf16[2,272,128]{2,1,0:T(8,128)(2,1)S(1)}, u32[]{:S(2)}, u32[]{:S(2)}) collective-permute-start(bf16[2,272,128]{2,1,0:T(8,128)(2,1)S(1)} %pad_maximum_fusion.3), channel_id=1, source_target_pairs={{0,2},{1,3},{2,0},{3,1},{4,6},{5,7},{6,4},{7,5},{8,10},{9,11},{10,... | collective-permute-start | bytes 417800 | tf_op jit(solution)/shard_map/ppermute | solution.py:300
  63.1 3.3 %collective-permute-done.7 = bf16[2,272,128]{2,1,0:T(8,128)(2,1)S(1)} collective-permute-done((bf16[2,272,128]{2,1,0:T(8,128)(2,1)S(1)}, bf16[2,272,128]{2,1,0:T(8,128)(2,1)S(1)}, u32[]{:S(2)}, u32[]{:S(2)}) %collective-permute-start.7) | collective-permute-done | bytes 139296 | tf_op jit(solution)/shard_map/ppermute | solution.py:300
  66.4 1.0 %fusion.17 = (bf16[1,272,128]{2,1,0:T(8,128)(2,1)S(1)}, bf16[1,272,128]{2,1,0:T(8,128)(2,1)S(1)}) fusion(bf16[2,272,128]{2,1,0:T(8,128)(2,1)S(1)} %collective-permute-done.7, bf16[2,272,128]{2,1,0:T(8,128)(2,1)} %collective-permute-done.4, s32[]{:T(128)S(6)} %select_n.94, bf16[2,2,272,128]{3,2,1,0:T(8,128)(2,1)} %collective-permute-done.3, s32[]{:T(128)S(6)} %select_n.93, ...), kind=kLoop, calls=%fused_computation.37 | loop fusion | flops 696320 | bytes 835600 | tf_op jit(solution)/shard_map/convert_element_type | solution.py:198
  67.5 2.8 %collective-permute-start.8 = (bf16[2,272,128]{2,1,0:T(8,128)(2,1)S(1)}, bf16[2,272,128]{2,1,0:T(8,128)(2,1)S(1)}, u32[]{:S(2)}, u32[]{:S(2)}) collective-permute-start(bf16[2,272,128]{2,1,0:T(8,128)(2,1)S(1)} %pad_maximum_fusion.4), channel_id=1, source_target_pairs={{0,4},{1,5},{2,6},{3,7},{4,0},{5,1},{6,2},{7,3},{8,12},{9,13},{10,... | collective-permute-start | bytes 417800 | tf_op jit(solution)/shard_map/ppermute | solution.py:300
  70.3 1.3 %collective-permute-start.11 = (bf16[2,16,512]{2,1,0:T(8,128)(2,1)S(1)}, bf16[2,16,512]{2,1,0:T(8,128)(2,1)S(1)}, u32[]{:S(2)}, u32[]{:S(2)}) collective-permute-start(bf16[2,16,512]{2,1,0:T(8,128)(2,1)S(1)} %get-tuple-element.49), channel_id=1, source_target_pairs={{1,0},{2,1},{3,2},{4,3},{5,4},{6,5},{7,6},{9,8},{10,9},{11,10},{12... | collective-permute-start | bytes 98312 | tf_op jit(solution)/shard_map/ppermute | solution.py:341
  71.6 4.5 %collective-permute-start.10 = (bf16[2,16,512]{2,1,0:T(8,128)(2,1)S(1)}, bf16[2,16,512]{2,1,0:T(8,128)(2,1)S(1)}, u32[]{:S(2)}, u32[]{:S(2)}) collective-permute-start(bf16[2,16,512]{2,1,0:T(8,128)(2,1)S(1)} %get-tuple-element.50), channel_id=1, source_target_pairs={{0,1},{1,2},{2,3},{3,4},{4,5},{5,6},{6,7},{8,9},{9,10},{10,11},{11... | collective-permute-start | bytes 98312 | tf_op jit(solution)/shard_map/ppermute | solution.py:340
  76.2 0.2 collective-permute-done.8
  76.4 1.5 %collective-permute-start.9 = (bf16[2,272,128]{2,1,0:T(8,128)(2,1)S(1)}, bf16[2,272,128]{2,1,0:T(8,128)(2,1)S(1)}, u32[]{:S(2)}, u32[]{:S(2)}) collective-permute-start(bf16[2,272,128]{2,1,0:T(8,128)(2,1)S(1)} %add_convert_fusion.2), channel_id=1, source_target_pairs={{0,2},{1,3},{2,0},{3,1},{4,6},{5,7},{6,4},{7,5},{8,10},{9,11},{10,... | collective-permute-start | bytes 417800 | tf_op jit(solution)/shard_map/ppermute | solution.py:300
  77.9 3.6 %collective-permute-done.9 = bf16[2,272,128]{2,1,0:T(8,128)(2,1)S(1)} collective-permute-done((bf16[2,272,128]{2,1,0:T(8,128)(2,1)S(1)}, bf16[2,272,128]{2,1,0:T(8,128)(2,1)S(1)}, u32[]{:S(2)}, u32[]{:S(2)}) %collective-permute-start.9) | collective-permute-done | bytes 139296 | tf_op jit(solution)/shard_map/ppermute | solution.py:300
  81.6 0.2 collective-permute-start.12
  81.8 1.6 %collective-permute-start.13 = (bf16[2,272,128]{2,1,0:T(8,128)(2,1)S(1)}, bf16[2,272,128]{2,1,0:T(8,128)(2,1)S(1)}, u32[]{:S(2)}, u32[]{:S(2)}) collective-permute-start(bf16[2,272,128]{2,1,0:T(8,128)(2,1)S(1)} %get-tuple-element.54), channel_id=1, source_target_pairs={{0,1},{1,0},{2,3},{3,2},{4,5},{5,4},{6,7},{7,6},{8,9},{9,8},{10,11... | collective-permute-start | bytes 417800 | tf_op jit(solution)/shard_map/ppermute | solution.py:300
  83.3 3.9 %collective-permute-done.12 = bf16[2,272,128]{2,1,0:T(8,128)(2,1)S(1)} collective-permute-done((bf16[2,272,128]{2,1,0:T(8,128)(2,1)S(1)}, bf16[2,272,128]{2,1,0:T(8,128)(2,1)S(1)}, u32[]{:S(2)}, u32[]{:S(2)}) %collective-permute-start.12) | collective-permute-done | bytes 139296 | tf_op jit(solution)/shard_map/ppermute | solution.py:300
  87.3 0.4 collective-permute-done.13
  87.7 2.3 %collective-permute-start.14 = (bf16[2,2,272,128]{3,2,1,0:T(8,128)(2,1)S(1)}, bf16[2,2,272,128]{3,2,1,0:T(8,128)(2,1)S(1)}, u32[]{:S(2)}, u32[]{:S(2)}) collective-permute-start(bf16[2,2,272,128]{3,2,1,0:T(8,128)(2,1)S(1)} %get-tuple-element.47), channel_id=1, source_target_pairs={{0,1},{1,0},{2,3},{3,2},{4,5},{5,4},{6,7},{7,6},{8,9},{9,8},{10,11... | collective-permute-start | bytes 835592 | tf_op jit(solution)/shard_map/ppermute | solution.py:300
  90.0 1.7 %collective-permute-start.15 = (bf16[2,2,272,128]{3,2,1,0:T(8,128)(2,1)S(1)}, bf16[2,2,272,128]{3,2,1,0:T(8,128)(2,1)S(1)}, u32[]{:S(2)}, u32[]{:S(2)}) collective-permute-start(bf16[2,2,272,128]{3,2,1,0:T(8,128)(2,1)S(1)} %get-tuple-element.48), channel_id=1, source_target_pairs={{0,16},{1,17},{2,18},{3,19},{4,20},{5,21},{6,22},{7,23},{8,24},{9,... | collective-permute-start | bytes 835592 | tf_op jit(solution)/shard_map/ppermute | solution.py:300
  91.6 2.5 %shard_map.127 = (bf16[2,128,512]{2,1,0:T(8,128)(2,1)}, bf16[2,128,512]{2,1,0:T(8,128)(2,1)}) custom-call(bf16[4,2,2,32,512]{4,3,2,1,0:T(8,128)(2,1)S(1)} %all-to-all-done.1.got, bf16[2,16,512]{2,1,0:T(8,128)(2,1)S(1)} %collective-permute-done.10.before, bf16[2,16,512]{2,1,0:T(8,128)(2,1)S(1)} %collective-permute-done.11.after, ...), custom_call_target="tpu_custom_call" | custom-call | tf_op jit(solution)/shard_map/pallas_call | solution.py:261
  94.1 0.1 pad_maximum_fusion.own
  94.2 0.1 collective-permute-start.16
  94.3 0.2 collective-permute-done.14
  94.5 2.0 %collective-permute-done.15 = bf16[2,2,272,128]{3,2,1,0:T(8,128)(2,1)S(1)} collective-permute-done((bf16[2,2,272,128]{3,2,1,0:T(8,128)(2,1)S(1)}, bf16[2,2,272,128]{3,2,1,0:T(8,128)(2,1)S(1)}, u32[]{:S(2)}, u32[]{:S(2)}) %collective-permute-start.15) | collective-permute-done | bytes 278560 | tf_op jit(solution)/shard_map/ppermute | solution.py:300
  96.6 0.1 collective-permute-start.17
  96.7 1.9 %collective-permute-done.17.other_far = bf16[2,2,2,272,128]{4,3,2,1,0:T(8,128)(2,1)S(1)} collective-permute-done((bf16[2,2,2,272,128]{4,3,2,1,0:T(8,128)(2,1)S(1)}, bf16[2,2,2,272,128]{4,3,2,1,0:T(8,128)(2,1)S(1)}, u32[]{:S(2)}, u32[]{:S(2)}) %collective-permute-start.17) | collective-permute-done | bytes 557088 | tf_op jit(solution)/shard_map/ppermute | solution.py:300
  98.6 3.2 %shard_map.128 = (f32[31,512]{1,0:T(8,128)}, f32[512,512]{1,0:T(8,128)}, f32[512,512]{1,0:T(8,128)}, f32[512,512]{1,0:T(8,128)}, f32[512,512]{1,0:T(8,128)}) custom-call(s32[4]{0:T(128)S(1)} %pad_add_fusion.bits, bf16[2,2,2,272,128]{4,3,2,1,0:T(8,128)(2,1)S(1)} %pad_maximum_fusion.own, bf16[2,2,2,272,128]{4,3,2,1,0:T(8,128)(2,1)S(1)} %pad_maximum_fusion.1.far, ...), custom_call_target="tpu_custom_call" | custom-call | tf_op jit(solution)/shard_map/pallas_call | solution.py:261
  (30 shorter events, 0.4 us)
Async XLA Ops:
  1.7 18.4 %copy-start.1 = (bf16[512,512]{1,0:T(8,128)(2,1)S(1)}, bf16[512,512]{1,0:T(8,128)(2,1)}, u32[]{:S(2)}) copy-start(bf16[512,512]{1,0:T(8,128)(2,1)} %wq.1) | copy-start | bytes 1572868
  1.7 18.4 %copy-start.2 = (bf16[512,512]{1,0:T(8,128)(2,1)S(1)}, bf16[512,512]{1,0:T(8,128)(2,1)}, u32[]{:S(2)}) copy-start(bf16[512,512]{1,0:T(8,128)(2,1)} %wk.1) | copy-start | bytes 1572868
  1.7 18.4 %copy-start.3 = (bf16[512,512]{1,0:T(8,128)(2,1)S(1)}, bf16[512,512]{1,0:T(8,128)(2,1)}, u32[]{:S(2)}) copy-start(bf16[512,512]{1,0:T(8,128)(2,1)} %wv.1) | copy-start | bytes 1572868
  1.8 18.4 %copy-start.5 = (f32[31,512]{1,0:T(8,128)S(1)}, f32[31,512]{1,0:T(8,128)}, u32[]{:S(2)}) copy-start(f32[31,512]{1,0:T(8,128)} %kern.3) | copy-start | bytes 190468
  14.8 4.5 %collective-permute-start.1 = (bf16[4,2,16,512]{3,2,1,0:T(8,128)(2,1)S(1)}, bf16[4,2,16,512]{3,2,1,0:T(8,128)(2,1)S(1)}, u32[]{:S(2)}, u32[]{:S(2)}) collective-permute-start(bf16[4,2,16,512]{3,2,1,0:T(8,128)(2,1)S(1)} %get-tuple-element.51), channel_id=1, source_target_pairs={{8,0},{16,8},{24,16},{1,24},{9,1},{17,9},{25,17},{2,25},{10,2},{18... | collective-permute-start | bytes 393224 | tf_op jit(solution)/shard_map/ppermute | solution.py:293
  16.1 4.0 %collective-permute-start = (bf16[4,2,16,512]{3,2,1,0:T(8,128)(2,1)S(1)}, bf16[4,2,16,512]{3,2,1,0:T(8,128)(2,1)S(1)}, u32[]{:S(2)}, u32[]{:S(2)}) collective-permute-start(bf16[4,2,16,512]{3,2,1,0:T(8,128)(2,1)S(1)} %get-tuple-element.52), channel_id=1, source_target_pairs={{0,8},{8,16},{16,24},{24,1},{1,9},{9,17},{17,25},{25,2},{2,10},{10... | collective-permute-start | bytes 393224 | tf_op jit(solution)/shard_map/ppermute | solution.py:292
  20.2 1.0 %copy-start.4 = (bf16[512,512]{1,0:T(8,128)(2,1)S(1)}, bf16[512,512]{1,0:T(8,128)(2,1)}, u32[]{:S(2)}) copy-start(bf16[512,512]{1,0:T(8,128)(2,1)} %wo.1) | copy-start | bytes 1572868
  32.3 4.4 %collective-permute-start.2 = (bf16[2,2,2,2,272,128]{5,4,3,2,1,0:T(8,128)(2,1)}, bf16[2,2,2,2,272,128]{5,4,3,2,1,0:T(8,128)(2,1)}, u32[]{:S(2)}, u32[]{:S(2)}) collective-permute-start(bf16[2,2,2,2,272,128]{5,4,3,2,1,0:T(8,128)(2,1)} %get-tuple-element.26), channel_id=1, source_target_pairs={{0,8},{1,9},{2,10},{3,11},{4,12},{5,13},{6,14},{7,15},{8,0},{9,1},... | collective-permute-start | bytes 3342344 | tf_op jit(solution)/shard_map/ppermute | solution.py:300
  38.8 9.9 %collective-permute-start.5 = (bf16[2,2,272,128]{3,2,1,0:T(8,128)(2,1)}, bf16[2,2,272,128]{3,2,1,0:T(8,128)(2,1)S(1)}, u32[]{:S(2)}, u32[]{:S(2)}) collective-permute-start(bf16[2,2,272,128]{3,2,1,0:T(8,128)(2,1)} %fusion.1), channel_id=1, source_target_pairs={{0,16},{1,17},{2,18},{3,19},{4,20},{5,21},{6,22},{7,23},{8,24},{9,... | collective-permute-start | bytes 835592 | tf_op jit(solution)/shard_map/ppermute | solution.py:300
  42.3 10.1 %collective-permute-start.3 = (bf16[2,2,272,128]{3,2,1,0:T(8,128)(2,1)}, bf16[2,2,272,128]{3,2,1,0:T(8,128)(2,1)}, u32[]{:S(2)}, u32[]{:S(2)}) collective-permute-start(bf16[2,2,272,128]{3,2,1,0:T(8,128)(2,1)} %fusion), channel_id=1, source_target_pairs={{0,1},{1,0},{2,3},{3,2},{4,5},{5,4},{6,7},{7,6},{8,9},{9,8},{10,11... | collective-permute-start | bytes 835592 | tf_op jit(solution)/shard_map/ppermute | solution.py:300
  44.4 16.4 %all-to-all-start.1 = ((bf16[4,2,2,32,512]{4,3,2,1,0:T(8,128)(2,1)}), bf16[4,2,2,32,512]{4,3,2,1,0:T(8,128)(2,1)S(1)}, u32[]{:S(2)}, u32[]{:S(2)}) async-start(bf16[4,2,2,32,512]{4,3,2,1,0:T(8,128)(2,1)} %get-tuple-element.27), calls=%async_computation.1 | async-start | bytes 1048576 | tf_op jit(solution)/shard_map/all_to_all | solution.py:318
  48.7 6.7 %collective-permute-start.6 = (bf16[2,272,128]{2,1,0:T(8,128)(2,1)S(1)}, bf16[2,272,128]{2,1,0:T(8,128)(2,1)S(1)}, u32[]{:S(2)}, u32[]{:S(2)}) collective-permute-start(bf16[2,272,128]{2,1,0:T(8,128)(2,1)S(1)} %fusion.6), channel_id=1, source_target_pairs={{0,1},{1,0},{2,3},{3,2},{4,5},{5,4},{6,7},{7,6},{8,9},{9,8},{10,11... | collective-permute-start | bytes 417800 | tf_op jit(solution)/shard_map/ppermute | solution.py:300
  53.3 6.4 %collective-permute-start.4 = (bf16[2,272,128]{2,1,0:T(8,128)(2,1)S(1)}, bf16[2,272,128]{2,1,0:T(8,128)(2,1)}, u32[]{:S(2)}, u32[]{:S(2)}) collective-permute-start(bf16[2,272,128]{2,1,0:T(8,128)(2,1)S(1)} %fusion.7), channel_id=1, source_target_pairs={{0,16},{1,17},{2,18},{3,19},{4,20},{5,21},{6,22},{7,23},{8,24},{9,... | collective-permute-start | bytes 417800 | tf_op jit(solution)/shard_map/ppermute | solution.py:300
  60.8 5.7 %collective-permute-start.7 = (bf16[2,272,128]{2,1,0:T(8,128)(2,1)S(1)}, bf16[2,272,128]{2,1,0:T(8,128)(2,1)S(1)}, u32[]{:S(2)}, u32[]{:S(2)}) collective-permute-start(bf16[2,272,128]{2,1,0:T(8,128)(2,1)S(1)} %pad_maximum_fusion.3), channel_id=1, source_target_pairs={{0,2},{1,3},{2,0},{3,1},{4,6},{5,7},{6,4},{7,5},{8,10},{9,11},{10,... | collective-permute-start | bytes 417800 | tf_op jit(solution)/shard_map/ppermute | solution.py:300
  67.5 8.8 %collective-permute-start.8 = (bf16[2,272,128]{2,1,0:T(8,128)(2,1)S(1)}, bf16[2,272,128]{2,1,0:T(8,128)(2,1)S(1)}, u32[]{:S(2)}, u32[]{:S(2)}) collective-permute-start(bf16[2,272,128]{2,1,0:T(8,128)(2,1)S(1)} %pad_maximum_fusion.4), channel_id=1, source_target_pairs={{0,4},{1,5},{2,6},{3,7},{4,0},{5,1},{6,2},{7,3},{8,12},{9,13},{10,... | collective-permute-start | bytes 417800 | tf_op jit(solution)/shard_map/ppermute | solution.py:300
  70.3 11.2 %collective-permute-start.11 = (bf16[2,16,512]{2,1,0:T(8,128)(2,1)S(1)}, bf16[2,16,512]{2,1,0:T(8,128)(2,1)S(1)}, u32[]{:S(2)}, u32[]{:S(2)}) collective-permute-start(bf16[2,16,512]{2,1,0:T(8,128)(2,1)S(1)} %get-tuple-element.49), channel_id=1, source_target_pairs={{1,0},{2,1},{3,2},{4,3},{5,4},{6,5},{7,6},{9,8},{10,9},{11,10},{12... | collective-permute-start | bytes 98312 | tf_op jit(solution)/shard_map/ppermute | solution.py:341
  71.6 9.9 %collective-permute-start.10 = (bf16[2,16,512]{2,1,0:T(8,128)(2,1)S(1)}, bf16[2,16,512]{2,1,0:T(8,128)(2,1)S(1)}, u32[]{:S(2)}, u32[]{:S(2)}) collective-permute-start(bf16[2,16,512]{2,1,0:T(8,128)(2,1)S(1)} %get-tuple-element.50), channel_id=1, source_target_pairs={{0,1},{1,2},{2,3},{3,4},{4,5},{5,6},{6,7},{8,9},{9,10},{10,11},{11... | collective-permute-start | bytes 98312 | tf_op jit(solution)/shard_map/ppermute | solution.py:340
  76.4 5.1 %collective-permute-start.9 = (bf16[2,272,128]{2,1,0:T(8,128)(2,1)S(1)}, bf16[2,272,128]{2,1,0:T(8,128)(2,1)S(1)}, u32[]{:S(2)}, u32[]{:S(2)}) collective-permute-start(bf16[2,272,128]{2,1,0:T(8,128)(2,1)S(1)} %add_convert_fusion.2), channel_id=1, source_target_pairs={{0,2},{1,3},{2,0},{3,1},{4,6},{5,7},{6,4},{7,5},{8,10},{9,11},{10,... | collective-permute-start | bytes 417800 | tf_op jit(solution)/shard_map/ppermute | solution.py:300
  81.5 10.1 %copy-start = (bf16[2,128,512]{2,1,0:T(8,128)(2,1)S(1)}, bf16[2,128,512]{2,1,0:T(8,128)(2,1)}, u32[]{:S(2)}) copy-start(bf16[2,128,512]{2,1,0:T(8,128)(2,1)} %cot.1) | copy-start | bytes 786436
  81.6 5.7 %collective-permute-start.12 = (bf16[2,272,128]{2,1,0:T(8,128)(2,1)S(1)}, bf16[2,272,128]{2,1,0:T(8,128)(2,1)S(1)}, u32[]{:S(2)}, u32[]{:S(2)}) collective-permute-start(bf16[2,272,128]{2,1,0:T(8,128)(2,1)S(1)} %get-tuple-element.53), channel_id=1, source_target_pairs={{0,16},{1,17},{2,18},{3,19},{4,20},{5,21},{6,22},{7,23},{8,24},{9,... | collective-permute-start | bytes 417800 | tf_op jit(solution)/shard_map/ppermute | solution.py:300
  81.8 5.8 %collective-permute-start.13 = (bf16[2,272,128]{2,1,0:T(8,128)(2,1)S(1)}, bf16[2,272,128]{2,1,0:T(8,128)(2,1)S(1)}, u32[]{:S(2)}, u32[]{:S(2)}) collective-permute-start(bf16[2,272,128]{2,1,0:T(8,128)(2,1)S(1)} %get-tuple-element.54), channel_id=1, source_target_pairs={{0,1},{1,0},{2,3},{3,2},{4,5},{5,4},{6,7},{7,6},{8,9},{9,8},{10,11... | collective-permute-start | bytes 417800 | tf_op jit(solution)/shard_map/ppermute | solution.py:300
  87.7 6.8 %collective-permute-start.14 = (bf16[2,2,272,128]{3,2,1,0:T(8,128)(2,1)S(1)}, bf16[2,2,272,128]{3,2,1,0:T(8,128)(2,1)S(1)}, u32[]{:S(2)}, u32[]{:S(2)}) collective-permute-start(bf16[2,2,272,128]{3,2,1,0:T(8,128)(2,1)S(1)} %get-tuple-element.47), channel_id=1, source_target_pairs={{0,1},{1,0},{2,3},{3,2},{4,5},{5,4},{6,7},{7,6},{8,9},{9,8},{10,11... | collective-permute-start | bytes 835592 | tf_op jit(solution)/shard_map/ppermute | solution.py:300
  90.0 6.5 %collective-permute-start.15 = (bf16[2,2,272,128]{3,2,1,0:T(8,128)(2,1)S(1)}, bf16[2,2,272,128]{3,2,1,0:T(8,128)(2,1)S(1)}, u32[]{:S(2)}, u32[]{:S(2)}) collective-permute-start(bf16[2,2,272,128]{3,2,1,0:T(8,128)(2,1)S(1)} %get-tuple-element.48), channel_id=1, source_target_pairs={{0,16},{1,17},{2,18},{3,19},{4,20},{5,21},{6,22},{7,23},{8,24},{9,... | collective-permute-start | bytes 835592 | tf_op jit(solution)/shard_map/ppermute | solution.py:300
  94.2 2.5 %collective-permute-start.16 = (bf16[2,2,2,272,128]{4,3,2,1,0:T(8,128)(2,1)S(1)}, bf16[2,2,2,272,128]{4,3,2,1,0:T(8,128)(2,1)S(1)}, u32[]{:S(2)}, u32[]{:S(2)}) collective-permute-start(bf16[2,2,2,272,128]{4,3,2,1,0:T(8,128)(2,1)S(1)} %pad_maximum_fusion.own), channel_id=1, source_target_pairs={{0,8},{1,9},{2,10},{3,11},{4,12},{5,13},{6,14},{7,15},{8,0},{9,1},... | collective-permute-start | bytes 1671176 | tf_op jit(solution)/shard_map/ppermute | solution.py:300
  96.6 2.0 %collective-permute-start.17 = (bf16[2,2,2,272,128]{4,3,2,1,0:T(8,128)(2,1)S(1)}, bf16[2,2,2,272,128]{4,3,2,1,0:T(8,128)(2,1)S(1)}, u32[]{:S(2)}, u32[]{:S(2)}) collective-permute-start(bf16[2,2,2,272,128]{4,3,2,1,0:T(8,128)(2,1)S(1)} %pad_maximum_fusion.1.far), channel_id=1, source_target_pairs={{0,8},{1,9},{2,10},{3,11},{4,12},{5,13},{6,14},{7,15},{8,0},{9,1},... | collective-permute-start | bytes 1671176 | tf_op jit(solution)/shard_map/ppermute | solution.py:300

commit v4 on v3

v4 whole, which is shorter than its diff:
```python
import functools
import math

import jax
import jax.numpy as jnp
from jax import lax
from jax.experimental import pallas as pl
from jax.experimental.pallas import tpu as pltpu
from jax.sharding import PartitionSpec as P

HEADS = 8
LANES = 128
HALO = 16
NT = (((1,), (1,)), ((), ()))
TN = (((0,), (0,)), ((), ()))
BF = jnp.bfloat16
F32 = jnp.float32
MIB = 1024 * 1024


def mm(left, right, dims=(((1,), (0,)), ((), ()))):
    return lax.dot_general(left, right, dims, preferred_element_type=F32)


def rolled(x, shift):
    return x if shift == 0 else pltpu.roll(x, x.shape[0] - shift, axis=0)


def window(x, taps, rows):
    acc = None
    for r in range(8):
        xr = rolled(x, r)
        for k in range(4):
            o = 8 * k + r
            if o == 0:
                continue
            term = xr[8 * k : 8 * k + rows] * taps(o)
            acc = term if acc is None else acc + term
    return acc


def sigmoid(v):
    return 0.5 * jnp.tanh(0.5 * v) + 0.5


def main_kernel(
    plan, bits, got, before, after, kern, wq_hbm, wk_hbm, wv_hbm, wo_hbm,
    back_out, a_keep, b_keep, a_send, b_send,
    frame_s, w_s, conv_s, left_s, right_s, q_s, k_s, v_s, u_s, dconv_s, tap_s, back, stage,
    frame_sem, cot_sem, w_sem, out_sem,
):
    groups, count, sub, width, factor = plan
    mics = groups * count
    cuts = sub // HALO
    block = mics * HALO
    rows = cuts * block
    cols = width // LANES

    loads = [
        pltpu.make_async_copy(got.at[a, 0], frame_s.at[a], frame_sem.at[a]) for a in range(groups)
    ]
    cots = [
        pltpu.make_async_copy(
            got.at[:, 1, :, pl.ds(c * HALO, HALO)], right_s.at[3, c], cot_sem.at[c]
        )
        for c in range(cuts)
    ]
    weights = [
        pltpu.make_async_copy(w, w_s.at[i], w_sem.at[i])
        for i, w in enumerate((wq_hbm, wk_hbm, wv_hbm, wo_hbm))
    ]
    for copy in loads + weights + cots:
        copy.start()
    for copy in loads:
        copy.wait()

    def frames_window(a, m, lanes):
        return jnp.concatenate(
            [before[a, m, :, lanes], frame_s[a, m, :, lanes], after[a, m, :, lanes]], axis=0
        ).astype(F32)

    def conv_step(n, _):
        a, m = n // count, n % count
        for lc in range(cols):
            lanes = slice(lc * LANES, (lc + 1) * LANES)
            conv = window(
                frames_window(a, m, lanes), lambda o: kern[o - 1 : o, lanes], sub
            )
            acted = (conv * sigmoid(conv)).astype(BF)
            for c in range(cuts):
                at = pl.multiple_of(c * block + n * HALO, HALO)
                conv_s[pl.ds(at, HALO), lanes] = conv[c * HALO : (c + 1) * HALO]
                left_s[0, pl.ds(at, HALO), lanes] = acted[c * HALO : (c + 1) * HALO]
        return 0

    lax.fori_loop(0, mics, conv_step, 0)
    for copy in weights + cots:
        copy.wait()

    def flat(i):
        return right_s[i].reshape(rows, width)

    def put(i, c, lanes, x):
        right_s[i, c, :, :, :, lanes] = x.astype(BF).reshape(groups, count, HALO, LANES)

    acted = left_s[0]
    q_s[...] = mm(acted, w_s[0]).astype(BF)
    k_s[...] = mm(acted, w_s[1]).astype(BF)
    v_s[...] = mm(acted, w_s[2]).astype(BF)
    u_s[...] = mm(flat(3), w_s[3], NT).astype(BF)

    depth = width // HEADS
    per = LANES // depth
    lane = lax.broadcasted_iota(jnp.int32, (block, LANES), 1)
    row_i = lax.broadcasted_iota(jnp.int32, (block, per * block), 0)
    col_i = lax.broadcasted_iota(jnp.int32, (block, per * block), 1)
    same = (row_i % HALO) == (col_i % HALO)

    def by_head(x):
        return jnp.concatenate(
            [jnp.where(lane // depth == h, x, jnp.zeros_like(x)) for h in range(per)], axis=0
        )

    def sums(x):
        return [
            jnp.sum(x[:, h * block : (h + 1) * block], axis=1, keepdims=True) for h in range(per)
        ]

    def each(x, values, op):
        return jnp.concatenate(
            [op(x[:, h * block : (h + 1) * block], values[h]) for h in range(per)], axis=1
        )

    def pick(x):
        out = x[:block]
        for h in range(1, per):
            out = jnp.where(lane // depth == h, x[h * block : (h + 1) * block], out)
        return out

    for c in range(cuts):
        part = slice(c * block, (c + 1) * block)
        for p in range(cols):
            lanes = slice(p * LANES, (p + 1) * LANES)
            q, u = q_s[part, lanes], u_s[part, lanes]
            kc, vc = by_head(k_s[part, lanes]), by_head(v_s[part, lanes])
            e = jnp.where(same, jnp.exp(mm(q, kc, NT) * factor), 0.0)
            w = each(e, [1.0 / x for x in sums(e)], lambda x, s: x * s)
            up = mm(u, vc, NT)
            inner = each(up, sums(w * up), lambda x, s: x - s) * w * factor
            wb, ib = w.astype(BF), inner.astype(BF)
            left_s[1, part, lanes] = mm(wb, vc).astype(BF)
            put(0, c, lanes, mm(ib, kc))
            put(1, c, lanes, pick(mm(ib, q, TN)))
            put(2, c, lanes, pick(mm(wb, u, TN)))

    dacted = mm(flat(0), w_s[0], NT) + mm(flat(1), w_s[1], NT) + mm(flat(2), w_s[2], NT)
    conv = conv_s[...]
    sig = sigmoid(conv)
    dconv_s[...] = dacted * sig * (1.0 + conv * (1.0 - sig))

    for lc in range(cols):
        lanes = slice(lc * LANES, (lc + 1) * LANES)

        def tap_step(n, accs):
            a, m = n // count, n % count
            x = frames_window(a, m, lanes)
            d = jnp.concatenate(
                [
                    dconv_s[pl.ds(pl.multiple_of(c * block + n * HALO, HALO), HALO), lanes]
                    for c in range(cuts)
                ],
                axis=0,
            )
            out = list(accs)
            for r in range(8):
                xr = rolled(x, r)
                for k in range(4):
                    o = 8 * k + r
                    if o == 0:
                        continue
                    prod = xr[8 * k : 8 * k + sub] * d
                    out[o - 1] = out[o - 1] + jnp.sum(prod.reshape(sub // 8, 8, LANES), axis=0)
            return tuple(out)

        accs = lax.fori_loop(0, mics, tap_step, tuple(jnp.zeros((8, LANES), F32) for _ in range(31)))
        tap_s[lc * 32 : lc * 32 + 32, :] = jnp.concatenate(
            [jnp.sum(x, axis=0, keepdims=True) for x in accs] + [jnp.zeros((1, LANES), F32)], axis=0
        )

    tap_s[cols * 32 :, :] = jnp.zeros((HALO, LANES), F32)
    core = bits[0]
    size = cols * width // 8
    copies = []
    for n, (out, owner, h) in enumerate(
        ((a_send, 1 - core, 0), (b_send, 1 - core, 1), (a_keep, core, 0), (b_keep, core, 1))
    ):
        i = owner * 2 + h
        grad = mm(left_s[i // 3], flat(i), TN).astype(BF)
        for piece in range(8):
            at = piece * size
            cb, at = at // width, at % width
            tail = tap_s[pl.ds(pl.multiple_of((i * 8 + piece) * cols, cols), HALO), :]
            where = (n, piece // 4, piece // 2 % 2, piece % 2)
            stage[(*where, slice(0, size), slice(None))] = grad[
                at : at + size, cb * LANES : (cb + 1) * LANES
            ]
            stage[(*where, slice(size, size + HALO), slice(None))] = tail.astype(BF)
        copy = pltpu.make_async_copy(stage.at[n], out, out_sem.at[n])
        copy.start()
        copies.append(copy)

    proj = mm(left_s[1], w_s[3])
    for n in range(mics):
        a, m = n // count, n % count
        for c in range(cuts):
            at = c * block + n * HALO
            part = slice(c * HALO, (c + 1) * HALO)
            back[a, 0, m, part, :] = (
                frame_s[a, m, part, :].astype(F32) + proj[at : at + HALO]
            ).astype(BF)
            back[a, 1, m, part, :] = dconv_s[at : at + HALO, :].astype(BF)
    copy = pltpu.make_async_copy(back, back_out, out_sem.at[4])
    copy.start()
    for copy in copies + [copy]:
        copy.wait()


def at(x, *where):
    rest = x.shape[len(where) :]
    start = [jnp.asarray(i, jnp.int32) for i in where] + [jnp.int32(0)] * len(rest)
    return lax.dynamic_slice(x, start, (1,) * len(where) + rest).reshape(rest)


def total(*parts):
    return functools.reduce(lambda x, y: x + y, [x.astype(F32) for x in parts]).astype(BF)


def final_kernel(
    plan, bits, a_own, b_own, a_far, b_far, a_other, b_other, a_other_far, b_other_far, taps, *refs
):
    width, norm = plan
    outs, tap_s = refs[:4], refs[4]
    cols = width // LANES
    size = cols * width // 8
    core, y, x, z = bits[0], bits[1], bits[2], bits[3]

    def emit(which, parts):
        for h in range(2):
            i = 2 * which + h
            first, second = (x, y) if h == 0 else (y, x)
            for b1 in range(2):
                part = parts[b1][h]
                for b2 in range(2):
                    for b3 in range(2):
                        piece = (first ^ b1) * 4 + (second ^ b2) * 2 + (z ^ b3)
                        flat = piece * size
                        cb, at = flat // width, flat % width
                        outs[i][
                            pl.ds(pl.multiple_of(at, size), size),
                            pl.ds(pl.multiple_of(cb * LANES, LANES), LANES),
                        ] = part[b2, b3, 0:size, :].astype(F32) * norm
                        tap_s[i * 8 + piece] = part[b2, b3, size : size + HALO, :].astype(F32) * norm

    for which in range(2):
        @pl.when(core == which)
        def _():
            emit(which, ((a_own, b_own), (a_far, b_far)))
            emit(1 - which, ((a_other, b_other), (a_other_far, b_other_far)))

    for g in range(32):
        row = g * cols
        lc, j = row // 32, row % 32
        kept = min(cols, 31 - j)
        taps[j : j + kept, lc * LANES : (lc + 1) * LANES] = tap_s[g, 0:kept]


def frame_kernel(plan, got, before, after, cot, kern, layer_out, frame_grad):
    groups, count, sub, width = plan
    cols = width // LANES

    def edge(a, m, lanes):
        first = before[m, :, lanes] if a == 0 else got[a - 1, 1, m, sub - HALO :, lanes]
        last = after[m, :, lanes] if a == groups - 1 else got[a + 1, 1, m, :HALO, lanes]
        return jnp.concatenate([first, got[a, 1, m, :, lanes], last], axis=0).astype(F32)

    def step(m, _):
        for a in range(groups):
            part = slice(a * sub, (a + 1) * sub)
            layer_out[m, part, :] = got[a, 0, m, :, :]
            for lc in range(cols):
                lanes = slice(lc * LANES, (lc + 1) * LANES)
                total = window(edge(a, m, lanes), lambda o: kern[31 - o : 32 - o, lanes], sub)
                frame_grad[m, part, lanes] = (cot[m, part, lanes].astype(F32) + total).astype(BF)
        return 0

    lax.fori_loop(0, count, step, 0)


def call(body, outs, scratch, limit, *args, spaces=(), out_space=pltpu.VMEM):
    spaces = list(spaces) + [pltpu.VMEM] * (len(args) - len(spaces))
    return pl.pallas_call(
        body,
        out_shape=outs,
        in_specs=[
            pl.BlockSpec(memory_space=pltpu.SMEM if x.dtype == jnp.int32 else space)
            for x, space in zip(args, spaces)
        ],
        out_specs=jax.tree.map(lambda _: pl.BlockSpec(memory_space=out_space), outs),
        scratch_shapes=scratch,
        compiler_params=pltpu.CompilerParams(vmem_limit_bytes=limit * MIB),
    )(*args)


def neighbours(groups, blocks):
    def flat(s):
        return (s % groups) * blocks + s // groups

    return [(flat(s), flat(s + 1)) for s in range(groups * blocks - 1)]


def shards(frames, cotangent, kernel, w_query, w_key, w_value, w_out):
    groups, blocks = lax.axis_size("mic"), lax.axis_size("tm")
    count, length, width = frames.shape
    sub = length // groups
    rows = groups * count * sub
    shape = jax.ShapeDtypeStruct

    send = jnp.stack([frames, cotangent]).reshape(2, count, groups, sub, width)
    got = lax.all_to_all(send.transpose(2, 0, 1, 3, 4), "mic", 0, 0, tiled=True)
    up = neighbours(groups, blocks)
    down = [(j, i) for i, j in up]
    before = lax.ppermute(got[:, 0, :, sub - HALO :, :], ("mic", "tm"), up)
    after = lax.ppermute(got[:, 0, :, :HALO, :], ("mic", "tm"), down)

    mic, tm = lax.axis_index("mic"), lax.axis_index("tm")
    bits = jnp.stack([mic % 2, mic // 2, tm % 2, tm // 2 % 2]).astype(jnp.int32)
    over_core, over_y, over_x, over_z = blocks, 2 * blocks, 1, 2

    def swap(x, mask):
        return lax.ppermute(x, ("mic", "tm"), [(f, f ^ mask) for f in range(groups * blocks)])

    factor = 1.0 / math.sqrt(width // HEADS)
    piece = (width * width // LANES // 8 + HALO, LANES)
    big = pltpu.VMEM((rows, width), BF)
    wide = pltpu.VMEM((rows, width), F32)
    half = shape((2, 2, 2, *piece), BF)
    moved = (groups, 2, count, sub, width)
    cuts = sub // HALO
    back, a_keep, b_keep, a_send, b_send = call(
        functools.partial(main_kernel, (groups, count, sub, width, factor)),
        (shape(moved, BF), half, half, half, half),
        [
            pltpu.VMEM((groups, count, sub, width), BF),
            pltpu.VMEM((4, width, width), BF),
            wide,
            pltpu.VMEM((2, rows, width), BF),
            pltpu.VMEM((4, cuts, groups, count, HALO, width), BF),
            big, big, big, big, wide,
            pltpu.VMEM((32 * width // LANES + HALO, LANES), F32),
            pltpu.VMEM(moved, BF),
            pltpu.VMEM((4, 2, 2, 2, *piece), BF),
            pltpu.SemaphoreType.DMA((groups,)),
            pltpu.SemaphoreType.DMA((cuts,)),
            pltpu.SemaphoreType.DMA((4,)),
            pltpu.SemaphoreType.DMA((5,)),
        ],
        28, bits, got, before, after, kernel, w_query, w_key, w_value, w_out,
        spaces=(pltpu.SMEM, pl.ANY, pltpu.VMEM, pltpu.VMEM, pltpu.VMEM) + (pl.ANY,) * 4,
        out_space=pl.ANY,
    )

    y, x, z = bits[1], bits[2], bits[3]
    a, b = [a_keep, swap(a_send, over_core)], [b_keep, swap(b_send, over_core)]
    home = lax.all_to_all(back, "mic", 0, 0, tiled=True)

    def halved(parts, bit, mask):
        got = swap(total(*(at(t, 1 - bit) for t in parts)), mask)
        return [at(t, bit) for t in parts] + [got]

    def line_sum(parts):
        mine = total(*halved(parts, z, over_z))
        mask = 2 * over_z
        while mask < blocks:
            mine = total(mine, swap(mine, mask))
            mask *= 2
        return mine

    a = halved(a, x, over_x)
    b = halved(b, y, over_y)
    a = halved(a, y, over_y)
    b = halved(b, x, over_x)
    b[-1], home = lax.optimization_barrier((b[-1], home))
    a, b = line_sum(a), line_sum(b)

    up = [(i, i + 1) for i in range(blocks - 1)]
    down = [(j, i) for i, j in up]
    before = lax.ppermute(home[groups - 1, 1, :, sub - HALO :, :], "tm", up)
    after = lax.ppermute(home[0, 1, :, :HALO, :], "tm", down)

    a = jnp.stack([a, swap(a, over_z)])
    b = jnp.stack([b, swap(b, over_z)])
    b, before, after = lax.optimization_barrier((b, before, after))
    layer_out, frame_grad = call(
        functools.partial(frame_kernel, (groups, count, sub, width)),
        (shape((count, length, width), BF), shape((count, length, width), BF)),
        [], 12, home, before, after, cotangent, kernel,
    )
    a = jnp.stack([a, swap(a, over_y)])
    b = jnp.stack([b, swap(b, over_x)])
    a_far, b_far = swap(a, over_x), swap(b, over_y)
    a_other, b_other = swap(a, over_core), swap(b, over_core)
    b_far, layer_out, frame_grad = lax.optimization_barrier((b_far, layer_out, frame_grad))
    a_other_far, b_other_far = swap(a_far, over_core), swap(b_far, over_core)

    norm = 1.0 / math.sqrt(groups * count * blocks * length)
    square = shape((width, width), F32)
    grads = call(
        functools.partial(final_kernel, (width, norm)),
        (shape((31, width), F32), square, square, square, square),
        [pltpu.VMEM((32, HALO, LANES), F32)],
        16, bits, a, b, a_far, b_far, a_other, b_other, a_other_far, b_other_far,
    )
    return (layer_out, frame_grad, *grads)


def solution(mesh):
    in_specs = (P("mic", "tm", None), P("mic", "tm", None), P(), P(), P(), P(), P())
    out_specs = (P("mic", "tm", None), P("mic", "tm", None), P(), P(), P(), P(), P())
    return jax.shard_map(shards, mesh=mesh, in_specs=in_specs, out_specs=out_specs, check_vma=False)
```

time: 102 us -> 99 us (0.971)
  waiting for transfers between devices: 25 us -> 18.2 us
  starting transfers between devices: 37.5 us -> 40.3 us
  local copies, waits for them, and re-layouts: 2.53 us -> 1.13 us
  other arithmetic: 6.1 us -> 7.21 us
    ppermute x14 -> x20, waiting for transfers between devices: 24.1 us -> 15.8 us  [swap(): lax.ppermute(x, ('mic', 'tm'), [(f, f ^ mask) for f in range(groups * blo...]
    ppermute x14 -> x20, starting transfers between devices: 23.8 us -> 26.5 us  [swap(): lax.ppermute(x, ('mic', 'tm'), [(f, f ^ mask) for f in range(groups * blo...]
    all_to_all x1, waiting for transfers between devices: 0.01 us -> 1.5 us  [shards(): home = lax.all_to_all(back, 'mic', 0, 0, tiled=True)]
    slice x2 -> x0, local copies, waits for them, and re-layouts: 1.38 us -> none  [shards(): a, b = ([keep[0], core_got[0]], [keep[1], core_got[1]])]
    convert_element_type x8 -> x10, other arithmetic: 4.66 us -> 5.97 us  [total(): functools.reduce(lambda x, y: x + y, [x.astype(F32) for x in parts])]
  transfers between devices with their start and end apart: 19 -> 25, of which waited for: 13 -> 13; matrix products, arithmetic and copies ran while one was open for 3% -> 6% of each run, Pallas kernels for 2% -> 3%
where the time goes in v4:
time: 99 us; the launch traced here: 98.4 us
  starting transfers between devices  40.3 us (41%)
  waiting for transfers between devices  18.2 us (18%)
  Pallas kernels  17.7 us (18%)
  blocking collectives  13 us (13%)
  other arithmetic  7.21 us (7%)
  local copies, waits for them, and re-layouts  1.13 us (1%)
    ppermute x20, starting transfers between devices, swap(): lax.ppermute(x, ('mic', 'tm'), [(f, f ^ mask) for f in range(groups * blo...  26.5 us
    pallas_call x3, Pallas kernels, call(): pl.pallas_call(body, out_shape=outs, in_specs=[pl.BlockSpec(memory_space=...  17.7 us
    ppermute x20, waiting for transfers between devices, swap(): lax.ppermute(x, ('mic', 'tm'), [(f, f ^ mask) for f in range(groups * blo...  15.8 us
    all_to_all x1, blocking collectives, shards(): got = lax.all_to_all(send.transpose(2, 0, 1, 3, 4), 'mic', 0, 0, tiled=True)  13 us
    convert_element_type x10, other arithmetic, total(): functools.reduce(lambda x, y: x + y, [x.astype(F32) for x in parts])  5.97 us
    ppermute x1, starting transfers between devices, shards(): before = lax.ppermute(home[groups - 1, 1, :, sub - HALO:, :], 'tm', up)  4.55 us
    all_to_all x1, starting transfers between devices, shards(): home = lax.all_to_all(back, 'mic', 0, 0, tiled=True)  3.47 us
    ppermute x1, starting transfers between devices, shards(): before = lax.ppermute(got[:, 0, :, sub - HALO:, :], ('mic', 'tm'), up)  3.04 us
  transfers between devices with their start and end apart: 25, of which 13 were waited for; matrix products, arithmetic and copies ran while one was open for 6% of the time, Pallas kernels for 3%

profile of v4, /device:TPU:0, one launch (start us, length us, event | category | flops | bytes accessed | tf_op | source)
XLA Modules:
  0.0 98.4 jit_solution(1794806253118163066)
XLA Ops:
  0.6 1.1 %maximum_bitcast_fusion = bf16[4,2,2,32,512]{4,3,0,2,1:T(8,128)(2,1)S(1)} fusion(bf16[1,2,4,32,512]{4,3,2,1,0:T(8,128)(2,1)} %bitcast.75, bf16[1,2,4,32,512]{4,3,2,1,0:T(8,128)(2,1)} %bitcast.79), kind=kLoop, calls=%fused_computation.2 | loop fusion | flops 262144 | bytes 1048576 | tf_op jit(solution)/shard_map/transpose | solution.py:329
  1.8 13.0 %all_to_all.10.got = bf16[4,2,2,32,512]{4,3,2,1,0:T(8,128)(2,1)S(1)} all-to-all(bf16[4,2,2,32,512]{4,3,2,1,0:T(8,128)(2,1)S(1)} %copy.18), channel_id=1, replica_groups=mesh['mic'=4,'tm'=8] {'mic'}, dimensions={0} | all-to-all | bytes 1048576 | tf_op jit(solution)/shard_map/all_to_all | solution.py:329
  14.8 1.4 %collective-permute-start.1 = (bf16[4,2,16,512]{3,2,1,0:T(8,128)(2,1)S(1)}, bf16[4,2,16,512]{3,2,1,0:T(8,128)(2,1)S(1)}, u32[]{:S(2)}, u32[]{:S(2)}) collective-permute-start(bf16[4,2,16,512]{3,2,1,0:T(8,128)(2,1)S(1)} %get-tuple-element.49), channel_id=1, source_target_pairs={{8,0},{16,8},{24,16},{1,24},{9,1},{17,9},{25,17},{2,25},{10,2},{18... | collective-permute-start | bytes 393224 | tf_op jit(solution)/shard_map/ppermute | solution.py:333
  16.3 3.0 %collective-permute-start = (bf16[4,2,16,512]{3,2,1,0:T(8,128)(2,1)S(1)}, bf16[4,2,16,512]{3,2,1,0:T(8,128)(2,1)S(1)}, u32[]{:S(2)}, u32[]{:S(2)}) collective-permute-start(bf16[4,2,16,512]{3,2,1,0:T(8,128)(2,1)S(1)} %get-tuple-element.50), channel_id=1, source_target_pairs={{0,8},{8,16},{16,24},{24,1},{1,9},{9,17},{17,25},{25,2},{2,10},{10... | collective-permute-start | bytes 393224 | tf_op jit(solution)/shard_map/ppermute | solution.py:332
  19.4 0.1 pad_add_fusion.bits
  19.4 0.8 collective-permute-done.before
  20.3 1.0 %copy-done.4 = bf16[512,512]{1,0:T(8,128)(2,1)S(1)} copy-done((bf16[512,512]{1,0:T(8,128)(2,1)S(1)}, bf16[512,512]{1,0:T(8,128)(2,1)}, u32[]{:S(2)}) %copy-start.4) | copy-done | bytes 524312
  21.3 12.0 %shard_map.126 = (bf16[4,2,2,32,512]{4,3,2,1,0:T(8,128)(2,1)}, bf16[2,2,2,272,128]{4,3,2,1,0:T(8,128)(2,1)S(1)}, bf16[2,2,2,272,128]{4,3,2,1,0:T(8,128)(2,1)S(1)...) custom-call(s32[4]{0:T(128)S(1)} %pad_add_fusion.bits, ...), custom_call_target="tpu_custom_call" | custom-call | tf_op jit(solution)/shard_map/pallas_call | solution.py:301
  33.4 1.7 %collective-permute-start.2 = (bf16[2,2,2,272,128]{4,3,2,1,0:T(8,128)(2,1)}, bf16[2,2,2,272,128]{4,3,2,1,0:T(8,128)(2,1)S(1)}, u32[]{:S(2)}, u32[]{:S(2)}) collective-permute-start(bf16[2,2,2,272,128]{4,3,2,1,0:T(8,128)(2,1)} %get-tuple-element.28), channel_id=1, source_target_pairs={{0,8},{1,9},{2,10},{3,11},{4,12},{5,13},{6,14},{7,15},{8,0},{9,1},... | collective-permute-start | bytes 1671176 | tf_op jit(solution)/shard_map/ppermute | solution.py:340
  35.1 0.1 collective-permute-start.12
  35.2 1.7 %collective-permute-done.2 = bf16[2,2,2,272,128]{4,3,2,1,0:T(8,128)(2,1)S(1)} collective-permute-done((bf16[2,2,2,272,128]{4,3,2,1,0:T(8,128)(2,1)}, bf16[2,2,2,272,128]{4,3,2,1,0:T(8,128)(2,1)S(1)}, u32[]{:S(2)}, u32[]{:S(2)}) %collective-permute-start.2) | collective-permute-done | bytes 557088 | tf_op jit(solution)/shard_map/ppermute | solution.py:340
  36.9 0.8 fusion
  37.7 2.7 %collective-permute-start.3 = (bf16[2,2,272,128]{3,2,1,0:T(8,128)(2,1)}, bf16[2,2,272,128]{3,2,1,0:T(8,128)(2,1)S(1)}, u32[]{:S(2)}, u32[]{:S(2)}) collective-permute-start(bf16[2,2,272,128]{3,2,1,0:T(8,128)(2,1)} %fusion), channel_id=1, source_target_pairs={{0,16},{1,17},{2,18},{3,19},{4,20},{5,21},{6,22},{7,23},{8,24},{9,... | collective-permute-start | bytes 835592 | tf_op jit(solution)/shard_map/ppermute | solution.py:340
  40.4 0.8 fusion.1
  41.2 2.1 %collective-permute-start.13 = (bf16[2,2,272,128]{3,2,1,0:T(8,128)(2,1)}, bf16[2,2,272,128]{3,2,1,0:T(8,128)(2,1)}, u32[]{:S(2)}, u32[]{:S(2)}) collective-permute-start(bf16[2,2,272,128]{3,2,1,0:T(8,128)(2,1)} %fusion.1), channel_id=1, source_target_pairs={{0,1},{1,0},{2,3},{3,2},{4,5},{5,4},{6,7},{7,6},{8,9},{9,8},{10,11... | collective-permute-start | bytes 835592 | tf_op jit(solution)/shard_map/ppermute | solution.py:340
  43.3 3.5 %all-to-all-start.1 = ((bf16[4,2,2,32,512]{4,3,2,1,0:T(8,128)(2,1)}), bf16[4,2,2,32,512]{4,3,2,1,0:T(8,128)(2,1)S(1)}, u32[]{:S(2)}, u32[]{:S(2)}) async-start(bf16[4,2,2,32,512]{4,3,2,1,0:T(8,128)(2,1)} %get-tuple-element.29), calls=%async_computation.1 | async-start | bytes 1048576 | tf_op jit(solution)/shard_map/all_to_all | solution.py:374
  46.8 0.7 collective-permute-done.3
  47.6 0.7 fusion.3
  48.3 3.5 %collective-permute-start.4 = (bf16[2,272,128]{2,1,0:T(8,128)(2,1)}, bf16[2,272,128]{2,1,0:T(8,128)(2,1)S(1)}, u32[]{:S(2)}, u32[]{:S(2)}) collective-permute-start(bf16[2,272,128]{2,1,0:T(8,128)(2,1)} %fusion.3), channel_id=1, source_target_pairs={{0,1},{1,0},{2,3},{3,2},{4,5},{5,4},{6,7},{7,6},{8,9},{9,8},{10,11... | collective-permute-start | bytes 417800 | tf_op jit(solution)/shard_map/ppermute | solution.py:340
  51.8 1.6 %fusion.2 = bf16[2,272,128]{2,1,0:T(8,128)(2,1)} fusion(bf16[2,2,272,128]{3,2,1,0:T(8,128)(2,1)} %collective-permute-done.13, s32[]{:T(128)S(6)} %select_n.93, bf16[2,2,2,272,128]{4,3,2,1,0:T(8,128)(2,1)S(1)} %collective-permute-done.12, s32[]{:T(128)S(6)} %select_n.90, s32[]{:T(128)S(6)} %select_n.98, bf16[2,2,2,272,128]{4,3,2,1,0:T(8,128)(2,1)S(1)} %get-tuple-element.39), kind=kLoop, calls=%fused_computation.8 | loop fusion | flops 417792 | bytes 557068 | tf_op jit(solution)/shard_map/convert_element_type | solution.py:235
  53.5 1.1 %collective-permute-start.14 = (bf16[2,272,128]{2,1,0:T(8,128)(2,1)}, bf16[2,272,128]{2,1,0:T(8,128)(2,1)S(1)}, u32[]{:S(2)}, u32[]{:S(2)}) collective-permute-start(bf16[2,272,128]{2,1,0:T(8,128)(2,1)} %fusion.2), channel_id=1, source_target_pairs={{0,16},{1,17},{2,18},{3,19},{4,20},{5,21},{6,22},{7,23},{8,24},{9,... | collective-permute-start | bytes 417800 | tf_op jit(solution)/shard_map/ppermute | solution.py:340
  54.6 1.5 %all-to-all-done.1.got = bf16[4,2,2,32,512]{4,3,2,1,0:T(8,128)(2,1)S(1)} async-done(((bf16[4,2,2,32,512]{4,3,2,1,0:T(8,128)(2,1)}), bf16[4,2,2,32,512]{4,3,2,1,0:T(8,128)(2,1)S(1)}, u32[]{:S(2)}, u32[]{:S(2)}) %all-to-all-start.1) | async-done | bytes 524320 | tf_op jit(solution)/shard_map/all_to_all | solution.py:374
  56.1 1.3 %collective-permute-start.9 = (bf16[2,16,512]{2,1,0:T(8,128)(2,1)S(1)}, bf16[2,16,512]{2,1,0:T(8,128)(2,1)S(1)}, u32[]{:S(2)}, u32[]{:S(2)}) collective-permute-start(bf16[2,16,512]{2,1,0:T(8,128)(2,1)S(1)} %get-tuple-element.47), channel_id=1, source_target_pairs={{1,0},{2,1},{3,2},{4,3},{5,4},{6,5},{7,6},{9,8},{10,9},{11,10},{12... | collective-permute-start | bytes 98312 | tf_op jit(solution)/shard_map/ppermute | solution.py:398
  57.4 4.5 %collective-permute-start.8 = (bf16[2,16,512]{2,1,0:T(8,128)(2,1)S(1)}, bf16[2,16,512]{2,1,0:T(8,128)(2,1)S(1)}, u32[]{:S(2)}, u32[]{:S(2)}) collective-permute-start(bf16[2,16,512]{2,1,0:T(8,128)(2,1)S(1)} %get-tuple-element.48), channel_id=1, source_target_pairs={{0,1},{1,2},{2,3},{3,4},{4,5},{5,6},{6,7},{8,9},{9,10},{10,11},{11... | collective-permute-start | bytes 98312 | tf_op jit(solution)/shard_map/ppermute | solution.py:397
  62.0 2.9 %collective-permute-start.5 = (bf16[272,128]{1,0:T(8,128)(2,1)S(1)}, bf16[272,128]{1,0:T(8,128)(2,1)S(1)}, u32[]{:S(2)}, u32[]{:S(2)}) collective-permute-start(bf16[272,128]{1,0:T(8,128)(2,1)S(1)} %fusion.7), channel_id=1, source_target_pairs={{0,2},{1,3},{2,0},{3,1},{4,6},{5,7},{6,4},{7,5},{8,10},{9,11},{10,... | collective-permute-start | bytes 208904 | tf_op jit(solution)/shard_map/ppermute | solution.py:340
  64.9 1.0 fusion.4
  65.9 0.1 collective-permute-start.15
  66.0 1.7 %collective-permute-done.5 = bf16[272,128]{1,0:T(8,128)(2,1)S(1)} collective-permute-done((bf16[272,128]{1,0:T(8,128)(2,1)S(1)}, bf16[272,128]{1,0:T(8,128)(2,1)S(1)}, u32[]{:S(2)}, u32[]{:S(2)}) %collective-permute-start.5) | collective-permute-done | bytes 69664 | tf_op jit(solution)/shard_map/ppermute | solution.py:340
  67.7 3.2 %collective-permute-start.6 = (bf16[272,128]{1,0:T(8,128)(2,1)S(1)}, bf16[272,128]{1,0:T(8,128)(2,1)S(1)}, u32[]{:S(2)}, u32[]{:S(2)}) collective-permute-start(bf16[272,128]{1,0:T(8,128)(2,1)S(1)} %fusion.9), channel_id=1, source_target_pairs={{0,4},{1,5},{2,6},{3,7},{4,0},{5,1},{6,2},{7,3},{8,12},{9,13},{10,... | collective-permute-start | bytes 208904 | tf_op jit(solution)/shard_map/ppermute | solution.py:340
  71.0 0.9 fusion.6
  71.9 2.4 %collective-permute-start.16 = (bf16[272,128]{1,0:T(8,128)(2,1)S(1)}, bf16[272,128]{1,0:T(8,128)(2,1)S(1)}, u32[]{:S(2)}, u32[]{:S(2)}) collective-permute-start(bf16[272,128]{1,0:T(8,128)(2,1)S(1)} %fusion.6), channel_id=1, source_target_pairs={{0,4},{1,5},{2,6},{3,7},{4,0},{5,1},{6,2},{7,3},{8,12},{9,13},{10,... | collective-permute-start | bytes 208904 | tf_op jit(solution)/shard_map/ppermute | solution.py:340
  74.3 0.7 collective-permute-done.6
  75.1 0.1 collective-permute-start.7
  75.1 2.3 %collective-permute-done.16 = bf16[272,128]{1,0:T(8,128)(2,1)S(1)} collective-permute-done((bf16[272,128]{1,0:T(8,128)(2,1)S(1)}, bf16[272,128]{1,0:T(8,128)(2,1)S(1)}, u32[]{:S(2)}, u32[]{:S(2)}) %collective-permute-start.16) | collective-permute-done | bytes 69664 | tf_op jit(solution)/shard_map/ppermute | solution.py:340
  77.5 1.2 %collective-permute-start.17 = (bf16[272,128]{1,0:T(8,128)(2,1)S(1)}, bf16[272,128]{1,0:T(8,128)(2,1)S(1)}, u32[]{:S(2)}, u32[]{:S(2)}) collective-permute-start(bf16[272,128]{1,0:T(8,128)(2,1)S(1)} %add_convert_fusion.2), channel_id=1, source_target_pairs={{0,2},{1,3},{2,0},{3,1},{4,6},{5,7},{6,4},{7,5},{8,10},{9,11},{10,... | collective-permute-start | bytes 208904 | tf_op jit(solution)/shard_map/ppermute | solution.py:340
  78.7 0.7 collective-permute-done.7
  79.5 1.7 %collective-permute-start.10 = (bf16[2,272,128]{2,1,0:T(8,128)(2,1)S(1)}, bf16[2,272,128]{2,1,0:T(8,128)(2,1)S(1)}, u32[]{:S(2)}, u32[]{:S(2)}) collective-permute-start(bf16[2,272,128]{2,1,0:T(8,128)(2,1)S(1)} %pad_maximum_fusion.2), channel_id=1, source_target_pairs={{0,1},{1,0},{2,3},{3,2},{4,5},{5,4},{6,7},{7,6},{8,9},{9,8},{10,11... | collective-permute-start | bytes 417800 | tf_op jit(solution)/shard_map/ppermute | solution.py:340
  81.2 0.7 collective-permute-done.17
  81.9 0.7 collective-permute-start.18
  82.6 2.0 %collective-permute-done.10 = bf16[2,272,128]{2,1,0:T(8,128)(2,1)S(1)} collective-permute-done((bf16[2,272,128]{2,1,0:T(8,128)(2,1)S(1)}, bf16[2,272,128]{2,1,0:T(8,128)(2,1)S(1)}, u32[]{:S(2)}, u32[]{:S(2)}) %collective-permute-start.10) | collective-permute-done | bytes 139296 | tf_op jit(solution)/shard_map/ppermute | solution.py:340
  84.6 0.7 collective-permute-start.11
  85.3 1.7 %collective-permute-done.18 = bf16[2,272,128]{2,1,0:T(8,128)(2,1)S(1)} collective-permute-done((bf16[2,272,128]{2,1,0:T(8,128)(2,1)S(1)}, bf16[2,272,128]{2,1,0:T(8,128)(2,1)S(1)}, u32[]{:S(2)}, u32[]{:S(2)}) %collective-permute-start.18) | collective-permute-done | bytes 139296 | tf_op jit(solution)/shard_map/ppermute | solution.py:340
  87.1 1.7 %collective-permute-start.19 = (bf16[2,2,272,128]{3,2,1,0:T(8,128)(2,1)S(1)}, bf16[2,2,272,128]{3,2,1,0:T(8,128)(2,1)S(1)}, u32[]{:S(2)}, u32[]{:S(2)}) collective-permute-start(bf16[2,2,272,128]{3,2,1,0:T(8,128)(2,1)S(1)} %pad_maximum_fusion.1.a_own), channel_id=1, source_target_pairs={{0,1},{1,0},{2,3},{3,2},{4,5},{5,4},{6,7},{7,6},{8,9},{9,8},{10,11... | collective-permute-start | bytes 835592 | tf_op jit(solution)/shard_map/ppermute | solution.py:340
  88.8 2.5 %shard_map.127 = (bf16[2,128,512]{2,1,0:T(8,128)(2,1)}, bf16[2,128,512]{2,1,0:T(8,128)(2,1)}) custom-call(bf16[4,2,2,32,512]{4,3,2,1,0:T(8,128)(2,1)S(1)} %all-to-all-done.1.got, bf16[2,16,512]{2,1,0:T(8,128)(2,1)S(1)} %collective-permute-done.8.before, bf16[2,16,512]{2,1,0:T(8,128)(2,1)S(1)} %collective-permute-done.9.after, ...), custom_call_target="tpu_custom_call" | custom-call | tf_op jit(solution)/shard_map/pallas_call | solution.py:301
  91.2 0.5 collective-permute-start.20
  91.8 1.9 %collective-permute-done.19.a_far = bf16[2,2,272,128]{3,2,1,0:T(8,128)(2,1)S(1)} collective-permute-done((bf16[2,2,272,128]{3,2,1,0:T(8,128)(2,1)S(1)}, bf16[2,2,272,128]{3,2,1,0:T(8,128)(2,1)S(1)}, u32[]{:S(2)}, u32[]{:S(2)}) %collective-permute-start.19) | collective-permute-done | bytes 278560 | tf_op jit(solution)/shard_map/ppermute | solution.py:340
  93.7 1.5 %collective-permute-done.22.a_other_far = bf16[2,2,272,128]{3,2,1,0:T(8,128)(2,1)S(1)} collective-permute-done((bf16[2,2,272,128]{3,2,1,0:T(8,128)(2,1)S(1)}, bf16[2,2,272,128]{3,2,1,0:T(8,128)(2,1)S(1)}, u32[]{:S(2)}, u32[]{:S(2)}) %collective-permute-start.22) | collective-permute-done | bytes 278560 | tf_op jit(solution)/shard_map/ppermute | solution.py:340
  95.2 3.2 %shard_map.128 = (f32[31,512]{1,0:T(8,128)}, f32[512,512]{1,0:T(8,128)}, f32[512,512]{1,0:T(8,128)}, f32[512,512]{1,0:T(8,128)}, f32[512,512]{1,0:T(8,128)}) custom-call(s32[4]{0:T(128)S(1)} %pad_add_fusion.bits, bf16[2,2,272,128]{3,2,1,0:T(8,128)(2,1)S(1)} %pad_maximum_fusion.1.a_own, bf16[2,2,272,128]{3,2,1,0:T(8,128)(2,1)S(1)} %pad_maximum_fusion.b_own, ...), custom_call_target="tpu_custom_call" | custom-call | tf_op jit(solution)/shard_map/pallas_call | solution.py:301
  (41 shorter events, 0.4 us)
Async XLA Ops:
  1.8 18.5 %copy-start.2 = (bf16[512,512]{1,0:T(8,128)(2,1)S(1)}, bf16[512,512]{1,0:T(8,128)(2,1)}, u32[]{:S(2)}) copy-start(bf16[512,512]{1,0:T(8,128)(2,1)} %wk_hbm.1) | copy-start | bytes 1572868
  1.8 18.5 %copy-start.3 = (bf16[512,512]{1,0:T(8,128)(2,1)S(1)}, bf16[512,512]{1,0:T(8,128)(2,1)}, u32[]{:S(2)}) copy-start(bf16[512,512]{1,0:T(8,128)(2,1)} %wv_hbm.1) | copy-start | bytes 1572868
  14.8 5.5 %copy-start.1 = (bf16[512,512]{1,0:T(8,128)(2,1)S(1)}, bf16[512,512]{1,0:T(8,128)(2,1)}, u32[]{:S(2)}) copy-start(bf16[512,512]{1,0:T(8,128)(2,1)} %wq_hbm.1) | copy-start | bytes 1572868
  14.8 5.5 %copy-start.5 = (f32[31,512]{1,0:T(8,128)S(1)}, f32[31,512]{1,0:T(8,128)}, u32[]{:S(2)}) copy-start(f32[31,512]{1,0:T(8,128)} %kern.3) | copy-start | bytes 190468
  14.8 4.6 %collective-permute-start.1 = (bf16[4,2,16,512]{3,2,1,0:T(8,128)(2,1)S(1)}, bf16[4,2,16,512]{3,2,1,0:T(8,128)(2,1)S(1)}, u32[]{:S(2)}, u32[]{:S(2)}) collective-permute-start(bf16[4,2,16,512]{3,2,1,0:T(8,128)(2,1)S(1)} %get-tuple-element.49), channel_id=1, source_target_pairs={{8,0},{16,8},{24,16},{1,24},{9,1},{17,9},{25,17},{2,25},{10,2},{18... | collective-permute-start | bytes 393224 | tf_op jit(solution)/shard_map/ppermute | solution.py:333
  16.3 4.0 %collective-permute-start = (bf16[4,2,16,512]{3,2,1,0:T(8,128)(2,1)S(1)}, bf16[4,2,16,512]{3,2,1,0:T(8,128)(2,1)S(1)}, u32[]{:S(2)}, u32[]{:S(2)}) collective-permute-start(bf16[4,2,16,512]{3,2,1,0:T(8,128)(2,1)S(1)} %get-tuple-element.50), channel_id=1, source_target_pairs={{0,8},{8,16},{16,24},{24,1},{1,9},{9,17},{17,25},{25,2},{2,10},{10... | collective-permute-start | bytes 393224 | tf_op jit(solution)/shard_map/ppermute | solution.py:332
  20.3 1.0 %copy-start.4 = (bf16[512,512]{1,0:T(8,128)(2,1)S(1)}, bf16[512,512]{1,0:T(8,128)(2,1)}, u32[]{:S(2)}) copy-start(bf16[512,512]{1,0:T(8,128)(2,1)} %wo_hbm.1) | copy-start | bytes 1572868
  33.4 3.5 %collective-permute-start.2 = (bf16[2,2,2,272,128]{4,3,2,1,0:T(8,128)(2,1)}, bf16[2,2,2,272,128]{4,3,2,1,0:T(8,128)(2,1)S(1)}, u32[]{:S(2)}, u32[]{:S(2)}) collective-permute-start(bf16[2,2,2,272,128]{4,3,2,1,0:T(8,128)(2,1)} %get-tuple-element.28), channel_id=1, source_target_pairs={{0,8},{1,9},{2,10},{3,11},{4,12},{5,13},{6,14},{7,15},{8,0},{9,1},... | collective-permute-start | bytes 1671176 | tf_op jit(solution)/shard_map/ppermute | solution.py:340
  35.1 5.3 %collective-permute-start.12 = (bf16[2,2,2,272,128]{4,3,2,1,0:T(8,128)(2,1)}, bf16[2,2,2,272,128]{4,3,2,1,0:T(8,128)(2,1)S(1)}, u32[]{:S(2)}, u32[]{:S(2)}) collective-permute-start(bf16[2,2,2,272,128]{4,3,2,1,0:T(8,128)(2,1)} %get-tuple-element.40), channel_id=1, source_target_pairs={{0,8},{1,9},{2,10},{3,11},{4,12},{5,13},{6,14},{7,15},{8,0},{9,1},... | collective-permute-start | bytes 1671176 | tf_op jit(solution)/shard_map/ppermute | solution.py:340
  37.7 9.9 %collective-permute-start.3 = (bf16[2,2,272,128]{3,2,1,0:T(8,128)(2,1)}, bf16[2,2,272,128]{3,2,1,0:T(8,128)(2,1)S(1)}, u32[]{:S(2)}, u32[]{:S(2)}) collective-permute-start(bf16[2,2,272,128]{3,2,1,0:T(8,128)(2,1)} %fusion), channel_id=1, source_target_pairs={{0,16},{1,17},{2,18},{3,19},{4,20},{5,21},{6,22},{7,23},{8,24},{9,... | collective-permute-start | bytes 835592 | tf_op jit(solution)/shard_map/ppermute | solution.py:340
  41.2 10.6 %collective-permute-start.13 = (bf16[2,2,272,128]{3,2,1,0:T(8,128)(2,1)}, bf16[2,2,272,128]{3,2,1,0:T(8,128)(2,1)}, u32[]{:S(2)}, u32[]{:S(2)}) collective-permute-start(bf16[2,2,272,128]{3,2,1,0:T(8,128)(2,1)} %fusion.1), channel_id=1, source_target_pairs={{0,1},{1,0},{2,3},{3,2},{4,5},{5,4},{6,7},{7,6},{8,9},{9,8},{10,11... | collective-permute-start | bytes 835592 | tf_op jit(solution)/shard_map/ppermute | solution.py:340
  43.3 12.8 %all-to-all-start.1 = ((bf16[4,2,2,32,512]{4,3,2,1,0:T(8,128)(2,1)}), bf16[4,2,2,32,512]{4,3,2,1,0:T(8,128)(2,1)S(1)}, u32[]{:S(2)}, u32[]{:S(2)}) async-start(bf16[4,2,2,32,512]{4,3,2,1,0:T(8,128)(2,1)} %get-tuple-element.29), calls=%async_computation.1 | async-start | bytes 1048576 | tf_op jit(solution)/shard_map/all_to_all | solution.py:374
  48.3 7.8 %collective-permute-start.4 = (bf16[2,272,128]{2,1,0:T(8,128)(2,1)}, bf16[2,272,128]{2,1,0:T(8,128)(2,1)S(1)}, u32[]{:S(2)}, u32[]{:S(2)}) collective-permute-start(bf16[2,272,128]{2,1,0:T(8,128)(2,1)} %fusion.3), channel_id=1, source_target_pairs={{0,1},{1,0},{2,3},{3,2},{4,5},{5,4},{6,7},{7,6},{8,9},{9,8},{10,11... | collective-permute-start | bytes 417800 | tf_op jit(solution)/shard_map/ppermute | solution.py:340
  53.5 11.4 %collective-permute-start.14 = (bf16[2,272,128]{2,1,0:T(8,128)(2,1)}, bf16[2,272,128]{2,1,0:T(8,128)(2,1)S(1)}, u32[]{:S(2)}, u32[]{:S(2)}) collective-permute-start(bf16[2,272,128]{2,1,0:T(8,128)(2,1)} %fusion.2), channel_id=1, source_target_pairs={{0,16},{1,17},{2,18},{3,19},{4,20},{5,21},{6,22},{7,23},{8,24},{9,... | collective-permute-start | bytes 417800 | tf_op jit(solution)/shard_map/ppermute | solution.py:340
  56.1 23.4 %collective-permute-start.9 = (bf16[2,16,512]{2,1,0:T(8,128)(2,1)S(1)}, bf16[2,16,512]{2,1,0:T(8,128)(2,1)S(1)}, u32[]{:S(2)}, u32[]{:S(2)}) collective-permute-start(bf16[2,16,512]{2,1,0:T(8,128)(2,1)S(1)} %get-tuple-element.47), channel_id=1, source_target_pairs={{1,0},{2,1},{3,2},{4,3},{5,4},{6,5},{7,6},{9,8},{10,9},{11,10},{12... | collective-permute-start | bytes 98312 | tf_op jit(solution)/shard_map/ppermute | solution.py:398
  57.4 22.1 %collective-permute-start.8 = (bf16[2,16,512]{2,1,0:T(8,128)(2,1)S(1)}, bf16[2,16,512]{2,1,0:T(8,128)(2,1)S(1)}, u32[]{:S(2)}, u32[]{:S(2)}) collective-permute-start(bf16[2,16,512]{2,1,0:T(8,128)(2,1)S(1)} %get-tuple-element.48), channel_id=1, source_target_pairs={{0,1},{1,2},{2,3},{3,4},{4,5},{5,6},{6,7},{8,9},{9,10},{10,11},{11... | collective-permute-start | bytes 98312 | tf_op jit(solution)/shard_map/ppermute | solution.py:397
  62.0 5.7 %collective-permute-start.5 = (bf16[272,128]{1,0:T(8,128)(2,1)S(1)}, bf16[272,128]{1,0:T(8,128)(2,1)S(1)}, u32[]{:S(2)}, u32[]{:S(2)}) collective-permute-start(bf16[272,128]{1,0:T(8,128)(2,1)S(1)} %fusion.7), channel_id=1, source_target_pairs={{0,2},{1,3},{2,0},{3,1},{4,6},{5,7},{6,4},{7,5},{8,10},{9,11},{10,... | collective-permute-start | bytes 208904 | tf_op jit(solution)/shard_map/ppermute | solution.py:340
  64.9 1.0 copy-start.6
  65.9 5.1 %collective-permute-start.15 = (bf16[272,128]{1,0:T(8,128)(2,1)S(1)}, bf16[272,128]{1,0:T(8,128)(2,1)S(1)}, u32[]{:S(2)}, u32[]{:S(2)}) collective-permute-start(bf16[272,128]{1,0:T(8,128)(2,1)S(1)} %fusion.4), channel_id=1, source_target_pairs={{0,2},{1,3},{2,0},{3,1},{4,6},{5,7},{6,4},{7,5},{8,10},{9,11},{10,... | collective-permute-start | bytes 208904 | tf_op jit(solution)/shard_map/ppermute | solution.py:340
  66.0 5.0 %copy-start.7 = (bf16[2,272,128]{2,1,0:T(8,128)(2,1)S(1)}, bf16[2,272,128]{2,1,0:T(8,128)(2,1)}, u32[]{:S(2)}) copy-start(bf16[2,272,128]{2,1,0:T(8,128)(2,1)} %copy-done.6) | copy-start | bytes 417796
  67.7 7.3 %collective-permute-start.6 = (bf16[272,128]{1,0:T(8,128)(2,1)S(1)}, bf16[272,128]{1,0:T(8,128)(2,1)S(1)}, u32[]{:S(2)}, u32[]{:S(2)}) collective-permute-start(bf16[272,128]{1,0:T(8,128)(2,1)S(1)} %fusion.9), channel_id=1, source_target_pairs={{0,4},{1,5},{2,6},{3,7},{4,0},{5,1},{6,2},{7,3},{8,12},{9,13},{10,... | collective-permute-start | bytes 208904 | tf_op jit(solution)/shard_map/ppermute | solution.py:340
  71.9 5.6 %collective-permute-start.16 = (bf16[272,128]{1,0:T(8,128)(2,1)S(1)}, bf16[272,128]{1,0:T(8,128)(2,1)S(1)}, u32[]{:S(2)}, u32[]{:S(2)}) collective-permute-start(bf16[272,128]{1,0:T(8,128)(2,1)S(1)} %fusion.6), channel_id=1, source_target_pairs={{0,4},{1,5},{2,6},{3,7},{4,0},{5,1},{6,2},{7,3},{8,12},{9,13},{10,... | collective-permute-start | bytes 208904 | tf_op jit(solution)/shard_map/ppermute | solution.py:340
  75.1 4.4 %collective-permute-start.7 = (bf16[272,128]{1,0:T(8,128)(2,1)S(1)}, bf16[272,128]{1,0:T(8,128)(2,1)S(1)}, u32[]{:S(2)}, u32[]{:S(2)}) collective-permute-start(bf16[272,128]{1,0:T(8,128)(2,1)S(1)} %add_convert_fusion.3), channel_id=1, source_target_pairs={{0,2},{1,3},{2,0},{3,1},{4,6},{5,7},{6,4},{7,5},{8,10},{9,11},{10,... | collective-permute-start | bytes 208904 | tf_op jit(solution)/shard_map/ppermute | solution.py:340
  77.5 4.4 %collective-permute-start.17 = (bf16[272,128]{1,0:T(8,128)(2,1)S(1)}, bf16[272,128]{1,0:T(8,128)(2,1)S(1)}, u32[]{:S(2)}, u32[]{:S(2)}) collective-permute-start(bf16[272,128]{1,0:T(8,128)(2,1)S(1)} %add_convert_fusion.2), channel_id=1, source_target_pairs={{0,2},{1,3},{2,0},{3,1},{4,6},{5,7},{6,4},{7,5},{8,10},{9,11},{10,... | collective-permute-start | bytes 208904 | tf_op jit(solution)/shard_map/ppermute | solution.py:340
  79.5 5.1 %collective-permute-start.10 = (bf16[2,272,128]{2,1,0:T(8,128)(2,1)S(1)}, bf16[2,272,128]{2,1,0:T(8,128)(2,1)S(1)}, u32[]{:S(2)}, u32[]{:S(2)}) collective-permute-start(bf16[2,272,128]{2,1,0:T(8,128)(2,1)S(1)} %pad_maximum_fusion.2), channel_id=1, source_target_pairs={{0,1},{1,0},{2,3},{3,2},{4,5},{5,4},{6,7},{7,6},{8,9},{9,8},{10,11... | collective-permute-start | bytes 417800 | tf_op jit(solution)/shard_map/ppermute | solution.py:340
  81.9 5.1 %collective-permute-start.18 = (bf16[2,272,128]{2,1,0:T(8,128)(2,1)S(1)}, bf16[2,272,128]{2,1,0:T(8,128)(2,1)S(1)}, u32[]{:S(2)}, u32[]{:S(2)}) collective-permute-start(bf16[2,272,128]{2,1,0:T(8,128)(2,1)S(1)} %get-tuple-element.52), channel_id=1, source_target_pairs={{0,16},{1,17},{2,18},{3,19},{4,20},{5,21},{6,22},{7,23},{8,24},{9,... | collective-permute-start | bytes 417800 | tf_op jit(solution)/shard_map/ppermute | solution.py:340
  84.6 7.1 %collective-permute-start.11 = (bf16[2,2,272,128]{3,2,1,0:T(8,128)(2,1)S(1)}, bf16[2,2,272,128]{3,2,1,0:T(8,128)(2,1)S(1)}, u32[]{:S(2)}, u32[]{:S(2)}) collective-permute-start(bf16[2,2,272,128]{3,2,1,0:T(8,128)(2,1)S(1)} %pad_maximum_fusion.b_own), channel_id=1, source_target_pairs={{0,16},{1,17},{2,18},{3,19},{4,20},{5,21},{6,22},{7,23},{8,24},{9,... | collective-permute-start | bytes 835592 | tf_op jit(solution)/shard_map/ppermute | solution.py:340
  87.0 1.8 %copy-start = (bf16[2,128,512]{2,1,0:T(8,128)(2,1)S(1)}, bf16[2,128,512]{2,1,0:T(8,128)(2,1)}, u32[]{:S(2)}) copy-start(bf16[2,128,512]{2,1,0:T(8,128)(2,1)} %cot.1) | copy-start | bytes 786436
  87.1 6.6 %collective-permute-start.19 = (bf16[2,2,272,128]{3,2,1,0:T(8,128)(2,1)S(1)}, bf16[2,2,272,128]{3,2,1,0:T(8,128)(2,1)S(1)}, u32[]{:S(2)}, u32[]{:S(2)}) collective-permute-start(bf16[2,2,272,128]{3,2,1,0:T(8,128)(2,1)S(1)} %pad_maximum_fusion.1.a_own), channel_id=1, source_target_pairs={{0,1},{1,0},{2,3},{3,2},{4,5},{5,4},{6,7},{7,6},{8,9},{9,8},{10,11... | collective-permute-start | bytes 835592 | tf_op jit(solution)/shard_map/ppermute | solution.py:340
  91.2 2.4 %collective-permute-start.21 = (bf16[2,2,272,128]{3,2,1,0:T(8,128)(2,1)S(1)}, bf16[2,2,272,128]{3,2,1,0:T(8,128)(2,1)S(1)}, u32[]{:S(2)}, u32[]{:S(2)}) collective-permute-start(bf16[2,2,272,128]{3,2,1,0:T(8,128)(2,1)S(1)} %pad_maximum_fusion.b_own), channel_id=1, source_target_pairs={{0,8},{1,9},{2,10},{3,11},{4,12},{5,13},{6,14},{7,15},{8,0},{9,1},... | collective-permute-start | bytes 835592 | tf_op jit(solution)/shard_map/ppermute | solution.py:340
  91.2 2.4 %collective-permute-start.20 = (bf16[2,2,272,128]{3,2,1,0:T(8,128)(2,1)S(1)}, bf16[2,2,272,128]{3,2,1,0:T(8,128)(2,1)S(1)}, u32[]{:S(2)}, u32[]{:S(2)}) collective-permute-start(bf16[2,2,272,128]{3,2,1,0:T(8,128)(2,1)S(1)} %pad_maximum_fusion.1.a_own), channel_id=1, source_target_pairs={{0,8},{1,9},{2,10},{3,11},{4,12},{5,13},{6,14},{7,15},{8,0},{9,1},... | collective-permute-start | bytes 835592 | tf_op jit(solution)/shard_map/ppermute | solution.py:340
  91.8 1.9 %collective-permute-start.23 = (bf16[2,2,272,128]{3,2,1,0:T(8,128)(2,1)S(1)}, bf16[2,2,272,128]{3,2,1,0:T(8,128)(2,1)S(1)}, u32[]{:S(2)}, u32[]{:S(2)}) collective-permute-start(bf16[2,2,272,128]{3,2,1,0:T(8,128)(2,1)S(1)} %collective-permute-done.11.b_far), channel_id=1, source_target_pairs={{0,8},{1,9},{2,10},{3,11},{4,12},{5,13},{6,14},{7,15},{8,0},{9,1},... | collective-permute-start | bytes 835592 | tf_op jit(solution)/shard_map/ppermute | solution.py:340
  93.7 1.6 %collective-permute-start.22 = (bf16[2,2,272,128]{3,2,1,0:T(8,128)(2,1)S(1)}, bf16[2,2,272,128]{3,2,1,0:T(8,128)(2,1)S(1)}, u32[]{:S(2)}, u32[]{:S(2)}) collective-permute-start(bf16[2,2,272,128]{3,2,1,0:T(8,128)(2,1)S(1)} %collective-permute-done.19.a_far), channel_id=1, source_target_pairs={{0,8},{1,9},{2,10},{3,11},{4,12},{5,13},{6,14},{7,15},{8,0},{9,1},... | collective-permute-start | bytes 835592 | tf_op jit(solution)/shard_map/ppermute | solution.py:340

commit v5 on v4

v5 whole, which is shorter than its diff:
```python
import functools
import math

import jax
import jax.numpy as jnp
from jax import lax
from jax.experimental import pallas as pl
from jax.experimental.pallas import tpu as pltpu
from jax.sharding import PartitionSpec as P

HEADS = 8
LANES = 128
HALO = 16
NT = (((1,), (1,)), ((), ()))
TN = (((0,), (0,)), ((), ()))
BF = jnp.bfloat16
F32 = jnp.float32
MIB = 1024 * 1024
CORE, Y, X, Z, ODD, SKIP, BLOCK_AT = range(7)


def mm(left, right, dims=(((1,), (0,)), ((), ()))):
    return lax.dot_general(left, right, dims, preferred_element_type=F32)


def rolled(x, shift):
    return x if shift == 0 else pltpu.roll(x, x.shape[0] - shift, axis=0)


def window(x, taps, rows):
    acc = None
    for r in range(8):
        xr = rolled(x, r)
        for k in range(4):
            o = 8 * k + r
            if o == 0:
                continue
            term = xr[8 * k : 8 * k + rows] * taps(o)
            acc = term if acc is None else acc + term
    return acc


def sigmoid(v):
    return 0.5 * jnp.tanh(0.5 * v) + 0.5


def scatter_kernel(plan, bits, frames, cot, *refs):
    sub, outs, sems = plan, refs[:8], refs[8]
    copies = []
    for i, source in enumerate((frames, cot)):
        for d in range(4):
            rows = pl.ds(pl.multiple_of(bits[BLOCK_AT + d] * sub, sub), sub)
            n = 4 * i + d
            copies.append(pltpu.make_async_copy(source.at[:, rows], outs[n], sems.at[n]))
    for copy in copies:
        copy.start()
    for copy in copies:
        copy.wait()


def edge_kernel(sub, bits, f0, f1, f2, f3, near, side):
    odd = bits[ODD]
    for d, f in enumerate((f0, f1, f2, f3)):
        last = sub - HALO
        near[d] = f[:, pl.ds(pl.multiple_of((1 - odd) * last, HALO), HALO), :]
        side[d] = f[:, pl.ds(pl.multiple_of(odd * last, HALO), HALO), :]


def main_kernel(
    plan, bits, f0, f1, f2, f3, c0, c1, c2, c3, near, side, kern, wq, wk, wv, wo,
    a_keep, b_keep, a_send, b_send, back_keep,
    frame_s, conv_s, left_s, right_s, q_s, k_s, v_s, u_s, dconv_s, tap_s,
):
    groups, count, sub, width, factor = plan
    mics = groups * count
    cuts = sub // HALO
    block = mics * HALO
    rows = cuts * block
    cols = width // LANES
    odd, skip = bits[ODD], bits[SKIP]
    is_odd = jnp.broadcast_to(odd, (HALO, LANES)) == 1

    for d, (f, cot) in enumerate(((f0, c0), (f1, c1), (f2, c2), (f3, c3))):
        frame_s[d] = f[...]
        for m in range(count):
            for c in range(cuts):
                right_s[3, c, d, m] = cot[m, c * HALO : (c + 1) * HALO, :]

    def frames_window(a, m, lanes):
        one = near[a ^ 1, m, :, lanes].astype(F32)
        two = side[a ^ skip, m, :, lanes].astype(F32)
        return jnp.concatenate(
            [
                jnp.where(is_odd, one, two),
                frame_s[a, m, :, lanes].astype(F32),
                jnp.where(is_odd, two, one),
            ],
            axis=0,
        )

    def conv_step(n, _):
        a, m = n // count, n % count
        for lc in range(cols):
            lanes = slice(lc * LANES, (lc + 1) * LANES)
            conv = window(
                frames_window(a, m, lanes), lambda o: kern[o - 1 : o, lanes], sub
            )
            acted = (conv * sigmoid(conv)).astype(BF)
            for c in range(cuts):
                at = pl.multiple_of(c * block + n * HALO, HALO)
                conv_s[pl.ds(at, HALO), lanes] = conv[c * HALO : (c + 1) * HALO]
                left_s[0, pl.ds(at, HALO), lanes] = acted[c * HALO : (c + 1) * HALO]
        return 0

    lax.fori_loop(0, mics, conv_step, 0)

    def flat(i):
        return right_s[i].reshape(rows, width)

    def put(i, c, lanes, x):
        right_s[i, c, :, :, :, lanes] = x.astype(BF).reshape(groups, count, HALO, LANES)

    acted = left_s[0]
    q_s[...] = mm(acted, wq[...]).astype(BF)
    k_s[...] = mm(acted, wk[...]).astype(BF)
    v_s[...] = mm(acted, wv[...]).astype(BF)
    u_s[...] = mm(flat(3), wo[...], NT).astype(BF)

    depth = width // HEADS
    per = LANES // depth
    lane = lax.broadcasted_iota(jnp.int32, (block, LANES), 1)
    row_i = lax.broadcasted_iota(jnp.int32, (block, per * block), 0)
    col_i = lax.broadcasted_iota(jnp.int32, (block, per * block), 1)
    same = (row_i % HALO) == (col_i % HALO)

    def by_head(x):
        return jnp.concatenate(
            [jnp.where(lane // depth == h, x, jnp.zeros_like(x)) for h in range(per)], axis=0
        )

    def sums(x):
        return [
            jnp.sum(x[:, h * block : (h + 1) * block], axis=1, keepdims=True) for h in range(per)
        ]

    def each(x, values, op):
        return jnp.concatenate(
            [op(x[:, h * block : (h + 1) * block], values[h]) for h in range(per)], axis=1
        )

    def pick(x):
        out = x[:block]
        for h in range(1, per):
            out = jnp.where(lane // depth == h, x[h * block : (h + 1) * block], out)
        return out

    for c in range(cuts):
        part = slice(c * block, (c + 1) * block)
        for p in range(cols):
            lanes = slice(p * LANES, (p + 1) * LANES)
            q, u = q_s[part, lanes], u_s[part, lanes]
            kc, vc = by_head(k_s[part, lanes]), by_head(v_s[part, lanes])
            e = jnp.where(same, jnp.exp(mm(q, kc, NT) * factor), 0.0)
            w = each(e, [1.0 / x for x in sums(e)], lambda x, s: x * s)
            up = mm(u, vc, NT)
            inner = each(up, sums(w * up), lambda x, s: x - s) * w * factor
            wb, ib = w.astype(BF), inner.astype(BF)
            left_s[1, part, lanes] = mm(wb, vc).astype(BF)
            put(0, c, lanes, mm(ib, kc))
            put(1, c, lanes, pick(mm(ib, q, TN)))
            put(2, c, lanes, pick(mm(wb, u, TN)))

    dacted = mm(flat(0), wq[...], NT) + mm(flat(1), wk[...], NT) + mm(flat(2), wv[...], NT)
    conv = conv_s[...]
    sig = sigmoid(conv)
    dconv_s[...] = dacted * sig * (1.0 + conv * (1.0 - sig))

    for lc in range(cols):
        lanes = slice(lc * LANES, (lc + 1) * LANES)

        def tap_step(n, accs):
            a, m = n // count, n % count
            x = frames_window(a, m, lanes)
            d = jnp.concatenate(
                [
                    dconv_s[pl.ds(pl.multiple_of(c * block + n * HALO, HALO), HALO), lanes]
                    for c in range(cuts)
                ],
                axis=0,
            )
            out = list(accs)
            for r in range(8):
                xr = rolled(x, r)
                for k in range(4):
                    o = 8 * k + r
                    if o == 0:
                        continue
                    prod = xr[8 * k : 8 * k + sub] * d
                    out[o - 1] = out[o - 1] + jnp.sum(prod.reshape(sub // 8, 8, LANES), axis=0)
            return tuple(out)

        accs = lax.fori_loop(0, mics, tap_step, tuple(jnp.zeros((8, LANES), F32) for _ in range(31)))
        tap_s[lc * 32 : lc * 32 + 32, :] = jnp.concatenate(
            [jnp.sum(x, axis=0, keepdims=True) for x in accs] + [jnp.zeros((1, LANES), F32)], axis=0
        )

    tap_s[cols * 32 :, :] = jnp.zeros((HALO, LANES), F32)
    size = cols * width // 8
    span = size + HALO
    core, y, x, z = bits[CORE], bits[Y], bits[X], bits[Z]
    for out, owner, h in (
        (a_send, 1 - core, 0), (b_send, 1 - core, 1), (a_keep, core, 0), (b_keep, core, 1)
    ):
        i = owner * 2 + h
        first, second = (x, y) if h == 0 else (y, x)
        grad = mm(left_s[i // 3], flat(i), TN).astype(BF)
        for piece in range(8):
            cb, at = piece * size // width, piece * size % width
            tail = tap_s[pl.ds(pl.multiple_of((i * 8 + piece) * cols, cols), HALO), :]
            rel = ((piece // 4) ^ first) * 4 + ((piece // 2 % 2) ^ second) * 2 + ((piece % 2) ^ z)
            start = pl.multiple_of(rel * span, HALO)
            out[pl.ds(start, size), :] = grad[at : at + size, cb * LANES : (cb + 1) * LANES]
            out[pl.ds(pl.multiple_of(start + size, HALO), HALO), :] = tail.astype(BF)

    proj = mm(left_s[1], wo[...])
    unit = 2 * count * cols * sub
    for d, (out, base) in enumerate(
        ((back_keep, 0), (b_send, 8 * span), (back_keep, unit), (b_send, 8 * span + unit))
    ):
        for m in range(count):
            for c in range(cuts):
                at = c * block + (d * count + m) * HALO
                part = slice(c * HALO, (c + 1) * HALO)
                layer = (frame_s[d, m, part, :].astype(F32) + proj[at : at + HALO]).astype(BF)
                dconv = dconv_s[at : at + HALO, :].astype(BF)
                for lc in range(cols):
                    for kind, value in enumerate((layer, dconv)):
                        to = base + ((kind * count + m) * cols + lc) * sub + c * HALO
                        out[to : to + HALO, :] = value[:, lc * LANES : (lc + 1) * LANES]


def total(*parts):
    return functools.reduce(lambda x, y: x + y, [x.astype(F32) for x in parts]).astype(BF)


def final_kernel(
    plan, bits, a_own, b_own, a_far, b_far, a_other, b_other, a_other_far, b_other_far, taps, *refs
):
    width, norm = plan
    outs, tap_s = refs[:4], refs[4]
    cols = width // LANES
    size = cols * width // 8
    span = size + HALO
    core, y, x, z = bits[CORE], bits[Y], bits[X], bits[Z]

    def emit(which, parts):
        for h in range(2):
            i = 2 * which + h
            first, second = (x, y) if h == 0 else (y, x)
            for rel in range(8):
                part, start = parts[rel // 4][h], rel % 4 * span
                piece = (first ^ (rel // 4)) * 4 + (second ^ (rel // 2 % 2)) * 2 + (z ^ (rel % 2))
                cb, at = piece * size // width, piece * size % width
                outs[i][
                    pl.ds(pl.multiple_of(at, size), size),
                    pl.ds(pl.multiple_of(cb * LANES, LANES), LANES),
                ] = part[start : start + size, :].astype(F32) * norm
                tap_s[i * 8 + piece] = part[start + size : start + span, :].astype(F32) * norm

    for which in range(2):
        @pl.when(core == which)
        def _():
            emit(which, ((a_own, b_own), (a_far, b_far)))
            emit(1 - which, ((a_other, b_other), (a_other_far, b_other_far)))

    for g in range(32):
        row = g * cols
        lc, j = row // 32, row % 32
        kept = min(cols, 31 - j)
        taps[j : j + kept, lc * LANES : (lc + 1) * LANES] = tap_s[g, 0:kept]


def home_kernel(plan, bits, own, core_got, y_got, layer_out, dconv, x_edge, z_edge):
    count, sub, cols, core_at, y_at = plan
    unit = 2 * count * cols * sub
    odd = bits[X]
    last = 3 * sub + sub - HALO
    for d, (ref, base) in enumerate(
        ((own, 0), (core_got, core_at), (y_got, y_at), (y_got, y_at + unit))
    ):
        to = pl.ds(pl.multiple_of(bits[BLOCK_AT + d] * sub, sub), sub)
        for m in range(count):
            for lc in range(cols):
                at = base + (m * cols + lc) * sub
                layer_out[m, to, lc * LANES : (lc + 1) * LANES] = ref[at : at + sub, :]
                at += count * cols * sub
                dconv[m, lc, to, :] = ref[at : at + sub, :]
    for m in range(count):
        for lc in range(cols):
            at = (m * cols + lc) * HALO
            x_rows = pl.ds(pl.multiple_of((1 - odd) * last, HALO), HALO)
            z_rows = pl.ds(pl.multiple_of(odd * last, HALO), HALO)
            x_edge[at : at + HALO, :] = dconv[m, lc, x_rows, :]
            z_edge[at : at + HALO, :] = dconv[m, lc, z_rows, :]


def frame_kernel(plan, bits, dconv, x_got, z_got, cot, kern, frame_grad):
    count, cols, x_at, length = plan
    is_odd = jnp.broadcast_to(bits[X], (HALO, LANES)) == 1

    def step(m, _):
        for lc in range(cols):
            lanes = slice(lc * LANES, (lc + 1) * LANES)
            at = pl.multiple_of((m * cols + lc) * HALO, HALO)
            one = x_got[pl.ds(pl.multiple_of(x_at + at, HALO), HALO), :].astype(F32)
            two = z_got[pl.ds(at, HALO), :].astype(F32)
            x = jnp.concatenate(
                [
                    jnp.where(is_odd, one, two),
                    dconv[m, lc].astype(F32),
                    jnp.where(is_odd, two, one),
                ],
                axis=0,
            )
            grad = window(x, lambda o: kern[31 - o : 32 - o, lanes], length)
            frame_grad[m, :, lanes] = (cot[m, :, lanes].astype(F32) + grad).astype(BF)
        return 0

    lax.fori_loop(0, count, step, 0)


def call(body, outs, scratch, limit, *args, space=pltpu.VMEM):
    return pl.pallas_call(
        body,
        out_shape=outs,
        in_specs=[
            pl.BlockSpec(memory_space=pltpu.SMEM if x.dtype == jnp.int32 else space)
            for x in args
        ],
        out_specs=jax.tree.map(lambda _: pl.BlockSpec(memory_space=space), outs),
        scratch_shapes=scratch,
        compiler_params=pltpu.CompilerParams(vmem_limit_bytes=limit * MIB),
    )(*args)


def shards(frames, cotangent, kernel, w_query, w_key, w_value, w_out):
    groups, blocks = lax.axis_size("mic"), lax.axis_size("tm")
    count, length, width = frames.shape
    sub = length // groups
    cuts = sub // HALO
    cols = width // LANES
    rows = groups * count * sub
    shape = jax.ShapeDtypeStruct

    mic, tm = lax.axis_index("mic"), lax.axis_index("tm")
    over_core, over_y, over_x, over_z = blocks, 2 * blocks, 1, 2

    def order(a):
        return (a ^ (a >> 1)) ^ (3 * (tm % 2))

    mine = order(mic)
    bits = jnp.stack(
        [mic % 2, mic // 2, tm % 2, tm // 2 % 2, mine % 2, 2 * ((mine + 1) // 2 % 2)]
        + [order(mic ^ d) for d in range(4)]
    ).astype(jnp.int32)

    def permute(x, pairs):
        return lax.ppermute(x, ("mic", "tm"), pairs)

    def swap(x, mask):
        return permute(x, [(f, f ^ mask) for f in range(groups * blocks)])

    def both(pairs):
        return pairs + [(j, i) for i, j in pairs]

    block = shape((count, sub, width), BF)
    parts = call(
        functools.partial(scatter_kernel, sub), (block,) * 8,
        [pltpu.SemaphoreType.DMA((8,))], 8, bits, frames, cotangent, space=pl.ANY,
    )
    masks = (0, over_core, over_y, over_core + over_y)
    got = {d: swap(parts[d], masks[d]) for d in (2, 3, 1)}
    f = [parts[0], got[1], got[2], got[3]]
    got = {d: swap(parts[4 + d], masks[d]) for d in (2, 3, 1)}
    c = [parts[4], got[1], got[2], got[3]]
    edge = shape((groups, count, HALO, width), BF)
    near, side = call(functools.partial(edge_kernel, sub), (edge, edge), [], 8, bits, *f)
    near = swap(near, over_core)
    side = permute(
        side,
        both([(blocks + t, 3 * blocks + t) for t in range(blocks)])
        + both([((2 - 2 * (t % 2)) * blocks + t, (2 - 2 * (t % 2)) * blocks + t + 1)
                for t in range(blocks - 1)]),
    )

    factor = 1.0 / math.sqrt(width // HEADS)
    size = width * width // LANES // 8
    span = size + HALO
    unit = 2 * count * cols * sub
    big = pltpu.VMEM((rows, width), BF)
    wide = pltpu.VMEM((rows, width), F32)

    def flat(n):
        return shape((n, LANES), BF)

    a_keep, b_keep, a_send, b_send, back_keep = call(
        functools.partial(main_kernel, (groups, count, sub, width, factor)),
        (flat(8 * span), flat(8 * span), flat(8 * span), flat(8 * span + 2 * unit), flat(2 * unit)),
        [
            pltpu.VMEM((groups, count, sub, width), BF),
            wide,
            pltpu.VMEM((2, rows, width), BF),
            pltpu.VMEM((4, cuts, groups, count, HALO, width), BF),
            big, big, big, big, wide,
            pltpu.VMEM((32 * cols + HALO, LANES), F32),
        ],
        24, bits, *f, *c, near, side, kernel, w_query, w_key, w_value, w_out,
    )

    def sent(parts, n):
        return total(*(t[n : 2 * n] for t in parts))

    def kept(parts, got, n):
        return [t[:n] for t in parts] + [got[:n]]

    def line_sum(parts):
        got = swap(sent(parts, span), over_z)
        mine = total(*kept(parts, got, span))
        mask = 2 * over_z
        while mask < blocks:
            mine = total(mine, swap(mine, mask))
            mask *= 2
        return mine

    a = [a_keep, swap(a_send, over_core)]
    core_got = swap(b_send, over_core)
    b = [b_keep, core_got]
    a = kept(a, swap(sent(a, 4 * span), over_x), 4 * span)
    y_got = swap(
        jnp.concatenate([sent(b, 4 * span), back_keep[unit:], core_got[8 * span + unit :]]), over_y
    )
    b = kept(b, y_got, 4 * span)
    a = kept(a, swap(sent(a, 2 * span), over_y), 2 * span)
    edge = flat(count * cols * HALO)
    layer_out, dconv, x_edge, z_edge = call(
        functools.partial(home_kernel, (count, sub, cols, 8 * span, 4 * span)),
        (shape(frames.shape, BF), shape((count, cols, length, LANES), BF), edge, edge),
        [], 8, bits, back_keep, core_got, y_got,
    )
    x_got = swap(jnp.concatenate([sent(b, 2 * span), x_edge]), over_x)
    b = kept(b, x_got, 2 * span)
    z_got = permute(
        z_edge,
        both([(m * blocks + t, m * blocks + t + 1)
              for m in range(groups) for t in range(1, blocks - 1, 2)]),
    )
    a, b = line_sum(a), line_sum(b)
    a = jnp.concatenate([a, swap(a, over_z)])
    b = jnp.concatenate([b, swap(b, over_z)])
    b, z_got = lax.optimization_barrier((b, z_got))
    frame_grad = call(
        functools.partial(frame_kernel, (count, cols, 2 * span, length)),
        shape(frames.shape, BF), [], 8, bits, dconv, x_got, z_got, cotangent, kernel,
    )
    a = jnp.concatenate([a, swap(a, over_y)])
    b = jnp.concatenate([b, swap(b, over_x)])
    a_far, b_far = swap(a, over_x), swap(b, over_y)
    a_other, b_other = swap(a, over_core), swap(b, over_core)
    b_far, frame_grad = lax.optimization_barrier((b_far, frame_grad))
    a_other_far, b_other_far = swap(a_far, over_core), swap(b_far, over_core)

    norm = 1.0 / math.sqrt(groups * count * blocks * length)
    square = shape((width, width), F32)
    grads = call(
        functools.partial(final_kernel, (width, norm)),
        (shape((31, width), F32), square, square, square, square),
        [pltpu.VMEM((32, HALO, LANES), F32)],
        16, bits, a, b, a_far, b_far, a_other, b_other, a_other_far, b_other_far,
    )
    return (layer_out, frame_grad, *grads)


def solution(mesh):
    in_specs = (P("mic", "tm", None), P("mic", "tm", None), P(), P(), P(), P(), P())
    out_specs = (P("mic", "tm", None), P("mic", "tm", None), P(), P(), P(), P(), P())
    return jax.shard_map(shards, mesh=mesh, in_specs=in_specs, out_specs=out_specs, check_vma=False)
```

time: 99 us -> 95.7 us (0.967)
  waiting for transfers between devices: 18.2 us -> 32.7 us
  blocking collectives: 13 us -> 0 us
  other arithmetic: 7.21 us -> 0.59 us
  local copies, waits for them, and re-layouts: 1.13 us -> 5.17 us
  starting transfers between devices: 40.3 us -> 36.8 us
  Pallas kernels: 17.7 us -> 19.2 us
    ppermute x24 -> x29, waiting for transfers between devices: 16.7 us -> 32.7 us  [permute(): return lax.ppermute(x, ('mic', 'tm'), pairs)]
    all_to_all x1 -> x0, blocking collectives: 13 us -> none  [shards(): got = lax.all_to_all(send.transpose(2, 0, 1, 3, 4), 'mic', 0, 0, tiled=True)]
    convert_element_type x10, other arithmetic: 5.97 us -> 0.5 us  [total(): functools.reduce(lambda x, y: x + y, [x.astype(F32) for x in parts])]
    unnamed x16 -> x17, local copies, waits for them, and re-layouts: 1.07 us -> 5.05 us
    all_to_all x1 -> x0, starting transfers between devices: 3.47 us -> none  [shards(): home = lax.all_to_all(back, 'mic', 0, 0, tiled=True)]
    pallas_call x3 -> x6, Pallas kernels: 17.7 us -> 19.2 us  [call(): pl.pallas_call(body, out_shape=outs, in_specs=[pl.BlockSpec(memory_space=...]
    all_to_all x1 -> x0, waiting for transfers between devices: 1.5 us -> none  [shards(): home = lax.all_to_all(back, 'mic', 0, 0, tiled=True)]
    transpose x1 -> x0, other arithmetic: 1.08 us -> none  [shards(): got = lax.all_to_all(send.transpose(2, 0, 1, 3, 4), 'mic', 0, 0, tiled=True)]
  transfers between devices with their start and end apart: 25 -> 29, of which waited for: 13 -> 16; matrix products, arithmetic and copies ran while one was open for 6% -> 1% of each run, Pallas kernels for 3% -> 4%
where the time goes in v5:
time: 95.7 us; the launch traced here: 95.4 us
  starting transfers between devices  36.8 us (38%)
  waiting for transfers between devices  32.7 us (34%)
  Pallas kernels  19.2 us (20%)
  local copies, waits for them, and re-layouts  5.17 us (5%)
    ppermute x29, starting transfers between devices, permute(): return lax.ppermute(x, ('mic', 'tm'), pairs)  36.8 us
    ppermute x29, waiting for transfers between devices, permute(): return lax.ppermute(x, ('mic', 'tm'), pairs)  32.7 us
    pallas_call x6, Pallas kernels, call(): pl.pallas_call(body, out_shape=outs, in_specs=[pl.BlockSpec(memory_space=...  19.2 us
    unnamed x17, local copies, waits for them, and re-layouts  5.05 us
  transfers between devices with their start and end apart: 29, of which 16 were waited for; matrix products, arithmetic and copies ran while one was open for 1% of the time, Pallas kernels for 4%

profile of v5, /device:TPU:0, one launch (start us, length us, event | category | flops | bytes accessed | tf_op | source)
XLA Modules:
  0.0 95.4 jit_solution(2788003177064779912)
XLA Ops:
  0.8 1.0 copy-done
  1.8 0.9 copy-done.6
  2.7 1.0 %shard_map.126 = (bf16[2,32,512]{2,1,0:T(8,128)(2,1)S(1)}, bf16[2,32,512]{2,1,0:T(8,128)(2,1)S(1)}, bf16[2,32,512]{2,1,0:T(8,128)(2,1)S(1)}, bf16[2,32,512]{2,1,...) custom-call(s32[10]{0:T(128)S(1)} %stack.43.bits, ...), custom_call_target="tpu_custom_call" | custom-call | tf_op jit(solution)/shard_map/pallas_call | solution.py:333
  3.7 0.5 collective-permute-start
  4.2 2.6 %collective-permute-start.1 = (bf16[2,32,512]{2,1,0:T(8,128)(2,1)S(1)}, bf16[2,32,512]{2,1,0:T(8,128)(2,1)S(1)}, u32[]{:S(2)}, u32[]{:S(2)}) collective-permute-start(bf16[2,32,512]{2,1,0:T(8,128)(2,1)S(1)} %get-tuple-element.37), channel_id=1, source_target_pairs={{0,16},{1,17},{2,18},{3,19},{4,20},{5,21},{6,22},{7,23},{8,24},{9,... | collective-permute-start | bytes 196616 | tf_op jit(solution)/shard_map/ppermute | solution.py:368
  6.9 2.6 %collective-permute-done.1.f2 = bf16[2,32,512]{2,1,0:T(8,128)(2,1)S(1)} collective-permute-done((bf16[2,32,512]{2,1,0:T(8,128)(2,1)S(1)}, bf16[2,32,512]{2,1,0:T(8,128)(2,1)S(1)}, u32[]{:S(2)}, u32[]{:S(2)}) %collective-permute-start.1) | collective-permute-done | bytes 65568 | tf_op jit(solution)/shard_map/ppermute | solution.py:368
  9.5 1.4 %collective-permute-done.2.f3 = bf16[2,32,512]{2,1,0:T(8,128)(2,1)S(1)} collective-permute-done((bf16[2,32,512]{2,1,0:T(8,128)(2,1)S(1)}, bf16[2,32,512]{2,1,0:T(8,128)(2,1)S(1)}, u32[]{:S(2)}, u32[]{:S(2)}) %collective-permute-start.2) | collective-permute-done | bytes 65568 | tf_op jit(solution)/shard_map/ppermute | solution.py:368
  10.9 0.6 shard_map.127
  11.7 0.7 collective-permute-start.7
  12.3 2.7 %collective-permute-start.3 = (bf16[2,32,512]{2,1,0:T(8,128)(2,1)S(1)}, bf16[2,32,512]{2,1,0:T(8,128)(2,1)S(1)}, u32[]{:S(2)}, u32[]{:S(2)}) collective-permute-start(bf16[2,32,512]{2,1,0:T(8,128)(2,1)S(1)} %get-tuple-element.40), channel_id=1, source_target_pairs={{0,8},{1,9},{2,10},{3,11},{4,12},{5,13},{6,14},{7,15},{8,0},{9,1},... | collective-permute-start | bytes 196616 | tf_op jit(solution)/shard_map/ppermute | solution.py:368
  15.1 1.6 %collective-permute-start.4 = (bf16[2,32,512]{2,1,0:T(8,128)(2,1)S(1)}, bf16[2,32,512]{2,1,0:T(8,128)(2,1)S(1)}, u32[]{:S(2)}, u32[]{:S(2)}) collective-permute-start(bf16[2,32,512]{2,1,0:T(8,128)(2,1)S(1)} %get-tuple-element.41), channel_id=1, source_target_pairs={{0,16},{1,17},{2,18},{3,19},{4,20},{5,21},{6,22},{7,23},{8,24},{9,... | collective-permute-start | bytes 196616 | tf_op jit(solution)/shard_map/ppermute | solution.py:368
  16.8 2.6 %collective-permute-done.4.c2 = bf16[2,32,512]{2,1,0:T(8,128)(2,1)S(1)} collective-permute-done((bf16[2,32,512]{2,1,0:T(8,128)(2,1)S(1)}, bf16[2,32,512]{2,1,0:T(8,128)(2,1)S(1)}, u32[]{:S(2)}, u32[]{:S(2)}) %collective-permute-start.4) | collective-permute-done | bytes 65568 | tf_op jit(solution)/shard_map/ppermute | solution.py:368
  19.4 1.4 %collective-permute-done.5.c3 = bf16[2,32,512]{2,1,0:T(8,128)(2,1)S(1)} collective-permute-done((bf16[2,32,512]{2,1,0:T(8,128)(2,1)S(1)}, bf16[2,32,512]{2,1,0:T(8,128)(2,1)S(1)}, u32[]{:S(2)}, u32[]{:S(2)}) %collective-permute-start.5) | collective-permute-done | bytes 65568 | tf_op jit(solution)/shard_map/ppermute | solution.py:368
  20.8 1.0 %copy-done.3 = bf16[512,512]{1,0:T(8,128)(2,1)S(1)} copy-done((bf16[512,512]{1,0:T(8,128)(2,1)S(1)}, bf16[512,512]{1,0:T(8,128)(2,1)}, u32[]{:S(2)}) %copy-start.3) | copy-done | bytes 524312
  21.8 1.0 %copy-done.4 = bf16[512,512]{1,0:T(8,128)(2,1)S(1)} copy-done((bf16[512,512]{1,0:T(8,128)(2,1)S(1)}, bf16[512,512]{1,0:T(8,128)(2,1)}, u32[]{:S(2)}) %copy-start.4) | copy-done | bytes 524312
  22.8 1.0 %copy-done.5 = bf16[512,512]{1,0:T(8,128)(2,1)S(1)} copy-done((bf16[512,512]{1,0:T(8,128)(2,1)S(1)}, bf16[512,512]{1,0:T(8,128)(2,1)}, u32[]{:S(2)}) %copy-start.5) | copy-done | bytes 524312
  23.9 10.3 %shard_map.128 = (bf16[2176,128]{1,0:T(8,128)(2,1)S(1)}, bf16[2176,128]{1,0:T(8,128)(2,1)S(1)}, bf16[2176,128]{1,0:T(8,128)(2,1)S(1)}, bf16[3200,128]{1,0:T(8,128)(2,1)S(1)}, bf16[1024,128]{1,0:T(8,128)(2,1)S(1)}) custom-call(s32[10]{0:T(128)S(1)} %stack.43.bits, bf16[2,32,512]{2,1,0:T(8,128)(2,1)S(1)} %get-tuple-element.35.f0, ...), custom_call_target="tpu_custom_call" | custom-call | tf_op jit(solution)/shard_map/pallas_call | solution.py:333
  34.5 0.4 collective-permute-start.17
  34.9 1.7 %collective-permute-done.8.core_got = bf16[3200,128]{1,0:T(8,128)(2,1)S(1)} collective-permute-done((bf16[3200,128]{1,0:T(8,128)(2,1)S(1)}, bf16[3200,128]{1,0:T(8,128)(2,1)S(1)}, u32[]{:S(2)}, u32[]{:S(2)}) %collective-permute-start.8) | collective-permute-done | bytes 819232 | tf_op jit(solution)/shard_map/ppermute | solution.py:368
  36.8 1.4 %collective-permute-start.9 = (bf16[2112,128]{1,0:T(8,128)(2,1)S(1)}, bf16[2112,128]{1,0:T(8,128)(2,1)S(1)}, u32[]{:S(2)}, u32[]{:S(2)}) collective-permute-start(bf16[2112,128]{1,0:T(8,128)(2,1)S(1)} %pad_maximum_fusion), channel_id=1, source_target_pairs={{0,16},{1,17},{2,18},{3,19},{4,20},{5,21},{6,22},{7,23},{8,24},{9,... | collective-permute-start | bytes 1622024 | tf_op jit(solution)/shard_map/ppermute | solution.py:368
  38.3 1.4 %collective-permute-start.18 = (bf16[1088,128]{1,0:T(8,128)(2,1)S(1)}, bf16[1088,128]{1,0:T(8,128)(2,1)S(1)}, u32[]{:S(2)}, u32[]{:S(2)}) collective-permute-start(bf16[1088,128]{1,0:T(8,128)(2,1)S(1)} %add_convert_fusion), channel_id=1, source_target_pairs={{0,1},{1,0},{2,3},{3,2},{4,5},{5,4},{6,7},{7,6},{8,9},{9,8},{10,11... | collective-permute-start | bytes 835592 | tf_op jit(solution)/shard_map/ppermute | solution.py:368
  39.7 7.2 %collective-permute-done.18 = bf16[1088,128]{1,0:T(8,128)(2,1)S(1)} collective-permute-done((bf16[1088,128]{1,0:T(8,128)(2,1)S(1)}, bf16[1088,128]{1,0:T(8,128)(2,1)S(1)}, u32[]{:S(2)}, u32[]{:S(2)}) %collective-permute-start.18) | collective-permute-done | bytes 278560 | tf_op jit(solution)/shard_map/ppermute | solution.py:368
  46.9 0.9 collective-permute-start.19
  47.9 4.1 %collective-permute-done.9.y_got = bf16[2112,128]{1,0:T(8,128)(2,1)S(1)} collective-permute-done((bf16[2112,128]{1,0:T(8,128)(2,1)S(1)}, bf16[2112,128]{1,0:T(8,128)(2,1)S(1)}, u32[]{:S(2)}, u32[]{:S(2)}) %collective-permute-start.9) | collective-permute-done | bytes 540704 | tf_op jit(solution)/shard_map/ppermute | solution.py:368
  52.0 1.3 %shard_map.129 = (bf16[2,128,512]{2,1,0:T(8,128)(2,1)}, bf16[2,4,128,128]{3,2,1,0:T(8,128)(2,1)S(1)}, bf16[128,128]{1,0:T(8,128)(2,1)S(1)}, bf16[128,128]{1,0:T(8,128)(2,1)S(1)}) custom-call(s32[10]{0:T(128)S(1)} %stack.43.bits, bf16[1024,128]{1,0:T(8,128)(2,1)S(1)} %get-tuple-element.45.own, bf16[3200,128]{1,0:T(8,128)(2,1)S(1)} %collective-permute-done.8.core_got, ...), custom_call_target="tpu_custom_call" | custom-call | tf_op jit(solution)/shard_map/pallas_call | solution.py:333
  53.3 1.5 %collective-permute-start.10 = (bf16[672,128]{1,0:T(8,128)(2,1)S(1)}, bf16[672,128]{1,0:T(8,128)(2,1)S(1)}, u32[]{:S(2)}, u32[]{:S(2)}) collective-permute-start(bf16[672,128]{1,0:T(8,128)(2,1)S(1)} %pad_maximum_fusion.2), channel_id=1, source_target_pairs={{0,1},{1,0},{2,3},{3,2},{4,5},{5,4},{6,7},{7,6},{8,9},{9,8},{10,11... | collective-permute-start | bytes 516104 | tf_op jit(solution)/shard_map/ppermute | solution.py:368
  54.9 1.7 %collective-permute-start.20 = (bf16[272,128]{1,0:T(8,128)(2,1)S(1)}, bf16[272,128]{1,0:T(8,128)(2,1)S(1)}, u32[]{:S(2)}, u32[]{:S(2)}) collective-permute-start(bf16[272,128]{1,0:T(8,128)(2,1)S(1)} %add_convert_fusion.6), channel_id=1, source_target_pairs={{0,2},{1,3},{2,0},{3,1},{4,6},{5,7},{6,4},{7,5},{8,10},{9,11},{10,... | collective-permute-start | bytes 208904 | tf_op jit(solution)/shard_map/ppermute | solution.py:368
  56.5 2.3 %collective-permute-done.10.x_got = bf16[672,128]{1,0:T(8,128)(2,1)S(1)} collective-permute-done((bf16[672,128]{1,0:T(8,128)(2,1)S(1)}, bf16[672,128]{1,0:T(8,128)(2,1)S(1)}, u32[]{:S(2)}, u32[]{:S(2)}) %collective-permute-start.10) | collective-permute-done | bytes 172064 | tf_op jit(solution)/shard_map/ppermute | solution.py:368
  58.8 1.7 %collective-permute-start.11 = (bf16[272,128]{1,0:T(8,128)(2,1)S(1)}, bf16[272,128]{1,0:T(8,128)(2,1)S(1)}, u32[]{:S(2)}, u32[]{:S(2)}) collective-permute-start(bf16[272,128]{1,0:T(8,128)(2,1)S(1)} %add_convert_fusion.9), channel_id=1, source_target_pairs={{0,2},{1,3},{2,0},{3,1},{4,6},{5,7},{6,4},{7,5},{8,10},{9,11},{10,... | collective-permute-start | bytes 208904 | tf_op jit(solution)/shard_map/ppermute | solution.py:368
  60.6 2.7 %collective-permute-start.21 = (bf16[272,128]{1,0:T(8,128)(2,1)S(1)}, bf16[272,128]{1,0:T(8,128)(2,1)S(1)}, u32[]{:S(2)}, u32[]{:S(2)}) collective-permute-start(bf16[272,128]{1,0:T(8,128)(2,1)S(1)} %add_convert_fusion.5), channel_id=1, source_target_pairs={{0,4},{1,5},{2,6},{3,7},{4,0},{5,1},{6,2},{7,3},{8,12},{9,13},{10,... | collective-permute-start | bytes 208904 | tf_op jit(solution)/shard_map/ppermute | solution.py:368
  63.3 3.4 %collective-permute-start.12 = (bf16[272,128]{1,0:T(8,128)(2,1)S(1)}, bf16[272,128]{1,0:T(8,128)(2,1)S(1)}, u32[]{:S(2)}, u32[]{:S(2)}) collective-permute-start(bf16[272,128]{1,0:T(8,128)(2,1)S(1)} %add_convert_fusion.8), channel_id=1, source_target_pairs={{0,4},{1,5},{2,6},{3,7},{4,0},{5,1},{6,2},{7,3},{8,12},{9,13},{10,... | collective-permute-start | bytes 208904 | tf_op jit(solution)/shard_map/ppermute | solution.py:368
  66.6 0.3 collective-permute-done.21
  67.0 0.9 collective-permute-start.22
  67.9 1.0 %collective-permute-done.12 = bf16[272,128]{1,0:T(8,128)(2,1)S(1)} collective-permute-done((bf16[272,128]{1,0:T(8,128)(2,1)S(1)}, bf16[272,128]{1,0:T(8,128)(2,1)S(1)}, u32[]{:S(2)}, u32[]{:S(2)}) %collective-permute-start.12) | collective-permute-done | bytes 69664 | tf_op jit(solution)/shard_map/ppermute | solution.py:368
  69.0 1.6 %collective-permute-start.13 = (bf16[272,128]{1,0:T(8,128)(2,1)S(1)}, bf16[272,128]{1,0:T(8,128)(2,1)S(1)}, u32[]{:S(2)}, u32[]{:S(2)}) collective-permute-start(bf16[272,128]{1,0:T(8,128)(2,1)S(1)} %add_convert_fusion.7), channel_id=1, source_target_pairs={{0,2},{1,3},{2,0},{3,1},{4,6},{5,7},{6,4},{7,5},{8,10},{9,11},{10,... | collective-permute-start | bytes 208904 | tf_op jit(solution)/shard_map/ppermute | solution.py:368
  70.6 0.8 collective-permute-done.22
  71.4 1.4 %collective-permute-start.23 = (bf16[544,128]{1,0:T(8,128)(2,1)S(1)}, bf16[544,128]{1,0:T(8,128)(2,1)S(1)}, u32[]{:S(2)}, u32[]{:S(2)}) collective-permute-start(bf16[544,128]{1,0:T(8,128)(2,1)S(1)} %pad_maximum_fusion.4), channel_id=1, source_target_pairs={{0,16},{1,17},{2,18},{3,19},{4,20},{5,21},{6,22},{7,23},{8,24},{9,... | collective-permute-start | bytes 417800 | tf_op jit(solution)/shard_map/ppermute | solution.py:368
  72.8 0.7 collective-permute-start.14
  73.4 0.3 collective-permute-done.13
  73.7 6.9 %collective-permute-start.15 = (bf16[544,128]{1,0:T(8,128)(2,1)S(1)}, bf16[544,128]{1,0:T(8,128)(2,1)S(1)}, u32[]{:S(2)}, u32[]{:S(2)}) collective-permute-start(bf16[544,128]{1,0:T(8,128)(2,1)S(1)} %pad_maximum_fusion.3), channel_id=1, source_target_pairs={{0,1},{1,0},{2,3},{3,2},{4,5},{5,4},{6,7},{7,6},{8,9},{9,8},{10,11... | collective-permute-start | bytes 417800 | tf_op jit(solution)/shard_map/ppermute | solution.py:368
  80.7 2.9 %collective-permute-done.15 = bf16[544,128]{1,0:T(8,128)(2,1)S(1)} collective-permute-done((bf16[544,128]{1,0:T(8,128)(2,1)S(1)}, bf16[544,128]{1,0:T(8,128)(2,1)S(1)}, u32[]{:S(2)}, u32[]{:S(2)}) %collective-permute-start.15) | collective-permute-done | bytes 139296 | tf_op jit(solution)/shard_map/ppermute | solution.py:368
  83.7 1.1 %collective-permute-start.16 = (bf16[1088,128]{1,0:T(8,128)(2,1)S(1)}, bf16[1088,128]{1,0:T(8,128)(2,1)S(1)}, u32[]{:S(2)}, u32[]{:S(2)}) collective-permute-start(bf16[1088,128]{1,0:T(8,128)(2,1)S(1)} %constant_dynamic-update-slice_fusion.b_own), channel_id=1, source_target_pairs={{0,16},{1,17},{2,18},{3,19},{4,20},{5,21},{6,22},{7,23},{8,24},{9,... | collective-permute-start | bytes 835592 | tf_op jit(solution)/shard_map/ppermute | solution.py:368
  84.8 2.5 %collective-permute-done.24.a_far = bf16[1088,128]{1,0:T(8,128)(2,1)S(1)} collective-permute-done((bf16[1088,128]{1,0:T(8,128)(2,1)S(1)}, bf16[1088,128]{1,0:T(8,128)(2,1)S(1)}, u32[]{:S(2)}, u32[]{:S(2)}) %collective-permute-start.24) | collective-permute-done | bytes 278560 | tf_op jit(solution)/shard_map/ppermute | solution.py:368
  87.3 2.8 %shard_map.130 = bf16[2,128,512]{2,1,0:T(8,128)(2,1)} custom-call(s32[10]{0:T(128)S(1)} %stack.43.bits, bf16[2,4,128,128]{3,2,1,0:T(8,128)(2,1)S(1)} %get-tuple-element.52.dconv, bf16[672,128]{1,0:T(8,128)(2,1)S(1)} %collective-permute-done.10.x_got, bf16[128,128]{1,0:T(8,128)(2,1)S(1)} %collective-permute-done.14.z_got, bf16[2,128,512]{2,1,0:T(8,128)(2,1)S(1)} %copy-done.1, ...), custom_call_target="tpu_custom_call" | custom-call | tf_op jit(solution)/shard_map/pallas_call | solution.py:333
  90.1 0.5 collective-permute-start.26
  90.6 1.2 %collective-permute-done.26.b_other = bf16[1088,128]{1,0:T(8,128)(2,1)S(1)} collective-permute-done((bf16[1088,128]{1,0:T(8,128)(2,1)S(1)}, bf16[1088,128]{1,0:T(8,128)(2,1)S(1)}, u32[]{:S(2)}, u32[]{:S(2)}) %collective-permute-start.26) | collective-permute-done | bytes 278560 | tf_op jit(solution)/shard_map/ppermute | solution.py:368
  91.8 0.4 collective-permute-done.28.b_other_far
  92.2 3.2 %shard_map.131 = (f32[31,512]{1,0:T(8,128)}, f32[512,512]{1,0:T(8,128)}, f32[512,512]{1,0:T(8,128)}, f32[512,512]{1,0:T(8,128)}, f32[512,512]{1,0:T(8,128)}) custom-call(s32[10]{0:T(128)S(1)} %stack.43.bits, bf16[1088,128]{1,0:T(8,128)(2,1)S(1)} %pad_maximum_fusion.1.a_own, bf16[1088,128]{1,0:T(8,128)(2,1)S(1)} %constant_dynamic-update-slice_fusion.b_own, ...), custom_call_target="tpu_custom_call" | custom-call | tf_op jit(solution)/shard_map/pallas_call | solution.py:333
  (52 shorter events, 1.5 us)
Async XLA Ops:
  0.6 20.1 %copy-start.7 = (f32[31,512]{1,0:T(8,128)S(1)}, f32[31,512]{1,0:T(8,128)}, u32[]{:S(2)}) copy-start(f32[31,512]{1,0:T(8,128)} %kern.3) | copy-start | bytes 190468
  0.8 1.0 %copy-start = (bf16[2,128,512]{2,1,0:T(8,128)(2,1)S(1)}, bf16[2,128,512]{2,1,0:T(8,128)(2,1)}, u32[]{:S(2)}) copy-start(bf16[2,128,512]{2,1,0:T(8,128)(2,1)} %cot.3) | copy-start | bytes 786436
  1.8 0.9 copy-start.6
  2.7 18.0 %copy-start.2 = (bf16[512,512]{1,0:T(8,128)(2,1)S(1)}, bf16[512,512]{1,0:T(8,128)(2,1)}, u32[]{:S(2)}) copy-start(bf16[512,512]{1,0:T(8,128)(2,1)} %wq.1) | copy-start | bytes 1572868
  3.7 3.2 %collective-permute-start = (bf16[2,32,512]{2,1,0:T(8,128)(2,1)S(1)}, bf16[2,32,512]{2,1,0:T(8,128)(2,1)S(1)}, u32[]{:S(2)}, u32[]{:S(2)}) collective-permute-start(bf16[2,32,512]{2,1,0:T(8,128)(2,1)S(1)} %get-tuple-element.36), channel_id=1, source_target_pairs={{0,8},{1,9},{2,10},{3,11},{4,12},{5,13},{6,14},{7,15},{8,0},{9,1},... | collective-permute-start | bytes 196616 | tf_op jit(solution)/shard_map/ppermute | solution.py:368
  4.2 5.3 %collective-permute-start.1 = (bf16[2,32,512]{2,1,0:T(8,128)(2,1)S(1)}, bf16[2,32,512]{2,1,0:T(8,128)(2,1)S(1)}, u32[]{:S(2)}, u32[]{:S(2)}) collective-permute-start(bf16[2,32,512]{2,1,0:T(8,128)(2,1)S(1)} %get-tuple-element.37), channel_id=1, source_target_pairs={{0,16},{1,17},{2,18},{3,19},{4,20},{5,21},{6,22},{7,23},{8,24},{9,... | collective-permute-start | bytes 196616 | tf_op jit(solution)/shard_map/ppermute | solution.py:368
  6.8 4.0 %collective-permute-start.2 = (bf16[2,32,512]{2,1,0:T(8,128)(2,1)S(1)}, bf16[2,32,512]{2,1,0:T(8,128)(2,1)S(1)}, u32[]{:S(2)}, u32[]{:S(2)}) collective-permute-start(bf16[2,32,512]{2,1,0:T(8,128)(2,1)S(1)} %get-tuple-element.38), channel_id=1, source_target_pairs={{0,24},{1,25},{2,26},{3,27},{4,28},{5,29},{6,30},{7,31},{8,16},{9,... | collective-permute-start | bytes 196616 | tf_op jit(solution)/shard_map/ppermute | solution.py:368
  11.5 9.3 %collective-permute-start.6 = (bf16[4,2,16,512]{3,2,1,0:T(8,128)(2,1)S(1)}, bf16[4,2,16,512]{3,2,1,0:T(8,128)(2,1)S(1)}, u32[]{:S(2)}, u32[]{:S(2)}) collective-permute-start(bf16[4,2,16,512]{3,2,1,0:T(8,128)(2,1)S(1)} %get-tuple-element.43), channel_id=1, source_target_pairs={{0,8},{1,9},{2,10},{3,11},{4,12},{5,13},{6,14},{7,15},{8,0},{9,1},... | collective-permute-start | bytes 393224 | tf_op jit(solution)/shard_map/ppermute | solution.py:368
  11.7 9.0 %collective-permute-start.7 = (bf16[4,2,16,512]{3,2,1,0:T(8,128)(2,1)S(1)}, bf16[4,2,16,512]{3,2,1,0:T(8,128)(2,1)S(1)}, u32[]{:S(2)}, u32[]{:S(2)}) collective-permute-start(bf16[4,2,16,512]{3,2,1,0:T(8,128)(2,1)S(1)} %get-tuple-element.44), channel_id=1, source_target_pairs={{8,24},{9,25},{10,26},{11,27},{12,28},{13,29},{14,30},{15,31},{24,... | collective-permute-start | bytes 393224 | tf_op jit(solution)/shard_map/ppermute | solution.py:368
  12.3 4.4 %collective-permute-start.3 = (bf16[2,32,512]{2,1,0:T(8,128)(2,1)S(1)}, bf16[2,32,512]{2,1,0:T(8,128)(2,1)S(1)}, u32[]{:S(2)}, u32[]{:S(2)}) collective-permute-start(bf16[2,32,512]{2,1,0:T(8,128)(2,1)S(1)} %get-tuple-element.40), channel_id=1, source_target_pairs={{0,8},{1,9},{2,10},{3,11},{4,12},{5,13},{6,14},{7,15},{8,0},{9,1},... | collective-permute-start | bytes 196616 | tf_op jit(solution)/shard_map/ppermute | solution.py:368
  15.1 4.3 %collective-permute-start.4 = (bf16[2,32,512]{2,1,0:T(8,128)(2,1)S(1)}, bf16[2,32,512]{2,1,0:T(8,128)(2,1)S(1)}, u32[]{:S(2)}, u32[]{:S(2)}) collective-permute-start(bf16[2,32,512]{2,1,0:T(8,128)(2,1)S(1)} %get-tuple-element.41), channel_id=1, source_target_pairs={{0,16},{1,17},{2,18},{3,19},{4,20},{5,21},{6,22},{7,23},{8,24},{9,... | collective-permute-start | bytes 196616 | tf_op jit(solution)/shard_map/ppermute | solution.py:368
  16.7 4.0 %collective-permute-start.5 = (bf16[2,32,512]{2,1,0:T(8,128)(2,1)S(1)}, bf16[2,32,512]{2,1,0:T(8,128)(2,1)S(1)}, u32[]{:S(2)}, u32[]{:S(2)}) collective-permute-start(bf16[2,32,512]{2,1,0:T(8,128)(2,1)S(1)} %get-tuple-element.42), channel_id=1, source_target_pairs={{0,24},{1,25},{2,26},{3,27},{4,28},{5,29},{6,30},{7,31},{8,16},{9,... | collective-permute-start | bytes 196616 | tf_op jit(solution)/shard_map/ppermute | solution.py:368
  20.7 1.0 %copy-start.3 = (bf16[512,512]{1,0:T(8,128)(2,1)S(1)}, bf16[512,512]{1,0:T(8,128)(2,1)}, u32[]{:S(2)}) copy-start(bf16[512,512]{1,0:T(8,128)(2,1)} %wk.1) | copy-start | bytes 1572868
  21.8 1.0 %copy-start.4 = (bf16[512,512]{1,0:T(8,128)(2,1)S(1)}, bf16[512,512]{1,0:T(8,128)(2,1)}, u32[]{:S(2)}) copy-start(bf16[512,512]{1,0:T(8,128)(2,1)} %wv.1) | copy-start | bytes 1572868
  22.8 1.0 %copy-start.5 = (bf16[512,512]{1,0:T(8,128)(2,1)S(1)}, bf16[512,512]{1,0:T(8,128)(2,1)}, u32[]{:S(2)}) copy-start(bf16[512,512]{1,0:T(8,128)(2,1)} %wo.1) | copy-start | bytes 1572868
  34.2 2.4 %collective-permute-start.8 = (bf16[3200,128]{1,0:T(8,128)(2,1)S(1)}, bf16[3200,128]{1,0:T(8,128)(2,1)S(1)}, u32[]{:S(2)}, u32[]{:S(2)}) collective-permute-start(bf16[3200,128]{1,0:T(8,128)(2,1)S(1)} %get-tuple-element.46), channel_id=1, source_target_pairs={{0,8},{1,9},{2,10},{3,11},{4,12},{5,13},{6,14},{7,15},{8,0},{9,1},... | collective-permute-start | bytes 2457608 | tf_op jit(solution)/shard_map/ppermute | solution.py:368
  34.5 3.7 %collective-permute-start.17 = (bf16[2176,128]{1,0:T(8,128)(2,1)S(1)}, bf16[2176,128]{1,0:T(8,128)(2,1)S(1)}, u32[]{:S(2)}, u32[]{:S(2)}) collective-permute-start(bf16[2176,128]{1,0:T(8,128)(2,1)S(1)} %get-tuple-element.56), channel_id=1, source_target_pairs={{0,8},{1,9},{2,10},{3,11},{4,12},{5,13},{6,14},{7,15},{8,0},{9,1},... | collective-permute-start | bytes 1671176 | tf_op jit(solution)/shard_map/ppermute | solution.py:368
  36.8 15.2 %collective-permute-start.9 = (bf16[2112,128]{1,0:T(8,128)(2,1)S(1)}, bf16[2112,128]{1,0:T(8,128)(2,1)S(1)}, u32[]{:S(2)}, u32[]{:S(2)}) collective-permute-start(bf16[2112,128]{1,0:T(8,128)(2,1)S(1)} %pad_maximum_fusion), channel_id=1, source_target_pairs={{0,16},{1,17},{2,18},{3,19},{4,20},{5,21},{6,22},{7,23},{8,24},{9,... | collective-permute-start | bytes 1622024 | tf_op jit(solution)/shard_map/ppermute | solution.py:368
  38.3 8.6 %collective-permute-start.18 = (bf16[1088,128]{1,0:T(8,128)(2,1)S(1)}, bf16[1088,128]{1,0:T(8,128)(2,1)S(1)}, u32[]{:S(2)}, u32[]{:S(2)}) collective-permute-start(bf16[1088,128]{1,0:T(8,128)(2,1)S(1)} %add_convert_fusion), channel_id=1, source_target_pairs={{0,1},{1,0},{2,3},{3,2},{4,5},{5,4},{6,7},{7,6},{8,9},{9,8},{10,11... | collective-permute-start | bytes 835592 | tf_op jit(solution)/shard_map/ppermute | solution.py:368
  46.9 7.9 %collective-permute-start.19 = (bf16[544,128]{1,0:T(8,128)(2,1)S(1)}, bf16[544,128]{1,0:T(8,128)(2,1)S(1)}, u32[]{:S(2)}, u32[]{:S(2)}) collective-permute-start(bf16[544,128]{1,0:T(8,128)(2,1)S(1)} %add_convert_fusion.2), channel_id=1, source_target_pairs={{0,16},{1,17},{2,18},{3,19},{4,20},{5,21},{6,22},{7,23},{8,24},{9,... | collective-permute-start | bytes 417800 | tf_op jit(solution)/shard_map/ppermute | solution.py:368
  53.3 5.5 %collective-permute-start.10 = (bf16[672,128]{1,0:T(8,128)(2,1)S(1)}, bf16[672,128]{1,0:T(8,128)(2,1)S(1)}, u32[]{:S(2)}, u32[]{:S(2)}) collective-permute-start(bf16[672,128]{1,0:T(8,128)(2,1)S(1)} %pad_maximum_fusion.2), channel_id=1, source_target_pairs={{0,1},{1,0},{2,3},{3,2},{4,5},{5,4},{6,7},{7,6},{8,9},{9,8},{10,11... | collective-permute-start | bytes 516104 | tf_op jit(solution)/shard_map/ppermute | solution.py:368
  54.9 5.6 %collective-permute-start.20 = (bf16[272,128]{1,0:T(8,128)(2,1)S(1)}, bf16[272,128]{1,0:T(8,128)(2,1)S(1)}, u32[]{:S(2)}, u32[]{:S(2)}) collective-permute-start(bf16[272,128]{1,0:T(8,128)(2,1)S(1)} %add_convert_fusion.6), channel_id=1, source_target_pairs={{0,2},{1,3},{2,0},{3,1},{4,6},{5,7},{6,4},{7,5},{8,10},{9,11},{10,... | collective-permute-start | bytes 208904 | tf_op jit(solution)/shard_map/ppermute | solution.py:368
  58.8 4.4 %collective-permute-start.11 = (bf16[272,128]{1,0:T(8,128)(2,1)S(1)}, bf16[272,128]{1,0:T(8,128)(2,1)S(1)}, u32[]{:S(2)}, u32[]{:S(2)}) collective-permute-start(bf16[272,128]{1,0:T(8,128)(2,1)S(1)} %add_convert_fusion.9), channel_id=1, source_target_pairs={{0,2},{1,3},{2,0},{3,1},{4,6},{5,7},{6,4},{7,5},{8,10},{9,11},{10,... | collective-permute-start | bytes 208904 | tf_op jit(solution)/shard_map/ppermute | solution.py:368
  60.6 6.4 %collective-permute-start.21 = (bf16[272,128]{1,0:T(8,128)(2,1)S(1)}, bf16[272,128]{1,0:T(8,128)(2,1)S(1)}, u32[]{:S(2)}, u32[]{:S(2)}) collective-permute-start(bf16[272,128]{1,0:T(8,128)(2,1)S(1)} %add_convert_fusion.5), channel_id=1, source_target_pairs={{0,4},{1,5},{2,6},{3,7},{4,0},{5,1},{6,2},{7,3},{8,12},{9,13},{10,... | collective-permute-start | bytes 208904 | tf_op jit(solution)/shard_map/ppermute | solution.py:368
  63.3 24.0 %copy-start.1 = (bf16[2,128,512]{2,1,0:T(8,128)(2,1)S(1)}, bf16[2,128,512]{2,1,0:T(8,128)(2,1)}, u32[]{:S(2)}) copy-start(bf16[2,128,512]{2,1,0:T(8,128)(2,1)} %cot.3) | copy-start | bytes 786436
  63.3 5.7 %collective-permute-start.12 = (bf16[272,128]{1,0:T(8,128)(2,1)S(1)}, bf16[272,128]{1,0:T(8,128)(2,1)S(1)}, u32[]{:S(2)}, u32[]{:S(2)}) collective-permute-start(bf16[272,128]{1,0:T(8,128)(2,1)S(1)} %add_convert_fusion.8), channel_id=1, source_target_pairs={{0,4},{1,5},{2,6},{3,7},{4,0},{5,1},{6,2},{7,3},{8,12},{9,13},{10,... | collective-permute-start | bytes 208904 | tf_op jit(solution)/shard_map/ppermute | solution.py:368
  67.0 4.4 %collective-permute-start.22 = (bf16[272,128]{1,0:T(8,128)(2,1)S(1)}, bf16[272,128]{1,0:T(8,128)(2,1)S(1)}, u32[]{:S(2)}, u32[]{:S(2)}) collective-permute-start(bf16[272,128]{1,0:T(8,128)(2,1)S(1)} %add_convert_fusion.4), channel_id=1, source_target_pairs={{0,2},{1,3},{2,0},{3,1},{4,6},{5,7},{6,4},{7,5},{8,10},{9,11},{10,... | collective-permute-start | bytes 208904 | tf_op jit(solution)/shard_map/ppermute | solution.py:368
  69.0 4.7 %collective-permute-start.13 = (bf16[272,128]{1,0:T(8,128)(2,1)S(1)}, bf16[272,128]{1,0:T(8,128)(2,1)S(1)}, u32[]{:S(2)}, u32[]{:S(2)}) collective-permute-start(bf16[272,128]{1,0:T(8,128)(2,1)S(1)} %add_convert_fusion.7), channel_id=1, source_target_pairs={{0,2},{1,3},{2,0},{3,1},{4,6},{5,7},{6,4},{7,5},{8,10},{9,11},{10,... | collective-permute-start | bytes 208904 | tf_op jit(solution)/shard_map/ppermute | solution.py:368
  71.4 9.2 %collective-permute-start.23 = (bf16[544,128]{1,0:T(8,128)(2,1)S(1)}, bf16[544,128]{1,0:T(8,128)(2,1)S(1)}, u32[]{:S(2)}, u32[]{:S(2)}) collective-permute-start(bf16[544,128]{1,0:T(8,128)(2,1)S(1)} %pad_maximum_fusion.4), channel_id=1, source_target_pairs={{0,16},{1,17},{2,18},{3,19},{4,20},{5,21},{6,22},{7,23},{8,24},{9,... | collective-permute-start | bytes 417800 | tf_op jit(solution)/shard_map/ppermute | solution.py:368
  72.8 0.9 collective-permute-start.14
  73.7 9.9 %collective-permute-start.15 = (bf16[544,128]{1,0:T(8,128)(2,1)S(1)}, bf16[544,128]{1,0:T(8,128)(2,1)S(1)}, u32[]{:S(2)}, u32[]{:S(2)}) collective-permute-start(bf16[544,128]{1,0:T(8,128)(2,1)S(1)} %pad_maximum_fusion.3), channel_id=1, source_target_pairs={{0,1},{1,0},{2,3},{3,2},{4,5},{5,4},{6,7},{7,6},{8,9},{9,8},{10,11... | collective-permute-start | bytes 417800 | tf_op jit(solution)/shard_map/ppermute | solution.py:368
  80.7 6.6 %collective-permute-start.24 = (bf16[1088,128]{1,0:T(8,128)(2,1)S(1)}, bf16[1088,128]{1,0:T(8,128)(2,1)S(1)}, u32[]{:S(2)}, u32[]{:S(2)}) collective-permute-start(bf16[1088,128]{1,0:T(8,128)(2,1)S(1)} %pad_maximum_fusion.1.a_own), channel_id=1, source_target_pairs={{0,1},{1,0},{2,3},{3,2},{4,5},{5,4},{6,7},{7,6},{8,9},{9,8},{10,11... | collective-permute-start | bytes 835592 | tf_op jit(solution)/shard_map/ppermute | solution.py:368
  83.7 6.9 %collective-permute-start.16 = (bf16[1088,128]{1,0:T(8,128)(2,1)S(1)}, bf16[1088,128]{1,0:T(8,128)(2,1)S(1)}, u32[]{:S(2)}, u32[]{:S(2)}) collective-permute-start(bf16[1088,128]{1,0:T(8,128)(2,1)S(1)} %constant_dynamic-update-slice_fusion.b_own), channel_id=1, source_target_pairs={{0,16},{1,17},{2,18},{3,19},{4,20},{5,21},{6,22},{7,23},{8,24},{9,... | collective-permute-start | bytes 835592 | tf_op jit(solution)/shard_map/ppermute | solution.py:368
  84.8 5.9 %collective-permute-start.25 = (bf16[1088,128]{1,0:T(8,128)(2,1)S(1)}, bf16[1088,128]{1,0:T(8,128)(2,1)S(1)}, u32[]{:S(2)}, u32[]{:S(2)}) collective-permute-start(bf16[1088,128]{1,0:T(8,128)(2,1)S(1)} %pad_maximum_fusion.1.a_own), channel_id=1, source_target_pairs={{0,8},{1,9},{2,10},{3,11},{4,12},{5,13},{6,14},{7,15},{8,0},{9,1},... | collective-permute-start | bytes 835592 | tf_op jit(solution)/shard_map/ppermute | solution.py:368
  87.3 3.4 %collective-permute-start.27 = (bf16[1088,128]{1,0:T(8,128)(2,1)S(1)}, bf16[1088,128]{1,0:T(8,128)(2,1)S(1)}, u32[]{:S(2)}, u32[]{:S(2)}) collective-permute-start(bf16[1088,128]{1,0:T(8,128)(2,1)S(1)} %collective-permute-done.24.a_far), channel_id=1, source_target_pairs={{0,8},{1,9},{2,10},{3,11},{4,12},{5,13},{6,14},{7,15},{8,0},{9,1},... | collective-permute-start | bytes 835592 | tf_op jit(solution)/shard_map/ppermute | solution.py:368
  90.1 1.7 %collective-permute-start.26 = (bf16[1088,128]{1,0:T(8,128)(2,1)S(1)}, bf16[1088,128]{1,0:T(8,128)(2,1)S(1)}, u32[]{:S(2)}, u32[]{:S(2)}) collective-permute-start(bf16[1088,128]{1,0:T(8,128)(2,1)S(1)} %constant_dynamic-update-slice_fusion.b_own), channel_id=1, source_target_pairs={{0,8},{1,9},{2,10},{3,11},{4,12},{5,13},{6,14},{7,15},{8,0},{9,1},... | collective-permute-start | bytes 835592 | tf_op jit(solution)/shard_map/ppermute | solution.py:368
  90.6 1.6 %collective-permute-start.28 = (bf16[1088,128]{1,0:T(8,128)(2,1)S(1)}, bf16[1088,128]{1,0:T(8,128)(2,1)S(1)}, u32[]{:S(2)}, u32[]{:S(2)}) collective-permute-start(bf16[1088,128]{1,0:T(8,128)(2,1)S(1)} %collective-permute-done.16.b_far), channel_id=1, source_target_pairs={{0,8},{1,9},{2,10},{3,11},{4,12},{5,13},{6,14},{7,15},{8,0},{9,1},... | collective-permute-start | bytes 835592 | tf_op jit(solution)/shard_map/ppermute | solution.py:368

commit v6 on v5

--- a/solution.py
+++ b/solution.py
@@ -16,7 +16,7 @@
 BF = jnp.bfloat16
 F32 = jnp.float32
 MIB = 1024 * 1024
-CORE, Y, X, Z, ODD, SKIP, BLOCK_AT = range(7)
+CORE, Y, X, Z, ZZ, ODD, SKIP, BLOCK_AT = range(8)
 
 
 def mm(left, right, dims=(((1,), (0,)), ((), ()))):
@@ -40,18 +40,20 @@
     return acc
 
 
+def ways(bits, half):
+    return [bits[i] for i in ((X, Y, Z), (Z, ZZ, X))[half]]
+
+
 def sigmoid(v):
     return 0.5 * jnp.tanh(0.5 * v) + 0.5
 
 
-def scatter_kernel(plan, bits, frames, cot, *refs):
-    sub, outs, sems = plan, refs[:8], refs[8]
+def scatter_kernel(sub, bits, source, *refs):
+    outs, sems = refs[:4], refs[4]
     copies = []
-    for i, source in enumerate((frames, cot)):
-        for d in range(4):
-            rows = pl.ds(pl.multiple_of(bits[BLOCK_AT + d] * sub, sub), sub)
-            n = 4 * i + d
-            copies.append(pltpu.make_async_copy(source.at[:, rows], outs[n], sems.at[n]))
+    for d in range(4):
+        rows = pl.ds(pl.multiple_of(bits[BLOCK_AT + d] * sub, sub), sub)
+        copies.append(pltpu.make_async_copy(source.at[:, rows], outs[d], sems.at[d]))
     for copy in copies:
         copy.start()
     for copy in copies:
@@ -66,10 +68,47 @@
         side[d] = f[:, pl.ds(pl.multiple_of(odd * last, HALO), HALO), :]
 
 
+def frames_window(bits, frames, near, side, a, m, lanes):
+    is_odd = jnp.broadcast_to(bits[ODD], (HALO, LANES)) == 1
+    one = near[a ^ 1, m, :, lanes].astype(F32)
+    two = side[a ^ bits[SKIP], m, :, lanes].astype(F32)
+    return jnp.concatenate(
+        [
+            jnp.where(is_odd, one, two),
+            frames[a, m, :, lanes].astype(F32),
+            jnp.where(is_odd, two, one),
+        ],
+        axis=0,
+    )
+
+
+def conv_kernel(plan, bits, f0, f1, f2, f3, near, side, kern, frames, conv_out, acted_out):
+    groups, count, sub, width = plan
+    mics = groups * count
+    cuts = sub // HALO
+    for d, f in enumerate((f0, f1, f2, f3)):
+        frames[d] = f[...]
+
+    def conv_step(n, _):
+        a, m = n // count, n % count
+        for lc in range(width // LANES):
+            lanes = slice(lc * LANES, (lc + 1) * LANES)
+            x = frames_window(bits, frames, near, side, a, m, lanes)
+            conv = window(x, lambda o: kern[o - 1 : o, lanes], sub)
+            acted = (conv * sigmoid(conv)).astype(BF)
+            for c in range(cuts):
+                at = pl.multiple_of((c * mics + n) * HALO, HALO)
+                conv_out[pl.ds(at, HALO), lanes] = conv[c * HALO : (c + 1) * HALO]
+                acted_out[pl.ds(at, HALO), lanes] = acted[c * HALO : (c + 1) * HALO]
+        return 0
+
+    lax.fori_loop(0, mics, conv_step, 0)
+
+
 def main_kernel(
-    plan, bits, f0, f1, f2, f3, c0, c1, c2, c3, near, side, kern, wq, wk, wv, wo,
-    a_keep, b_keep, a_send, b_send, back_keep,
-    frame_s, conv_s, left_s, right_s, q_s, k_s, v_s, u_s, dconv_s, tap_s,
+    plan, bits, frames, conv_in, acted_in, c0, c1, c2, c3, near, side, weights,
+    a_keep, b_keep, a_send, b_send, back_keep, back_send,
+    left_s, right_s, q_s, k_s, v_s, u_s, dconv_s, tap_s,
 ):
     groups, count, sub, width, factor = plan
     mics = groups * count
@@ -77,42 +116,13 @@
     block = mics * HALO
     rows = cuts * block
     cols = width // LANES
-    odd, skip = bits[ODD], bits[SKIP]
-    is_odd = jnp.broadcast_to(odd, (HALO, LANES)) == 1
-
-    for d, (f, cot) in enumerate(((f0, c0), (f1, c1), (f2, c2), (f3, c3))):
-        frame_s[d] = f[...]
+
+    wq, wk, wv, wo = (weights.at[i] for i in range(4))
+    left_s[0] = acted_in[...]
+    for d, cot in enumerate((c0, c1, c2, c3)):
         for m in range(count):
             for c in range(cuts):
                 right_s[3, c, d, m] = cot[m, c * HALO : (c + 1) * HALO, :]
-
-    def frames_window(a, m, lanes):
-        one = near[a ^ 1, m, :, lanes].astype(F32)
-        two = side[a ^ skip, m, :, lanes].astype(F32)
-        return jnp.concatenate(
-            [
-                jnp.where(is_odd, one, two),
-                frame_s[a, m, :, lanes].astype(F32),
-                jnp.where(is_odd, two, one),
-            ],
-            axis=0,
-        )
-
-    def conv_step(n, _):
-        a, m = n // count, n % count
-        for lc in range(cols):
-            lanes = slice(lc * LANES, (lc + 1) * LANES)
-            conv = window(
-                frames_window(a, m, lanes), lambda o: kern[o - 1 : o, lanes], sub
-            )
-            acted = (conv * sigmoid(conv)).astype(BF)
-            for c in range(cuts):
-                at = pl.multiple_of(c * block + n * HALO, HALO)
-                conv_s[pl.ds(at, HALO), lanes] = conv[c * HALO : (c + 1) * HALO]
-                left_s[0, pl.ds(at, HALO), lanes] = acted[c * HALO : (c + 1) * HALO]
-        return 0
-
-    lax.fori_loop(0, mics, conv_step, 0)
 
     def flat(i):
         return right_s[i].reshape(rows, width)
@@ -171,7 +181,7 @@
             put(2, c, lanes, pick(mm(wb, u, TN)))
 
     dacted = mm(flat(0), wq[...], NT) + mm(flat(1), wk[...], NT) + mm(flat(2), wv[...], NT)
-    conv = conv_s[...]
+    conv = conv_in[...]
     sig = sigmoid(conv)
     dconv_s[...] = dacted * sig * (1.0 + conv * (1.0 - sig))
 
@@ -180,7 +190,7 @@
 
         def tap_step(n, accs):
             a, m = n // count, n % count
-            x = frames_window(a, m, lanes)
+            x = frames_window(bits, frames, near, side, a, m, lanes)
             d = jnp.concatenate(
                 [
                     dconv_s[pl.ds(pl.multiple_of(c * block + n * HALO, HALO), HALO), lanes]
@@ -207,17 +217,17 @@
     tap_s[cols * 32 :, :] = jnp.zeros((HALO, LANES), F32)
     size = cols * width // 8
     span = size + HALO
-    core, y, x, z = bits[CORE], bits[Y], bits[X], bits[Z]
+    core = bits[CORE]
     for out, owner, h in (
         (a_send, 1 - core, 0), (b_send, 1 - core, 1), (a_keep, core, 0), (b_keep, core, 1)
     ):
         i = owner * 2 + h
-        first, second = (x, y) if h == 0 else (y, x)
+        first, second, third = ways(bits, h)
         grad = mm(left_s[i // 3], flat(i), TN).astype(BF)
         for piece in range(8):
             cb, at = piece * size // width, piece * size % width
             tail = tap_s[pl.ds(pl.multiple_of((i * 8 + piece) * cols, cols), HALO), :]
-            rel = ((piece // 4) ^ first) * 4 + ((piece // 2 % 2) ^ second) * 2 + ((piece % 2) ^ z)
+            rel = ((piece // 4) ^ first) * 4 + ((piece // 2 % 2) ^ second) * 2 + ((piece % 2) ^ third)
             start = pl.multiple_of(rel * span, HALO)
             out[pl.ds(start, size), :] = grad[at : at + size, cb * LANES : (cb + 1) * LANES]
             out[pl.ds(pl.multiple_of(start + size, HALO), HALO), :] = tail.astype(BF)
@@ -225,13 +235,13 @@
     proj = mm(left_s[1], wo[...])
     unit = 2 * count * cols * sub
     for d, (out, base) in enumerate(
-        ((back_keep, 0), (b_send, 8 * span), (back_keep, unit), (b_send, 8 * span + unit))
+        ((back_keep, 0), (back_send, 0), (back_keep, unit), (back_send, unit))
     ):
         for m in range(count):
             for c in range(cuts):
                 at = c * block + (d * count + m) * HALO
                 part = slice(c * HALO, (c + 1) * HALO)
-                layer = (frame_s[d, m, part, :].astype(F32) + proj[at : at + HALO]).astype(BF)
+                layer = (frames[d, m, part, :].astype(F32) + proj[at : at + HALO]).astype(BF)
                 dconv = dconv_s[at : at + HALO, :].astype(BF)
                 for lc in range(cols):
                     for kind, value in enumerate((layer, dconv)):
@@ -243,50 +253,60 @@
     return functools.reduce(lambda x, y: x + y, [x.astype(F32) for x in parts]).astype(BF)
 
 
-def final_kernel(
-    plan, bits, a_own, b_own, a_far, b_far, a_other, b_other, a_other_far, b_other_far, taps, *refs
-):
+def final_kernel(plan, first_call, bits, a_near, b_near, a_far, b_far, *refs):
     width, norm = plan
-    outs, tap_s = refs[:4], refs[4]
     cols = width // LANES
     size = cols * width // 8
     span = size + HALO
-    core, y, x, z = bits[CORE], bits[Y], bits[X], bits[Z]
-
-    def emit(which, parts):
-        for h in range(2):
-            i = 2 * which + h
-            first, second = (x, y) if h == 0 else (y, x)
-            for rel in range(8):
-                part, start = parts[rel // 4][h], rel % 4 * span
-                piece = (first ^ (rel // 4)) * 4 + (second ^ (rel // 2 % 2)) * 2 + (z ^ (rel % 2))
-                cb, at = piece * size // width, piece * size % width
-                outs[i][
-                    pl.ds(pl.multiple_of(at, size), size),
-                    pl.ds(pl.multiple_of(cb * LANES, LANES), LANES),
-                ] = part[start : start + size, :].astype(F32) * norm
-                tap_s[i * 8 + piece] = part[start + size : start + span, :].astype(F32) * norm
-
-    for which in range(2):
-        @pl.when(core == which)
-        def _():
-            emit(which, ((a_own, b_own), (a_far, b_far)))
-            emit(1 - which, ((a_other, b_other), (a_other_far, b_other_far)))
-
-    for g in range(32):
-        row = g * cols
-        lc, j = row // 32, row % 32
-        kept = min(cols, 31 - j)
-        taps[j : j + kept, lc * LANES : (lc + 1) * LANES] = tap_s[g, 0:kept]
+    if first_call:
+        outs, tails, (grad_s, sems) = refs[:4], refs[4], refs[5:]
+    else:
+        tails, outs, taps, (grad_s, sems, tail_s) = refs[4], refs[5:9], refs[9], refs[10:]
+    core = bits[CORE]
+    owner = core if first_call else 1 - core
+    for h in range(2):
+        first, second, third = ways(bits, h)
+        parts = ((a_near, a_far), (b_near, b_far))[h]
+        for rel in range(8):
+            part, start = parts[rel // 4], rel % 4 * span
+            piece = (first ^ (rel // 4)) * 4 + (second ^ (rel // 2 % 2)) * 2 + (third ^ (rel % 2))
+            cb, at = piece * size // width, piece * size % width
+            grad_s[
+                h,
+                pl.ds(pl.multiple_of(at, size), size),
+                pl.ds(pl.multiple_of(cb * LANES, LANES), LANES),
+            ] = part[start : start + size, :].astype(F32) * norm
+            tail = part[start + size : start + span, :].astype(F32) * norm
+            if first_call:
+                tails[h * 8 + piece] = tail
+            else:
+                tail_s[owner * 16 + h * 8 + piece] = tail
+        for which in range(2):
+            @pl.when(owner == which)
+            def _():
+                pltpu.make_async_copy(grad_s.at[h], outs[2 * which + h], sems.at[h]).start()
+    if not first_call:
+        for n in range(16):
+            tail_s[core * 16 + n] = tails[n]
+        for g in range(32):
+            row = g * cols
+            lc, j = row // 32, row % 32
+            kept = min(cols, 31 - j)
+            taps[j : j + kept, lc * LANES : (lc + 1) * LANES] = tail_s[g, 0:kept]
+    for h in range(2):
+        for which in range(2):
+            @pl.when(owner == which)
+            def _():
+                pltpu.make_async_copy(grad_s.at[h], outs[2 * which + h], sems.at[h]).wait()
 
 
 def home_kernel(plan, bits, own, core_got, y_got, layer_out, dconv, x_edge, z_edge):
-    count, sub, cols, core_at, y_at = plan
+    count, sub, cols = plan
     unit = 2 * count * cols * sub
     odd = bits[X]
     last = 3 * sub + sub - HALO
     for d, (ref, base) in enumerate(
-        ((own, 0), (core_got, core_at), (y_got, y_at), (y_got, y_at + unit))
+        ((own, 0), (core_got, 0), (y_got, 0), (y_got, unit))
     ):
         to = pl.ds(pl.multiple_of(bits[BLOCK_AT + d] * sub, sub), sub)
         for m in range(count):
@@ -329,16 +349,21 @@
     lax.fori_loop(0, count, step, 0)
 
 
-def call(body, outs, scratch, limit, *args, space=pltpu.VMEM):
+def call(body, outs, scratch, limit, *args, hbm=(), hbm_outs=(), aliases=None):
+    spaces = [pltpu.HBM if i in hbm else pltpu.VMEM for i in range(len(args))]
     return pl.pallas_call(
         body,
         out_shape=outs,
         in_specs=[
             pl.BlockSpec(memory_space=pltpu.SMEM if x.dtype == jnp.int32 else space)
-            for x in args
+            for x, space in zip(args, spaces)
         ],
-        out_specs=jax.tree.map(lambda _: pl.BlockSpec(memory_space=space), outs),
+        out_specs=tuple(
+            pl.BlockSpec(memory_space=pltpu.HBM if i in hbm_outs else pltpu.VMEM)
+            for i in range(len(outs))
+        ),
         scratch_shapes=scratch,
+        input_output_aliases=aliases or {},
         compiler_params=pltpu.CompilerParams(vmem_limit_bytes=limit * MIB),
     )(*args)
 
@@ -360,7 +385,7 @@
 
     mine = order(mic)
     bits = jnp.stack(
-        [mic % 2, mic // 2, tm % 2, tm // 2 % 2, mine % 2, 2 * ((mine + 1) // 2 % 2)]
+        [mic % 2, mic // 2, tm % 2, tm // 2 % 2, tm // 4 % 2, mine % 2, 2 * ((mine + 1) // 2 % 2)]
         + [order(mic ^ d) for d in range(4)]
     ).astype(jnp.int32)
 
@@ -374,17 +399,21 @@
         return pairs + [(j, i) for i, j in pairs]
 
     block = shape((count, sub, width), BF)
-    parts = call(
-        functools.partial(scatter_kernel, sub), (block,) * 8,
-        [pltpu.SemaphoreType.DMA((8,))], 8, bits, frames, cotangent, space=pl.ANY,
-    )
     masks = (0, over_core, over_y, over_core + over_y)
-    got = {d: swap(parts[d], masks[d]) for d in (2, 3, 1)}
-    f = [parts[0], got[1], got[2], got[3]]
-    got = {d: swap(parts[4 + d], masks[d]) for d in (2, 3, 1)}
-    c = [parts[4], got[1], got[2], got[3]]
+
+    def scattered(x):
+        parts = call(
+            functools.partial(scatter_kernel, sub), (block,) * 4,
+            [pltpu.SemaphoreType.DMA((4,))], 8, bits, x, hbm=(1,),
+        )
+        got = {d: swap(parts[d], masks[d]) for d in (2, 3, 1)}
+        return [parts[0], got[1], got[2], got[3]]
+
+    f, c = scattered(frames), scattered(cotangent)
+    weights = jnp.stack([w_query, w_key, w_value, w_out])
     edge = shape((groups, count, HALO, width), BF)
     near, side = call(functools.partial(edge_kernel, sub), (edge, edge), [], 8, bits, *f)
+    near, side, weights = lax.optimization_barrier((near, side, weights))
     near = swap(near, over_core)
     side = permute(
         side,
@@ -403,19 +432,25 @@
     def flat(n):
         return shape((n, LANES), BF)
 
-    a_keep, b_keep, a_send, b_send, back_keep = call(
+    moved = shape((groups, count, sub, width), BF)
+    placed, conv, acted = call(
+        functools.partial(conv_kernel, (groups, count, sub, width)),
+        (moved, shape((rows, width), F32), shape((rows, width), BF)),
+        [], 8, bits, *f, near, side, kernel,
+    )
+    a_keep, b_keep, a_send, b_send, back_keep, back_send = call(
         functools.partial(main_kernel, (groups, count, sub, width, factor)),
-        (flat(8 * span), flat(8 * span), flat(8 * span), flat(8 * span + 2 * unit), flat(2 * unit)),
+        (flat(8 * span),) * 4 + (flat(2 * unit),) * 2,
         [
-            pltpu.VMEM((groups, count, sub, width), BF),
-            wide,
             pltpu.VMEM((2, rows, width), BF),
             pltpu.VMEM((4, cuts, groups, count, HALO, width), BF),
             big, big, big, big, wide,
             pltpu.VMEM((32 * cols + HALO, LANES), F32),
         ],
-        24, bits, *f, *c, near, side, kernel, w_query, w_key, w_value, w_out,
-    )
+        24, bits, placed, conv, acted, *c, near, side, weights,
+    )
+
+    lines = [2**i for i in range(1, blocks.bit_length() - 1)]
 
     def sent(parts, n):
         return total(*(t[n : 2 * n] for t in parts))
@@ -423,61 +458,70 @@
     def kept(parts, got, n):
         return [t[:n] for t in parts] + [got[:n]]
 
-    def line_sum(parts):
-        got = swap(sent(parts, span), over_z)
-        mine = total(*kept(parts, got, span))
-        mask = 2 * over_z
-        while mask < blocks:
+    def halved(parts, n, mask):
+        return kept(parts, swap(sent(parts, n), mask), n)
+
+    def exchanged(parts, masks):
+        mine = total(*parts)
+        for mask in masks:
             mine = total(mine, swap(mine, mask))
-            mask *= 2
         return mine
 
+    def doubled(x, mask):
+        return jnp.concatenate([x, swap(x, mask)])
+
     a = [a_keep, swap(a_send, over_core)]
-    core_got = swap(b_send, over_core)
-    b = [b_keep, core_got]
-    a = kept(a, swap(sent(a, 4 * span), over_x), 4 * span)
-    y_got = swap(
-        jnp.concatenate([sent(b, 4 * span), back_keep[unit:], core_got[8 * span + unit :]]), over_y
-    )
-    b = kept(b, y_got, 4 * span)
-    a = kept(a, swap(sent(a, 2 * span), over_y), 2 * span)
+    b = [b_keep, swap(b_send, over_core)]
+    core_got = swap(back_send, over_core)
+    a = halved(a, 4 * span, over_x)
+    b = halved(b, 4 * span, lines[0])
+    y_got = swap(jnp.concatenate([back_keep[unit:], core_got[unit:]]), over_y)
     edge = flat(count * cols * HALO)
     layer_out, dconv, x_edge, z_edge = call(
-        functools.partial(home_kernel, (count, sub, cols, 8 * span, 4 * span)),
+        functools.partial(home_kernel, (count, sub, cols)),
         (shape(frames.shape, BF), shape((count, cols, length, LANES), BF), edge, edge),
         [], 8, bits, back_keep, core_got, y_got,
     )
-    x_got = swap(jnp.concatenate([sent(b, 2 * span), x_edge]), over_x)
-    b = kept(b, x_got, 2 * span)
     z_got = permute(
         z_edge,
         both([(m * blocks + t, m * blocks + t + 1)
               for m in range(groups) for t in range(1, blocks - 1, 2)]),
     )
-    a, b = line_sum(a), line_sum(b)
-    a = jnp.concatenate([a, swap(a, over_z)])
-    b = jnp.concatenate([b, swap(b, over_z)])
+    a = halved(a, 2 * span, over_y)
+    b = halved(b, 2 * span, lines[1])
+    a = halved(a, span, lines[0])
+    x_got = swap(jnp.concatenate([sent(b, span), x_edge]), over_x)
+    b = kept(b, x_got, span)
+    a = exchanged(a, lines[1:])
+    b = exchanged(b, [over_y] + lines[2:])
+    a = doubled(a, lines[0])
+    b = doubled(b, over_x)
     b, z_got = lax.optimization_barrier((b, z_got))
-    frame_grad = call(
-        functools.partial(frame_kernel, (count, cols, 2 * span, length)),
-        shape(frames.shape, BF), [], 8, bits, dconv, x_got, z_got, cotangent, kernel,
-    )
-    a = jnp.concatenate([a, swap(a, over_y)])
-    b = jnp.concatenate([b, swap(b, over_x)])
-    a_far, b_far = swap(a, over_x), swap(b, over_y)
+    (frame_grad,) = call(
+        functools.partial(frame_kernel, (count, cols, span, length)),
+        (shape(frames.shape, BF),), [], 8, bits, dconv, x_got, z_got, cotangent, kernel,
+    )
+    a = doubled(a, over_y)
+    b = doubled(b, lines[1])
+    a_far, b_far = swap(a, over_x), swap(b, lines[0])
     a_other, b_other = swap(a, over_core), swap(b, over_core)
-    b_far, frame_grad = lax.optimization_barrier((b_far, frame_grad))
     a_other_far, b_other_far = swap(a_far, over_core), swap(b_far, over_core)
 
     norm = 1.0 / math.sqrt(groups * count * blocks * length)
     square = shape((width, width), F32)
-    grads = call(
-        functools.partial(final_kernel, (width, norm)),
-        (shape((31, width), F32), square, square, square, square),
-        [pltpu.VMEM((32, HALO, LANES), F32)],
-        16, bits, a, b, a_far, b_far, a_other, b_other, a_other_far, b_other_far,
-    )
-    return (layer_out, frame_grad, *grads)
+    scratch = [pltpu.VMEM((2, width, width), F32), pltpu.SemaphoreType.DMA((2,))]
+    final = functools.partial(final_kernel, (width, norm))
+    *grads, tails = call(
+        functools.partial(final, True), (square,) * 4 + (shape((16, HALO, LANES), F32),), scratch,
+        8, bits, a, b, a_far, b_far, hbm_outs=range(4),
+    )
+    *grads, kernel_grad = call(
+        functools.partial(final, False), (square,) * 4 + (shape((31, width), F32),),
+        scratch + [pltpu.VMEM((32, HALO, LANES), F32)],
+        8, bits, a_other, b_other, a_other_far, b_other_far, *grads, tails,
+        hbm=range(5, 9), hbm_outs=range(4), aliases={5 + i: i for i in range(4)},
+    )
+    return (layer_out, frame_grad, kernel_grad, *grads)
 
 
 def solution(mesh):

time: 95.7 us -> 89.9 us (0.939)
  waiting for transfers between devices: 32.7 us -> 28.1 us
  local copies, waits for them, and re-layouts: 5.17 us -> 1.1 us
  Pallas kernels: 19.2 us -> 21.9 us
  other arithmetic: 0.59 us -> 2.4 us
  starting transfers between devices: 36.8 us -> 35.1 us
    ppermute x29 -> x31, waiting for transfers between devices: 32.7 us -> 28.1 us  [permute(): return lax.ppermute(x, ('mic', 'tm'), pairs)]
    unnamed x17 -> x7, local copies, waits for them, and re-layouts: 5.05 us -> 0.97 us
    pallas_call x6 -> x9, Pallas kernels: 19.2 us -> 21.9 us  [call(): pl.pallas_call(body, out_shape=outs, in_specs=[pl.BlockSpec(memory_space=...]
    another operation x0 -> x1, other arithmetic: none -> 1.82 us  [shards(): weights = jnp.stack([w_query, w_key, w_value, w_out])]
    ppermute x29 -> x31, starting transfers between devices: 36.8 us -> 35.1 us  [permute(): return lax.ppermute(x, ('mic', 'tm'), pairs)]
  transfers between devices with their start and end apart: 29 -> 31, of which waited for: 16 -> 16; matrix products, arithmetic and copies ran while one was open for 1% -> 3% of each run, Pallas kernels for 4% -> 11%
where the time goes in v6:
time: 89.9 us; the launch traced here: 89.7 us
  starting transfers between devices  35.1 us (39%)
  waiting for transfers between devices  28.1 us (31%)
  Pallas kernels  21.9 us (24%)
  other arithmetic  2.4 us (3%)
  local copies, waits for them, and re-layouts  1.1 us (1%)
  between operations  1.02 us (1%)
    ppermute x31, starting transfers between devices, permute(): return lax.ppermute(x, ('mic', 'tm'), pairs)  35.1 us
    ppermute x31, waiting for transfers between devices, permute(): return lax.ppermute(x, ('mic', 'tm'), pairs)  28.1 us
    pallas_call x9, Pallas kernels, call(): pl.pallas_call(body, out_shape=outs, in_specs=[pl.BlockSpec(memory_space=...  21.9 us
    another operation x1, other arithmetic, shards(): weights = jnp.stack([w_query, w_key, w_value, w_out])  1.82 us
  transfers between devices with their start and end apart: 31, of which 16 were waited for; matrix products, arithmetic and copies ran while one was open for 3% of the time, Pallas kernels for 11%

profile of v6, /device:TPU:0, one launch (start us, length us, event | category | flops | bytes accessed | tf_op | source)
XLA Modules:
  0.0 89.7 jit_solution(4261902063337673068)
XLA Ops:
  0.9 0.9 %copy-done.1 = bf16[2,128,512]{2,1,0:T(8,128)(2,1)S(1)} copy-done((bf16[2,128,512]{2,1,0:T(8,128)(2,1)S(1)}, bf16[2,128,512]{2,1,0:T(8,128)(2,1)}, u32[]{:S(2)}) %copy-start.1) | copy-done | bytes 262168
  1.8 0.8 shard_map.126
  2.6 0.5 collective-permute-start
  3.1 2.6 %collective-permute-start.1 = (bf16[2,32,512]{2,1,0:T(8,128)(2,1)S(1)}, bf16[2,32,512]{2,1,0:T(8,128)(2,1)S(1)}, u32[]{:S(2)}, u32[]{:S(2)}) collective-permute-start(bf16[2,32,512]{2,1,0:T(8,128)(2,1)S(1)} %get-tuple-element.47), channel_id=1, source_target_pairs={{0,16},{1,17},{2,18},{3,19},{4,20},{5,21},{6,22},{7,23},{8,24},{9,... | collective-permute-start | bytes 196616 | tf_op jit(solution)/shard_map/ppermute | solution.py:393
  5.8 1.8 %pad_maximum_fusion.weights = bf16[4,512,512]{2,1,0:T(8,128)(2,1)S(1)} fusion(bf16[1,512,512]{2,1,0:T(8,128)(2,1)} %bitcast.15, bf16[1,512,512]{2,1,0:T(8,128)(2,1)} %bitcast.16, bf16[1,512,512]{2,1,0:T(8,128)(2,1)} %bitcast.17, bf16[1,512,512]{2,1,0:T(8,128)(2,1)} %bitcast.18), kind=kLoop, calls=%fused_computation | loop fusion | flops 3145728 | bytes 4194304 | tf_op jit(solution)/shard_map/stack | solution.py:413
  7.6 0.8 collective-permute-done.1.f2
  8.4 1.4 %collective-permute-done.2.f3 = bf16[2,32,512]{2,1,0:T(8,128)(2,1)S(1)} collective-permute-done((bf16[2,32,512]{2,1,0:T(8,128)(2,1)S(1)}, bf16[2,32,512]{2,1,0:T(8,128)(2,1)S(1)}, u32[]{:S(2)}, u32[]{:S(2)}) %collective-permute-start.2) | collective-permute-done | bytes 65568 | tf_op jit(solution)/shard_map/ppermute | solution.py:393
  9.7 0.6 shard_map.127
  10.3 0.2 collective-permute-start.3
  10.5 0.7 collective-permute-start.4
  11.2 0.8 shard_map.129
  12.0 2.7 %collective-permute-start.5 = (bf16[2,32,512]{2,1,0:T(8,128)(2,1)S(1)}, bf16[2,32,512]{2,1,0:T(8,128)(2,1)S(1)}, u32[]{:S(2)}, u32[]{:S(2)}) collective-permute-start(bf16[2,32,512]{2,1,0:T(8,128)(2,1)S(1)} %get-tuple-element.57), channel_id=1, source_target_pairs={{0,8},{1,9},{2,10},{3,11},{4,12},{5,13},{6,14},{7,15},{8,0},{9,1},... | collective-permute-start | bytes 196616 | tf_op jit(solution)/shard_map/ppermute | solution.py:393
  14.7 1.6 %collective-permute-start.6 = (bf16[2,32,512]{2,1,0:T(8,128)(2,1)S(1)}, bf16[2,32,512]{2,1,0:T(8,128)(2,1)S(1)}, u32[]{:S(2)}, u32[]{:S(2)}) collective-permute-start(bf16[2,32,512]{2,1,0:T(8,128)(2,1)S(1)} %get-tuple-element.58), channel_id=1, source_target_pairs={{0,16},{1,17},{2,18},{3,19},{4,20},{5,21},{6,22},{7,23},{8,24},{9,... | collective-permute-start | bytes 196616 | tf_op jit(solution)/shard_map/ppermute | solution.py:393
  16.4 2.5 %shard_map.128 = (bf16[4,2,32,512]{3,2,1,0:T(8,128)(2,1)S(1)}, f32[256,512]{1,0:T(8,128)S(1)}, bf16[256,512]{1,0:T(8,128)(2,1)S(1)}) custom-call(s32[11]{0:T(128)S(1)} %stack.62.bits, bf16[2,32,512]{2,1,0:T(8,128)(2,1)S(1)} %get-tuple-element.45.f0, bf16[2,32,512]{2,1,0:T(8,128)(2,1)S(1)} %collective-permute-done.f1, ...), custom_call_target="tpu_custom_call" | custom-call | tf_op jit(solution)/shard_map/pallas_call | solution.py:354
  19.0 1.4 %collective-permute-done.7.c3 = bf16[2,32,512]{2,1,0:T(8,128)(2,1)S(1)} collective-permute-done((bf16[2,32,512]{2,1,0:T(8,128)(2,1)S(1)}, bf16[2,32,512]{2,1,0:T(8,128)(2,1)S(1)}, u32[]{:S(2)}, u32[]{:S(2)}) %collective-permute-start.7) | collective-permute-done | bytes 65568 | tf_op jit(solution)/shard_map/ppermute | solution.py:393
  20.3 8.4 %shard_map.130 = (bf16[2176,128]{1,0:T(8,128)(2,1)S(1)}, bf16[2176,128]{1,0:T(8,128)(2,1)S(1)}, bf16[2176,128]{1,0:T(8,128)(2,1)S(1)}, bf16[2176,128]{1,0:T(8,12...) custom-call(s32[11]{0:T(128)S(1)} %stack.62.bits, ...), custom_call_target="tpu_custom_call" | custom-call | tf_op jit(solution)/shard_map/pallas_call | solution.py:354
  29.0 0.4 collective-permute-start.8
  29.6 1.6 %collective-permute-done.8.core_got = bf16[1024,128]{1,0:T(8,128)(2,1)S(1)} collective-permute-done((bf16[1024,128]{1,0:T(8,128)(2,1)S(1)}, bf16[1024,128]{1,0:T(8,128)(2,1)S(1)}, u32[]{:S(2)}, u32[]{:S(2)}) %collective-permute-start.8) | collective-permute-done | bytes 262176 | tf_op jit(solution)/shard_map/ppermute | solution.py:393
  31.2 1.4 %collective-permute-start.9 = (bf16[1024,128]{1,0:T(8,128)(2,1)S(1)}, bf16[1024,128]{1,0:T(8,128)(2,1)S(1)}, u32[]{:S(2)}, u32[]{:S(2)}) collective-permute-start(bf16[1024,128]{1,0:T(8,128)(2,1)S(1)} %pad_maximum_fusion.2), channel_id=1, source_target_pairs={{0,16},{1,17},{2,18},{3,19},{4,20},{5,21},{6,22},{7,23},{8,24},{9,... | collective-permute-start | bytes 786440 | tf_op jit(solution)/shard_map/ppermute | solution.py:393
  32.7 1.3 %collective-permute-start.18 = (bf16[1088,128]{1,0:T(8,128)(2,1)S(1)}, bf16[1088,128]{1,0:T(8,128)(2,1)S(1)}, u32[]{:S(2)}, u32[]{:S(2)}) collective-permute-start(bf16[1088,128]{1,0:T(8,128)(2,1)S(1)} %add_convert_fusion), channel_id=1, source_target_pairs={{0,1},{1,0},{2,3},{3,2},{4,5},{5,4},{6,7},{7,6},{8,9},{9,8},{10,11... | collective-permute-start | bytes 835592 | tf_op jit(solution)/shard_map/ppermute | solution.py:393
  34.0 1.6 %collective-permute-start.11 = (bf16[1088,128]{1,0:T(8,128)(2,1)S(1)}, bf16[1088,128]{1,0:T(8,128)(2,1)S(1)}, u32[]{:S(2)}, u32[]{:S(2)}) collective-permute-start(bf16[1088,128]{1,0:T(8,128)(2,1)S(1)} %add_convert_fusion.1), channel_id=1, source_target_pairs={{0,2},{1,3},{2,0},{3,1},{4,6},{5,7},{6,4},{7,5},{8,10},{9,11},{10,... | collective-permute-start | bytes 835592 | tf_op jit(solution)/shard_map/ppermute | solution.py:393
  35.6 4.0 %collective-permute-done.9.y_got = bf16[1024,128]{1,0:T(8,128)(2,1)S(1)} collective-permute-done((bf16[1024,128]{1,0:T(8,128)(2,1)S(1)}, bf16[1024,128]{1,0:T(8,128)(2,1)S(1)}, u32[]{:S(2)}, u32[]{:S(2)}) %collective-permute-start.9) | collective-permute-done | bytes 262176 | tf_op jit(solution)/shard_map/ppermute | solution.py:393
  39.6 1.3 %shard_map.131 = (bf16[2,128,512]{2,1,0:T(8,128)(2,1)}, bf16[2,4,128,128]{3,2,1,0:T(8,128)(2,1)S(1)}, bf16[128,128]{1,0:T(8,128)(2,1)S(1)}, bf16[128,128]{1,0:T(8,128)(2,1)S(1)}) custom-call(s32[11]{0:T(128)S(1)} %stack.62.bits, bf16[1024,128]{1,0:T(8,128)(2,1)S(1)} %get-tuple-element.61.own, bf16[1024,128]{1,0:T(8,128)(2,1)S(1)} %collective-permute-done.8.core_got, ...), custom_call_target="tpu_custom_call" | custom-call | tf_op jit(solution)/shard_map/pallas_call | solution.py:354
  40.9 0.7 collective-permute-start.16
  41.6 1.5 %collective-permute-start.19 = (bf16[544,128]{1,0:T(8,128)(2,1)S(1)}, bf16[544,128]{1,0:T(8,128)(2,1)S(1)}, u32[]{:S(2)}, u32[]{:S(2)}) collective-permute-start(bf16[544,128]{1,0:T(8,128)(2,1)S(1)} %add_convert_fusion.2), channel_id=1, source_target_pairs={{0,16},{1,17},{2,18},{3,19},{4,20},{5,21},{6,22},{7,23},{8,24},{9,... | collective-permute-start | bytes 417800 | tf_op jit(solution)/shard_map/ppermute | solution.py:393
  43.2 4.8 %collective-permute-start.12 = (bf16[544,128]{1,0:T(8,128)(2,1)S(1)}, bf16[544,128]{1,0:T(8,128)(2,1)S(1)}, u32[]{:S(2)}, u32[]{:S(2)}) collective-permute-start(bf16[544,128]{1,0:T(8,128)(2,1)S(1)} %add_convert_fusion.3), channel_id=1, source_target_pairs={{0,4},{1,5},{2,6},{3,7},{4,0},{5,1},{6,2},{7,3},{8,12},{9,13},{10,... | collective-permute-start | bytes 417800 | tf_op jit(solution)/shard_map/ppermute | solution.py:393
  48.1 3.4 %collective-permute-start.20 = (bf16[272,128]{1,0:T(8,128)(2,1)S(1)}, bf16[272,128]{1,0:T(8,128)(2,1)S(1)}, u32[]{:S(2)}, u32[]{:S(2)}) collective-permute-start(bf16[272,128]{1,0:T(8,128)(2,1)S(1)} %add_convert_fusion.6), channel_id=1, source_target_pairs={{0,2},{1,3},{2,0},{3,1},{4,6},{5,7},{6,4},{7,5},{8,10},{9,11},{10,... | collective-permute-start | bytes 208904 | tf_op jit(solution)/shard_map/ppermute | solution.py:393
  51.5 2.6 %collective-permute-done.12 = bf16[544,128]{1,0:T(8,128)(2,1)S(1)} collective-permute-done((bf16[544,128]{1,0:T(8,128)(2,1)S(1)}, bf16[544,128]{1,0:T(8,128)(2,1)S(1)}, u32[]{:S(2)}, u32[]{:S(2)}) %collective-permute-start.12) | collective-permute-done | bytes 139296 | tf_op jit(solution)/shard_map/ppermute | solution.py:393
  54.2 2.0 %collective-permute-start.13 = (bf16[400,128]{1,0:T(8,128)(2,1)S(1)}, bf16[400,128]{1,0:T(8,128)(2,1)S(1)}, u32[]{:S(2)}, u32[]{:S(2)}) collective-permute-start(bf16[400,128]{1,0:T(8,128)(2,1)S(1)} %pad_maximum_fusion.5), channel_id=1, source_target_pairs={{0,1},{1,0},{2,3},{3,2},{4,5},{5,4},{6,7},{7,6},{8,9},{9,8},{10,11... | collective-permute-start | bytes 307208 | tf_op jit(solution)/shard_map/ppermute | solution.py:393
  56.2 0.9 %collective-permute-start.21 = (bf16[272,128]{1,0:T(8,128)(2,1)S(1)}, bf16[272,128]{1,0:T(8,128)(2,1)S(1)}, u32[]{:S(2)}, u32[]{:S(2)}) collective-permute-start(bf16[272,128]{1,0:T(8,128)(2,1)S(1)} %add_convert_fusion.5), channel_id=1, source_target_pairs={{0,4},{1,5},{2,6},{3,7},{4,0},{5,1},{6,2},{7,3},{8,12},{9,13},{10,... | collective-permute-start | bytes 208904 | tf_op jit(solution)/shard_map/ppermute | solution.py:393
  57.1 1.8 %collective-permute-done.13.x_got = bf16[400,128]{1,0:T(8,128)(2,1)S(1)} collective-permute-done((bf16[400,128]{1,0:T(8,128)(2,1)S(1)}, bf16[400,128]{1,0:T(8,128)(2,1)S(1)}, u32[]{:S(2)}, u32[]{:S(2)}) %collective-permute-start.13) | collective-permute-done | bytes 102432 | tf_op jit(solution)/shard_map/ppermute | solution.py:393
  58.9 1.5 %collective-permute-start.14 = (bf16[272,128]{1,0:T(8,128)(2,1)S(1)}, bf16[272,128]{1,0:T(8,128)(2,1)S(1)}, u32[]{:S(2)}, u32[]{:S(2)}) collective-permute-start(bf16[272,128]{1,0:T(8,128)(2,1)S(1)} %add_convert_fusion.8), channel_id=1, source_target_pairs={{0,16},{1,17},{2,18},{3,19},{4,20},{5,21},{6,22},{7,23},{8,24},{9,... | collective-permute-start | bytes 208904 | tf_op jit(solution)/shard_map/ppermute | solution.py:393
  60.5 1.0 %collective-permute-done.21 = bf16[272,128]{1,0:T(8,128)(2,1)S(1)} collective-permute-done((bf16[272,128]{1,0:T(8,128)(2,1)S(1)}, bf16[272,128]{1,0:T(8,128)(2,1)S(1)}, u32[]{:S(2)}, u32[]{:S(2)}) %collective-permute-start.21) | collective-permute-done | bytes 69664 | tf_op jit(solution)/shard_map/ppermute | solution.py:393
  61.6 1.7 %collective-permute-done.14 = bf16[272,128]{1,0:T(8,128)(2,1)S(1)} collective-permute-done((bf16[272,128]{1,0:T(8,128)(2,1)S(1)}, bf16[272,128]{1,0:T(8,128)(2,1)S(1)}, u32[]{:S(2)}, u32[]{:S(2)}) %collective-permute-start.14) | collective-permute-done | bytes 69664 | tf_op jit(solution)/shard_map/ppermute | solution.py:393
  63.3 2.0 %collective-permute-start.15 = (bf16[272,128]{1,0:T(8,128)(2,1)S(1)}, bf16[272,128]{1,0:T(8,128)(2,1)S(1)}, u32[]{:S(2)}, u32[]{:S(2)}) collective-permute-start(bf16[272,128]{1,0:T(8,128)(2,1)S(1)} %add_convert_fusion.7), channel_id=1, source_target_pairs={{0,1},{1,0},{2,3},{3,2},{4,5},{5,4},{6,7},{7,6},{8,9},{9,8},{10,11... | collective-permute-start | bytes 208904 | tf_op jit(solution)/shard_map/ppermute | solution.py:393
  65.3 0.6 collective-permute-done.22
  65.9 1.2 %collective-permute-start.23 = (bf16[544,128]{1,0:T(8,128)(2,1)S(1)}, bf16[544,128]{1,0:T(8,128)(2,1)S(1)}, u32[]{:S(2)}, u32[]{:S(2)}) collective-permute-start(bf16[544,128]{1,0:T(8,128)(2,1)S(1)} %pad_maximum_fusion.4), channel_id=1, source_target_pairs={{0,16},{1,17},{2,18},{3,19},{4,20},{5,21},{6,22},{7,23},{8,24},{9,... | collective-permute-start | bytes 417800 | tf_op jit(solution)/shard_map/ppermute | solution.py:393
  67.1 0.6 collective-permute-done.15
  67.7 1.4 %collective-permute-start.25 = (bf16[544,128]{1,0:T(8,128)(2,1)S(1)}, bf16[544,128]{1,0:T(8,128)(2,1)S(1)}, u32[]{:S(2)}, u32[]{:S(2)}) collective-permute-start(bf16[544,128]{1,0:T(8,128)(2,1)S(1)} %pad_maximum_fusion.3), channel_id=1, source_target_pairs={{0,4},{1,5},{2,6},{3,7},{4,0},{5,1},{6,2},{7,3},{8,12},{9,13},{10,... | collective-permute-start | bytes 417800 | tf_op jit(solution)/shard_map/ppermute | solution.py:393
  69.1 1.9 %collective-permute-done.23 = bf16[544,128]{1,0:T(8,128)(2,1)S(1)} collective-permute-done((bf16[544,128]{1,0:T(8,128)(2,1)S(1)}, bf16[544,128]{1,0:T(8,128)(2,1)S(1)}, u32[]{:S(2)}, u32[]{:S(2)}) %collective-permute-start.23) | collective-permute-done | bytes 139296 | tf_op jit(solution)/shard_map/ppermute | solution.py:393
  71.1 1.4 %collective-permute-start.27 = (bf16[1088,128]{1,0:T(8,128)(2,1)S(1)}, bf16[1088,128]{1,0:T(8,128)(2,1)S(1)}, u32[]{:S(2)}, u32[]{:S(2)}) collective-permute-start(bf16[1088,128]{1,0:T(8,128)(2,1)S(1)} %pad_maximum_fusion.1.a_near), channel_id=1, source_target_pairs={{0,1},{1,0},{2,3},{3,2},{4,5},{5,4},{6,7},{7,6},{8,9},{9,8},{10,11... | collective-permute-start | bytes 835592 | tf_op jit(solution)/shard_map/ppermute | solution.py:393
  72.4 3.0 %collective-permute-done.25 = bf16[544,128]{1,0:T(8,128)(2,1)S(1)} collective-permute-done((bf16[544,128]{1,0:T(8,128)(2,1)S(1)}, bf16[544,128]{1,0:T(8,128)(2,1)S(1)}, u32[]{:S(2)}, u32[]{:S(2)}) %collective-permute-start.25) | collective-permute-done | bytes 139296 | tf_op jit(solution)/shard_map/ppermute | solution.py:393
  75.5 0.5 collective-permute-start.26
  76.0 1.6 %collective-permute-done.27.a_far = bf16[1088,128]{1,0:T(8,128)(2,1)S(1)} collective-permute-done((bf16[1088,128]{1,0:T(8,128)(2,1)S(1)}, bf16[1088,128]{1,0:T(8,128)(2,1)S(1)}, u32[]{:S(2)}, u32[]{:S(2)}) %collective-permute-start.27) | collective-permute-done | bytes 278560 | tf_op jit(solution)/shard_map/ppermute | solution.py:393
  77.7 4.3 %collective-permute-done.29.b_far = bf16[1088,128]{1,0:T(8,128)(2,1)S(1)} collective-permute-done((bf16[1088,128]{1,0:T(8,128)(2,1)S(1)}, bf16[1088,128]{1,0:T(8,128)(2,1)S(1)}, u32[]{:S(2)}, u32[]{:S(2)}) %collective-permute-start.29) | collective-permute-done | bytes 278560 | tf_op jit(solution)/shard_map/ppermute | solution.py:393
  82.0 2.9 %shard_map.132 = bf16[2,128,512]{2,1,0:T(8,128)(2,1)} custom-call(s32[11]{0:T(128)S(1)} %stack.62.bits, bf16[2,4,128,128]{3,2,1,0:T(8,128)(2,1)S(1)} %get-tuple-element.64.dconv, bf16[400,128]{1,0:T(8,128)(2,1)S(1)} %collective-permute-done.13.x_got, bf16[128,128]{1,0:T(8,128)(2,1)S(1)} %collective-permute-done.16.z_got, bf16[2,128,512]{2,1,0:T(8,128)(2,1)S(1)} %copy-done, ...), custom_call_target="tpu_custom_call" | custom-call | tf_op jit(solution)/shard_map/pallas_call | solution.py:354
  84.9 2.1 %shard_map.133 = (f32[512,512]{1,0:T(8,128)}, f32[512,512]{1,0:T(8,128)}, f32[512,512]{1,0:T(8,128)}, f32[512,512]{1,0:T(8,128)}, f32[16,16,128]{2,1,0:T(8,128)S(1)}) custom-call(s32[11]{0:T(128)S(1)} %stack.62.bits, bf16[1088,128]{1,0:T(8,128)(2,1)S(1)} %pad_maximum_fusion.1.a_near, bf16[1088,128]{1,0:T(8,128)(2,1)S(1)} %constant_dynamic-update-slice_fusion.b_near, ...), custom_call_target="tpu_custom_call" | custom-call | tf_op jit(solution)/shard_map/pallas_call | solution.py:354
  87.0 2.7 %shard_map.134 = (f32[512,512]{1,0:T(8,128)}, f32[512,512]{1,0:T(8,128)}, f32[512,512]{1,0:T(8,128)}, f32[512,512]{1,0:T(8,128)}, f32[31,512]{1,0:T(8,128)}) custom-call(s32[11]{0:T(128)S(1)} %stack.62.bits, bf16[1088,128]{1,0:T(8,128)(2,1)S(1)} %collective-permute-done.24.a_near, ...), custom_call_target="tpu_custom_call", output_to_operand_aliasing={{0}: (5, {}), {1}: (6, {}), {2}: (7, {}), {3}: (8, {})} | custom-call | tf_op jit(solution)/shard_map/pallas_call | solution.py:354
  (50 shorter events, 1.6 us)
Async XLA Ops:
  0.8 1.0 %copy-start.1 = (bf16[2,128,512]{2,1,0:T(8,128)(2,1)S(1)}, bf16[2,128,512]{2,1,0:T(8,128)(2,1)}, u32[]{:S(2)}) copy-start(bf16[2,128,512]{2,1,0:T(8,128)(2,1)} %source.2) | copy-start | bytes 786436
  2.6 5.0 %collective-permute-start = (bf16[2,32,512]{2,1,0:T(8,128)(2,1)S(1)}, bf16[2,32,512]{2,1,0:T(8,128)(2,1)S(1)}, u32[]{:S(2)}, u32[]{:S(2)}) collective-permute-start(bf16[2,32,512]{2,1,0:T(8,128)(2,1)S(1)} %get-tuple-element.46), channel_id=1, source_target_pairs={{0,8},{1,9},{2,10},{3,11},{4,12},{5,13},{6,14},{7,15},{8,0},{9,1},... | collective-permute-start | bytes 196616 | tf_op jit(solution)/shard_map/ppermute | solution.py:393
  3.1 5.3 %collective-permute-start.1 = (bf16[2,32,512]{2,1,0:T(8,128)(2,1)S(1)}, bf16[2,32,512]{2,1,0:T(8,128)(2,1)S(1)}, u32[]{:S(2)}, u32[]{:S(2)}) collective-permute-start(bf16[2,32,512]{2,1,0:T(8,128)(2,1)S(1)} %get-tuple-element.47), channel_id=1, source_target_pairs={{0,16},{1,17},{2,18},{3,19},{4,20},{5,21},{6,22},{7,23},{8,24},{9,... | collective-permute-start | bytes 196616 | tf_op jit(solution)/shard_map/ppermute | solution.py:393
  5.7 4.0 %collective-permute-start.2 = (bf16[2,32,512]{2,1,0:T(8,128)(2,1)S(1)}, bf16[2,32,512]{2,1,0:T(8,128)(2,1)S(1)}, u32[]{:S(2)}, u32[]{:S(2)}) collective-permute-start(bf16[2,32,512]{2,1,0:T(8,128)(2,1)S(1)} %get-tuple-element.48), channel_id=1, source_target_pairs={{0,24},{1,25},{2,26},{3,27},{4,28},{5,29},{6,30},{7,31},{8,16},{9,... | collective-permute-start | bytes 196616 | tf_op jit(solution)/shard_map/ppermute | solution.py:393
  5.7 5.4 %copy-start = (bf16[2,128,512]{2,1,0:T(8,128)(2,1)S(1)}, bf16[2,128,512]{2,1,0:T(8,128)(2,1)}, u32[]{:S(2)}) copy-start(bf16[2,128,512]{2,1,0:T(8,128)(2,1)} %cot.1) | copy-start | bytes 786436
  5.8 10.6 %copy-start.2 = (f32[31,512]{1,0:T(8,128)S(1)}, f32[31,512]{1,0:T(8,128)}, u32[]{:S(2)}) copy-start(f32[31,512]{1,0:T(8,128)} %kern.3) | copy-start | bytes 190468
  10.3 6.1 %collective-permute-start.3 = (bf16[4,2,16,512]{3,2,1,0:T(8,128)(2,1)S(1)}, bf16[4,2,16,512]{3,2,1,0:T(8,128)(2,1)S(1)}, u32[]{:S(2)}, u32[]{:S(2)}) collective-permute-start(bf16[4,2,16,512]{3,2,1,0:T(8,128)(2,1)S(1)} %get-tuple-element.51), channel_id=1, source_target_pairs={{0,8},{1,9},{2,10},{3,11},{4,12},{5,13},{6,14},{7,15},{8,0},{9,1},... | collective-permute-start | bytes 393224 | tf_op jit(solution)/shard_map/ppermute | solution.py:393
  10.5 5.8 %collective-permute-start.4 = (bf16[4,2,16,512]{3,2,1,0:T(8,128)(2,1)S(1)}, bf16[4,2,16,512]{3,2,1,0:T(8,128)(2,1)S(1)}, u32[]{:S(2)}, u32[]{:S(2)}) collective-permute-start(bf16[4,2,16,512]{3,2,1,0:T(8,128)(2,1)S(1)} %get-tuple-element.52), channel_id=1, source_target_pairs={{8,24},{9,25},{10,26},{11,27},{12,28},{13,29},{14,30},{15,31},{24,... | collective-permute-start | bytes 393224 | tf_op jit(solution)/shard_map/ppermute | solution.py:393
  12.0 6.9 %collective-permute-start.5 = (bf16[2,32,512]{2,1,0:T(8,128)(2,1)S(1)}, bf16[2,32,512]{2,1,0:T(8,128)(2,1)S(1)}, u32[]{:S(2)}, u32[]{:S(2)}) collective-permute-start(bf16[2,32,512]{2,1,0:T(8,128)(2,1)S(1)} %get-tuple-element.57), channel_id=1, source_target_pairs={{0,8},{1,9},{2,10},{3,11},{4,12},{5,13},{6,14},{7,15},{8,0},{9,1},... | collective-permute-start | bytes 196616 | tf_op jit(solution)/shard_map/ppermute | solution.py:393
  14.7 4.3 %collective-permute-start.6 = (bf16[2,32,512]{2,1,0:T(8,128)(2,1)S(1)}, bf16[2,32,512]{2,1,0:T(8,128)(2,1)S(1)}, u32[]{:S(2)}, u32[]{:S(2)}) collective-permute-start(bf16[2,32,512]{2,1,0:T(8,128)(2,1)S(1)} %get-tuple-element.58), channel_id=1, source_target_pairs={{0,16},{1,17},{2,18},{3,19},{4,20},{5,21},{6,22},{7,23},{8,24},{9,... | collective-permute-start | bytes 196616 | tf_op jit(solution)/shard_map/ppermute | solution.py:393
  16.3 4.0 %collective-permute-start.7 = (bf16[2,32,512]{2,1,0:T(8,128)(2,1)S(1)}, bf16[2,32,512]{2,1,0:T(8,128)(2,1)S(1)}, u32[]{:S(2)}, u32[]{:S(2)}) collective-permute-start(bf16[2,32,512]{2,1,0:T(8,128)(2,1)S(1)} %get-tuple-element.59), channel_id=1, source_target_pairs={{0,24},{1,25},{2,26},{3,27},{4,28},{5,29},{6,30},{7,31},{8,16},{9,... | collective-permute-start | bytes 196616 | tf_op jit(solution)/shard_map/ppermute | solution.py:393
  28.7 3.8 %collective-permute-start.17 = (bf16[2176,128]{1,0:T(8,128)(2,1)S(1)}, bf16[2176,128]{1,0:T(8,128)(2,1)S(1)}, u32[]{:S(2)}, u32[]{:S(2)}) collective-permute-start(bf16[2176,128]{1,0:T(8,128)(2,1)S(1)} %get-tuple-element.71), channel_id=1, source_target_pairs={{0,8},{1,9},{2,10},{3,11},{4,12},{5,13},{6,14},{7,15},{8,0},{9,1},... | collective-permute-start | bytes 1671176 | tf_op jit(solution)/shard_map/ppermute | solution.py:393
  29.0 2.2 %collective-permute-start.8 = (bf16[1024,128]{1,0:T(8,128)(2,1)S(1)}, bf16[1024,128]{1,0:T(8,128)(2,1)S(1)}, u32[]{:S(2)}, u32[]{:S(2)}) collective-permute-start(bf16[1024,128]{1,0:T(8,128)(2,1)S(1)} %get-tuple-element.62), channel_id=1, source_target_pairs={{0,8},{1,9},{2,10},{3,11},{4,12},{5,13},{6,14},{7,15},{8,0},{9,1},... | collective-permute-start | bytes 786440 | tf_op jit(solution)/shard_map/ppermute | solution.py:393
  29.3 4.6 %collective-permute-start.10 = (bf16[2176,128]{1,0:T(8,128)(2,1)S(1)}, bf16[2176,128]{1,0:T(8,128)(2,1)S(1)}, u32[]{:S(2)}, u32[]{:S(2)}) collective-permute-start(bf16[2176,128]{1,0:T(8,128)(2,1)S(1)} %get-tuple-element.66), channel_id=1, source_target_pairs={{0,8},{1,9},{2,10},{3,11},{4,12},{5,13},{6,14},{7,15},{8,0},{9,1},... | collective-permute-start | bytes 1671176 | tf_op jit(solution)/shard_map/ppermute | solution.py:393
  31.2 8.4 %collective-permute-start.9 = (bf16[1024,128]{1,0:T(8,128)(2,1)S(1)}, bf16[1024,128]{1,0:T(8,128)(2,1)S(1)}, u32[]{:S(2)}, u32[]{:S(2)}) collective-permute-start(bf16[1024,128]{1,0:T(8,128)(2,1)S(1)} %pad_maximum_fusion.2), channel_id=1, source_target_pairs={{0,16},{1,17},{2,18},{3,19},{4,20},{5,21},{6,22},{7,23},{8,24},{9,... | collective-permute-start | bytes 786440 | tf_op jit(solution)/shard_map/ppermute | solution.py:393
  32.7 8.9 %collective-permute-start.18 = (bf16[1088,128]{1,0:T(8,128)(2,1)S(1)}, bf16[1088,128]{1,0:T(8,128)(2,1)S(1)}, u32[]{:S(2)}, u32[]{:S(2)}) collective-permute-start(bf16[1088,128]{1,0:T(8,128)(2,1)S(1)} %add_convert_fusion), channel_id=1, source_target_pairs={{0,1},{1,0},{2,3},{3,2},{4,5},{5,4},{6,7},{7,6},{8,9},{9,8},{10,11... | collective-permute-start | bytes 835592 | tf_op jit(solution)/shard_map/ppermute | solution.py:393
  34.0 9.2 %collective-permute-start.11 = (bf16[1088,128]{1,0:T(8,128)(2,1)S(1)}, bf16[1088,128]{1,0:T(8,128)(2,1)S(1)}, u32[]{:S(2)}, u32[]{:S(2)}) collective-permute-start(bf16[1088,128]{1,0:T(8,128)(2,1)S(1)} %add_convert_fusion.1), channel_id=1, source_target_pairs={{0,2},{1,3},{2,0},{3,1},{4,6},{5,7},{6,4},{7,5},{8,10},{9,11},{10,... | collective-permute-start | bytes 835592 | tf_op jit(solution)/shard_map/ppermute | solution.py:393
  40.9 26.8 %collective-permute-start.16 = (bf16[128,128]{1,0:T(8,128)(2,1)S(1)}, bf16[128,128]{1,0:T(8,128)(2,1)S(1)}, u32[]{:S(2)}, u32[]{:S(2)}) collective-permute-start(bf16[128,128]{1,0:T(8,128)(2,1)S(1)} %get-tuple-element.68), channel_id=1, source_target_pairs={{1,2},{3,4},{5,6},{9,10},{11,12},{13,14},{17,18},{19,20},{21,22},{... | collective-permute-start | bytes 98312 | tf_op jit(solution)/shard_map/ppermute | solution.py:393
  41.6 6.4 %collective-permute-start.19 = (bf16[544,128]{1,0:T(8,128)(2,1)S(1)}, bf16[544,128]{1,0:T(8,128)(2,1)S(1)}, u32[]{:S(2)}, u32[]{:S(2)}) collective-permute-start(bf16[544,128]{1,0:T(8,128)(2,1)S(1)} %add_convert_fusion.2), channel_id=1, source_target_pairs={{0,16},{1,17},{2,18},{3,19},{4,20},{5,21},{6,22},{7,23},{8,24},{9,... | collective-permute-start | bytes 417800 | tf_op jit(solution)/shard_map/ppermute | solution.py:393
  43.2 10.8 %collective-permute-start.12 = (bf16[544,128]{1,0:T(8,128)(2,1)S(1)}, bf16[544,128]{1,0:T(8,128)(2,1)S(1)}, u32[]{:S(2)}, u32[]{:S(2)}) collective-permute-start(bf16[544,128]{1,0:T(8,128)(2,1)S(1)} %add_convert_fusion.3), channel_id=1, source_target_pairs={{0,4},{1,5},{2,6},{3,7},{4,0},{5,1},{6,2},{7,3},{8,12},{9,13},{10,... | collective-permute-start | bytes 417800 | tf_op jit(solution)/shard_map/ppermute | solution.py:393
  48.1 8.0 %collective-permute-start.20 = (bf16[272,128]{1,0:T(8,128)(2,1)S(1)}, bf16[272,128]{1,0:T(8,128)(2,1)S(1)}, u32[]{:S(2)}, u32[]{:S(2)}) collective-permute-start(bf16[272,128]{1,0:T(8,128)(2,1)S(1)} %add_convert_fusion.6), channel_id=1, source_target_pairs={{0,2},{1,3},{2,0},{3,1},{4,6},{5,7},{6,4},{7,5},{8,10},{9,11},{10,... | collective-permute-start | bytes 208904 | tf_op jit(solution)/shard_map/ppermute | solution.py:393
  54.2 4.7 %collective-permute-start.13 = (bf16[400,128]{1,0:T(8,128)(2,1)S(1)}, bf16[400,128]{1,0:T(8,128)(2,1)S(1)}, u32[]{:S(2)}, u32[]{:S(2)}) collective-permute-start(bf16[400,128]{1,0:T(8,128)(2,1)S(1)} %pad_maximum_fusion.5), channel_id=1, source_target_pairs={{0,1},{1,0},{2,3},{3,2},{4,5},{5,4},{6,7},{7,6},{8,9},{9,8},{10,11... | collective-permute-start | bytes 307208 | tf_op jit(solution)/shard_map/ppermute | solution.py:393
  56.2 5.3 %collective-permute-start.21 = (bf16[272,128]{1,0:T(8,128)(2,1)S(1)}, bf16[272,128]{1,0:T(8,128)(2,1)S(1)}, u32[]{:S(2)}, u32[]{:S(2)}) collective-permute-start(bf16[272,128]{1,0:T(8,128)(2,1)S(1)} %add_convert_fusion.5), channel_id=1, source_target_pairs={{0,4},{1,5},{2,6},{3,7},{4,0},{5,1},{6,2},{7,3},{8,12},{9,13},{10,... | collective-permute-start | bytes 208904 | tf_op jit(solution)/shard_map/ppermute | solution.py:393
  58.9 4.4 %collective-permute-start.14 = (bf16[272,128]{1,0:T(8,128)(2,1)S(1)}, bf16[272,128]{1,0:T(8,128)(2,1)S(1)}, u32[]{:S(2)}, u32[]{:S(2)}) collective-permute-start(bf16[272,128]{1,0:T(8,128)(2,1)S(1)} %add_convert_fusion.8), channel_id=1, source_target_pairs={{0,16},{1,17},{2,18},{3,19},{4,20},{5,21},{6,22},{7,23},{8,24},{9,... | collective-permute-start | bytes 208904 | tf_op jit(solution)/shard_map/ppermute | solution.py:393
  61.5 4.4 %collective-permute-start.22 = (bf16[272,128]{1,0:T(8,128)(2,1)S(1)}, bf16[272,128]{1,0:T(8,128)(2,1)S(1)}, u32[]{:S(2)}, u32[]{:S(2)}) collective-permute-start(bf16[272,128]{1,0:T(8,128)(2,1)S(1)} %add_convert_fusion.4), channel_id=1, source_target_pairs={{0,2},{1,3},{2,0},{3,1},{4,6},{5,7},{6,4},{7,5},{8,10},{9,11},{10,... | collective-permute-start | bytes 208904 | tf_op jit(solution)/shard_map/ppermute | solution.py:393
  63.3 4.4 %collective-permute-start.15 = (bf16[272,128]{1,0:T(8,128)(2,1)S(1)}, bf16[272,128]{1,0:T(8,128)(2,1)S(1)}, u32[]{:S(2)}, u32[]{:S(2)}) collective-permute-start(bf16[272,128]{1,0:T(8,128)(2,1)S(1)} %add_convert_fusion.7), channel_id=1, source_target_pairs={{0,1},{1,0},{2,3},{3,2},{4,5},{5,4},{6,7},{7,6},{8,9},{9,8},{10,11... | collective-permute-start | bytes 208904 | tf_op jit(solution)/shard_map/ppermute | solution.py:393
  65.9 5.1 %collective-permute-start.23 = (bf16[544,128]{1,0:T(8,128)(2,1)S(1)}, bf16[544,128]{1,0:T(8,128)(2,1)S(1)}, u32[]{:S(2)}, u32[]{:S(2)}) collective-permute-start(bf16[544,128]{1,0:T(8,128)(2,1)S(1)} %pad_maximum_fusion.4), channel_id=1, source_target_pairs={{0,16},{1,17},{2,18},{3,19},{4,20},{5,21},{6,22},{7,23},{8,24},{9,... | collective-permute-start | bytes 417800 | tf_op jit(solution)/shard_map/ppermute | solution.py:393
  67.7 7.6 %collective-permute-start.25 = (bf16[544,128]{1,0:T(8,128)(2,1)S(1)}, bf16[544,128]{1,0:T(8,128)(2,1)S(1)}, u32[]{:S(2)}, u32[]{:S(2)}) collective-permute-start(bf16[544,128]{1,0:T(8,128)(2,1)S(1)} %pad_maximum_fusion.3), channel_id=1, source_target_pairs={{0,4},{1,5},{2,6},{3,7},{4,0},{5,1},{6,2},{7,3},{8,12},{9,13},{10,... | collective-permute-start | bytes 417800 | tf_op jit(solution)/shard_map/ppermute | solution.py:393
  71.1 6.6 %collective-permute-start.27 = (bf16[1088,128]{1,0:T(8,128)(2,1)S(1)}, bf16[1088,128]{1,0:T(8,128)(2,1)S(1)}, u32[]{:S(2)}, u32[]{:S(2)}) collective-permute-start(bf16[1088,128]{1,0:T(8,128)(2,1)S(1)} %pad_maximum_fusion.1.a_near), channel_id=1, source_target_pairs={{0,1},{1,0},{2,3},{3,2},{4,5},{5,4},{6,7},{7,6},{8,9},{9,8},{10,11... | collective-permute-start | bytes 835592 | tf_op jit(solution)/shard_map/ppermute | solution.py:393
  75.4 6.6 %collective-permute-start.29 = (bf16[1088,128]{1,0:T(8,128)(2,1)S(1)}, bf16[1088,128]{1,0:T(8,128)(2,1)S(1)}, u32[]{:S(2)}, u32[]{:S(2)}) collective-permute-start(bf16[1088,128]{1,0:T(8,128)(2,1)S(1)} %constant_dynamic-update-slice_fusion.b_near), channel_id=1, source_target_pairs={{0,2},{1,3},{2,0},{3,1},{4,6},{5,7},{6,4},{7,5},{8,10},{9,11},{10,... | collective-permute-start | bytes 835592 | tf_op jit(solution)/shard_map/ppermute | solution.py:393
  75.5 11.5 %collective-permute-start.24 = (bf16[1088,128]{1,0:T(8,128)(2,1)S(1)}, bf16[1088,128]{1,0:T(8,128)(2,1)S(1)}, u32[]{:S(2)}, u32[]{:S(2)}) collective-permute-start(bf16[1088,128]{1,0:T(8,128)(2,1)S(1)} %pad_maximum_fusion.1.a_near), channel_id=1, source_target_pairs={{0,8},{1,9},{2,10},{3,11},{4,12},{5,13},{6,14},{7,15},{8,0},{9,1},... | collective-permute-start | bytes 835592 | tf_op jit(solution)/shard_map/ppermute | solution.py:393
  75.5 11.4 %collective-permute-start.26 = (bf16[1088,128]{1,0:T(8,128)(2,1)S(1)}, bf16[1088,128]{1,0:T(8,128)(2,1)S(1)}, u32[]{:S(2)}, u32[]{:S(2)}) collective-permute-start(bf16[1088,128]{1,0:T(8,128)(2,1)S(1)} %constant_dynamic-update-slice_fusion.b_near), channel_id=1, source_target_pairs={{0,8},{1,9},{2,10},{3,11},{4,12},{5,13},{6,14},{7,15},{8,0},{9,1},... | collective-permute-start | bytes 835592 | tf_op jit(solution)/shard_map/ppermute | solution.py:393
  77.7 9.3 %collective-permute-start.28 = (bf16[1088,128]{1,0:T(8,128)(2,1)S(1)}, bf16[1088,128]{1,0:T(8,128)(2,1)S(1)}, u32[]{:S(2)}, u32[]{:S(2)}) collective-permute-start(bf16[1088,128]{1,0:T(8,128)(2,1)S(1)} %collective-permute-done.27.a_far), channel_id=1, source_target_pairs={{0,8},{1,9},{2,10},{3,11},{4,12},{5,13},{6,14},{7,15},{8,0},{9,1},... | collective-permute-start | bytes 835592 | tf_op jit(solution)/shard_map/ppermute | solution.py:393
  82.0 5.0 %collective-permute-start.30 = (bf16[1088,128]{1,0:T(8,128)(2,1)S(1)}, bf16[1088,128]{1,0:T(8,128)(2,1)S(1)}, u32[]{:S(2)}, u32[]{:S(2)}) collective-permute-start(bf16[1088,128]{1,0:T(8,128)(2,1)S(1)} %collective-permute-done.29.b_far), channel_id=1, source_target_pairs={{0,8},{1,9},{2,10},{3,11},{4,12},{5,13},{6,14},{7,15},{8,0},{9,1},... | collective-permute-start | bytes 835592 | tf_op jit(solution)/shard_map/ppermute | solution.py:393

commit v7 on v6

v7 whole, which is shorter than its diff:
```python
import functools
import math

import jax
import jax.numpy as jnp
from jax import lax
from jax.experimental import pallas as pl
from jax.experimental.pallas import tpu as pltpu
from jax.sharding import PartitionSpec as P

HEADS = 8
LANES = 128
HALO = 16
NT = (((1,), (1,)), ((), ()))
TN = (((0,), (0,)), ((), ()))
BF = jnp.bfloat16
F32 = jnp.float32
MIB = 1024 * 1024
CHAINS = 2
CORE, Y, X, Z, ZZ, BLOCK_AT = range(6)


def mm(left, right, dims=(((1,), (0,)), ((), ()))):
    return lax.dot_general(left, right, dims, preferred_element_type=F32)


def rolled(x, shift):
    return x if shift == 0 else pltpu.roll(x, x.shape[0] - shift, axis=0)


def window(x, taps, rows):
    acc = None
    for r in range(8):
        xr = rolled(x, r)
        for k in range(4):
            o = 8 * k + r
            if o == 0:
                continue
            term = xr[8 * k : 8 * k + rows] * taps(o)
            acc = term if acc is None else acc + term
    return acc


def ways(bits, half):
    return (bits[X], bits[Y], bits[Z]) if half == 0 else (bits[Z], bits[ZZ], 0)


def sigmoid(v):
    return 0.5 * jnp.tanh(0.5 * v) + 0.5


def scatter_kernel(sub, bits, source, *refs):
    outs, sems = refs[:4], refs[4]
    copies = []
    for d in range(4):
        rows = pl.ds(pl.multiple_of(bits[BLOCK_AT + d] * sub, sub), sub)
        copies.append(pltpu.make_async_copy(source.at[:, rows], outs[d], sems.at[d]))
    for copy in copies:
        copy.start()
    for copy in copies:
        copy.wait()


def padded(bits, rows, x_got, z_got, m, lanes):
    is_odd = jnp.broadcast_to(bits[X], (HALO, LANES)) == 1
    one, two = x_got[m, :, lanes].astype(F32), z_got[m, :, lanes].astype(F32)
    return jnp.concatenate(
        [
            jnp.where(is_odd, one, two),
            rows[m, :, lanes].astype(F32),
            jnp.where(is_odd, two, one),
        ],
        axis=0,
    )


def lanes_of(width):
    return [slice(at, at + LANES) for at in range(0, width, LANES)]


def conv_kernel(sub, bits, frames, x_got, z_got, kern, conv_out, *refs):
    outs, act_s = refs[:4], refs[4]
    count, length, width = frames.shape
    half = length // 2

    def step(m, _):
        for lanes in lanes_of(width):
            x = padded(bits, frames, x_got, z_got, m, lanes)
            for at in (0, half):
                conv = window(
                    x[at : at + half + 2 * HALO], lambda o: kern[o - 1 : o, lanes], half
                )
                conv_out[m, at : at + half, lanes] = conv
                act_s[m, at : at + half, lanes] = (conv * sigmoid(conv)).astype(BF)
        return 0

    lax.fori_loop(0, count, step, 0)
    for d, out in enumerate(outs):
        out[...] = act_s[:, pl.ds(pl.multiple_of(bits[BLOCK_AT + d] * sub, sub), sub), :]


def main_kernel(
    plan, bits, a0, a1, a2, a3, c0, c1, c2, c3, weights,
    a_keep, b_keep, a_send, b_send, back_keep, back_send,
    left_s, right_s, q_s, k_s, v_s, u_s,
):
    groups, count, sub, width, factor = plan
    mics = groups * count
    cuts = sub // HALO
    block = mics * HALO
    rows = cuts * block
    cols = width // LANES

    wq, wk, wv, wo = (weights.at[i] for i in range(4))
    for d, (act, cot) in enumerate(((a0, c0), (a1, c1), (a2, c2), (a3, c3))):
        for m in range(count):
            for c in range(cuts):
                part = slice(c * HALO, (c + 1) * HALO)
                at = c * block + (d * count + m) * HALO
                left_s[0, at : at + HALO, :] = act[m, part, :]
                right_s[3, c, d, m] = cot[m, part, :]

    def flat(i):
        return right_s[i].reshape(rows, width)

    def put(i, c, lanes, x):
        right_s[i, c, :, :, :, lanes] = x.astype(BF).reshape(groups, count, HALO, LANES)

    acted = left_s[0]
    q_s[...] = mm(acted, wq[...]).astype(BF)
    k_s[...] = mm(acted, wk[...]).astype(BF)
    v_s[...] = mm(acted, wv[...]).astype(BF)
    u_s[...] = mm(flat(3), wo[...], NT).astype(BF)

    depth = width // HEADS
    per = LANES // depth
    lane = lax.broadcasted_iota(jnp.int32, (block, LANES), 1)
    row_i = lax.broadcasted_iota(jnp.int32, (block, per * block), 0)
    col_i = lax.broadcasted_iota(jnp.int32, (block, per * block), 1)
    same = (row_i % HALO) == (col_i % HALO)

    def by_head(x):
        return jnp.concatenate(
            [jnp.where(lane // depth == h, x, jnp.zeros_like(x)) for h in range(per)], axis=0
        )

    def sums(x):
        return [
            jnp.sum(x[:, h * block : (h + 1) * block], axis=1, keepdims=True) for h in range(per)
        ]

    def each(x, values, op):
        return jnp.concatenate(
            [op(x[:, h * block : (h + 1) * block], values[h]) for h in range(per)], axis=1
        )

    def pick(x):
        out = x[:block]
        for h in range(1, per):
            out = jnp.where(lane // depth == h, x[h * block : (h + 1) * block], out)
        return out

    for c in range(cuts):
        part = slice(c * block, (c + 1) * block)
        for p in range(cols):
            lanes = slice(p * LANES, (p + 1) * LANES)
            q, u = q_s[part, lanes], u_s[part, lanes]
            kc, vc = by_head(k_s[part, lanes]), by_head(v_s[part, lanes])
            e = jnp.where(same, jnp.exp(mm(q, kc, NT) * factor), 0.0)
            w = each(e, [1.0 / x for x in sums(e)], lambda x, s: x * s)
            up = mm(u, vc, NT)
            inner = each(up, sums(w * up), lambda x, s: x - s) * w * factor
            wb, ib = w.astype(BF), inner.astype(BF)
            left_s[1, part, lanes] = mm(wb, vc).astype(BF)
            put(0, c, lanes, mm(ib, kc))
            put(1, c, lanes, pick(mm(ib, q, TN)))
            put(2, c, lanes, pick(mm(wb, u, TN)))

    dacted = mm(flat(0), wq[...], NT) + mm(flat(1), wk[...], NT) + mm(flat(2), wv[...], NT)
    size = cols * width // 8 // CHAINS
    core = bits[CORE]
    for out, owner, h in (
        (a_send, 1 - core, 0), (b_send, 1 - core, 1), (a_keep, core, 0), (b_keep, core, 1)
    ):
        i = owner * 2 + h
        first, second, third = ways(bits, h)
        grad = mm(left_s[i // 3], flat(i), TN).astype(BF)
        for piece in range(8):
            rel = ((piece // 4) ^ first) * 4 + ((piece // 2 % 2) ^ second) * 2 + ((piece % 2) ^ third)
            for chain in range(CHAINS):
                at = (piece * CHAINS + chain) * size
                cb, at = at // width, at % width
                start = pl.multiple_of((chain * 8 + rel) * size, size)
                out[pl.ds(start, size), :] = grad[at : at + size, cb * LANES : (cb + 1) * LANES]

    unit = 2 * count * cols * sub
    for d, (out, base) in enumerate(
        ((back_keep, 0), (back_send, 0), (back_keep, unit), (back_send, unit))
    ):
        for m in range(count):
            for c in range(cuts):
                at = c * block + (d * count + m) * HALO
                for kind in range(2):
                    rows_of = left_s[1, at : at + HALO, :] if kind == 0 else dacted[
                        at : at + HALO
                    ].astype(BF)
                    for lc in range(cols):
                        to = base + ((kind * count + m) * cols + lc) * sub + c * HALO
                        out[to : to + HALO, :] = rows_of[:, lc * LANES : (lc + 1) * LANES]


def total(*parts):
    return functools.reduce(lambda x, y: x + y, [x.astype(F32) for x in parts]).astype(BF)


def final_kernel(plan, first_call, bits, *refs):
    width, norm = plan
    cols = width // LANES
    size = cols * width // 8 // CHAINS
    got, refs = refs[: 2 * CHAINS], refs[2 * CHAINS :]
    if first_call:
        taps, outs, tap_grad, grad_s, sems = refs[0], refs[1:5], refs[5], refs[6], refs[7]
        for lc in range(cols):
            tap_grad[:, lc * LANES : (lc + 1) * LANES] = (
                taps[lc * 32 : lc * 32 + 31, :].astype(F32) * norm
            )
    else:
        outs, grad_s, sems = refs[4:8], refs[8], refs[9]
    core = bits[CORE]
    owner = core if first_call else 1 - core
    for h in range(2):
        first, second, third = ways(bits, h)
        for rel in range(8):
            piece = (first ^ (rel // 4)) * 4 + (second ^ (rel // 2 % 2)) * 2 + (third ^ (rel % 2))
            for chain in range(CHAINS):
                at = (piece * CHAINS + chain) * size
                cb, at = at // width, at % width
                grad_s[
                    h,
                    pl.ds(pl.multiple_of(at, size), size),
                    pl.ds(pl.multiple_of(cb * LANES, LANES), LANES),
                ] = got[h * CHAINS + chain][rel * size : (rel + 1) * size, :].astype(F32) * norm
        for which in range(2):
            @pl.when(owner == which)
            def _():
                pltpu.make_async_copy(grad_s.at[h], outs[2 * which + h], sems.at[h]).start()
    for h in range(2):
        for which in range(2):
            @pl.when(owner == which)
            def _():
                pltpu.make_async_copy(grad_s.at[h], outs[2 * which + h], sems.at[h]).wait()


def home_chunks(plan, bits, own, core_got, y_got, kind):
    count, sub, cols = plan
    part = count * cols * sub
    for d, (ref, base) in enumerate(
        ((own, 0), (core_got, 0), (y_got, 0), (y_got, 2 * part))
    ):
        to = pl.ds(pl.multiple_of(bits[BLOCK_AT + d] * sub, sub), sub)
        for m in range(count):
            for lc in range(cols):
                at = base + kind * part + (m * cols + lc) * sub
                yield ref[at : at + sub, :], m, to, slice(lc * LANES, (lc + 1) * LANES)


def dconv_kernel(plan, bits, own, core_got, y_got, conv_in, dconv, x_edge, z_edge):
    for dacted, m, to, lanes in home_chunks(plan, bits, own, core_got, y_got, 1):
        conv = conv_in[m, to, lanes]
        sig = sigmoid(conv)
        dconv[m, to, lanes] = dacted.astype(F32) * sig * (1.0 + conv * (1.0 - sig))
    last = dconv.shape[1] - HALO
    odd = bits[X]
    x_edge[...] = dconv[:, pl.ds(pl.multiple_of((1 - odd) * last, HALO), HALO), :].astype(BF)
    z_edge[...] = dconv[:, pl.ds(pl.multiple_of(odd * last, HALO), HALO), :].astype(BF)


def layer_kernel(plan, bits, own, core_got, y_got, frames, weights, layer_out, mix_s):
    for mixed, m, to, lanes in home_chunks(plan, bits, own, core_got, y_got, 0):
        mix_s[m, to, lanes] = mixed
    for m in range(plan[0]):
        proj = mm(mix_s[m], weights[3])
        layer_out[m] = (frames[m].astype(F32) + proj).astype(BF)


def tap_kernel(sub, bits, frames, x_got, z_got, dconv, taps, pad_s):
    count, length, width = frames.shape
    for m in range(count):
        for lanes in lanes_of(width):
            pad_s[m, :, lanes] = padded(bits, frames, x_got, z_got, m, lanes)
    for lc, lanes in enumerate(lanes_of(width)):

        def step(n, accs):
            m = n // (length // sub)
            at = pl.multiple_of(n % (length // sub) * sub, sub)
            x = pad_s[m, pl.ds(at, sub + 2 * HALO), lanes]
            d = dconv[m, pl.ds(at, sub), lanes]
            out = list(accs)
            for r in range(8):
                xr = rolled(x, r)
                for k in range(4):
                    o = 8 * k + r
                    if o == 0:
                        continue
                    prod = xr[8 * k : 8 * k + sub] * d
                    out[o - 1] = out[o - 1] + jnp.sum(prod.reshape(sub // 8, 8, LANES), axis=0)
            return tuple(out)

        zeros = tuple(jnp.zeros((8, LANES), F32) for _ in range(31))
        accs = lax.fori_loop(0, count * (length // sub), step, zeros)
        taps[lc * 32 : lc * 32 + 32, :] = jnp.concatenate(
            [jnp.sum(x, axis=0, keepdims=True) for x in accs] + [jnp.zeros((1, LANES), F32)], axis=0
        ).astype(BF)


def frame_kernel(bits, dconv, x_got, z_got, cot, kern, frame_grad):
    count, length, width = dconv.shape
    half = length // 2

    def step(m, _):
        for lanes in lanes_of(width):
            x = padded(bits, dconv, x_got, z_got, m, lanes)
            for at in (0, half):
                part = slice(at, at + half)
                grad = window(
                    x[at : at + half + 2 * HALO], lambda o: kern[31 - o : 32 - o, lanes], half
                )
                frame_grad[m, part, lanes] = (cot[m, part, lanes].astype(F32) + grad).astype(BF)
        return 0

    lax.fori_loop(0, count, step, 0)


def call(body, outs, scratch, limit, *args, hbm=(), hbm_outs=(), aliases=None):
    spaces = [pltpu.HBM if i in hbm else pltpu.VMEM for i in range(len(args))]
    return pl.pallas_call(
        body,
        out_shape=outs,
        in_specs=[
            pl.BlockSpec(memory_space=pltpu.SMEM if x.dtype == jnp.int32 else space)
            for x, space in zip(args, spaces)
        ],
        out_specs=tuple(
            pl.BlockSpec(memory_space=pltpu.HBM if i in hbm_outs else pltpu.VMEM)
            for i in range(len(outs))
        ),
        scratch_shapes=scratch,
        input_output_aliases=aliases or {},
        compiler_params=pltpu.CompilerParams(vmem_limit_bytes=limit * MIB),
    )(*args)


def shards(frames, cotangent, kernel, w_query, w_key, w_value, w_out):
    groups, blocks = lax.axis_size("mic"), lax.axis_size("tm")
    count, length, width = frames.shape
    sub = length // groups
    cuts = sub // HALO
    cols = width // LANES
    rows = groups * count * sub
    shape = jax.ShapeDtypeStruct

    mic, tm = lax.axis_index("mic"), lax.axis_index("tm")
    over_core, over_y, over_x = blocks, 2 * blocks, 1
    lines = [2**i for i in range(1, blocks.bit_length() - 1)]
    odd = tm % 2
    bits = jnp.stack(
        [mic % 2, mic // 2, odd, tm // 2 % 2, tm // 4 % 2] + [mic ^ d for d in range(4)]
    ).astype(jnp.int32)

    def permute(x, pairs):
        return lax.ppermute(x, ("mic", "tm"), pairs)

    def swap(x, mask):
        return permute(x, [(f, f ^ mask) for f in range(groups * blocks)])

    def swap_edges(x_edge, z_edge):
        pairs = [(m * blocks + t, m * blocks + t + 1)
                 for m in range(groups) for t in range(1, blocks - 1, 2)]
        return swap(x_edge, over_x), permute(z_edge, pairs + [(j, i) for i, j in pairs])

    def spread(parts):
        masks = (0, over_core, over_y, over_core + over_y)
        got = {d: swap(parts[d], masks[d]) for d in (2, 3, 1)}
        return [parts[0], got[1], got[2], got[3]]

    last = length - HALO
    frame_x, frame_z = swap_edges(
        lax.dynamic_slice_in_dim(frames, (1 - odd) * last, HALO, axis=1),
        lax.dynamic_slice_in_dim(frames, odd * last, HALO, axis=1),
    )
    block = shape((count, sub, width), BF)
    cot_parts = spread(
        call(
            functools.partial(scatter_kernel, sub), (block,) * 4,
            [pltpu.SemaphoreType.DMA((4,))], 8, bits, cotangent, hbm=(1,),
        )
    )
    weights = jnp.stack([w_query, w_key, w_value, w_out])
    wide = shape(frames.shape, F32)
    here = pltpu.VMEM(frames.shape, BF)
    conv, *acted = call(
        functools.partial(conv_kernel, sub), (wide,) + (block,) * 4, [here],
        8, bits, frames, frame_x, frame_z, kernel,
    )
    *acted, weights = lax.optimization_barrier((*acted, weights))

    factor = 1.0 / math.sqrt(width // HEADS)
    part = width * width // LANES // CHAINS
    unit = 2 * count * cols * sub
    big = pltpu.VMEM((rows, width), BF)

    def flat(n):
        return shape((n, LANES), BF)

    a_keep, b_keep, a_send, b_send, back_keep, back_send = call(
        functools.partial(main_kernel, (groups, count, sub, width, factor)),
        (flat(CHAINS * part),) * 4 + (flat(2 * unit),) * 2,
        [
            pltpu.VMEM((2, rows, width), BF),
            pltpu.VMEM((4, cuts, groups, count, HALO, width), BF),
            big, big, big, big,
        ],
        24, bits, *spread(acted), *cot_parts, weights,
    )

    def halved(parts, mask):
        n = parts[0].shape[0] // 2
        return [t[:n] for t in parts] + [swap(total(*(t[n:] for t in parts)), mask)]

    def exchanged(x, masks):
        for mask in masks:
            x = total(x, swap(x, mask))
        return x

    def doubled(x, mask):
        return jnp.concatenate([x, swap(x, mask)])

    def chains(*arrays):
        return [[t[i * part : (i + 1) * part] for t in arrays] for i in range(CHAINS)]

    def after(x, y):
        return lax.optimization_barrier((x, y))[0]

    a = chains(a_keep, swap(a_send, over_core))
    b = chains(b_keep, swap(b_send, over_core))
    core_got = swap(back_send, over_core)
    y_got = swap(jnp.concatenate([back_keep[unit:], core_got[unit:]]), over_y)
    a = [halved(t, over_x) for t in a]
    b = [halved(t, lines[0]) for t in b]
    plan = (count, sub, cols)
    y_got = after(y_got, (a[0][-1], b[0][-1]))
    home = (bits, back_keep, core_got, y_got)
    edge = shape((count, HALO, width), BF)
    dconv, x_edge, z_edge = call(
        functools.partial(dconv_kernel, plan), (wide, edge, edge), [], 8, *home, conv
    )
    x_edge, z_edge = swap_edges(x_edge, z_edge)
    a = [halved(t, over_y) for t in a]
    b = [halved(t, lines[1]) for t in b]
    (taps,) = call(
        functools.partial(tap_kernel, sub), (flat(32 * cols),),
        [pltpu.VMEM((count, length + 2 * HALO, width), F32)],
        8, bits, frames, frame_x, frame_z, after(dconv, a[0][-1]),
    )
    taps = exchanged(taps, lines + [over_x, over_y, over_core])
    a = [exchanged(total(*halved(t, lines[0])), lines[1:]) for t in a]
    b = [exchanged(total(*t), [over_x, over_y] + lines[2:]) for t in b]
    (frame_grad,) = call(
        frame_kernel, (shape(frames.shape, BF),), [], 8,
        bits, after(dconv, a[0]), x_edge, z_edge, cotangent, kernel,
    )
    a = [doubled(t, lines[0]) for t in a]
    b = [doubled(t, lines[1]) for t in b]
    (layer_out,) = call(
        functools.partial(layer_kernel, plan), (shape(frames.shape, BF),), [here],
        10, *home, after(frames, a[0]), weights,
    )
    a = [doubled(t, over_y) for t in a]
    a = [doubled(t, over_x) for t in a]
    b = [doubled(t, lines[0]) for t in b]
    *a, b[-1], frame_grad, layer_out = lax.optimization_barrier(
        (*a, b[-1], frame_grad, layer_out)
    )
    other = [swap(t, over_core) for t in a + b]

    norm = 1.0 / math.sqrt(groups * count * blocks * length)
    square = shape((width, width), F32)
    scratch = [pltpu.VMEM((2, width, width), F32), pltpu.SemaphoreType.DMA((2,))]
    final = functools.partial(final_kernel, (width, norm))
    *grads, kernel_grad = call(
        functools.partial(final, True), (square,) * 4 + (shape((31, width), F32),), scratch,
        8, bits, *a, *b, taps, hbm_outs=range(4),
    )
    first = 1 + 2 * CHAINS
    grads = call(
        functools.partial(final, False), (square,) * 4, scratch,
        8, bits, *other, *grads, hbm=range(first, first + 4), hbm_outs=range(4),
        aliases={first + i: i for i in range(4)},
    )
    return (layer_out, frame_grad, kernel_grad, *grads)


def solution(mesh):
    in_specs = (P("mic", "tm", None), P("mic", "tm", None), P(), P(), P(), P(), P())
    out_specs = (P("mic", "tm", None), P("mic", "tm", None), P(), P(), P(), P(), P())
    return jax.shard_map(shards, mesh=mesh, in_specs=in_specs, out_specs=out_specs, check_vma=False)
```

time: 89.9 us -> 105 us (1.17)
  starting transfers between devices: 35.1 us -> 50.8 us
  waiting for transfers between devices: 28.1 us -> 26.3 us
    ppermute x31 -> x49, starting transfers between devices: 35.1 us -> 50.8 us  [permute(): return lax.ppermute(x, ('mic', 'tm'), pairs)]
    ppermute x31 -> x49, waiting for transfers between devices: 28.1 us -> 26.3 us  [permute(): return lax.ppermute(x, ('mic', 'tm'), pairs)]
  transfers between devices with their start and end apart: 31 -> 49, of which waited for: 16 -> 16; matrix products, arithmetic and copies ran while one was open for 3% -> 3% of each run, Pallas kernels for 11% -> 13%
where the time goes in v7:
time: 105 us; the launch traced here: 104 us
  starting transfers between devices  50.8 us (48%)
  waiting for transfers between devices  26.3 us (25%)
  Pallas kernels  21.7 us (21%)
  other arithmetic  2.56 us (2%)
  local copies, waits for them, and re-layouts  1.86 us (2%)
  between operations  1.21 us (1%)
    ppermute x49, starting transfers between devices, permute(): return lax.ppermute(x, ('mic', 'tm'), pairs)  50.8 us
    ppermute x49, waiting for transfers between devices, permute(): return lax.ppermute(x, ('mic', 'tm'), pairs)  26.3 us
    pallas_call x9, Pallas kernels, call(): pl.pallas_call(body, out_shape=outs, in_specs=[pl.BlockSpec(memory_space=...  21.7 us
  transfers between devices with their start and end apart: 49, of which 16 were waited for; matrix products, arithmetic and copies ran while one was open for 3% of the time, Pallas kernels for 13%

profile of v7, /device:TPU:0, one launch (start us, length us, event | category | flops | bytes accessed | tf_op | source)
XLA Modules:
  0.0 104.4 jit_solution(10668190541059980472)
XLA Ops:
  0.7 0.8 constant_dynamic-slice_fusion
  2.1 5.8 %collective-permute-start = (bf16[2,16,512]{2,1,0:T(8,128)(2,1)S(1)}, bf16[2,16,512]{2,1,0:T(8,128)(2,1)S(1)}, u32[]{:S(2)}, u32[]{:S(2)}) collective-permute-start(bf16[2,16,512]{2,1,0:T(8,128)(2,1)S(1)} %get-tuple-element.100), channel_id=1, source_target_pairs={{0,1},{1,0},{2,3},{3,2},{4,5},{5,4},{6,7},{7,6},{8,9},{9,8},{10,11... | collective-permute-start | bytes 98312 | tf_op jit(solution)/shard_map/ppermute | solution.py:371
  8.0 1.0 copy-done.1
  9.8 1.6 %collective-permute-start.6 = (bf16[2,32,512]{2,1,0:T(8,128)(2,1)S(1)}, bf16[2,32,512]{2,1,0:T(8,128)(2,1)S(1)}, u32[]{:S(2)}, u32[]{:S(2)}) collective-permute-start(bf16[2,32,512]{2,1,0:T(8,128)(2,1)S(1)} %get-tuple-element.58), channel_id=1, source_target_pairs={{0,16},{1,17},{2,18},{3,19},{4,20},{5,21},{6,22},{7,23},{8,24},{9,... | collective-permute-start | bytes 196616 | tf_op jit(solution)/shard_map/ppermute | solution.py:371
  11.7 1.8 %pad_maximum_fusion.weights = bf16[4,512,512]{2,1,0:T(8,128)(2,1)S(1)} fusion(bf16[1,512,512]{2,1,0:T(8,128)(2,1)} %bitcast.13, bf16[1,512,512]{2,1,0:T(8,128)(2,1)} %bitcast.14, bf16[1,512,512]{2,1,0:T(8,128)(2,1)} %bitcast.15, bf16[1,512,512]{2,1,0:T(8,128)(2,1)} %bitcast.16), kind=kLoop, calls=%fused_computation | loop fusion | flops 3145728 | bytes 4194304 | tf_op jit(solution)/shard_map/stack | solution.py:398
  13.5 2.2 %shard_map.126 = (f32[2,128,512]{2,1,0:T(8,128)S(1)}, bf16[2,32,512]{2,1,0:T(8,128)(2,1)S(1)}, bf16[2,32,512]{2,1,0:T(8,128)(2,1)S(1)}, bf16[2,32,512]{2,1,0:T(8,128)(2,1)S(1)}, bf16[2,32,512]{2,1,0:T(8,128)(2,1)S(1)}) custom-call(s32[9]{0:T(128)S(1)} %stack.54.bits, bf16[2,128,512]{2,1,0:T(8,128)(2,1)S(1)} %copy-done, ...), custom_call_target="tpu_custom_call" | custom-call | tf_op jit(solution)/shard_map/pallas_call | solution.py:336
  16.2 1.6 %collective-permute-start.3 = (bf16[2,32,512]{2,1,0:T(8,128)(2,1)S(1)}, bf16[2,32,512]{2,1,0:T(8,128)(2,1)S(1)}, u32[]{:S(2)}, u32[]{:S(2)}) collective-permute-start(bf16[2,32,512]{2,1,0:T(8,128)(2,1)S(1)} %get-tuple-element.54), channel_id=1, source_target_pairs={{0,16},{1,17},{2,18},{3,19},{4,20},{5,21},{6,22},{7,23},{8,24},{9,... | collective-permute-start | bytes 196616 | tf_op jit(solution)/shard_map/ppermute | solution.py:371
  17.8 2.7 %collective-permute-done.3.a2 = bf16[2,32,512]{2,1,0:T(8,128)(2,1)S(1)} collective-permute-done((bf16[2,32,512]{2,1,0:T(8,128)(2,1)S(1)}, bf16[2,32,512]{2,1,0:T(8,128)(2,1)S(1)}, u32[]{:S(2)}, u32[]{:S(2)}) %collective-permute-start.3) | collective-permute-done | bytes 65568 | tf_op jit(solution)/shard_map/ppermute | solution.py:371
  20.5 1.7 %collective-permute-done.4.a3 = bf16[2,32,512]{2,1,0:T(8,128)(2,1)S(1)} collective-permute-done((bf16[2,32,512]{2,1,0:T(8,128)(2,1)S(1)}, bf16[2,32,512]{2,1,0:T(8,128)(2,1)S(1)}, u32[]{:S(2)}, u32[]{:S(2)}) %collective-permute-start.4) | collective-permute-done | bytes 65568 | tf_op jit(solution)/shard_map/ppermute | solution.py:371
  22.1 5.8 %shard_map.128 = (bf16[2048,128]{1,0:T(8,128)(2,1)S(1)}, bf16[2048,128]{1,0:T(8,128)(2,1)S(1)}, bf16[2048,128]{1,0:T(8,128)(2,1)S(1)}, bf16[2048,128]{1,0:T(8,12...) custom-call(s32[9]{0:T(128)S(1)} %stack.54.bits, ...), custom_call_target="tpu_custom_call" | custom-call | tf_op jit(solution)/shard_map/pallas_call | solution.py:336
  28.6 1.6 %collective-permute-done.30.core_got = bf16[1024,128]{1,0:T(8,128)(2,1)S(1)} collective-permute-done((bf16[1024,128]{1,0:T(8,128)(2,1)S(1)}, bf16[1024,128]{1,0:T(8,128)(2,1)S(1)}, u32[]{:S(2)}, u32[]{:S(2)}) %collective-permute-start.30) | collective-permute-done | bytes 262176 | tf_op jit(solution)/shard_map/ppermute | solution.py:371
  31.3 1.9 %collective-permute-start.9 = (bf16[512,128]{1,0:T(8,128)(2,1)S(1)}, bf16[512,128]{1,0:T(8,128)(2,1)S(1)}, u32[]{:S(2)}, u32[]{:S(2)}) collective-permute-start(bf16[512,128]{1,0:T(8,128)(2,1)S(1)} %get-tuple-element.98), channel_id=1, source_target_pairs={{0,1},{1,0},{2,3},{3,2},{4,5},{5,4},{6,7},{7,6},{8,9},{9,8},{10,11... | collective-permute-start | bytes 393224 | tf_op jit(solution)/shard_map/ppermute | solution.py:371
  33.3 1.6 %collective-permute-start.32 = (bf16[512,128]{1,0:T(8,128)(2,1)S(1)}, bf16[512,128]{1,0:T(8,128)(2,1)S(1)}, u32[]{:S(2)}, u32[]{:S(2)}) collective-permute-start(bf16[512,128]{1,0:T(8,128)(2,1)S(1)} %get-tuple-element.91), channel_id=1, source_target_pairs={{0,2},{1,3},{2,0},{3,1},{4,6},{5,7},{6,4},{7,5},{8,10},{9,11},{10,... | collective-permute-start | bytes 393224 | tf_op jit(solution)/shard_map/ppermute | solution.py:371
  35.4 2.2 %collective-permute-done.16 = bf16[512,128]{1,0:T(8,128)(2,1)S(1)} collective-permute-done((bf16[512,128]{1,0:T(8,128)(2,1)S(1)}, bf16[512,128]{1,0:T(8,128)(2,1)S(1)}, u32[]{:S(2)}, u32[]{:S(2)}) %collective-permute-start.16) | collective-permute-done | bytes 131104 | tf_op jit(solution)/shard_map/ppermute | solution.py:371
  37.5 1.9 %collective-permute-done.9 = bf16[512,128]{1,0:T(8,128)(2,1)S(1)} collective-permute-done((bf16[512,128]{1,0:T(8,128)(2,1)S(1)}, bf16[512,128]{1,0:T(8,128)(2,1)S(1)}, u32[]{:S(2)}, u32[]{:S(2)}) %collective-permute-start.9) | collective-permute-done | bytes 131104 | tf_op jit(solution)/shard_map/ppermute | solution.py:371
  39.5 1.2 %collective-permute-start.17 = (bf16[256,128]{1,0:T(8,128)(2,1)S(1)}, bf16[256,128]{1,0:T(8,128)(2,1)S(1)}, u32[]{:S(2)}, u32[]{:S(2)}) collective-permute-start(bf16[256,128]{1,0:T(8,128)(2,1)S(1)} %get-tuple-element.95), channel_id=1, source_target_pairs={{0,16},{1,17},{2,18},{3,19},{4,20},{5,21},{6,22},{7,23},{8,24},{9,... | collective-permute-start | bytes 196616 | tf_op jit(solution)/shard_map/ppermute | solution.py:371
  40.7 0.9 collective-permute-start.10
  42.7 0.8 collective-permute-start.34
  43.8 5.3 %collective-permute-start.35 = (bf16[256,128]{1,0:T(8,128)(2,1)S(1)}, bf16[256,128]{1,0:T(8,128)(2,1)S(1)}, u32[]{:S(2)}, u32[]{:S(2)}) collective-permute-start(bf16[256,128]{1,0:T(8,128)(2,1)S(1)} %add_convert_fusion.7), channel_id=1, source_target_pairs={{0,4},{1,5},{2,6},{3,7},{4,0},{5,1},{6,2},{7,3},{8,12},{9,13},{10,... | collective-permute-start | bytes 196616 | tf_op jit(solution)/shard_map/ppermute | solution.py:371
  49.2 1.6 %collective-permute-start.18 = (bf16[128,128]{1,0:T(8,128)(2,1)S(1)}, bf16[128,128]{1,0:T(8,128)(2,1)S(1)}, u32[]{:S(2)}, u32[]{:S(2)}) collective-permute-start(bf16[128,128]{1,0:T(8,128)(2,1)S(1)} %add_convert_fusion.21), channel_id=1, source_target_pairs={{0,2},{1,3},{2,0},{3,1},{4,6},{5,7},{6,4},{7,5},{8,10},{9,11},{10,... | collective-permute-start | bytes 98312 | tf_op jit(solution)/shard_map/ppermute | solution.py:371
  50.8 2.8 %shard_map.132 = bf16[128,128]{1,0:T(8,128)(2,1)S(1)} custom-call(s32[9]{0:T(128)S(1)} %stack.54.bits, bf16[2,128,512]{2,1,0:T(8,128)(2,1)S(1)} %copy-done, bf16[2,16,512]{2,1,0:T(8,128)(2,1)S(1)} %collective-permute-done.x_got, bf16[2,16,512]{2,1,0:T(8,128)(2,1)S(1)} %collective-permute-done.1.z_got, f32[2,128,512]{2,1,0:T(8,128)S(1)} %get-tuple-element.79.dconv), custom_call_target="tpu_custom_call" | custom-call | tf_op jit(solution)/shard_map/pallas_call | solution.py:336
  54.5 1.7 %collective-permute-start.36 = (bf16[256,128]{1,0:T(8,128)(2,1)S(1)}, bf16[256,128]{1,0:T(8,128)(2,1)S(1)}, u32[]{:S(2)}, u32[]{:S(2)}) collective-permute-start(bf16[256,128]{1,0:T(8,128)(2,1)S(1)} %get-tuple-element.89), channel_id=1, source_target_pairs={{0,1},{1,0},{2,3},{3,2},{4,5},{5,4},{6,7},{7,6},{8,9},{9,8},{10,11... | collective-permute-start | bytes 196616 | tf_op jit(solution)/shard_map/ppermute | solution.py:371
  56.2 1.4 %collective-permute-done.40 = bf16[128,128]{1,0:T(8,128)(2,1)S(1)} collective-permute-done((bf16[128,128]{1,0:T(8,128)(2,1)S(1)}, bf16[128,128]{1,0:T(8,128)(2,1)S(1)}, u32[]{:S(2)}, u32[]{:S(2)}) %collective-permute-start.40) | collective-permute-done | bytes 32800 | tf_op jit(solution)/shard_map/ppermute | solution.py:371
  58.4 1.4 %collective-permute-done.25 = bf16[256,128]{1,0:T(8,128)(2,1)S(1)} collective-permute-done((bf16[256,128]{1,0:T(8,128)(2,1)S(1)}, bf16[256,128]{1,0:T(8,128)(2,1)S(1)}, u32[]{:S(2)}, u32[]{:S(2)}) %collective-permute-start.25) | collective-permute-done | bytes 65568 | tf_op jit(solution)/shard_map/ppermute | solution.py:371
  60.0 1.5 %collective-permute-done.11 = bf16[128,128]{1,0:T(8,128)(2,1)S(1)} collective-permute-done((bf16[128,128]{1,0:T(8,128)(2,1)S(1)}, bf16[128,128]{1,0:T(8,128)(2,1)S(1)}, u32[]{:S(2)}, u32[]{:S(2)}) %collective-permute-start.11) | collective-permute-done | bytes 32800 | tf_op jit(solution)/shard_map/ppermute | solution.py:371
  61.6 1.3 %collective-permute-start.41 = (bf16[128,128]{1,0:T(8,128)(2,1)S(1)}, bf16[128,128]{1,0:T(8,128)(2,1)S(1)}, u32[]{:S(2)}, u32[]{:S(2)}) collective-permute-start(bf16[128,128]{1,0:T(8,128)(2,1)S(1)} %add_convert_fusion.18), channel_id=1, source_target_pairs={{0,4},{1,5},{2,6},{3,7},{4,0},{5,1},{6,2},{7,3},{8,12},{9,13},{10,... | collective-permute-start | bytes 98312 | tf_op jit(solution)/shard_map/ppermute | solution.py:371
  62.9 2.1 %collective-permute-done.19 = bf16[128,128]{1,0:T(8,128)(2,1)S(1)} collective-permute-done((bf16[128,128]{1,0:T(8,128)(2,1)S(1)}, bf16[128,128]{1,0:T(8,128)(2,1)S(1)}, u32[]{:S(2)}, u32[]{:S(2)}) %collective-permute-start.19) | collective-permute-done | bytes 32800 | tf_op jit(solution)/shard_map/ppermute | solution.py:371
  65.0 1.4 %collective-permute-done.41 = bf16[128,128]{1,0:T(8,128)(2,1)S(1)} collective-permute-done((bf16[128,128]{1,0:T(8,128)(2,1)S(1)}, bf16[128,128]{1,0:T(8,128)(2,1)S(1)}, u32[]{:S(2)}, u32[]{:S(2)}) %collective-permute-start.41) | collective-permute-done | bytes 32800 | tf_op jit(solution)/shard_map/ppermute | solution.py:371
  66.4 1.4 %collective-permute-start.20 = (bf16[128,128]{1,0:T(8,128)(2,1)S(1)}, bf16[128,128]{1,0:T(8,128)(2,1)S(1)}, u32[]{:S(2)}, u32[]{:S(2)}) collective-permute-start(bf16[128,128]{1,0:T(8,128)(2,1)S(1)} %add_convert_fusion.19), channel_id=1, source_target_pairs={{0,2},{1,3},{2,0},{3,1},{4,6},{5,7},{6,4},{7,5},{8,10},{9,11},{10,... | collective-permute-start | bytes 98312 | tf_op jit(solution)/shard_map/ppermute | solution.py:371
  67.8 1.5 %collective-permute-start.42 = (bf16[128,128]{1,0:T(8,128)(2,1)S(1)}, bf16[128,128]{1,0:T(8,128)(2,1)S(1)}, u32[]{:S(2)}, u32[]{:S(2)}) collective-permute-start(bf16[128,128]{1,0:T(8,128)(2,1)S(1)} %add_convert_fusion.17), channel_id=1, source_target_pairs={{0,1},{1,0},{2,3},{3,2},{4,5},{5,4},{6,7},{7,6},{8,9},{9,8},{10,11... | collective-permute-start | bytes 98312 | tf_op jit(solution)/shard_map/ppermute | solution.py:371
  69.8 1.8 %collective-permute-start.26 = (bf16[256,128]{1,0:T(8,128)(2,1)S(1)}, bf16[256,128]{1,0:T(8,128)(2,1)S(1)}, u32[]{:S(2)}, u32[]{:S(2)}) collective-permute-start(bf16[256,128]{1,0:T(8,128)(2,1)S(1)} %add_convert_fusion.10), channel_id=1, source_target_pairs={{0,1},{1,0},{2,3},{3,2},{4,5},{5,4},{6,7},{7,6},{8,9},{9,8},{10,11... | collective-permute-start | bytes 196616 | tf_op jit(solution)/shard_map/ppermute | solution.py:371
  71.8 1.2 %collective-permute-start.37 = (bf16[256,128]{1,0:T(8,128)(2,1)S(1)}, bf16[256,128]{1,0:T(8,128)(2,1)S(1)}, u32[]{:S(2)}, u32[]{:S(2)}) collective-permute-start(bf16[256,128]{1,0:T(8,128)(2,1)S(1)} %add_convert_fusion.5), channel_id=1, source_target_pairs={{0,16},{1,17},{2,18},{3,19},{4,20},{5,21},{6,22},{7,23},{8,24},{9,... | collective-permute-start | bytes 196616 | tf_op jit(solution)/shard_map/ppermute | solution.py:371
  73.8 0.8 collective-permute-start.21
  74.6 1.3 %collective-permute-start.43 = (bf16[128,128]{1,0:T(8,128)(2,1)S(1)}, bf16[128,128]{1,0:T(8,128)(2,1)S(1)}, u32[]{:S(2)}, u32[]{:S(2)}) collective-permute-start(bf16[128,128]{1,0:T(8,128)(2,1)S(1)} %add_convert_fusion.16), channel_id=1, source_target_pairs={{0,16},{1,17},{2,18},{3,19},{4,20},{5,21},{6,22},{7,23},{8,24},{9,... | collective-permute-start | bytes 98312 | tf_op jit(solution)/shard_map/ppermute | solution.py:371
  75.9 2.8 %shard_map.130 = bf16[2,128,512]{2,1,0:T(8,128)(2,1)} custom-call(s32[9]{0:T(128)S(1)} %stack.54.bits, f32[2,128,512]{2,1,0:T(8,128)S(1)} %get-tuple-element.79.dconv, bf16[2,16,512]{2,1,0:T(8,128)(2,1)S(1)} %collective-permute-done.33.x_got, bf16[2,16,512]{2,1,0:T(8,128)(2,1)S(1)} %collective-permute-done.34.z_got, bf16[2,128,512]{2,1,0:T(8,128)(2,1)S(1)} %copy-done.2, ...), custom_call_target="tpu_custom_call" | custom-call | tf_op jit(solution)/shard_map/pallas_call | solution.py:336
  78.8 0.8 collective-permute-start.14
  79.6 1.3 %collective-permute-start.27 = (bf16[256,128]{1,0:T(8,128)(2,1)S(1)}, bf16[256,128]{1,0:T(8,128)(2,1)S(1)}, u32[]{:S(2)}, u32[]{:S(2)}) collective-permute-start(bf16[256,128]{1,0:T(8,128)(2,1)S(1)} %add_convert_fusion.9), channel_id=1, source_target_pairs={{0,16},{1,17},{2,18},{3,19},{4,20},{5,21},{6,22},{7,23},{8,24},{9,... | collective-permute-start | bytes 196616 | tf_op jit(solution)/shard_map/ppermute | solution.py:371
  81.0 1.8 %collective-permute-start.38 = (bf16[256,128]{1,0:T(8,128)(2,1)S(1)}, bf16[256,128]{1,0:T(8,128)(2,1)S(1)}, u32[]{:S(2)}, u32[]{:S(2)}) collective-permute-start(bf16[256,128]{1,0:T(8,128)(2,1)S(1)} %add_convert_fusion.4), channel_id=1, source_target_pairs={{0,4},{1,5},{2,6},{3,7},{4,0},{5,1},{6,2},{7,3},{8,12},{9,13},{10,... | collective-permute-start | bytes 196616 | tf_op jit(solution)/shard_map/ppermute | solution.py:371
  82.7 1.6 %shard_map.131 = bf16[2,128,512]{2,1,0:T(8,128)(2,1)} custom-call(s32[9]{0:T(128)S(1)} %stack.54.bits, bf16[1024,128]{1,0:T(8,128)(2,1)S(1)} %get-tuple-element.65.own, bf16[1024,128]{1,0:T(8,128)(2,1)S(1)} %collective-permute-done.30.core_got, bf16[1024,128]{1,0:T(8,128)(2,1)S(1)} %collective-permute-done.31.y_got, bf16[2,128,512]{2,1,0:T(8,128)(2,1)S(1)} %copy-done, ...), custom_call_target="tpu_custom_call" | custom-call | tf_op jit(solution)/shard_map/pallas_call | solution.py:336
  84.3 1.8 %collective-permute-start.22 = (bf16[512,128]{1,0:T(8,128)(2,1)S(1)}, bf16[512,128]{1,0:T(8,128)(2,1)S(1)}, u32[]{:S(2)}, u32[]{:S(2)}) collective-permute-start(bf16[512,128]{1,0:T(8,128)(2,1)S(1)} %pad_maximum_fusion.7), channel_id=1, source_target_pairs={{0,1},{1,0},{2,3},{3,2},{4,5},{5,4},{6,7},{7,6},{8,9},{9,8},{10,11... | collective-permute-start | bytes 393224 | tf_op jit(solution)/shard_map/ppermute | solution.py:371
  86.5 1.3 %collective-permute-start.28 = (bf16[256,128]{1,0:T(8,128)(2,1)S(1)}, bf16[256,128]{1,0:T(8,128)(2,1)S(1)}, u32[]{:S(2)}, u32[]{:S(2)}) collective-permute-start(bf16[256,128]{1,0:T(8,128)(2,1)S(1)} %add_convert_fusion.8), channel_id=1, source_target_pairs={{0,4},{1,5},{2,6},{3,7},{4,0},{5,1},{6,2},{7,3},{8,12},{9,13},{10,... | collective-permute-start | bytes 196616 | tf_op jit(solution)/shard_map/ppermute | solution.py:371
  87.8 1.4 %collective-permute-start.39 = (bf16[512,128]{1,0:T(8,128)(2,1)S(1)}, bf16[512,128]{1,0:T(8,128)(2,1)S(1)}, u32[]{:S(2)}, u32[]{:S(2)}) collective-permute-start(bf16[512,128]{1,0:T(8,128)(2,1)S(1)} %pad_maximum_fusion.9), channel_id=1, source_target_pairs={{0,2},{1,3},{2,0},{3,1},{4,6},{5,7},{6,4},{7,5},{8,10},{9,11},{10,... | collective-permute-start | bytes 393224 | tf_op jit(solution)/shard_map/ppermute | solution.py:371
  89.2 2.6 %collective-permute-done.28 = bf16[256,128]{1,0:T(8,128)(2,1)S(1)} collective-permute-done((bf16[256,128]{1,0:T(8,128)(2,1)S(1)}, bf16[256,128]{1,0:T(8,128)(2,1)S(1)}, u32[]{:S(2)}, u32[]{:S(2)}) %collective-permute-start.28) | collective-permute-done | bytes 65568 | tf_op jit(solution)/shard_map/ppermute | solution.py:371
  91.8 1.3 %collective-permute-start.29 = (bf16[512,128]{1,0:T(8,128)(2,1)S(1)}, bf16[512,128]{1,0:T(8,128)(2,1)S(1)}, u32[]{:S(2)}, u32[]{:S(2)}) collective-permute-start(bf16[512,128]{1,0:T(8,128)(2,1)S(1)} %pad_maximum_fusion.8), channel_id=1, source_target_pairs={{0,2},{1,3},{2,0},{3,1},{4,6},{5,7},{6,4},{7,5},{8,10},{9,11},{10,... | collective-permute-start | bytes 393224 | tf_op jit(solution)/shard_map/ppermute | solution.py:371
  93.3 3.5 %collective-permute-done.29 = bf16[512,128]{1,0:T(8,128)(2,1)S(1)} collective-permute-done((bf16[512,128]{1,0:T(8,128)(2,1)S(1)}, bf16[512,128]{1,0:T(8,128)(2,1)S(1)}, u32[]{:S(2)}, u32[]{:S(2)}) %collective-permute-start.29) | collective-permute-done | bytes 131104 | tf_op jit(solution)/shard_map/ppermute | solution.py:371
  98.0 1.2 %collective-permute-done.44 = bf16[128,128]{1,0:T(8,128)(2,1)S(1)} collective-permute-done((bf16[128,128]{1,0:T(8,128)(2,1)S(1)}, bf16[128,128]{1,0:T(8,128)(2,1)S(1)}, u32[]{:S(2)}, u32[]{:S(2)}) %collective-permute-start.44) | collective-permute-done | bytes 32800 | tf_op jit(solution)/shard_map/ppermute | solution.py:371
  99.3 2.8 %shard_map.133 = (f32[512,512]{1,0:T(8,128)}, f32[512,512]{1,0:T(8,128)}, f32[512,512]{1,0:T(8,128)}, f32[512,512]{1,0:T(8,128)}, f32[31,512]{1,0:T(8,128)}) custom-call(s32[9]{0:T(128)S(1)} %stack.54.bits, bf16[1024,128]{1,0:T(8,128)(2,1)S(1)} %pad_maximum_fusion.1.refs_0_, bf16[1024,128]{1,0:T(8,128)(2,1)S(1)} %pad_maximum_fusion.2.refs_1_, ...), custom_call_target="tpu_custom_call" | custom-call | tf_op jit(solution)/shard_map/pallas_call | solution.py:336
  102.1 2.1 %shard_map.134 = (f32[512,512]{1,0:T(8,128)}, f32[512,512]{1,0:T(8,128)}, f32[512,512]{1,0:T(8,128)}, f32[512,512]{1,0:T(8,128)}) custom-call(s32[9]{0:T(128)S(1)} %stack.54.bits, bf16[1024,128]{1,0:T(8,128)(2,1)S(1)} %collective-permute-done.45.refs_0_, ...), custom_call_target="tpu_custom_call", output_to_operand_aliasing={{0}: (5, {}), {1}: (6, {}), {2}: (7, {}), {3}: (8, {})} | custom-call | tf_op jit(solution)/shard_map/pallas_call | solution.py:336
  (103 shorter events, 11.2 us)
Async XLA Ops:
  1.4 12.0 %collective-permute-start.1 = (bf16[2,16,512]{2,1,0:T(8,128)(2,1)S(1)}, bf16[2,16,512]{2,1,0:T(8,128)(2,1)S(1)}, u32[]{:S(2)}, u32[]{:S(2)}) collective-permute-start(bf16[2,16,512]{2,1,0:T(8,128)(2,1)S(1)} %get-tuple-element.99), channel_id=1, source_target_pairs={{1,2},{3,4},{5,6},{9,10},{11,12},{13,14},{17,18},{19,20},{21,22},{... | collective-permute-start | bytes 98312 | tf_op jit(solution)/shard_map/ppermute | solution.py:371
  2.1 11.4 %collective-permute-start = (bf16[2,16,512]{2,1,0:T(8,128)(2,1)S(1)}, bf16[2,16,512]{2,1,0:T(8,128)(2,1)S(1)}, u32[]{:S(2)}, u32[]{:S(2)}) collective-permute-start(bf16[2,16,512]{2,1,0:T(8,128)(2,1)S(1)} %get-tuple-element.100), channel_id=1, source_target_pairs={{0,1},{1,0},{2,3},{3,2},{4,5},{5,4},{6,7},{7,6},{8,9},{9,8},{10,11... | collective-permute-start | bytes 98312 | tf_op jit(solution)/shard_map/ppermute | solution.py:371
  9.7 8.0 %collective-permute-start.5 = (bf16[2,32,512]{2,1,0:T(8,128)(2,1)S(1)}, bf16[2,32,512]{2,1,0:T(8,128)(2,1)S(1)}, u32[]{:S(2)}, u32[]{:S(2)}) collective-permute-start(bf16[2,32,512]{2,1,0:T(8,128)(2,1)S(1)} %get-tuple-element.57), channel_id=1, source_target_pairs={{0,8},{1,9},{2,10},{3,11},{4,12},{5,13},{6,14},{7,15},{8,0},{9,1},... | collective-permute-start | bytes 196616 | tf_op jit(solution)/shard_map/ppermute | solution.py:371
  9.8 8.0 %collective-permute-start.6 = (bf16[2,32,512]{2,1,0:T(8,128)(2,1)S(1)}, bf16[2,32,512]{2,1,0:T(8,128)(2,1)S(1)}, u32[]{:S(2)}, u32[]{:S(2)}) collective-permute-start(bf16[2,32,512]{2,1,0:T(8,128)(2,1)S(1)} %get-tuple-element.58), channel_id=1, source_target_pairs={{0,16},{1,17},{2,18},{3,19},{4,20},{5,21},{6,22},{7,23},{8,24},{9,... | collective-permute-start | bytes 196616 | tf_op jit(solution)/shard_map/ppermute | solution.py:371
  11.4 6.4 %collective-permute-start.7 = (bf16[2,32,512]{2,1,0:T(8,128)(2,1)S(1)}, bf16[2,32,512]{2,1,0:T(8,128)(2,1)S(1)}, u32[]{:S(2)}, u32[]{:S(2)}) collective-permute-start(bf16[2,32,512]{2,1,0:T(8,128)(2,1)S(1)} %get-tuple-element.59), channel_id=1, source_target_pairs={{0,24},{1,25},{2,26},{3,27},{4,28},{5,29},{6,30},{7,31},{8,16},{9,... | collective-permute-start | bytes 196616 | tf_op jit(solution)/shard_map/ppermute | solution.py:371
  15.8 2.0 %collective-permute-start.2 = (bf16[2,32,512]{2,1,0:T(8,128)(2,1)S(1)}, bf16[2,32,512]{2,1,0:T(8,128)(2,1)S(1)}, u32[]{:S(2)}, u32[]{:S(2)}) collective-permute-start(bf16[2,32,512]{2,1,0:T(8,128)(2,1)S(1)} %get-tuple-element.53), channel_id=1, source_target_pairs={{0,8},{1,9},{2,10},{3,11},{4,12},{5,13},{6,14},{7,15},{8,0},{9,1},... | collective-permute-start | bytes 196616 | tf_op jit(solution)/shard_map/ppermute | solution.py:371
  16.2 4.3 %collective-permute-start.3 = (bf16[2,32,512]{2,1,0:T(8,128)(2,1)S(1)}, bf16[2,32,512]{2,1,0:T(8,128)(2,1)S(1)}, u32[]{:S(2)}, u32[]{:S(2)}) collective-permute-start(bf16[2,32,512]{2,1,0:T(8,128)(2,1)S(1)} %get-tuple-element.54), channel_id=1, source_target_pairs={{0,16},{1,17},{2,18},{3,19},{4,20},{5,21},{6,22},{7,23},{8,24},{9,... | collective-permute-start | bytes 196616 | tf_op jit(solution)/shard_map/ppermute | solution.py:371
  17.7 4.4 %collective-permute-start.4 = (bf16[2,32,512]{2,1,0:T(8,128)(2,1)S(1)}, bf16[2,32,512]{2,1,0:T(8,128)(2,1)S(1)}, u32[]{:S(2)}, u32[]{:S(2)}) collective-permute-start(bf16[2,32,512]{2,1,0:T(8,128)(2,1)S(1)} %get-tuple-element.55), channel_id=1, source_target_pairs={{0,24},{1,25},{2,26},{3,27},{4,28},{5,29},{6,30},{7,31},{8,16},{9,... | collective-permute-start | bytes 196616 | tf_op jit(solution)/shard_map/ppermute | solution.py:371
  27.9 3.1 %collective-permute-start.8 = (bf16[2048,128]{1,0:T(8,128)(2,1)S(1)}, bf16[2048,128]{1,0:T(8,128)(2,1)S(1)}, u32[]{:S(2)}, u32[]{:S(2)}) collective-permute-start(bf16[2048,128]{1,0:T(8,128)(2,1)S(1)} %get-tuple-element.62), channel_id=1, source_target_pairs={{0,8},{1,9},{2,10},{3,11},{4,12},{5,13},{6,14},{7,15},{8,0},{9,1},... | collective-permute-start | bytes 1572872 | tf_op jit(solution)/shard_map/ppermute | solution.py:371
  28.1 2.2 %collective-permute-start.30 = (bf16[1024,128]{1,0:T(8,128)(2,1)S(1)}, bf16[1024,128]{1,0:T(8,128)(2,1)S(1)}, u32[]{:S(2)}, u32[]{:S(2)}) collective-permute-start(bf16[1024,128]{1,0:T(8,128)(2,1)S(1)} %get-tuple-element.66), channel_id=1, source_target_pairs={{0,8},{1,9},{2,10},{3,11},{4,12},{5,13},{6,14},{7,15},{8,0},{9,1},... | collective-permute-start | bytes 786440 | tf_op jit(solution)/shard_map/ppermute | solution.py:371
  28.5 4.7 %collective-permute-start.23 = (bf16[2048,128]{1,0:T(8,128)(2,1)S(1)}, bf16[2048,128]{1,0:T(8,128)(2,1)S(1)}, u32[]{:S(2)}, u32[]{:S(2)}) collective-permute-start(bf16[2048,128]{1,0:T(8,128)(2,1)S(1)} %get-tuple-element.64), channel_id=1, source_target_pairs={{0,8},{1,9},{2,10},{3,11},{4,12},{5,13},{6,14},{7,15},{8,0},{9,1},... | collective-permute-start | bytes 1572872 | tf_op jit(solution)/shard_map/ppermute | solution.py:371
  30.3 11.3 %collective-permute-start.31 = (bf16[1024,128]{1,0:T(8,128)(2,1)S(1)}, bf16[1024,128]{1,0:T(8,128)(2,1)S(1)}, u32[]{:S(2)}, u32[]{:S(2)}) collective-permute-start(bf16[1024,128]{1,0:T(8,128)(2,1)S(1)} %pad_maximum_fusion.4), channel_id=1, source_target_pairs={{0,16},{1,17},{2,18},{3,19},{4,20},{5,21},{6,22},{7,23},{8,24},{9,... | collective-permute-start | bytes 786440 | tf_op jit(solution)/shard_map/ppermute | solution.py:371
  31.1 6.4 %collective-permute-start.16 = (bf16[512,128]{1,0:T(8,128)(2,1)S(1)}, bf16[512,128]{1,0:T(8,128)(2,1)S(1)}, u32[]{:S(2)}, u32[]{:S(2)}) collective-permute-start(bf16[512,128]{1,0:T(8,128)(2,1)S(1)} %get-tuple-element.97), channel_id=1, source_target_pairs={{0,1},{1,0},{2,3},{3,2},{4,5},{5,4},{6,7},{7,6},{8,9},{9,8},{10,11... | collective-permute-start | bytes 393224 | tf_op jit(solution)/shard_map/ppermute | solution.py:371
  31.3 8.2 %collective-permute-start.9 = (bf16[512,128]{1,0:T(8,128)(2,1)S(1)}, bf16[512,128]{1,0:T(8,128)(2,1)S(1)}, u32[]{:S(2)}, u32[]{:S(2)}) collective-permute-start(bf16[512,128]{1,0:T(8,128)(2,1)S(1)} %get-tuple-element.98), channel_id=1, source_target_pairs={{0,1},{1,0},{2,3},{3,2},{4,5},{5,4},{6,7},{7,6},{8,9},{9,8},{10,11... | collective-permute-start | bytes 393224 | tf_op jit(solution)/shard_map/ppermute | solution.py:371
  33.3 8.3 %collective-permute-start.32 = (bf16[512,128]{1,0:T(8,128)(2,1)S(1)}, bf16[512,128]{1,0:T(8,128)(2,1)S(1)}, u32[]{:S(2)}, u32[]{:S(2)}) collective-permute-start(bf16[512,128]{1,0:T(8,128)(2,1)S(1)} %get-tuple-element.91), channel_id=1, source_target_pairs={{0,2},{1,3},{2,0},{3,1},{4,6},{5,7},{6,4},{7,5},{8,10},{9,11},{10,... | collective-permute-start | bytes 393224 | tf_op jit(solution)/shard_map/ppermute | solution.py:371
  34.9 18.7 %collective-permute-start.24 = (bf16[512,128]{1,0:T(8,128)(2,1)S(1)}, bf16[512,128]{1,0:T(8,128)(2,1)S(1)}, u32[]{:S(2)}, u32[]{:S(2)}) collective-permute-start(bf16[512,128]{1,0:T(8,128)(2,1)S(1)} %get-tuple-element.92), channel_id=1, source_target_pairs={{0,2},{1,3},{2,0},{3,1},{4,6},{5,7},{6,4},{7,5},{8,10},{9,11},{10,... | collective-permute-start | bytes 393224 | tf_op jit(solution)/shard_map/ppermute | solution.py:371
  39.5 4.3 %collective-permute-start.17 = (bf16[256,128]{1,0:T(8,128)(2,1)S(1)}, bf16[256,128]{1,0:T(8,128)(2,1)S(1)}, u32[]{:S(2)}, u32[]{:S(2)}) collective-permute-start(bf16[256,128]{1,0:T(8,128)(2,1)S(1)} %get-tuple-element.95), channel_id=1, source_target_pairs={{0,16},{1,17},{2,18},{3,19},{4,20},{5,21},{6,22},{7,23},{8,24},{9,... | collective-permute-start | bytes 196616 | tf_op jit(solution)/shard_map/ppermute | solution.py:371
  40.7 8.4 %collective-permute-start.10 = (bf16[256,128]{1,0:T(8,128)(2,1)S(1)}, bf16[256,128]{1,0:T(8,128)(2,1)S(1)}, u32[]{:S(2)}, u32[]{:S(2)}) collective-permute-start(bf16[256,128]{1,0:T(8,128)(2,1)S(1)} %get-tuple-element.96), channel_id=1, source_target_pairs={{0,16},{1,17},{2,18},{3,19},{4,20},{5,21},{6,22},{7,23},{8,24},{9,... | collective-permute-start | bytes 196616 | tf_op jit(solution)/shard_map/ppermute | solution.py:371
  42.4 31.4 %collective-permute-start.33 = (bf16[2,16,512]{2,1,0:T(8,128)(2,1)S(1)}, bf16[2,16,512]{2,1,0:T(8,128)(2,1)S(1)}, u32[]{:S(2)}, u32[]{:S(2)}) collective-permute-start(bf16[2,16,512]{2,1,0:T(8,128)(2,1)S(1)} %get-tuple-element.71), channel_id=1, source_target_pairs={{0,1},{1,0},{2,3},{3,2},{4,5},{5,4},{6,7},{7,6},{8,9},{9,8},{10,11... | collective-permute-start | bytes 98312 | tf_op jit(solution)/shard_map/ppermute | solution.py:371
  42.7 31.9 %collective-permute-start.34 = (bf16[2,16,512]{2,1,0:T(8,128)(2,1)S(1)}, bf16[2,16,512]{2,1,0:T(8,128)(2,1)S(1)}, u32[]{:S(2)}, u32[]{:S(2)}) collective-permute-start(bf16[2,16,512]{2,1,0:T(8,128)(2,1)S(1)} %get-tuple-element.72), channel_id=1, source_target_pairs={{1,2},{3,4},{5,6},{9,10},{11,12},{13,14},{17,18},{19,20},{21,22},{... | collective-permute-start | bytes 98312 | tf_op jit(solution)/shard_map/ppermute | solution.py:371
  43.8 10.3 %collective-permute-start.35 = (bf16[256,128]{1,0:T(8,128)(2,1)S(1)}, bf16[256,128]{1,0:T(8,128)(2,1)S(1)}, u32[]{:S(2)}, u32[]{:S(2)}) collective-permute-start(bf16[256,128]{1,0:T(8,128)(2,1)S(1)} %add_convert_fusion.7), channel_id=1, source_target_pairs={{0,4},{1,5},{2,6},{3,7},{4,0},{5,1},{6,2},{7,3},{8,12},{9,13},{10,... | collective-permute-start | bytes 196616 | tf_op jit(solution)/shard_map/ppermute | solution.py:371
  49.2 5.3 %collective-permute-start.18 = (bf16[128,128]{1,0:T(8,128)(2,1)S(1)}, bf16[128,128]{1,0:T(8,128)(2,1)S(1)}, u32[]{:S(2)}, u32[]{:S(2)}) collective-permute-start(bf16[128,128]{1,0:T(8,128)(2,1)S(1)} %add_convert_fusion.21), channel_id=1, source_target_pairs={{0,2},{1,3},{2,0},{3,1},{4,6},{5,7},{6,4},{7,5},{8,10},{9,11},{10,... | collective-permute-start | bytes 98312 | tf_op jit(solution)/shard_map/ppermute | solution.py:371
  53.7 4.0 %collective-permute-start.40 = (bf16[128,128]{1,0:T(8,128)(2,1)S(1)}, bf16[128,128]{1,0:T(8,128)(2,1)S(1)}, u32[]{:S(2)}, u32[]{:S(2)}) collective-permute-start(bf16[128,128]{1,0:T(8,128)(2,1)S(1)} %shard_map.132), channel_id=1, source_target_pairs={{0,2},{1,3},{2,0},{3,1},{4,6},{5,7},{6,4},{7,5},{8,10},{9,11},{10,... | collective-permute-start | bytes 98312 | tf_op jit(solution)/shard_map/ppermute | solution.py:371
  54.2 5.6 %collective-permute-start.25 = (bf16[256,128]{1,0:T(8,128)(2,1)S(1)}, bf16[256,128]{1,0:T(8,128)(2,1)S(1)}, u32[]{:S(2)}, u32[]{:S(2)}) collective-permute-start(bf16[256,128]{1,0:T(8,128)(2,1)S(1)} %get-tuple-element.90), channel_id=1, source_target_pairs={{0,4},{1,5},{2,6},{3,7},{4,0},{5,1},{6,2},{7,3},{8,12},{9,13},{10,... | collective-permute-start | bytes 196616 | tf_op jit(solution)/shard_map/ppermute | solution.py:371
  54.5 13.3 %collective-permute-start.36 = (bf16[256,128]{1,0:T(8,128)(2,1)S(1)}, bf16[256,128]{1,0:T(8,128)(2,1)S(1)}, u32[]{:S(2)}, u32[]{:S(2)}) collective-permute-start(bf16[256,128]{1,0:T(8,128)(2,1)S(1)} %get-tuple-element.89), channel_id=1, source_target_pairs={{0,1},{1,0},{2,3},{3,2},{4,5},{5,4},{6,7},{7,6},{8,9},{9,8},{10,11... | collective-permute-start | bytes 196616 | tf_op jit(solution)/shard_map/ppermute | solution.py:371
  57.6 3.9 %collective-permute-start.11 = (bf16[128,128]{1,0:T(8,128)(2,1)S(1)}, bf16[128,128]{1,0:T(8,128)(2,1)S(1)}, u32[]{:S(2)}, u32[]{:S(2)}) collective-permute-start(bf16[128,128]{1,0:T(8,128)(2,1)S(1)} %get-tuple-element.94), channel_id=1, source_target_pairs={{0,2},{1,3},{2,0},{3,1},{4,6},{5,7},{6,4},{7,5},{8,10},{9,11},{10,... | collective-permute-start | bytes 98312 | tf_op jit(solution)/shard_map/ppermute | solution.py:371
  59.8 5.2 %collective-permute-start.19 = (bf16[128,128]{1,0:T(8,128)(2,1)S(1)}, bf16[128,128]{1,0:T(8,128)(2,1)S(1)}, u32[]{:S(2)}, u32[]{:S(2)}) collective-permute-start(bf16[128,128]{1,0:T(8,128)(2,1)S(1)} %get-tuple-element.93), channel_id=1, source_target_pairs={{0,4},{1,5},{2,6},{3,7},{4,0},{5,1},{6,2},{7,3},{8,12},{9,13},{10,... | collective-permute-start | bytes 98312 | tf_op jit(solution)/shard_map/ppermute | solution.py:371
  61.6 4.8 %collective-permute-start.41 = (bf16[128,128]{1,0:T(8,128)(2,1)S(1)}, bf16[128,128]{1,0:T(8,128)(2,1)S(1)}, u32[]{:S(2)}, u32[]{:S(2)}) collective-permute-start(bf16[128,128]{1,0:T(8,128)(2,1)S(1)} %add_convert_fusion.18), channel_id=1, source_target_pairs={{0,4},{1,5},{2,6},{3,7},{4,0},{5,1},{6,2},{7,3},{8,12},{9,13},{10,... | collective-permute-start | bytes 98312 | tf_op jit(solution)/shard_map/ppermute | solution.py:371
  65.0 4.8 %collective-permute-start.12 = (bf16[128,128]{1,0:T(8,128)(2,1)S(1)}, bf16[128,128]{1,0:T(8,128)(2,1)S(1)}, u32[]{:S(2)}, u32[]{:S(2)}) collective-permute-start(bf16[128,128]{1,0:T(8,128)(2,1)S(1)} %add_convert_fusion.23), channel_id=1, source_target_pairs={{0,4},{1,5},{2,6},{3,7},{4,0},{5,1},{6,2},{7,3},{8,12},{9,13},{10,... | collective-permute-start | bytes 98312 | tf_op jit(solution)/shard_map/ppermute | solution.py:371
  66.4 6.6 %collective-permute-start.20 = (bf16[128,128]{1,0:T(8,128)(2,1)S(1)}, bf16[128,128]{1,0:T(8,128)(2,1)S(1)}, u32[]{:S(2)}, u32[]{:S(2)}) collective-permute-start(bf16[128,128]{1,0:T(8,128)(2,1)S(1)} %add_convert_fusion.19), channel_id=1, source_target_pairs={{0,2},{1,3},{2,0},{3,1},{4,6},{5,7},{6,4},{7,5},{8,10},{9,11},{10,... | collective-permute-start | bytes 98312 | tf_op jit(solution)/shard_map/ppermute | solution.py:371
  67.8 4.0 %collective-permute-start.42 = (bf16[128,128]{1,0:T(8,128)(2,1)S(1)}, bf16[128,128]{1,0:T(8,128)(2,1)S(1)}, u32[]{:S(2)}, u32[]{:S(2)}) collective-permute-start(bf16[128,128]{1,0:T(8,128)(2,1)S(1)} %add_convert_fusion.17), channel_id=1, source_target_pairs={{0,1},{1,0},{2,3},{3,2},{4,5},{5,4},{6,7},{7,6},{8,9},{9,8},{10,11... | collective-permute-start | bytes 98312 | tf_op jit(solution)/shard_map/ppermute | solution.py:371
  69.8 9.8 %collective-permute-start.26 = (bf16[256,128]{1,0:T(8,128)(2,1)S(1)}, bf16[256,128]{1,0:T(8,128)(2,1)S(1)}, u32[]{:S(2)}, u32[]{:S(2)}) collective-permute-start(bf16[256,128]{1,0:T(8,128)(2,1)S(1)} %add_convert_fusion.10), channel_id=1, source_target_pairs={{0,1},{1,0},{2,3},{3,2},{4,5},{5,4},{6,7},{7,6},{8,9},{9,8},{10,11... | collective-permute-start | bytes 196616 | tf_op jit(solution)/shard_map/ppermute | solution.py:371
  71.8 9.1 %collective-permute-start.37 = (bf16[256,128]{1,0:T(8,128)(2,1)S(1)}, bf16[256,128]{1,0:T(8,128)(2,1)S(1)}, u32[]{:S(2)}, u32[]{:S(2)}) collective-permute-start(bf16[256,128]{1,0:T(8,128)(2,1)S(1)} %add_convert_fusion.5), channel_id=1, source_target_pairs={{0,16},{1,17},{2,18},{3,19},{4,20},{5,21},{6,22},{7,23},{8,24},{9,... | collective-permute-start | bytes 196616 | tf_op jit(solution)/shard_map/ppermute | solution.py:371
  73.0 5.7 %collective-permute-start.13 = (bf16[128,128]{1,0:T(8,128)(2,1)S(1)}, bf16[128,128]{1,0:T(8,128)(2,1)S(1)}, u32[]{:S(2)}, u32[]{:S(2)}) collective-permute-start(bf16[128,128]{1,0:T(8,128)(2,1)S(1)} %add_convert_fusion.22), channel_id=1, source_target_pairs={{0,2},{1,3},{2,0},{3,1},{4,6},{5,7},{6,4},{7,5},{8,10},{9,11},{10,... | collective-permute-start | bytes 98312 | tf_op jit(solution)/shard_map/ppermute | solution.py:371
  73.8 10.5 %collective-permute-start.21 = (bf16[256,128]{1,0:T(8,128)(2,1)S(1)}, bf16[256,128]{1,0:T(8,128)(2,1)S(1)}, u32[]{:S(2)}, u32[]{:S(2)}) collective-permute-start(bf16[256,128]{1,0:T(8,128)(2,1)S(1)} %pad_maximum_fusion.11), channel_id=1, source_target_pairs={{0,16},{1,17},{2,18},{3,19},{4,20},{5,21},{6,22},{7,23},{8,24},{9,... | collective-permute-start | bytes 196616 | tf_op jit(solution)/shard_map/ppermute | solution.py:371
  74.6 22.9 %collective-permute-start.43 = (bf16[128,128]{1,0:T(8,128)(2,1)S(1)}, bf16[128,128]{1,0:T(8,128)(2,1)S(1)}, u32[]{:S(2)}, u32[]{:S(2)}) collective-permute-start(bf16[128,128]{1,0:T(8,128)(2,1)S(1)} %add_convert_fusion.16), channel_id=1, source_target_pairs={{0,16},{1,17},{2,18},{3,19},{4,20},{5,21},{6,22},{7,23},{8,24},{9,... | collective-permute-start | bytes 98312 | tf_op jit(solution)/shard_map/ppermute | solution.py:371
  78.8 7.4 %collective-permute-start.14 = (bf16[256,128]{1,0:T(8,128)(2,1)S(1)}, bf16[256,128]{1,0:T(8,128)(2,1)S(1)}, u32[]{:S(2)}, u32[]{:S(2)}) collective-permute-start(bf16[256,128]{1,0:T(8,128)(2,1)S(1)} %pad_maximum_fusion.10), channel_id=1, source_target_pairs={{0,16},{1,17},{2,18},{3,19},{4,20},{5,21},{6,22},{7,23},{8,24},{9,... | collective-permute-start | bytes 196616 | tf_op jit(solution)/shard_map/ppermute | solution.py:371
  79.6 6.9 %collective-permute-start.27 = (bf16[256,128]{1,0:T(8,128)(2,1)S(1)}, bf16[256,128]{1,0:T(8,128)(2,1)S(1)}, u32[]{:S(2)}, u32[]{:S(2)}) collective-permute-start(bf16[256,128]{1,0:T(8,128)(2,1)S(1)} %add_convert_fusion.9), channel_id=1, source_target_pairs={{0,16},{1,17},{2,18},{3,19},{4,20},{5,21},{6,22},{7,23},{8,24},{9,... | collective-permute-start | bytes 196616 | tf_op jit(solution)/shard_map/ppermute | solution.py:371
  81.0 6.9 %collective-permute-start.38 = (bf16[256,128]{1,0:T(8,128)(2,1)S(1)}, bf16[256,128]{1,0:T(8,128)(2,1)S(1)}, u32[]{:S(2)}, u32[]{:S(2)}) collective-permute-start(bf16[256,128]{1,0:T(8,128)(2,1)S(1)} %add_convert_fusion.4), channel_id=1, source_target_pairs={{0,4},{1,5},{2,6},{3,7},{4,0},{5,1},{6,2},{7,3},{8,12},{9,13},{10,... | collective-permute-start | bytes 196616 | tf_op jit(solution)/shard_map/ppermute | solution.py:371
  84.3 8.8 %collective-permute-start.22 = (bf16[512,128]{1,0:T(8,128)(2,1)S(1)}, bf16[512,128]{1,0:T(8,128)(2,1)S(1)}, u32[]{:S(2)}, u32[]{:S(2)}) collective-permute-start(bf16[512,128]{1,0:T(8,128)(2,1)S(1)} %pad_maximum_fusion.7), channel_id=1, source_target_pairs={{0,1},{1,0},{2,3},{3,2},{4,5},{5,4},{6,7},{7,6},{8,9},{9,8},{10,11... | collective-permute-start | bytes 393224 | tf_op jit(solution)/shard_map/ppermute | solution.py:371
  86.2 7.1 %collective-permute-start.15 = (bf16[512,128]{1,0:T(8,128)(2,1)S(1)}, bf16[512,128]{1,0:T(8,128)(2,1)S(1)}, u32[]{:S(2)}, u32[]{:S(2)}) collective-permute-start(bf16[512,128]{1,0:T(8,128)(2,1)S(1)} %pad_maximum_fusion.6), channel_id=1, source_target_pairs={{0,1},{1,0},{2,3},{3,2},{4,5},{5,4},{6,7},{7,6},{8,9},{9,8},{10,11... | collective-permute-start | bytes 393224 | tf_op jit(solution)/shard_map/ppermute | solution.py:371
  86.5 5.3 %collective-permute-start.28 = (bf16[256,128]{1,0:T(8,128)(2,1)S(1)}, bf16[256,128]{1,0:T(8,128)(2,1)S(1)}, u32[]{:S(2)}, u32[]{:S(2)}) collective-permute-start(bf16[256,128]{1,0:T(8,128)(2,1)S(1)} %add_convert_fusion.8), channel_id=1, source_target_pairs={{0,4},{1,5},{2,6},{3,7},{4,0},{5,1},{6,2},{7,3},{8,12},{9,13},{10,... | collective-permute-start | bytes 196616 | tf_op jit(solution)/shard_map/ppermute | solution.py:371
  87.8 5.3 %collective-permute-start.39 = (bf16[512,128]{1,0:T(8,128)(2,1)S(1)}, bf16[512,128]{1,0:T(8,128)(2,1)S(1)}, u32[]{:S(2)}, u32[]{:S(2)}) collective-permute-start(bf16[512,128]{1,0:T(8,128)(2,1)S(1)} %pad_maximum_fusion.9), channel_id=1, source_target_pairs={{0,2},{1,3},{2,0},{3,1},{4,6},{5,7},{6,4},{7,5},{8,10},{9,11},{10,... | collective-permute-start | bytes 393224 | tf_op jit(solution)/shard_map/ppermute | solution.py:371
  91.8 5.0 %collective-permute-start.29 = (bf16[512,128]{1,0:T(8,128)(2,1)S(1)}, bf16[512,128]{1,0:T(8,128)(2,1)S(1)}, u32[]{:S(2)}, u32[]{:S(2)}) collective-permute-start(bf16[512,128]{1,0:T(8,128)(2,1)S(1)} %pad_maximum_fusion.8), channel_id=1, source_target_pairs={{0,2},{1,3},{2,0},{3,1},{4,6},{5,7},{6,4},{7,5},{8,10},{9,11},{10,... | collective-permute-start | bytes 393224 | tf_op jit(solution)/shard_map/ppermute | solution.py:371
  93.2 8.8 %collective-permute-start.47 = (bf16[1024,128]{1,0:T(8,128)(2,1)S(1)}, bf16[1024,128]{1,0:T(8,128)(2,1)S(1)}, u32[]{:S(2)}, u32[]{:S(2)}) collective-permute-start(bf16[1024,128]{1,0:T(8,128)(2,1)S(1)} %pad_maximum_fusion.5.refs_2_), channel_id=1, source_target_pairs={{0,8},{1,9},{2,10},{3,11},{4,12},{5,13},{6,14},{7,15},{8,0},{9,1},... | collective-permute-start | bytes 786440 | tf_op jit(solution)/shard_map/ppermute | solution.py:371
  96.9 5.2 %collective-permute-start.45 = (bf16[1024,128]{1,0:T(8,128)(2,1)S(1)}, bf16[1024,128]{1,0:T(8,128)(2,1)S(1)}, u32[]{:S(2)}, u32[]{:S(2)}) collective-permute-start(bf16[1024,128]{1,0:T(8,128)(2,1)S(1)} %pad_maximum_fusion.1.refs_0_), channel_id=1, source_target_pairs={{0,8},{1,9},{2,10},{3,11},{4,12},{5,13},{6,14},{7,15},{8,0},{9,1},... | collective-permute-start | bytes 786440 | tf_op jit(solution)/shard_map/ppermute | solution.py:371
  96.9 5.1 %collective-permute-start.46 = (bf16[1024,128]{1,0:T(8,128)(2,1)S(1)}, bf16[1024,128]{1,0:T(8,128)(2,1)S(1)}, u32[]{:S(2)}, u32[]{:S(2)}) collective-permute-start(bf16[1024,128]{1,0:T(8,128)(2,1)S(1)} %pad_maximum_fusion.2.refs_1_), channel_id=1, source_target_pairs={{0,8},{1,9},{2,10},{3,11},{4,12},{5,13},{6,14},{7,15},{8,0},{9,1},... | collective-permute-start | bytes 786440 | tf_op jit(solution)/shard_map/ppermute | solution.py:371
  97.4 4.6 %collective-permute-start.48 = (bf16[1024,128]{1,0:T(8,128)(2,1)S(1)}, bf16[1024,128]{1,0:T(8,128)(2,1)S(1)}, u32[]{:S(2)}, u32[]{:S(2)}) collective-permute-start(bf16[1024,128]{1,0:T(8,128)(2,1)S(1)} %pad_maximum_fusion.3.refs_3_), channel_id=1, source_target_pairs={{0,8},{1,9},{2,10},{3,11},{4,12},{5,13},{6,14},{7,15},{8,0},{9,1},... | collective-permute-start | bytes 786440 | tf_op jit(solution)/shard_map/ppermute | solution.py:371
  (5 other events, 39.9 us)

commit v8 on v7

--- a/solution.py
+++ b/solution.py
@@ -16,7 +16,6 @@
 BF = jnp.bfloat16
 F32 = jnp.float32
 MIB = 1024 * 1024
-CHAINS = 2
 CORE, Y, X, Z, ZZ, BLOCK_AT = range(6)
 
 
@@ -42,23 +41,11 @@
 
 
 def ways(bits, half):
-    return (bits[X], bits[Y], bits[Z]) if half == 0 else (bits[Z], bits[ZZ], 0)
+    return [bits[i] for i in ((X, Y, ZZ), (Z, X, Y))[half]]
 
 
 def sigmoid(v):
     return 0.5 * jnp.tanh(0.5 * v) + 0.5
-
-
-def scatter_kernel(sub, bits, source, *refs):
-    outs, sems = refs[:4], refs[4]
-    copies = []
-    for d in range(4):
-        rows = pl.ds(pl.multiple_of(bits[BLOCK_AT + d] * sub, sub), sub)
-        copies.append(pltpu.make_async_copy(source.at[:, rows], outs[d], sems.at[d]))
-    for copy in copies:
-        copy.start()
-    for copy in copies:
-        copy.wait()
 
 
 def padded(bits, rows, x_got, z_got, m, lanes):
@@ -177,7 +164,7 @@
             put(2, c, lanes, pick(mm(wb, u, TN)))
 
     dacted = mm(flat(0), wq[...], NT) + mm(flat(1), wk[...], NT) + mm(flat(2), wv[...], NT)
-    size = cols * width // 8 // CHAINS
+    size = cols * width // 8
     core = bits[CORE]
     for out, owner, h in (
         (a_send, 1 - core, 0), (b_send, 1 - core, 1), (a_keep, core, 0), (b_keep, core, 1)
@@ -187,11 +174,10 @@
         grad = mm(left_s[i // 3], flat(i), TN).astype(BF)
         for piece in range(8):
             rel = ((piece // 4) ^ first) * 4 + ((piece // 2 % 2) ^ second) * 2 + ((piece % 2) ^ third)
-            for chain in range(CHAINS):
-                at = (piece * CHAINS + chain) * size
-                cb, at = at // width, at % width
-                start = pl.multiple_of((chain * 8 + rel) * size, size)
-                out[pl.ds(start, size), :] = grad[at : at + size, cb * LANES : (cb + 1) * LANES]
+            cb, at = piece * size // width, piece * size % width
+            out[pl.ds(pl.multiple_of(rel * size, size), size), :] = grad[
+                at : at + size, cb * LANES : (cb + 1) * LANES
+            ]
 
     unit = 2 * count * cols * sub
     for d, (out, base) in enumerate(
@@ -213,42 +199,39 @@
     return functools.reduce(lambda x, y: x + y, [x.astype(F32) for x in parts]).astype(BF)
 
 
-def final_kernel(plan, first_call, bits, *refs):
-    width, norm = plan
+def final_kernel(plan, bits, *refs):
+    kinds, first_call, width, norm = plan
     cols = width // LANES
-    size = cols * width // 8 // CHAINS
-    got, refs = refs[: 2 * CHAINS], refs[2 * CHAINS :]
-    if first_call:
-        taps, outs, tap_grad, grad_s, sems = refs[0], refs[1:5], refs[5], refs[6], refs[7]
-        for lc in range(cols):
-            tap_grad[:, lc * LANES : (lc + 1) * LANES] = (
-                taps[lc * 32 : lc * 32 + 31, :].astype(F32) * norm
-            )
-    else:
-        outs, grad_s, sems = refs[4:8], refs[8], refs[9]
+    size = cols * width // 8
+    got, refs = refs[: len(kinds)], refs[len(kinds) :]
+    if not first_call:
+        refs = refs[4:]
+    outs, piece_s, sems = refs[:4], refs[4], refs[5]
     core = bits[CORE]
-    owner = core if first_call else 1 - core
-    for h in range(2):
+    copies = []
+    for n, (own, h, far) in enumerate(kinds):
+        owner = core if own else 1 - core
         first, second, third = ways(bits, h)
-        for rel in range(8):
-            piece = (first ^ (rel // 4)) * 4 + (second ^ (rel // 2 % 2)) * 2 + (third ^ (rel % 2))
-            for chain in range(CHAINS):
-                at = (piece * CHAINS + chain) * size
-                cb, at = at // width, at % width
-                grad_s[
-                    h,
-                    pl.ds(pl.multiple_of(at, size), size),
-                    pl.ds(pl.multiple_of(cb * LANES, LANES), LANES),
-                ] = got[h * CHAINS + chain][rel * size : (rel + 1) * size, :].astype(F32) * norm
-        for which in range(2):
-            @pl.when(owner == which)
-            def _():
-                pltpu.make_async_copy(grad_s.at[h], outs[2 * which + h], sems.at[h]).start()
-    for h in range(2):
-        for which in range(2):
-            @pl.when(owner == which)
-            def _():
-                pltpu.make_async_copy(grad_s.at[h], outs[2 * which + h], sems.at[h]).wait()
+        for rel in range(4):
+            k = 4 * n + rel
+            piece_s[k] = got[n][rel * size : (rel + 1) * size, :].astype(F32) * norm
+            piece = (first ^ far) * 4 + (second ^ (rel // 2)) * 2 + (third ^ (rel % 2))
+            cb, at = piece * size // width, piece * size % width
+            rows = pl.ds(pl.multiple_of(at, size), size)
+            lanes = pl.ds(pl.multiple_of(cb * LANES, LANES), LANES)
+            for which in range(2):
+                copy = pltpu.make_async_copy(
+                    piece_s.at[k], outs[2 * which + h].at[rows, lanes], sems.at[k]
+                )
+                copies.append((owner == which, copy))
+                pl.when(owner == which)(copy.start)
+    for here, copy in copies:
+        pl.when(here)(copy.wait)
+
+
+def tap_grad_kernel(norm, taps, grad):
+    for lc, lanes in enumerate(lanes_of(grad.shape[1])):
+        grad[:, lanes] = taps[lc * 32 : lc * 32 + 31, :].astype(F32) * norm
 
 
 def home_chunks(plan, bits, own, core_got, y_got, kind):
@@ -388,24 +371,23 @@
         lax.dynamic_slice_in_dim(frames, (1 - odd) * last, HALO, axis=1),
         lax.dynamic_slice_in_dim(frames, odd * last, HALO, axis=1),
     )
+    cot_parts = spread(
+        [lax.dynamic_slice_in_dim(cotangent, (mic ^ d) * sub, sub, axis=1) for d in range(4)]
+    )
     block = shape((count, sub, width), BF)
-    cot_parts = spread(
-        call(
-            functools.partial(scatter_kernel, sub), (block,) * 4,
-            [pltpu.SemaphoreType.DMA((4,))], 8, bits, cotangent, hbm=(1,),
-        )
-    )
-    weights = jnp.stack([w_query, w_key, w_value, w_out])
     wide = shape(frames.shape, F32)
     here = pltpu.VMEM(frames.shape, BF)
     conv, *acted = call(
         functools.partial(conv_kernel, sub), (wide,) + (block,) * 4, [here],
         8, bits, frames, frame_x, frame_z, kernel,
     )
-    *acted, weights = lax.optimization_barrier((*acted, weights))
+    own_acted, *weights = lax.optimization_barrier(
+        (acted[0], w_query, w_key, w_value, w_out)
+    )
+    weights = jnp.stack(weights)
 
     factor = 1.0 / math.sqrt(width // HEADS)
-    part = width * width // LANES // CHAINS
+    part = width * width // LANES
     unit = 2 * count * cols * sub
     big = pltpu.VMEM((rows, width), BF)
 
@@ -414,13 +396,13 @@
 
     a_keep, b_keep, a_send, b_send, back_keep, back_send = call(
         functools.partial(main_kernel, (groups, count, sub, width, factor)),
-        (flat(CHAINS * part),) * 4 + (flat(2 * unit),) * 2,
+        (flat(part),) * 4 + (flat(2 * unit),) * 2,
         [
             pltpu.VMEM((2, rows, width), BF),
             pltpu.VMEM((4, cuts, groups, count, HALO, width), BF),
             big, big, big, big,
         ],
-        24, bits, *spread(acted), *cot_parts, weights,
+        24, bits, *spread([own_acted] + acted[1:]), *cot_parts, weights,
     )
 
     def halved(parts, mask):
@@ -435,67 +417,76 @@
     def doubled(x, mask):
         return jnp.concatenate([x, swap(x, mask)])
 
-    def chains(*arrays):
-        return [[t[i * part : (i + 1) * part] for t in arrays] for i in range(CHAINS)]
-
     def after(x, y):
         return lax.optimization_barrier((x, y))[0]
 
-    a = chains(a_keep, swap(a_send, over_core))
-    b = chains(b_keep, swap(b_send, over_core))
+    a = [a_keep, swap(a_send, over_core)]
+    b = [b_keep, swap(b_send, over_core)]
     core_got = swap(back_send, over_core)
     y_got = swap(jnp.concatenate([back_keep[unit:], core_got[unit:]]), over_y)
-    a = [halved(t, over_x) for t in a]
-    b = [halved(t, lines[0]) for t in b]
+    a = halved(a, over_x)
+    b = halved(b, lines[0])
     plan = (count, sub, cols)
-    y_got = after(y_got, (a[0][-1], b[0][-1]))
+    y_got = after(y_got, (a[-1], b[-1]))
     home = (bits, back_keep, core_got, y_got)
     edge = shape((count, HALO, width), BF)
     dconv, x_edge, z_edge = call(
         functools.partial(dconv_kernel, plan), (wide, edge, edge), [], 8, *home, conv
     )
     x_edge, z_edge = swap_edges(x_edge, z_edge)
-    a = [halved(t, over_y) for t in a]
-    b = [halved(t, lines[1]) for t in b]
+    a = halved(a, over_y)
+    b = halved(b, over_x)
     (taps,) = call(
         functools.partial(tap_kernel, sub), (flat(32 * cols),),
         [pltpu.VMEM((count, length + 2 * HALO, width), F32)],
-        8, bits, frames, frame_x, frame_z, after(dconv, a[0][-1]),
-    )
-    taps = exchanged(taps, lines + [over_x, over_y, over_core])
-    a = [exchanged(total(*halved(t, lines[0])), lines[1:]) for t in a]
-    b = [exchanged(total(*t), [over_x, over_y] + lines[2:]) for t in b]
+        8, bits, frames, frame_x, frame_z, after(dconv, a[-1]),
+    )
+    taps = exchanged(taps, lines)
+    a = exchanged(total(*halved(a, lines[1])), lines[:1] + lines[2:])
+    b = exchanged(total(*halved(b, over_y)), lines[1:])
     (frame_grad,) = call(
         frame_kernel, (shape(frames.shape, BF),), [], 8,
-        bits, after(dconv, a[0]), x_edge, z_edge, cotangent, kernel,
-    )
-    a = [doubled(t, lines[0]) for t in a]
-    b = [doubled(t, lines[1]) for t in b]
+        bits, after(dconv, a), x_edge, z_edge, cotangent, kernel,
+    )
+    a = doubled(after(a, (taps, z_edge)), lines[1])
+    b = doubled(b, over_y)
+    taps = exchanged(taps, [over_x, over_y])
     (layer_out,) = call(
         functools.partial(layer_kernel, plan), (shape(frames.shape, BF),), [here],
-        10, *home, after(frames, a[0]), weights,
-    )
-    a = [doubled(t, over_y) for t in a]
-    a = [doubled(t, over_x) for t in a]
-    b = [doubled(t, lines[0]) for t in b]
-    *a, b[-1], frame_grad, layer_out = lax.optimization_barrier(
-        (*a, b[-1], frame_grad, layer_out)
-    )
-    other = [swap(t, over_core) for t in a + b]
+        10, *home, after(frames, a), weights,
+    )
+    a = doubled(a, over_y)
+    b = doubled(after(b, taps), over_x)
+    taps = exchanged(taps, [over_core])
 
     norm = 1.0 / math.sqrt(groups * count * blocks * length)
     square = shape((width, width), F32)
-    scratch = [pltpu.VMEM((2, width, width), F32), pltpu.SemaphoreType.DMA((2,))]
-    final = functools.partial(final_kernel, (width, norm))
-    *grads, kernel_grad = call(
-        functools.partial(final, True), (square,) * 4 + (shape((31, width), F32),), scratch,
-        8, bits, *a, *b, taps, hbm_outs=range(4),
-    )
-    first = 1 + 2 * CHAINS
-    grads = call(
-        functools.partial(final, False), (square,) * 4, scratch,
-        8, bits, *other, *grads, hbm=range(first, first + 4), hbm_outs=range(4),
-        aliases={first + i: i for i in range(4)},
+
+    def final(kinds, parts, grads):
+        first = 1 + len(parts)
+        return call(
+            functools.partial(final_kernel, (kinds, not grads, width, norm)), (square,) * 4,
+            [
+                pltpu.VMEM((4 * len(parts), part // 8, LANES), F32),
+                pltpu.SemaphoreType.DMA((4 * len(parts),)),
+            ],
+            10, bits, *parts, *grads, hbm=range(first, first + len(grads)), hbm_outs=range(4),
+            aliases={first + i: i for i in range(len(grads))},
+        )
+
+    a_far, b_far = swap(a, over_x), swap(b, lines[0])
+    a_other, b_other = swap(a, over_core), swap(b, over_core)
+    grads = final(
+        ((1, 0, 0), (1, 1, 0), (0, 0, 0), (0, 1, 0)), (a, b, a_other, b_other), ()
+    )
+    a_far, b_far, taps, frame_grad, layer_out, *grads = lax.optimization_barrier(
+        (a_far, b_far, taps, frame_grad, layer_out, *grads)
+    )
+    a_other, b_other = swap(a_far, over_core), swap(b_far, over_core)
+    grads = final(((1, 0, 1), (1, 1, 1)), (a_far, b_far), grads)
+    grads = final(((0, 0, 1), (0, 1, 1)), (a_other, b_other), grads)
+    (kernel_grad,) = call(
+        functools.partial(tap_grad_kernel, norm), (shape((31, width), F32),), [], 4, taps
     )
     return (layer_out, frame_grad, kernel_grad, *grads)
 

time: 105 us -> 94 us (0.90)
  starting transfers between devices: 50.8 us -> 43.5 us
  waiting for transfers between devices: 26.3 us -> 21.2 us
  local copies, waits for them, and re-layouts: 1.86 us -> 3.73 us
    ppermute x49 -> x37, starting transfers between devices: 50.8 us -> 43.5 us  [permute(): return lax.ppermute(x, ('mic', 'tm'), pairs)]
    ppermute x49 -> x37, waiting for transfers between devices: 26.3 us -> 21.2 us  [permute(): return lax.ppermute(x, ('mic', 'tm'), pairs)]
    pallas_call x9 -> x10, Pallas kernels: 21.7 us -> 21.9 us  [call(): pl.pallas_call(body, out_shape=outs, in_specs=[pl.BlockSpec(memory_space=...]
  transfers between devices with their start and end apart: 49 -> 37, of which waited for: 16 -> 15; matrix products, arithmetic and copies ran while one was open for 3% -> 4% of each run, Pallas kernels for 13% -> 15%
where the time goes in v8:
time: 94 us; the launch traced here: 93.7 us
  starting transfers between devices  43.5 us (46%)
  Pallas kernels  21.9 us (23%)
  waiting for transfers between devices  21.2 us (23%)
  local copies, waits for them, and re-layouts  3.73 us (4%)
  other arithmetic  2.34 us (2%)
  between operations  0.95 us (1%)
    ppermute x37, starting transfers between devices, permute(): return lax.ppermute(x, ('mic', 'tm'), pairs)  43.5 us
    pallas_call x10, Pallas kernels, call(): pl.pallas_call(body, out_shape=outs, in_specs=[pl.BlockSpec(memory_space=...  21.9 us
    ppermute x37, waiting for transfers between devices, permute(): return lax.ppermute(x, ('mic', 'tm'), pairs)  21.2 us
  transfers between devices with their start and end apart: 37, of which 15 were waited for; matrix products, arithmetic and copies ran while one was open for 4% of the time, Pallas kernels for 15%

profile of v8, /device:TPU:0, one launch (start us, length us, event | category | flops | bytes accessed | tf_op | source)
XLA Modules:
  0.0 93.7 jit_solution(5948863446148860046)
XLA Ops:
  0.7 1.0 %constant_dynamic-slice_fusion = (bf16[2,32,512]{2,1,0:T(8,128)(2,1)S(1)}, bf16[2,32,512]{2,1,0:T(8,128)(2,1)S(1)}, bf16[2,32,512]{2,1,0:T(8,128)(2,1)S(1)}, bf16[2,32,512]{2,1,0:T(8,128)(2,1)S(1)}) fusion(bf16[2,128,512]{2,1,0:T(8,128)(2,1)} %cot.1, s32[]{:T(128)S(6)} %select_n.59, s32[]{:T(128)S(6)} %select_n.58, s32[]{:T(128)S(6)} %select_n.57, ...), kind=kLoop, calls=%fused_computation.25 | loop fusion | bytes 524304 | tf_op jit(solution)/shard_map/dynamic_slice | solution.py:375
  2.1 0.8 constant_dynamic-slice_fusion.4
  2.9 2.5 %collective-permute-start = (bf16[2,16,512]{2,1,0:T(8,128)(2,1)S(1)}, bf16[2,16,512]{2,1,0:T(8,128)(2,1)S(1)}, u32[]{:S(2)}, u32[]{:S(2)}) collective-permute-start(bf16[2,16,512]{2,1,0:T(8,128)(2,1)S(1)} %get-tuple-element.104), channel_id=1, source_target_pairs={{0,1},{1,0},{2,3},{3,2},{4,5},{5,4},{6,7},{7,6},{8,9},{9,8},{10,11... | collective-permute-start | bytes 98312 | tf_op jit(solution)/shard_map/ppermute | solution.py:354
  5.5 0.7 collective-permute-start.1
  6.1 1.6 %collective-permute-start.6 = (bf16[2,32,512]{2,1,0:T(8,128)(2,1)S(1)}, bf16[2,32,512]{2,1,0:T(8,128)(2,1)S(1)}, u32[]{:S(2)}, u32[]{:S(2)}) collective-permute-start(bf16[2,32,512]{2,1,0:T(8,128)(2,1)S(1)} %get-tuple-element.100), channel_id=1, source_target_pairs={{0,16},{1,17},{2,18},{3,19},{4,20},{5,21},{6,22},{7,23},{8,24},{9,... | collective-permute-start | bytes 196616 | tf_op jit(solution)/shard_map/ppermute | solution.py:354
  7.8 0.9 %copy-done = bf16[2,128,512]{2,1,0:T(8,128)(2,1)S(1)} copy-done((bf16[2,128,512]{2,1,0:T(8,128)(2,1)S(1)}, bf16[2,128,512]{2,1,0:T(8,128)(2,1)}, u32[]{:S(2)}) %copy-start) | copy-done | bytes 262168
  8.8 0.8 copy-done.3
  9.6 2.2 %shard_map.126 = (f32[2,128,512]{2,1,0:T(8,128)S(1)}, bf16[2,32,512]{2,1,0:T(8,128)(2,1)S(1)}, bf16[2,32,512]{2,1,0:T(8,128)(2,1)S(1)}, bf16[2,32,512]{2,1,0:T(8,128)(2,1)S(1)}, bf16[2,32,512]{2,1,0:T(8,128)(2,1)S(1)}) custom-call(s32[9]{0:T(128)S(1)} %stack.54.bits, bf16[2,128,512]{2,1,0:T(8,128)(2,1)S(1)} %copy-done, ...), custom_call_target="tpu_custom_call" | custom-call | tf_op jit(solution)/shard_map/pallas_call | solution.py:319
  11.9 0.7 collective-permute-start.2
  12.5 1.5 %collective-permute-start.3 = (bf16[2,32,512]{2,1,0:T(8,128)(2,1)S(1)}, bf16[2,32,512]{2,1,0:T(8,128)(2,1)S(1)}, u32[]{:S(2)}, u32[]{:S(2)}) collective-permute-start(bf16[2,32,512]{2,1,0:T(8,128)(2,1)S(1)} %get-tuple-element.56), channel_id=1, source_target_pairs={{0,16},{1,17},{2,18},{3,19},{4,20},{5,21},{6,22},{7,23},{8,24},{9,... | collective-permute-start | bytes 196616 | tf_op jit(solution)/shard_map/ppermute | solution.py:354
  14.1 1.8 %pad_maximum_fusion.weights = bf16[4,512,512]{2,1,0:T(8,128)(2,1)S(1)} fusion(bf16[1,512,512]{2,1,0:T(8,128)(2,1)} %bitcast.13, bf16[1,512,512]{2,1,0:T(8,128)(2,1)} %bitcast.14, bf16[1,512,512]{2,1,0:T(8,128)(2,1)} %bitcast.15, bf16[1,512,512]{2,1,0:T(8,128)(2,1)} %bitcast.16), kind=kLoop, calls=%fused_computation | loop fusion | flops 3145728 | bytes 4194304 | tf_op jit(solution)/shard_map/stack | solution.py:387
  15.9 0.9 collective-permute-done.3.a2
  16.8 1.6 %collective-permute-done.4.a3 = bf16[2,32,512]{2,1,0:T(8,128)(2,1)S(1)} collective-permute-done((bf16[2,32,512]{2,1,0:T(8,128)(2,1)S(1)}, bf16[2,32,512]{2,1,0:T(8,128)(2,1)S(1)}, u32[]{:S(2)}, u32[]{:S(2)}) %collective-permute-start.4) | collective-permute-done | bytes 65568 | tf_op jit(solution)/shard_map/ppermute | solution.py:354
  18.4 5.8 %shard_map.127 = (bf16[2048,128]{1,0:T(8,128)(2,1)S(1)}, bf16[2048,128]{1,0:T(8,128)(2,1)S(1)}, bf16[2048,128]{1,0:T(8,128)(2,1)S(1)}, bf16[2048,128]{1,0:T(8,12...) custom-call(s32[9]{0:T(128)S(1)} %stack.54.bits, ...), custom_call_target="tpu_custom_call" | custom-call | tf_op jit(solution)/shard_map/pallas_call | solution.py:319
  25.0 2.4 %collective-permute-done.13.core_got = bf16[1024,128]{1,0:T(8,128)(2,1)S(1)} collective-permute-done((bf16[1024,128]{1,0:T(8,128)(2,1)S(1)}, bf16[1024,128]{1,0:T(8,128)(2,1)S(1)}, u32[]{:S(2)}, u32[]{:S(2)}) %collective-permute-start.13) | collective-permute-done | bytes 262176 | tf_op jit(solution)/shard_map/ppermute | solution.py:354
  27.5 4.1 %collective-permute-start.9 = (bf16[1024,128]{1,0:T(8,128)(2,1)S(1)}, bf16[1024,128]{1,0:T(8,128)(2,1)S(1)}, u32[]{:S(2)}, u32[]{:S(2)}) collective-permute-start(bf16[1024,128]{1,0:T(8,128)(2,1)S(1)} %add_convert_fusion.1), channel_id=1, source_target_pairs={{0,1},{1,0},{2,3},{3,2},{4,5},{5,4},{6,7},{7,6},{8,9},{9,8},{10,11... | collective-permute-start | bytes 786440 | tf_op jit(solution)/shard_map/ppermute | solution.py:354
  31.7 1.6 %collective-permute-start.16 = (bf16[1024,128]{1,0:T(8,128)(2,1)S(1)}, bf16[1024,128]{1,0:T(8,128)(2,1)S(1)}, u32[]{:S(2)}, u32[]{:S(2)}) collective-permute-start(bf16[1024,128]{1,0:T(8,128)(2,1)S(1)} %add_convert_fusion), channel_id=1, source_target_pairs={{0,2},{1,3},{2,0},{3,1},{4,6},{5,7},{6,4},{7,5},{8,10},{9,11},{10,... | collective-permute-start | bytes 786440 | tf_op jit(solution)/shard_map/ppermute | solution.py:354
  33.3 1.4 %collective-permute-start.14 = (bf16[1024,128]{1,0:T(8,128)(2,1)S(1)}, bf16[1024,128]{1,0:T(8,128)(2,1)S(1)}, u32[]{:S(2)}, u32[]{:S(2)}) collective-permute-start(bf16[1024,128]{1,0:T(8,128)(2,1)S(1)} %pad_maximum_fusion.1), channel_id=1, source_target_pairs={{0,16},{1,17},{2,18},{3,19},{4,20},{5,21},{6,22},{7,23},{8,24},{9,... | collective-permute-start | bytes 786440 | tf_op jit(solution)/shard_map/ppermute | solution.py:354
  34.7 3.5 %collective-permute-done.9 = bf16[1024,128]{1,0:T(8,128)(2,1)S(1)} collective-permute-done((bf16[1024,128]{1,0:T(8,128)(2,1)S(1)}, bf16[1024,128]{1,0:T(8,128)(2,1)S(1)}, u32[]{:S(2)}, u32[]{:S(2)}) %collective-permute-start.9) | collective-permute-done | bytes 262176 | tf_op jit(solution)/shard_map/ppermute | solution.py:354
  38.3 1.5 %collective-permute-start.10 = (bf16[512,128]{1,0:T(8,128)(2,1)S(1)}, bf16[512,128]{1,0:T(8,128)(2,1)S(1)}, u32[]{:S(2)}, u32[]{:S(2)}) collective-permute-start(bf16[512,128]{1,0:T(8,128)(2,1)S(1)} %add_convert_fusion.3), channel_id=1, source_target_pairs={{0,16},{1,17},{2,18},{3,19},{4,20},{5,21},{6,22},{7,23},{8,24},{9,... | collective-permute-start | bytes 393224 | tf_op jit(solution)/shard_map/ppermute | solution.py:354
  39.9 1.8 %collective-permute-start.23 = (bf16[512,128]{1,0:T(8,128)(2,1)S(1)}, bf16[512,128]{1,0:T(8,128)(2,1)S(1)}, u32[]{:S(2)}, u32[]{:S(2)}) collective-permute-start(bf16[512,128]{1,0:T(8,128)(2,1)S(1)} %add_convert_fusion.2), channel_id=1, source_target_pairs={{0,1},{1,0},{2,3},{3,2},{4,5},{5,4},{6,7},{7,6},{8,9},{9,8},{10,11... | collective-permute-start | bytes 393224 | tf_op jit(solution)/shard_map/ppermute | solution.py:354
  41.7 0.7 shard_map.128
  42.5 0.7 collective-permute-start.19
  43.2 4.3 %collective-permute-start.32 = (bf16[2,16,512]{2,1,0:T(8,128)(2,1)S(1)}, bf16[2,16,512]{2,1,0:T(8,128)(2,1)S(1)}, u32[]{:S(2)}, u32[]{:S(2)}) collective-permute-start(bf16[2,16,512]{2,1,0:T(8,128)(2,1)S(1)} %get-tuple-element.76), channel_id=1, source_target_pairs={{0,1},{1,0},{2,3},{3,2},{4,5},{5,4},{6,7},{7,6},{8,9},{9,8},{10,11... | collective-permute-start | bytes 98312 | tf_op jit(solution)/shard_map/ppermute | solution.py:354
  47.4 2.8 %shard_map.129 = bf16[128,128]{1,0:T(8,128)(2,1)S(1)} custom-call(s32[9]{0:T(128)S(1)} %stack.54.bits, bf16[2,128,512]{2,1,0:T(8,128)(2,1)S(1)} %copy-done.1, bf16[2,16,512]{2,1,0:T(8,128)(2,1)S(1)} %collective-permute-done.x_got, bf16[2,16,512]{2,1,0:T(8,128)(2,1)S(1)} %collective-permute-done.1.z_got, f32[2,128,512]{2,1,0:T(8,128)S(1)} %get-tuple-element.75.dconv), custom_call_target="tpu_custom_call" | custom-call | tf_op jit(solution)/shard_map/pallas_call | solution.py:319
  50.3 1.6 %collective-permute-start.17 = (bf16[128,128]{1,0:T(8,128)(2,1)S(1)}, bf16[128,128]{1,0:T(8,128)(2,1)S(1)}, u32[]{:S(2)}, u32[]{:S(2)}) collective-permute-start(bf16[128,128]{1,0:T(8,128)(2,1)S(1)} %shard_map.129), channel_id=1, source_target_pairs={{0,2},{1,3},{2,0},{3,1},{4,6},{5,7},{6,4},{7,5},{8,10},{9,11},{10,... | collective-permute-start | bytes 98312 | tf_op jit(solution)/shard_map/ppermute | solution.py:354
  52.0 1.3 %collective-permute-start.24 = (bf16[256,128]{1,0:T(8,128)(2,1)S(1)}, bf16[256,128]{1,0:T(8,128)(2,1)S(1)}, u32[]{:S(2)}, u32[]{:S(2)}) collective-permute-start(bf16[256,128]{1,0:T(8,128)(2,1)S(1)} %add_convert_fusion.6), channel_id=1, source_target_pairs={{0,16},{1,17},{2,18},{3,19},{4,20},{5,21},{6,22},{7,23},{8,24},{9,... | collective-permute-start | bytes 196616 | tf_op jit(solution)/shard_map/ppermute | solution.py:354
  53.3 1.0 %collective-permute-done.17 = bf16[128,128]{1,0:T(8,128)(2,1)S(1)} collective-permute-done((bf16[128,128]{1,0:T(8,128)(2,1)S(1)}, bf16[128,128]{1,0:T(8,128)(2,1)S(1)}, u32[]{:S(2)}, u32[]{:S(2)}) %collective-permute-start.17) | collective-permute-done | bytes 32800 | tf_op jit(solution)/shard_map/ppermute | solution.py:354
  54.3 2.4 %collective-permute-start.18 = (bf16[128,128]{1,0:T(8,128)(2,1)S(1)}, bf16[128,128]{1,0:T(8,128)(2,1)S(1)}, u32[]{:S(2)}, u32[]{:S(2)}) collective-permute-start(bf16[128,128]{1,0:T(8,128)(2,1)S(1)} %add_convert_fusion.14), channel_id=1, source_target_pairs={{0,4},{1,5},{2,6},{3,7},{4,0},{5,1},{6,2},{7,3},{8,12},{9,13},{10,... | collective-permute-start | bytes 98312 | tf_op jit(solution)/shard_map/ppermute | solution.py:354
  57.4 2.0 %collective-permute-done.18 = bf16[128,128]{1,0:T(8,128)(2,1)S(1)} collective-permute-done((bf16[128,128]{1,0:T(8,128)(2,1)S(1)}, bf16[128,128]{1,0:T(8,128)(2,1)S(1)}, u32[]{:S(2)}, u32[]{:S(2)}) %collective-permute-start.18) | collective-permute-done | bytes 32800 | tf_op jit(solution)/shard_map/ppermute | solution.py:354
  60.0 2.7 %collective-permute-start.25 = (bf16[256,128]{1,0:T(8,128)(2,1)S(1)}, bf16[256,128]{1,0:T(8,128)(2,1)S(1)}, u32[]{:S(2)}, u32[]{:S(2)}) collective-permute-start(bf16[256,128]{1,0:T(8,128)(2,1)S(1)} %add_convert_fusion.5), channel_id=1, source_target_pairs={{0,4},{1,5},{2,6},{3,7},{4,0},{5,1},{6,2},{7,3},{8,12},{9,13},{10,... | collective-permute-start | bytes 196616 | tf_op jit(solution)/shard_map/ppermute | solution.py:354
  63.1 3.1 %collective-permute-start.12 = (bf16[256,128]{1,0:T(8,128)(2,1)S(1)}, bf16[256,128]{1,0:T(8,128)(2,1)S(1)}, u32[]{:S(2)}, u32[]{:S(2)}) collective-permute-start(bf16[256,128]{1,0:T(8,128)(2,1)S(1)} %add_convert_fusion.8), channel_id=1, source_target_pairs={{0,2},{1,3},{2,0},{3,1},{4,6},{5,7},{6,4},{7,5},{8,10},{9,11},{10,... | collective-permute-start | bytes 196616 | tf_op jit(solution)/shard_map/ppermute | solution.py:354
  66.2 1.0 %collective-permute-start.28 = (bf16[128,128]{1,0:T(8,128)(2,1)S(1)}, bf16[128,128]{1,0:T(8,128)(2,1)S(1)}, u32[]{:S(2)}, u32[]{:S(2)}) collective-permute-start(bf16[128,128]{1,0:T(8,128)(2,1)S(1)} %add_convert_fusion.12), channel_id=1, source_target_pairs={{0,16},{1,17},{2,18},{3,19},{4,20},{5,21},{6,22},{7,23},{8,24},{9,... | collective-permute-start | bytes 98312 | tf_op jit(solution)/shard_map/ppermute | solution.py:354
  67.2 1.1 %collective-permute-start.26 = (bf16[256,128]{1,0:T(8,128)(2,1)S(1)}, bf16[256,128]{1,0:T(8,128)(2,1)S(1)}, u32[]{:S(2)}, u32[]{:S(2)}) collective-permute-start(bf16[256,128]{1,0:T(8,128)(2,1)S(1)} %add_convert_fusion.4), channel_id=1, source_target_pairs={{0,16},{1,17},{2,18},{3,19},{4,20},{5,21},{6,22},{7,23},{8,24},{9,... | collective-permute-start | bytes 196616 | tf_op jit(solution)/shard_map/ppermute | solution.py:354
  68.4 1.5 %collective-permute-start.20 = (bf16[256,128]{1,0:T(8,128)(2,1)S(1)}, bf16[256,128]{1,0:T(8,128)(2,1)S(1)}, u32[]{:S(2)}, u32[]{:S(2)}) collective-permute-start(bf16[256,128]{1,0:T(8,128)(2,1)S(1)} %add_convert_fusion.7), channel_id=1, source_target_pairs={{0,4},{1,5},{2,6},{3,7},{4,0},{5,1},{6,2},{7,3},{8,12},{9,13},{10,... | collective-permute-start | bytes 196616 | tf_op jit(solution)/shard_map/ppermute | solution.py:354
  70.5 1.0 %collective-permute-done.26 = bf16[256,128]{1,0:T(8,128)(2,1)S(1)} collective-permute-done((bf16[256,128]{1,0:T(8,128)(2,1)S(1)}, bf16[256,128]{1,0:T(8,128)(2,1)S(1)}, u32[]{:S(2)}, u32[]{:S(2)}) %collective-permute-start.26) | collective-permute-done | bytes 65568 | tf_op jit(solution)/shard_map/ppermute | solution.py:354
  71.7 2.0 %collective-permute-done.20 = bf16[256,128]{1,0:T(8,128)(2,1)S(1)} collective-permute-done((bf16[256,128]{1,0:T(8,128)(2,1)S(1)}, bf16[256,128]{1,0:T(8,128)(2,1)S(1)}, u32[]{:S(2)}, u32[]{:S(2)}) %collective-permute-start.20) | collective-permute-done | bytes 65568 | tf_op jit(solution)/shard_map/ppermute | solution.py:354
  73.7 1.0 %collective-permute-start.21 = (bf16[512,128]{1,0:T(8,128)(2,1)S(1)}, bf16[512,128]{1,0:T(8,128)(2,1)S(1)}, u32[]{:S(2)}, u32[]{:S(2)}) collective-permute-start(bf16[512,128]{1,0:T(8,128)(2,1)S(1)} %get-tuple-element.105), channel_id=1, source_target_pairs={{0,16},{1,17},{2,18},{3,19},{4,20},{5,21},{6,22},{7,23},{8,24},{9,... | collective-permute-start | bytes 393224 | tf_op jit(solution)/shard_map/ppermute | solution.py:354
  74.7 1.9 %collective-permute-done.29 = bf16[512,128]{1,0:T(8,128)(2,1)S(1)} collective-permute-done((bf16[512,128]{1,0:T(8,128)(2,1)S(1)}, bf16[512,128]{1,0:T(8,128)(2,1)S(1)}, u32[]{:S(2)}, u32[]{:S(2)}) %collective-permute-start.29) | collective-permute-done | bytes 131104 | tf_op jit(solution)/shard_map/ppermute | solution.py:354
  76.7 2.0 %collective-permute-done.21 = bf16[512,128]{1,0:T(8,128)(2,1)S(1)} collective-permute-done((bf16[512,128]{1,0:T(8,128)(2,1)S(1)}, bf16[512,128]{1,0:T(8,128)(2,1)S(1)}, u32[]{:S(2)}, u32[]{:S(2)}) %collective-permute-start.21) | collective-permute-done | bytes 131104 | tf_op jit(solution)/shard_map/ppermute | solution.py:354
  78.8 2.1 %collective-permute-start.30 = (bf16[1024,128]{1,0:T(8,128)(2,1)S(1)}, bf16[1024,128]{1,0:T(8,128)(2,1)S(1)}, u32[]{:S(2)}, u32[]{:S(2)}) collective-permute-start(bf16[1024,128]{1,0:T(8,128)(2,1)S(1)} %constant_dynamic-update-slice_fusion.5.refs_1_), channel_id=1, source_target_pairs={{0,2},{1,3},{2,0},{3,1},{4,6},{5,7},{6,4},{7,5},{8,10},{9,11},{10,... | collective-permute-start | bytes 786440 | tf_op jit(solution)/shard_map/ppermute | solution.py:354
  81.1 2.8 %shard_map.130 = bf16[2,128,512]{2,1,0:T(8,128)(2,1)} custom-call(s32[9]{0:T(128)S(1)} %stack.54.bits, f32[2,128,512]{2,1,0:T(8,128)S(1)} %get-tuple-element.75.dconv, bf16[2,16,512]{2,1,0:T(8,128)(2,1)S(1)} %collective-permute-done.32.x_got, bf16[2,16,512]{2,1,0:T(8,128)(2,1)S(1)} %collective-permute-done.19.z_got, bf16[2,128,512]{2,1,0:T(8,128)(2,1)S(1)} %copy-done.2, ...), custom_call_target="tpu_custom_call" | custom-call | tf_op jit(solution)/shard_map/pallas_call | solution.py:319
  84.0 1.6 %shard_map.131 = bf16[2,128,512]{2,1,0:T(8,128)(2,1)} custom-call(s32[9]{0:T(128)S(1)} %stack.54.bits, bf16[1024,128]{1,0:T(8,128)(2,1)S(1)} %get-tuple-element.64.own, bf16[1024,128]{1,0:T(8,128)(2,1)S(1)} %collective-permute-done.13.core_got, bf16[1024,128]{1,0:T(8,128)(2,1)S(1)} %collective-permute-done.14.y_got, bf16[2,128,512]{2,1,0:T(8,128)(2,1)S(1)} %copy-done.1, ...), custom_call_target="tpu_custom_call" | custom-call | tf_op jit(solution)/shard_map/pallas_call | solution.py:319
  85.5 2.0 %shard_map.132 = (f32[512,512]{1,0:T(8,128)}, f32[512,512]{1,0:T(8,128)}, f32[512,512]{1,0:T(8,128)}, f32[512,512]{1,0:T(8,128)}) custom-call(s32[9]{0:T(128)S(1)} %stack.54.bits, bf16[1024,128]{1,0:T(8,128)(2,1)S(1)} %constant_dynamic-update-slice_fusion.2.refs_0_, bf16[1024,128]{1,0:T(8,128)(2,1)S(1)} %constant_dynamic-update-slice_fusion.5.refs_1_, ...), custom_call_target="tpu_custom_call" | custom-call | tf_op jit(solution)/shard_map/pallas_call | solution.py:319
  87.8 1.5 %collective-permute-done.22.refs_0_ = bf16[1024,128]{1,0:T(8,128)(2,1)S(1)} collective-permute-done((bf16[1024,128]{1,0:T(8,128)(2,1)S(1)}, bf16[1024,128]{1,0:T(8,128)(2,1)S(1)}, u32[]{:S(2)}, u32[]{:S(2)}) %collective-permute-start.22) | collective-permute-done | bytes 262176 | tf_op jit(solution)/shard_map/ppermute | solution.py:354
  89.8 0.6 shard_map.133
  90.4 1.6 %shard_map.134 = (f32[512,512]{1,0:T(8,128)}, f32[512,512]{1,0:T(8,128)}, f32[512,512]{1,0:T(8,128)}, f32[512,512]{1,0:T(8,128)}) custom-call(s32[9]{0:T(128)S(1)} %stack.54.bits, bf16[1024,128]{1,0:T(8,128)(2,1)S(1)} %collective-permute-done.22.refs_0_, ...), custom_call_target="tpu_custom_call", output_to_operand_aliasing={{0}: (3, {}), {1}: (4, {}), {2}: (5, {}), {3}: (6, {})} | custom-call | tf_op jit(solution)/shard_map/pallas_call | solution.py:319
  92.1 1.6 %shard_map.135 = (f32[512,512]{1,0:T(8,128)}, f32[512,512]{1,0:T(8,128)}, f32[512,512]{1,0:T(8,128)}, f32[512,512]{1,0:T(8,128)}) custom-call(s32[9]{0:T(128)S(1)} %stack.54.bits, bf16[1024,128]{1,0:T(8,128)(2,1)S(1)} %collective-permute-done.35.refs_0_, ...), custom_call_target="tpu_custom_call", output_to_operand_aliasing={{0}: (3, {}), {1}: (4, {}), {2}: (5, {}), {3}: (6, {})} | custom-call | tf_op jit(solution)/shard_map/pallas_call | solution.py:319
  (74 shorter events, 5.5 us)
Async XLA Ops:
  1.6 12.4 %collective-permute-start.5 = (bf16[2,32,512]{2,1,0:T(8,128)(2,1)S(1)}, bf16[2,32,512]{2,1,0:T(8,128)(2,1)S(1)}, u32[]{:S(2)}, u32[]{:S(2)}) collective-permute-start(bf16[2,32,512]{2,1,0:T(8,128)(2,1)S(1)} %get-tuple-element.101), channel_id=1, source_target_pairs={{0,8},{1,9},{2,10},{3,11},{4,12},{5,13},{6,14},{7,15},{8,0},{9,1},... | collective-permute-start | bytes 196616 | tf_op jit(solution)/shard_map/ppermute | solution.py:354
  2.9 4.9 %collective-permute-start = (bf16[2,16,512]{2,1,0:T(8,128)(2,1)S(1)}, bf16[2,16,512]{2,1,0:T(8,128)(2,1)S(1)}, u32[]{:S(2)}, u32[]{:S(2)}) collective-permute-start(bf16[2,16,512]{2,1,0:T(8,128)(2,1)S(1)} %get-tuple-element.104), channel_id=1, source_target_pairs={{0,1},{1,0},{2,3},{3,2},{4,5},{5,4},{6,7},{7,6},{8,9},{9,8},{10,11... | collective-permute-start | bytes 98312 | tf_op jit(solution)/shard_map/ppermute | solution.py:354
  5.5 2.4 %collective-permute-start.1 = (bf16[2,16,512]{2,1,0:T(8,128)(2,1)S(1)}, bf16[2,16,512]{2,1,0:T(8,128)(2,1)S(1)}, u32[]{:S(2)}, u32[]{:S(2)}) collective-permute-start(bf16[2,16,512]{2,1,0:T(8,128)(2,1)S(1)} %get-tuple-element.103), channel_id=1, source_target_pairs={{1,2},{3,4},{5,6},{9,10},{11,12},{13,14},{17,18},{19,20},{21,22},{... | collective-permute-start | bytes 98312 | tf_op jit(solution)/shard_map/ppermute | solution.py:354
  6.1 9.7 %collective-permute-start.6 = (bf16[2,32,512]{2,1,0:T(8,128)(2,1)S(1)}, bf16[2,32,512]{2,1,0:T(8,128)(2,1)S(1)}, u32[]{:S(2)}, u32[]{:S(2)}) collective-permute-start(bf16[2,32,512]{2,1,0:T(8,128)(2,1)S(1)} %get-tuple-element.100), channel_id=1, source_target_pairs={{0,16},{1,17},{2,18},{3,19},{4,20},{5,21},{6,22},{7,23},{8,24},{9,... | collective-permute-start | bytes 196616 | tf_op jit(solution)/shard_map/ppermute | solution.py:354
  7.7 8.2 %collective-permute-start.7 = (bf16[2,32,512]{2,1,0:T(8,128)(2,1)S(1)}, bf16[2,32,512]{2,1,0:T(8,128)(2,1)S(1)}, u32[]{:S(2)}, u32[]{:S(2)}) collective-permute-start(bf16[2,32,512]{2,1,0:T(8,128)(2,1)S(1)} %get-tuple-element.99), channel_id=1, source_target_pairs={{0,24},{1,25},{2,26},{3,27},{4,28},{5,29},{6,30},{7,31},{8,16},{9,... | collective-permute-start | bytes 196616 | tf_op jit(solution)/shard_map/ppermute | solution.py:354
  7.8 1.0 %copy-start = (bf16[2,128,512]{2,1,0:T(8,128)(2,1)S(1)}, bf16[2,128,512]{2,1,0:T(8,128)(2,1)}, u32[]{:S(2)}) copy-start(bf16[2,128,512]{2,1,0:T(8,128)(2,1)} %frames.4) | copy-start | bytes 786436
  8.8 0.8 copy-start.3
  11.9 4.0 %collective-permute-start.2 = (bf16[2,32,512]{2,1,0:T(8,128)(2,1)S(1)}, bf16[2,32,512]{2,1,0:T(8,128)(2,1)S(1)}, u32[]{:S(2)}, u32[]{:S(2)}) collective-permute-start(bf16[2,32,512]{2,1,0:T(8,128)(2,1)S(1)} %get-tuple-element.55), channel_id=1, source_target_pairs={{0,8},{1,9},{2,10},{3,11},{4,12},{5,13},{6,14},{7,15},{8,0},{9,1},... | collective-permute-start | bytes 196616 | tf_op jit(solution)/shard_map/ppermute | solution.py:354
  12.5 4.3 %collective-permute-start.3 = (bf16[2,32,512]{2,1,0:T(8,128)(2,1)S(1)}, bf16[2,32,512]{2,1,0:T(8,128)(2,1)S(1)}, u32[]{:S(2)}, u32[]{:S(2)}) collective-permute-start(bf16[2,32,512]{2,1,0:T(8,128)(2,1)S(1)} %get-tuple-element.56), channel_id=1, source_target_pairs={{0,16},{1,17},{2,18},{3,19},{4,20},{5,21},{6,22},{7,23},{8,24},{9,... | collective-permute-start | bytes 196616 | tf_op jit(solution)/shard_map/ppermute | solution.py:354
  14.1 4.4 %collective-permute-start.4 = (bf16[2,32,512]{2,1,0:T(8,128)(2,1)S(1)}, bf16[2,32,512]{2,1,0:T(8,128)(2,1)S(1)}, u32[]{:S(2)}, u32[]{:S(2)}) collective-permute-start(bf16[2,32,512]{2,1,0:T(8,128)(2,1)S(1)} %get-tuple-element.57), channel_id=1, source_target_pairs={{0,24},{1,25},{2,26},{3,27},{4,28},{5,29},{6,30},{7,31},{8,16},{9,... | collective-permute-start | bytes 196616 | tf_op jit(solution)/shard_map/ppermute | solution.py:354
  24.3 3.1 %collective-permute-start.8 = (bf16[2048,128]{1,0:T(8,128)(2,1)S(1)}, bf16[2048,128]{1,0:T(8,128)(2,1)S(1)}, u32[]{:S(2)}, u32[]{:S(2)}) collective-permute-start(bf16[2048,128]{1,0:T(8,128)(2,1)S(1)} %get-tuple-element.63), channel_id=1, source_target_pairs={{0,8},{1,9},{2,10},{3,11},{4,12},{5,13},{6,14},{7,15},{8,0},{9,1},... | collective-permute-start | bytes 1572872 | tf_op jit(solution)/shard_map/ppermute | solution.py:354
  24.4 7.1 %collective-permute-start.15 = (bf16[2048,128]{1,0:T(8,128)(2,1)S(1)}, bf16[2048,128]{1,0:T(8,128)(2,1)S(1)}, u32[]{:S(2)}, u32[]{:S(2)}) collective-permute-start(bf16[2048,128]{1,0:T(8,128)(2,1)S(1)} %get-tuple-element.67), channel_id=1, source_target_pairs={{0,8},{1,9},{2,10},{3,11},{4,12},{5,13},{6,14},{7,15},{8,0},{9,1},... | collective-permute-start | bytes 1572872 | tf_op jit(solution)/shard_map/ppermute | solution.py:354
  24.9 2.5 %collective-permute-start.13 = (bf16[1024,128]{1,0:T(8,128)(2,1)S(1)}, bf16[1024,128]{1,0:T(8,128)(2,1)S(1)}, u32[]{:S(2)}, u32[]{:S(2)}) collective-permute-start(bf16[1024,128]{1,0:T(8,128)(2,1)S(1)} %get-tuple-element.65), channel_id=1, source_target_pairs={{0,8},{1,9},{2,10},{3,11},{4,12},{5,13},{6,14},{7,15},{8,0},{9,1},... | collective-permute-start | bytes 786440 | tf_op jit(solution)/shard_map/ppermute | solution.py:354
  27.4 20.0 %copy-start.1 = (bf16[2,128,512]{2,1,0:T(8,128)(2,1)S(1)}, bf16[2,128,512]{2,1,0:T(8,128)(2,1)}, u32[]{:S(2)}) copy-start(bf16[2,128,512]{2,1,0:T(8,128)(2,1)} %frames.4) | copy-start | bytes 786436
  27.5 10.7 %collective-permute-start.9 = (bf16[1024,128]{1,0:T(8,128)(2,1)S(1)}, bf16[1024,128]{1,0:T(8,128)(2,1)S(1)}, u32[]{:S(2)}, u32[]{:S(2)}) collective-permute-start(bf16[1024,128]{1,0:T(8,128)(2,1)S(1)} %add_convert_fusion.1), channel_id=1, source_target_pairs={{0,1},{1,0},{2,3},{3,2},{4,5},{5,4},{6,7},{7,6},{8,9},{9,8},{10,11... | collective-permute-start | bytes 786440 | tf_op jit(solution)/shard_map/ppermute | solution.py:354
  31.7 8.2 %collective-permute-start.16 = (bf16[1024,128]{1,0:T(8,128)(2,1)S(1)}, bf16[1024,128]{1,0:T(8,128)(2,1)S(1)}, u32[]{:S(2)}, u32[]{:S(2)}) collective-permute-start(bf16[1024,128]{1,0:T(8,128)(2,1)S(1)} %add_convert_fusion), channel_id=1, source_target_pairs={{0,2},{1,3},{2,0},{3,1},{4,6},{5,7},{6,4},{7,5},{8,10},{9,11},{10,... | collective-permute-start | bytes 786440 | tf_op jit(solution)/shard_map/ppermute | solution.py:354
  33.3 8.4 %collective-permute-start.14 = (bf16[1024,128]{1,0:T(8,128)(2,1)S(1)}, bf16[1024,128]{1,0:T(8,128)(2,1)S(1)}, u32[]{:S(2)}, u32[]{:S(2)}) collective-permute-start(bf16[1024,128]{1,0:T(8,128)(2,1)S(1)} %pad_maximum_fusion.1), channel_id=1, source_target_pairs={{0,16},{1,17},{2,18},{3,19},{4,20},{5,21},{6,22},{7,23},{8,24},{9,... | collective-permute-start | bytes 786440 | tf_op jit(solution)/shard_map/ppermute | solution.py:354
  38.3 9.2 %collective-permute-start.10 = (bf16[512,128]{1,0:T(8,128)(2,1)S(1)}, bf16[512,128]{1,0:T(8,128)(2,1)S(1)}, u32[]{:S(2)}, u32[]{:S(2)}) collective-permute-start(bf16[512,128]{1,0:T(8,128)(2,1)S(1)} %add_convert_fusion.3), channel_id=1, source_target_pairs={{0,16},{1,17},{2,18},{3,19},{4,20},{5,21},{6,22},{7,23},{8,24},{9,... | collective-permute-start | bytes 393224 | tf_op jit(solution)/shard_map/ppermute | solution.py:354
  39.9 12.0 %collective-permute-start.23 = (bf16[512,128]{1,0:T(8,128)(2,1)S(1)}, bf16[512,128]{1,0:T(8,128)(2,1)S(1)}, u32[]{:S(2)}, u32[]{:S(2)}) collective-permute-start(bf16[512,128]{1,0:T(8,128)(2,1)S(1)} %add_convert_fusion.2), channel_id=1, source_target_pairs={{0,1},{1,0},{2,3},{3,2},{4,5},{5,4},{6,7},{7,6},{8,9},{9,8},{10,11... | collective-permute-start | bytes 393224 | tf_op jit(solution)/shard_map/ppermute | solution.py:354
  42.5 25.9 %collective-permute-start.19 = (bf16[2,16,512]{2,1,0:T(8,128)(2,1)S(1)}, bf16[2,16,512]{2,1,0:T(8,128)(2,1)S(1)}, u32[]{:S(2)}, u32[]{:S(2)}) collective-permute-start(bf16[2,16,512]{2,1,0:T(8,128)(2,1)S(1)} %get-tuple-element.72), channel_id=1, source_target_pairs={{1,2},{3,4},{5,6},{9,10},{11,12},{13,14},{17,18},{19,20},{21,22},{... | collective-permute-start | bytes 98312 | tf_op jit(solution)/shard_map/ppermute | solution.py:354
  43.2 37.8 %collective-permute-start.32 = (bf16[2,16,512]{2,1,0:T(8,128)(2,1)S(1)}, bf16[2,16,512]{2,1,0:T(8,128)(2,1)S(1)}, u32[]{:S(2)}, u32[]{:S(2)}) collective-permute-start(bf16[2,16,512]{2,1,0:T(8,128)(2,1)S(1)} %get-tuple-element.76), channel_id=1, source_target_pairs={{0,1},{1,0},{2,3},{3,2},{4,5},{5,4},{6,7},{7,6},{8,9},{9,8},{10,11... | collective-permute-start | bytes 98312 | tf_op jit(solution)/shard_map/ppermute | solution.py:354
  47.4 33.7 %copy-start.2 = (bf16[2,128,512]{2,1,0:T(8,128)(2,1)S(1)}, bf16[2,128,512]{2,1,0:T(8,128)(2,1)}, u32[]{:S(2)}) copy-start(bf16[2,128,512]{2,1,0:T(8,128)(2,1)} %cot.1) | copy-start | bytes 786436
  47.4 33.7 %copy-start.4 = (f32[31,512]{1,0:T(8,128)S(1)}, f32[31,512]{1,0:T(8,128)}, u32[]{:S(2)}) copy-start(f32[31,512]{1,0:T(8,128)} %kern.3) | copy-start | bytes 190468
  50.3 4.0 %collective-permute-start.17 = (bf16[128,128]{1,0:T(8,128)(2,1)S(1)}, bf16[128,128]{1,0:T(8,128)(2,1)S(1)}, u32[]{:S(2)}, u32[]{:S(2)}) collective-permute-start(bf16[128,128]{1,0:T(8,128)(2,1)S(1)} %shard_map.129), channel_id=1, source_target_pairs={{0,2},{1,3},{2,0},{3,1},{4,6},{5,7},{6,4},{7,5},{8,10},{9,11},{10,... | collective-permute-start | bytes 98312 | tf_op jit(solution)/shard_map/ppermute | solution.py:354
  52.0 8.0 %collective-permute-start.24 = (bf16[256,128]{1,0:T(8,128)(2,1)S(1)}, bf16[256,128]{1,0:T(8,128)(2,1)S(1)}, u32[]{:S(2)}, u32[]{:S(2)}) collective-permute-start(bf16[256,128]{1,0:T(8,128)(2,1)S(1)} %add_convert_fusion.6), channel_id=1, source_target_pairs={{0,16},{1,17},{2,18},{3,19},{4,20},{5,21},{6,22},{7,23},{8,24},{9,... | collective-permute-start | bytes 196616 | tf_op jit(solution)/shard_map/ppermute | solution.py:354
  54.3 5.0 %collective-permute-start.18 = (bf16[128,128]{1,0:T(8,128)(2,1)S(1)}, bf16[128,128]{1,0:T(8,128)(2,1)S(1)}, u32[]{:S(2)}, u32[]{:S(2)}) collective-permute-start(bf16[128,128]{1,0:T(8,128)(2,1)S(1)} %add_convert_fusion.14), channel_id=1, source_target_pairs={{0,4},{1,5},{2,6},{3,7},{4,0},{5,1},{6,2},{7,3},{8,12},{9,13},{10,... | collective-permute-start | bytes 98312 | tf_op jit(solution)/shard_map/ppermute | solution.py:354
  56.8 6.2 %collective-permute-start.11 = (bf16[256,128]{1,0:T(8,128)(2,1)S(1)}, bf16[256,128]{1,0:T(8,128)(2,1)S(1)}, u32[]{:S(2)}, u32[]{:S(2)}) collective-permute-start(bf16[256,128]{1,0:T(8,128)(2,1)S(1)} %add_convert_fusion.9), channel_id=1, source_target_pairs={{0,4},{1,5},{2,6},{3,7},{4,0},{5,1},{6,2},{7,3},{8,12},{9,13},{10,... | collective-permute-start | bytes 196616 | tf_op jit(solution)/shard_map/ppermute | solution.py:354
  59.3 6.8 %collective-permute-start.27 = (bf16[128,128]{1,0:T(8,128)(2,1)S(1)}, bf16[128,128]{1,0:T(8,128)(2,1)S(1)}, u32[]{:S(2)}, u32[]{:S(2)}) collective-permute-start(bf16[128,128]{1,0:T(8,128)(2,1)S(1)} %add_convert_fusion.13), channel_id=1, source_target_pairs={{0,1},{1,0},{2,3},{3,2},{4,5},{5,4},{6,7},{7,6},{8,9},{9,8},{10,11... | collective-permute-start | bytes 98312 | tf_op jit(solution)/shard_map/ppermute | solution.py:354
  60.0 7.2 %collective-permute-start.25 = (bf16[256,128]{1,0:T(8,128)(2,1)S(1)}, bf16[256,128]{1,0:T(8,128)(2,1)S(1)}, u32[]{:S(2)}, u32[]{:S(2)}) collective-permute-start(bf16[256,128]{1,0:T(8,128)(2,1)S(1)} %add_convert_fusion.5), channel_id=1, source_target_pairs={{0,4},{1,5},{2,6},{3,7},{4,0},{5,1},{6,2},{7,3},{8,12},{9,13},{10,... | collective-permute-start | bytes 196616 | tf_op jit(solution)/shard_map/ppermute | solution.py:354
  63.1 5.3 %collective-permute-start.12 = (bf16[256,128]{1,0:T(8,128)(2,1)S(1)}, bf16[256,128]{1,0:T(8,128)(2,1)S(1)}, u32[]{:S(2)}, u32[]{:S(2)}) collective-permute-start(bf16[256,128]{1,0:T(8,128)(2,1)S(1)} %add_convert_fusion.8), channel_id=1, source_target_pairs={{0,2},{1,3},{2,0},{3,1},{4,6},{5,7},{6,4},{7,5},{8,10},{9,11},{10,... | collective-permute-start | bytes 196616 | tf_op jit(solution)/shard_map/ppermute | solution.py:354
  66.2 4.3 %collective-permute-start.28 = (bf16[128,128]{1,0:T(8,128)(2,1)S(1)}, bf16[128,128]{1,0:T(8,128)(2,1)S(1)}, u32[]{:S(2)}, u32[]{:S(2)}) collective-permute-start(bf16[128,128]{1,0:T(8,128)(2,1)S(1)} %add_convert_fusion.12), channel_id=1, source_target_pairs={{0,16},{1,17},{2,18},{3,19},{4,20},{5,21},{6,22},{7,23},{8,24},{9,... | collective-permute-start | bytes 98312 | tf_op jit(solution)/shard_map/ppermute | solution.py:354
  67.2 4.3 %collective-permute-start.26 = (bf16[256,128]{1,0:T(8,128)(2,1)S(1)}, bf16[256,128]{1,0:T(8,128)(2,1)S(1)}, u32[]{:S(2)}, u32[]{:S(2)}) collective-permute-start(bf16[256,128]{1,0:T(8,128)(2,1)S(1)} %add_convert_fusion.4), channel_id=1, source_target_pairs={{0,16},{1,17},{2,18},{3,19},{4,20},{5,21},{6,22},{7,23},{8,24},{9,... | collective-permute-start | bytes 196616 | tf_op jit(solution)/shard_map/ppermute | solution.py:354
  68.4 5.2 %collective-permute-start.20 = (bf16[256,128]{1,0:T(8,128)(2,1)S(1)}, bf16[256,128]{1,0:T(8,128)(2,1)S(1)}, u32[]{:S(2)}, u32[]{:S(2)}) collective-permute-start(bf16[256,128]{1,0:T(8,128)(2,1)S(1)} %add_convert_fusion.7), channel_id=1, source_target_pairs={{0,4},{1,5},{2,6},{3,7},{4,0},{5,1},{6,2},{7,3},{8,12},{9,13},{10,... | collective-permute-start | bytes 196616 | tf_op jit(solution)/shard_map/ppermute | solution.py:354
  71.6 5.0 %collective-permute-start.29 = (bf16[512,128]{1,0:T(8,128)(2,1)S(1)}, bf16[512,128]{1,0:T(8,128)(2,1)S(1)}, u32[]{:S(2)}, u32[]{:S(2)}) collective-permute-start(bf16[512,128]{1,0:T(8,128)(2,1)S(1)} %pad_maximum_fusion.2), channel_id=1, source_target_pairs={{0,1},{1,0},{2,3},{3,2},{4,5},{5,4},{6,7},{7,6},{8,9},{9,8},{10,11... | collective-permute-start | bytes 393224 | tf_op jit(solution)/shard_map/ppermute | solution.py:354
  73.7 5.0 %collective-permute-start.21 = (bf16[512,128]{1,0:T(8,128)(2,1)S(1)}, bf16[512,128]{1,0:T(8,128)(2,1)S(1)}, u32[]{:S(2)}, u32[]{:S(2)}) collective-permute-start(bf16[512,128]{1,0:T(8,128)(2,1)S(1)} %get-tuple-element.105), channel_id=1, source_target_pairs={{0,16},{1,17},{2,18},{3,19},{4,20},{5,21},{6,22},{7,23},{8,24},{9,... | collective-permute-start | bytes 393224 | tf_op jit(solution)/shard_map/ppermute | solution.py:354
  76.6 8.9 %collective-permute-start.34 = (bf16[1024,128]{1,0:T(8,128)(2,1)S(1)}, bf16[1024,128]{1,0:T(8,128)(2,1)S(1)}, u32[]{:S(2)}, u32[]{:S(2)}) collective-permute-start(bf16[1024,128]{1,0:T(8,128)(2,1)S(1)} %constant_dynamic-update-slice_fusion.5.refs_1_), channel_id=1, source_target_pairs={{0,8},{1,9},{2,10},{3,11},{4,12},{5,13},{6,14},{7,15},{8,0},{9,1},... | collective-permute-start | bytes 786440 | tf_op jit(solution)/shard_map/ppermute | solution.py:354
  78.7 6.8 %collective-permute-start.33 = (bf16[1024,128]{1,0:T(8,128)(2,1)S(1)}, bf16[1024,128]{1,0:T(8,128)(2,1)S(1)}, u32[]{:S(2)}, u32[]{:S(2)}) collective-permute-start(bf16[1024,128]{1,0:T(8,128)(2,1)S(1)} %constant_dynamic-update-slice_fusion.2.refs_0_), channel_id=1, source_target_pairs={{0,8},{1,9},{2,10},{3,11},{4,12},{5,13},{6,14},{7,15},{8,0},{9,1},... | collective-permute-start | bytes 786440 | tf_op jit(solution)/shard_map/ppermute | solution.py:354
  78.8 9.0 %collective-permute-start.30 = (bf16[1024,128]{1,0:T(8,128)(2,1)S(1)}, bf16[1024,128]{1,0:T(8,128)(2,1)S(1)}, u32[]{:S(2)}, u32[]{:S(2)}) collective-permute-start(bf16[1024,128]{1,0:T(8,128)(2,1)S(1)} %constant_dynamic-update-slice_fusion.5.refs_1_), channel_id=1, source_target_pairs={{0,2},{1,3},{2,0},{3,1},{4,6},{5,7},{6,4},{7,5},{8,10},{9,11},{10,... | collective-permute-start | bytes 786440 | tf_op jit(solution)/shard_map/ppermute | solution.py:354
  80.9 8.4 %collective-permute-start.22 = (bf16[1024,128]{1,0:T(8,128)(2,1)S(1)}, bf16[1024,128]{1,0:T(8,128)(2,1)S(1)}, u32[]{:S(2)}, u32[]{:S(2)}) collective-permute-start(bf16[1024,128]{1,0:T(8,128)(2,1)S(1)} %constant_dynamic-update-slice_fusion.2.refs_0_), channel_id=1, source_target_pairs={{0,1},{1,0},{2,3},{3,2},{4,5},{5,4},{6,7},{7,6},{8,9},{9,8},{10,11... | collective-permute-start | bytes 786440 | tf_op jit(solution)/shard_map/ppermute | solution.py:354
  80.9 3.0 %collective-permute-start.31 = (bf16[128,128]{1,0:T(8,128)(2,1)S(1)}, bf16[128,128]{1,0:T(8,128)(2,1)S(1)}, u32[]{:S(2)}, u32[]{:S(2)}) collective-permute-start(bf16[128,128]{1,0:T(8,128)(2,1)S(1)} %add_convert_fusion.11), channel_id=1, source_target_pairs={{0,8},{1,9},{2,10},{3,11},{4,12},{5,13},{6,14},{7,15},{8,0},{9,1},... | collective-permute-start | bytes 98312 | tf_op jit(solution)/shard_map/ppermute | solution.py:354
  89.3 2.7 %collective-permute-start.35 = (bf16[1024,128]{1,0:T(8,128)(2,1)S(1)}, bf16[1024,128]{1,0:T(8,128)(2,1)S(1)}, u32[]{:S(2)}, u32[]{:S(2)}) collective-permute-start(bf16[1024,128]{1,0:T(8,128)(2,1)S(1)} %collective-permute-done.22.refs_0_), channel_id=1, source_target_pairs={{0,8},{1,9},{2,10},{3,11},{4,12},{5,13},{6,14},{7,15},{8,0},{9,1},... | collective-permute-start | bytes 786440 | tf_op jit(solution)/shard_map/ppermute | solution.py:354
  89.3 2.7 %collective-permute-start.36 = (bf16[1024,128]{1,0:T(8,128)(2,1)S(1)}, bf16[1024,128]{1,0:T(8,128)(2,1)S(1)}, u32[]{:S(2)}, u32[]{:S(2)}) collective-permute-start(bf16[1024,128]{1,0:T(8,128)(2,1)S(1)} %collective-permute-done.30.refs_1_), channel_id=1, source_target_pairs={{0,8},{1,9},{2,10},{3,11},{4,12},{5,13},{6,14},{7,15},{8,0},{9,1},... | collective-permute-start | bytes 786440 | tf_op jit(solution)/shard_map/ppermute | solution.py:354

commit v9 on v8

--- a/solution.py
+++ b/solution.py
@@ -48,17 +48,20 @@
     return 0.5 * jnp.tanh(0.5 * v) + 0.5
 
 
-def padded(bits, rows, x_got, z_got, m, lanes):
+def padded(bits, rows, one, two):
     is_odd = jnp.broadcast_to(bits[X], (HALO, LANES)) == 1
-    one, two = x_got[m, :, lanes].astype(F32), z_got[m, :, lanes].astype(F32)
+    one, two = one.astype(F32), two.astype(F32)
     return jnp.concatenate(
-        [
-            jnp.where(is_odd, one, two),
-            rows[m, :, lanes].astype(F32),
-            jnp.where(is_odd, two, one),
-        ],
-        axis=0,
-    )
+        [jnp.where(is_odd, one, two), rows.astype(F32), jnp.where(is_odd, two, one)], axis=0
+    )
+
+
+def near_edge(bits):
+    return pl.ds(pl.multiple_of(bits[X] * HALO, HALO), HALO)
+
+
+def padded_frames(bits, frames, x_got, z_got, m, lanes):
+    return padded(bits, frames[m, :, lanes], x_got[m, near_edge(bits), lanes], z_got[m, :, lanes])
 
 
 def lanes_of(width):
@@ -72,7 +75,7 @@
 
     def step(m, _):
         for lanes in lanes_of(width):
-            x = padded(bits, frames, x_got, z_got, m, lanes)
+            x = padded_frames(bits, frames, x_got, z_got, m, lanes)
             for at in (0, half):
                 conv = window(
                     x[at : at + half + 2 * HALO], lambda o: kern[o - 1 : o, lanes], half
@@ -204,9 +207,12 @@
     cols = width // LANES
     size = cols * width // 8
     got, refs = refs[: len(kinds)], refs[len(kinds) :]
-    if not first_call:
-        refs = refs[4:]
-    outs, piece_s, sems = refs[:4], refs[4], refs[5]
+    if first_call:
+        taps, *outs, tap_grad, piece_s, sems = refs
+        for lc, lanes in enumerate(lanes_of(width)):
+            tap_grad[:, lanes] = taps[lc * 32 : lc * 32 + 31, :].astype(F32) * norm
+    else:
+        outs, piece_s, sems = refs[4:8], refs[8], refs[9]
     core = bits[CORE]
     copies = []
     for n, (own, h, far) in enumerate(kinds):
@@ -229,11 +235,6 @@
         pl.when(here)(copy.wait)
 
 
-def tap_grad_kernel(norm, taps, grad):
-    for lc, lanes in enumerate(lanes_of(grad.shape[1])):
-        grad[:, lanes] = taps[lc * 32 : lc * 32 + 31, :].astype(F32) * norm
-
-
 def home_chunks(plan, bits, own, core_got, y_got, kind):
     count, sub, cols = plan
     part = count * cols * sub
@@ -247,15 +248,17 @@
                 yield ref[at : at + sub, :], m, to, slice(lc * LANES, (lc + 1) * LANES)
 
 
-def dconv_kernel(plan, bits, own, core_got, y_got, conv_in, dconv, x_edge, z_edge):
+def dconv_kernel(plan, bits, own, core_got, y_got, conv_in, dconv, edges):
     for dacted, m, to, lanes in home_chunks(plan, bits, own, core_got, y_got, 1):
         conv = conv_in[m, to, lanes]
         sig = sigmoid(conv)
         dconv[m, to, lanes] = dacted.astype(F32) * sig * (1.0 + conv * (1.0 - sig))
-    last = dconv.shape[1] - HALO
-    odd = bits[X]
-    x_edge[...] = dconv[:, pl.ds(pl.multiple_of((1 - odd) * last, HALO), HALO), :].astype(BF)
-    z_edge[...] = dconv[:, pl.ds(pl.multiple_of(odd * last, HALO), HALO), :].astype(BF)
+    count, length, width = dconv.shape
+    for m in range(count):
+        for lc, lanes in enumerate(lanes_of(width)):
+            at = (m * plan[2] + lc) * 2 * HALO
+            edges[at : at + HALO, :] = dconv[m, :HALO, lanes].astype(BF)
+            edges[at + HALO : at + 2 * HALO, :] = dconv[m, length - HALO :, lanes].astype(BF)
 
 
 def layer_kernel(plan, bits, own, core_got, y_got, frames, weights, layer_out, mix_s):
@@ -270,7 +273,7 @@
     count, length, width = frames.shape
     for m in range(count):
         for lanes in lanes_of(width):
-            pad_s[m, :, lanes] = padded(bits, frames, x_got, z_got, m, lanes)
+            pad_s[m, :, lanes] = padded_frames(bits, frames, x_got, z_got, m, lanes)
     for lc, lanes in enumerate(lanes_of(width)):
 
         def step(n, accs):
@@ -301,8 +304,11 @@
     half = length // 2
 
     def step(m, _):
-        for lanes in lanes_of(width):
-            x = padded(bits, dconv, x_got, z_got, m, lanes)
+        for lc, lanes in enumerate(lanes_of(width)):
+            n = m * (width // LANES) + lc
+            x_rows = pl.ds(pl.multiple_of((2 * n + bits[X]) * HALO, HALO), HALO)
+            z_rows = pl.ds(pl.multiple_of(n * HALO, HALO), HALO)
+            x = padded(bits, dconv[m, :, lanes], x_got[x_rows, :], z_got[z_rows, :])
             for at in (0, half):
                 part = slice(at, at + half)
                 grad = window(
@@ -356,21 +362,22 @@
     def swap(x, mask):
         return permute(x, [(f, f ^ mask) for f in range(groups * blocks)])
 
-    def swap_edges(x_edge, z_edge):
-        pairs = [(m * blocks + t, m * blocks + t + 1)
-                 for m in range(groups) for t in range(1, blocks - 1, 2)]
-        return swap(x_edge, over_x), permute(z_edge, pairs + [(j, i) for i, j in pairs])
+    def passed_on(x, axis):
+        x = lax.dynamic_slice_in_dim(x, (1 - odd) * HALO, HALO, axis=axis)
+        pairs = [(t, t + 2) if t % 2 == 0 else (t + 2, t) for t in range(blocks - 2)]
+        return permute(
+            x, [(m * blocks + i, m * blocks + j) for m in range(groups) for i, j in pairs]
+        )
 
     def spread(parts):
         masks = (0, over_core, over_y, over_core + over_y)
         got = {d: swap(parts[d], masks[d]) for d in (2, 3, 1)}
         return [parts[0], got[1], got[2], got[3]]
 
-    last = length - HALO
-    frame_x, frame_z = swap_edges(
-        lax.dynamic_slice_in_dim(frames, (1 - odd) * last, HALO, axis=1),
-        lax.dynamic_slice_in_dim(frames, odd * last, HALO, axis=1),
-    )
+    frame_x = swap(
+        jnp.concatenate([frames[:, :HALO], frames[:, length - HALO :]], axis=1), over_x
+    )
+    frame_z = passed_on(frame_x, 1)
     cot_parts = spread(
         [lax.dynamic_slice_in_dim(cotangent, (mic ^ d) * sub, sub, axis=1) for d in range(4)]
     )
@@ -429,11 +436,10 @@
     plan = (count, sub, cols)
     y_got = after(y_got, (a[-1], b[-1]))
     home = (bits, back_keep, core_got, y_got)
-    edge = shape((count, HALO, width), BF)
-    dconv, x_edge, z_edge = call(
-        functools.partial(dconv_kernel, plan), (wide, edge, edge), [], 8, *home, conv
-    )
-    x_edge, z_edge = swap_edges(x_edge, z_edge)
+    dconv, edges = call(
+        functools.partial(dconv_kernel, plan), (wide, flat(2 * count * cols * HALO)), [], 8,
+        *home, conv,
+    )
     a = halved(a, over_y)
     b = halved(b, over_x)
     (taps,) = call(
@@ -441,53 +447,62 @@
         [pltpu.VMEM((count, length + 2 * HALO, width), F32)],
         8, bits, frames, frame_x, frame_z, after(dconv, a[-1]),
     )
-    taps = exchanged(taps, lines)
-    a = exchanged(total(*halved(a, lines[1])), lines[:1] + lines[2:])
+    n = taps.shape[0]
+    got = swap(jnp.concatenate([taps, edges]), over_x)
+    taps, x_edge = total(taps, got[:n]), got[n:]
+    z_edge = passed_on(x_edge.reshape(count * cols, 2 * HALO, LANES), 1).reshape(-1, LANES)
+    k = a[0].shape[0] // 2
+    got = swap(jnp.concatenate([total(*(t[k:] for t in a)), taps]), lines[1])
+    a = total(*(t[:k] for t in a), got[:k])
+    taps = total(taps, got[k:])
+    a = exchanged(jnp.concatenate([a, taps]), lines[:1] + lines[2:])
+    a, taps = a[:k], a[k:]
     b = exchanged(total(*halved(b, over_y)), lines[1:])
+    a = doubled(after(a, z_edge), lines[1])
+    got = swap(jnp.concatenate([b, taps]), over_y)
+    k = b.shape[0]
+    b, taps = jnp.concatenate([b, got[:k]]), total(taps, got[k:])
     (frame_grad,) = call(
         frame_kernel, (shape(frames.shape, BF),), [], 8,
         bits, after(dconv, a), x_edge, z_edge, cotangent, kernel,
     )
-    a = doubled(after(a, (taps, z_edge)), lines[1])
-    b = doubled(b, over_y)
-    taps = exchanged(taps, [over_x, over_y])
     (layer_out,) = call(
         functools.partial(layer_kernel, plan), (shape(frames.shape, BF),), [here],
         10, *home, after(frames, a), weights,
     )
     a = doubled(a, over_y)
-    b = doubled(after(b, taps), over_x)
-    taps = exchanged(taps, [over_core])
+    b = doubled(b, over_x)
 
     norm = 1.0 / math.sqrt(groups * count * blocks * length)
     square = shape((width, width), F32)
 
-    def final(kinds, parts, grads):
+    def final(kinds, parts, grads, taps=()):
         first = 1 + len(parts)
         return call(
-            functools.partial(final_kernel, (kinds, not grads, width, norm)), (square,) * 4,
+            functools.partial(final_kernel, (kinds, not grads, width, norm)),
+            (square,) * 4 + (shape((31, width), F32),) * len(taps),
             [
-                pltpu.VMEM((4 * len(parts), part // 8, LANES), F32),
-                pltpu.SemaphoreType.DMA((4 * len(parts),)),
+                pltpu.VMEM((4 * len(kinds), part // 8, LANES), F32),
+                pltpu.SemaphoreType.DMA((4 * len(kinds),)),
             ],
-            10, bits, *parts, *grads, hbm=range(first, first + len(grads)), hbm_outs=range(4),
-            aliases={first + i: i for i in range(len(grads))},
+            10, bits, *parts, *taps, *grads, hbm=range(first, first + len(grads)),
+            hbm_outs=range(4), aliases={first + i: i for i in range(len(grads))},
         )
 
     a_far, b_far = swap(a, over_x), swap(b, lines[0])
-    a_other, b_other = swap(a, over_core), swap(b, over_core)
-    grads = final(
-        ((1, 0, 0), (1, 1, 0), (0, 0, 0), (0, 1, 0)), (a, b, a_other, b_other), ()
-    )
-    a_far, b_far, taps, frame_grad, layer_out, *grads = lax.optimization_barrier(
-        (a_far, b_far, taps, frame_grad, layer_out, *grads)
+    a_other, b_other = after((jnp.concatenate([a, taps]), b), frame_grad)
+    a_other, b_other = swap(a_other, over_core), swap(b_other, over_core)
+    k = a.shape[0]
+    taps = total(taps, a_other[k:])
+    *grads, kernel_grad = final(
+        ((1, 0, 0), (1, 1, 0), (0, 0, 0), (0, 1, 0)), (a, b, a_other, b_other), (), (taps,)
+    )
+    a_far, b_far, frame_grad, layer_out, *grads = lax.optimization_barrier(
+        (a_far, b_far, frame_grad, layer_out, *grads)
     )
     a_other, b_other = swap(a_far, over_core), swap(b_far, over_core)
     grads = final(((1, 0, 1), (1, 1, 1)), (a_far, b_far), grads)
     grads = final(((0, 0, 1), (0, 1, 1)), (a_other, b_other), grads)
-    (kernel_grad,) = call(
-        functools.partial(tap_grad_kernel, norm), (shape((31, width), F32),), [], 4, taps
-    )
     return (layer_out, frame_grad, kernel_grad, *grads)
 
 

time: 94 us -> 96.5 us (1.027)
  waiting for transfers between devices: 21.2 us -> 25.6 us
  starting transfers between devices: 43.5 us -> 41.5 us
    ppermute x37 -> x32, waiting for transfers between devices: 21.2 us -> 25.6 us  [permute(): return lax.ppermute(x, ('mic', 'tm'), pairs)]
    ppermute x37 -> x32, starting transfers between devices: 43.5 us -> 41.5 us  [permute(): return lax.ppermute(x, ('mic', 'tm'), pairs)]
    pallas_call x10 -> x9, Pallas kernels: 21.9 us -> 21.9 us  [call(): pl.pallas_call(body, out_shape=outs, in_specs=[pl.BlockSpec(memory_space=...]
  transfers between devices with their start and end apart: 37 -> 32, of which waited for: 15 -> 14; matrix products, arithmetic and copies ran while one was open for 4% -> 4% of each run, Pallas kernels for 15% -> 15%
where the time goes in v9:
time: 96.5 us; the launch traced here: 96.1 us
  starting transfers between devices  41.5 us (43%)
  waiting for transfers between devices  25.6 us (27%)
  Pallas kernels  21.9 us (23%)
  local copies, waits for them, and re-layouts  3.72 us (4%)
  other arithmetic  2.42 us (3%)
  between operations  1 us (1%)
    ppermute x32, starting transfers between devices, permute(): return lax.ppermute(x, ('mic', 'tm'), pairs)  41.5 us
    ppermute x32, waiting for transfers between devices, permute(): return lax.ppermute(x, ('mic', 'tm'), pairs)  25.6 us
    pallas_call x9, Pallas kernels, call(): pl.pallas_call(body, out_shape=outs, in_specs=[pl.BlockSpec(memory_space=...  21.9 us
  transfers between devices with their start and end apart: 32, of which 14 were waited for; matrix products, arithmetic and copies ran while one was open for 4% of the time, Pallas kernels for 15%

profile of v9, /device:TPU:0, one launch (start us, length us, event | category | flops | bytes accessed | tf_op | source)
XLA Modules:
  0.0 96.1 jit_solution(207710391971247244)
XLA Ops:
  0.6 0.8 fusion
  1.4 3.0 %collective-permute-start = (bf16[2,32,512]{2,1,0:T(8,128)(2,1)S(1)}, bf16[2,32,512]{2,1,0:T(8,128)(2,1)S(1)}, u32[]{:S(2)}, u32[]{:S(2)}) collective-permute-start(bf16[2,32,512]{2,1,0:T(8,128)(2,1)S(1)} %pad_maximum_fusion.9), channel_id=1, source_target_pairs={{0,1},{1,0},{2,3},{3,2},{4,5},{5,4},{6,7},{7,6},{8,9},{9,8},{10,11... | collective-permute-start | bytes 196616 | tf_op jit(solution)/shard_map/ppermute | solution.py:360
  4.4 1.0 constant_dynamic-slice_fusion.1
  5.5 1.2 %collective-permute-done.x_got = bf16[2,32,512]{2,1,0:T(8,128)(2,1)S(1)} collective-permute-done((bf16[2,32,512]{2,1,0:T(8,128)(2,1)S(1)}, bf16[2,32,512]{2,1,0:T(8,128)(2,1)S(1)}, u32[]{:S(2)}, u32[]{:S(2)}) %collective-permute-start) | collective-permute-done | bytes 65568 | tf_op jit(solution)/shard_map/ppermute | solution.py:360
  6.7 4.0 %collective-permute-start.1 = (bf16[2,16,512]{2,1,0:T(8,128)(2,1)S(1)}, bf16[2,16,512]{2,1,0:T(8,128)(2,1)S(1)}, u32[]{:S(2)}, u32[]{:S(2)}) collective-permute-start(bf16[2,16,512]{2,1,0:T(8,128)(2,1)S(1)} %constant_dynamic-slice_fusion.5), channel_id=1, source_target_pairs={{0,2},{3,1},{2,4},{5,3},{4,6},{7,5},{8,10},{11,9},{10,12},{13,11},... | collective-permute-start | bytes 98312 | tf_op jit(solution)/shard_map/ppermute | solution.py:360
  10.7 1.6 %collective-permute-start.6 = (bf16[2,32,512]{2,1,0:T(8,128)(2,1)S(1)}, bf16[2,32,512]{2,1,0:T(8,128)(2,1)S(1)}, u32[]{:S(2)}, u32[]{:S(2)}) collective-permute-start(bf16[2,32,512]{2,1,0:T(8,128)(2,1)S(1)} %get-tuple-element.100), channel_id=1, source_target_pairs={{0,16},{1,17},{2,18},{3,19},{4,20},{5,21},{6,22},{7,23},{8,24},{9,... | collective-permute-start | bytes 196616 | tf_op jit(solution)/shard_map/ppermute | solution.py:360
  12.4 0.9 copy-done
  13.3 0.8 copy-done.3
  14.2 2.2 %shard_map.126 = (f32[2,128,512]{2,1,0:T(8,128)S(1)}, bf16[2,32,512]{2,1,0:T(8,128)(2,1)S(1)}, bf16[2,32,512]{2,1,0:T(8,128)(2,1)S(1)}, bf16[2,32,512]{2,1,0:T(8,128)(2,1)S(1)}, bf16[2,32,512]{2,1,0:T(8,128)(2,1)S(1)}) custom-call(s32[9]{0:T(128)S(1)} %stack.54.bits, bf16[2,128,512]{2,1,0:T(8,128)(2,1)S(1)} %copy-done, ...), custom_call_target="tpu_custom_call" | custom-call | tf_op jit(solution)/shard_map/pallas_call | solution.py:325
  16.4 0.7 collective-permute-start.2
  17.1 1.5 %collective-permute-start.3 = (bf16[2,32,512]{2,1,0:T(8,128)(2,1)S(1)}, bf16[2,32,512]{2,1,0:T(8,128)(2,1)S(1)}, u32[]{:S(2)}, u32[]{:S(2)}) collective-permute-start(bf16[2,32,512]{2,1,0:T(8,128)(2,1)S(1)} %get-tuple-element.56), channel_id=1, source_target_pairs={{0,16},{1,17},{2,18},{3,19},{4,20},{5,21},{6,22},{7,23},{8,24},{9,... | collective-permute-start | bytes 196616 | tf_op jit(solution)/shard_map/ppermute | solution.py:360
  18.6 1.8 %pad_maximum_fusion.weights = bf16[4,512,512]{2,1,0:T(8,128)(2,1)S(1)} fusion(bf16[1,512,512]{2,1,0:T(8,128)(2,1)} %bitcast.17, bf16[1,512,512]{2,1,0:T(8,128)(2,1)} %bitcast.18, bf16[1,512,512]{2,1,0:T(8,128)(2,1)} %bitcast.19, bf16[1,512,512]{2,1,0:T(8,128)(2,1)} %bitcast.20), kind=kLoop, calls=%fused_computation | loop fusion | flops 3145728 | bytes 4194304 | tf_op jit(solution)/shard_map/stack | solution.py:394
  20.4 0.9 collective-permute-done.3.a2
  21.3 1.6 %collective-permute-done.4.a3 = bf16[2,32,512]{2,1,0:T(8,128)(2,1)S(1)} collective-permute-done((bf16[2,32,512]{2,1,0:T(8,128)(2,1)S(1)}, bf16[2,32,512]{2,1,0:T(8,128)(2,1)S(1)}, u32[]{:S(2)}, u32[]{:S(2)}) %collective-permute-start.4) | collective-permute-done | bytes 65568 | tf_op jit(solution)/shard_map/ppermute | solution.py:360
  23.0 5.8 %shard_map.127 = (bf16[2048,128]{1,0:T(8,128)(2,1)S(1)}, bf16[2048,128]{1,0:T(8,128)(2,1)S(1)}, bf16[2048,128]{1,0:T(8,128)(2,1)S(1)}, bf16[2048,128]{1,0:T(8,12...) custom-call(s32[9]{0:T(128)S(1)} %stack.54.bits, ...), custom_call_target="tpu_custom_call" | custom-call | tf_op jit(solution)/shard_map/pallas_call | solution.py:325
  29.5 2.4 %collective-permute-done.11.core_got = bf16[1024,128]{1,0:T(8,128)(2,1)S(1)} collective-permute-done((bf16[1024,128]{1,0:T(8,128)(2,1)S(1)}, bf16[1024,128]{1,0:T(8,128)(2,1)S(1)}, u32[]{:S(2)}, u32[]{:S(2)}) %collective-permute-start.11) | collective-permute-done | bytes 262176 | tf_op jit(solution)/shard_map/ppermute | solution.py:360
  32.0 1.4 %collective-permute-start.14 = (bf16[1024,128]{1,0:T(8,128)(2,1)S(1)}, bf16[1024,128]{1,0:T(8,128)(2,1)S(1)}, u32[]{:S(2)}, u32[]{:S(2)}) collective-permute-start(bf16[1024,128]{1,0:T(8,128)(2,1)S(1)} %add_convert_fusion), channel_id=1, source_target_pairs={{0,2},{1,3},{2,0},{3,1},{4,6},{5,7},{6,4},{7,5},{8,10},{9,11},{10,... | collective-permute-start | bytes 786440 | tf_op jit(solution)/shard_map/ppermute | solution.py:360
  33.5 1.6 %collective-permute-start.9 = (bf16[1024,128]{1,0:T(8,128)(2,1)S(1)}, bf16[1024,128]{1,0:T(8,128)(2,1)S(1)}, u32[]{:S(2)}, u32[]{:S(2)}) collective-permute-start(bf16[1024,128]{1,0:T(8,128)(2,1)S(1)} %add_convert_fusion.1), channel_id=1, source_target_pairs={{0,1},{1,0},{2,3},{3,2},{4,5},{5,4},{6,7},{7,6},{8,9},{9,8},{10,11... | collective-permute-start | bytes 786440 | tf_op jit(solution)/shard_map/ppermute | solution.py:360
  35.1 1.4 %collective-permute-start.12 = (bf16[1024,128]{1,0:T(8,128)(2,1)S(1)}, bf16[1024,128]{1,0:T(8,128)(2,1)S(1)}, u32[]{:S(2)}, u32[]{:S(2)}) collective-permute-start(bf16[1024,128]{1,0:T(8,128)(2,1)S(1)} %pad_maximum_fusion.2), channel_id=1, source_target_pairs={{0,16},{1,17},{2,18},{3,19},{4,20},{5,21},{6,22},{7,23},{8,24},{9,... | collective-permute-start | bytes 786440 | tf_op jit(solution)/shard_map/ppermute | solution.py:360
  36.5 3.9 %collective-permute-done.14 = bf16[1024,128]{1,0:T(8,128)(2,1)S(1)} collective-permute-done((bf16[1024,128]{1,0:T(8,128)(2,1)S(1)}, bf16[1024,128]{1,0:T(8,128)(2,1)S(1)}, u32[]{:S(2)}, u32[]{:S(2)}) %collective-permute-start.14) | collective-permute-done | bytes 262176 | tf_op jit(solution)/shard_map/ppermute | solution.py:360
  40.5 1.4 %collective-permute-start.22 = (bf16[512,128]{1,0:T(8,128)(2,1)S(1)}, bf16[512,128]{1,0:T(8,128)(2,1)S(1)}, u32[]{:S(2)}, u32[]{:S(2)}) collective-permute-start(bf16[512,128]{1,0:T(8,128)(2,1)S(1)} %add_convert_fusion.2), channel_id=1, source_target_pairs={{0,1},{1,0},{2,3},{3,2},{4,5},{5,4},{6,7},{7,6},{8,9},{9,8},{10,11... | collective-permute-start | bytes 393224 | tf_op jit(solution)/shard_map/ppermute | solution.py:360
  41.9 1.5 %collective-permute-start.10 = (bf16[512,128]{1,0:T(8,128)(2,1)S(1)}, bf16[512,128]{1,0:T(8,128)(2,1)S(1)}, u32[]{:S(2)}, u32[]{:S(2)}) collective-permute-start(bf16[512,128]{1,0:T(8,128)(2,1)S(1)} %add_convert_fusion.3), channel_id=1, source_target_pairs={{0,16},{1,17},{2,18},{3,19},{4,20},{5,21},{6,22},{7,23},{8,24},{9,... | collective-permute-start | bytes 393224 | tf_op jit(solution)/shard_map/ppermute | solution.py:360
  43.5 0.7 shard_map.128
  44.2 1.3 %collective-permute-done.22 = bf16[512,128]{1,0:T(8,128)(2,1)S(1)} collective-permute-done((bf16[512,128]{1,0:T(8,128)(2,1)S(1)}, bf16[512,128]{1,0:T(8,128)(2,1)S(1)}, u32[]{:S(2)}, u32[]{:S(2)}) %collective-permute-start.22) | collective-permute-done | bytes 131104 | tf_op jit(solution)/shard_map/ppermute | solution.py:360
  45.6 1.3 %collective-permute-start.23 = (bf16[256,128]{1,0:T(8,128)(2,1)S(1)}, bf16[256,128]{1,0:T(8,128)(2,1)S(1)}, u32[]{:S(2)}, u32[]{:S(2)}) collective-permute-start(bf16[256,128]{1,0:T(8,128)(2,1)S(1)} %add_convert_fusion.7), channel_id=1, source_target_pairs={{0,16},{1,17},{2,18},{3,19},{4,20},{5,21},{6,22},{7,23},{8,24},{9,... | collective-permute-start | bytes 196616 | tf_op jit(solution)/shard_map/ppermute | solution.py:360
  47.3 2.8 %shard_map.129 = bf16[128,128]{1,0:T(8,128)(2,1)S(1)} custom-call(s32[9]{0:T(128)S(1)} %stack.54.bits, bf16[2,128,512]{2,1,0:T(8,128)(2,1)S(1)} %copy-done.1, bf16[2,32,512]{2,1,0:T(8,128)(2,1)S(1)} %collective-permute-done.x_got, bf16[2,16,512]{2,1,0:T(8,128)(2,1)S(1)} %collective-permute-done.1.z_got, f32[2,128,512]{2,1,0:T(8,128)S(1)} %get-tuple-element.74.dconv), custom_call_target="tpu_custom_call" | custom-call | tf_op jit(solution)/shard_map/pallas_call | solution.py:325
  50.1 1.7 %collective-permute-start.15 = (bf16[384,128]{1,0:T(8,128)(2,1)S(1)}, bf16[384,128]{1,0:T(8,128)(2,1)S(1)}, u32[]{:S(2)}, u32[]{:S(2)}) collective-permute-start(bf16[384,128]{1,0:T(8,128)(2,1)S(1)} %pad_maximum_fusion.5), channel_id=1, source_target_pairs={{0,1},{1,0},{2,3},{3,2},{4,5},{5,4},{6,7},{7,6},{8,9},{9,8},{10,11... | collective-permute-start | bytes 294920 | tf_op jit(solution)/shard_map/ppermute | solution.py:360
  51.9 2.2 %collective-permute-start.24 = (bf16[256,128]{1,0:T(8,128)(2,1)S(1)}, bf16[256,128]{1,0:T(8,128)(2,1)S(1)}, u32[]{:S(2)}, u32[]{:S(2)}) collective-permute-start(bf16[256,128]{1,0:T(8,128)(2,1)S(1)} %add_convert_fusion.6), channel_id=1, source_target_pairs={{0,4},{1,5},{2,6},{3,7},{4,0},{5,1},{6,2},{7,3},{8,12},{9,13},{10,... | collective-permute-start | bytes 196616 | tf_op jit(solution)/shard_map/ppermute | solution.py:360
  54.1 0.7 collective-permute-done.15
  54.8 3.1 %collective-permute-start.16 = (bf16[384,128]{1,0:T(8,128)(2,1)S(1)}, bf16[384,128]{1,0:T(8,128)(2,1)S(1)}, u32[]{:S(2)}, u32[]{:S(2)}) collective-permute-start(bf16[384,128]{1,0:T(8,128)(2,1)S(1)} %pad_maximum_fusion.6), channel_id=1, source_target_pairs={{0,4},{1,5},{2,6},{3,7},{4,0},{5,1},{6,2},{7,3},{8,12},{9,13},{10,... | collective-permute-start | bytes 294920 | tf_op jit(solution)/shard_map/ppermute | solution.py:360
  57.9 2.7 %collective-permute-start.18 = (bf16[8,16,128]{2,1,0:T(8,128)(2,1)S(1)}, bf16[8,16,128]{2,1,0:T(8,128)(2,1)S(1)}, u32[]{:S(2)}, u32[]{:S(2)}) collective-permute-start(bf16[8,16,128]{2,1,0:T(8,128)(2,1)S(1)} %constant_dynamic-slice_fusion), channel_id=1, source_target_pairs={{0,2},{3,1},{2,4},{5,3},{4,6},{7,5},{8,10},{11,9},{10,12},{13,11},... | collective-permute-start | bytes 98312 | tf_op jit(solution)/shard_map/ppermute | solution.py:360
  60.7 1.8 %collective-permute-start.17 = (bf16[384,128]{1,0:T(8,128)(2,1)S(1)}, bf16[384,128]{1,0:T(8,128)(2,1)S(1)}, u32[]{:S(2)}, u32[]{:S(2)}) collective-permute-start(bf16[384,128]{1,0:T(8,128)(2,1)S(1)} %pad_maximum_fusion.7), channel_id=1, source_target_pairs={{0,2},{1,3},{2,0},{3,1},{4,6},{5,7},{6,4},{7,5},{8,10},{9,11},{10,... | collective-permute-start | bytes 294920 | tf_op jit(solution)/shard_map/ppermute | solution.py:360
  62.6 2.8 %collective-permute-done.17 = bf16[384,128]{1,0:T(8,128)(2,1)S(1)} collective-permute-done((bf16[384,128]{1,0:T(8,128)(2,1)S(1)}, bf16[384,128]{1,0:T(8,128)(2,1)S(1)}, u32[]{:S(2)}, u32[]{:S(2)}) %collective-permute-start.17) | collective-permute-done | bytes 98336 | tf_op jit(solution)/shard_map/ppermute | solution.py:360
  65.5 1.8 %collective-permute-start.25 = (bf16[384,128]{1,0:T(8,128)(2,1)S(1)}, bf16[384,128]{1,0:T(8,128)(2,1)S(1)}, u32[]{:S(2)}, u32[]{:S(2)}) collective-permute-start(bf16[384,128]{1,0:T(8,128)(2,1)S(1)} %pad_maximum_fusion.8), channel_id=1, source_target_pairs={{0,16},{1,17},{2,18},{3,19},{4,20},{5,21},{6,22},{7,23},{8,24},{9,... | collective-permute-start | bytes 294920 | tf_op jit(solution)/shard_map/ppermute | solution.py:360
  67.3 3.9 %collective-permute-start.19 = (bf16[256,128]{1,0:T(8,128)(2,1)S(1)}, bf16[256,128]{1,0:T(8,128)(2,1)S(1)}, u32[]{:S(2)}, u32[]{:S(2)}) collective-permute-start(bf16[256,128]{1,0:T(8,128)(2,1)S(1)} %slice.200), channel_id=1, source_target_pairs={{0,4},{1,5},{2,6},{3,7},{4,0},{5,1},{6,2},{7,3},{8,12},{9,13},{10,... | collective-permute-start | bytes 196616 | tf_op jit(solution)/shard_map/ppermute | solution.py:360
  71.2 2.9 %collective-permute-done.19 = bf16[256,128]{1,0:T(8,128)(2,1)S(1)} collective-permute-done((bf16[256,128]{1,0:T(8,128)(2,1)S(1)}, bf16[256,128]{1,0:T(8,128)(2,1)S(1)}, u32[]{:S(2)}, u32[]{:S(2)}) %collective-permute-start.19) | collective-permute-done | bytes 65568 | tf_op jit(solution)/shard_map/ppermute | solution.py:360
  74.5 2.8 %shard_map.130 = bf16[2,128,512]{2,1,0:T(8,128)(2,1)} custom-call(s32[9]{0:T(128)S(1)} %stack.54.bits, f32[2,128,512]{2,1,0:T(8,128)S(1)} %get-tuple-element.74.dconv, bf16[256,128]{1,0:T(8,128)(2,1)S(1)} %slice.201.x_got, bf16[128,128]{1,0:T(8,128)(2,1)S(1)} %bitcast.16, bf16[2,128,512]{2,1,0:T(8,128)(2,1)S(1)} %copy-done.2, f32[31,512]{1,0:T(8,128)S(1)} %copy-done.4), custom_call_target="tpu_custom_call" | custom-call | tf_op jit(solution)/shard_map/pallas_call | solution.py:325
  77.4 1.3 %collective-permute-start.26 = (bf16[512,128]{1,0:T(8,128)(2,1)S(1)}, bf16[512,128]{1,0:T(8,128)(2,1)S(1)}, u32[]{:S(2)}, u32[]{:S(2)}) collective-permute-start(bf16[512,128]{1,0:T(8,128)(2,1)S(1)} %pad_maximum_fusion.4), channel_id=1, source_target_pairs={{0,1},{1,0},{2,3},{3,2},{4,5},{5,4},{6,7},{7,6},{8,9},{9,8},{10,11... | collective-permute-start | bytes 393224 | tf_op jit(solution)/shard_map/ppermute | solution.py:360
  79.1 3.3 %collective-permute-done.26 = bf16[512,128]{1,0:T(8,128)(2,1)S(1)} collective-permute-done((bf16[512,128]{1,0:T(8,128)(2,1)S(1)}, bf16[512,128]{1,0:T(8,128)(2,1)S(1)}, u32[]{:S(2)}, u32[]{:S(2)}) %collective-permute-start.26) | collective-permute-done | bytes 131104 | tf_op jit(solution)/shard_map/ppermute | solution.py:360
  82.5 0.5 collective-permute-start.29
  83.0 1.3 %collective-permute-start.21 = (bf16[1024,128]{1,0:T(8,128)(2,1)S(1)}, bf16[1024,128]{1,0:T(8,128)(2,1)S(1)}, u32[]{:S(2)}, u32[]{:S(2)}) collective-permute-start(bf16[1024,128]{1,0:T(8,128)(2,1)S(1)} %constant_dynamic-update-slice_fusion.2.refs_0_), channel_id=1, source_target_pairs={{0,1},{1,0},{2,3},{3,2},{4,5},{5,4},{6,7},{7,6},{8,9},{9,8},{10,11... | collective-permute-start | bytes 786440 | tf_op jit(solution)/shard_map/ppermute | solution.py:360
  84.4 1.6 %shard_map.131 = bf16[2,128,512]{2,1,0:T(8,128)(2,1)} custom-call(s32[9]{0:T(128)S(1)} %stack.54.bits, bf16[1024,128]{1,0:T(8,128)(2,1)S(1)} %get-tuple-element.64.own, bf16[1024,128]{1,0:T(8,128)(2,1)S(1)} %collective-permute-done.11.core_got, bf16[1024,128]{1,0:T(8,128)(2,1)S(1)} %collective-permute-done.12.y_got, bf16[2,128,512]{2,1,0:T(8,128)(2,1)S(1)} %copy-done.1, ...), custom_call_target="tpu_custom_call" | custom-call | tf_op jit(solution)/shard_map/pallas_call | solution.py:325
  86.0 2.6 %shard_map.132 = (f32[512,512]{1,0:T(8,128)}, f32[512,512]{1,0:T(8,128)}, f32[512,512]{1,0:T(8,128)}, f32[512,512]{1,0:T(8,128)}, f32[31,512]{1,0:T(8,128)}) custom-call(s32[9]{0:T(128)S(1)} %stack.54.bits, bf16[1024,128]{1,0:T(8,128)(2,1)S(1)} %constant_dynamic-update-slice_fusion.2.refs_0_, bf16[1024,128]{1,0:T(8,128)(2,1)S(1)} %pad_maximum_fusion.3.refs_1_, ...), custom_call_target="tpu_custom_call" | custom-call | tf_op jit(solution)/shard_map/pallas_call | solution.py:325
  88.6 2.8 %collective-permute-done.21.refs_0_ = bf16[1024,128]{1,0:T(8,128)(2,1)S(1)} collective-permute-done((bf16[1024,128]{1,0:T(8,128)(2,1)S(1)}, bf16[1024,128]{1,0:T(8,128)(2,1)S(1)}, u32[]{:S(2)}, u32[]{:S(2)}) %collective-permute-start.21) | collective-permute-done | bytes 262176 | tf_op jit(solution)/shard_map/ppermute | solution.py:360
  91.4 1.0 %collective-permute-done.27.refs_1_ = bf16[1024,128]{1,0:T(8,128)(2,1)S(1)} collective-permute-done((bf16[1024,128]{1,0:T(8,128)(2,1)S(1)}, bf16[1024,128]{1,0:T(8,128)(2,1)S(1)}, u32[]{:S(2)}, u32[]{:S(2)}) %collective-permute-start.27) | collective-permute-done | bytes 262176 | tf_op jit(solution)/shard_map/ppermute | solution.py:360
  92.4 0.5 collective-permute-start.31
  92.9 1.6 %shard_map.133 = (f32[512,512]{1,0:T(8,128)}, f32[512,512]{1,0:T(8,128)}, f32[512,512]{1,0:T(8,128)}, f32[512,512]{1,0:T(8,128)}) custom-call(s32[9]{0:T(128)S(1)} %stack.54.bits, bf16[1024,128]{1,0:T(8,128)(2,1)S(1)} %collective-permute-done.21.refs_0_, ...), custom_call_target="tpu_custom_call", output_to_operand_aliasing={{0}: (3, {}), {1}: (4, {}), {2}: (5, {}), {3}: (6, {})} | custom-call | tf_op jit(solution)/shard_map/pallas_call | solution.py:325
  94.5 1.6 %shard_map.134 = (f32[512,512]{1,0:T(8,128)}, f32[512,512]{1,0:T(8,128)}, f32[512,512]{1,0:T(8,128)}, f32[512,512]{1,0:T(8,128)}) custom-call(s32[9]{0:T(128)S(1)} %stack.54.bits, bf16[1024,128]{1,0:T(8,128)(2,1)S(1)} %collective-permute-done.30.refs_0_, ...), custom_call_target="tpu_custom_call", output_to_operand_aliasing={{0}: (3, {}), {1}: (4, {}), {2}: (5, {}), {3}: (6, {})} | custom-call | tf_op jit(solution)/shard_map/pallas_call | solution.py:325
  (73 shorter events, 2.8 us)
Async XLA Ops:
  1.4 5.2 %collective-permute-start = (bf16[2,32,512]{2,1,0:T(8,128)(2,1)S(1)}, bf16[2,32,512]{2,1,0:T(8,128)(2,1)S(1)}, u32[]{:S(2)}, u32[]{:S(2)}) collective-permute-start(bf16[2,32,512]{2,1,0:T(8,128)(2,1)S(1)} %pad_maximum_fusion.9), channel_id=1, source_target_pairs={{0,1},{1,0},{2,3},{3,2},{4,5},{5,4},{6,7},{7,6},{8,9},{9,8},{10,11... | collective-permute-start | bytes 196616 | tf_op jit(solution)/shard_map/ppermute | solution.py:360
  5.4 13.2 %collective-permute-start.5 = (bf16[2,32,512]{2,1,0:T(8,128)(2,1)S(1)}, bf16[2,32,512]{2,1,0:T(8,128)(2,1)S(1)}, u32[]{:S(2)}, u32[]{:S(2)}) collective-permute-start(bf16[2,32,512]{2,1,0:T(8,128)(2,1)S(1)} %get-tuple-element.101), channel_id=1, source_target_pairs={{0,8},{1,9},{2,10},{3,11},{4,12},{5,13},{6,14},{7,15},{8,0},{9,1},... | collective-permute-start | bytes 196616 | tf_op jit(solution)/shard_map/ppermute | solution.py:360
  6.7 5.7 %collective-permute-start.1 = (bf16[2,16,512]{2,1,0:T(8,128)(2,1)S(1)}, bf16[2,16,512]{2,1,0:T(8,128)(2,1)S(1)}, u32[]{:S(2)}, u32[]{:S(2)}) collective-permute-start(bf16[2,16,512]{2,1,0:T(8,128)(2,1)S(1)} %constant_dynamic-slice_fusion.5), channel_id=1, source_target_pairs={{0,2},{3,1},{2,4},{5,3},{4,6},{7,5},{8,10},{11,9},{10,12},{13,11},... | collective-permute-start | bytes 98312 | tf_op jit(solution)/shard_map/ppermute | solution.py:360
  10.7 9.7 %collective-permute-start.6 = (bf16[2,32,512]{2,1,0:T(8,128)(2,1)S(1)}, bf16[2,32,512]{2,1,0:T(8,128)(2,1)S(1)}, u32[]{:S(2)}, u32[]{:S(2)}) collective-permute-start(bf16[2,32,512]{2,1,0:T(8,128)(2,1)S(1)} %get-tuple-element.100), channel_id=1, source_target_pairs={{0,16},{1,17},{2,18},{3,19},{4,20},{5,21},{6,22},{7,23},{8,24},{9,... | collective-permute-start | bytes 196616 | tf_op jit(solution)/shard_map/ppermute | solution.py:360
  12.3 8.1 %collective-permute-start.7 = (bf16[2,32,512]{2,1,0:T(8,128)(2,1)S(1)}, bf16[2,32,512]{2,1,0:T(8,128)(2,1)S(1)}, u32[]{:S(2)}, u32[]{:S(2)}) collective-permute-start(bf16[2,32,512]{2,1,0:T(8,128)(2,1)S(1)} %get-tuple-element.99), channel_id=1, source_target_pairs={{0,24},{1,25},{2,26},{3,27},{4,28},{5,29},{6,30},{7,31},{8,16},{9,... | collective-permute-start | bytes 196616 | tf_op jit(solution)/shard_map/ppermute | solution.py:360
  12.4 1.0 copy-start
  13.3 0.8 copy-start.3
  16.4 4.0 %collective-permute-start.2 = (bf16[2,32,512]{2,1,0:T(8,128)(2,1)S(1)}, bf16[2,32,512]{2,1,0:T(8,128)(2,1)S(1)}, u32[]{:S(2)}, u32[]{:S(2)}) collective-permute-start(bf16[2,32,512]{2,1,0:T(8,128)(2,1)S(1)} %get-tuple-element.55), channel_id=1, source_target_pairs={{0,8},{1,9},{2,10},{3,11},{4,12},{5,13},{6,14},{7,15},{8,0},{9,1},... | collective-permute-start | bytes 196616 | tf_op jit(solution)/shard_map/ppermute | solution.py:360
  17.1 4.3 %collective-permute-start.3 = (bf16[2,32,512]{2,1,0:T(8,128)(2,1)S(1)}, bf16[2,32,512]{2,1,0:T(8,128)(2,1)S(1)}, u32[]{:S(2)}, u32[]{:S(2)}) collective-permute-start(bf16[2,32,512]{2,1,0:T(8,128)(2,1)S(1)} %get-tuple-element.56), channel_id=1, source_target_pairs={{0,16},{1,17},{2,18},{3,19},{4,20},{5,21},{6,22},{7,23},{8,24},{9,... | collective-permute-start | bytes 196616 | tf_op jit(solution)/shard_map/ppermute | solution.py:360
  18.6 4.4 %collective-permute-start.4 = (bf16[2,32,512]{2,1,0:T(8,128)(2,1)S(1)}, bf16[2,32,512]{2,1,0:T(8,128)(2,1)S(1)}, u32[]{:S(2)}, u32[]{:S(2)}) collective-permute-start(bf16[2,32,512]{2,1,0:T(8,128)(2,1)S(1)} %get-tuple-element.57), channel_id=1, source_target_pairs={{0,24},{1,25},{2,26},{3,27},{4,28},{5,29},{6,30},{7,31},{8,16},{9,... | collective-permute-start | bytes 196616 | tf_op jit(solution)/shard_map/ppermute | solution.py:360
  28.8 3.1 %collective-permute-start.13 = (bf16[2048,128]{1,0:T(8,128)(2,1)S(1)}, bf16[2048,128]{1,0:T(8,128)(2,1)S(1)}, u32[]{:S(2)}, u32[]{:S(2)}) collective-permute-start(bf16[2048,128]{1,0:T(8,128)(2,1)S(1)} %get-tuple-element.67), channel_id=1, source_target_pairs={{0,8},{1,9},{2,10},{3,11},{4,12},{5,13},{6,14},{7,15},{8,0},{9,1},... | collective-permute-start | bytes 1572872 | tf_op jit(solution)/shard_map/ppermute | solution.py:360
  29.0 4.5 %collective-permute-start.8 = (bf16[2048,128]{1,0:T(8,128)(2,1)S(1)}, bf16[2048,128]{1,0:T(8,128)(2,1)S(1)}, u32[]{:S(2)}, u32[]{:S(2)}) collective-permute-start(bf16[2048,128]{1,0:T(8,128)(2,1)S(1)} %get-tuple-element.63), channel_id=1, source_target_pairs={{0,8},{1,9},{2,10},{3,11},{4,12},{5,13},{6,14},{7,15},{8,0},{9,1},... | collective-permute-start | bytes 1572872 | tf_op jit(solution)/shard_map/ppermute | solution.py:360
  29.4 2.5 %collective-permute-start.11 = (bf16[1024,128]{1,0:T(8,128)(2,1)S(1)}, bf16[1024,128]{1,0:T(8,128)(2,1)S(1)}, u32[]{:S(2)}, u32[]{:S(2)}) collective-permute-start(bf16[1024,128]{1,0:T(8,128)(2,1)S(1)} %get-tuple-element.65), channel_id=1, source_target_pairs={{0,8},{1,9},{2,10},{3,11},{4,12},{5,13},{6,14},{7,15},{8,0},{9,1},... | collective-permute-start | bytes 786440 | tf_op jit(solution)/shard_map/ppermute | solution.py:360
  32.0 15.2 %copy-start.1 = (bf16[2,128,512]{2,1,0:T(8,128)(2,1)S(1)}, bf16[2,128,512]{2,1,0:T(8,128)(2,1)}, u32[]{:S(2)}) copy-start(bf16[2,128,512]{2,1,0:T(8,128)(2,1)} %frames.4) | copy-start | bytes 786436
  32.0 8.4 %collective-permute-start.14 = (bf16[1024,128]{1,0:T(8,128)(2,1)S(1)}, bf16[1024,128]{1,0:T(8,128)(2,1)S(1)}, u32[]{:S(2)}, u32[]{:S(2)}) collective-permute-start(bf16[1024,128]{1,0:T(8,128)(2,1)S(1)} %add_convert_fusion), channel_id=1, source_target_pairs={{0,2},{1,3},{2,0},{3,1},{4,6},{5,7},{6,4},{7,5},{8,10},{9,11},{10,... | collective-permute-start | bytes 786440 | tf_op jit(solution)/shard_map/ppermute | solution.py:360
  33.5 8.3 %collective-permute-start.9 = (bf16[1024,128]{1,0:T(8,128)(2,1)S(1)}, bf16[1024,128]{1,0:T(8,128)(2,1)S(1)}, u32[]{:S(2)}, u32[]{:S(2)}) collective-permute-start(bf16[1024,128]{1,0:T(8,128)(2,1)S(1)} %add_convert_fusion.1), channel_id=1, source_target_pairs={{0,1},{1,0},{2,3},{3,2},{4,5},{5,4},{6,7},{7,6},{8,9},{9,8},{10,11... | collective-permute-start | bytes 786440 | tf_op jit(solution)/shard_map/ppermute | solution.py:360
  35.1 8.3 %collective-permute-start.12 = (bf16[1024,128]{1,0:T(8,128)(2,1)S(1)}, bf16[1024,128]{1,0:T(8,128)(2,1)S(1)}, u32[]{:S(2)}, u32[]{:S(2)}) collective-permute-start(bf16[1024,128]{1,0:T(8,128)(2,1)S(1)} %pad_maximum_fusion.2), channel_id=1, source_target_pairs={{0,16},{1,17},{2,18},{3,19},{4,20},{5,21},{6,22},{7,23},{8,24},{9,... | collective-permute-start | bytes 786440 | tf_op jit(solution)/shard_map/ppermute | solution.py:360
  40.5 5.0 %collective-permute-start.22 = (bf16[512,128]{1,0:T(8,128)(2,1)S(1)}, bf16[512,128]{1,0:T(8,128)(2,1)S(1)}, u32[]{:S(2)}, u32[]{:S(2)}) collective-permute-start(bf16[512,128]{1,0:T(8,128)(2,1)S(1)} %add_convert_fusion.2), channel_id=1, source_target_pairs={{0,1},{1,0},{2,3},{3,2},{4,5},{5,4},{6,7},{7,6},{8,9},{9,8},{10,11... | collective-permute-start | bytes 393224 | tf_op jit(solution)/shard_map/ppermute | solution.py:360
  41.9 5.3 %collective-permute-start.10 = (bf16[512,128]{1,0:T(8,128)(2,1)S(1)}, bf16[512,128]{1,0:T(8,128)(2,1)S(1)}, u32[]{:S(2)}, u32[]{:S(2)}) collective-permute-start(bf16[512,128]{1,0:T(8,128)(2,1)S(1)} %add_convert_fusion.3), channel_id=1, source_target_pairs={{0,16},{1,17},{2,18},{3,19},{4,20},{5,21},{6,22},{7,23},{8,24},{9,... | collective-permute-start | bytes 393224 | tf_op jit(solution)/shard_map/ppermute | solution.py:360
  45.6 6.3 %collective-permute-start.23 = (bf16[256,128]{1,0:T(8,128)(2,1)S(1)}, bf16[256,128]{1,0:T(8,128)(2,1)S(1)}, u32[]{:S(2)}, u32[]{:S(2)}) collective-permute-start(bf16[256,128]{1,0:T(8,128)(2,1)S(1)} %add_convert_fusion.7), channel_id=1, source_target_pairs={{0,16},{1,17},{2,18},{3,19},{4,20},{5,21},{6,22},{7,23},{8,24},{9,... | collective-permute-start | bytes 196616 | tf_op jit(solution)/shard_map/ppermute | solution.py:360
  47.3 27.2 %copy-start.2 = (bf16[2,128,512]{2,1,0:T(8,128)(2,1)S(1)}, bf16[2,128,512]{2,1,0:T(8,128)(2,1)}, u32[]{:S(2)}) copy-start(bf16[2,128,512]{2,1,0:T(8,128)(2,1)} %cot.1) | copy-start | bytes 786436
  47.3 27.2 %copy-start.4 = (f32[31,512]{1,0:T(8,128)S(1)}, f32[31,512]{1,0:T(8,128)}, u32[]{:S(2)}) copy-start(f32[31,512]{1,0:T(8,128)} %kern.3) | copy-start | bytes 190468
  50.1 4.7 %collective-permute-start.15 = (bf16[384,128]{1,0:T(8,128)(2,1)S(1)}, bf16[384,128]{1,0:T(8,128)(2,1)S(1)}, u32[]{:S(2)}, u32[]{:S(2)}) collective-permute-start(bf16[384,128]{1,0:T(8,128)(2,1)S(1)} %pad_maximum_fusion.5), channel_id=1, source_target_pairs={{0,1},{1,0},{2,3},{3,2},{4,5},{5,4},{6,7},{7,6},{8,9},{9,8},{10,11... | collective-permute-start | bytes 294920 | tf_op jit(solution)/shard_map/ppermute | solution.py:360
  51.9 10.7 %collective-permute-start.24 = (bf16[256,128]{1,0:T(8,128)(2,1)S(1)}, bf16[256,128]{1,0:T(8,128)(2,1)S(1)}, u32[]{:S(2)}, u32[]{:S(2)}) collective-permute-start(bf16[256,128]{1,0:T(8,128)(2,1)S(1)} %add_convert_fusion.6), channel_id=1, source_target_pairs={{0,4},{1,5},{2,6},{3,7},{4,0},{5,1},{6,2},{7,3},{8,12},{9,13},{10,... | collective-permute-start | bytes 196616 | tf_op jit(solution)/shard_map/ppermute | solution.py:360
  54.8 5.8 %collective-permute-start.16 = (bf16[384,128]{1,0:T(8,128)(2,1)S(1)}, bf16[384,128]{1,0:T(8,128)(2,1)S(1)}, u32[]{:S(2)}, u32[]{:S(2)}) collective-permute-start(bf16[384,128]{1,0:T(8,128)(2,1)S(1)} %pad_maximum_fusion.6), channel_id=1, source_target_pairs={{0,4},{1,5},{2,6},{3,7},{4,0},{5,1},{6,2},{7,3},{8,12},{9,13},{10,... | collective-permute-start | bytes 294920 | tf_op jit(solution)/shard_map/ppermute | solution.py:360
  57.9 9.4 %collective-permute-start.18 = (bf16[8,16,128]{2,1,0:T(8,128)(2,1)S(1)}, bf16[8,16,128]{2,1,0:T(8,128)(2,1)S(1)}, u32[]{:S(2)}, u32[]{:S(2)}) collective-permute-start(bf16[8,16,128]{2,1,0:T(8,128)(2,1)S(1)} %constant_dynamic-slice_fusion), channel_id=1, source_target_pairs={{0,2},{3,1},{2,4},{5,3},{4,6},{7,5},{8,10},{11,9},{10,12},{13,11},... | collective-permute-start | bytes 98312 | tf_op jit(solution)/shard_map/ppermute | solution.py:360
  60.7 4.7 %collective-permute-start.17 = (bf16[384,128]{1,0:T(8,128)(2,1)S(1)}, bf16[384,128]{1,0:T(8,128)(2,1)S(1)}, u32[]{:S(2)}, u32[]{:S(2)}) collective-permute-start(bf16[384,128]{1,0:T(8,128)(2,1)S(1)} %pad_maximum_fusion.7), channel_id=1, source_target_pairs={{0,2},{1,3},{2,0},{3,1},{4,6},{5,7},{6,4},{7,5},{8,10},{9,11},{10,... | collective-permute-start | bytes 294920 | tf_op jit(solution)/shard_map/ppermute | solution.py:360
  65.5 11.8 %collective-permute-start.25 = (bf16[384,128]{1,0:T(8,128)(2,1)S(1)}, bf16[384,128]{1,0:T(8,128)(2,1)S(1)}, u32[]{:S(2)}, u32[]{:S(2)}) collective-permute-start(bf16[384,128]{1,0:T(8,128)(2,1)S(1)} %pad_maximum_fusion.8), channel_id=1, source_target_pairs={{0,16},{1,17},{2,18},{3,19},{4,20},{5,21},{6,22},{7,23},{8,24},{9,... | collective-permute-start | bytes 294920 | tf_op jit(solution)/shard_map/ppermute | solution.py:360
  67.3 6.7 %collective-permute-start.19 = (bf16[256,128]{1,0:T(8,128)(2,1)S(1)}, bf16[256,128]{1,0:T(8,128)(2,1)S(1)}, u32[]{:S(2)}, u32[]{:S(2)}) collective-permute-start(bf16[256,128]{1,0:T(8,128)(2,1)S(1)} %slice.200), channel_id=1, source_target_pairs={{0,4},{1,5},{2,6},{3,7},{4,0},{5,1},{6,2},{7,3},{8,12},{9,13},{10,... | collective-permute-start | bytes 196616 | tf_op jit(solution)/shard_map/ppermute | solution.py:360
  74.0 5.0 %collective-permute-start.20 = (bf16[512,128]{1,0:T(8,128)(2,1)S(1)}, bf16[512,128]{1,0:T(8,128)(2,1)S(1)}, u32[]{:S(2)}, u32[]{:S(2)}) collective-permute-start(bf16[512,128]{1,0:T(8,128)(2,1)S(1)} %get-tuple-element.105), channel_id=1, source_target_pairs={{0,16},{1,17},{2,18},{3,19},{4,20},{5,21},{6,22},{7,23},{8,24},{9,... | collective-permute-start | bytes 393224 | tf_op jit(solution)/shard_map/ppermute | solution.py:360
  77.4 5.0 %collective-permute-start.26 = (bf16[512,128]{1,0:T(8,128)(2,1)S(1)}, bf16[512,128]{1,0:T(8,128)(2,1)S(1)}, u32[]{:S(2)}, u32[]{:S(2)}) collective-permute-start(bf16[512,128]{1,0:T(8,128)(2,1)S(1)} %pad_maximum_fusion.4), channel_id=1, source_target_pairs={{0,1},{1,0},{2,3},{3,2},{4,5},{5,4},{6,7},{7,6},{8,9},{9,8},{10,11... | collective-permute-start | bytes 393224 | tf_op jit(solution)/shard_map/ppermute | solution.py:360
  82.4 3.5 %collective-permute-start.28 = (bf16[1152,128]{1,0:T(8,128)(2,1)S(1)}, bf16[1152,128]{1,0:T(8,128)(2,1)S(1)}, u32[]{:S(2)}, u32[]{:S(2)}) collective-permute-start(bf16[1152,128]{1,0:T(8,128)(2,1)S(1)} %pad_maximum_fusion.1), channel_id=1, source_target_pairs={{0,8},{1,9},{2,10},{3,11},{4,12},{5,13},{6,14},{7,15},{8,0},{9,1},... | collective-permute-start | bytes 884744 | tf_op jit(solution)/shard_map/ppermute | solution.py:360
  82.5 3.5 %collective-permute-start.29 = (bf16[1024,128]{1,0:T(8,128)(2,1)S(1)}, bf16[1024,128]{1,0:T(8,128)(2,1)S(1)}, u32[]{:S(2)}, u32[]{:S(2)}) collective-permute-start(bf16[1024,128]{1,0:T(8,128)(2,1)S(1)} %pad_maximum_fusion.3.refs_1_), channel_id=1, source_target_pairs={{0,8},{1,9},{2,10},{3,11},{4,12},{5,13},{6,14},{7,15},{8,0},{9,1},... | collective-permute-start | bytes 786440 | tf_op jit(solution)/shard_map/ppermute | solution.py:360
  83.0 8.4 %collective-permute-start.21 = (bf16[1024,128]{1,0:T(8,128)(2,1)S(1)}, bf16[1024,128]{1,0:T(8,128)(2,1)S(1)}, u32[]{:S(2)}, u32[]{:S(2)}) collective-permute-start(bf16[1024,128]{1,0:T(8,128)(2,1)S(1)} %constant_dynamic-update-slice_fusion.2.refs_0_), channel_id=1, source_target_pairs={{0,1},{1,0},{2,3},{3,2},{4,5},{5,4},{6,7},{7,6},{8,9},{9,8},{10,11... | collective-permute-start | bytes 786440 | tf_op jit(solution)/shard_map/ppermute | solution.py:360
  84.3 8.0 %collective-permute-start.27 = (bf16[1024,128]{1,0:T(8,128)(2,1)S(1)}, bf16[1024,128]{1,0:T(8,128)(2,1)S(1)}, u32[]{:S(2)}, u32[]{:S(2)}) collective-permute-start(bf16[1024,128]{1,0:T(8,128)(2,1)S(1)} %pad_maximum_fusion.3.refs_1_), channel_id=1, source_target_pairs={{0,2},{1,3},{2,0},{3,1},{4,6},{5,7},{6,4},{7,5},{8,10},{9,11},{10,... | collective-permute-start | bytes 786440 | tf_op jit(solution)/shard_map/ppermute | solution.py:360
  92.4 2.1 %collective-permute-start.30 = (bf16[1024,128]{1,0:T(8,128)(2,1)S(1)}, bf16[1024,128]{1,0:T(8,128)(2,1)S(1)}, u32[]{:S(2)}, u32[]{:S(2)}) collective-permute-start(bf16[1024,128]{1,0:T(8,128)(2,1)S(1)} %collective-permute-done.21.refs_0_), channel_id=1, source_target_pairs={{0,8},{1,9},{2,10},{3,11},{4,12},{5,13},{6,14},{7,15},{8,0},{9,1},... | collective-permute-start | bytes 786440 | tf_op jit(solution)/shard_map/ppermute | solution.py:360
  92.4 2.1 %collective-permute-start.31 = (bf16[1024,128]{1,0:T(8,128)(2,1)S(1)}, bf16[1024,128]{1,0:T(8,128)(2,1)S(1)}, u32[]{:S(2)}, u32[]{:S(2)}) collective-permute-start(bf16[1024,128]{1,0:T(8,128)(2,1)S(1)} %collective-permute-done.27.refs_1_), channel_id=1, source_target_pairs={{0,8},{1,9},{2,10},{3,11},{4,12},{5,13},{6,14},{7,15},{8,0},{9,1},... | collective-permute-start | bytes 786440 | tf_op jit(solution)/shard_map/ppermute | solution.py:360

commit v10 on v9

--- a/solution.py
+++ b/solution.py
@@ -56,12 +56,8 @@
     )
 
 
-def near_edge(bits):
-    return pl.ds(pl.multiple_of(bits[X] * HALO, HALO), HALO)
-
-
 def padded_frames(bits, frames, x_got, z_got, m, lanes):
-    return padded(bits, frames[m, :, lanes], x_got[m, near_edge(bits), lanes], z_got[m, :, lanes])
+    return padded(bits, frames[m, :, lanes], x_got[m, :, lanes], z_got[m, :, lanes])
 
 
 def lanes_of(width):
@@ -70,7 +66,7 @@
 
 def conv_kernel(sub, bits, frames, x_got, z_got, kern, conv_out, *refs):
     outs, act_s = refs[:4], refs[4]
-    count, length, width = frames.shape
+    count, length, width = conv_out.shape
     half = length // 2
 
     def step(m, _):
@@ -203,16 +199,15 @@
 
 
 def final_kernel(plan, bits, *refs):
-    kinds, first_call, width, norm = plan
+    kinds, first_call, with_taps, width, norm = plan
     cols = width // LANES
     size = cols * width // 8
     got, refs = refs[: len(kinds)], refs[len(kinds) :]
-    if first_call:
-        taps, *outs, tap_grad, piece_s, sems = refs
+    if with_taps:
+        taps, refs, tap_grad = refs[0], refs[1:-3] + refs[-2:], refs[-3]
         for lc, lanes in enumerate(lanes_of(width)):
             tap_grad[:, lanes] = taps[lc * 32 : lc * 32 + 31, :].astype(F32) * norm
-    else:
-        outs, piece_s, sems = refs[4:8], refs[8], refs[9]
+    *outs, piece_s, sems = refs if first_call else refs[4:]
     core = bits[CORE]
     copies = []
     for n, (own, h, far) in enumerate(kinds):
@@ -248,17 +243,20 @@
                 yield ref[at : at + sub, :], m, to, slice(lc * LANES, (lc + 1) * LANES)
 
 
-def dconv_kernel(plan, bits, own, core_got, y_got, conv_in, dconv, edges):
+def dconv_kernel(plan, bits, own, core_got, y_got, conv_in, dconv, x_edge, z_edge):
     for dacted, m, to, lanes in home_chunks(plan, bits, own, core_got, y_got, 1):
         conv = conv_in[m, to, lanes]
         sig = sigmoid(conv)
         dconv[m, to, lanes] = dacted.astype(F32) * sig * (1.0 + conv * (1.0 - sig))
     count, length, width = dconv.shape
+    odd, last = bits[X], length - HALO
     for m in range(count):
         for lc, lanes in enumerate(lanes_of(width)):
-            at = (m * plan[2] + lc) * 2 * HALO
-            edges[at : at + HALO, :] = dconv[m, :HALO, lanes].astype(BF)
-            edges[at + HALO : at + 2 * HALO, :] = dconv[m, length - HALO :, lanes].astype(BF)
+            at = (m * plan[2] + lc) * HALO
+            x_rows = pl.ds(pl.multiple_of((1 - odd) * last, HALO), HALO)
+            z_rows = pl.ds(pl.multiple_of(odd * last, HALO), HALO)
+            x_edge[at : at + HALO, :] = dconv[m, x_rows, lanes].astype(BF)
+            z_edge[at : at + HALO, :] = dconv[m, z_rows, lanes].astype(BF)
 
 
 def layer_kernel(plan, bits, own, core_got, y_got, frames, weights, layer_out, mix_s):
@@ -270,7 +268,7 @@
 
 
 def tap_kernel(sub, bits, frames, x_got, z_got, dconv, taps, pad_s):
-    count, length, width = frames.shape
+    count, length, width = dconv.shape
     for m in range(count):
         for lanes in lanes_of(width):
             pad_s[m, :, lanes] = padded_frames(bits, frames, x_got, z_got, m, lanes)
@@ -299,22 +297,23 @@
         ).astype(BF)
 
 
-def frame_kernel(bits, dconv, x_got, z_got, cot, kern, frame_grad):
+def frame_kernel(bits, dconv, x_got, z_got, both, kern, frame_grad):
     count, length, width = dconv.shape
     half = length // 2
 
     def step(m, _):
         for lc, lanes in enumerate(lanes_of(width)):
             n = m * (width // LANES) + lc
-            x_rows = pl.ds(pl.multiple_of((2 * n + bits[X]) * HALO, HALO), HALO)
-            z_rows = pl.ds(pl.multiple_of(n * HALO, HALO), HALO)
-            x = padded(bits, dconv[m, :, lanes], x_got[x_rows, :], z_got[z_rows, :])
+            rows = pl.ds(pl.multiple_of(n * HALO, HALO), HALO)
+            x = padded(bits, dconv[m, :, lanes], x_got[rows, :], z_got[rows, :])
             for at in (0, half):
                 part = slice(at, at + half)
                 grad = window(
                     x[at : at + half + 2 * HALO], lambda o: kern[31 - o : 32 - o, lanes], half
                 )
-                frame_grad[m, part, lanes] = (cot[m, part, lanes].astype(F32) + grad).astype(BF)
+                frame_grad[m, part, lanes] = (
+                    both[count + m, part, lanes].astype(F32) + grad
+                ).astype(BF)
         return 0
 
     lax.fori_loop(0, count, step, 0)
@@ -362,31 +361,33 @@
     def swap(x, mask):
         return permute(x, [(f, f ^ mask) for f in range(groups * blocks)])
 
-    def passed_on(x, axis):
-        x = lax.dynamic_slice_in_dim(x, (1 - odd) * HALO, HALO, axis=axis)
-        pairs = [(t, t + 2) if t % 2 == 0 else (t + 2, t) for t in range(blocks - 2)]
-        return permute(
-            x, [(m * blocks + i, m * blocks + j) for m in range(groups) for i, j in pairs]
-        )
+    def swap_beyond(x):
+        pairs = [(m * blocks + t, m * blocks + t + 1)
+                 for m in range(groups) for t in range(1, blocks - 1, 2)]
+        return permute(x, pairs + [(j, i) for i, j in pairs])
 
     def spread(parts):
         masks = (0, over_core, over_y, over_core + over_y)
         got = {d: swap(parts[d], masks[d]) for d in (2, 3, 1)}
         return [parts[0], got[1], got[2], got[3]]
 
-    frame_x = swap(
-        jnp.concatenate([frames[:, :HALO], frames[:, length - HALO :]], axis=1), over_x
-    )
-    frame_z = passed_on(frame_x, 1)
+    last = length - HALO
+    frame_x = swap(lax.dynamic_slice_in_dim(frames, (1 - odd) * last, HALO, axis=1), over_x)
+    frame_z = swap_beyond(lax.dynamic_slice_in_dim(frames, odd * last, HALO, axis=1))
+    both = jnp.concatenate([frames, cotangent])
+    taps_in = jnp.pad(kernel, ((0, 1), (0, 0)))
     cot_parts = spread(
-        [lax.dynamic_slice_in_dim(cotangent, (mic ^ d) * sub, sub, axis=1) for d in range(4)]
+        [
+            lax.dynamic_slice(both, (count, (mic ^ d) * sub, 0), (count, sub, width))
+            for d in range(4)
+        ]
     )
     block = shape((count, sub, width), BF)
     wide = shape(frames.shape, F32)
     here = pltpu.VMEM(frames.shape, BF)
     conv, *acted = call(
         functools.partial(conv_kernel, sub), (wide,) + (block,) * 4, [here],
-        8, bits, frames, frame_x, frame_z, kernel,
+        8, bits, both, frame_x, frame_z, taps_in,
     )
     own_acted, *weights = lax.optimization_barrier(
         (acted[0], w_query, w_key, w_value, w_out)
@@ -436,50 +437,47 @@
     plan = (count, sub, cols)
     y_got = after(y_got, (a[-1], b[-1]))
     home = (bits, back_keep, core_got, y_got)
-    dconv, edges = call(
-        functools.partial(dconv_kernel, plan), (wide, flat(2 * count * cols * HALO)), [], 8,
-        *home, conv,
+    edge = flat(count * cols * HALO)
+    dconv, x_edge, z_edge = call(
+        functools.partial(dconv_kernel, plan), (wide, edge, edge), [], 8, *home, conv
     )
     a = halved(a, over_y)
     b = halved(b, over_x)
+    a = halved(a, lines[1])
     (taps,) = call(
         functools.partial(tap_kernel, sub), (flat(32 * cols),),
         [pltpu.VMEM((count, length + 2 * HALO, width), F32)],
-        8, bits, frames, frame_x, frame_z, after(dconv, a[-1]),
+        8, bits, both, frame_x, frame_z, after(dconv, a[-1]),
     )
     n = taps.shape[0]
-    got = swap(jnp.concatenate([taps, edges]), over_x)
+    got = swap(jnp.concatenate([taps, x_edge]), over_x)
     taps, x_edge = total(taps, got[:n]), got[n:]
-    z_edge = passed_on(x_edge.reshape(count * cols, 2 * HALO, LANES), 1).reshape(-1, LANES)
-    k = a[0].shape[0] // 2
-    got = swap(jnp.concatenate([total(*(t[k:] for t in a)), taps]), lines[1])
-    a = total(*(t[:k] for t in a), got[:k])
-    taps = total(taps, got[k:])
-    a = exchanged(jnp.concatenate([a, taps]), lines[:1] + lines[2:])
-    a, taps = a[:k], a[k:]
+
+    def doubled_with(x, taps, mask):
+        got = swap(jnp.concatenate([x, taps]), mask)
+        return jnp.concatenate([x, got[: x.shape[0]]]), total(taps, got[x.shape[0] :])
+
+    a = exchanged(total(*a), lines[:1] + lines[2:])
     b = exchanged(total(*halved(b, over_y)), lines[1:])
-    a = doubled(after(a, z_edge), lines[1])
-    got = swap(jnp.concatenate([b, taps]), over_y)
-    k = b.shape[0]
-    b, taps = jnp.concatenate([b, got[:k]]), total(taps, got[k:])
-    (frame_grad,) = call(
-        frame_kernel, (shape(frames.shape, BF),), [], 8,
-        bits, after(dconv, a), x_edge, z_edge, cotangent, kernel,
-    )
+    z_edge = swap_beyond(after(z_edge, a))
+    a, taps = doubled_with(a, taps, lines[1])
+    for mask in lines[2:]:
+        taps = total(taps, swap(taps, mask))
+    b = doubled(b, over_y)
     (layer_out,) = call(
         functools.partial(layer_kernel, plan), (shape(frames.shape, BF),), [here],
-        10, *home, after(frames, a), weights,
-    )
-    a = doubled(a, over_y)
+        10, *home, after(both, a), weights,
+    )
+    a, taps = doubled_with(a, taps, over_y)
     b = doubled(b, over_x)
 
     norm = 1.0 / math.sqrt(groups * count * blocks * length)
     square = shape((width, width), F32)
 
     def final(kinds, parts, grads, taps=()):
-        first = 1 + len(parts)
+        first = 1 + len(parts) + len(taps)
         return call(
-            functools.partial(final_kernel, (kinds, not grads, width, norm)),
+            functools.partial(final_kernel, (kinds, not grads, bool(taps), width, norm)),
             (square,) * 4 + (shape((31, width), F32),) * len(taps),
             [
                 pltpu.VMEM((4 * len(kinds), part // 8, LANES), F32),
@@ -489,20 +487,24 @@
             hbm_outs=range(4), aliases={first + i: i for i in range(len(grads))},
         )
 
-    a_far, b_far = swap(a, over_x), swap(b, lines[0])
-    a_other, b_other = after((jnp.concatenate([a, taps]), b), frame_grad)
+    a_far, b_far = swap(a, over_x), swap(jnp.concatenate([b, taps]), lines[0])
+    (frame_grad,) = call(
+        frame_kernel, (shape(frames.shape, BF),), [], 8,
+        bits, after(dconv, (a, b)), x_edge, z_edge, both, taps_in,
+    )
+    a_other, b_other = after((a, b), frame_grad)
     a_other, b_other = swap(a_other, over_core), swap(b_other, over_core)
-    k = a.shape[0]
-    taps = total(taps, a_other[k:])
-    *grads, kernel_grad = final(
-        ((1, 0, 0), (1, 1, 0), (0, 0, 0), (0, 1, 0)), (a, b, a_other, b_other), (), (taps,)
-    )
+    grads = final(((1, 0, 0), (1, 1, 0), (0, 0, 0), (0, 1, 0)), (a, b, a_other, b_other), ())
     a_far, b_far, frame_grad, layer_out, *grads = lax.optimization_barrier(
         (a_far, b_far, frame_grad, layer_out, *grads)
     )
-    a_other, b_other = swap(a_far, over_core), swap(b_far, over_core)
+    k = b.shape[0]
+    taps = total(taps, b_far[k:])
+    a_other = swap(a_far, over_core)
+    b_other = swap(jnp.concatenate([b_far[:k], taps]), over_core)
+    taps = total(taps, b_other[k:])
     grads = final(((1, 0, 1), (1, 1, 1)), (a_far, b_far), grads)
-    grads = final(((0, 0, 1), (0, 1, 1)), (a_other, b_other), grads)
+    *grads, kernel_grad = final(((0, 0, 1), (0, 1, 1)), (a_other, b_other), grads, (taps,))
     return (layer_out, frame_grad, kernel_grad, *grads)
 
 

time: 96.5 us -> 91.3 us (0.946)
  starting transfers between devices: 41.5 us -> 33.8 us
  waiting for transfers between devices: 25.6 us -> 29.5 us
  other arithmetic: 2.42 us -> 0.94 us
    ppermute x32, starting transfers between devices: 41.5 us -> 33.8 us  [permute(): return lax.ppermute(x, ('mic', 'tm'), pairs)]
    ppermute x32, waiting for transfers between devices: 25.6 us -> 29.5 us  [permute(): return lax.ppermute(x, ('mic', 'tm'), pairs)]
    another operation x1, other arithmetic: 1.78 us -> 0.26 us  [shards(): weights = jnp.stack(weights)]
  transfers between devices with their start and end apart: 32 -> 32, of which waited for: 14 -> 12; matrix products, arithmetic and copies ran while one was open for 4% -> 3% of each run, Pallas kernels for 15% -> 15%
where the time goes in v10:
time: 91.3 us; the launch traced here: 91 us
  starting transfers between devices  33.8 us (37%)
  waiting for transfers between devices  29.5 us (32%)
  Pallas kernels  21.8 us (24%)
  local copies, waits for them, and re-layouts  3.89 us (4%)
  between operations  1.11 us (1%)
  other arithmetic  0.94 us (1%)
    ppermute x32, starting transfers between devices, permute(): return lax.ppermute(x, ('mic', 'tm'), pairs)  33.8 us
    ppermute x32, waiting for transfers between devices, permute(): return lax.ppermute(x, ('mic', 'tm'), pairs)  29.5 us
    pallas_call x9, Pallas kernels, call(): pl.pallas_call(body, out_shape=outs, in_specs=[pl.BlockSpec(memory_space=...  21.8 us
  transfers between devices with their start and end apart: 32, of which 12 were waited for; matrix products, arithmetic and copies ran while one was open for 3% of the time, Pallas kernels for 15%

profile of v10, /device:TPU:0, one launch (start us, length us, event | category | flops | bytes accessed | tf_op | source)
XLA Modules:
  0.0 91.0 jit_solution(10866341028800773632)
XLA Ops:
  0.7 1.1 %constant_dynamic-update-slice_fusion.1 = bf16[4,128,512]{2,1,0:T(8,128)(2,1)S(1)} fusion(bf16[2,128,512]{2,1,0:T(8,128)(2,1)} %param.7), kind=kLoop, calls=%fused_computation.26 | loop fusion | bytes 524288
  1.8 1.0 %constant_dynamic-update-slice_fusion.frames.both = bf16[4,128,512]{2,1,0:T(8,128)(2,1)S(1)} fusion(bf16[4,128,512]{2,1,0:T(8,128)(2,1)S(1)} %constant_dynamic-update-slice_fusion.1, bf16[2,128,512]{2,1,0:T(8,128)(2,1)} %param.8), kind=kLoop, calls=%fused_computation.25 | loop fusion | bytes 524288 | tf_op jit(solution)/shard_map/concatenate | solution.py:377
  2.8 0.5 collective-permute-start.5
  3.3 0.8 constant_dynamic-slice_fusion.4
  4.1 2.5 %collective-permute-start = (bf16[2,16,512]{2,1,0:T(8,128)(2,1)S(1)}, bf16[2,16,512]{2,1,0:T(8,128)(2,1)S(1)}, u32[]{:S(2)}, u32[]{:S(2)}) collective-permute-start(bf16[2,16,512]{2,1,0:T(8,128)(2,1)S(1)} %get-tuple-element.104), channel_id=1, source_target_pairs={{0,1},{1,0},{2,3},{3,2},{4,5},{5,4},{6,7},{7,6},{8,9},{9,8},{10,11... | collective-permute-start | bytes 98312 | tf_op jit(solution)/shard_map/ppermute | solution.py:359
  6.7 0.7 collective-permute-start.1
  7.3 1.6 %collective-permute-start.6 = (bf16[2,32,512]{2,1,0:T(8,128)(2,1)S(1)}, bf16[2,32,512]{2,1,0:T(8,128)(2,1)S(1)}, u32[]{:S(2)}, u32[]{:S(2)}) collective-permute-start(bf16[2,32,512]{2,1,0:T(8,128)(2,1)S(1)} %get-tuple-element.100), channel_id=1, source_target_pairs={{0,16},{1,17},{2,18},{3,19},{4,20},{5,21},{6,22},{7,23},{8,24},{9,... | collective-permute-start | bytes 196616 | tf_op jit(solution)/shard_map/ppermute | solution.py:359
  8.9 0.8 pad.4.kern
  9.9 2.2 %shard_map.126 = (f32[2,128,512]{2,1,0:T(8,128)S(1)}, bf16[2,32,512]{2,1,0:T(8,128)(2,1)S(1)}, bf16[2,32,512]{2,1,0:T(8,128)(2,1)S(1)}, bf16[2,32,512]{2,1,0:T(8,128)(2,1)S(1)}, bf16[2,32,512]{2,1,0:T(8,128)(2,1)S(1)}) custom-call(s32[9]{0:T(128)S(1)} %stack.54.bits, bf16[4,128,512]{2,1,0:T(8,128)(2,1)S(1)} %constant_dynamic-update-slice_fusion.frames.both, ...), custom_call_target="tpu_custom_call" | custom-call | tf_op jit(solution)/shard_map/pallas_call | solution.py:324
  12.1 0.7 collective-permute-start.2
  12.7 1.5 %collective-permute-start.3 = (bf16[2,32,512]{2,1,0:T(8,128)(2,1)S(1)}, bf16[2,32,512]{2,1,0:T(8,128)(2,1)S(1)}, u32[]{:S(2)}, u32[]{:S(2)}) collective-permute-start(bf16[2,32,512]{2,1,0:T(8,128)(2,1)S(1)} %get-tuple-element.56), channel_id=1, source_target_pairs={{0,16},{1,17},{2,18},{3,19},{4,20},{5,21},{6,22},{7,23},{8,24},{9,... | collective-permute-start | bytes 196616 | tf_op jit(solution)/shard_map/ppermute | solution.py:359
  14.3 0.3 pad_maximum_fusion.weights
  14.6 2.4 %collective-permute-done.3.a2 = bf16[2,32,512]{2,1,0:T(8,128)(2,1)S(1)} collective-permute-done((bf16[2,32,512]{2,1,0:T(8,128)(2,1)S(1)}, bf16[2,32,512]{2,1,0:T(8,128)(2,1)S(1)}, u32[]{:S(2)}, u32[]{:S(2)}) %collective-permute-start.3) | collective-permute-done | bytes 65568 | tf_op jit(solution)/shard_map/ppermute | solution.py:359
  17.0 1.6 %collective-permute-done.4.a3 = bf16[2,32,512]{2,1,0:T(8,128)(2,1)S(1)} collective-permute-done((bf16[2,32,512]{2,1,0:T(8,128)(2,1)S(1)}, bf16[2,32,512]{2,1,0:T(8,128)(2,1)S(1)}, u32[]{:S(2)}, u32[]{:S(2)}) %collective-permute-start.4) | collective-permute-done | bytes 65568 | tf_op jit(solution)/shard_map/ppermute | solution.py:359
  18.6 5.8 %shard_map.127 = (bf16[2048,128]{1,0:T(8,128)(2,1)S(1)}, bf16[2048,128]{1,0:T(8,128)(2,1)S(1)}, bf16[2048,128]{1,0:T(8,128)(2,1)S(1)}, bf16[2048,128]{1,0:T(8,12...) custom-call(s32[9]{0:T(128)S(1)} %stack.54.bits, ...), custom_call_target="tpu_custom_call" | custom-call | tf_op jit(solution)/shard_map/pallas_call | solution.py:324
  24.6 0.4 collective-permute-start.13
  25.2 1.7 %collective-permute-done.13.core_got = bf16[1024,128]{1,0:T(8,128)(2,1)S(1)} collective-permute-done((bf16[1024,128]{1,0:T(8,128)(2,1)S(1)}, bf16[1024,128]{1,0:T(8,128)(2,1)S(1)}, u32[]{:S(2)}, u32[]{:S(2)}) %collective-permute-start.13) | collective-permute-done | bytes 262176 | tf_op jit(solution)/shard_map/ppermute | solution.py:359
  26.9 0.8 collective-permute-start.14
  27.7 4.3 %collective-permute-start.9 = (bf16[1024,128]{1,0:T(8,128)(2,1)S(1)}, bf16[1024,128]{1,0:T(8,128)(2,1)S(1)}, u32[]{:S(2)}, u32[]{:S(2)}) collective-permute-start(bf16[1024,128]{1,0:T(8,128)(2,1)S(1)} %add_convert_fusion.1), channel_id=1, source_target_pairs={{0,1},{1,0},{2,3},{3,2},{4,5},{5,4},{6,7},{7,6},{8,9},{9,8},{10,11... | collective-permute-start | bytes 786440 | tf_op jit(solution)/shard_map/ppermute | solution.py:359
  32.1 1.7 %collective-permute-start.16 = (bf16[1024,128]{1,0:T(8,128)(2,1)S(1)}, bf16[1024,128]{1,0:T(8,128)(2,1)S(1)}, u32[]{:S(2)}, u32[]{:S(2)}) collective-permute-start(bf16[1024,128]{1,0:T(8,128)(2,1)S(1)} %add_convert_fusion), channel_id=1, source_target_pairs={{0,2},{1,3},{2,0},{3,1},{4,6},{5,7},{6,4},{7,5},{8,10},{9,11},{10,... | collective-permute-start | bytes 786440 | tf_op jit(solution)/shard_map/ppermute | solution.py:359
  33.8 4.8 %collective-permute-done.9 = bf16[1024,128]{1,0:T(8,128)(2,1)S(1)} collective-permute-done((bf16[1024,128]{1,0:T(8,128)(2,1)S(1)}, bf16[1024,128]{1,0:T(8,128)(2,1)S(1)}, u32[]{:S(2)}, u32[]{:S(2)}) %collective-permute-start.9) | collective-permute-done | bytes 262176 | tf_op jit(solution)/shard_map/ppermute | solution.py:359
  38.7 1.2 %collective-permute-start.10 = (bf16[512,128]{1,0:T(8,128)(2,1)S(1)}, bf16[512,128]{1,0:T(8,128)(2,1)S(1)}, u32[]{:S(2)}, u32[]{:S(2)}) collective-permute-start(bf16[512,128]{1,0:T(8,128)(2,1)S(1)} %add_convert_fusion.3), channel_id=1, source_target_pairs={{0,16},{1,17},{2,18},{3,19},{4,20},{5,21},{6,22},{7,23},{8,24},{9,... | collective-permute-start | bytes 393224 | tf_op jit(solution)/shard_map/ppermute | solution.py:359
  39.8 0.4 collective-permute-done.16
  40.3 1.4 %collective-permute-start.21 = (bf16[512,128]{1,0:T(8,128)(2,1)S(1)}, bf16[512,128]{1,0:T(8,128)(2,1)S(1)}, u32[]{:S(2)}, u32[]{:S(2)}) collective-permute-start(bf16[512,128]{1,0:T(8,128)(2,1)S(1)} %add_convert_fusion.2), channel_id=1, source_target_pairs={{0,1},{1,0},{2,3},{3,2},{4,5},{5,4},{6,7},{7,6},{8,9},{9,8},{10,11... | collective-permute-start | bytes 393224 | tf_op jit(solution)/shard_map/ppermute | solution.py:359
  41.7 0.7 shard_map.128
  42.5 1.2 %collective-permute-done.10 = bf16[512,128]{1,0:T(8,128)(2,1)S(1)} collective-permute-done((bf16[512,128]{1,0:T(8,128)(2,1)S(1)}, bf16[512,128]{1,0:T(8,128)(2,1)S(1)}, u32[]{:S(2)}, u32[]{:S(2)}) %collective-permute-start.10) | collective-permute-done | bytes 131104 | tf_op jit(solution)/shard_map/ppermute | solution.py:359
  43.7 3.3 %collective-permute-start.11 = (bf16[256,128]{1,0:T(8,128)(2,1)S(1)}, bf16[256,128]{1,0:T(8,128)(2,1)S(1)}, u32[]{:S(2)}, u32[]{:S(2)}) collective-permute-start(bf16[256,128]{1,0:T(8,128)(2,1)S(1)} %add_convert_fusion.9), channel_id=1, source_target_pairs={{0,4},{1,5},{2,6},{3,7},{4,0},{5,1},{6,2},{7,3},{8,12},{9,13},{10,... | collective-permute-start | bytes 196616 | tf_op jit(solution)/shard_map/ppermute | solution.py:359
  47.1 0.6 collective-permute-start.22
  47.7 1.6 %collective-permute-done.11 = bf16[256,128]{1,0:T(8,128)(2,1)S(1)} collective-permute-done((bf16[256,128]{1,0:T(8,128)(2,1)S(1)}, bf16[256,128]{1,0:T(8,128)(2,1)S(1)}, u32[]{:S(2)}, u32[]{:S(2)}) %collective-permute-start.11) | collective-permute-done | bytes 65568 | tf_op jit(solution)/shard_map/ppermute | solution.py:359
  49.4 2.0 %collective-permute-start.12 = (bf16[256,128]{1,0:T(8,128)(2,1)S(1)}, bf16[256,128]{1,0:T(8,128)(2,1)S(1)}, u32[]{:S(2)}, u32[]{:S(2)}) collective-permute-start(bf16[256,128]{1,0:T(8,128)(2,1)S(1)} %add_convert_fusion.8), channel_id=1, source_target_pairs={{0,2},{1,3},{2,0},{3,1},{4,6},{5,7},{6,4},{7,5},{8,10},{9,11},{10,... | collective-permute-start | bytes 196616 | tf_op jit(solution)/shard_map/ppermute | solution.py:359
  51.5 3.2 %collective-permute-start.23 = (bf16[256,128]{1,0:T(8,128)(2,1)S(1)}, bf16[256,128]{1,0:T(8,128)(2,1)S(1)}, u32[]{:S(2)}, u32[]{:S(2)}) collective-permute-start(bf16[256,128]{1,0:T(8,128)(2,1)S(1)} %add_convert_fusion.5), channel_id=1, source_target_pairs={{0,4},{1,5},{2,6},{3,7},{4,0},{5,1},{6,2},{7,3},{8,12},{9,13},{10,... | collective-permute-start | bytes 196616 | tf_op jit(solution)/shard_map/ppermute | solution.py:359
  54.7 2.8 %shard_map.129 = bf16[128,128]{1,0:T(8,128)(2,1)S(1)} custom-call(s32[9]{0:T(128)S(1)} %stack.54.bits, bf16[4,128,512]{2,1,0:T(8,128)(2,1)S(1)} %constant_dynamic-update-slice_fusion.frames.both, bf16[2,16,512]{2,1,0:T(8,128)(2,1)S(1)} %collective-permute-done.x_got, bf16[2,16,512]{2,1,0:T(8,128)(2,1)S(1)} %collective-permute-done.1.z_got, ...), custom_call_target="tpu_custom_call" | custom-call | tf_op jit(solution)/shard_map/pallas_call | solution.py:324
  57.7 0.7 collective-permute-start.24
  58.4 3.8 %collective-permute-done.17 = bf16[256,128]{1,0:T(8,128)(2,1)S(1)} collective-permute-done((bf16[256,128]{1,0:T(8,128)(2,1)S(1)}, bf16[256,128]{1,0:T(8,128)(2,1)S(1)}, u32[]{:S(2)}, u32[]{:S(2)}) %collective-permute-start.17) | collective-permute-done | bytes 65568 | tf_op jit(solution)/shard_map/ppermute | solution.py:359
  62.4 1.7 %collective-permute-start.25 = (bf16[512,128]{1,0:T(8,128)(2,1)S(1)}, bf16[512,128]{1,0:T(8,128)(2,1)S(1)}, u32[]{:S(2)}, u32[]{:S(2)}) collective-permute-start(bf16[512,128]{1,0:T(8,128)(2,1)S(1)} %pad_maximum_fusion.7), channel_id=1, source_target_pairs={{0,1},{1,0},{2,3},{3,2},{4,5},{5,4},{6,7},{7,6},{8,9},{9,8},{10,11... | collective-permute-start | bytes 393224 | tf_op jit(solution)/shard_map/ppermute | solution.py:359
  64.1 4.9 %collective-permute-done.18 = bf16[384,128]{1,0:T(8,128)(2,1)S(1)} collective-permute-done((bf16[384,128]{1,0:T(8,128)(2,1)S(1)}, bf16[384,128]{1,0:T(8,128)(2,1)S(1)}, u32[]{:S(2)}, u32[]{:S(2)}) %collective-permute-start.18) | collective-permute-done | bytes 98336 | tf_op jit(solution)/shard_map/ppermute | solution.py:359
  69.1 0.7 collective-permute-start.19
  69.8 0.7 collective-permute-start.27
  70.5 4.0 %collective-permute-done.19 = bf16[640,128]{1,0:T(8,128)(2,1)S(1)} collective-permute-done((bf16[640,128]{1,0:T(8,128)(2,1)S(1)}, bf16[640,128]{1,0:T(8,128)(2,1)S(1)}, u32[]{:S(2)}, u32[]{:S(2)}) %collective-permute-start.19) | collective-permute-done | bytes 163872 | tf_op jit(solution)/shard_map/ppermute | solution.py:359
  74.6 2.8 %shard_map.130 = bf16[2,128,512]{2,1,0:T(8,128)(2,1)} custom-call(s32[9]{0:T(128)S(1)} %stack.54.bits, f32[2,128,512]{2,1,0:T(8,128)S(1)} %get-tuple-element.73.dconv, bf16[128,128]{1,0:T(8,128)(2,1)S(1)} %slice.202.x_got, bf16[128,128]{1,0:T(8,128)(2,1)S(1)} %collective-permute-done.27.z_got, ...), custom_call_target="tpu_custom_call" | custom-call | tf_op jit(solution)/shard_map/pallas_call | solution.py:324
  77.5 0.5 collective-permute-start.29
  78.0 2.0 %collective-permute-start.20 = (bf16[1024,128]{1,0:T(8,128)(2,1)S(1)}, bf16[1024,128]{1,0:T(8,128)(2,1)S(1)}, u32[]{:S(2)}, u32[]{:S(2)}) collective-permute-start(bf16[1024,128]{1,0:T(8,128)(2,1)S(1)} %pad_maximum_fusion.4.refs_0_), channel_id=1, source_target_pairs={{0,1},{1,0},{2,3},{3,2},{4,5},{5,4},{6,7},{7,6},{8,9},{9,8},{10,11... | collective-permute-start | bytes 786440 | tf_op jit(solution)/shard_map/ppermute | solution.py:359
  80.0 1.6 %shard_map.131 = bf16[2,128,512]{2,1,0:T(8,128)(2,1)} custom-call(s32[9]{0:T(128)S(1)} %stack.54.bits, bf16[1024,128]{1,0:T(8,128)(2,1)S(1)} %get-tuple-element.64.own, bf16[1024,128]{1,0:T(8,128)(2,1)S(1)} %collective-permute-done.13.core_got, bf16[1024,128]{1,0:T(8,128)(2,1)S(1)} %collective-permute-done.14.y_got, ...), custom_call_target="tpu_custom_call" | custom-call | tf_op jit(solution)/shard_map/pallas_call | solution.py:324
  81.6 2.0 %shard_map.132 = (f32[512,512]{1,0:T(8,128)}, f32[512,512]{1,0:T(8,128)}, f32[512,512]{1,0:T(8,128)}, f32[512,512]{1,0:T(8,128)}) custom-call(s32[9]{0:T(128)S(1)} %stack.54.bits, bf16[1024,128]{1,0:T(8,128)(2,1)S(1)} %pad_maximum_fusion.4.refs_0_, bf16[1024,128]{1,0:T(8,128)(2,1)S(1)} %pad_maximum_fusion.5.refs_1_, ...), custom_call_target="tpu_custom_call" | custom-call | tf_op jit(solution)/shard_map/pallas_call | solution.py:324
  83.6 2.9 %collective-permute-done.20.refs_0_ = bf16[1024,128]{1,0:T(8,128)(2,1)S(1)} collective-permute-done((bf16[1024,128]{1,0:T(8,128)(2,1)S(1)}, bf16[1024,128]{1,0:T(8,128)(2,1)S(1)}, u32[]{:S(2)}, u32[]{:S(2)}) %collective-permute-start.20) | collective-permute-done | bytes 262176 | tf_op jit(solution)/shard_map/ppermute | solution.py:359
  86.6 0.5 collective-permute-start.30
  87.1 1.6 %shard_map.133 = (f32[512,512]{1,0:T(8,128)}, f32[512,512]{1,0:T(8,128)}, f32[512,512]{1,0:T(8,128)}, f32[512,512]{1,0:T(8,128)}) custom-call(s32[9]{0:T(128)S(1)} %stack.54.bits, bf16[1024,128]{1,0:T(8,128)(2,1)S(1)} %collective-permute-done.20.refs_0_, ...), custom_call_target="tpu_custom_call", output_to_operand_aliasing={{0}: (3, {}), {1}: (4, {}), {2}: (5, {}), {3}: (6, {})} | custom-call | tf_op jit(solution)/shard_map/pallas_call | solution.py:324
  88.7 2.2 %shard_map.134 = (f32[512,512]{1,0:T(8,128)}, f32[512,512]{1,0:T(8,128)}, f32[512,512]{1,0:T(8,128)}, f32[512,512]{1,0:T(8,128)}, f32[31,512]{1,0:T(8,128)}) custom-call(s32[9]{0:T(128)S(1)} %stack.54.bits, bf16[1024,128]{1,0:T(8,128)(2,1)S(1)} %collective-permute-done.30.refs_0_, ...), custom_call_target="tpu_custom_call", output_to_operand_aliasing={{0}: (4, {}), {1}: (5, {}), {2}: (6, {}), {3}: (7, {})} | custom-call | tf_op jit(solution)/shard_map/pallas_call | solution.py:324
  (70 shorter events, 1.6 us)
Async XLA Ops:
  0.6 13.6 %copy-start.3 = (bf16[512,512]{1,0:T(8,128)(2,1)S(1)}, bf16[512,512]{1,0:T(8,128)(2,1)}, u32[]{:S(2)}) copy-start(bf16[512,512]{1,0:T(8,128)(2,1)} %param.10) | copy-start | bytes 1572868
  0.6 13.6 %copy-start.2 = (bf16[512,512]{1,0:T(8,128)(2,1)S(1)}, bf16[512,512]{1,0:T(8,128)(2,1)}, u32[]{:S(2)}) copy-start(bf16[512,512]{1,0:T(8,128)(2,1)} %param.11) | copy-start | bytes 1572868
  0.7 13.6 %copy-start.1 = (bf16[512,512]{1,0:T(8,128)(2,1)S(1)}, bf16[512,512]{1,0:T(8,128)(2,1)}, u32[]{:S(2)}) copy-start(bf16[512,512]{1,0:T(8,128)(2,1)} %param.12) | copy-start | bytes 1572868
  0.7 13.6 %copy-start = (bf16[512,512]{1,0:T(8,128)(2,1)S(1)}, bf16[512,512]{1,0:T(8,128)(2,1)}, u32[]{:S(2)}) copy-start(bf16[512,512]{1,0:T(8,128)(2,1)} %param.13) | copy-start | bytes 1572868
  2.8 11.4 %collective-permute-start.5 = (bf16[2,32,512]{2,1,0:T(8,128)(2,1)S(1)}, bf16[2,32,512]{2,1,0:T(8,128)(2,1)S(1)}, u32[]{:S(2)}, u32[]{:S(2)}) collective-permute-start(bf16[2,32,512]{2,1,0:T(8,128)(2,1)S(1)} %get-tuple-element.101), channel_id=1, source_target_pairs={{0,8},{1,9},{2,10},{3,11},{4,12},{5,13},{6,14},{7,15},{8,0},{9,1},... | collective-permute-start | bytes 196616 | tf_op jit(solution)/shard_map/ppermute | solution.py:359
  4.1 5.7 %collective-permute-start = (bf16[2,16,512]{2,1,0:T(8,128)(2,1)S(1)}, bf16[2,16,512]{2,1,0:T(8,128)(2,1)S(1)}, u32[]{:S(2)}, u32[]{:S(2)}) collective-permute-start(bf16[2,16,512]{2,1,0:T(8,128)(2,1)S(1)} %get-tuple-element.104), channel_id=1, source_target_pairs={{0,1},{1,0},{2,3},{3,2},{4,5},{5,4},{6,7},{7,6},{8,9},{9,8},{10,11... | collective-permute-start | bytes 98312 | tf_op jit(solution)/shard_map/ppermute | solution.py:359
  6.7 3.2 %collective-permute-start.1 = (bf16[2,16,512]{2,1,0:T(8,128)(2,1)S(1)}, bf16[2,16,512]{2,1,0:T(8,128)(2,1)S(1)}, u32[]{:S(2)}, u32[]{:S(2)}) collective-permute-start(bf16[2,16,512]{2,1,0:T(8,128)(2,1)S(1)} %get-tuple-element.103), channel_id=1, source_target_pairs={{1,2},{3,4},{5,6},{9,10},{11,12},{13,14},{17,18},{19,20},{21,22},{... | collective-permute-start | bytes 98312 | tf_op jit(solution)/shard_map/ppermute | solution.py:359
  7.3 7.3 %collective-permute-start.6 = (bf16[2,32,512]{2,1,0:T(8,128)(2,1)S(1)}, bf16[2,32,512]{2,1,0:T(8,128)(2,1)S(1)}, u32[]{:S(2)}, u32[]{:S(2)}) collective-permute-start(bf16[2,32,512]{2,1,0:T(8,128)(2,1)S(1)} %get-tuple-element.100), channel_id=1, source_target_pairs={{0,16},{1,17},{2,18},{3,19},{4,20},{5,21},{6,22},{7,23},{8,24},{9,... | collective-permute-start | bytes 196616 | tf_op jit(solution)/shard_map/ppermute | solution.py:359
  8.9 5.7 %collective-permute-start.7 = (bf16[2,32,512]{2,1,0:T(8,128)(2,1)S(1)}, bf16[2,32,512]{2,1,0:T(8,128)(2,1)S(1)}, u32[]{:S(2)}, u32[]{:S(2)}) collective-permute-start(bf16[2,32,512]{2,1,0:T(8,128)(2,1)S(1)} %get-tuple-element.99), channel_id=1, source_target_pairs={{0,24},{1,25},{2,26},{3,27},{4,28},{5,29},{6,30},{7,31},{8,16},{9,... | collective-permute-start | bytes 196616 | tf_op jit(solution)/shard_map/ppermute | solution.py:359
  12.1 2.5 %collective-permute-start.2 = (bf16[2,32,512]{2,1,0:T(8,128)(2,1)S(1)}, bf16[2,32,512]{2,1,0:T(8,128)(2,1)S(1)}, u32[]{:S(2)}, u32[]{:S(2)}) collective-permute-start(bf16[2,32,512]{2,1,0:T(8,128)(2,1)S(1)} %get-tuple-element.55), channel_id=1, source_target_pairs={{0,8},{1,9},{2,10},{3,11},{4,12},{5,13},{6,14},{7,15},{8,0},{9,1},... | collective-permute-start | bytes 196616 | tf_op jit(solution)/shard_map/ppermute | solution.py:359
  12.7 4.3 %collective-permute-start.3 = (bf16[2,32,512]{2,1,0:T(8,128)(2,1)S(1)}, bf16[2,32,512]{2,1,0:T(8,128)(2,1)S(1)}, u32[]{:S(2)}, u32[]{:S(2)}) collective-permute-start(bf16[2,32,512]{2,1,0:T(8,128)(2,1)S(1)} %get-tuple-element.56), channel_id=1, source_target_pairs={{0,16},{1,17},{2,18},{3,19},{4,20},{5,21},{6,22},{7,23},{8,24},{9,... | collective-permute-start | bytes 196616 | tf_op jit(solution)/shard_map/ppermute | solution.py:359
  14.3 4.4 %collective-permute-start.4 = (bf16[2,32,512]{2,1,0:T(8,128)(2,1)S(1)}, bf16[2,32,512]{2,1,0:T(8,128)(2,1)S(1)}, u32[]{:S(2)}, u32[]{:S(2)}) collective-permute-start(bf16[2,32,512]{2,1,0:T(8,128)(2,1)S(1)} %get-tuple-element.57), channel_id=1, source_target_pairs={{0,24},{1,25},{2,26},{3,27},{4,28},{5,29},{6,30},{7,31},{8,16},{9,... | collective-permute-start | bytes 196616 | tf_op jit(solution)/shard_map/ppermute | solution.py:359
  24.5 3.2 %collective-permute-start.8 = (bf16[2048,128]{1,0:T(8,128)(2,1)S(1)}, bf16[2048,128]{1,0:T(8,128)(2,1)S(1)}, u32[]{:S(2)}, u32[]{:S(2)}) collective-permute-start(bf16[2048,128]{1,0:T(8,128)(2,1)S(1)} %get-tuple-element.63), channel_id=1, source_target_pairs={{0,8},{1,9},{2,10},{3,11},{4,12},{5,13},{6,14},{7,15},{8,0},{9,1},... | collective-permute-start | bytes 1572872 | tf_op jit(solution)/shard_map/ppermute | solution.py:359
  24.6 2.2 %collective-permute-start.13 = (bf16[1024,128]{1,0:T(8,128)(2,1)S(1)}, bf16[1024,128]{1,0:T(8,128)(2,1)S(1)}, u32[]{:S(2)}, u32[]{:S(2)}) collective-permute-start(bf16[1024,128]{1,0:T(8,128)(2,1)S(1)} %get-tuple-element.65), channel_id=1, source_target_pairs={{0,8},{1,9},{2,10},{3,11},{4,12},{5,13},{6,14},{7,15},{8,0},{9,1},... | collective-permute-start | bytes 786440 | tf_op jit(solution)/shard_map/ppermute | solution.py:359
  25.1 7.0 %collective-permute-start.15 = (bf16[2048,128]{1,0:T(8,128)(2,1)S(1)}, bf16[2048,128]{1,0:T(8,128)(2,1)S(1)}, u32[]{:S(2)}, u32[]{:S(2)}) collective-permute-start(bf16[2048,128]{1,0:T(8,128)(2,1)S(1)} %get-tuple-element.67), channel_id=1, source_target_pairs={{0,8},{1,9},{2,10},{3,11},{4,12},{5,13},{6,14},{7,15},{8,0},{9,1},... | collective-permute-start | bytes 1572872 | tf_op jit(solution)/shard_map/ppermute | solution.py:359
  26.9 13.0 %collective-permute-start.14 = (bf16[1024,128]{1,0:T(8,128)(2,1)S(1)}, bf16[1024,128]{1,0:T(8,128)(2,1)S(1)}, u32[]{:S(2)}, u32[]{:S(2)}) collective-permute-start(bf16[1024,128]{1,0:T(8,128)(2,1)S(1)} %pad_maximum_fusion.3), channel_id=1, source_target_pairs={{0,16},{1,17},{2,18},{3,19},{4,20},{5,21},{6,22},{7,23},{8,24},{9,... | collective-permute-start | bytes 786440 | tf_op jit(solution)/shard_map/ppermute | solution.py:359
  27.7 10.9 %collective-permute-start.9 = (bf16[1024,128]{1,0:T(8,128)(2,1)S(1)}, bf16[1024,128]{1,0:T(8,128)(2,1)S(1)}, u32[]{:S(2)}, u32[]{:S(2)}) collective-permute-start(bf16[1024,128]{1,0:T(8,128)(2,1)S(1)} %add_convert_fusion.1), channel_id=1, source_target_pairs={{0,1},{1,0},{2,3},{3,2},{4,5},{5,4},{6,7},{7,6},{8,9},{9,8},{10,11... | collective-permute-start | bytes 786440 | tf_op jit(solution)/shard_map/ppermute | solution.py:359
  32.1 8.1 %collective-permute-start.16 = (bf16[1024,128]{1,0:T(8,128)(2,1)S(1)}, bf16[1024,128]{1,0:T(8,128)(2,1)S(1)}, u32[]{:S(2)}, u32[]{:S(2)}) collective-permute-start(bf16[1024,128]{1,0:T(8,128)(2,1)S(1)} %add_convert_fusion), channel_id=1, source_target_pairs={{0,2},{1,3},{2,0},{3,1},{4,6},{5,7},{6,4},{7,5},{8,10},{9,11},{10,... | collective-permute-start | bytes 786440 | tf_op jit(solution)/shard_map/ppermute | solution.py:359
  38.7 5.0 %collective-permute-start.10 = (bf16[512,128]{1,0:T(8,128)(2,1)S(1)}, bf16[512,128]{1,0:T(8,128)(2,1)S(1)}, u32[]{:S(2)}, u32[]{:S(2)}) collective-permute-start(bf16[512,128]{1,0:T(8,128)(2,1)S(1)} %add_convert_fusion.3), channel_id=1, source_target_pairs={{0,16},{1,17},{2,18},{3,19},{4,20},{5,21},{6,22},{7,23},{8,24},{9,... | collective-permute-start | bytes 393224 | tf_op jit(solution)/shard_map/ppermute | solution.py:359
  40.3 6.8 %collective-permute-start.21 = (bf16[512,128]{1,0:T(8,128)(2,1)S(1)}, bf16[512,128]{1,0:T(8,128)(2,1)S(1)}, u32[]{:S(2)}, u32[]{:S(2)}) collective-permute-start(bf16[512,128]{1,0:T(8,128)(2,1)S(1)} %add_convert_fusion.2), channel_id=1, source_target_pairs={{0,1},{1,0},{2,3},{3,2},{4,5},{5,4},{6,7},{7,6},{8,9},{9,8},{10,11... | collective-permute-start | bytes 393224 | tf_op jit(solution)/shard_map/ppermute | solution.py:359
  43.7 5.6 %collective-permute-start.11 = (bf16[256,128]{1,0:T(8,128)(2,1)S(1)}, bf16[256,128]{1,0:T(8,128)(2,1)S(1)}, u32[]{:S(2)}, u32[]{:S(2)}) collective-permute-start(bf16[256,128]{1,0:T(8,128)(2,1)S(1)} %add_convert_fusion.9), channel_id=1, source_target_pairs={{0,4},{1,5},{2,6},{3,7},{4,0},{5,1},{6,2},{7,3},{8,12},{9,13},{10,... | collective-permute-start | bytes 196616 | tf_op jit(solution)/shard_map/ppermute | solution.py:359
  47.1 4.3 %collective-permute-start.22 = (bf16[256,128]{1,0:T(8,128)(2,1)S(1)}, bf16[256,128]{1,0:T(8,128)(2,1)S(1)}, u32[]{:S(2)}, u32[]{:S(2)}) collective-permute-start(bf16[256,128]{1,0:T(8,128)(2,1)S(1)} %add_convert_fusion.6), channel_id=1, source_target_pairs={{0,16},{1,17},{2,18},{3,19},{4,20},{5,21},{6,22},{7,23},{8,24},{9,... | collective-permute-start | bytes 196616 | tf_op jit(solution)/shard_map/ppermute | solution.py:359
  49.4 9.0 %collective-permute-start.12 = (bf16[256,128]{1,0:T(8,128)(2,1)S(1)}, bf16[256,128]{1,0:T(8,128)(2,1)S(1)}, u32[]{:S(2)}, u32[]{:S(2)}) collective-permute-start(bf16[256,128]{1,0:T(8,128)(2,1)S(1)} %add_convert_fusion.8), channel_id=1, source_target_pairs={{0,2},{1,3},{2,0},{3,1},{4,6},{5,7},{6,4},{7,5},{8,10},{9,11},{10,... | collective-permute-start | bytes 196616 | tf_op jit(solution)/shard_map/ppermute | solution.py:359
  51.5 6.2 %collective-permute-start.23 = (bf16[256,128]{1,0:T(8,128)(2,1)S(1)}, bf16[256,128]{1,0:T(8,128)(2,1)S(1)}, u32[]{:S(2)}, u32[]{:S(2)}) collective-permute-start(bf16[256,128]{1,0:T(8,128)(2,1)S(1)} %add_convert_fusion.5), channel_id=1, source_target_pairs={{0,4},{1,5},{2,6},{3,7},{4,0},{5,1},{6,2},{7,3},{8,12},{9,13},{10,... | collective-permute-start | bytes 196616 | tf_op jit(solution)/shard_map/ppermute | solution.py:359
  57.6 4.7 %collective-permute-start.17 = (bf16[256,128]{1,0:T(8,128)(2,1)S(1)}, bf16[256,128]{1,0:T(8,128)(2,1)S(1)}, u32[]{:S(2)}, u32[]{:S(2)}) collective-permute-start(bf16[256,128]{1,0:T(8,128)(2,1)S(1)} %pad_maximum_fusion.9), channel_id=1, source_target_pairs={{0,1},{1,0},{2,3},{3,2},{4,5},{5,4},{6,7},{7,6},{8,9},{9,8},{10,11... | collective-permute-start | bytes 196616 | tf_op jit(solution)/shard_map/ppermute | solution.py:359
  57.7 4.7 %collective-permute-start.24 = (bf16[256,128]{1,0:T(8,128)(2,1)S(1)}, bf16[256,128]{1,0:T(8,128)(2,1)S(1)}, u32[]{:S(2)}, u32[]{:S(2)}) collective-permute-start(bf16[256,128]{1,0:T(8,128)(2,1)S(1)} %add_convert_fusion.4), channel_id=1, source_target_pairs={{0,16},{1,17},{2,18},{3,19},{4,20},{5,21},{6,22},{7,23},{8,24},{9,... | collective-permute-start | bytes 196616 | tf_op jit(solution)/shard_map/ppermute | solution.py:359
  62.3 6.8 %collective-permute-start.18 = (bf16[384,128]{1,0:T(8,128)(2,1)S(1)}, bf16[384,128]{1,0:T(8,128)(2,1)S(1)}, u32[]{:S(2)}, u32[]{:S(2)}) collective-permute-start(bf16[384,128]{1,0:T(8,128)(2,1)S(1)} %pad_maximum_fusion.8), channel_id=1, source_target_pairs={{0,4},{1,5},{2,6},{3,7},{4,0},{5,1},{6,2},{7,3},{8,12},{9,13},{10,... | collective-permute-start | bytes 294920 | tf_op jit(solution)/shard_map/ppermute | solution.py:359
  62.4 8.1 %collective-permute-start.25 = (bf16[512,128]{1,0:T(8,128)(2,1)S(1)}, bf16[512,128]{1,0:T(8,128)(2,1)S(1)}, u32[]{:S(2)}, u32[]{:S(2)}) collective-permute-start(bf16[512,128]{1,0:T(8,128)(2,1)S(1)} %pad_maximum_fusion.7), channel_id=1, source_target_pairs={{0,1},{1,0},{2,3},{3,2},{4,5},{5,4},{6,7},{7,6},{8,9},{9,8},{10,11... | collective-permute-start | bytes 393224 | tf_op jit(solution)/shard_map/ppermute | solution.py:359
  69.1 5.4 %collective-permute-start.19 = (bf16[640,128]{1,0:T(8,128)(2,1)S(1)}, bf16[640,128]{1,0:T(8,128)(2,1)S(1)}, u32[]{:S(2)}, u32[]{:S(2)}) collective-permute-start(bf16[640,128]{1,0:T(8,128)(2,1)S(1)} %pad_maximum_fusion.6), channel_id=1, source_target_pairs={{0,16},{1,17},{2,18},{3,19},{4,20},{5,21},{6,22},{7,23},{8,24},{9,... | collective-permute-start | bytes 491528 | tf_op jit(solution)/shard_map/ppermute | solution.py:359
  69.8 4.8 %collective-permute-start.27 = (bf16[128,128]{1,0:T(8,128)(2,1)S(1)}, bf16[128,128]{1,0:T(8,128)(2,1)S(1)}, u32[]{:S(2)}, u32[]{:S(2)}) collective-permute-start(bf16[128,128]{1,0:T(8,128)(2,1)S(1)} %get-tuple-element.75), channel_id=1, source_target_pairs={{1,2},{3,4},{5,6},{9,10},{11,12},{13,14},{17,18},{19,20},{21,22},{... | collective-permute-start | bytes 98312 | tf_op jit(solution)/shard_map/ppermute | solution.py:359
  74.5 11.9 %collective-permute-start.26 = (bf16[1152,128]{1,0:T(8,128)(2,1)S(1)}, bf16[1152,128]{1,0:T(8,128)(2,1)S(1)}, u32[]{:S(2)}, u32[]{:S(2)}) collective-permute-start(bf16[1152,128]{1,0:T(8,128)(2,1)S(1)} %pad_maximum_fusion.1), channel_id=1, source_target_pairs={{0,2},{1,3},{2,0},{3,1},{4,6},{5,7},{6,4},{7,5},{8,10},{9,11},{10,... | collective-permute-start | bytes 884744 | tf_op jit(solution)/shard_map/ppermute | solution.py:359
  77.5 4.1 %collective-permute-start.28 = (bf16[1024,128]{1,0:T(8,128)(2,1)S(1)}, bf16[1024,128]{1,0:T(8,128)(2,1)S(1)}, u32[]{:S(2)}, u32[]{:S(2)}) collective-permute-start(bf16[1024,128]{1,0:T(8,128)(2,1)S(1)} %pad_maximum_fusion.4.refs_0_), channel_id=1, source_target_pairs={{0,8},{1,9},{2,10},{3,11},{4,12},{5,13},{6,14},{7,15},{8,0},{9,1},... | collective-permute-start | bytes 786440 | tf_op jit(solution)/shard_map/ppermute | solution.py:359
  77.5 4.1 %collective-permute-start.29 = (bf16[1024,128]{1,0:T(8,128)(2,1)S(1)}, bf16[1024,128]{1,0:T(8,128)(2,1)S(1)}, u32[]{:S(2)}, u32[]{:S(2)}) collective-permute-start(bf16[1024,128]{1,0:T(8,128)(2,1)S(1)} %pad_maximum_fusion.5.refs_1_), channel_id=1, source_target_pairs={{0,8},{1,9},{2,10},{3,11},{4,12},{5,13},{6,14},{7,15},{8,0},{9,1},... | collective-permute-start | bytes 786440 | tf_op jit(solution)/shard_map/ppermute | solution.py:359
  78.0 8.5 %collective-permute-start.20 = (bf16[1024,128]{1,0:T(8,128)(2,1)S(1)}, bf16[1024,128]{1,0:T(8,128)(2,1)S(1)}, u32[]{:S(2)}, u32[]{:S(2)}) collective-permute-start(bf16[1024,128]{1,0:T(8,128)(2,1)S(1)} %pad_maximum_fusion.4.refs_0_), channel_id=1, source_target_pairs={{0,1},{1,0},{2,3},{3,2},{4,5},{5,4},{6,7},{7,6},{8,9},{9,8},{10,11... | collective-permute-start | bytes 786440 | tf_op jit(solution)/shard_map/ppermute | solution.py:359
  86.5 2.2 %collective-permute-start.31 = (bf16[1152,128]{1,0:T(8,128)(2,1)S(1)}, bf16[1152,128]{1,0:T(8,128)(2,1)S(1)}, u32[]{:S(2)}, u32[]{:S(2)}) collective-permute-start(bf16[1152,128]{1,0:T(8,128)(2,1)S(1)} %pad_maximum_fusion.2), channel_id=1, source_target_pairs={{0,8},{1,9},{2,10},{3,11},{4,12},{5,13},{6,14},{7,15},{8,0},{9,1},... | collective-permute-start | bytes 884744 | tf_op jit(solution)/shard_map/ppermute | solution.py:359
  86.6 2.1 %collective-permute-start.30 = (bf16[1024,128]{1,0:T(8,128)(2,1)S(1)}, bf16[1024,128]{1,0:T(8,128)(2,1)S(1)}, u32[]{:S(2)}, u32[]{:S(2)}) collective-permute-start(bf16[1024,128]{1,0:T(8,128)(2,1)S(1)} %collective-permute-done.20.refs_0_), channel_id=1, source_target_pairs={{0,8},{1,9},{2,10},{3,11},{4,12},{5,13},{6,14},{7,15},{8,0},{9,1},... | collective-permute-start | bytes 786440 | tf_op jit(solution)/shard_map/ppermute | solution.py:359

commit v11 on v10

--- a/solution.py
+++ b/solution.py
@@ -243,20 +243,18 @@
                 yield ref[at : at + sub, :], m, to, slice(lc * LANES, (lc + 1) * LANES)
 
 
-def dconv_kernel(plan, bits, own, core_got, y_got, conv_in, dconv, x_edge, z_edge):
+def dconv_kernel(plan, bits, own, core_got, y_got, conv_in, dconv, first_edge, last_edge):
     for dacted, m, to, lanes in home_chunks(plan, bits, own, core_got, y_got, 1):
         conv = conv_in[m, to, lanes]
         sig = sigmoid(conv)
         dconv[m, to, lanes] = dacted.astype(F32) * sig * (1.0 + conv * (1.0 - sig))
     count, length, width = dconv.shape
-    odd, last = bits[X], length - HALO
+    last = length - HALO
     for m in range(count):
         for lc, lanes in enumerate(lanes_of(width)):
             at = (m * plan[2] + lc) * HALO
-            x_rows = pl.ds(pl.multiple_of((1 - odd) * last, HALO), HALO)
-            z_rows = pl.ds(pl.multiple_of(odd * last, HALO), HALO)
-            x_edge[at : at + HALO, :] = dconv[m, x_rows, lanes].astype(BF)
-            z_edge[at : at + HALO, :] = dconv[m, z_rows, lanes].astype(BF)
+            first_edge[at : at + HALO, :] = dconv[m, :HALO, lanes].astype(BF)
+            last_edge[at : at + HALO, :] = dconv[m, last:, lanes].astype(BF)
 
 
 def layer_kernel(plan, bits, own, core_got, y_got, frames, weights, layer_out, mix_s):
@@ -297,15 +295,19 @@
         ).astype(BF)
 
 
-def frame_kernel(bits, dconv, x_got, z_got, both, kern, frame_grad):
+def frame_kernel(bits, dconv, x_got, z_got, other_got, both, kern, frame_grad):
     count, length, width = dconv.shape
     half = length // 2
+    n_edge = z_got.shape[0]
+    by_z = jnp.broadcast_to(bits[X] ^ bits[Z], (HALO, LANES)) == 1
 
     def step(m, _):
         for lc, lanes in enumerate(lanes_of(width)):
-            n = m * (width // LANES) + lc
-            rows = pl.ds(pl.multiple_of(n * HALO, HALO), HALO)
-            x = padded(bits, dconv[m, :, lanes], x_got[rows, :], z_got[rows, :])
+            at = (m * (width // LANES) + lc) * HALO
+            rows = pl.ds(pl.multiple_of(at, HALO), HALO)
+            x_rows = pl.ds(pl.multiple_of(bits[X] * n_edge + at, HALO), HALO)
+            two = jnp.where(by_z, z_got[rows, :].astype(F32), other_got[rows, :].astype(F32))
+            x = padded(bits, dconv[m, :, lanes], x_got[x_rows, :], two)
             for at in (0, half):
                 part = slice(at, at + half)
                 grad = window(
@@ -438,7 +440,7 @@
     y_got = after(y_got, (a[-1], b[-1]))
     home = (bits, back_keep, core_got, y_got)
     edge = flat(count * cols * HALO)
-    dconv, x_edge, z_edge = call(
+    dconv, *edges = call(
         functools.partial(dconv_kernel, plan), (wide, edge, edge), [], 8, *home, conv
     )
     a = halved(a, over_y)
@@ -450,25 +452,26 @@
         8, bits, both, frame_x, frame_z, after(dconv, a[-1]),
     )
     n = taps.shape[0]
-    got = swap(jnp.concatenate([taps, x_edge]), over_x)
-    taps, x_edge = total(taps, got[:n]), got[n:]
-
-    def doubled_with(x, taps, mask):
-        got = swap(jnp.concatenate([x, taps]), mask)
-        return jnp.concatenate([x, got[: x.shape[0]]]), total(taps, got[x.shape[0] :])
-
+    got = swap(jnp.concatenate([taps, *edges]), over_x)
+    taps, x_got = total(taps, got[:n]), got[n:]
+    passed = lax.dynamic_slice_in_dim(x_got, (1 - odd) * edge.shape[0], edge.shape[0], axis=0)
     a = exchanged(total(*a), lines[:1] + lines[2:])
     b = exchanged(total(*halved(b, over_y)), lines[1:])
-    z_edge = swap_beyond(after(z_edge, a))
-    a, taps = doubled_with(a, taps, lines[1])
-    for mask in lines[2:]:
-        taps = total(taps, swap(taps, mask))
+    taps = exchanged(taps, lines[1:])
+    passed = after(passed, a)
+    pairs = [(m * blocks + t, m * blocks + t + 2)
+             for m in range(groups) for t in range(2, blocks - 2) if t // 2 % 2]
+    z_got = swap(passed, lines[0])
+    other_got = permute(passed, pairs + [(j, i) for i, j in pairs])
+    a = doubled(a, lines[1])
     b = doubled(b, over_y)
     (layer_out,) = call(
         functools.partial(layer_kernel, plan), (shape(frames.shape, BF),), [here],
         10, *home, after(both, a), weights,
     )
-    a, taps = doubled_with(a, taps, over_y)
+    got = swap(jnp.concatenate([a, taps]), over_y)
+    n = a.shape[0]
+    a, taps = jnp.concatenate([a, got[:n]]), total(taps, got[n:])
     b = doubled(b, over_x)
 
     norm = 1.0 / math.sqrt(groups * count * blocks * length)
@@ -488,12 +491,11 @@
         )
 
     a_far, b_far = swap(a, over_x), swap(jnp.concatenate([b, taps]), lines[0])
+    a_other, b_other = swap(a, over_core), swap(b, over_core)
     (frame_grad,) = call(
         frame_kernel, (shape(frames.shape, BF),), [], 8,
-        bits, after(dconv, (a, b)), x_edge, z_edge, both, taps_in,
-    )
-    a_other, b_other = after((a, b), frame_grad)
-    a_other, b_other = swap(a_other, over_core), swap(b_other, over_core)
+        bits, after(dconv, (a_other, b_other)), x_got, z_got, other_got, both, taps_in,
+    )
     grads = final(((1, 0, 0), (1, 1, 0), (0, 0, 0), (0, 1, 0)), (a, b, a_other, b_other), ())
     a_far, b_far, frame_grad, layer_out, *grads = lax.optimization_barrier(
         (a_far, b_far, frame_grad, layer_out, *grads)

time: 91.3 us -> 99.7 us (1.092)
  waiting for transfers between devices: 29.5 us -> 21.7 us
  starting transfers between devices: 33.8 us -> 40.1 us
  local copies, waits for them, and re-layouts: 3.89 us -> 8.16 us
  other arithmetic: 0.94 us -> 5.15 us
  Pallas kernels: 21.8 us -> 23 us
    ppermute x32 -> x34, waiting for transfers between devices: 29.5 us -> 21.7 us  [permute(): return lax.ppermute(x, ('mic', 'tm'), pairs)]
    ppermute x32 -> x34, starting transfers between devices: 33.8 us -> 40.1 us  [permute(): return lax.ppermute(x, ('mic', 'tm'), pairs)]
    unnamed x9 -> x17, local copies, waits for them, and re-layouts: 1.13 us -> 2.95 us
    another operation x1, other arithmetic: 0.26 us -> 1.62 us  [shards(): weights = jnp.stack(weights)]
    pallas_call x9, Pallas kernels: 21.8 us -> 23 us  [call(): pl.pallas_call(body, out_shape=outs, in_specs=[pl.BlockSpec(memory_space=...]
  transfers between devices with their start and end apart: 32 -> 34, of which waited for: 12 -> 12; matrix products, arithmetic and copies ran while one was open for 3% -> 7% of each run, Pallas kernels for 15% -> 15%
where the time goes in v11:
time: 99.7 us; the launch traced here: 99.1 us
  starting transfers between devices  40.1 us (40%)
  Pallas kernels  23 us (23%)
  waiting for transfers between devices  21.7 us (22%)
  local copies, waits for them, and re-layouts  8.16 us (8%)
  other arithmetic  5.15 us (5%)
  between operations  1.01 us (1%)
    ppermute x34, starting transfers between devices, permute(): return lax.ppermute(x, ('mic', 'tm'), pairs)  40.1 us
    pallas_call x9, Pallas kernels, call(): pl.pallas_call(body, out_shape=outs, in_specs=[pl.BlockSpec(memory_space=...  23 us
    ppermute x34, waiting for transfers between devices, permute(): return lax.ppermute(x, ('mic', 'tm'), pairs)  21.7 us
    unnamed x17, local copies, waits for them, and re-layouts  2.95 us
  transfers between devices with their start and end apart: 34, of which 12 were waited for; matrix products, arithmetic and copies ran while one was open for 7% of the time, Pallas kernels for 15%

profile of v11, /device:TPU:0, one launch (start us, length us, event | category | flops | bytes accessed | tf_op | source)
XLA Modules:
  0.0 99.1 jit_solution(18181790304299016097)
XLA Ops:
  0.7 1.0 %constant_dynamic-update-slice_fusion.1 = bf16[4,128,512]{2,1,0:T(8,128)(2,1)S(1)} fusion(bf16[2,128,512]{2,1,0:T(8,128)(2,1)} %param.7), kind=kLoop, calls=%fused_computation.25 | loop fusion | bytes 524288
  1.7 1.0 constant_dynamic-update-slice_fusion.frames.both
  3.4 2.4 %collective-permute-start.7 = (bf16[2,32,512]{2,1,0:T(8,128)(2,1)S(1)}, bf16[2,32,512]{2,1,0:T(8,128)(2,1)S(1)}, u32[]{:S(2)}, u32[]{:S(2)}) collective-permute-start(bf16[2,32,512]{2,1,0:T(8,128)(2,1)S(1)} %get-tuple-element.95), channel_id=1, source_target_pairs={{0,24},{1,25},{2,26},{3,27},{4,28},{5,29},{6,30},{7,31},{8,16},{9,... | collective-permute-start | bytes 196616 | tf_op jit(solution)/shard_map/ppermute | solution.py:361
  5.8 0.8 constant_dynamic-slice_fusion.5
  7.2 4.3 %collective-permute-start = (bf16[2,16,512]{2,1,0:T(8,128)(2,1)S(1)}, bf16[2,16,512]{2,1,0:T(8,128)(2,1)S(1)}, u32[]{:S(2)}, u32[]{:S(2)}) collective-permute-start(bf16[2,16,512]{2,1,0:T(8,128)(2,1)S(1)} %get-tuple-element.100), channel_id=1, source_target_pairs={{0,1},{1,0},{2,3},{3,2},{4,5},{5,4},{6,7},{7,6},{8,9},{9,8},{10,11... | collective-permute-start | bytes 98312 | tf_op jit(solution)/shard_map/ppermute | solution.py:361
  12.1 0.8 pad.4.kern
  13.5 2.2 %shard_map.126 = (f32[2,128,512]{2,1,0:T(8,128)S(1)}, bf16[2,32,512]{2,1,0:T(8,128)(2,1)S(1)}, bf16[2,32,512]{2,1,0:T(8,128)(2,1)S(1)}, bf16[2,32,512]{2,1,0:T(8,128)(2,1)S(1)}, bf16[2,32,512]{2,1,0:T(8,128)(2,1)S(1)}) custom-call(s32[9]{0:T(128)S(1)} %stack.54.bits, bf16[4,128,512]{2,1,0:T(8,128)(2,1)S(1)} %constant_dynamic-update-slice_fusion.frames.both, ...), custom_call_target="tpu_custom_call" | custom-call | tf_op jit(solution)/shard_map/pallas_call | solution.py:326
  15.8 1.5 %collective-permute-start.3 = (bf16[2,32,512]{2,1,0:T(8,128)(2,1)S(1)}, bf16[2,32,512]{2,1,0:T(8,128)(2,1)S(1)}, u32[]{:S(2)}, u32[]{:S(2)}) collective-permute-start(bf16[2,32,512]{2,1,0:T(8,128)(2,1)S(1)} %get-tuple-element.54), channel_id=1, source_target_pairs={{0,16},{1,17},{2,18},{3,19},{4,20},{5,21},{6,22},{7,23},{8,24},{9,... | collective-permute-start | bytes 196616 | tf_op jit(solution)/shard_map/ppermute | solution.py:361
  17.7 1.6 %pad_maximum_fusion.weights = bf16[4,512,512]{2,1,0:T(8,128)(2,1)S(1)} fusion(bf16[1,512,512]{2,1,0:T(8,128)(2,1)S(1)} %bitcast.13, bf16[1,512,512]{2,1,0:T(8,128)(2,1)} %bitcast.14, bf16[1,512,512]{2,1,0:T(8,128)(2,1)} %bitcast.15, bf16[1,512,512]{2,1,0:T(8,128)(2,1)} %bitcast.16), kind=kLoop, calls=%fused_computation | loop fusion | flops 3145728 | bytes 4194304 | tf_op jit(solution)/shard_map/stack | solution.py:397
  19.3 1.0 collective-permute-done.3.a2
  20.3 1.4 %collective-permute-done.4.a3 = bf16[2,32,512]{2,1,0:T(8,128)(2,1)S(1)} collective-permute-done((bf16[2,32,512]{2,1,0:T(8,128)(2,1)S(1)}, bf16[2,32,512]{2,1,0:T(8,128)(2,1)S(1)}, u32[]{:S(2)}, u32[]{:S(2)}) %collective-permute-start.4) | collective-permute-done | bytes 65568 | tf_op jit(solution)/shard_map/ppermute | solution.py:361
  21.7 5.8 %shard_map.127 = (bf16[2048,128]{1,0:T(8,128)(2,1)S(1)}, bf16[2048,128]{1,0:T(8,128)(2,1)S(1)}, bf16[2048,128]{1,0:T(8,128)(2,1)S(1)}, bf16[2048,128]{1,0:T(8,12...) custom-call(s32[9]{0:T(128)S(1)} %stack.54.bits, ...), custom_call_target="tpu_custom_call" | custom-call | tf_op jit(solution)/shard_map/pallas_call | solution.py:326
  28.2 1.6 %collective-permute-done.14.core_got = bf16[1024,128]{1,0:T(8,128)(2,1)S(1)} collective-permute-done((bf16[1024,128]{1,0:T(8,128)(2,1)S(1)}, bf16[1024,128]{1,0:T(8,128)(2,1)S(1)}, u32[]{:S(2)}, u32[]{:S(2)}) %collective-permute-start.14) | collective-permute-done | bytes 262176 | tf_op jit(solution)/shard_map/ppermute | solution.py:361
  29.9 0.8 collective-permute-start.15
  30.8 1.6 %collective-permute-start.9 = (bf16[1024,128]{1,0:T(8,128)(2,1)S(1)}, bf16[1024,128]{1,0:T(8,128)(2,1)S(1)}, u32[]{:S(2)}, u32[]{:S(2)}) collective-permute-start(bf16[1024,128]{1,0:T(8,128)(2,1)S(1)} %add_convert_fusion.1), channel_id=1, source_target_pairs={{0,1},{1,0},{2,3},{3,2},{4,5},{5,4},{6,7},{7,6},{8,9},{9,8},{10,11... | collective-permute-start | bytes 786440 | tf_op jit(solution)/shard_map/ppermute | solution.py:361
  32.4 1.6 %collective-permute-start.17 = (bf16[1024,128]{1,0:T(8,128)(2,1)S(1)}, bf16[1024,128]{1,0:T(8,128)(2,1)S(1)}, u32[]{:S(2)}, u32[]{:S(2)}) collective-permute-start(bf16[1024,128]{1,0:T(8,128)(2,1)S(1)} %add_convert_fusion), channel_id=1, source_target_pairs={{0,2},{1,3},{2,0},{3,1},{4,6},{5,7},{6,4},{7,5},{8,10},{9,11},{10,... | collective-permute-start | bytes 786440 | tf_op jit(solution)/shard_map/ppermute | solution.py:361
  34.1 5.1 %collective-permute-done.9 = bf16[1024,128]{1,0:T(8,128)(2,1)S(1)} collective-permute-done((bf16[1024,128]{1,0:T(8,128)(2,1)S(1)}, bf16[1024,128]{1,0:T(8,128)(2,1)S(1)}, u32[]{:S(2)}, u32[]{:S(2)}) %collective-permute-start.9) | collective-permute-done | bytes 262176 | tf_op jit(solution)/shard_map/ppermute | solution.py:361
  39.2 1.1 %collective-permute-start.10 = (bf16[512,128]{1,0:T(8,128)(2,1)S(1)}, bf16[512,128]{1,0:T(8,128)(2,1)S(1)}, u32[]{:S(2)}, u32[]{:S(2)}) collective-permute-start(bf16[512,128]{1,0:T(8,128)(2,1)S(1)} %add_convert_fusion.3), channel_id=1, source_target_pairs={{0,16},{1,17},{2,18},{3,19},{4,20},{5,21},{6,22},{7,23},{8,24},{9,... | collective-permute-start | bytes 393224 | tf_op jit(solution)/shard_map/ppermute | solution.py:361
  40.4 1.7 %collective-permute-start.22 = (bf16[512,128]{1,0:T(8,128)(2,1)S(1)}, bf16[512,128]{1,0:T(8,128)(2,1)S(1)}, u32[]{:S(2)}, u32[]{:S(2)}) collective-permute-start(bf16[512,128]{1,0:T(8,128)(2,1)S(1)} %add_convert_fusion.2), channel_id=1, source_target_pairs={{0,1},{1,0},{2,3},{3,2},{4,5},{5,4},{6,7},{7,6},{8,9},{9,8},{10,11... | collective-permute-start | bytes 393224 | tf_op jit(solution)/shard_map/ppermute | solution.py:361
  42.2 0.7 shard_map.128
  42.9 1.3 %collective-permute-done.10 = bf16[512,128]{1,0:T(8,128)(2,1)S(1)} collective-permute-done((bf16[512,128]{1,0:T(8,128)(2,1)S(1)}, bf16[512,128]{1,0:T(8,128)(2,1)S(1)}, u32[]{:S(2)}, u32[]{:S(2)}) %collective-permute-start.10) | collective-permute-done | bytes 131104 | tf_op jit(solution)/shard_map/ppermute | solution.py:361
  44.3 2.7 %collective-permute-start.11 = (bf16[256,128]{1,0:T(8,128)(2,1)S(1)}, bf16[256,128]{1,0:T(8,128)(2,1)S(1)}, u32[]{:S(2)}, u32[]{:S(2)}) collective-permute-start(bf16[256,128]{1,0:T(8,128)(2,1)S(1)} %add_convert_fusion.9), channel_id=1, source_target_pairs={{0,4},{1,5},{2,6},{3,7},{4,0},{5,1},{6,2},{7,3},{8,12},{9,13},{10,... | collective-permute-start | bytes 196616 | tf_op jit(solution)/shard_map/ppermute | solution.py:361
  47.0 1.3 %collective-permute-start.23 = (bf16[256,128]{1,0:T(8,128)(2,1)S(1)}, bf16[256,128]{1,0:T(8,128)(2,1)S(1)}, u32[]{:S(2)}, u32[]{:S(2)}) collective-permute-start(bf16[256,128]{1,0:T(8,128)(2,1)S(1)} %add_convert_fusion.6), channel_id=1, source_target_pairs={{0,16},{1,17},{2,18},{3,19},{4,20},{5,21},{6,22},{7,23},{8,24},{9,... | collective-permute-start | bytes 196616 | tf_op jit(solution)/shard_map/ppermute | solution.py:361
  48.3 1.2 %collective-permute-done.11 = bf16[256,128]{1,0:T(8,128)(2,1)S(1)} collective-permute-done((bf16[256,128]{1,0:T(8,128)(2,1)S(1)}, bf16[256,128]{1,0:T(8,128)(2,1)S(1)}, u32[]{:S(2)}, u32[]{:S(2)}) %collective-permute-start.11) | collective-permute-done | bytes 65568 | tf_op jit(solution)/shard_map/ppermute | solution.py:361
  49.6 1.7 %collective-permute-start.12 = (bf16[256,128]{1,0:T(8,128)(2,1)S(1)}, bf16[256,128]{1,0:T(8,128)(2,1)S(1)}, u32[]{:S(2)}, u32[]{:S(2)}) collective-permute-start(bf16[256,128]{1,0:T(8,128)(2,1)S(1)} %add_convert_fusion.8), channel_id=1, source_target_pairs={{0,2},{1,3},{2,0},{3,1},{4,6},{5,7},{6,4},{7,5},{8,10},{9,11},{10,... | collective-permute-start | bytes 196616 | tf_op jit(solution)/shard_map/ppermute | solution.py:361
  51.3 2.8 %shard_map.129 = bf16[128,128]{1,0:T(8,128)(2,1)S(1)} custom-call(s32[9]{0:T(128)S(1)} %stack.54.bits, bf16[4,128,512]{2,1,0:T(8,128)(2,1)S(1)} %constant_dynamic-update-slice_fusion.frames.both, bf16[2,16,512]{2,1,0:T(8,128)(2,1)S(1)} %collective-permute-done.x_got, bf16[2,16,512]{2,1,0:T(8,128)(2,1)S(1)} %collective-permute-done.1.z_got, ...), custom_call_target="tpu_custom_call" | custom-call | tf_op jit(solution)/shard_map/pallas_call | solution.py:326
  54.1 1.3 %collective-permute-start.18 = (bf16[384,128]{1,0:T(8,128)(2,1)S(1)}, bf16[384,128]{1,0:T(8,128)(2,1)S(1)}, u32[]{:S(2)}, u32[]{:S(2)}) collective-permute-start(bf16[384,128]{1,0:T(8,128)(2,1)S(1)} %pad_maximum_fusion.8), channel_id=1, source_target_pairs={{0,1},{1,0},{2,3},{3,2},{4,5},{5,4},{6,7},{7,6},{8,9},{9,8},{10,11... | collective-permute-start | bytes 294920 | tf_op jit(solution)/shard_map/ppermute | solution.py:361
  55.5 1.8 %collective-permute-start.24 = (bf16[256,128]{1,0:T(8,128)(2,1)S(1)}, bf16[256,128]{1,0:T(8,128)(2,1)S(1)}, u32[]{:S(2)}, u32[]{:S(2)}) collective-permute-start(bf16[256,128]{1,0:T(8,128)(2,1)S(1)} %add_convert_fusion.5), channel_id=1, source_target_pairs={{0,4},{1,5},{2,6},{3,7},{4,0},{5,1},{6,2},{7,3},{8,12},{9,13},{10,... | collective-permute-start | bytes 196616 | tf_op jit(solution)/shard_map/ppermute | solution.py:361
  57.3 1.3 %collective-permute-start.13 = (bf16[256,128]{1,0:T(8,128)(2,1)S(1)}, bf16[256,128]{1,0:T(8,128)(2,1)S(1)}, u32[]{:S(2)}, u32[]{:S(2)}) collective-permute-start(bf16[256,128]{1,0:T(8,128)(2,1)S(1)} %add_convert_fusion.7), channel_id=1, source_target_pairs={{0,4},{1,5},{2,6},{3,7},{4,0},{5,1},{6,2},{7,3},{8,12},{9,13},{10,... | collective-permute-start | bytes 196616 | tf_op jit(solution)/shard_map/ppermute | solution.py:361
  58.6 2.9 %collective-permute-done.24 = bf16[256,128]{1,0:T(8,128)(2,1)S(1)} collective-permute-done((bf16[256,128]{1,0:T(8,128)(2,1)S(1)}, bf16[256,128]{1,0:T(8,128)(2,1)S(1)}, u32[]{:S(2)}, u32[]{:S(2)}) %collective-permute-start.24) | collective-permute-done | bytes 65568 | tf_op jit(solution)/shard_map/ppermute | solution.py:361
  61.5 2.1 %collective-permute-start.25 = (bf16[256,128]{1,0:T(8,128)(2,1)S(1)}, bf16[256,128]{1,0:T(8,128)(2,1)S(1)}, u32[]{:S(2)}, u32[]{:S(2)}) collective-permute-start(bf16[256,128]{1,0:T(8,128)(2,1)S(1)} %add_convert_fusion.4), channel_id=1, source_target_pairs={{0,16},{1,17},{2,18},{3,19},{4,20},{5,21},{6,22},{7,23},{8,24},{9,... | collective-permute-start | bytes 196616 | tf_op jit(solution)/shard_map/ppermute | solution.py:361
  63.7 0.9 collective-permute-start.19
  64.6 2.0 %collective-permute-done.25 = bf16[256,128]{1,0:T(8,128)(2,1)S(1)} collective-permute-done((bf16[256,128]{1,0:T(8,128)(2,1)S(1)}, bf16[256,128]{1,0:T(8,128)(2,1)S(1)}, u32[]{:S(2)}, u32[]{:S(2)}) %collective-permute-start.25) | collective-permute-done | bytes 65568 | tf_op jit(solution)/shard_map/ppermute | solution.py:361
  66.6 1.4 %collective-permute-start.26 = (bf16[512,128]{1,0:T(8,128)(2,1)S(1)}, bf16[512,128]{1,0:T(8,128)(2,1)S(1)}, u32[]{:S(2)}, u32[]{:S(2)}) collective-permute-start(bf16[512,128]{1,0:T(8,128)(2,1)S(1)} %pad_maximum_fusion.7), channel_id=1, source_target_pairs={{0,1},{1,0},{2,3},{3,2},{4,5},{5,4},{6,7},{7,6},{8,9},{9,8},{10,11... | collective-permute-start | bytes 393224 | tf_op jit(solution)/shard_map/ppermute | solution.py:361
  69.3 2.3 %collective-permute-done.26 = bf16[512,128]{1,0:T(8,128)(2,1)S(1)} collective-permute-done((bf16[512,128]{1,0:T(8,128)(2,1)S(1)}, bf16[512,128]{1,0:T(8,128)(2,1)S(1)}, u32[]{:S(2)}, u32[]{:S(2)}) %collective-permute-start.26) | collective-permute-done | bytes 131104 | tf_op jit(solution)/shard_map/ppermute | solution.py:361
  72.3 1.7 %collective-permute-done.20 = bf16[640,128]{1,0:T(8,128)(2,1)S(1)} collective-permute-done((bf16[640,128]{1,0:T(8,128)(2,1)S(1)}, bf16[640,128]{1,0:T(8,128)(2,1)S(1)}, u32[]{:S(2)}, u32[]{:S(2)}) %collective-permute-start.20) | collective-permute-done | bytes 163872 | tf_op jit(solution)/shard_map/ppermute | solution.py:361
  74.8 1.1 %collective-permute-start.27 = (bf16[1152,128]{1,0:T(8,128)(2,1)}, bf16[1152,128]{1,0:T(8,128)(2,1)}, u32[]{:S(2)}, u32[]{:S(2)}) collective-permute-start(bf16[1152,128]{1,0:T(8,128)(2,1)} %pad_maximum_fusion.1), channel_id=1, source_target_pairs={{0,2},{1,3},{2,0},{3,1},{4,6},{5,7},{6,4},{7,5},{8,10},{9,11},{10,... | collective-permute-start | bytes 884744 | tf_op jit(solution)/shard_map/ppermute | solution.py:361
  76.8 0.8 slice.192.x_got
  78.3 5.1 %collective-permute-start.30 = (bf16[128,128]{1,0:T(8,128)(2,1)S(1)}, bf16[128,128]{1,0:T(8,128)(2,1)S(1)}, u32[]{:S(2)}, u32[]{:S(2)}) collective-permute-start(bf16[128,128]{1,0:T(8,128)(2,1)S(1)} %constant_dynamic-slice_fusion), channel_id=1, source_target_pairs={{0,2},{1,3},{2,0},{3,1},{4,6},{5,7},{6,4},{7,5},{8,10},{9,11},{10,... | collective-permute-start | bytes 98312 | tf_op jit(solution)/shard_map/ppermute | solution.py:361
  83.4 0.9 copy-done.1
  84.3 0.9 copy-done.3
  85.3 1.6 %shard_map.131 = bf16[2,128,512]{2,1,0:T(8,128)(2,1)} custom-call(s32[9]{0:T(128)S(1)} %stack.54.bits, bf16[1024,128]{1,0:T(8,128)(2,1)S(1)} %get-tuple-element.62.own, bf16[1024,128]{1,0:T(8,128)(2,1)S(1)} %copy-done.1, bf16[1024,128]{1,0:T(8,128)(2,1)S(1)} %copy-done.3, bf16[4,128,512]{2,1,0:T(8,128)(2,1)S(1)} %constant_dynamic-update-slice_fusion.frames.both, ...), custom_call_target="tpu_custom_call" | custom-call | tf_op jit(solution)/shard_map/pallas_call | solution.py:326
  86.9 2.7 %shard_map.132 = (f32[512,512]{1,0:T(8,128)}, f32[512,512]{1,0:T(8,128)}, f32[512,512]{1,0:T(8,128)}, f32[512,512]{1,0:T(8,128)}) custom-call(s32[9]{0:T(128)S(1)} %stack.54.bits, bf16[1024,128]{1,0:T(8,128)(2,1)} %pad_maximum_fusion.4.refs_0_, bf16[1024,128]{1,0:T(8,128)(2,1)} %pad_maximum_fusion.5.refs_1_, ...), custom_call_target="tpu_custom_call" | custom-call | tf_op jit(solution)/shard_map/pallas_call | solution.py:326
  89.6 2.8 %shard_map.130 = bf16[2,128,512]{2,1,0:T(8,128)(2,1)} custom-call(s32[9]{0:T(128)S(1)} %stack.54.bits, f32[2,128,512]{2,1,0:T(8,128)S(1)} %get-tuple-element.72.dconv, bf16[256,128]{1,0:T(8,128)(2,1)S(1)} %slice.192.x_got, bf16[128,128]{1,0:T(8,128)(2,1)S(1)} %collective-permute-done.30.z_got, bf16[128,128]{1,0:T(8,128)(2,1)S(1)} %collective-permute-done.31.other_got, ...), custom_call_target="tpu_custom_call" | custom-call | tf_op jit(solution)/shard_map/pallas_call | solution.py:326
  92.4 0.8 add_convert_fusion.11
  93.1 1.0 slice.167
  94.7 2.1 %shard_map.133 = (f32[512,512]{1,0:T(8,128)}, f32[512,512]{1,0:T(8,128)}, f32[512,512]{1,0:T(8,128)}, f32[512,512]{1,0:T(8,128)}) custom-call(s32[9]{0:T(128)S(1)} %stack.54.bits, bf16[1024,128]{1,0:T(8,128)(2,1)} %collective-permute-done.21.refs_0_, ...), custom_call_target="tpu_custom_call", output_to_operand_aliasing={{0}: (3, {}), {1}: (4, {}), {2}: (5, {}), {3}: (6, {})} | custom-call | tf_op jit(solution)/shard_map/pallas_call | solution.py:326
  96.9 2.2 %shard_map.134 = (f32[512,512]{1,0:T(8,128)}, f32[512,512]{1,0:T(8,128)}, f32[512,512]{1,0:T(8,128)}, f32[512,512]{1,0:T(8,128)}, f32[31,512]{1,0:T(8,128)}) custom-call(s32[9]{0:T(128)S(1)} %stack.54.bits, bf16[1024,128]{1,0:T(8,128)(2,1)S(1)} %collective-permute-done.32.refs_0_, ...), custom_call_target="tpu_custom_call", output_to_operand_aliasing={{0}: (4, {}), {1}: (5, {}), {2}: (6, {}), {3}: (7, {})} | custom-call | tf_op jit(solution)/shard_map/pallas_call | solution.py:326
  (81 shorter events, 9.2 us)
Async XLA Ops:
  0.6 17.0 %copy-start.4 = (bf16[512,512]{1,0:T(8,128)(2,1)S(1)}, bf16[512,512]{1,0:T(8,128)(2,1)}, u32[]{:S(2)}) copy-start(bf16[512,512]{1,0:T(8,128)(2,1)} %param.13) | copy-start | bytes 1572868
  3.4 13.9 %collective-permute-start.7 = (bf16[2,32,512]{2,1,0:T(8,128)(2,1)S(1)}, bf16[2,32,512]{2,1,0:T(8,128)(2,1)S(1)}, u32[]{:S(2)}, u32[]{:S(2)}) collective-permute-start(bf16[2,32,512]{2,1,0:T(8,128)(2,1)S(1)} %get-tuple-element.95), channel_id=1, source_target_pairs={{0,24},{1,25},{2,26},{3,27},{4,28},{5,29},{6,30},{7,31},{8,16},{9,... | collective-permute-start | bytes 196616 | tf_op jit(solution)/shard_map/ppermute | solution.py:361
  6.6 6.5 %collective-permute-start.1 = (bf16[2,16,512]{2,1,0:T(8,128)(2,1)S(1)}, bf16[2,16,512]{2,1,0:T(8,128)(2,1)S(1)}, u32[]{:S(2)}, u32[]{:S(2)}) collective-permute-start(bf16[2,16,512]{2,1,0:T(8,128)(2,1)S(1)} %get-tuple-element.99), channel_id=1, source_target_pairs={{1,2},{3,4},{5,6},{9,10},{11,12},{13,14},{17,18},{19,20},{21,22},{... | collective-permute-start | bytes 98312 | tf_op jit(solution)/shard_map/ppermute | solution.py:361
  7.2 6.3 %collective-permute-start = (bf16[2,16,512]{2,1,0:T(8,128)(2,1)S(1)}, bf16[2,16,512]{2,1,0:T(8,128)(2,1)S(1)}, u32[]{:S(2)}, u32[]{:S(2)}) collective-permute-start(bf16[2,16,512]{2,1,0:T(8,128)(2,1)S(1)} %get-tuple-element.100), channel_id=1, source_target_pairs={{0,1},{1,0},{2,3},{3,2},{4,5},{5,4},{6,7},{7,6},{8,9},{9,8},{10,11... | collective-permute-start | bytes 98312 | tf_op jit(solution)/shard_map/ppermute | solution.py:361
  11.6 7.7 %collective-permute-start.6 = (bf16[2,32,512]{2,1,0:T(8,128)(2,1)}, bf16[2,32,512]{2,1,0:T(8,128)(2,1)S(1)}, u32[]{:S(2)}, u32[]{:S(2)}) collective-permute-start(bf16[2,32,512]{2,1,0:T(8,128)(2,1)} %get-tuple-element.96), channel_id=1, source_target_pairs={{0,16},{1,17},{2,18},{3,19},{4,20},{5,21},{6,22},{7,23},{8,24},{9,... | collective-permute-start | bytes 196616 | tf_op jit(solution)/shard_map/ppermute | solution.py:361
  12.1 7.2 %collective-permute-start.5 = (bf16[2,32,512]{2,1,0:T(8,128)(2,1)}, bf16[2,32,512]{2,1,0:T(8,128)(2,1)S(1)}, u32[]{:S(2)}, u32[]{:S(2)}) collective-permute-start(bf16[2,32,512]{2,1,0:T(8,128)(2,1)} %get-tuple-element.97), channel_id=1, source_target_pairs={{0,8},{1,9},{2,10},{3,11},{4,12},{5,13},{6,14},{7,15},{8,0},{9,1},... | collective-permute-start | bytes 196616 | tf_op jit(solution)/shard_map/ppermute | solution.py:361
  15.7 3.6 %collective-permute-start.2 = (bf16[2,32,512]{2,1,0:T(8,128)(2,1)S(1)}, bf16[2,32,512]{2,1,0:T(8,128)(2,1)S(1)}, u32[]{:S(2)}, u32[]{:S(2)}) collective-permute-start(bf16[2,32,512]{2,1,0:T(8,128)(2,1)S(1)} %get-tuple-element.53), channel_id=1, source_target_pairs={{0,8},{1,9},{2,10},{3,11},{4,12},{5,13},{6,14},{7,15},{8,0},{9,1},... | collective-permute-start | bytes 196616 | tf_op jit(solution)/shard_map/ppermute | solution.py:361
  15.8 4.5 %collective-permute-start.3 = (bf16[2,32,512]{2,1,0:T(8,128)(2,1)S(1)}, bf16[2,32,512]{2,1,0:T(8,128)(2,1)S(1)}, u32[]{:S(2)}, u32[]{:S(2)}) collective-permute-start(bf16[2,32,512]{2,1,0:T(8,128)(2,1)S(1)} %get-tuple-element.54), channel_id=1, source_target_pairs={{0,16},{1,17},{2,18},{3,19},{4,20},{5,21},{6,22},{7,23},{8,24},{9,... | collective-permute-start | bytes 196616 | tf_op jit(solution)/shard_map/ppermute | solution.py:361
  17.3 4.4 %collective-permute-start.4 = (bf16[2,32,512]{2,1,0:T(8,128)(2,1)S(1)}, bf16[2,32,512]{2,1,0:T(8,128)(2,1)S(1)}, u32[]{:S(2)}, u32[]{:S(2)}) collective-permute-start(bf16[2,32,512]{2,1,0:T(8,128)(2,1)S(1)} %get-tuple-element.55), channel_id=1, source_target_pairs={{0,24},{1,25},{2,26},{3,27},{4,28},{5,29},{6,30},{7,31},{8,16},{9,... | collective-permute-start | bytes 196616 | tf_op jit(solution)/shard_map/ppermute | solution.py:361
  27.5 3.2 %collective-permute-start.8 = (bf16[2048,128]{1,0:T(8,128)(2,1)S(1)}, bf16[2048,128]{1,0:T(8,128)(2,1)S(1)}, u32[]{:S(2)}, u32[]{:S(2)}) collective-permute-start(bf16[2048,128]{1,0:T(8,128)(2,1)S(1)} %get-tuple-element.61), channel_id=1, source_target_pairs={{0,8},{1,9},{2,10},{3,11},{4,12},{5,13},{6,14},{7,15},{8,0},{9,1},... | collective-permute-start | bytes 1572872 | tf_op jit(solution)/shard_map/ppermute | solution.py:361
  27.7 2.2 %collective-permute-start.14 = (bf16[1024,128]{1,0:T(8,128)(2,1)S(1)}, bf16[1024,128]{1,0:T(8,128)(2,1)S(1)}, u32[]{:S(2)}, u32[]{:S(2)}) collective-permute-start(bf16[1024,128]{1,0:T(8,128)(2,1)S(1)} %get-tuple-element.63), channel_id=1, source_target_pairs={{0,8},{1,9},{2,10},{3,11},{4,12},{5,13},{6,14},{7,15},{8,0},{9,1},... | collective-permute-start | bytes 786440 | tf_op jit(solution)/shard_map/ppermute | solution.py:361
  28.1 4.3 %collective-permute-start.16 = (bf16[2048,128]{1,0:T(8,128)(2,1)S(1)}, bf16[2048,128]{1,0:T(8,128)(2,1)S(1)}, u32[]{:S(2)}, u32[]{:S(2)}) collective-permute-start(bf16[2048,128]{1,0:T(8,128)(2,1)S(1)} %get-tuple-element.65), channel_id=1, source_target_pairs={{0,8},{1,9},{2,10},{3,11},{4,12},{5,13},{6,14},{7,15},{8,0},{9,1},... | collective-permute-start | bytes 1572872 | tf_op jit(solution)/shard_map/ppermute | solution.py:361
  29.9 13.0 %copy-start = (bf16[1024,128]{1,0:T(8,128)(2,1)}, bf16[1024,128]{1,0:T(8,128)(2,1)S(1)}, u32[]{:S(2)}) copy-start(bf16[1024,128]{1,0:T(8,128)(2,1)S(1)} %collective-permute-done.14.core_got) | copy-start | bytes 786436
  29.9 10.4 %collective-permute-start.15 = (bf16[1024,128]{1,0:T(8,128)(2,1)S(1)}, bf16[1024,128]{1,0:T(8,128)(2,1)S(1)}, u32[]{:S(2)}, u32[]{:S(2)}) collective-permute-start(bf16[1024,128]{1,0:T(8,128)(2,1)S(1)} %pad_maximum_fusion.3), channel_id=1, source_target_pairs={{0,16},{1,17},{2,18},{3,19},{4,20},{5,21},{6,22},{7,23},{8,24},{9,... | collective-permute-start | bytes 786440 | tf_op jit(solution)/shard_map/ppermute | solution.py:361
  30.8 8.4 %collective-permute-start.9 = (bf16[1024,128]{1,0:T(8,128)(2,1)S(1)}, bf16[1024,128]{1,0:T(8,128)(2,1)S(1)}, u32[]{:S(2)}, u32[]{:S(2)}) collective-permute-start(bf16[1024,128]{1,0:T(8,128)(2,1)S(1)} %add_convert_fusion.1), channel_id=1, source_target_pairs={{0,1},{1,0},{2,3},{3,2},{4,5},{5,4},{6,7},{7,6},{8,9},{9,8},{10,11... | collective-permute-start | bytes 786440 | tf_op jit(solution)/shard_map/ppermute | solution.py:361
  32.4 7.9 %collective-permute-start.17 = (bf16[1024,128]{1,0:T(8,128)(2,1)S(1)}, bf16[1024,128]{1,0:T(8,128)(2,1)S(1)}, u32[]{:S(2)}, u32[]{:S(2)}) collective-permute-start(bf16[1024,128]{1,0:T(8,128)(2,1)S(1)} %add_convert_fusion), channel_id=1, source_target_pairs={{0,2},{1,3},{2,0},{3,1},{4,6},{5,7},{6,4},{7,5},{8,10},{9,11},{10,... | collective-permute-start | bytes 786440 | tf_op jit(solution)/shard_map/ppermute | solution.py:361
  39.2 5.0 %collective-permute-start.10 = (bf16[512,128]{1,0:T(8,128)(2,1)S(1)}, bf16[512,128]{1,0:T(8,128)(2,1)S(1)}, u32[]{:S(2)}, u32[]{:S(2)}) collective-permute-start(bf16[512,128]{1,0:T(8,128)(2,1)S(1)} %add_convert_fusion.3), channel_id=1, source_target_pairs={{0,16},{1,17},{2,18},{3,19},{4,20},{5,21},{6,22},{7,23},{8,24},{9,... | collective-permute-start | bytes 393224 | tf_op jit(solution)/shard_map/ppermute | solution.py:361
  40.4 13.8 %copy-start.2 = (bf16[1024,128]{1,0:T(8,128)(2,1)}, bf16[1024,128]{1,0:T(8,128)(2,1)S(1)}, u32[]{:S(2)}) copy-start(bf16[1024,128]{1,0:T(8,128)(2,1)S(1)} %collective-permute-done.15.y_got) | copy-start | bytes 786436
  40.4 6.6 %collective-permute-start.22 = (bf16[512,128]{1,0:T(8,128)(2,1)S(1)}, bf16[512,128]{1,0:T(8,128)(2,1)S(1)}, u32[]{:S(2)}, u32[]{:S(2)}) collective-permute-start(bf16[512,128]{1,0:T(8,128)(2,1)S(1)} %add_convert_fusion.2), channel_id=1, source_target_pairs={{0,1},{1,0},{2,3},{3,2},{4,5},{5,4},{6,7},{7,6},{8,9},{9,8},{10,11... | collective-permute-start | bytes 393224 | tf_op jit(solution)/shard_map/ppermute | solution.py:361
  44.3 5.3 %collective-permute-start.11 = (bf16[256,128]{1,0:T(8,128)(2,1)S(1)}, bf16[256,128]{1,0:T(8,128)(2,1)S(1)}, u32[]{:S(2)}, u32[]{:S(2)}) collective-permute-start(bf16[256,128]{1,0:T(8,128)(2,1)S(1)} %add_convert_fusion.9), channel_id=1, source_target_pairs={{0,4},{1,5},{2,6},{3,7},{4,0},{5,1},{6,2},{7,3},{8,12},{9,13},{10,... | collective-permute-start | bytes 196616 | tf_op jit(solution)/shard_map/ppermute | solution.py:361
  47.0 8.4 %collective-permute-start.23 = (bf16[256,128]{1,0:T(8,128)(2,1)S(1)}, bf16[256,128]{1,0:T(8,128)(2,1)S(1)}, u32[]{:S(2)}, u32[]{:S(2)}) collective-permute-start(bf16[256,128]{1,0:T(8,128)(2,1)S(1)} %add_convert_fusion.6), channel_id=1, source_target_pairs={{0,16},{1,17},{2,18},{3,19},{4,20},{5,21},{6,22},{7,23},{8,24},{9,... | collective-permute-start | bytes 196616 | tf_op jit(solution)/shard_map/ppermute | solution.py:361
  49.6 7.7 %collective-permute-start.12 = (bf16[256,128]{1,0:T(8,128)(2,1)S(1)}, bf16[256,128]{1,0:T(8,128)(2,1)S(1)}, u32[]{:S(2)}, u32[]{:S(2)}) collective-permute-start(bf16[256,128]{1,0:T(8,128)(2,1)S(1)} %add_convert_fusion.8), channel_id=1, source_target_pairs={{0,2},{1,3},{2,0},{3,1},{4,6},{5,7},{6,4},{7,5},{8,10},{9,11},{10,... | collective-permute-start | bytes 196616 | tf_op jit(solution)/shard_map/ppermute | solution.py:361
  54.1 9.5 %collective-permute-start.18 = (bf16[384,128]{1,0:T(8,128)(2,1)S(1)}, bf16[384,128]{1,0:T(8,128)(2,1)S(1)}, u32[]{:S(2)}, u32[]{:S(2)}) collective-permute-start(bf16[384,128]{1,0:T(8,128)(2,1)S(1)} %pad_maximum_fusion.8), channel_id=1, source_target_pairs={{0,1},{1,0},{2,3},{3,2},{4,5},{5,4},{6,7},{7,6},{8,9},{9,8},{10,11... | collective-permute-start | bytes 294920 | tf_op jit(solution)/shard_map/ppermute | solution.py:361
  55.5 6.0 %collective-permute-start.24 = (bf16[256,128]{1,0:T(8,128)(2,1)S(1)}, bf16[256,128]{1,0:T(8,128)(2,1)S(1)}, u32[]{:S(2)}, u32[]{:S(2)}) collective-permute-start(bf16[256,128]{1,0:T(8,128)(2,1)S(1)} %add_convert_fusion.5), channel_id=1, source_target_pairs={{0,4},{1,5},{2,6},{3,7},{4,0},{5,1},{6,2},{7,3},{8,12},{9,13},{10,... | collective-permute-start | bytes 196616 | tf_op jit(solution)/shard_map/ppermute | solution.py:361
  57.3 11.3 %collective-permute-start.13 = (bf16[256,128]{1,0:T(8,128)(2,1)S(1)}, bf16[256,128]{1,0:T(8,128)(2,1)S(1)}, u32[]{:S(2)}, u32[]{:S(2)}) collective-permute-start(bf16[256,128]{1,0:T(8,128)(2,1)S(1)} %add_convert_fusion.7), channel_id=1, source_target_pairs={{0,4},{1,5},{2,6},{3,7},{4,0},{5,1},{6,2},{7,3},{8,12},{9,13},{10,... | collective-permute-start | bytes 196616 | tf_op jit(solution)/shard_map/ppermute | solution.py:361
  61.5 5.0 %collective-permute-start.25 = (bf16[256,128]{1,0:T(8,128)(2,1)S(1)}, bf16[256,128]{1,0:T(8,128)(2,1)S(1)}, u32[]{:S(2)}, u32[]{:S(2)}) collective-permute-start(bf16[256,128]{1,0:T(8,128)(2,1)S(1)} %add_convert_fusion.4), channel_id=1, source_target_pairs={{0,16},{1,17},{2,18},{3,19},{4,20},{5,21},{6,22},{7,23},{8,24},{9,... | collective-permute-start | bytes 196616 | tf_op jit(solution)/shard_map/ppermute | solution.py:361
  63.7 2.9 %copy-start.7 = (bf16[384,128]{1,0:T(8,128)(2,1)}, bf16[384,128]{1,0:T(8,128)(2,1)S(1)}, u32[]{:S(2)}) copy-start(bf16[384,128]{1,0:T(8,128)(2,1)S(1)} %collective-permute-done.18) | copy-start | bytes 294916
  63.7 4.9 %collective-permute-start.19 = (bf16[128,128]{1,0:T(8,128)(2,1)S(1)}, bf16[128,128]{1,0:T(8,128)(2,1)S(1)}, u32[]{:S(2)}, u32[]{:S(2)}) collective-permute-start(bf16[128,128]{1,0:T(8,128)(2,1)S(1)} %add_convert_fusion.14), channel_id=1, source_target_pairs={{0,4},{1,5},{2,6},{3,7},{4,0},{5,1},{6,2},{7,3},{8,12},{9,13},{10,... | collective-permute-start | bytes 98312 | tf_op jit(solution)/shard_map/ppermute | solution.py:361
  66.6 5.0 %collective-permute-start.26 = (bf16[512,128]{1,0:T(8,128)(2,1)S(1)}, bf16[512,128]{1,0:T(8,128)(2,1)S(1)}, u32[]{:S(2)}, u32[]{:S(2)}) collective-permute-start(bf16[512,128]{1,0:T(8,128)(2,1)S(1)} %pad_maximum_fusion.7), channel_id=1, source_target_pairs={{0,1},{1,0},{2,3},{3,2},{4,5},{5,4},{6,7},{7,6},{8,9},{9,8},{10,11... | collective-permute-start | bytes 393224 | tf_op jit(solution)/shard_map/ppermute | solution.py:361
  68.6 5.4 %collective-permute-start.20 = (bf16[640,128]{1,0:T(8,128)(2,1)S(1)}, bf16[640,128]{1,0:T(8,128)(2,1)S(1)}, u32[]{:S(2)}, u32[]{:S(2)}) collective-permute-start(bf16[640,128]{1,0:T(8,128)(2,1)S(1)} %pad_maximum_fusion.6), channel_id=1, source_target_pairs={{0,16},{1,17},{2,18},{3,19},{4,20},{5,21},{6,22},{7,23},{8,24},{9,... | collective-permute-start | bytes 491528 | tf_op jit(solution)/shard_map/ppermute | solution.py:361
  72.3 6.0 %collective-permute-start.29 = (bf16[1024,128]{1,0:T(8,128)(2,1)}, bf16[1024,128]{1,0:T(8,128)(2,1)}, u32[]{:S(2)}, u32[]{:S(2)}) collective-permute-start(bf16[1024,128]{1,0:T(8,128)(2,1)} %pad_maximum_fusion.5.refs_1_), channel_id=1, source_target_pairs={{0,8},{1,9},{2,10},{3,11},{4,12},{5,13},{6,14},{7,15},{8,0},{9,1},... | collective-permute-start | bytes 786440 | tf_op jit(solution)/shard_map/ppermute | solution.py:361
  74.0 2.5 %copy-start.5 = (bf16[128,128]{1,0:T(8,128)(2,1)}, bf16[128,128]{1,0:T(8,128)(2,1)S(1)}, u32[]{:S(2)}) copy-start(bf16[128,128]{1,0:T(8,128)(2,1)S(1)} %add_convert_fusion.12) | copy-start | bytes 98308
  74.8 17.6 %collective-permute-start.27 = (bf16[1152,128]{1,0:T(8,128)(2,1)}, bf16[1152,128]{1,0:T(8,128)(2,1)}, u32[]{:S(2)}, u32[]{:S(2)}) collective-permute-start(bf16[1152,128]{1,0:T(8,128)(2,1)} %pad_maximum_fusion.1), channel_id=1, source_target_pairs={{0,2},{1,3},{2,0},{3,1},{4,6},{5,7},{6,4},{7,5},{8,10},{9,11},{10,... | collective-permute-start | bytes 884744 | tf_op jit(solution)/shard_map/ppermute | solution.py:361
  76.6 10.3 %collective-permute-start.28 = (bf16[1024,128]{1,0:T(8,128)(2,1)}, bf16[1024,128]{1,0:T(8,128)(2,1)}, u32[]{:S(2)}, u32[]{:S(2)}) collective-permute-start(bf16[1024,128]{1,0:T(8,128)(2,1)} %pad_maximum_fusion.4.refs_0_), channel_id=1, source_target_pairs={{0,8},{1,9},{2,10},{3,11},{4,12},{5,13},{6,14},{7,15},{8,0},{9,1},... | collective-permute-start | bytes 786440 | tf_op jit(solution)/shard_map/ppermute | solution.py:361
  76.6 15.8 %collective-permute-start.21 = (bf16[1024,128]{1,0:T(8,128)(2,1)}, bf16[1024,128]{1,0:T(8,128)(2,1)}, u32[]{:S(2)}, u32[]{:S(2)}) collective-permute-start(bf16[1024,128]{1,0:T(8,128)(2,1)} %pad_maximum_fusion.4.refs_0_), channel_id=1, source_target_pairs={{0,1},{1,0},{2,3},{3,2},{4,5},{5,4},{6,7},{7,6},{8,9},{9,8},{10,11... | collective-permute-start | bytes 786440 | tf_op jit(solution)/shard_map/ppermute | solution.py:361
  77.6 11.9 %collective-permute-start.31 = (bf16[128,128]{1,0:T(8,128)(2,1)S(1)}, bf16[128,128]{1,0:T(8,128)(2,1)S(1)}, u32[]{:S(2)}, u32[]{:S(2)}) collective-permute-start(bf16[128,128]{1,0:T(8,128)(2,1)S(1)} %constant_dynamic-slice_fusion), channel_id=1, source_target_pairs={{2,4},{3,5},{10,12},{11,13},{18,20},{19,21},{26,28},{27,29},{4,2},... | collective-permute-start | bytes 98312 | tf_op jit(solution)/shard_map/ppermute | solution.py:361
  78.3 11.2 %collective-permute-start.30 = (bf16[128,128]{1,0:T(8,128)(2,1)S(1)}, bf16[128,128]{1,0:T(8,128)(2,1)S(1)}, u32[]{:S(2)}, u32[]{:S(2)}) collective-permute-start(bf16[128,128]{1,0:T(8,128)(2,1)S(1)} %constant_dynamic-slice_fusion), channel_id=1, source_target_pairs={{0,2},{1,3},{2,0},{3,1},{4,6},{5,7},{6,4},{7,5},{8,10},{9,11},{10,... | collective-permute-start | bytes 98312 | tf_op jit(solution)/shard_map/ppermute | solution.py:361
  83.4 0.9 copy-start.1
  84.3 0.9 copy-start.3
  86.9 5.5 %copy-start.6 = (bf16[128,128]{1,0:T(8,128)(2,1)S(1)}, bf16[128,128]{1,0:T(8,128)(2,1)}, u32[]{:S(2)}) copy-start(bf16[128,128]{1,0:T(8,128)(2,1)} %copy-done.5) | copy-start | bytes 98308
  94.1 2.7 %collective-permute-start.33 = (bf16[1152,128]{1,0:T(8,128)(2,1)S(1)}, bf16[1152,128]{1,0:T(8,128)(2,1)S(1)}, u32[]{:S(2)}, u32[]{:S(2)}) collective-permute-start(bf16[1152,128]{1,0:T(8,128)(2,1)S(1)} %pad_maximum_fusion.2), channel_id=1, source_target_pairs={{0,8},{1,9},{2,10},{3,11},{4,12},{5,13},{6,14},{7,15},{8,0},{9,1},... | collective-permute-start | bytes 884744 | tf_op jit(solution)/shard_map/ppermute | solution.py:361
  94.2 2.6 %collective-permute-start.32 = (bf16[1024,128]{1,0:T(8,128)(2,1)}, bf16[1024,128]{1,0:T(8,128)(2,1)S(1)}, u32[]{:S(2)}, u32[]{:S(2)}) collective-permute-start(bf16[1024,128]{1,0:T(8,128)(2,1)} %collective-permute-done.21.refs_0_), channel_id=1, source_target_pairs={{0,8},{1,9},{2,10},{3,11},{4,12},{5,13},{6,14},{7,15},{8,0},{9,1},... | collective-permute-start | bytes 786440 | tf_op jit(solution)/shard_map/ppermute | solution.py:361

commit v12 on v10

--- a/solution.py
+++ b/solution.py
@@ -16,7 +16,7 @@
 BF = jnp.bfloat16
 F32 = jnp.float32
 MIB = 1024 * 1024
-CORE, Y, X, Z, ZZ, BLOCK_AT = range(6)
+CORE, X, OWN, OTHER, BLOCK_AT = 0, 1, 2, 5, 8
 
 
 def mm(left, right, dims=(((1,), (0,)), ((), ()))):
@@ -40,8 +40,8 @@
     return acc
 
 
-def ways(bits, half):
-    return [bits[i] for i in ((X, Y, ZZ), (Z, X, Y))[half]]
+def ways(bits, own):
+    return [bits[(OWN if own else OTHER) + i] for i in range(3)]
 
 
 def sigmoid(v):
@@ -86,7 +86,7 @@
 
 
 def main_kernel(
-    plan, bits, a0, a1, a2, a3, c0, c1, c2, c3, weights,
+    plan, bits, c0, c1, c2, c3, a0, a1, a2, a3, weights,
     a_keep, b_keep, a_send, b_send, back_keep, back_send,
     left_s, right_s, q_s, k_s, v_s, u_s,
 ):
@@ -169,7 +169,7 @@
         (a_send, 1 - core, 0), (b_send, 1 - core, 1), (a_keep, core, 0), (b_keep, core, 1)
     ):
         i = owner * 2 + h
-        first, second, third = ways(bits, h)
+        first, second, third = ways(bits, out is a_keep or out is b_keep)
         grad = mm(left_s[i // 3], flat(i), TN).astype(BF)
         for piece in range(8):
             rel = ((piece // 4) ^ first) * 4 + ((piece // 2 % 2) ^ second) * 2 + ((piece % 2) ^ third)
@@ -212,7 +212,7 @@
     copies = []
     for n, (own, h, far) in enumerate(kinds):
         owner = core if own else 1 - core
-        first, second, third = ways(bits, h)
+        first, second, third = ways(bits, own)
         for rel in range(4):
             k = 4 * n + rel
             piece_s[k] = got[n][rel * size : (rel + 1) * size, :].astype(F32) * norm
@@ -297,23 +297,20 @@
         ).astype(BF)
 
 
-def frame_kernel(bits, dconv, x_got, z_got, both, kern, frame_grad):
+def frame_kernel(bits, dconv, x_got, z_got, cot, kern, frame_grad):
     count, length, width = dconv.shape
     half = length // 2
 
     def step(m, _):
         for lc, lanes in enumerate(lanes_of(width)):
-            n = m * (width // LANES) + lc
-            rows = pl.ds(pl.multiple_of(n * HALO, HALO), HALO)
+            rows = pl.ds(pl.multiple_of((m * (width // LANES) + lc) * HALO, HALO), HALO)
             x = padded(bits, dconv[m, :, lanes], x_got[rows, :], z_got[rows, :])
             for at in (0, half):
                 part = slice(at, at + half)
                 grad = window(
                     x[at : at + half + 2 * HALO], lambda o: kern[31 - o : 32 - o, lanes], half
                 )
-                frame_grad[m, part, lanes] = (
-                    both[count + m, part, lanes].astype(F32) + grad
-                ).astype(BF)
+                frame_grad[m, part, lanes] = (cot[m, part, lanes].astype(F32) + grad).astype(BF)
         return 0
 
     lax.fori_loop(0, count, step, 0)
@@ -350,16 +347,24 @@
     mic, tm = lax.axis_index("mic"), lax.axis_index("tm")
     over_core, over_y, over_x = blocks, 2 * blocks, 1
     lines = [2**i for i in range(1, blocks.bit_length() - 1)]
-    odd = tm % 2
-    bits = jnp.stack(
-        [mic % 2, mic // 2, odd, tm // 2 % 2, tm // 4 % 2] + [mic ^ d for d in range(4)]
-    ).astype(jnp.int32)
+    core, odd = mic % 2, tm % 2
+    axes = [(over_x, lines[0]), (over_y, over_x), (lines[1], over_y)]
+    whole_axes = [(lines[0], lines[1])] + [(m, m) for m in lines[2:]]
+    flat_at = mic * blocks + tm
+
+    def bit(mask):
+        return (flat_at // mask) % 2
+
+    own = [jnp.where(core == 0, bit(i), bit(j)) for i, j in axes]
+    other = [jnp.where(core == 0, bit(j), bit(i)) for i, j in axes]
+    bits = jnp.stack([core, odd] + own + other + [mic ^ d for d in range(4)]).astype(jnp.int32)
 
     def permute(x, pairs):
         return lax.ppermute(x, ("mic", "tm"), pairs)
 
-    def swap(x, mask):
-        return permute(x, [(f, f ^ mask) for f in range(groups * blocks)])
+    def swap(x, even, odd=None):
+        masks = (even, even if odd is None else odd)
+        return permute(x, [(f, f ^ masks[f // blocks % 2]) for f in range(groups * blocks)])
 
     def swap_beyond(x):
         pairs = [(m * blocks + t, m * blocks + t + 1)
@@ -374,25 +379,20 @@
     last = length - HALO
     frame_x = swap(lax.dynamic_slice_in_dim(frames, (1 - odd) * last, HALO, axis=1), over_x)
     frame_z = swap_beyond(lax.dynamic_slice_in_dim(frames, odd * last, HALO, axis=1))
-    both = jnp.concatenate([frames, cotangent])
-    taps_in = jnp.pad(kernel, ((0, 1), (0, 0)))
-    cot_parts = spread(
-        [
-            lax.dynamic_slice(both, (count, (mic ^ d) * sub, 0), (count, sub, width))
-            for d in range(4)
-        ]
-    )
     block = shape((count, sub, width), BF)
     wide = shape(frames.shape, F32)
     here = pltpu.VMEM(frames.shape, BF)
     conv, *acted = call(
         functools.partial(conv_kernel, sub), (wide,) + (block,) * 4, [here],
-        8, bits, both, frame_x, frame_z, taps_in,
-    )
-    own_acted, *weights = lax.optimization_barrier(
-        (acted[0], w_query, w_key, w_value, w_out)
+        8, bits, frames, frame_x, frame_z, kernel,
+    )
+    own_acted, cot_late, *weights = lax.optimization_barrier(
+        (acted[0], cotangent, w_query, w_key, w_value, w_out)
     )
     weights = jnp.stack(weights)
+    cot_parts = spread(
+        [lax.dynamic_slice_in_dim(cot_late, (mic ^ d) * sub, sub, axis=1) for d in range(4)]
+    )
 
     factor = 1.0 / math.sqrt(width // HEADS)
     part = width * width // LANES
@@ -410,20 +410,24 @@
             pltpu.VMEM((4, cuts, groups, count, HALO, width), BF),
             big, big, big, big,
         ],
-        24, bits, *spread([own_acted] + acted[1:]), *cot_parts, weights,
-    )
-
-    def halved(parts, mask):
+        24, bits, *cot_parts, *spread([own_acted] + acted[1:]), weights,
+    )
+
+    def halved(parts, pair):
         n = parts[0].shape[0] // 2
-        return [t[:n] for t in parts] + [swap(total(*(t[n:] for t in parts)), mask)]
-
-    def exchanged(x, masks):
-        for mask in masks:
-            x = total(x, swap(x, mask))
+        return [t[:n] for t in parts] + [swap(total(*(t[n:] for t in parts)), *pair)]
+
+    def exchanged(x, pairs):
+        for pair in pairs:
+            x = total(x, swap(x, *pair))
         return x
 
-    def doubled(x, mask):
-        return jnp.concatenate([x, swap(x, mask)])
+    def doubled(x, pair):
+        return jnp.concatenate([x, swap(x, *pair)])
+
+    def doubled_with(x, taps, pair):
+        got = swap(jnp.concatenate([x, taps]), *pair)
+        return jnp.concatenate([x, got[: x.shape[0]]]), total(taps, got[x.shape[0] :])
 
     def after(x, y):
         return lax.optimization_barrier((x, y))[0]
@@ -432,8 +436,8 @@
     b = [b_keep, swap(b_send, over_core)]
     core_got = swap(back_send, over_core)
     y_got = swap(jnp.concatenate([back_keep[unit:], core_got[unit:]]), over_y)
-    a = halved(a, over_x)
-    b = halved(b, lines[0])
+    a = halved(a, axes[0])
+    b = halved(b, axes[0])
     plan = (count, sub, cols)
     y_got = after(y_got, (a[-1], b[-1]))
     home = (bits, back_keep, core_got, y_got)
@@ -441,35 +445,22 @@
     dconv, x_edge, z_edge = call(
         functools.partial(dconv_kernel, plan), (wide, edge, edge), [], 8, *home, conv
     )
-    a = halved(a, over_y)
-    b = halved(b, over_x)
-    a = halved(a, lines[1])
+    a = halved(a, axes[1])
+    b = halved(b, axes[1])
     (taps,) = call(
         functools.partial(tap_kernel, sub), (flat(32 * cols),),
         [pltpu.VMEM((count, length + 2 * HALO, width), F32)],
-        8, bits, both, frame_x, frame_z, after(dconv, a[-1]),
-    )
-    n = taps.shape[0]
-    got = swap(jnp.concatenate([taps, x_edge]), over_x)
-    taps, x_edge = total(taps, got[:n]), got[n:]
-
-    def doubled_with(x, taps, mask):
-        got = swap(jnp.concatenate([x, taps]), mask)
-        return jnp.concatenate([x, got[: x.shape[0]]]), total(taps, got[x.shape[0] :])
-
-    a = exchanged(total(*a), lines[:1] + lines[2:])
-    b = exchanged(total(*halved(b, over_y)), lines[1:])
-    z_edge = swap_beyond(after(z_edge, a))
-    a, taps = doubled_with(a, taps, lines[1])
-    for mask in lines[2:]:
-        taps = total(taps, swap(taps, mask))
-    b = doubled(b, over_y)
-    (layer_out,) = call(
-        functools.partial(layer_kernel, plan), (shape(frames.shape, BF),), [here],
-        10, *home, after(both, a), weights,
-    )
-    a, taps = doubled_with(a, taps, over_y)
-    b = doubled(b, over_x)
+        8, bits, frames, frame_x, frame_z, after(dconv, a[-1]),
+    )
+    taps = exchanged(taps, whole_axes)
+    x_got = swap(x_edge, over_x)
+    a = exchanged(total(*halved(a, axes[2])), whole_axes)
+    b = exchanged(total(*halved(b, axes[2])), whole_axes)
+    z_got = swap_beyond(after(z_edge, (x_got, a)))
+    a = doubled(after(a, x_got), axes[2])
+    b, taps = doubled_with(b, taps, axes[2])
+    a = doubled(after(a, z_got), axes[1])
+    b, taps = doubled_with(b, taps, axes[1])
 
     norm = 1.0 / math.sqrt(groups * count * blocks * length)
     square = shape((width, width), F32)
@@ -487,13 +478,16 @@
             hbm_outs=range(4), aliases={first + i: i for i in range(len(grads))},
         )
 
-    a_far, b_far = swap(a, over_x), swap(jnp.concatenate([b, taps]), lines[0])
+    a_far, b_far = swap(a, *axes[0]), swap(jnp.concatenate([b, taps]), *axes[0])
+    a_other, b_other = swap(a, over_core), swap(b, over_core)
     (frame_grad,) = call(
         frame_kernel, (shape(frames.shape, BF),), [], 8,
-        bits, after(dconv, (a, b)), x_edge, z_edge, both, taps_in,
-    )
-    a_other, b_other = after((a, b), frame_grad)
-    a_other, b_other = swap(a_other, over_core), swap(b_other, over_core)
+        bits, after(dconv, a), x_got, z_got, cotangent, kernel,
+    )
+    (layer_out,) = call(
+        functools.partial(layer_kernel, plan), (shape(frames.shape, BF),), [here],
+        10, *home, after(frames, a), weights,
+    )
     grads = final(((1, 0, 0), (1, 1, 0), (0, 0, 0), (0, 1, 0)), (a, b, a_other, b_other), ())
     a_far, b_far, frame_grad, layer_out, *grads = lax.optimization_barrier(
         (a_far, b_far, frame_grad, layer_out, *grads)

time: 91.3 us -> 96.9 us (1.061)
  starting transfers between devices: 33.8 us -> 39.4 us
  waiting for transfers between devices: 29.5 us -> 27.9 us
  other arithmetic: 0.94 us -> 2.43 us
    ppermute x32 -> x33, starting transfers between devices: 33.8 us -> 39.4 us  [permute(): return lax.ppermute(x, ('mic', 'tm'), pairs)]
    ppermute x32 -> x33, waiting for transfers between devices: 29.5 us -> 27.9 us  [permute(): return lax.ppermute(x, ('mic', 'tm'), pairs)]
    another operation x1, other arithmetic: 0.26 us -> 1.78 us  [shards(): weights = jnp.stack(weights)]
  transfers between devices with their start and end apart: 32 -> 33, of which waited for: 12 -> 14; matrix products, arithmetic and copies ran while one was open for 3% -> 3% of each run, Pallas kernels for 15% -> 12%
where the time goes in v12:
time: 96.9 us; the launch traced here: 96.6 us
  starting transfers between devices  39.4 us (41%)
  waiting for transfers between devices  27.9 us (29%)
  Pallas kernels  21.9 us (23%)
  local copies, waits for them, and re-layouts  3.74 us (4%)
  other arithmetic  2.43 us (3%)
  between operations  1.12 us (1%)
    ppermute x33, starting transfers between devices, permute(): return lax.ppermute(x, ('mic', 'tm'), pairs)  39.4 us
    ppermute x33, waiting for transfers between devices, permute(): return lax.ppermute(x, ('mic', 'tm'), pairs)  27.9 us
    pallas_call x9, Pallas kernels, call(): pl.pallas_call(body, out_shape=outs, in_specs=[pl.BlockSpec(memory_space=...  21.9 us
  transfers between devices with their start and end apart: 33, of which 14 were waited for; matrix products, arithmetic and copies ran while one was open for 3% of the time, Pallas kernels for 12%

profile of v12, /device:TPU:0, one launch (start us, length us, event | category | flops | bytes accessed | tf_op | source)
XLA Modules:
  0.0 96.6 jit_solution(8443323523244333649)
XLA Ops:
  0.7 0.8 constant_dynamic-slice_fusion.4
  1.4 2.9 %collective-permute-start = (bf16[2,16,512]{2,1,0:T(8,128)(2,1)S(1)}, bf16[2,16,512]{2,1,0:T(8,128)(2,1)S(1)}, u32[]{:S(2)}, u32[]{:S(2)}) collective-permute-start(bf16[2,16,512]{2,1,0:T(8,128)(2,1)S(1)} %get-tuple-element.108), channel_id=1, source_target_pairs={{0,1},{1,0},{2,3},{3,2},{4,5},{5,4},{6,7},{7,6},{8,9},{9,8},{10,11... | collective-permute-start | bytes 98312 | tf_op jit(solution)/shard_map/ppermute | solution.py:363
  4.4 0.7 collective-permute-start.1
  5.3 1.0 %collective-permute-done.x_got = bf16[2,16,512]{2,1,0:T(8,128)(2,1)S(1)} collective-permute-done((bf16[2,16,512]{2,1,0:T(8,128)(2,1)S(1)}, bf16[2,16,512]{2,1,0:T(8,128)(2,1)S(1)}, u32[]{:S(2)}, u32[]{:S(2)}) %collective-permute-start) | collective-permute-done | bytes 32800 | tf_op jit(solution)/shard_map/ppermute | solution.py:363
  6.3 0.9 copy-done
  7.2 0.8 copy-done.3
  8.1 2.2 %shard_map.126 = (f32[2,128,512]{2,1,0:T(8,128)S(1)}, bf16[2,32,512]{2,1,0:T(8,128)(2,1)S(1)}, bf16[2,32,512]{2,1,0:T(8,128)(2,1)S(1)}, bf16[2,32,512]{2,1,0:T(8,128)(2,1)S(1)}, bf16[2,32,512]{2,1,0:T(8,128)(2,1)S(1)}) custom-call(s32[12]{0:T(128)S(1)} %stack.66.bits, bf16[2,128,512]{2,1,0:T(8,128)(2,1)S(1)} %copy-done, ...), custom_call_target="tpu_custom_call" | custom-call | tf_op jit(solution)/shard_map/pallas_call | solution.py:321
  10.3 1.0 %constant_dynamic-slice_fusion = (bf16[2,32,512]{2,1,0:T(8,128)(2,1)S(1)}, bf16[2,32,512]{2,1,0:T(8,128)(2,1)S(1)}, bf16[2,32,512]{2,1,0:T(8,128)(2,1)S(1)}, bf16[2,32,512]{2,1,0:T(8,128)(2,1)S(1)}) fusion(bf16[2,128,512]{2,1,0:T(8,128)(2,1)} %cot.1, s32[]{:T(128)S(6)} %select_n.118, s32[]{:T(128)S(6)} %select_n.117, s32[]{:T(128)S(6)} %select_n.116, ...), kind=kLoop, calls=%fused_computation.25 | loop fusion | bytes 524304 | tf_op jit(solution)/shard_map/dynamic_slice | solution.py:394
  11.4 2.1 %collective-permute-start.3 = (bf16[2,32,512]{2,1,0:T(8,128)(2,1)S(1)}, bf16[2,32,512]{2,1,0:T(8,128)(2,1)S(1)}, u32[]{:S(2)}, u32[]{:S(2)}) collective-permute-start(bf16[2,32,512]{2,1,0:T(8,128)(2,1)S(1)} %get-tuple-element.104), channel_id=1, source_target_pairs={{0,16},{1,17},{2,18},{3,19},{4,20},{5,21},{6,22},{7,23},{8,24},{9,... | collective-permute-start | bytes 196616 | tf_op jit(solution)/shard_map/ppermute | solution.py:363
  13.7 1.9 %collective-permute-start.6 = (bf16[2,32,512]{2,1,0:T(8,128)(2,1)S(1)}, bf16[2,32,512]{2,1,0:T(8,128)(2,1)S(1)}, u32[]{:S(2)}, u32[]{:S(2)}) collective-permute-start(bf16[2,32,512]{2,1,0:T(8,128)(2,1)S(1)} %get-tuple-element.59), channel_id=1, source_target_pairs={{0,16},{1,17},{2,18},{3,19},{4,20},{5,21},{6,22},{7,23},{8,24},{9,... | collective-permute-start | bytes 196616 | tf_op jit(solution)/shard_map/ppermute | solution.py:363
  15.6 1.8 %pad_maximum_fusion.weights = bf16[4,512,512]{2,1,0:T(8,128)(2,1)S(1)} fusion(bf16[1,512,512]{2,1,0:T(8,128)(2,1)} %bitcast.16, bf16[1,512,512]{2,1,0:T(8,128)(2,1)} %bitcast.17, bf16[1,512,512]{2,1,0:T(8,128)(2,1)} %bitcast.18, bf16[1,512,512]{2,1,0:T(8,128)(2,1)} %bitcast.19), kind=kLoop, calls=%fused_computation | loop fusion | flops 3145728 | bytes 4194304 | tf_op jit(solution)/shard_map/stack | solution.py:392
  17.5 2.1 %collective-permute-done.6.a2 = bf16[2,32,512]{2,1,0:T(8,128)(2,1)S(1)} collective-permute-done((bf16[2,32,512]{2,1,0:T(8,128)(2,1)S(1)}, bf16[2,32,512]{2,1,0:T(8,128)(2,1)S(1)}, u32[]{:S(2)}, u32[]{:S(2)}) %collective-permute-start.6) | collective-permute-done | bytes 65568 | tf_op jit(solution)/shard_map/ppermute | solution.py:363
  19.6 0.7 collective-permute-done.7.a3
  20.3 5.8 %shard_map.127 = (bf16[2048,128]{1,0:T(8,128)(2,1)S(1)}, bf16[2048,128]{1,0:T(8,128)(2,1)S(1)}, bf16[2048,128]{1,0:T(8,128)(2,1)S(1)}, bf16[2048,128]{1,0:T(8,12...) custom-call(s32[12]{0:T(128)S(1)} %stack.66.bits, ...), custom_call_target="tpu_custom_call" | custom-call | tf_op jit(solution)/shard_map/pallas_call | solution.py:321
  26.4 0.3 collective-permute-start.13
  27.0 1.6 %collective-permute-done.13.core_got = bf16[1024,128]{1,0:T(8,128)(2,1)S(1)} collective-permute-done((bf16[1024,128]{1,0:T(8,128)(2,1)S(1)}, bf16[1024,128]{1,0:T(8,128)(2,1)S(1)}, u32[]{:S(2)}, u32[]{:S(2)}) %collective-permute-start.13) | collective-permute-done | bytes 262176 | tf_op jit(solution)/shard_map/ppermute | solution.py:363
  28.6 1.4 %collective-permute-start.14 = (bf16[1024,128]{1,0:T(8,128)(2,1)S(1)}, bf16[1024,128]{1,0:T(8,128)(2,1)S(1)}, u32[]{:S(2)}, u32[]{:S(2)}) collective-permute-start(bf16[1024,128]{1,0:T(8,128)(2,1)S(1)} %pad_maximum_fusion.3), channel_id=1, source_target_pairs={{0,16},{1,17},{2,18},{3,19},{4,20},{5,21},{6,22},{7,23},{8,24},{9,... | collective-permute-start | bytes 786440 | tf_op jit(solution)/shard_map/ppermute | solution.py:363
  30.1 4.9 %collective-permute-start.16 = (bf16[1024,128]{1,0:T(8,128)(2,1)S(1)}, bf16[1024,128]{1,0:T(8,128)(2,1)S(1)}, u32[]{:S(2)}, u32[]{:S(2)}) collective-permute-start(bf16[1024,128]{1,0:T(8,128)(2,1)S(1)} %add_convert_fusion), channel_id=1, source_target_pairs={{0,1},{1,0},{2,3},{3,2},{4,5},{5,4},{6,7},{7,6},{8,10},{9,11},{10,... | collective-permute-start | bytes 786440 | tf_op jit(solution)/shard_map/ppermute | solution.py:363
  35.1 4.2 %collective-permute-done.16 = bf16[1024,128]{1,0:T(8,128)(2,1)S(1)} collective-permute-done((bf16[1024,128]{1,0:T(8,128)(2,1)S(1)}, bf16[1024,128]{1,0:T(8,128)(2,1)S(1)}, u32[]{:S(2)}, u32[]{:S(2)}) %collective-permute-start.16) | collective-permute-done | bytes 262176 | tf_op jit(solution)/shard_map/ppermute | solution.py:363
  39.4 0.7 collective-permute-start.22
  40.1 2.4 %collective-permute-done.9 = bf16[1024,128]{1,0:T(8,128)(2,1)S(1)} collective-permute-done((bf16[1024,128]{1,0:T(8,128)(2,1)S(1)}, bf16[1024,128]{1,0:T(8,128)(2,1)S(1)}, u32[]{:S(2)}, u32[]{:S(2)}) %collective-permute-start.9) | collective-permute-done | bytes 262176 | tf_op jit(solution)/shard_map/ppermute | solution.py:363
  42.6 0.9 collective-permute-start.10
  43.4 0.7 shard_map.128
  44.2 2.5 %collective-permute-start.17 = (bf16[128,128]{1,0:T(8,128)(2,1)S(1)}, bf16[128,128]{1,0:T(8,128)(2,1)S(1)}, u32[]{:S(2)}, u32[]{:S(2)}) collective-permute-start(bf16[128,128]{1,0:T(8,128)(2,1)S(1)} %get-tuple-element.73), channel_id=1, source_target_pairs={{0,1},{1,0},{2,3},{3,2},{4,5},{5,4},{6,7},{7,6},{8,9},{9,8},{10,11... | collective-permute-start | bytes 98312 | tf_op jit(solution)/shard_map/ppermute | solution.py:363
  46.8 2.6 %collective-permute-start.23 = (bf16[256,128]{1,0:T(8,128)(2,1)S(1)}, bf16[256,128]{1,0:T(8,128)(2,1)S(1)}, u32[]{:S(2)}, u32[]{:S(2)}) collective-permute-start(bf16[256,128]{1,0:T(8,128)(2,1)S(1)} %add_convert_fusion.6), channel_id=1, source_target_pairs={{0,4},{1,5},{2,6},{3,7},{4,0},{5,1},{6,2},{7,3},{8,24},{9,25},{10,... | collective-permute-start | bytes 196616 | tf_op jit(solution)/shard_map/ppermute | solution.py:363
  49.4 2.8 %shard_map.129 = bf16[128,128]{1,0:T(8,128)(2,1)S(1)} custom-call(s32[12]{0:T(128)S(1)} %stack.66.bits, bf16[2,128,512]{2,1,0:T(8,128)(2,1)S(1)} %copy-done.1, bf16[2,16,512]{2,1,0:T(8,128)(2,1)S(1)} %collective-permute-done.x_got, bf16[2,16,512]{2,1,0:T(8,128)(2,1)S(1)} %collective-permute-done.1.z_got, f32[2,128,512]{2,1,0:T(8,128)S(1)} %get-tuple-element.80.dconv), custom_call_target="tpu_custom_call" | custom-call | tf_op jit(solution)/shard_map/pallas_call | solution.py:321
  52.3 2.2 %collective-permute-start.25 = (bf16[128,128]{1,0:T(8,128)(2,1)S(1)}, bf16[128,128]{1,0:T(8,128)(2,1)S(1)}, u32[]{:S(2)}, u32[]{:S(2)}) collective-permute-start(bf16[128,128]{1,0:T(8,128)(2,1)S(1)} %shard_map.129), channel_id=1, source_target_pairs={{0,2},{1,3},{2,0},{3,1},{4,6},{5,7},{6,4},{7,5},{8,12},{9,13},{10,... | collective-permute-start | bytes 98312 | tf_op jit(solution)/shard_map/ppermute | solution.py:363
  54.5 2.6 %collective-permute-start.11 = (bf16[256,128]{1,0:T(8,128)(2,1)S(1)}, bf16[256,128]{1,0:T(8,128)(2,1)S(1)}, u32[]{:S(2)}, u32[]{:S(2)}) collective-permute-start(bf16[256,128]{1,0:T(8,128)(2,1)S(1)} %add_convert_fusion.9), channel_id=1, source_target_pairs={{0,4},{1,5},{2,6},{3,7},{4,0},{5,1},{6,2},{7,3},{8,24},{9,25},{10,... | collective-permute-start | bytes 196616 | tf_op jit(solution)/shard_map/ppermute | solution.py:363
  57.1 5.3 %collective-permute-done.11 = bf16[256,128]{1,0:T(8,128)(2,1)S(1)} collective-permute-done((bf16[256,128]{1,0:T(8,128)(2,1)S(1)}, bf16[256,128]{1,0:T(8,128)(2,1)S(1)}, u32[]{:S(2)}, u32[]{:S(2)}) %collective-permute-start.11) | collective-permute-done | bytes 65568 | tf_op jit(solution)/shard_map/ppermute | solution.py:363
  62.6 2.1 %collective-permute-start.24 = (bf16[256,128]{1,0:T(8,128)(2,1)S(1)}, bf16[256,128]{1,0:T(8,128)(2,1)S(1)}, u32[]{:S(2)}, u32[]{:S(2)}) collective-permute-start(bf16[256,128]{1,0:T(8,128)(2,1)S(1)} %add_convert_fusion.5), channel_id=1, source_target_pairs={{0,2},{1,3},{2,0},{3,1},{4,6},{5,7},{6,4},{7,5},{8,12},{9,13},{10,... | collective-permute-start | bytes 196616 | tf_op jit(solution)/shard_map/ppermute | solution.py:363
  64.7 2.1 %collective-permute-done.12 = bf16[256,128]{1,0:T(8,128)(2,1)S(1)} collective-permute-done((bf16[256,128]{1,0:T(8,128)(2,1)S(1)}, bf16[256,128]{1,0:T(8,128)(2,1)S(1)}, u32[]{:S(2)}, u32[]{:S(2)}) %collective-permute-start.12) | collective-permute-done | bytes 65568 | tf_op jit(solution)/shard_map/ppermute | solution.py:363
  66.8 0.7 collective-permute-start.18
  67.5 2.4 %collective-permute-start.26 = (bf16[384,128]{1,0:T(8,128)(2,1)S(1)}, bf16[384,128]{1,0:T(8,128)(2,1)S(1)}, u32[]{:S(2)}, u32[]{:S(2)}) collective-permute-start(bf16[384,128]{1,0:T(8,128)(2,1)S(1)} %pad_maximum_fusion.7), channel_id=1, source_target_pairs={{0,4},{1,5},{2,6},{3,7},{4,0},{5,1},{6,2},{7,3},{8,24},{9,25},{10,... | collective-permute-start | bytes 294920 | tf_op jit(solution)/shard_map/ppermute | solution.py:363
  69.9 0.7 collective-permute-start.19
  70.6 1.6 %collective-permute-done.18 = bf16[256,128]{1,0:T(8,128)(2,1)S(1)} collective-permute-done((bf16[256,128]{1,0:T(8,128)(2,1)S(1)}, bf16[256,128]{1,0:T(8,128)(2,1)S(1)}, u32[]{:S(2)}, u32[]{:S(2)}) %collective-permute-start.18) | collective-permute-done | bytes 65568 | tf_op jit(solution)/shard_map/ppermute | solution.py:363
  72.2 0.7 collective-permute-start.20
  72.9 1.4 %collective-permute-done.26 = bf16[384,128]{1,0:T(8,128)(2,1)S(1)} collective-permute-done((bf16[384,128]{1,0:T(8,128)(2,1)S(1)}, bf16[384,128]{1,0:T(8,128)(2,1)S(1)}, u32[]{:S(2)}, u32[]{:S(2)}) %collective-permute-start.26) | collective-permute-done | bytes 98336 | tf_op jit(solution)/shard_map/ppermute | solution.py:363
  74.3 0.7 collective-permute-start.27
  75.1 2.2 %collective-permute-done.20 = bf16[512,128]{1,0:T(8,128)(2,1)S(1)} collective-permute-done((bf16[512,128]{1,0:T(8,128)(2,1)S(1)}, bf16[512,128]{1,0:T(8,128)(2,1)S(1)}, u32[]{:S(2)}, u32[]{:S(2)}) %collective-permute-start.20) | collective-permute-done | bytes 131104 | tf_op jit(solution)/shard_map/ppermute | solution.py:363
  77.4 2.4 %collective-permute-done.27 = bf16[640,128]{1,0:T(8,128)(2,1)S(1)} collective-permute-done((bf16[640,128]{1,0:T(8,128)(2,1)S(1)}, bf16[640,128]{1,0:T(8,128)(2,1)S(1)}, u32[]{:S(2)}, u32[]{:S(2)}) %collective-permute-start.27) | collective-permute-done | bytes 163872 | tf_op jit(solution)/shard_map/ppermute | solution.py:363
  79.8 4.7 %collective-permute-start.28 = (bf16[1152,128]{1,0:T(8,128)(2,1)S(1)}, bf16[1152,128]{1,0:T(8,128)(2,1)S(1)}, u32[]{:S(2)}, u32[]{:S(2)}) collective-permute-start(bf16[1152,128]{1,0:T(8,128)(2,1)S(1)} %pad_maximum_fusion.1), channel_id=1, source_target_pairs={{0,1},{1,0},{2,3},{3,2},{4,5},{5,4},{6,7},{7,6},{8,10},{9,11},{10,... | collective-permute-start | bytes 884744 | tf_op jit(solution)/shard_map/ppermute | solution.py:363
  84.7 1.6 %shard_map.131 = bf16[2,128,512]{2,1,0:T(8,128)(2,1)} custom-call(s32[12]{0:T(128)S(1)} %stack.66.bits, bf16[1024,128]{1,0:T(8,128)(2,1)S(1)} %get-tuple-element.67.own, bf16[1024,128]{1,0:T(8,128)(2,1)S(1)} %collective-permute-done.13.core_got, bf16[1024,128]{1,0:T(8,128)(2,1)S(1)} %collective-permute-done.14.y_got, bf16[2,128,512]{2,1,0:T(8,128)(2,1)S(1)} %copy-done.1, ...), custom_call_target="tpu_custom_call" | custom-call | tf_op jit(solution)/shard_map/pallas_call | solution.py:321
  86.3 2.8 %shard_map.130 = bf16[2,128,512]{2,1,0:T(8,128)(2,1)} custom-call(s32[12]{0:T(128)S(1)} %stack.66.bits, f32[2,128,512]{2,1,0:T(8,128)S(1)} %get-tuple-element.80.dconv, bf16[128,128]{1,0:T(8,128)(2,1)S(1)} %collective-permute-done.17.x_got, bf16[128,128]{1,0:T(8,128)(2,1)S(1)} %collective-permute-done.19.z_got, bf16[2,128,512]{2,1,0:T(8,128)(2,1)S(1)} %copy-done.2, ...), custom_call_target="tpu_custom_call" | custom-call | tf_op jit(solution)/shard_map/pallas_call | solution.py:321
  89.2 2.0 %shard_map.132 = (f32[512,512]{1,0:T(8,128)}, f32[512,512]{1,0:T(8,128)}, f32[512,512]{1,0:T(8,128)}, f32[512,512]{1,0:T(8,128)}) custom-call(s32[12]{0:T(128)S(1)} %stack.66.bits, bf16[1024,128]{1,0:T(8,128)(2,1)S(1)} %constant_dynamic-update-slice_fusion.refs_0_, bf16[1024,128]{1,0:T(8,128)(2,1)S(1)} %pad_maximum_fusion.4.refs_1_, ...), custom_call_target="tpu_custom_call" | custom-call | tf_op jit(solution)/shard_map/pallas_call | solution.py:321
  91.2 0.9 collective-permute-done.21.refs_0_
  92.2 0.5 collective-permute-start.31
  92.7 1.6 %shard_map.133 = (f32[512,512]{1,0:T(8,128)}, f32[512,512]{1,0:T(8,128)}, f32[512,512]{1,0:T(8,128)}, f32[512,512]{1,0:T(8,128)}) custom-call(s32[12]{0:T(128)S(1)} %stack.66.bits, bf16[1024,128]{1,0:T(8,128)(2,1)S(1)} %collective-permute-done.21.refs_0_, ...), custom_call_target="tpu_custom_call", output_to_operand_aliasing={{0}: (3, {}), {1}: (4, {}), {2}: (5, {}), {3}: (6, {})} | custom-call | tf_op jit(solution)/shard_map/pallas_call | solution.py:321
  94.3 2.2 %shard_map.134 = (f32[512,512]{1,0:T(8,128)}, f32[512,512]{1,0:T(8,128)}, f32[512,512]{1,0:T(8,128)}, f32[512,512]{1,0:T(8,128)}, f32[31,512]{1,0:T(8,128)}) custom-call(s32[12]{0:T(128)S(1)} %stack.66.bits, bf16[1024,128]{1,0:T(8,128)(2,1)S(1)} %collective-permute-done.31.refs_0_, ...), custom_call_target="tpu_custom_call", output_to_operand_aliasing={{0}: (4, {}), {1}: (5, {}), {2}: (6, {}), {3}: (7, {})} | custom-call | tf_op jit(solution)/shard_map/pallas_call | solution.py:321
  (70 shorter events, 2.2 us)
Async XLA Ops:
  1.4 4.8 %collective-permute-start = (bf16[2,16,512]{2,1,0:T(8,128)(2,1)S(1)}, bf16[2,16,512]{2,1,0:T(8,128)(2,1)S(1)}, u32[]{:S(2)}, u32[]{:S(2)}) collective-permute-start(bf16[2,16,512]{2,1,0:T(8,128)(2,1)S(1)} %get-tuple-element.108), channel_id=1, source_target_pairs={{0,1},{1,0},{2,3},{3,2},{4,5},{5,4},{6,7},{7,6},{8,9},{9,8},{10,11... | collective-permute-start | bytes 98312 | tf_op jit(solution)/shard_map/ppermute | solution.py:363
  4.4 1.9 %collective-permute-start.1 = (bf16[2,16,512]{2,1,0:T(8,128)(2,1)S(1)}, bf16[2,16,512]{2,1,0:T(8,128)(2,1)S(1)}, u32[]{:S(2)}, u32[]{:S(2)}) collective-permute-start(bf16[2,16,512]{2,1,0:T(8,128)(2,1)S(1)} %get-tuple-element.107), channel_id=1, source_target_pairs={{1,2},{3,4},{5,6},{9,10},{11,12},{13,14},{17,18},{19,20},{21,22},{... | collective-permute-start | bytes 98312 | tf_op jit(solution)/shard_map/ppermute | solution.py:363
  6.3 1.0 copy-start
  7.2 0.8 copy-start.3
  11.3 4.3 %collective-permute-start.2 = (bf16[2,32,512]{2,1,0:T(8,128)(2,1)S(1)}, bf16[2,32,512]{2,1,0:T(8,128)(2,1)S(1)}, u32[]{:S(2)}, u32[]{:S(2)}) collective-permute-start(bf16[2,32,512]{2,1,0:T(8,128)(2,1)S(1)} %get-tuple-element.105), channel_id=1, source_target_pairs={{0,8},{1,9},{2,10},{3,11},{4,12},{5,13},{6,14},{7,15},{8,0},{9,1},... | collective-permute-start | bytes 196616 | tf_op jit(solution)/shard_map/ppermute | solution.py:363
  11.4 6.0 %collective-permute-start.3 = (bf16[2,32,512]{2,1,0:T(8,128)(2,1)S(1)}, bf16[2,32,512]{2,1,0:T(8,128)(2,1)S(1)}, u32[]{:S(2)}, u32[]{:S(2)}) collective-permute-start(bf16[2,32,512]{2,1,0:T(8,128)(2,1)S(1)} %get-tuple-element.104), channel_id=1, source_target_pairs={{0,16},{1,17},{2,18},{3,19},{4,20},{5,21},{6,22},{7,23},{8,24},{9,... | collective-permute-start | bytes 196616 | tf_op jit(solution)/shard_map/ppermute | solution.py:363
  13.5 4.0 %collective-permute-start.4 = (bf16[2,32,512]{2,1,0:T(8,128)(2,1)S(1)}, bf16[2,32,512]{2,1,0:T(8,128)(2,1)S(1)}, u32[]{:S(2)}, u32[]{:S(2)}) collective-permute-start(bf16[2,32,512]{2,1,0:T(8,128)(2,1)S(1)} %get-tuple-element.103), channel_id=1, source_target_pairs={{0,24},{1,25},{2,26},{3,27},{4,28},{5,29},{6,30},{7,31},{8,16},{9,... | collective-permute-start | bytes 196616 | tf_op jit(solution)/shard_map/ppermute | solution.py:363
  13.6 4.0 %collective-permute-start.5 = (bf16[2,32,512]{2,1,0:T(8,128)(2,1)S(1)}, bf16[2,32,512]{2,1,0:T(8,128)(2,1)S(1)}, u32[]{:S(2)}, u32[]{:S(2)}) collective-permute-start(bf16[2,32,512]{2,1,0:T(8,128)(2,1)S(1)} %get-tuple-element.58), channel_id=1, source_target_pairs={{0,8},{1,9},{2,10},{3,11},{4,12},{5,13},{6,14},{7,15},{8,0},{9,1},... | collective-permute-start | bytes 196616 | tf_op jit(solution)/shard_map/ppermute | solution.py:363
  13.7 5.9 %collective-permute-start.6 = (bf16[2,32,512]{2,1,0:T(8,128)(2,1)S(1)}, bf16[2,32,512]{2,1,0:T(8,128)(2,1)S(1)}, u32[]{:S(2)}, u32[]{:S(2)}) collective-permute-start(bf16[2,32,512]{2,1,0:T(8,128)(2,1)S(1)} %get-tuple-element.59), channel_id=1, source_target_pairs={{0,16},{1,17},{2,18},{3,19},{4,20},{5,21},{6,22},{7,23},{8,24},{9,... | collective-permute-start | bytes 196616 | tf_op jit(solution)/shard_map/ppermute | solution.py:363
  15.6 4.7 %collective-permute-start.7 = (bf16[2,32,512]{2,1,0:T(8,128)(2,1)S(1)}, bf16[2,32,512]{2,1,0:T(8,128)(2,1)S(1)}, u32[]{:S(2)}, u32[]{:S(2)}) collective-permute-start(bf16[2,32,512]{2,1,0:T(8,128)(2,1)S(1)} %get-tuple-element.60), channel_id=1, source_target_pairs={{0,24},{1,25},{2,26},{3,27},{4,28},{5,29},{6,30},{7,31},{8,16},{9,... | collective-permute-start | bytes 196616 | tf_op jit(solution)/shard_map/ppermute | solution.py:363
  26.2 3.8 %collective-permute-start.15 = (bf16[2048,128]{1,0:T(8,128)(2,1)S(1)}, bf16[2048,128]{1,0:T(8,128)(2,1)S(1)}, u32[]{:S(2)}, u32[]{:S(2)}) collective-permute-start(bf16[2048,128]{1,0:T(8,128)(2,1)S(1)} %get-tuple-element.70), channel_id=1, source_target_pairs={{0,8},{1,9},{2,10},{3,11},{4,12},{5,13},{6,14},{7,15},{8,0},{9,1},... | collective-permute-start | bytes 1572872 | tf_op jit(solution)/shard_map/ppermute | solution.py:363
  26.4 2.1 %collective-permute-start.13 = (bf16[1024,128]{1,0:T(8,128)(2,1)S(1)}, bf16[1024,128]{1,0:T(8,128)(2,1)S(1)}, u32[]{:S(2)}, u32[]{:S(2)}) collective-permute-start(bf16[1024,128]{1,0:T(8,128)(2,1)S(1)} %get-tuple-element.68), channel_id=1, source_target_pairs={{0,8},{1,9},{2,10},{3,11},{4,12},{5,13},{6,14},{7,15},{8,0},{9,1},... | collective-permute-start | bytes 786440 | tf_op jit(solution)/shard_map/ppermute | solution.py:363
  26.8 8.2 %collective-permute-start.8 = (bf16[2048,128]{1,0:T(8,128)(2,1)S(1)}, bf16[2048,128]{1,0:T(8,128)(2,1)S(1)}, u32[]{:S(2)}, u32[]{:S(2)}) collective-permute-start(bf16[2048,128]{1,0:T(8,128)(2,1)S(1)} %get-tuple-element.66), channel_id=1, source_target_pairs={{0,8},{1,9},{2,10},{3,11},{4,12},{5,13},{6,14},{7,15},{8,0},{9,1},... | collective-permute-start | bytes 1572872 | tf_op jit(solution)/shard_map/ppermute | solution.py:363
  28.6 11.5 %collective-permute-start.14 = (bf16[1024,128]{1,0:T(8,128)(2,1)S(1)}, bf16[1024,128]{1,0:T(8,128)(2,1)S(1)}, u32[]{:S(2)}, u32[]{:S(2)}) collective-permute-start(bf16[1024,128]{1,0:T(8,128)(2,1)S(1)} %pad_maximum_fusion.3), channel_id=1, source_target_pairs={{0,16},{1,17},{2,18},{3,19},{4,20},{5,21},{6,22},{7,23},{8,24},{9,... | collective-permute-start | bytes 786440 | tf_op jit(solution)/shard_map/ppermute | solution.py:363
  30.0 19.4 %copy-start.1 = (bf16[2,128,512]{2,1,0:T(8,128)(2,1)S(1)}, bf16[2,128,512]{2,1,0:T(8,128)(2,1)}, u32[]{:S(2)}) copy-start(bf16[2,128,512]{2,1,0:T(8,128)(2,1)} %frames.4) | copy-start | bytes 786436
  30.1 9.2 %collective-permute-start.16 = (bf16[1024,128]{1,0:T(8,128)(2,1)S(1)}, bf16[1024,128]{1,0:T(8,128)(2,1)S(1)}, u32[]{:S(2)}, u32[]{:S(2)}) collective-permute-start(bf16[1024,128]{1,0:T(8,128)(2,1)S(1)} %add_convert_fusion), channel_id=1, source_target_pairs={{0,1},{1,0},{2,3},{3,2},{4,5},{5,4},{6,7},{7,6},{8,10},{9,11},{10,... | collective-permute-start | bytes 786440 | tf_op jit(solution)/shard_map/ppermute | solution.py:363
  35.0 7.5 %collective-permute-start.9 = (bf16[1024,128]{1,0:T(8,128)(2,1)S(1)}, bf16[1024,128]{1,0:T(8,128)(2,1)S(1)}, u32[]{:S(2)}, u32[]{:S(2)}) collective-permute-start(bf16[1024,128]{1,0:T(8,128)(2,1)S(1)} %add_convert_fusion.1), channel_id=1, source_target_pairs={{0,1},{1,0},{2,3},{3,2},{4,5},{5,4},{6,7},{7,6},{8,10},{9,11},{10,... | collective-permute-start | bytes 786440 | tf_op jit(solution)/shard_map/ppermute | solution.py:363
  39.4 7.4 %collective-permute-start.22 = (bf16[512,128]{1,0:T(8,128)(2,1)S(1)}, bf16[512,128]{1,0:T(8,128)(2,1)S(1)}, u32[]{:S(2)}, u32[]{:S(2)}) collective-permute-start(bf16[512,128]{1,0:T(8,128)(2,1)S(1)} %add_convert_fusion.2), channel_id=1, source_target_pairs={{0,16},{1,17},{2,18},{3,19},{4,20},{5,21},{6,22},{7,23},{8,9},{9,8... | collective-permute-start | bytes 393224 | tf_op jit(solution)/shard_map/ppermute | solution.py:363
  42.6 6.9 %collective-permute-start.10 = (bf16[512,128]{1,0:T(8,128)(2,1)S(1)}, bf16[512,128]{1,0:T(8,128)(2,1)S(1)}, u32[]{:S(2)}, u32[]{:S(2)}) collective-permute-start(bf16[512,128]{1,0:T(8,128)(2,1)S(1)} %add_convert_fusion.3), channel_id=1, source_target_pairs={{0,16},{1,17},{2,18},{3,19},{4,20},{5,21},{6,22},{7,23},{8,9},{9,8... | collective-permute-start | bytes 393224 | tf_op jit(solution)/shard_map/ppermute | solution.py:363
  44.2 22.6 %collective-permute-start.17 = (bf16[128,128]{1,0:T(8,128)(2,1)S(1)}, bf16[128,128]{1,0:T(8,128)(2,1)S(1)}, u32[]{:S(2)}, u32[]{:S(2)}) collective-permute-start(bf16[128,128]{1,0:T(8,128)(2,1)S(1)} %get-tuple-element.73), channel_id=1, source_target_pairs={{0,1},{1,0},{2,3},{3,2},{4,5},{5,4},{6,7},{7,6},{8,9},{9,8},{10,11... | collective-permute-start | bytes 98312 | tf_op jit(solution)/shard_map/ppermute | solution.py:363
  46.8 15.8 %collective-permute-start.23 = (bf16[256,128]{1,0:T(8,128)(2,1)S(1)}, bf16[256,128]{1,0:T(8,128)(2,1)S(1)}, u32[]{:S(2)}, u32[]{:S(2)}) collective-permute-start(bf16[256,128]{1,0:T(8,128)(2,1)S(1)} %add_convert_fusion.6), channel_id=1, source_target_pairs={{0,4},{1,5},{2,6},{3,7},{4,0},{5,1},{6,2},{7,3},{8,24},{9,25},{10,... | collective-permute-start | bytes 196616 | tf_op jit(solution)/shard_map/ppermute | solution.py:363
  52.3 4.9 %collective-permute-start.25 = (bf16[128,128]{1,0:T(8,128)(2,1)S(1)}, bf16[128,128]{1,0:T(8,128)(2,1)S(1)}, u32[]{:S(2)}, u32[]{:S(2)}) collective-permute-start(bf16[128,128]{1,0:T(8,128)(2,1)S(1)} %shard_map.129), channel_id=1, source_target_pairs={{0,2},{1,3},{2,0},{3,1},{4,6},{5,7},{6,4},{7,5},{8,12},{9,13},{10,... | collective-permute-start | bytes 98312 | tf_op jit(solution)/shard_map/ppermute | solution.py:363
  54.5 7.9 %collective-permute-start.11 = (bf16[256,128]{1,0:T(8,128)(2,1)S(1)}, bf16[256,128]{1,0:T(8,128)(2,1)S(1)}, u32[]{:S(2)}, u32[]{:S(2)}) collective-permute-start(bf16[256,128]{1,0:T(8,128)(2,1)S(1)} %add_convert_fusion.9), channel_id=1, source_target_pairs={{0,4},{1,5},{2,6},{3,7},{4,0},{5,1},{6,2},{7,3},{8,24},{9,25},{10,... | collective-permute-start | bytes 196616 | tf_op jit(solution)/shard_map/ppermute | solution.py:363
  62.5 4.3 %collective-permute-start.12 = (bf16[256,128]{1,0:T(8,128)(2,1)S(1)}, bf16[256,128]{1,0:T(8,128)(2,1)S(1)}, u32[]{:S(2)}, u32[]{:S(2)}) collective-permute-start(bf16[256,128]{1,0:T(8,128)(2,1)S(1)} %add_convert_fusion.8), channel_id=1, source_target_pairs={{0,2},{1,3},{2,0},{3,1},{4,6},{5,7},{6,4},{7,5},{8,12},{9,13},{10,... | collective-permute-start | bytes 196616 | tf_op jit(solution)/shard_map/ppermute | solution.py:363
  62.6 4.9 %collective-permute-start.24 = (bf16[256,128]{1,0:T(8,128)(2,1)S(1)}, bf16[256,128]{1,0:T(8,128)(2,1)S(1)}, u32[]{:S(2)}, u32[]{:S(2)}) collective-permute-start(bf16[256,128]{1,0:T(8,128)(2,1)S(1)} %add_convert_fusion.5), channel_id=1, source_target_pairs={{0,2},{1,3},{2,0},{3,1},{4,6},{5,7},{6,4},{7,5},{8,12},{9,13},{10,... | collective-permute-start | bytes 196616 | tf_op jit(solution)/shard_map/ppermute | solution.py:363
  66.8 5.4 %collective-permute-start.18 = (bf16[256,128]{1,0:T(8,128)(2,1)S(1)}, bf16[256,128]{1,0:T(8,128)(2,1)S(1)}, u32[]{:S(2)}, u32[]{:S(2)}) collective-permute-start(bf16[256,128]{1,0:T(8,128)(2,1)S(1)} %add_convert_fusion.7), channel_id=1, source_target_pairs={{0,4},{1,5},{2,6},{3,7},{4,0},{5,1},{6,2},{7,3},{8,24},{9,25},{10,... | collective-permute-start | bytes 196616 | tf_op jit(solution)/shard_map/ppermute | solution.py:363
  67.5 6.8 %collective-permute-start.26 = (bf16[384,128]{1,0:T(8,128)(2,1)S(1)}, bf16[384,128]{1,0:T(8,128)(2,1)S(1)}, u32[]{:S(2)}, u32[]{:S(2)}) collective-permute-start(bf16[384,128]{1,0:T(8,128)(2,1)S(1)} %pad_maximum_fusion.7), channel_id=1, source_target_pairs={{0,4},{1,5},{2,6},{3,7},{4,0},{5,1},{6,2},{7,3},{8,24},{9,25},{10,... | collective-permute-start | bytes 294920 | tf_op jit(solution)/shard_map/ppermute | solution.py:363
  69.9 2.3 %collective-permute-start.19 = (bf16[128,128]{1,0:T(8,128)(2,1)S(1)}, bf16[128,128]{1,0:T(8,128)(2,1)S(1)}, u32[]{:S(2)}, u32[]{:S(2)}) collective-permute-start(bf16[128,128]{1,0:T(8,128)(2,1)S(1)} %get-tuple-element.76), channel_id=1, source_target_pairs={{1,2},{3,4},{5,6},{9,10},{11,12},{13,14},{17,18},{19,20},{21,22},{... | collective-permute-start | bytes 98312 | tf_op jit(solution)/shard_map/ppermute | solution.py:363
  72.2 5.0 %collective-permute-start.20 = (bf16[512,128]{1,0:T(8,128)(2,1)S(1)}, bf16[512,128]{1,0:T(8,128)(2,1)S(1)}, u32[]{:S(2)}, u32[]{:S(2)}) collective-permute-start(bf16[512,128]{1,0:T(8,128)(2,1)S(1)} %pad_maximum_fusion.6), channel_id=1, source_target_pairs={{0,16},{1,17},{2,18},{3,19},{4,20},{5,21},{6,22},{7,23},{8,9},{9,8... | collective-permute-start | bytes 393224 | tf_op jit(solution)/shard_map/ppermute | solution.py:363
  74.3 5.4 %collective-permute-start.27 = (bf16[640,128]{1,0:T(8,128)(2,1)S(1)}, bf16[640,128]{1,0:T(8,128)(2,1)S(1)}, u32[]{:S(2)}, u32[]{:S(2)}) collective-permute-start(bf16[640,128]{1,0:T(8,128)(2,1)S(1)} %pad_maximum_fusion.5), channel_id=1, source_target_pairs={{0,16},{1,17},{2,18},{3,19},{4,20},{5,21},{6,22},{7,23},{8,9},{9,8... | collective-permute-start | bytes 491528 | tf_op jit(solution)/shard_map/ppermute | solution.py:363
  77.3 11.9 %collective-permute-start.29 = (bf16[1024,128]{1,0:T(8,128)(2,1)S(1)}, bf16[1024,128]{1,0:T(8,128)(2,1)S(1)}, u32[]{:S(2)}, u32[]{:S(2)}) collective-permute-start(bf16[1024,128]{1,0:T(8,128)(2,1)S(1)} %constant_dynamic-update-slice_fusion.refs_0_), channel_id=1, source_target_pairs={{0,8},{1,9},{2,10},{3,11},{4,12},{5,13},{6,14},{7,15},{8,0},{9,1},... | collective-permute-start | bytes 786440 | tf_op jit(solution)/shard_map/ppermute | solution.py:363
  79.8 6.5 %copy-start.2 = (bf16[2,128,512]{2,1,0:T(8,128)(2,1)S(1)}, bf16[2,128,512]{2,1,0:T(8,128)(2,1)}, u32[]{:S(2)}) copy-start(bf16[2,128,512]{2,1,0:T(8,128)(2,1)} %cot.1) | copy-start | bytes 786436
  79.8 6.5 %copy-start.4 = (f32[31,512]{1,0:T(8,128)S(1)}, f32[31,512]{1,0:T(8,128)}, u32[]{:S(2)}) copy-start(f32[31,512]{1,0:T(8,128)} %kern.3) | copy-start | bytes 190468
  79.8 12.2 %collective-permute-start.28 = (bf16[1152,128]{1,0:T(8,128)(2,1)S(1)}, bf16[1152,128]{1,0:T(8,128)(2,1)S(1)}, u32[]{:S(2)}, u32[]{:S(2)}) collective-permute-start(bf16[1152,128]{1,0:T(8,128)(2,1)S(1)} %pad_maximum_fusion.1), channel_id=1, source_target_pairs={{0,1},{1,0},{2,3},{3,2},{4,5},{5,4},{6,7},{7,6},{8,10},{9,11},{10,... | collective-permute-start | bytes 884744 | tf_op jit(solution)/shard_map/ppermute | solution.py:363
  84.5 4.6 %collective-permute-start.30 = (bf16[1024,128]{1,0:T(8,128)(2,1)S(1)}, bf16[1024,128]{1,0:T(8,128)(2,1)S(1)}, u32[]{:S(2)}, u32[]{:S(2)}) collective-permute-start(bf16[1024,128]{1,0:T(8,128)(2,1)S(1)} %pad_maximum_fusion.4.refs_1_), channel_id=1, source_target_pairs={{0,8},{1,9},{2,10},{3,11},{4,12},{5,13},{6,14},{7,15},{8,0},{9,1},... | collective-permute-start | bytes 786440 | tf_op jit(solution)/shard_map/ppermute | solution.py:363
  84.6 7.4 %collective-permute-start.21 = (bf16[1024,128]{1,0:T(8,128)(2,1)S(1)}, bf16[1024,128]{1,0:T(8,128)(2,1)S(1)}, u32[]{:S(2)}, u32[]{:S(2)}) collective-permute-start(bf16[1024,128]{1,0:T(8,128)(2,1)S(1)} %constant_dynamic-update-slice_fusion.refs_0_), channel_id=1, source_target_pairs={{0,1},{1,0},{2,3},{3,2},{4,5},{5,4},{6,7},{7,6},{8,10},{9,11},{10,... | collective-permute-start | bytes 786440 | tf_op jit(solution)/shard_map/ppermute | solution.py:363
  92.1 2.2 %collective-permute-start.32 = (bf16[1152,128]{1,0:T(8,128)(2,1)S(1)}, bf16[1152,128]{1,0:T(8,128)(2,1)S(1)}, u32[]{:S(2)}, u32[]{:S(2)}) collective-permute-start(bf16[1152,128]{1,0:T(8,128)(2,1)S(1)} %pad_maximum_fusion.2), channel_id=1, source_target_pairs={{0,8},{1,9},{2,10},{3,11},{4,12},{5,13},{6,14},{7,15},{8,0},{9,1},... | collective-permute-start | bytes 884744 | tf_op jit(solution)/shard_map/ppermute | solution.py:363
  92.2 2.1 %collective-permute-start.31 = (bf16[1024,128]{1,0:T(8,128)(2,1)S(1)}, bf16[1024,128]{1,0:T(8,128)(2,1)S(1)}, u32[]{:S(2)}, u32[]{:S(2)}) collective-permute-start(bf16[1024,128]{1,0:T(8,128)(2,1)S(1)} %collective-permute-done.21.refs_0_), channel_id=1, source_target_pairs={{0,8},{1,9},{2,10},{3,11},{4,12},{5,13},{6,14},{7,15},{8,0},{9,1},... | collective-permute-start | bytes 786440 | tf_op jit(solution)/shard_map/ppermute | solution.py:363

commit v13 on v6

--- a/solution.py
+++ b/solution.py
@@ -41,23 +41,11 @@
 
 
 def ways(bits, half):
-    return [bits[i] for i in ((X, Y, Z), (Z, ZZ, X))[half]]
+    return [bits[i] for i in ((X, Y, Z), (Z, X, ZZ))[half]]
 
 
 def sigmoid(v):
     return 0.5 * jnp.tanh(0.5 * v) + 0.5
-
-
-def scatter_kernel(sub, bits, source, *refs):
-    outs, sems = refs[:4], refs[4]
-    copies = []
-    for d in range(4):
-        rows = pl.ds(pl.multiple_of(bits[BLOCK_AT + d] * sub, sub), sub)
-        copies.append(pltpu.make_async_copy(source.at[:, rows], outs[d], sems.at[d]))
-    for copy in copies:
-        copy.start()
-    for copy in copies:
-        copy.wait()
 
 
 def edge_kernel(sub, bits, f0, f1, f2, f3, near, side):
@@ -216,21 +204,22 @@
 
     tap_s[cols * 32 :, :] = jnp.zeros((HALO, LANES), F32)
     size = cols * width // 8
-    span = size + HALO
     core = bits[CORE]
     for out, owner, h in (
         (a_send, 1 - core, 0), (b_send, 1 - core, 1), (a_keep, core, 0), (b_keep, core, 1)
     ):
         i = owner * 2 + h
+        span = size + HALO * (1 - h)
         first, second, third = ways(bits, h)
         grad = mm(left_s[i // 3], flat(i), TN).astype(BF)
         for piece in range(8):
             cb, at = piece * size // width, piece * size % width
-            tail = tap_s[pl.ds(pl.multiple_of((i * 8 + piece) * cols, cols), HALO), :]
             rel = ((piece // 4) ^ first) * 4 + ((piece // 2 % 2) ^ second) * 2 + ((piece % 2) ^ third)
             start = pl.multiple_of(rel * span, HALO)
             out[pl.ds(start, size), :] = grad[at : at + size, cb * LANES : (cb + 1) * LANES]
-            out[pl.ds(pl.multiple_of(start + size, HALO), HALO), :] = tail.astype(BF)
+            if h == 0:
+                tail = tap_s[pl.ds(pl.multiple_of((owner * 8 + piece) * 8, 8), HALO), :]
+                out[pl.ds(pl.multiple_of(start + size, HALO), HALO), :] = tail.astype(BF)
 
     proj = mm(left_s[1], wo[...])
     unit = 2 * count * cols * sub
@@ -253,51 +242,49 @@
     return functools.reduce(lambda x, y: x + y, [x.astype(F32) for x in parts]).astype(BF)
 
 
-def final_kernel(plan, first_call, bits, a_near, b_near, a_far, b_far, *refs):
-    width, norm = plan
+def final_kernel(plan, bits, *refs):
+    kinds, first_call, with_taps, width, norm = plan
     cols = width // LANES
     size = cols * width // 8
     span = size + HALO
-    if first_call:
-        outs, tails, (grad_s, sems) = refs[:4], refs[4], refs[5:]
-    else:
-        tails, outs, taps, (grad_s, sems, tail_s) = refs[4], refs[5:9], refs[9], refs[10:]
     core = bits[CORE]
-    owner = core if first_call else 1 - core
-    for h in range(2):
+
+    def piece_of(h, far, rel):
         first, second, third = ways(bits, h)
-        parts = ((a_near, a_far), (b_near, b_far))[h]
-        for rel in range(8):
-            part, start = parts[rel // 4], rel % 4 * span
-            piece = (first ^ (rel // 4)) * 4 + (second ^ (rel // 2 % 2)) * 2 + (third ^ (rel % 2))
+        return (first ^ far) * 4 + (second ^ (rel // 2)) * 2 + (third ^ (rel % 2))
+
+    got, refs = refs[: len(kinds)], refs[len(kinds) :]
+    if with_taps:
+        tap_refs, refs, tap_grad, tap_s = refs[:4], refs[4:-4] + refs[-3:-1], refs[-4], refs[-1]
+        for n, ref in enumerate(tap_refs):
+            owner = core if n < 2 else 1 - core
+            for rel in range(4):
+                at = rel * span + size
+                tap_s[owner * 8 + piece_of(0, n % 2, rel)] = ref[at : at + HALO, :].astype(F32) * norm
+        for g in range(16):
+            lc, j = g // 4, g % 4 * 8
+            kept = min(8, 31 - j)
+            tap_grad[j : j + kept, lc * LANES : (lc + 1) * LANES] = tap_s[g, 0:kept]
+    *outs, piece_s, sems = refs if first_call else refs[4:]
+    copies = []
+    for n, (own, h, far) in enumerate(kinds):
+        owner = core if own else 1 - core
+        for rel in range(4):
+            k = 4 * n + rel
+            at = rel * (size + HALO * (1 - h))
+            piece_s[k] = got[n][at : at + size, :].astype(F32) * norm
+            piece = piece_of(h, far, rel)
             cb, at = piece * size // width, piece * size % width
-            grad_s[
-                h,
-                pl.ds(pl.multiple_of(at, size), size),
-                pl.ds(pl.multiple_of(cb * LANES, LANES), LANES),
-            ] = part[start : start + size, :].astype(F32) * norm
-            tail = part[start + size : start + span, :].astype(F32) * norm
-            if first_call:
-                tails[h * 8 + piece] = tail
-            else:
-                tail_s[owner * 16 + h * 8 + piece] = tail
-        for which in range(2):
-            @pl.when(owner == which)
-            def _():
-                pltpu.make_async_copy(grad_s.at[h], outs[2 * which + h], sems.at[h]).start()
-    if not first_call:
-        for n in range(16):
-            tail_s[core * 16 + n] = tails[n]
-        for g in range(32):
-            row = g * cols
-            lc, j = row // 32, row % 32
-            kept = min(cols, 31 - j)
-            taps[j : j + kept, lc * LANES : (lc + 1) * LANES] = tail_s[g, 0:kept]
-    for h in range(2):
-        for which in range(2):
-            @pl.when(owner == which)
-            def _():
-                pltpu.make_async_copy(grad_s.at[h], outs[2 * which + h], sems.at[h]).wait()
+            rows = pl.ds(pl.multiple_of(at, size), size)
+            lanes = pl.ds(pl.multiple_of(cb * LANES, LANES), LANES)
+            for which in range(2):
+                copy = pltpu.make_async_copy(
+                    piece_s.at[k], outs[2 * which + h].at[rows, lanes], sems.at[k]
+                )
+                copies.append((owner == which, copy))
+                pl.when(owner == which)(copy.start)
+    for here, copy in copies:
+        pl.when(here)(copy.wait)
 
 
 def home_kernel(plan, bits, own, core_got, y_got, layer_out, dconv, x_edge, z_edge):
@@ -398,14 +385,12 @@
     def both(pairs):
         return pairs + [(j, i) for i, j in pairs]
 
-    block = shape((count, sub, width), BF)
     masks = (0, over_core, over_y, over_core + over_y)
 
     def scattered(x):
-        parts = call(
-            functools.partial(scatter_kernel, sub), (block,) * 4,
-            [pltpu.SemaphoreType.DMA((4,))], 8, bits, x, hbm=(1,),
-        )
+        parts = [
+            lax.dynamic_slice_in_dim(x, order(mic ^ d) * sub, sub, axis=1) for d in range(4)
+        ]
         got = {d: swap(parts[d], masks[d]) for d in (2, 3, 1)}
         return [parts[0], got[1], got[2], got[3]]
 
@@ -440,7 +425,7 @@
     )
     a_keep, b_keep, a_send, b_send, back_keep, back_send = call(
         functools.partial(main_kernel, (groups, count, sub, width, factor)),
-        (flat(8 * span),) * 4 + (flat(2 * unit),) * 2,
+        (flat(8 * span), flat(8 * size)) * 2 + (flat(2 * unit),) * 2,
         [
             pltpu.VMEM((2, rows, width), BF),
             pltpu.VMEM((4, cuts, groups, count, HALO, width), BF),
@@ -452,14 +437,12 @@
 
     lines = [2**i for i in range(1, blocks.bit_length() - 1)]
 
-    def sent(parts, n):
-        return total(*(t[n : 2 * n] for t in parts))
-
-    def kept(parts, got, n):
-        return [t[:n] for t in parts] + [got[:n]]
-
-    def halved(parts, n, mask):
-        return kept(parts, swap(sent(parts, n), mask), n)
+    def after(x, y):
+        return lax.optimization_barrier((x, y))[0]
+
+    def halved(parts, mask):
+        n = parts[0].shape[0] // 2
+        return [t[:n] for t in parts] + [swap(total(*(t[n:] for t in parts)), mask)]
 
     def exchanged(parts, masks):
         mine = total(*parts)
@@ -473,8 +456,8 @@
     a = [a_keep, swap(a_send, over_core)]
     b = [b_keep, swap(b_send, over_core)]
     core_got = swap(back_send, over_core)
-    a = halved(a, 4 * span, over_x)
-    b = halved(b, 4 * span, lines[0])
+    a = halved(a, over_x)
+    b = halved(b, lines[0])
     y_got = swap(jnp.concatenate([back_keep[unit:], core_got[unit:]]), over_y)
     edge = flat(count * cols * HALO)
     layer_out, dconv, x_edge, z_edge = call(
@@ -482,44 +465,56 @@
         (shape(frames.shape, BF), shape((count, cols, length, LANES), BF), edge, edge),
         [], 8, bits, back_keep, core_got, y_got,
     )
+    a = halved(a, over_y)
+    b = halved(b, over_x)
+    a = halved(a, lines[0])
+    b = halved(b, lines[1])
+    a = exchanged(a, lines[1:])
+    b = exchanged(b, [over_y] + lines[2:])
+    x_got = swap(x_edge, over_x)
     z_got = permute(
-        z_edge,
+        after(z_edge, a),
         both([(m * blocks + t, m * blocks + t + 1)
               for m in range(groups) for t in range(1, blocks - 1, 2)]),
     )
-    a = halved(a, 2 * span, over_y)
-    b = halved(b, 2 * span, lines[1])
-    a = halved(a, span, lines[0])
-    x_got = swap(jnp.concatenate([sent(b, span), x_edge]), over_x)
-    b = kept(b, x_got, span)
-    a = exchanged(a, lines[1:])
-    b = exchanged(b, [over_y] + lines[2:])
     a = doubled(a, lines[0])
-    b = doubled(b, over_x)
-    b, z_got = lax.optimization_barrier((b, z_got))
-    (frame_grad,) = call(
-        functools.partial(frame_kernel, (count, cols, span, length)),
-        (shape(frames.shape, BF),), [], 8, bits, dconv, x_got, z_got, cotangent, kernel,
-    )
-    a = doubled(a, over_y)
     b = doubled(b, lines[1])
+    a = doubled(after(a, x_got), over_y)
+    b = doubled(after(b, z_got), over_x)
+
+    norm = 1.0 / math.sqrt(groups * count * blocks * length)
+    square = shape((width, width), F32)
+
+    def final(kinds, parts, grads, taps=()):
+        first = 1 + len(parts) + len(taps)
+        scratch = [
+            pltpu.VMEM((4 * len(kinds), size, LANES), F32),
+            pltpu.SemaphoreType.DMA((4 * len(kinds),)),
+        ]
+        return call(
+            functools.partial(final_kernel, (kinds, not grads, bool(taps), width, norm)),
+            (square,) * 4 + (shape((31, width), F32),) * bool(taps),
+            scratch + [pltpu.VMEM((16, HALO, LANES), F32)] * bool(taps),
+            10, bits, *parts, *taps, *grads, hbm=range(first, first + len(grads)),
+            hbm_outs=range(4), aliases={first + i: i for i in range(len(grads))},
+        )
+
     a_far, b_far = swap(a, over_x), swap(b, lines[0])
     a_other, b_other = swap(a, over_core), swap(b, over_core)
-    a_other_far, b_other_far = swap(a_far, over_core), swap(b_far, over_core)
-
-    norm = 1.0 / math.sqrt(groups * count * blocks * length)
-    square = shape((width, width), F32)
-    scratch = [pltpu.VMEM((2, width, width), F32), pltpu.SemaphoreType.DMA((2,))]
-    final = functools.partial(final_kernel, (width, norm))
-    *grads, tails = call(
-        functools.partial(final, True), (square,) * 4 + (shape((16, HALO, LANES), F32),), scratch,
-        8, bits, a, b, a_far, b_far, hbm_outs=range(4),
-    )
-    *grads, kernel_grad = call(
-        functools.partial(final, False), (square,) * 4 + (shape((31, width), F32),),
-        scratch + [pltpu.VMEM((32, HALO, LANES), F32)],
-        8, bits, a_other, b_other, a_other_far, b_other_far, *grads, tails,
-        hbm=range(5, 9), hbm_outs=range(4), aliases={5 + i: i for i in range(4)},
+    (frame_grad,) = call(
+        functools.partial(frame_kernel, (count, cols, 0, length)),
+        (shape(frames.shape, BF),), [], 8,
+        bits, after(dconv, a), x_got, z_got, cotangent, kernel,
+    )
+    grads = final(((1, 0, 0), (1, 1, 0), (0, 0, 0), (0, 1, 0)), (a, b, a_other, b_other), ())
+    a_far, b_far, frame_grad, *grads = lax.optimization_barrier(
+        (a_far, b_far, frame_grad, *grads)
+    )
+    taps = (a, a_far, a_other)
+    a_other, b_other = swap(a_far, over_core), swap(b_far, over_core)
+    grads = final(((1, 0, 1), (1, 1, 1)), (a_far, b_far), grads)
+    *grads, kernel_grad = final(
+        ((0, 0, 1), (0, 1, 1)), (a_other, b_other), grads, (*taps, a_other)
     )
     return (layer_out, frame_grad, kernel_grad, *grads)
 

time: 89.9 us -> 87.7 us (0.976)
  waiting for transfers between devices: 28.1 us -> 23.6 us
  starting transfers between devices: 35.1 us -> 37.9 us
    ppermute x31 -> x32, waiting for transfers between devices: 28.1 us -> 23.6 us  [permute(): return lax.ppermute(x, ('mic', 'tm'), pairs)]
    ppermute x31 -> x32, starting transfers between devices: 35.1 us -> 37.9 us  [permute(): return lax.ppermute(x, ('mic', 'tm'), pairs)]
    dynamic_slice x0 -> x2, local copies, waits for them, and re-layouts: none -> 1 us  [scattered(): lax.dynamic_slice_in_dim(x, order(mic ^ d) * sub, sub, axis=1)]
    unnamed x7 -> x6, local copies, waits for them, and re-layouts: 0.97 us -> 0.03 us
    pallas_call x9 -> x8, Pallas kernels: 21.9 us -> 21.4 us  [call(): pl.pallas_call(body, out_shape=outs, in_specs=[pl.BlockSpec(memory_space=...]
  transfers between devices with their start and end apart: 31 -> 32, of which waited for: 16 -> 14; matrix products, arithmetic and copies ran while one was open for 3% -> 3% of each run, Pallas kernels for 11% -> 12%
where the time goes in v13:
time: 87.7 us; the launch traced here: 87.5 us
  starting transfers between devices  37.9 us (43%)
  waiting for transfers between devices  23.6 us (27%)
  Pallas kernels  21.4 us (24%)
  other arithmetic  2.35 us (3%)
  local copies, waits for them, and re-layouts  1.17 us (1%)
  between operations  1.04 us (1%)
    ppermute x32, starting transfers between devices, permute(): return lax.ppermute(x, ('mic', 'tm'), pairs)  37.9 us
    ppermute x32, waiting for transfers between devices, permute(): return lax.ppermute(x, ('mic', 'tm'), pairs)  23.6 us
    pallas_call x8, Pallas kernels, call(): pl.pallas_call(body, out_shape=outs, in_specs=[pl.BlockSpec(memory_space=...  21.4 us
    another operation x1, other arithmetic, shards(): weights = jnp.stack([w_query, w_key, w_value, w_out])  1.82 us
  transfers between devices with their start and end apart: 32, of which 14 were waited for; matrix products, arithmetic and copies ran while one was open for 3% of the time, Pallas kernels for 12%

profile of v13, /device:TPU:0, one launch (start us, length us, event | category | flops | bytes accessed | tf_op | source)
XLA Modules:
  0.0 87.5 jit_solution(7778090086801701008)
XLA Ops:
  0.7 1.0 %constant_dynamic-slice_fusion.4 = (bf16[2,32,512]{2,1,0:T(8,128)(2,1)S(1)}, bf16[2,32,512]{2,1,0:T(8,128)(2,1)S(1)}, bf16[2,32,512]{2,1,0:T(8,128)(2,1)S(1)}, bf16[2,32,512]{2,1,0:T(8,128)(2,1)S(1)}) fusion(bf16[2,128,512]{2,1,0:T(8,128)(2,1)} %param.7, s32[]{:T(128)S(6)} %select_n.95, s32[]{:T(128)S(6)} %select_n.93, s32[]{:T(128)S(6)} %select_n.92, ...), kind=kLoop, calls=%fused_computation.22 | loop fusion | bytes 524304 | tf_op jit(solution)/shard_map/dynamic_slice | solution.py:392
  1.7 0.5 collective-permute-start
  2.2 2.6 %collective-permute-start.1 = (bf16[2,32,512]{2,1,0:T(8,128)(2,1)S(1)}, bf16[2,32,512]{2,1,0:T(8,128)(2,1)S(1)}, u32[]{:S(2)}, u32[]{:S(2)}) collective-permute-start(bf16[2,32,512]{2,1,0:T(8,128)(2,1)S(1)} %get-tuple-element.98), channel_id=1, source_target_pairs={{0,16},{1,17},{2,18},{3,19},{4,20},{5,21},{6,22},{7,23},{8,24},{9,... | collective-permute-start | bytes 196616 | tf_op jit(solution)/shard_map/ppermute | solution.py:380
  4.8 1.8 %pad_maximum_fusion.weights = bf16[4,512,512]{2,1,0:T(8,128)(2,1)S(1)} fusion(bf16[1,512,512]{2,1,0:T(8,128)(2,1)} %bitcast.15, bf16[1,512,512]{2,1,0:T(8,128)(2,1)} %bitcast.16, bf16[1,512,512]{2,1,0:T(8,128)(2,1)} %bitcast.17, bf16[1,512,512]{2,1,0:T(8,128)(2,1)} %bitcast.18), kind=kLoop, calls=%fused_computation | loop fusion | flops 3145728 | bytes 4194304 | tf_op jit(solution)/shard_map/stack | solution.py:398
  6.9 0.6 collective-permute-done.1.f2
  7.5 1.4 %collective-permute-done.2.f3 = bf16[2,32,512]{2,1,0:T(8,128)(2,1)S(1)} collective-permute-done((bf16[2,32,512]{2,1,0:T(8,128)(2,1)S(1)}, bf16[2,32,512]{2,1,0:T(8,128)(2,1)S(1)}, u32[]{:S(2)}, u32[]{:S(2)}) %collective-permute-start.2) | collective-permute-done | bytes 65568 | tf_op jit(solution)/shard_map/ppermute | solution.py:380
  8.8 0.6 shard_map.126
  9.4 0.2 collective-permute-start.3
  9.6 0.7 collective-permute-start.4
  10.3 2.7 %collective-permute-start.5 = (bf16[2,32,512]{2,1,0:T(8,128)(2,1)S(1)}, bf16[2,32,512]{2,1,0:T(8,128)(2,1)S(1)}, u32[]{:S(2)}, u32[]{:S(2)}) collective-permute-start(bf16[2,32,512]{2,1,0:T(8,128)(2,1)S(1)} %get-tuple-element.93), channel_id=1, source_target_pairs={{0,8},{1,9},{2,10},{3,11},{4,12},{5,13},{6,14},{7,15},{8,0},{9,1},... | collective-permute-start | bytes 196616 | tf_op jit(solution)/shard_map/ppermute | solution.py:380
  13.0 1.6 %collective-permute-start.6 = (bf16[2,32,512]{2,1,0:T(8,128)(2,1)S(1)}, bf16[2,32,512]{2,1,0:T(8,128)(2,1)S(1)}, u32[]{:S(2)}, u32[]{:S(2)}) collective-permute-start(bf16[2,32,512]{2,1,0:T(8,128)(2,1)S(1)} %get-tuple-element.92), channel_id=1, source_target_pairs={{0,16},{1,17},{2,18},{3,19},{4,20},{5,21},{6,22},{7,23},{8,24},{9,... | collective-permute-start | bytes 196616 | tf_op jit(solution)/shard_map/ppermute | solution.py:380
  14.7 2.5 %shard_map.127 = (bf16[4,2,32,512]{3,2,1,0:T(8,128)(2,1)S(1)}, f32[256,512]{1,0:T(8,128)S(1)}, bf16[256,512]{1,0:T(8,128)(2,1)S(1)}) custom-call(s32[11]{0:T(128)S(1)} %stack.62.bits, bf16[2,32,512]{2,1,0:T(8,128)(2,1)S(1)} %get-tuple-element.97.f0, bf16[2,32,512]{2,1,0:T(8,128)(2,1)S(1)} %collective-permute-done.f1, ...), custom_call_target="tpu_custom_call" | custom-call | tf_op jit(solution)/shard_map/pallas_call | solution.py:341
  17.3 1.4 %collective-permute-done.7.c3 = bf16[2,32,512]{2,1,0:T(8,128)(2,1)S(1)} collective-permute-done((bf16[2,32,512]{2,1,0:T(8,128)(2,1)S(1)}, bf16[2,32,512]{2,1,0:T(8,128)(2,1)S(1)}, u32[]{:S(2)}, u32[]{:S(2)}) %collective-permute-start.7) | collective-permute-done | bytes 65568 | tf_op jit(solution)/shard_map/ppermute | solution.py:380
  18.7 8.4 %shard_map.128 = (bf16[2176,128]{1,0:T(8,128)(2,1)S(1)}, bf16[2048,128]{1,0:T(8,128)(2,1)S(1)}, bf16[2176,128]{1,0:T(8,128)(2,1)S(1)}, bf16[2048,128]{1,0:T(8,12...) custom-call(s32[11]{0:T(128)S(1)} %stack.62.bits, ...), custom_call_target="tpu_custom_call" | custom-call | tf_op jit(solution)/shard_map/pallas_call | solution.py:341
  27.1 0.2 collective-permute-start.19
  27.4 0.4 collective-permute-start.8
  27.9 1.6 %collective-permute-done.8.core_got = bf16[1024,128]{1,0:T(8,128)(2,1)S(1)} collective-permute-done((bf16[1024,128]{1,0:T(8,128)(2,1)S(1)}, bf16[1024,128]{1,0:T(8,128)(2,1)S(1)}, u32[]{:S(2)}, u32[]{:S(2)}) %collective-permute-start.8) | collective-permute-done | bytes 262176 | tf_op jit(solution)/shard_map/ppermute | solution.py:380
  29.5 1.8 %collective-permute-start.9 = (bf16[1024,128]{1,0:T(8,128)(2,1)S(1)}, bf16[1024,128]{1,0:T(8,128)(2,1)S(1)}, u32[]{:S(2)}, u32[]{:S(2)}) collective-permute-start(bf16[1024,128]{1,0:T(8,128)(2,1)S(1)} %pad_maximum_fusion.1), channel_id=1, source_target_pairs={{0,16},{1,17},{2,18},{3,19},{4,20},{5,21},{6,22},{7,23},{8,24},{9,... | collective-permute-start | bytes 786440 | tf_op jit(solution)/shard_map/ppermute | solution.py:380
  31.4 1.7 %collective-permute-start.20 = (bf16[1024,128]{1,0:T(8,128)(2,1)S(1)}, bf16[1024,128]{1,0:T(8,128)(2,1)S(1)}, u32[]{:S(2)}, u32[]{:S(2)}) collective-permute-start(bf16[1024,128]{1,0:T(8,128)(2,1)S(1)} %add_convert_fusion.1), channel_id=1, source_target_pairs={{0,2},{1,3},{2,0},{3,1},{4,6},{5,7},{6,4},{7,5},{8,10},{9,11},{10,... | collective-permute-start | bytes 786440 | tf_op jit(solution)/shard_map/ppermute | solution.py:380
  33.1 1.6 %collective-permute-start.11 = (bf16[1088,128]{1,0:T(8,128)(2,1)S(1)}, bf16[1088,128]{1,0:T(8,128)(2,1)S(1)}, u32[]{:S(2)}, u32[]{:S(2)}) collective-permute-start(bf16[1088,128]{1,0:T(8,128)(2,1)S(1)} %add_convert_fusion), channel_id=1, source_target_pairs={{0,1},{1,0},{2,3},{3,2},{4,5},{5,4},{6,7},{7,6},{8,9},{9,8},{10,11... | collective-permute-start | bytes 835592 | tf_op jit(solution)/shard_map/ppermute | solution.py:380
  34.7 3.3 %collective-permute-done.9.y_got = bf16[1024,128]{1,0:T(8,128)(2,1)S(1)} collective-permute-done((bf16[1024,128]{1,0:T(8,128)(2,1)S(1)}, bf16[1024,128]{1,0:T(8,128)(2,1)S(1)}, u32[]{:S(2)}, u32[]{:S(2)}) %collective-permute-start.9) | collective-permute-done | bytes 262176 | tf_op jit(solution)/shard_map/ppermute | solution.py:380
  38.0 1.3 %shard_map.129 = (bf16[2,128,512]{2,1,0:T(8,128)(2,1)}, bf16[2,4,128,128]{3,2,1,0:T(8,128)(2,1)S(1)}, bf16[128,128]{1,0:T(8,128)(2,1)S(1)}, bf16[128,128]{1,0:T(8,128)(2,1)S(1)}) custom-call(s32[11]{0:T(128)S(1)} %stack.62.bits, bf16[1024,128]{1,0:T(8,128)(2,1)S(1)} %get-tuple-element.57.own, bf16[1024,128]{1,0:T(8,128)(2,1)S(1)} %collective-permute-done.8.core_got, ...), custom_call_target="tpu_custom_call" | custom-call | tf_op jit(solution)/shard_map/pallas_call | solution.py:341
  39.3 2.6 %collective-permute-start.16 = (bf16[128,128]{1,0:T(8,128)(2,1)S(1)}, bf16[128,128]{1,0:T(8,128)(2,1)S(1)}, u32[]{:S(2)}, u32[]{:S(2)}) collective-permute-start(bf16[128,128]{1,0:T(8,128)(2,1)S(1)} %get-tuple-element.62), channel_id=1, source_target_pairs={{0,1},{1,0},{2,3},{3,2},{4,5},{5,4},{6,7},{7,6},{8,9},{9,8},{10,11... | collective-permute-start | bytes 98312 | tf_op jit(solution)/shard_map/ppermute | solution.py:380
  42.1 1.1 %collective-permute-start.12 = (bf16[544,128]{1,0:T(8,128)(2,1)S(1)}, bf16[544,128]{1,0:T(8,128)(2,1)S(1)}, u32[]{:S(2)}, u32[]{:S(2)}) collective-permute-start(bf16[544,128]{1,0:T(8,128)(2,1)S(1)} %add_convert_fusion.2), channel_id=1, source_target_pairs={{0,16},{1,17},{2,18},{3,19},{4,20},{5,21},{6,22},{7,23},{8,24},{9,... | collective-permute-start | bytes 417800 | tf_op jit(solution)/shard_map/ppermute | solution.py:380
  43.3 3.7 %collective-permute-done.21 = bf16[512,128]{1,0:T(8,128)(2,1)S(1)} collective-permute-done((bf16[512,128]{1,0:T(8,128)(2,1)S(1)}, bf16[512,128]{1,0:T(8,128)(2,1)S(1)}, u32[]{:S(2)}, u32[]{:S(2)}) %collective-permute-start.21) | collective-permute-done | bytes 131104 | tf_op jit(solution)/shard_map/ppermute | solution.py:380
  47.0 2.7 %collective-permute-start.22 = (bf16[256,128]{1,0:T(8,128)(2,1)S(1)}, bf16[256,128]{1,0:T(8,128)(2,1)S(1)}, u32[]{:S(2)}, u32[]{:S(2)}) collective-permute-start(bf16[256,128]{1,0:T(8,128)(2,1)S(1)} %add_convert_fusion.9), channel_id=1, source_target_pairs={{0,4},{1,5},{2,6},{3,7},{4,0},{5,1},{6,2},{7,3},{8,12},{9,13},{10,... | collective-permute-start | bytes 196616 | tf_op jit(solution)/shard_map/ppermute | solution.py:380
  49.8 0.6 collective-permute-start.13
  50.3 1.9 %collective-permute-done.22 = bf16[256,128]{1,0:T(8,128)(2,1)S(1)} collective-permute-done((bf16[256,128]{1,0:T(8,128)(2,1)S(1)}, bf16[256,128]{1,0:T(8,128)(2,1)S(1)}, u32[]{:S(2)}, u32[]{:S(2)}) %collective-permute-start.22) | collective-permute-done | bytes 65568 | tf_op jit(solution)/shard_map/ppermute | solution.py:380
  52.3 0.6 collective-permute-start.23
  52.9 1.2 %collective-permute-done.13 = bf16[272,128]{1,0:T(8,128)(2,1)S(1)} collective-permute-done((bf16[272,128]{1,0:T(8,128)(2,1)S(1)}, bf16[272,128]{1,0:T(8,128)(2,1)S(1)}, u32[]{:S(2)}, u32[]{:S(2)}) %collective-permute-start.13) | collective-permute-done | bytes 69664 | tf_op jit(solution)/shard_map/ppermute | solution.py:380
  54.2 1.5 %collective-permute-start.14 = (bf16[272,128]{1,0:T(8,128)(2,1)S(1)}, bf16[272,128]{1,0:T(8,128)(2,1)S(1)}, u32[]{:S(2)}, u32[]{:S(2)}) collective-permute-start(bf16[272,128]{1,0:T(8,128)(2,1)S(1)} %add_convert_fusion.5), channel_id=1, source_target_pairs={{0,4},{1,5},{2,6},{3,7},{4,0},{5,1},{6,2},{7,3},{8,12},{9,13},{10,... | collective-permute-start | bytes 208904 | tf_op jit(solution)/shard_map/ppermute | solution.py:380
  55.7 0.9 %collective-permute-done.23 = bf16[256,128]{1,0:T(8,128)(2,1)S(1)} collective-permute-done((bf16[256,128]{1,0:T(8,128)(2,1)S(1)}, bf16[256,128]{1,0:T(8,128)(2,1)S(1)}, u32[]{:S(2)}, u32[]{:S(2)}) %collective-permute-start.23) | collective-permute-done | bytes 65568 | tf_op jit(solution)/shard_map/ppermute | solution.py:380
  56.7 2.7 %collective-permute-start.24 = (bf16[256,128]{1,0:T(8,128)(2,1)S(1)}, bf16[256,128]{1,0:T(8,128)(2,1)S(1)}, u32[]{:S(2)}, u32[]{:S(2)}) collective-permute-start(bf16[256,128]{1,0:T(8,128)(2,1)S(1)} %add_convert_fusion.7), channel_id=1, source_target_pairs={{0,4},{1,5},{2,6},{3,7},{4,0},{5,1},{6,2},{7,3},{8,12},{9,13},{10,... | collective-permute-start | bytes 196616 | tf_op jit(solution)/shard_map/ppermute | solution.py:380
  59.3 0.9 collective-permute-done.14
  60.2 0.5 collective-permute-start.15
  60.7 0.7 collective-permute-start.25
  61.4 0.9 %collective-permute-done.24 = bf16[256,128]{1,0:T(8,128)(2,1)S(1)} collective-permute-done((bf16[256,128]{1,0:T(8,128)(2,1)S(1)}, bf16[256,128]{1,0:T(8,128)(2,1)S(1)}, u32[]{:S(2)}, u32[]{:S(2)}) %collective-permute-start.24) | collective-permute-done | bytes 65568 | tf_op jit(solution)/shard_map/ppermute | solution.py:380
  62.3 2.3 %collective-permute-done.15 = bf16[272,128]{1,0:T(8,128)(2,1)S(1)} collective-permute-done((bf16[272,128]{1,0:T(8,128)(2,1)S(1)}, bf16[272,128]{1,0:T(8,128)(2,1)S(1)}, u32[]{:S(2)}, u32[]{:S(2)}) %collective-permute-start.15) | collective-permute-done | bytes 69664 | tf_op jit(solution)/shard_map/ppermute | solution.py:380
  64.8 4.9 %collective-permute-start.26 = (bf16[512,128]{1,0:T(8,128)(2,1)S(1)}, bf16[512,128]{1,0:T(8,128)(2,1)S(1)}, u32[]{:S(2)}, u32[]{:S(2)}) collective-permute-start(bf16[512,128]{1,0:T(8,128)(2,1)S(1)} %pad_maximum_fusion.3), channel_id=1, source_target_pairs={{0,1},{1,0},{2,3},{3,2},{4,5},{5,4},{6,7},{7,6},{8,9},{9,8},{10,11... | collective-permute-start | bytes 393224 | tf_op jit(solution)/shard_map/ppermute | solution.py:380
  69.9 4.5 %collective-permute-start.18 = (bf16[1088,128]{1,0:T(8,128)(2,1)S(1)}, bf16[1088,128]{1,0:T(8,128)(2,1)S(1)}, u32[]{:S(2)}, u32[]{:S(2)}) collective-permute-start(bf16[1088,128]{1,0:T(8,128)(2,1)S(1)} %constant_dynamic-update-slice_fusion.refs_0_.refs_2_), channel_id=1, source_target_pairs={{0,1},{1,0},{2,3},{3,2},{4,5},{5,4},{6,7},{7,6},{8,9},{9,8},{10,11... | collective-permute-start | bytes 835592 | tf_op jit(solution)/shard_map/ppermute | solution.py:380
  74.3 0.2 collective-permute-start.29
  74.6 0.4 collective-permute-start.27
  74.9 2.8 %shard_map.130 = bf16[2,128,512]{2,1,0:T(8,128)(2,1)} custom-call(s32[11]{0:T(128)S(1)} %stack.62.bits, bf16[2,4,128,128]{3,2,1,0:T(8,128)(2,1)S(1)} %get-tuple-element.70.dconv, bf16[128,128]{1,0:T(8,128)(2,1)S(1)} %collective-permute-done.16.x_got, bf16[128,128]{1,0:T(8,128)(2,1)S(1)} %collective-permute-done.25.z_got, bf16[2,128,512]{2,1,0:T(8,128)(2,1)S(1)} %copy-done, ...), custom_call_target="tpu_custom_call" | custom-call | tf_op jit(solution)/shard_map/pallas_call | solution.py:341
  77.8 2.0 %shard_map.131 = (f32[512,512]{1,0:T(8,128)}, f32[512,512]{1,0:T(8,128)}, f32[512,512]{1,0:T(8,128)}, f32[512,512]{1,0:T(8,128)}) custom-call(s32[11]{0:T(128)S(1)} %stack.62.bits, bf16[1088,128]{1,0:T(8,128)(2,1)S(1)} %constant_dynamic-update-slice_fusion.refs_0_.refs_2_, bf16[1024,128]{1,0:T(8,128)(2,1)S(1)} %constant_dynamic-update-slice_fusion.2.refs_1_, ...), custom_call_target="tpu_custom_call" | custom-call | tf_op jit(solution)/shard_map/pallas_call | solution.py:341
  79.8 3.4 %collective-permute-done.27.refs_1_ = bf16[1024,128]{1,0:T(8,128)(2,1)S(1)} collective-permute-done((bf16[1024,128]{1,0:T(8,128)(2,1)S(1)}, bf16[1024,128]{1,0:T(8,128)(2,1)S(1)}, u32[]{:S(2)}, u32[]{:S(2)}) %collective-permute-start.27) | collective-permute-done | bytes 262176 | tf_op jit(solution)/shard_map/ppermute | solution.py:380
  83.1 0.5 collective-permute-start.31
  83.6 1.6 %shard_map.132 = (f32[512,512]{1,0:T(8,128)}, f32[512,512]{1,0:T(8,128)}, f32[512,512]{1,0:T(8,128)}, f32[512,512]{1,0:T(8,128)}) custom-call(s32[11]{0:T(128)S(1)} %stack.62.bits, bf16[1088,128]{1,0:T(8,128)(2,1)S(1)} %collective-permute-done.18.refs_0_.refs_3_, ...), custom_call_target="tpu_custom_call", output_to_operand_aliasing={{0}: (3, {}), {1}: (4, {}), {2}: (5, {}), {3}: (6, {})} | custom-call | tf_op jit(solution)/shard_map/pallas_call | solution.py:341
  85.2 2.2 %shard_map.133 = (f32[512,512]{1,0:T(8,128)}, f32[512,512]{1,0:T(8,128)}, f32[512,512]{1,0:T(8,128)}, f32[512,512]{1,0:T(8,128)}, f32[31,512]{1,0:T(8,128)}) custom-call(s32[11]{0:T(128)S(1)} %stack.62.bits, bf16[1088,128]{1,0:T(8,128)(2,1)S(1)} %collective-permute-done.30.refs_0_.refs_5_, ...), custom_call_target="tpu_custom_call", output_to_operand_aliasing={{0}: (7, {}), {1}: (8, {}), {2}: (9, {}), {3}: (10, {})} | custom-call | tf_op jit(solution)/shard_map/pallas_call | solution.py:341
  (51 shorter events, 1.5 us)
Async XLA Ops:
  1.7 5.2 %collective-permute-start = (bf16[2,32,512]{2,1,0:T(8,128)(2,1)S(1)}, bf16[2,32,512]{2,1,0:T(8,128)(2,1)S(1)}, u32[]{:S(2)}, u32[]{:S(2)}) collective-permute-start(bf16[2,32,512]{2,1,0:T(8,128)(2,1)S(1)} %get-tuple-element.96), channel_id=1, source_target_pairs={{0,8},{1,9},{2,10},{3,11},{4,12},{5,13},{6,14},{7,15},{8,0},{9,1},... | collective-permute-start | bytes 196616 | tf_op jit(solution)/shard_map/ppermute | solution.py:380
  2.2 5.3 %collective-permute-start.1 = (bf16[2,32,512]{2,1,0:T(8,128)(2,1)S(1)}, bf16[2,32,512]{2,1,0:T(8,128)(2,1)S(1)}, u32[]{:S(2)}, u32[]{:S(2)}) collective-permute-start(bf16[2,32,512]{2,1,0:T(8,128)(2,1)S(1)} %get-tuple-element.98), channel_id=1, source_target_pairs={{0,16},{1,17},{2,18},{3,19},{4,20},{5,21},{6,22},{7,23},{8,24},{9,... | collective-permute-start | bytes 196616 | tf_op jit(solution)/shard_map/ppermute | solution.py:380
  4.8 4.0 %collective-permute-start.2 = (bf16[2,32,512]{2,1,0:T(8,128)(2,1)S(1)}, bf16[2,32,512]{2,1,0:T(8,128)(2,1)S(1)}, u32[]{:S(2)}, u32[]{:S(2)}) collective-permute-start(bf16[2,32,512]{2,1,0:T(8,128)(2,1)S(1)} %get-tuple-element.95), channel_id=1, source_target_pairs={{0,24},{1,25},{2,26},{3,27},{4,28},{5,29},{6,30},{7,31},{8,16},{9,... | collective-permute-start | bytes 196616 | tf_op jit(solution)/shard_map/ppermute | solution.py:380
  4.8 5.4 %copy-start = (bf16[2,128,512]{2,1,0:T(8,128)(2,1)S(1)}, bf16[2,128,512]{2,1,0:T(8,128)(2,1)}, u32[]{:S(2)}) copy-start(bf16[2,128,512]{2,1,0:T(8,128)(2,1)} %cot.1) | copy-start | bytes 786436
  4.8 9.9 %copy-start.1 = (f32[31,512]{1,0:T(8,128)S(1)}, f32[31,512]{1,0:T(8,128)}, u32[]{:S(2)}) copy-start(f32[31,512]{1,0:T(8,128)} %kern.3) | copy-start | bytes 190468
  9.4 5.3 %collective-permute-start.3 = (bf16[4,2,16,512]{3,2,1,0:T(8,128)(2,1)S(1)}, bf16[4,2,16,512]{3,2,1,0:T(8,128)(2,1)S(1)}, u32[]{:S(2)}, u32[]{:S(2)}) collective-permute-start(bf16[4,2,16,512]{3,2,1,0:T(8,128)(2,1)S(1)} %get-tuple-element.51), channel_id=1, source_target_pairs={{0,8},{1,9},{2,10},{3,11},{4,12},{5,13},{6,14},{7,15},{8,0},{9,1},... | collective-permute-start | bytes 393224 | tf_op jit(solution)/shard_map/ppermute | solution.py:380
  9.6 5.1 %collective-permute-start.4 = (bf16[4,2,16,512]{3,2,1,0:T(8,128)(2,1)S(1)}, bf16[4,2,16,512]{3,2,1,0:T(8,128)(2,1)S(1)}, u32[]{:S(2)}, u32[]{:S(2)}) collective-permute-start(bf16[4,2,16,512]{3,2,1,0:T(8,128)(2,1)S(1)} %get-tuple-element.52), channel_id=1, source_target_pairs={{8,24},{9,25},{10,26},{11,27},{12,28},{13,29},{14,30},{15,31},{24,... | collective-permute-start | bytes 393224 | tf_op jit(solution)/shard_map/ppermute | solution.py:380
  10.3 6.9 %collective-permute-start.5 = (bf16[2,32,512]{2,1,0:T(8,128)(2,1)S(1)}, bf16[2,32,512]{2,1,0:T(8,128)(2,1)S(1)}, u32[]{:S(2)}, u32[]{:S(2)}) collective-permute-start(bf16[2,32,512]{2,1,0:T(8,128)(2,1)S(1)} %get-tuple-element.93), channel_id=1, source_target_pairs={{0,8},{1,9},{2,10},{3,11},{4,12},{5,13},{6,14},{7,15},{8,0},{9,1},... | collective-permute-start | bytes 196616 | tf_op jit(solution)/shard_map/ppermute | solution.py:380
  13.0 4.3 %collective-permute-start.6 = (bf16[2,32,512]{2,1,0:T(8,128)(2,1)S(1)}, bf16[2,32,512]{2,1,0:T(8,128)(2,1)S(1)}, u32[]{:S(2)}, u32[]{:S(2)}) collective-permute-start(bf16[2,32,512]{2,1,0:T(8,128)(2,1)S(1)} %get-tuple-element.92), channel_id=1, source_target_pairs={{0,16},{1,17},{2,18},{3,19},{4,20},{5,21},{6,22},{7,23},{8,24},{9,... | collective-permute-start | bytes 196616 | tf_op jit(solution)/shard_map/ppermute | solution.py:380
  14.7 4.0 %collective-permute-start.7 = (bf16[2,32,512]{2,1,0:T(8,128)(2,1)S(1)}, bf16[2,32,512]{2,1,0:T(8,128)(2,1)S(1)}, u32[]{:S(2)}, u32[]{:S(2)}) collective-permute-start(bf16[2,32,512]{2,1,0:T(8,128)(2,1)S(1)} %get-tuple-element.91), channel_id=1, source_target_pairs={{0,24},{1,25},{2,26},{3,27},{4,28},{5,29},{6,30},{7,31},{8,16},{9,... | collective-permute-start | bytes 196616 | tf_op jit(solution)/shard_map/ppermute | solution.py:380
  27.1 4.2 %collective-permute-start.19 = (bf16[2048,128]{1,0:T(8,128)(2,1)S(1)}, bf16[2048,128]{1,0:T(8,128)(2,1)S(1)}, u32[]{:S(2)}, u32[]{:S(2)}) collective-permute-start(bf16[2048,128]{1,0:T(8,128)(2,1)S(1)} %get-tuple-element.65), channel_id=1, source_target_pairs={{0,8},{1,9},{2,10},{3,11},{4,12},{5,13},{6,14},{7,15},{8,0},{9,1},... | collective-permute-start | bytes 1572872 | tf_op jit(solution)/shard_map/ppermute | solution.py:380
  27.4 2.1 %collective-permute-start.8 = (bf16[1024,128]{1,0:T(8,128)(2,1)S(1)}, bf16[1024,128]{1,0:T(8,128)(2,1)S(1)}, u32[]{:S(2)}, u32[]{:S(2)}) collective-permute-start(bf16[1024,128]{1,0:T(8,128)(2,1)S(1)} %get-tuple-element.58), channel_id=1, source_target_pairs={{0,8},{1,9},{2,10},{3,11},{4,12},{5,13},{6,14},{7,15},{8,0},{9,1},... | collective-permute-start | bytes 786440 | tf_op jit(solution)/shard_map/ppermute | solution.py:380
  27.7 5.3 %collective-permute-start.10 = (bf16[2176,128]{1,0:T(8,128)(2,1)S(1)}, bf16[2176,128]{1,0:T(8,128)(2,1)S(1)}, u32[]{:S(2)}, u32[]{:S(2)}) collective-permute-start(bf16[2176,128]{1,0:T(8,128)(2,1)S(1)} %get-tuple-element.61), channel_id=1, source_target_pairs={{0,8},{1,9},{2,10},{3,11},{4,12},{5,13},{6,14},{7,15},{8,0},{9,1},... | collective-permute-start | bytes 1671176 | tf_op jit(solution)/shard_map/ppermute | solution.py:380
  29.5 8.4 %collective-permute-start.9 = (bf16[1024,128]{1,0:T(8,128)(2,1)S(1)}, bf16[1024,128]{1,0:T(8,128)(2,1)S(1)}, u32[]{:S(2)}, u32[]{:S(2)}) collective-permute-start(bf16[1024,128]{1,0:T(8,128)(2,1)S(1)} %pad_maximum_fusion.1), channel_id=1, source_target_pairs={{0,16},{1,17},{2,18},{3,19},{4,20},{5,21},{6,22},{7,23},{8,24},{9,... | collective-permute-start | bytes 786440 | tf_op jit(solution)/shard_map/ppermute | solution.py:380
  31.4 10.5 %collective-permute-start.20 = (bf16[1024,128]{1,0:T(8,128)(2,1)S(1)}, bf16[1024,128]{1,0:T(8,128)(2,1)S(1)}, u32[]{:S(2)}, u32[]{:S(2)}) collective-permute-start(bf16[1024,128]{1,0:T(8,128)(2,1)S(1)} %add_convert_fusion.1), channel_id=1, source_target_pairs={{0,2},{1,3},{2,0},{3,1},{4,6},{5,7},{6,4},{7,5},{8,10},{9,11},{10,... | collective-permute-start | bytes 786440 | tf_op jit(solution)/shard_map/ppermute | solution.py:380
  33.1 8.9 %collective-permute-start.11 = (bf16[1088,128]{1,0:T(8,128)(2,1)S(1)}, bf16[1088,128]{1,0:T(8,128)(2,1)S(1)}, u32[]{:S(2)}, u32[]{:S(2)}) collective-permute-start(bf16[1088,128]{1,0:T(8,128)(2,1)S(1)} %add_convert_fusion), channel_id=1, source_target_pairs={{0,1},{1,0},{2,3},{3,2},{4,5},{5,4},{6,7},{7,6},{8,9},{9,8},{10,11... | collective-permute-start | bytes 835592 | tf_op jit(solution)/shard_map/ppermute | solution.py:380
  39.3 25.4 %collective-permute-start.16 = (bf16[128,128]{1,0:T(8,128)(2,1)S(1)}, bf16[128,128]{1,0:T(8,128)(2,1)S(1)}, u32[]{:S(2)}, u32[]{:S(2)}) collective-permute-start(bf16[128,128]{1,0:T(8,128)(2,1)S(1)} %get-tuple-element.62), channel_id=1, source_target_pairs={{0,1},{1,0},{2,3},{3,2},{4,5},{5,4},{6,7},{7,6},{8,9},{9,8},{10,11... | collective-permute-start | bytes 98312 | tf_op jit(solution)/shard_map/ppermute | solution.py:380
  42.0 5.0 %collective-permute-start.21 = (bf16[512,128]{1,0:T(8,128)(2,1)S(1)}, bf16[512,128]{1,0:T(8,128)(2,1)S(1)}, u32[]{:S(2)}, u32[]{:S(2)}) collective-permute-start(bf16[512,128]{1,0:T(8,128)(2,1)S(1)} %add_convert_fusion.3), channel_id=1, source_target_pairs={{0,1},{1,0},{2,3},{3,2},{4,5},{5,4},{6,7},{7,6},{8,9},{9,8},{10,11... | collective-permute-start | bytes 393224 | tf_op jit(solution)/shard_map/ppermute | solution.py:380
  42.1 7.6 %collective-permute-start.12 = (bf16[544,128]{1,0:T(8,128)(2,1)S(1)}, bf16[544,128]{1,0:T(8,128)(2,1)S(1)}, u32[]{:S(2)}, u32[]{:S(2)}) collective-permute-start(bf16[544,128]{1,0:T(8,128)(2,1)S(1)} %add_convert_fusion.2), channel_id=1, source_target_pairs={{0,16},{1,17},{2,18},{3,19},{4,20},{5,21},{6,22},{7,23},{8,24},{9,... | collective-permute-start | bytes 417800 | tf_op jit(solution)/shard_map/ppermute | solution.py:380
  47.0 5.2 %collective-permute-start.22 = (bf16[256,128]{1,0:T(8,128)(2,1)S(1)}, bf16[256,128]{1,0:T(8,128)(2,1)S(1)}, u32[]{:S(2)}, u32[]{:S(2)}) collective-permute-start(bf16[256,128]{1,0:T(8,128)(2,1)S(1)} %add_convert_fusion.9), channel_id=1, source_target_pairs={{0,4},{1,5},{2,6},{3,7},{4,0},{5,1},{6,2},{7,3},{8,12},{9,13},{10,... | collective-permute-start | bytes 196616 | tf_op jit(solution)/shard_map/ppermute | solution.py:380
  49.8 4.4 %collective-permute-start.13 = (bf16[272,128]{1,0:T(8,128)(2,1)S(1)}, bf16[272,128]{1,0:T(8,128)(2,1)S(1)}, u32[]{:S(2)}, u32[]{:S(2)}) collective-permute-start(bf16[272,128]{1,0:T(8,128)(2,1)S(1)} %add_convert_fusion.6), channel_id=1, source_target_pairs={{0,2},{1,3},{2,0},{3,1},{4,6},{5,7},{6,4},{7,5},{8,10},{9,11},{10,... | collective-permute-start | bytes 208904 | tf_op jit(solution)/shard_map/ppermute | solution.py:380
  52.3 4.3 %collective-permute-start.23 = (bf16[256,128]{1,0:T(8,128)(2,1)S(1)}, bf16[256,128]{1,0:T(8,128)(2,1)S(1)}, u32[]{:S(2)}, u32[]{:S(2)}) collective-permute-start(bf16[256,128]{1,0:T(8,128)(2,1)S(1)} %add_convert_fusion.8), channel_id=1, source_target_pairs={{0,16},{1,17},{2,18},{3,19},{4,20},{5,21},{6,22},{7,23},{8,24},{9,... | collective-permute-start | bytes 196616 | tf_op jit(solution)/shard_map/ppermute | solution.py:380
  54.2 6.0 %collective-permute-start.14 = (bf16[272,128]{1,0:T(8,128)(2,1)S(1)}, bf16[272,128]{1,0:T(8,128)(2,1)S(1)}, u32[]{:S(2)}, u32[]{:S(2)}) collective-permute-start(bf16[272,128]{1,0:T(8,128)(2,1)S(1)} %add_convert_fusion.5), channel_id=1, source_target_pairs={{0,4},{1,5},{2,6},{3,7},{4,0},{5,1},{6,2},{7,3},{8,12},{9,13},{10,... | collective-permute-start | bytes 208904 | tf_op jit(solution)/shard_map/ppermute | solution.py:380
  56.7 5.6 %collective-permute-start.24 = (bf16[256,128]{1,0:T(8,128)(2,1)S(1)}, bf16[256,128]{1,0:T(8,128)(2,1)S(1)}, u32[]{:S(2)}, u32[]{:S(2)}) collective-permute-start(bf16[256,128]{1,0:T(8,128)(2,1)S(1)} %add_convert_fusion.7), channel_id=1, source_target_pairs={{0,4},{1,5},{2,6},{3,7},{4,0},{5,1},{6,2},{7,3},{8,12},{9,13},{10,... | collective-permute-start | bytes 196616 | tf_op jit(solution)/shard_map/ppermute | solution.py:380
  60.2 4.4 %collective-permute-start.15 = (bf16[272,128]{1,0:T(8,128)(2,1)S(1)}, bf16[272,128]{1,0:T(8,128)(2,1)S(1)}, u32[]{:S(2)}, u32[]{:S(2)}) collective-permute-start(bf16[272,128]{1,0:T(8,128)(2,1)S(1)} %add_convert_fusion.4), channel_id=1, source_target_pairs={{0,2},{1,3},{2,0},{3,1},{4,6},{5,7},{6,4},{7,5},{8,10},{9,11},{10,... | collective-permute-start | bytes 208904 | tf_op jit(solution)/shard_map/ppermute | solution.py:380
  60.7 1.6 %collective-permute-start.25 = (bf16[128,128]{1,0:T(8,128)(2,1)S(1)}, bf16[128,128]{1,0:T(8,128)(2,1)S(1)}, u32[]{:S(2)}, u32[]{:S(2)}) collective-permute-start(bf16[128,128]{1,0:T(8,128)(2,1)S(1)} %get-tuple-element.67), channel_id=1, source_target_pairs={{1,2},{3,4},{5,6},{9,10},{11,12},{13,14},{17,18},{19,20},{21,22},{... | collective-permute-start | bytes 98312 | tf_op jit(solution)/shard_map/ppermute | solution.py:380
  64.6 5.1 %collective-permute-start.17 = (bf16[544,128]{1,0:T(8,128)(2,1)S(1)}, bf16[544,128]{1,0:T(8,128)(2,1)S(1)}, u32[]{:S(2)}, u32[]{:S(2)}) collective-permute-start(bf16[544,128]{1,0:T(8,128)(2,1)S(1)} %pad_maximum_fusion.2), channel_id=1, source_target_pairs={{0,16},{1,17},{2,18},{3,19},{4,20},{5,21},{6,22},{7,23},{8,24},{9,... | collective-permute-start | bytes 417800 | tf_op jit(solution)/shard_map/ppermute | solution.py:380
  64.8 9.5 %collective-permute-start.26 = (bf16[512,128]{1,0:T(8,128)(2,1)S(1)}, bf16[512,128]{1,0:T(8,128)(2,1)S(1)}, u32[]{:S(2)}, u32[]{:S(2)}) collective-permute-start(bf16[512,128]{1,0:T(8,128)(2,1)S(1)} %pad_maximum_fusion.3), channel_id=1, source_target_pairs={{0,1},{1,0},{2,3},{3,2},{4,5},{5,4},{6,7},{7,6},{8,9},{9,8},{10,11... | collective-permute-start | bytes 393224 | tf_op jit(solution)/shard_map/ppermute | solution.py:380
  69.8 8.0 %collective-permute-start.28 = (bf16[1088,128]{1,0:T(8,128)(2,1)S(1)}, bf16[1088,128]{1,0:T(8,128)(2,1)S(1)}, u32[]{:S(2)}, u32[]{:S(2)}) collective-permute-start(bf16[1088,128]{1,0:T(8,128)(2,1)S(1)} %constant_dynamic-update-slice_fusion.refs_0_.refs_2_), channel_id=1, source_target_pairs={{0,8},{1,9},{2,10},{3,11},{4,12},{5,13},{6,14},{7,15},{8,0},{9,1},... | collective-permute-start | bytes 835592 | tf_op jit(solution)/shard_map/ppermute | solution.py:380
  69.9 13.3 %collective-permute-start.18 = (bf16[1088,128]{1,0:T(8,128)(2,1)S(1)}, bf16[1088,128]{1,0:T(8,128)(2,1)S(1)}, u32[]{:S(2)}, u32[]{:S(2)}) collective-permute-start(bf16[1088,128]{1,0:T(8,128)(2,1)S(1)} %constant_dynamic-update-slice_fusion.refs_0_.refs_2_), channel_id=1, source_target_pairs={{0,1},{1,0},{2,3},{3,2},{4,5},{5,4},{6,7},{7,6},{8,9},{9,8},{10,11... | collective-permute-start | bytes 835592 | tf_op jit(solution)/shard_map/ppermute | solution.py:380
  74.3 3.4 %collective-permute-start.29 = (bf16[1024,128]{1,0:T(8,128)(2,1)S(1)}, bf16[1024,128]{1,0:T(8,128)(2,1)S(1)}, u32[]{:S(2)}, u32[]{:S(2)}) collective-permute-start(bf16[1024,128]{1,0:T(8,128)(2,1)S(1)} %constant_dynamic-update-slice_fusion.2.refs_1_), channel_id=1, source_target_pairs={{0,8},{1,9},{2,10},{3,11},{4,12},{5,13},{6,14},{7,15},{8,0},{9,1},... | collective-permute-start | bytes 786440 | tf_op jit(solution)/shard_map/ppermute | solution.py:380
  74.6 8.6 %collective-permute-start.27 = (bf16[1024,128]{1,0:T(8,128)(2,1)S(1)}, bf16[1024,128]{1,0:T(8,128)(2,1)S(1)}, u32[]{:S(2)}, u32[]{:S(2)}) collective-permute-start(bf16[1024,128]{1,0:T(8,128)(2,1)S(1)} %constant_dynamic-update-slice_fusion.2.refs_1_), channel_id=1, source_target_pairs={{0,2},{1,3},{2,0},{3,1},{4,6},{5,7},{6,4},{7,5},{8,10},{9,11},{10,... | collective-permute-start | bytes 786440 | tf_op jit(solution)/shard_map/ppermute | solution.py:380
  83.1 2.1 %collective-permute-start.30 = (bf16[1088,128]{1,0:T(8,128)(2,1)S(1)}, bf16[1088,128]{1,0:T(8,128)(2,1)S(1)}, u32[]{:S(2)}, u32[]{:S(2)}) collective-permute-start(bf16[1088,128]{1,0:T(8,128)(2,1)S(1)} %collective-permute-done.18.refs_0_.refs_3_), channel_id=1, source_target_pairs={{0,8},{1,9},{2,10},{3,11},{4,12},{5,13},{6,14},{7,15},{8,0},{9,1},... | collective-permute-start | bytes 835592 | tf_op jit(solution)/shard_map/ppermute | solution.py:380
  83.1 2.1 %collective-permute-start.31 = (bf16[1024,128]{1,0:T(8,128)(2,1)S(1)}, bf16[1024,128]{1,0:T(8,128)(2,1)S(1)}, u32[]{:S(2)}, u32[]{:S(2)}) collective-permute-start(bf16[1024,128]{1,0:T(8,128)(2,1)S(1)} %collective-permute-done.27.refs_1_), channel_id=1, source_target_pairs={{0,8},{1,9},{2,10},{3,11},{4,12},{5,13},{6,14},{7,15},{8,0},{9,1},... | collective-permute-start | bytes 786440 | tf_op jit(solution)/shard_map/ppermute | solution.py:380

commit v14 on v13

--- a/solution.py
+++ b/solution.py
@@ -48,9 +48,9 @@
     return 0.5 * jnp.tanh(0.5 * v) + 0.5
 
 
-def edge_kernel(sub, bits, f0, f1, f2, f3, near, side):
+def edge_kernel(sub, bits, f0, pair, f2, f3, near, side):
     odd = bits[ODD]
-    for d, f in enumerate((f0, f1, f2, f3)):
+    for d, f in enumerate((f0, pair.at[0], f2, f3)):
         last = sub - HALO
         near[d] = f[:, pl.ds(pl.multiple_of((1 - odd) * last, HALO), HALO), :]
         side[d] = f[:, pl.ds(pl.multiple_of(odd * last, HALO), HALO), :]
@@ -70,11 +70,11 @@
     )
 
 
-def conv_kernel(plan, bits, f0, f1, f2, f3, near, side, kern, frames, conv_out, acted_out):
+def conv_kernel(plan, bits, f0, pair, f2, f3, near, side, kern, frames, conv_out, acted_out):
     groups, count, sub, width = plan
     mics = groups * count
     cuts = sub // HALO
-    for d, f in enumerate((f0, f1, f2, f3)):
+    for d, f in enumerate((f0, pair.at[0], f2, f3)):
         frames[d] = f[...]
 
     def conv_step(n, _):
@@ -94,9 +94,9 @@
 
 
 def main_kernel(
-    plan, bits, frames, conv_in, acted_in, c0, c1, c2, c3, near, side, weights,
+    plan, bits, frames, conv_in, acted_in, c0, pair, c2, c3, near, side, weights,
     a_keep, b_keep, a_send, b_send, back_keep, back_send,
-    left_s, right_s, q_s, k_s, v_s, u_s, dconv_s, tap_s,
+    left_s, turned_s, right_s, q_s, k_s, v_s, u_s, dconv_s, tap_s,
 ):
     groups, count, sub, width, factor = plan
     mics = groups * count
@@ -107,7 +107,7 @@
 
     wq, wk, wv, wo = (weights.at[i] for i in range(4))
     left_s[0] = acted_in[...]
-    for d, cot in enumerate((c0, c1, c2, c3)):
+    for d, cot in enumerate((c0, pair.at[1], c2, c3)):
         for m in range(count):
             for c in range(cuts):
                 right_s[3, c, d, m] = cot[m, c * HALO : (c + 1) * HALO, :]
@@ -123,6 +123,7 @@
     k_s[...] = mm(acted, wk[...]).astype(BF)
     v_s[...] = mm(acted, wv[...]).astype(BF)
     u_s[...] = mm(flat(3), wo[...], NT).astype(BF)
+    turned_s[0] = acted.T
 
     depth = width // HEADS
     per = LANES // depth
@@ -168,6 +169,7 @@
             put(1, c, lanes, pick(mm(ib, q, TN)))
             put(2, c, lanes, pick(mm(wb, u, TN)))
 
+    turned_s[1] = left_s[1].T
     dacted = mm(flat(0), wq[...], NT) + mm(flat(1), wk[...], NT) + mm(flat(2), wv[...], NT)
     conv = conv_in[...]
     sig = sigmoid(conv)
@@ -211,7 +213,7 @@
         i = owner * 2 + h
         span = size + HALO * (1 - h)
         first, second, third = ways(bits, h)
-        grad = mm(left_s[i // 3], flat(i), TN).astype(BF)
+        grad = mm(turned_s[i // 3], flat(i)).astype(BF)
         for piece in range(8):
             cb, at = piece * size // width, piece * size % width
             rel = ((piece // 4) ^ first) * 4 + ((piece // 2 % 2) ^ second) * 2 + ((piece % 2) ^ third)
@@ -256,15 +258,6 @@
     got, refs = refs[: len(kinds)], refs[len(kinds) :]
     if with_taps:
         tap_refs, refs, tap_grad, tap_s = refs[:4], refs[4:-4] + refs[-3:-1], refs[-4], refs[-1]
-        for n, ref in enumerate(tap_refs):
-            owner = core if n < 2 else 1 - core
-            for rel in range(4):
-                at = rel * span + size
-                tap_s[owner * 8 + piece_of(0, n % 2, rel)] = ref[at : at + HALO, :].astype(F32) * norm
-        for g in range(16):
-            lc, j = g // 4, g % 4 * 8
-            kept = min(8, 31 - j)
-            tap_grad[j : j + kept, lc * LANES : (lc + 1) * LANES] = tap_s[g, 0:kept]
     *outs, piece_s, sems = refs if first_call else refs[4:]
     copies = []
     for n, (own, h, far) in enumerate(kinds):
@@ -283,15 +276,24 @@
                 )
                 copies.append((owner == which, copy))
                 pl.when(owner == which)(copy.start)
+    if with_taps:
+        for n, ref in enumerate(tap_refs):
+            owner = core if n < 2 else 1 - core
+            for rel in range(4):
+                at = rel * span + size
+                tap_s[owner * 8 + piece_of(0, n % 2, rel)] = ref[at : at + HALO, :].astype(F32) * norm
+        for g in range(16):
+            lc, j = g // 4, g % 4 * 8
+            kept = min(8, 31 - j)
+            tap_grad[j : j + kept, lc * LANES : (lc + 1) * LANES] = tap_s[g, 0:kept]
     for here, copy in copies:
         pl.when(here)(copy.wait)
 
 
-def home_kernel(plan, bits, own, core_got, y_got, layer_out, dconv, x_edge, z_edge):
+def home_kernel(plan, bits, own, core_got, y_got, layer_out, dconv, first_edge, last_edge):
     count, sub, cols = plan
     unit = 2 * count * cols * sub
-    odd = bits[X]
-    last = 3 * sub + sub - HALO
+    last = 4 * sub - HALO
     for d, (ref, base) in enumerate(
         ((own, 0), (core_got, 0), (y_got, 0), (y_got, unit))
     ):
@@ -305,22 +307,23 @@
     for m in range(count):
         for lc in range(cols):
             at = (m * cols + lc) * HALO
-            x_rows = pl.ds(pl.multiple_of((1 - odd) * last, HALO), HALO)
-            z_rows = pl.ds(pl.multiple_of(odd * last, HALO), HALO)
-            x_edge[at : at + HALO, :] = dconv[m, lc, x_rows, :]
-            z_edge[at : at + HALO, :] = dconv[m, lc, z_rows, :]
-
-
-def frame_kernel(plan, bits, dconv, x_got, z_got, cot, kern, frame_grad):
-    count, cols, x_at, length = plan
+            first_edge[at : at + HALO, :] = dconv[m, lc, :HALO, :]
+            last_edge[at : at + HALO, :] = dconv[m, lc, last:, :]
+
+
+def frame_kernel(plan, bits, dconv, x_got, z_got, other_got, cot, kern, frame_grad):
+    count, cols, length = plan
     is_odd = jnp.broadcast_to(bits[X], (HALO, LANES)) == 1
+    by_z = jnp.broadcast_to(bits[X] ^ bits[Z], (HALO, LANES)) == 1
 
     def step(m, _):
         for lc in range(cols):
             lanes = slice(lc * LANES, (lc + 1) * LANES)
-            at = pl.multiple_of((m * cols + lc) * HALO, HALO)
-            one = x_got[pl.ds(pl.multiple_of(x_at + at, HALO), HALO), :].astype(F32)
-            two = z_got[pl.ds(at, HALO), :].astype(F32)
+            at = (m * cols + lc) * HALO
+            rows = pl.ds(pl.multiple_of(at, HALO), HALO)
+            x_rows = pl.ds(pl.multiple_of(bits[X] * count * cols * HALO + at, HALO), HALO)
+            one = x_got[x_rows, :].astype(F32)
+            two = jnp.where(by_z, z_got[rows, :].astype(F32), other_got[rows, :].astype(F32))
             x = jnp.concatenate(
                 [
                     jnp.where(is_odd, one, two),
@@ -387,17 +390,16 @@
 
     masks = (0, over_core, over_y, over_core + over_y)
 
-    def scattered(x):
-        parts = [
-            lax.dynamic_slice_in_dim(x, order(mic ^ d) * sub, sub, axis=1) for d in range(4)
-        ]
-        got = {d: swap(parts[d], masks[d]) for d in (2, 3, 1)}
-        return [parts[0], got[1], got[2], got[3]]
-
-    f, c = scattered(frames), scattered(cotangent)
+    def sub_block(x, d):
+        return lax.dynamic_slice_in_dim(x, order(mic ^ d) * sub, sub, axis=1)
+
+    f, c = [[sub_block(x, d) for d in range(4)] for x in (frames, cotangent)]
+    f[2], f[3] = (swap(f[d], masks[d]) for d in (2, 3))
+    near_pair = swap(jnp.stack([f[1], c[1]]), masks[1])
+    c[2], c[3] = (swap(c[d], masks[d]) for d in (2, 3))
     weights = jnp.stack([w_query, w_key, w_value, w_out])
     edge = shape((groups, count, HALO, width), BF)
-    near, side = call(functools.partial(edge_kernel, sub), (edge, edge), [], 8, bits, *f)
+    near, side = call(functools.partial(edge_kernel, sub), (edge, edge), [], 8, bits, f[0], near_pair, f[2], f[3])
     near, side, weights = lax.optimization_barrier((near, side, weights))
     near = swap(near, over_core)
     side = permute(
@@ -421,18 +423,19 @@
     placed, conv, acted = call(
         functools.partial(conv_kernel, (groups, count, sub, width)),
         (moved, shape((rows, width), F32), shape((rows, width), BF)),
-        [], 8, bits, *f, near, side, kernel,
+        [], 8, bits, f[0], near_pair, f[2], f[3], near, side, kernel,
     )
     a_keep, b_keep, a_send, b_send, back_keep, back_send = call(
         functools.partial(main_kernel, (groups, count, sub, width, factor)),
         (flat(8 * span), flat(8 * size)) * 2 + (flat(2 * unit),) * 2,
         [
             pltpu.VMEM((2, rows, width), BF),
+            pltpu.VMEM((2, width, rows), BF),
             pltpu.VMEM((4, cuts, groups, count, HALO, width), BF),
             big, big, big, big, wide,
             pltpu.VMEM((32 * cols + HALO, LANES), F32),
         ],
-        24, bits, placed, conv, acted, *c, near, side, weights,
+        24, bits, placed, conv, acted, c[0], near_pair, c[2], c[3], near, side, weights,
     )
 
     lines = [2**i for i in range(1, blocks.bit_length() - 1)]
@@ -459,28 +462,32 @@
     a = halved(a, over_x)
     b = halved(b, lines[0])
     y_got = swap(jnp.concatenate([back_keep[unit:], core_got[unit:]]), over_y)
+    y_got = after(y_got, (a[-1], b[-1]))
     edge = flat(count * cols * HALO)
-    layer_out, dconv, x_edge, z_edge = call(
+    layer_out, dconv, *edges = call(
         functools.partial(home_kernel, (count, sub, cols)),
         (shape(frames.shape, BF), shape((count, cols, length, LANES), BF), edge, edge),
         [], 8, bits, back_keep, core_got, y_got,
     )
+    x_got = swap(jnp.concatenate(edges), over_x)
+    n_edge = edge.shape[0]
+    passed = lax.dynamic_slice_in_dim(x_got, (1 - tm % 2) * n_edge, n_edge, axis=0)
     a = halved(a, over_y)
     b = halved(b, over_x)
-    a = halved(a, lines[0])
+    got = swap(jnp.concatenate([total(*(t[span:] for t in a)), passed]), lines[0])
+    a, z_got = [t[:span] for t in a] + [got[:span]], got[span:]
     b = halved(b, lines[1])
     a = exchanged(a, lines[1:])
     b = exchanged(b, [over_y] + lines[2:])
-    x_got = swap(x_edge, over_x)
-    z_got = permute(
-        after(z_edge, a),
-        both([(m * blocks + t, m * blocks + t + 1)
-              for m in range(groups) for t in range(1, blocks - 1, 2)]),
+    other_got = permute(
+        after(passed, a),
+        both([(m * blocks + t, m * blocks + t + 2)
+              for m in range(groups) for t in range(2, blocks - 2) if t // 2 % 2]),
     )
     a = doubled(a, lines[0])
     b = doubled(b, lines[1])
-    a = doubled(after(a, x_got), over_y)
-    b = doubled(after(b, z_got), over_x)
+    a = doubled(a, over_y)
+    b = doubled(after(b, other_got), over_x)
 
     norm = 1.0 / math.sqrt(groups * count * blocks * length)
     square = shape((width, width), F32)
@@ -502,9 +509,9 @@
     a_far, b_far = swap(a, over_x), swap(b, lines[0])
     a_other, b_other = swap(a, over_core), swap(b, over_core)
     (frame_grad,) = call(
-        functools.partial(frame_kernel, (count, cols, 0, length)),
+        functools.partial(frame_kernel, (count, cols, length)),
         (shape(frames.shape, BF),), [], 8,
-        bits, after(dconv, a), x_got, z_got, cotangent, kernel,
+        bits, after(dconv, a), x_got, z_got, other_got, cotangent, kernel,
     )
     grads = final(((1, 0, 0), (1, 1, 0), (0, 0, 0), (0, 1, 0)), (a, b, a_other, b_other), ())
     a_far, b_far, frame_grad, *grads = lax.optimization_barrier(

time: 87.7 us -> 89.7 us (1.023)
  starting transfers between devices: 37.9 us -> 34.2 us
  other arithmetic: 2.35 us -> 5.8 us
  waiting for transfers between devices: 23.6 us -> 24.8 us
  local copies, waits for them, and re-layouts: 1.17 us -> 2.1 us
    ppermute x32 -> x31, starting transfers between devices: 37.9 us -> 34.2 us  [permute(): return lax.ppermute(x, ('mic', 'tm'), pairs)]
    convert_element_type x10, other arithmetic: 0.48 us -> 3.2 us  [total(): functools.reduce(lambda x, y: x + y, [x.astype(F32) for x in parts])]
    ppermute x32 -> x31, waiting for transfers between devices: 23.6 us -> 24.8 us  [permute(): return lax.ppermute(x, ('mic', 'tm'), pairs)]
    dynamic_slice x2 -> x3, local copies, waits for them, and re-layouts: 1 us -> 1.95 us  [the longest x2 1.94 us: sub_block(): return lax.dynamic_slice_in_dim(x, order(mic ^ d) * sub, sub, axis=1)]
  transfers between devices with their start and end apart: 32 -> 31, of which waited for: 14 -> 16; matrix products, arithmetic and copies ran while one was open for 3% -> 7% of each run, Pallas kernels for 12% -> 11%
where the time goes in v14:
time: 89.7 us; the launch traced here: 89.3 us
  starting transfers between devices  34.2 us (38%)
  waiting for transfers between devices  24.8 us (28%)
  Pallas kernels  21.3 us (24%)
  other arithmetic  5.8 us (6%)
  local copies, waits for them, and re-layouts  2.1 us (2%)
  between operations  1.07 us (1%)
    ppermute x31, starting transfers between devices, permute(): return lax.ppermute(x, ('mic', 'tm'), pairs)  34.2 us
    ppermute x31, waiting for transfers between devices, permute(): return lax.ppermute(x, ('mic', 'tm'), pairs)  24.8 us
    pallas_call x8, Pallas kernels, call(): pl.pallas_call(body, out_shape=outs, in_specs=[pl.BlockSpec(memory_space=...  21.3 us
    convert_element_type x10, other arithmetic, total(): functools.reduce(lambda x, y: x + y, [x.astype(F32) for x in parts])  3.2 us
    dynamic_slice x2, local copies, waits for them, and re-layouts, sub_block(): return lax.dynamic_slice_in_dim(x, order(mic ^ d) * sub, sub, axis=1)  1.94 us
    another operation x1, other arithmetic, shards(): weights = jnp.stack([w_query, w_key, w_value, w_out])  1.81 us
  transfers between devices with their start and end apart: 31, of which 16 were waited for; matrix products, arithmetic and copies ran while one was open for 7% of the time, Pallas kernels for 11%

profile of v14, /device:TPU:0, one launch (start us, length us, event | category | flops | bytes accessed | tf_op | source)
XLA Modules:
  0.0 89.3 jit_solution(15354635922707606611)
XLA Ops:
  0.7 1.0 %constant_dynamic-slice_fusion.1 = (bf16[2,32,512]{2,1,0:T(8,128)(2,1)S(1)}, bf16[2,32,512]{2,1,0:T(8,128)(2,1)S(1)}, bf16[2,32,512]{2,1,0:T(8,128)(2,1)S(1)}, bf16[1,2,32,512]{3,2,1,0:T(8,128)(2,1)S(1)}) fusion(bf16[2,128,512]{2,1,0:T(8,128)(2,1)} %cot.1, s32[]{:T(128)S(6)} %select_n.100, s32[]{:T(128)S(6)} %select_n.99, s32[]{:T(128)S(6)} %select_n.97, ...), kind=kLoop, calls=%fused_computation.23 | loop fusion | bytes 524304 | tf_op jit(solution)/shard_map/dynamic_slice | solution.py:394
  1.7 1.0 %constant_dynamic-slice_fusion.4 = (bf16[2,32,512]{2,1,0:T(8,128)(2,1)S(1)}, bf16[1,2,32,512]{3,2,1,0:T(8,128)(2,1)S(1)}, bf16[2,32,512]{2,1,0:T(8,128)(2,1)S(1)}, bf16[2,32,512]{2,1,0:T(8,128)(2,1)S(1)}) fusion(bf16[2,128,512]{2,1,0:T(8,128)(2,1)} %param.7, s32[]{:T(128)S(6)} %select_n.100, s32[]{:T(128)S(6)} %select_n.98, s32[]{:T(128)S(6)} %select_n.97, ...), kind=kLoop, calls=%fused_computation.26 | loop fusion | bytes 524304 | tf_op jit(solution)/shard_map/dynamic_slice | solution.py:394
  2.7 0.5 collective-permute-start
  3.2 2.6 %collective-permute-start.1 = (bf16[2,32,512]{2,1,0:T(8,128)(2,1)S(1)}, bf16[2,32,512]{2,1,0:T(8,128)(2,1)S(1)}, u32[]{:S(2)}, u32[]{:S(2)}) collective-permute-start(bf16[2,32,512]{2,1,0:T(8,128)(2,1)S(1)} %get-tuple-element.98), channel_id=1, source_target_pairs={{0,16},{1,17},{2,18},{3,19},{4,20},{5,21},{6,22},{7,23},{8,24},{9,... | collective-permute-start | bytes 196616 | tf_op jit(solution)/shard_map/ppermute | solution.py:383
  5.8 1.8 %pad_maximum_fusion.weights = bf16[4,512,512]{2,1,0:T(8,128)(2,1)S(1)} fusion(bf16[1,512,512]{2,1,0:T(8,128)(2,1)} %bitcast.19, bf16[1,512,512]{2,1,0:T(8,128)(2,1)} %bitcast.20, bf16[1,512,512]{2,1,0:T(8,128)(2,1)} %bitcast.21, bf16[1,512,512]{2,1,0:T(8,128)(2,1)} %bitcast.22), kind=kLoop, calls=%fused_computation | loop fusion | flops 3145728 | bytes 4194304 | tf_op jit(solution)/shard_map/stack | solution.py:400
  7.9 0.6 collective-permute-done.1.f2
  8.5 1.4 %collective-permute-done.2.f3 = bf16[2,32,512]{2,1,0:T(8,128)(2,1)S(1)} collective-permute-done((bf16[2,32,512]{2,1,0:T(8,128)(2,1)S(1)}, bf16[2,32,512]{2,1,0:T(8,128)(2,1)S(1)}, u32[]{:S(2)}, u32[]{:S(2)}) %collective-permute-start.2) | collective-permute-done | bytes 65568 | tf_op jit(solution)/shard_map/ppermute | solution.py:383
  9.8 0.6 shard_map.126
  10.6 0.7 collective-permute-start.4
  11.3 4.2 %collective-permute-start.5 = (bf16[2,32,512]{2,1,0:T(8,128)(2,1)S(1)}, bf16[2,32,512]{2,1,0:T(8,128)(2,1)S(1)}, u32[]{:S(2)}, u32[]{:S(2)}) collective-permute-start(bf16[2,32,512]{2,1,0:T(8,128)(2,1)S(1)} %get-tuple-element.92), channel_id=1, source_target_pairs={{0,16},{1,17},{2,18},{3,19},{4,20},{5,21},{6,22},{7,23},{8,24},{9,... | collective-permute-start | bytes 196616 | tf_op jit(solution)/shard_map/ppermute | solution.py:383
  15.6 2.5 %shard_map.127 = (bf16[4,2,32,512]{3,2,1,0:T(8,128)(2,1)S(1)}, f32[256,512]{1,0:T(8,128)S(1)}, bf16[256,512]{1,0:T(8,128)(2,1)S(1)}) custom-call(s32[11]{0:T(128)S(1)} %stack.71.bits, bf16[2,32,512]{2,1,0:T(8,128)(2,1)S(1)} %get-tuple-element.97.f0, bf16[2,2,32,512]{3,2,1,0:T(8,128)(2,1)S(1)} %collective-permute-done.pair, ...), custom_call_target="tpu_custom_call" | custom-call | tf_op jit(solution)/shard_map/pallas_call | solution.py:344
  18.3 1.4 %collective-permute-done.6.c3 = bf16[2,32,512]{2,1,0:T(8,128)(2,1)S(1)} collective-permute-done((bf16[2,32,512]{2,1,0:T(8,128)(2,1)S(1)}, bf16[2,32,512]{2,1,0:T(8,128)(2,1)S(1)}, u32[]{:S(2)}, u32[]{:S(2)}) %collective-permute-start.6) | collective-permute-done | bytes 65568 | tf_op jit(solution)/shard_map/ppermute | solution.py:383
  19.7 8.4 %shard_map.128 = (bf16[2176,128]{1,0:T(8,128)(2,1)S(1)}, bf16[2048,128]{1,0:T(8,128)(2,1)S(1)}, bf16[2176,128]{1,0:T(8,128)(2,1)S(1)}, bf16[2048,128]{1,0:T(8,12...) custom-call(s32[11]{0:T(128)S(1)} %stack.71.bits, ...), custom_call_target="tpu_custom_call" | custom-call | tf_op jit(solution)/shard_map/pallas_call | solution.py:344
  28.7 1.7 %collective-permute-done.7.core_got = bf16[1024,128]{1,0:T(8,128)(2,1)S(1)} collective-permute-done((bf16[1024,128]{1,0:T(8,128)(2,1)S(1)}, bf16[1024,128]{1,0:T(8,128)(2,1)S(1)}, u32[]{:S(2)}, u32[]{:S(2)}) %collective-permute-start.7) | collective-permute-done | bytes 262176 | tf_op jit(solution)/shard_map/ppermute | solution.py:383
  30.5 2.8 %collective-permute-start.10 = (bf16[1088,128]{1,0:T(8,128)(2,1)S(1)}, bf16[1088,128]{1,0:T(8,128)(2,1)S(1)}, u32[]{:S(2)}, u32[]{:S(2)}) collective-permute-start(bf16[1088,128]{1,0:T(8,128)(2,1)S(1)} %add_convert_fusion), channel_id=1, source_target_pairs={{0,1},{1,0},{2,3},{3,2},{4,5},{5,4},{6,7},{7,6},{8,9},{9,8},{10,11... | collective-permute-start | bytes 835592 | tf_op jit(solution)/shard_map/ppermute | solution.py:383
  33.3 0.7 pad_maximum_fusion.2
  34.0 0.6 collective-permute-start.8
  34.7 1.6 %collective-permute-start.12 = (bf16[1024,128]{1,0:T(8,128)(2,1)S(1)}, bf16[1024,128]{1,0:T(8,128)(2,1)}, u32[]{:S(2)}, u32[]{:S(2)}) collective-permute-start(bf16[1024,128]{1,0:T(8,128)(2,1)S(1)} %add_convert_fusion.1), channel_id=1, source_target_pairs={{0,2},{1,3},{2,0},{3,1},{4,6},{5,7},{6,4},{7,5},{8,10},{9,11},{10,... | collective-permute-start | bytes 786440 | tf_op jit(solution)/shard_map/ppermute | solution.py:383
  36.3 4.0 %collective-permute-done.10 = bf16[1088,128]{1,0:T(8,128)(2,1)S(1)} collective-permute-done((bf16[1088,128]{1,0:T(8,128)(2,1)S(1)}, bf16[1088,128]{1,0:T(8,128)(2,1)S(1)}, u32[]{:S(2)}, u32[]{:S(2)}) %collective-permute-start.10) | collective-permute-done | bytes 278560 | tf_op jit(solution)/shard_map/ppermute | solution.py:383
  40.3 0.9 collective-permute-start.13
  41.2 1.1 %collective-permute-done.8.y_got = bf16[1024,128]{1,0:T(8,128)(2,1)S(1)} collective-permute-done((bf16[1024,128]{1,0:T(8,128)(2,1)}, bf16[1024,128]{1,0:T(8,128)(2,1)S(1)}, u32[]{:S(2)}, u32[]{:S(2)}) %collective-permute-start.8) | collective-permute-done | bytes 262176 | tf_op jit(solution)/shard_map/ppermute | solution.py:383
  42.6 1.3 %shard_map.129 = (bf16[2,128,512]{2,1,0:T(8,128)(2,1)}, bf16[2,4,128,128]{3,2,1,0:T(8,128)(2,1)S(1)}, bf16[128,128]{1,0:T(8,128)(2,1)S(1)}, bf16[128,128]{1,0:T(8,128)(2,1)S(1)}) custom-call(s32[11]{0:T(128)S(1)} %stack.71.bits, bf16[1024,128]{1,0:T(8,128)(2,1)S(1)} %get-tuple-element.57.own, bf16[1024,128]{1,0:T(8,128)(2,1)S(1)} %collective-permute-done.7.core_got, ...), custom_call_target="tpu_custom_call" | custom-call | tf_op jit(solution)/shard_map/pallas_call | solution.py:344
  44.0 0.6 collective-permute-start.14
  44.6 1.0 %add_convert_fusion.3 = bf16[512,128]{1,0:T(8,128)(2,1)S(1)} fusion(bf16[1024,128]{1,0:T(8,128)(2,1)} %collective-permute-done.12, bf16[2048,128]{1,0:T(8,128)(2,1)S(1)} %collective-permute-done.11, bf16[2048,128]{1,0:T(8,128)(2,1)} %copy-done.1), kind=kLoop, calls=%fused_computation.6 | loop fusion | flops 393216 | bytes 524288 | tf_op jit(solution)/shard_map/convert_element_type | solution.py:244
  45.6 1.6 %collective-permute-start.20 = (bf16[512,128]{1,0:T(8,128)(2,1)S(1)}, bf16[512,128]{1,0:T(8,128)(2,1)S(1)}, u32[]{:S(2)}, u32[]{:S(2)}) collective-permute-start(bf16[512,128]{1,0:T(8,128)(2,1)S(1)} %add_convert_fusion.3), channel_id=1, source_target_pairs={{0,1},{1,0},{2,3},{3,2},{4,5},{5,4},{6,7},{7,6},{8,9},{9,8},{10,11... | collective-permute-start | bytes 393224 | tf_op jit(solution)/shard_map/ppermute | solution.py:383
  47.1 1.8 %collective-permute-done.14.x_got = bf16[256,128]{1,0:T(8,128)(2,1)S(1)} collective-permute-done((bf16[256,128]{1,0:T(8,128)(2,1)S(1)}, bf16[256,128]{1,0:T(8,128)(2,1)S(1)}, u32[]{:S(2)}, u32[]{:S(2)}) %collective-permute-start.14) | collective-permute-done | bytes 65568 | tf_op jit(solution)/shard_map/ppermute | solution.py:383
  49.0 1.6 %collective-permute-start.15 = (bf16[400,128]{1,0:T(8,128)(2,1)S(1)}, bf16[400,128]{1,0:T(8,128)(2,1)S(1)}, u32[]{:S(2)}, u32[]{:S(2)}) collective-permute-start(bf16[400,128]{1,0:T(8,128)(2,1)S(1)} %pad_maximum_fusion.6), channel_id=1, source_target_pairs={{0,2},{1,3},{2,0},{3,1},{4,6},{5,7},{6,4},{7,5},{8,10},{9,11},{10,... | collective-permute-start | bytes 307208 | tf_op jit(solution)/shard_map/ppermute | solution.py:383
  50.6 0.9 %add_convert_fusion.9 = bf16[256,128]{1,0:T(8,128)(2,1)S(1)} fusion(bf16[512,128]{1,0:T(8,128)(2,1)S(1)} %collective-permute-done.20, bf16[1024,128]{1,0:T(8,128)(2,1)} %collective-permute-done.12, bf16[2048,128]{1,0:T(8,128)(2,1)S(1)} %collective-permute-done.11, bf16[2048,128]{1,0:T(8,128)(2,1)} %copy-done.1), kind=kLoop, calls=%fused_computation.15 | loop fusion | flops 262144 | bytes 327680 | tf_op jit(solution)/shard_map/convert_element_type | solution.py:244
  51.5 2.6 %collective-permute-start.21 = (bf16[256,128]{1,0:T(8,128)(2,1)S(1)}, bf16[256,128]{1,0:T(8,128)(2,1)S(1)}, u32[]{:S(2)}, u32[]{:S(2)}) collective-permute-start(bf16[256,128]{1,0:T(8,128)(2,1)S(1)} %add_convert_fusion.9), channel_id=1, source_target_pairs={{0,4},{1,5},{2,6},{3,7},{4,0},{5,1},{6,2},{7,3},{8,12},{9,13},{10,... | collective-permute-start | bytes 196616 | tf_op jit(solution)/shard_map/ppermute | solution.py:383
  54.5 2.3 %collective-permute-start.16 = (bf16[272,128]{1,0:T(8,128)(2,1)S(1)}, bf16[272,128]{1,0:T(8,128)(2,1)S(1)}, u32[]{:S(2)}, u32[]{:S(2)}) collective-permute-start(bf16[272,128]{1,0:T(8,128)(2,1)S(1)} %add_convert_fusion.5), channel_id=1, source_target_pairs={{0,4},{1,5},{2,6},{3,7},{4,0},{5,1},{6,2},{7,3},{8,12},{9,13},{10,... | collective-permute-start | bytes 208904 | tf_op jit(solution)/shard_map/ppermute | solution.py:383
  56.8 1.8 %collective-permute-done.21 = bf16[256,128]{1,0:T(8,128)(2,1)S(1)} collective-permute-done((bf16[256,128]{1,0:T(8,128)(2,1)S(1)}, bf16[256,128]{1,0:T(8,128)(2,1)S(1)}, u32[]{:S(2)}, u32[]{:S(2)}) %collective-permute-start.21) | collective-permute-done | bytes 65568 | tf_op jit(solution)/shard_map/ppermute | solution.py:383
  58.6 0.9 %add_convert_fusion.8 = bf16[256,128]{1,0:T(8,128)(2,1)S(1)} fusion(bf16[256,128]{1,0:T(8,128)(2,1)S(1)} %collective-permute-done.21, bf16[512,128]{1,0:T(8,128)(2,1)S(1)} %collective-permute-done.20, bf16[1024,128]{1,0:T(8,128)(2,1)} %collective-permute-done.12, bf16[2048,128]{1,0:T(8,128)(2,1)S(1)} %collective-permute-done.11, bf16[2048,128]{1,0:T(8,128)(2,1)} %copy-done.1), kind=kLoop, calls=%fused_computation.14 | loop fusion | flops 327680 | bytes 393216 | tf_op jit(solution)/shard_map/convert_element_type | solution.py:244
  59.6 1.3 %collective-permute-start.22 = (bf16[256,128]{1,0:T(8,128)(2,1)S(1)}, bf16[256,128]{1,0:T(8,128)(2,1)S(1)}, u32[]{:S(2)}, u32[]{:S(2)}) collective-permute-start(bf16[256,128]{1,0:T(8,128)(2,1)S(1)} %add_convert_fusion.8), channel_id=1, source_target_pairs={{0,16},{1,17},{2,18},{3,19},{4,20},{5,21},{6,22},{7,23},{8,24},{9,... | collective-permute-start | bytes 196616 | tf_op jit(solution)/shard_map/ppermute | solution.py:383
  61.2 2.7 %collective-permute-done.22 = bf16[256,128]{1,0:T(8,128)(2,1)S(1)} collective-permute-done((bf16[256,128]{1,0:T(8,128)(2,1)S(1)}, bf16[256,128]{1,0:T(8,128)(2,1)S(1)}, u32[]{:S(2)}, u32[]{:S(2)}) %collective-permute-start.22) | collective-permute-done | bytes 65568 | tf_op jit(solution)/shard_map/ppermute | solution.py:383
  63.9 0.9 collective-permute-start.23
  64.8 0.7 collective-permute-start.24
  65.5 1.5 %collective-permute-start.18 = (bf16[544,128]{1,0:T(8,128)(2,1)S(1)}, bf16[544,128]{1,0:T(8,128)(2,1)S(1)}, u32[]{:S(2)}, u32[]{:S(2)}) collective-permute-start(bf16[544,128]{1,0:T(8,128)(2,1)S(1)} %pad_maximum_fusion.3), channel_id=1, source_target_pairs={{0,16},{1,17},{2,18},{3,19},{4,20},{5,21},{6,22},{7,23},{8,24},{9,... | collective-permute-start | bytes 417800 | tf_op jit(solution)/shard_map/ppermute | solution.py:383
  67.0 2.5 %collective-permute-done.23 = bf16[256,128]{1,0:T(8,128)(2,1)S(1)} collective-permute-done((bf16[256,128]{1,0:T(8,128)(2,1)S(1)}, bf16[256,128]{1,0:T(8,128)(2,1)S(1)}, u32[]{:S(2)}, u32[]{:S(2)}) %collective-permute-start.23) | collective-permute-done | bytes 65568 | tf_op jit(solution)/shard_map/ppermute | solution.py:383
  69.5 1.3 %collective-permute-start.25 = (bf16[512,128]{1,0:T(8,128)(2,1)S(1)}, bf16[512,128]{1,0:T(8,128)(2,1)S(1)}, u32[]{:S(2)}, u32[]{:S(2)}) collective-permute-start(bf16[512,128]{1,0:T(8,128)(2,1)S(1)} %pad_maximum_fusion.5), channel_id=1, source_target_pairs={{0,1},{1,0},{2,3},{3,2},{4,5},{5,4},{6,7},{7,6},{8,9},{9,8},{10,11... | collective-permute-start | bytes 393224 | tf_op jit(solution)/shard_map/ppermute | solution.py:383
  71.0 1.3 %collective-permute-start.19 = (bf16[1088,128]{1,0:T(8,128)(2,1)S(1)}, bf16[1088,128]{1,0:T(8,128)(2,1)S(1)}, u32[]{:S(2)}, u32[]{:S(2)}) collective-permute-start(bf16[1088,128]{1,0:T(8,128)(2,1)S(1)} %pad_maximum_fusion.1.refs_0_.refs_2_), channel_id=1, source_target_pairs={{0,1},{1,0},{2,3},{3,2},{4,5},{5,4},{6,7},{7,6},{8,9},{9,8},{10,11... | collective-permute-start | bytes 835592 | tf_op jit(solution)/shard_map/ppermute | solution.py:383
  72.2 2.9 %collective-permute-done.25 = bf16[512,128]{1,0:T(8,128)(2,1)S(1)} collective-permute-done((bf16[512,128]{1,0:T(8,128)(2,1)S(1)}, bf16[512,128]{1,0:T(8,128)(2,1)S(1)}, u32[]{:S(2)}, u32[]{:S(2)}) %collective-permute-start.25) | collective-permute-done | bytes 131104 | tf_op jit(solution)/shard_map/ppermute | solution.py:383
  75.2 2.8 %collective-permute-start.26 = (bf16[1024,128]{1,0:T(8,128)(2,1)S(1)}, bf16[1024,128]{1,0:T(8,128)(2,1)S(1)}, u32[]{:S(2)}, u32[]{:S(2)}) collective-permute-start(bf16[1024,128]{1,0:T(8,128)(2,1)S(1)} %constant_dynamic-update-slice_fusion.refs_1_), channel_id=1, source_target_pairs={{0,2},{1,3},{2,0},{3,1},{4,6},{5,7},{6,4},{7,5},{8,10},{9,11},{10,... | collective-permute-start | bytes 786440 | tf_op jit(solution)/shard_map/ppermute | solution.py:383
  78.0 2.8 %shard_map.130 = bf16[2,128,512]{2,1,0:T(8,128)(2,1)} custom-call(s32[11]{0:T(128)S(1)} %stack.71.bits, bf16[2,4,128,128]{3,2,1,0:T(8,128)(2,1)S(1)} %get-tuple-element.70.dconv, bf16[256,128]{1,0:T(8,128)(2,1)S(1)} %collective-permute-done.14.x_got, bf16[128,128]{1,0:T(8,128)(2,1)S(1)} %slice.170.z_got, ...), custom_call_target="tpu_custom_call" | custom-call | tf_op jit(solution)/shard_map/pallas_call | solution.py:344
  80.9 2.0 %shard_map.131 = (f32[512,512]{1,0:T(8,128)}, f32[512,512]{1,0:T(8,128)}, f32[512,512]{1,0:T(8,128)}, f32[512,512]{1,0:T(8,128)}) custom-call(s32[11]{0:T(128)S(1)} %stack.71.bits, bf16[1088,128]{1,0:T(8,128)(2,1)S(1)} %pad_maximum_fusion.1.refs_0_.refs_2_, bf16[1024,128]{1,0:T(8,128)(2,1)S(1)} %constant_dynamic-update-slice_fusion.refs_1_, ...), custom_call_target="tpu_custom_call" | custom-call | tf_op jit(solution)/shard_map/pallas_call | solution.py:344
  82.9 2.0 %collective-permute-done.26.refs_1_ = bf16[1024,128]{1,0:T(8,128)(2,1)S(1)} collective-permute-done((bf16[1024,128]{1,0:T(8,128)(2,1)S(1)}, bf16[1024,128]{1,0:T(8,128)(2,1)S(1)}, u32[]{:S(2)}, u32[]{:S(2)}) %collective-permute-start.26) | collective-permute-done | bytes 262176 | tf_op jit(solution)/shard_map/ppermute | solution.py:383
  84.9 0.5 collective-permute-start.30
  85.4 1.6 %shard_map.132 = (f32[512,512]{1,0:T(8,128)}, f32[512,512]{1,0:T(8,128)}, f32[512,512]{1,0:T(8,128)}, f32[512,512]{1,0:T(8,128)}) custom-call(s32[11]{0:T(128)S(1)} %stack.71.bits, bf16[1088,128]{1,0:T(8,128)(2,1)S(1)} %collective-permute-done.19.refs_0_.refs_3_, ...), custom_call_target="tpu_custom_call", output_to_operand_aliasing={{0}: (3, {}), {1}: (4, {}), {2}: (5, {}), {3}: (6, {})} | custom-call | tf_op jit(solution)/shard_map/pallas_call | solution.py:344
  87.1 2.2 %shard_map.133 = (f32[512,512]{1,0:T(8,128)}, f32[512,512]{1,0:T(8,128)}, f32[512,512]{1,0:T(8,128)}, f32[512,512]{1,0:T(8,128)}, f32[31,512]{1,0:T(8,128)}) custom-call(s32[11]{0:T(128)S(1)} %stack.71.bits, bf16[1088,128]{1,0:T(8,128)(2,1)S(1)} %collective-permute-done.29.refs_0_.refs_5_, ...), custom_call_target="tpu_custom_call", output_to_operand_aliasing={{0}: (7, {}), {1}: (8, {}), {2}: (9, {}), {3}: (10, {})} | custom-call | tf_op jit(solution)/shard_map/pallas_call | solution.py:344
  (55 shorter events, 2.8 us)
Async XLA Ops:
  2.7 7.2 %collective-permute-start = (bf16[2,2,32,512]{3,2,1,0:T(8,128)(2,1)S(1)}, bf16[2,2,32,512]{3,2,1,0:T(8,128)(2,1)S(1)}, u32[]{:S(2)}, u32[]{:S(2)}) collective-permute-start(bf16[2,2,32,512]{3,2,1,0:T(8,128)(2,1)S(1)} %pad_maximum_fusion.4), channel_id=1, source_target_pairs={{0,8},{1,9},{2,10},{3,11},{4,12},{5,13},{6,14},{7,15},{8,0},{9,1},... | collective-permute-start | bytes 393224 | tf_op jit(solution)/shard_map/ppermute | solution.py:383
  3.2 5.3 %collective-permute-start.1 = (bf16[2,32,512]{2,1,0:T(8,128)(2,1)S(1)}, bf16[2,32,512]{2,1,0:T(8,128)(2,1)S(1)}, u32[]{:S(2)}, u32[]{:S(2)}) collective-permute-start(bf16[2,32,512]{2,1,0:T(8,128)(2,1)S(1)} %get-tuple-element.98), channel_id=1, source_target_pairs={{0,16},{1,17},{2,18},{3,19},{4,20},{5,21},{6,22},{7,23},{8,24},{9,... | collective-permute-start | bytes 196616 | tf_op jit(solution)/shard_map/ppermute | solution.py:383
  5.8 4.0 %collective-permute-start.2 = (bf16[2,32,512]{2,1,0:T(8,128)(2,1)S(1)}, bf16[2,32,512]{2,1,0:T(8,128)(2,1)S(1)}, u32[]{:S(2)}, u32[]{:S(2)}) collective-permute-start(bf16[2,32,512]{2,1,0:T(8,128)(2,1)S(1)} %get-tuple-element.95), channel_id=1, source_target_pairs={{0,24},{1,25},{2,26},{3,27},{4,28},{5,29},{6,30},{7,31},{8,16},{9,... | collective-permute-start | bytes 196616 | tf_op jit(solution)/shard_map/ppermute | solution.py:383
  5.8 9.7 %copy-start.2 = (f32[31,512]{1,0:T(8,128)S(1)}, f32[31,512]{1,0:T(8,128)}, u32[]{:S(2)}) copy-start(f32[31,512]{1,0:T(8,128)} %kern.3) | copy-start | bytes 190468
  10.4 5.2 %collective-permute-start.3 = (bf16[4,2,16,512]{3,2,1,0:T(8,128)(2,1)S(1)}, bf16[4,2,16,512]{3,2,1,0:T(8,128)(2,1)S(1)}, u32[]{:S(2)}, u32[]{:S(2)}) collective-permute-start(bf16[4,2,16,512]{3,2,1,0:T(8,128)(2,1)S(1)} %get-tuple-element.51), channel_id=1, source_target_pairs={{0,8},{1,9},{2,10},{3,11},{4,12},{5,13},{6,14},{7,15},{8,0},{9,1},... | collective-permute-start | bytes 393224 | tf_op jit(solution)/shard_map/ppermute | solution.py:383
  10.6 4.9 %collective-permute-start.4 = (bf16[4,2,16,512]{3,2,1,0:T(8,128)(2,1)S(1)}, bf16[4,2,16,512]{3,2,1,0:T(8,128)(2,1)S(1)}, u32[]{:S(2)}, u32[]{:S(2)}) collective-permute-start(bf16[4,2,16,512]{3,2,1,0:T(8,128)(2,1)S(1)} %get-tuple-element.52), channel_id=1, source_target_pairs={{8,24},{9,25},{10,26},{11,27},{12,28},{13,29},{14,30},{15,31},{24,... | collective-permute-start | bytes 393224 | tf_op jit(solution)/shard_map/ppermute | solution.py:383
  11.3 7.0 %collective-permute-start.5 = (bf16[2,32,512]{2,1,0:T(8,128)(2,1)S(1)}, bf16[2,32,512]{2,1,0:T(8,128)(2,1)S(1)}, u32[]{:S(2)}, u32[]{:S(2)}) collective-permute-start(bf16[2,32,512]{2,1,0:T(8,128)(2,1)S(1)} %get-tuple-element.92), channel_id=1, source_target_pairs={{0,16},{1,17},{2,18},{3,19},{4,20},{5,21},{6,22},{7,23},{8,24},{9,... | collective-permute-start | bytes 196616 | tf_op jit(solution)/shard_map/ppermute | solution.py:383
  15.5 4.1 %collective-permute-start.6 = (bf16[2,32,512]{2,1,0:T(8,128)(2,1)S(1)}, bf16[2,32,512]{2,1,0:T(8,128)(2,1)S(1)}, u32[]{:S(2)}, u32[]{:S(2)}) collective-permute-start(bf16[2,32,512]{2,1,0:T(8,128)(2,1)S(1)} %get-tuple-element.91), channel_id=1, source_target_pairs={{0,24},{1,25},{2,26},{3,27},{4,28},{5,29},{6,30},{7,31},{8,16},{9,... | collective-permute-start | bytes 196616 | tf_op jit(solution)/shard_map/ppermute | solution.py:383
  28.0 6.6 %copy-start.1 = (bf16[2048,128]{1,0:T(8,128)(2,1)}, bf16[2048,128]{1,0:T(8,128)(2,1)S(1)}, u32[]{:S(2)}) copy-start(bf16[2048,128]{1,0:T(8,128)(2,1)S(1)} %get-tuple-element.61) | copy-start | bytes 1572868
  28.0 2.4 %collective-permute-start.9 = (bf16[2176,128]{1,0:T(8,128)(2,1)S(1)}, bf16[2176,128]{1,0:T(8,128)(2,1)S(1)}, u32[]{:S(2)}, u32[]{:S(2)}) collective-permute-start(bf16[2176,128]{1,0:T(8,128)(2,1)S(1)} %get-tuple-element.60), channel_id=1, source_target_pairs={{0,8},{1,9},{2,10},{3,11},{4,12},{5,13},{6,14},{7,15},{8,0},{9,1},... | collective-permute-start | bytes 1671176 | tf_op jit(solution)/shard_map/ppermute | solution.py:383
  28.1 2.3 %collective-permute-start.7 = (bf16[1024,128]{1,0:T(8,128)(2,1)S(1)}, bf16[1024,128]{1,0:T(8,128)(2,1)S(1)}, u32[]{:S(2)}, u32[]{:S(2)}) collective-permute-start(bf16[1024,128]{1,0:T(8,128)(2,1)S(1)} %get-tuple-element.58), channel_id=1, source_target_pairs={{0,8},{1,9},{2,10},{3,11},{4,12},{5,13},{6,14},{7,15},{8,0},{9,1},... | collective-permute-start | bytes 786440 | tf_op jit(solution)/shard_map/ppermute | solution.py:383
  28.6 6.0 %collective-permute-start.11 = (bf16[2048,128]{1,0:T(8,128)(2,1)S(1)}, bf16[2048,128]{1,0:T(8,128)(2,1)S(1)}, u32[]{:S(2)}, u32[]{:S(2)}) collective-permute-start(bf16[2048,128]{1,0:T(8,128)(2,1)S(1)} %get-tuple-element.62), channel_id=1, source_target_pairs={{0,8},{1,9},{2,10},{3,11},{4,12},{5,13},{6,14},{7,15},{8,0},{9,1},... | collective-permute-start | bytes 1572872 | tf_op jit(solution)/shard_map/ppermute | solution.py:383
  30.5 9.7 %collective-permute-start.10 = (bf16[1088,128]{1,0:T(8,128)(2,1)S(1)}, bf16[1088,128]{1,0:T(8,128)(2,1)S(1)}, u32[]{:S(2)}, u32[]{:S(2)}) collective-permute-start(bf16[1088,128]{1,0:T(8,128)(2,1)S(1)} %add_convert_fusion), channel_id=1, source_target_pairs={{0,1},{1,0},{2,3},{3,2},{4,5},{5,4},{6,7},{7,6},{8,9},{9,8},{10,11... | collective-permute-start | bytes 835592 | tf_op jit(solution)/shard_map/ppermute | solution.py:383
  34.0 8.3 %collective-permute-start.8 = (bf16[1024,128]{1,0:T(8,128)(2,1)}, bf16[1024,128]{1,0:T(8,128)(2,1)S(1)}, u32[]{:S(2)}, u32[]{:S(2)}) collective-permute-start(bf16[1024,128]{1,0:T(8,128)(2,1)} %pad_maximum_fusion.2), channel_id=1, source_target_pairs={{0,16},{1,17},{2,18},{3,19},{4,20},{5,21},{6,22},{7,23},{8,24},{9,... | collective-permute-start | bytes 786440 | tf_op jit(solution)/shard_map/ppermute | solution.py:383
  34.7 8.0 %collective-permute-start.12 = (bf16[1024,128]{1,0:T(8,128)(2,1)S(1)}, bf16[1024,128]{1,0:T(8,128)(2,1)}, u32[]{:S(2)}, u32[]{:S(2)}) collective-permute-start(bf16[1024,128]{1,0:T(8,128)(2,1)S(1)} %add_convert_fusion.1), channel_id=1, source_target_pairs={{0,2},{1,3},{2,0},{3,1},{4,6},{5,7},{6,4},{7,5},{8,10},{9,11},{10,... | collective-permute-start | bytes 786440 | tf_op jit(solution)/shard_map/ppermute | solution.py:383
  40.3 8.6 %collective-permute-start.13 = (bf16[544,128]{1,0:T(8,128)(2,1)S(1)}, bf16[544,128]{1,0:T(8,128)(2,1)S(1)}, u32[]{:S(2)}, u32[]{:S(2)}) collective-permute-start(bf16[544,128]{1,0:T(8,128)(2,1)S(1)} %add_convert_fusion.2), channel_id=1, source_target_pairs={{0,16},{1,17},{2,18},{3,19},{4,20},{5,21},{6,22},{7,23},{8,24},{9,... | collective-permute-start | bytes 417800 | tf_op jit(solution)/shard_map/ppermute | solution.py:383
  44.0 34.1 %copy-start = (bf16[2,128,512]{2,1,0:T(8,128)(2,1)S(1)}, bf16[2,128,512]{2,1,0:T(8,128)(2,1)}, u32[]{:S(2)}) copy-start(bf16[2,128,512]{2,1,0:T(8,128)(2,1)} %cot.1) | copy-start | bytes 786436
  44.0 5.0 %collective-permute-start.14 = (bf16[256,128]{1,0:T(8,128)(2,1)S(1)}, bf16[256,128]{1,0:T(8,128)(2,1)S(1)}, u32[]{:S(2)}, u32[]{:S(2)}) collective-permute-start(bf16[256,128]{1,0:T(8,128)(2,1)S(1)} %pad_maximum_fusion.7), channel_id=1, source_target_pairs={{0,1},{1,0},{2,3},{3,2},{4,5},{5,4},{6,7},{7,6},{8,9},{9,8},{10,11... | collective-permute-start | bytes 196616 | tf_op jit(solution)/shard_map/ppermute | solution.py:383
  45.6 5.0 %collective-permute-start.20 = (bf16[512,128]{1,0:T(8,128)(2,1)S(1)}, bf16[512,128]{1,0:T(8,128)(2,1)S(1)}, u32[]{:S(2)}, u32[]{:S(2)}) collective-permute-start(bf16[512,128]{1,0:T(8,128)(2,1)S(1)} %add_convert_fusion.3), channel_id=1, source_target_pairs={{0,1},{1,0},{2,3},{3,2},{4,5},{5,4},{6,7},{7,6},{8,9},{9,8},{10,11... | collective-permute-start | bytes 393224 | tf_op jit(solution)/shard_map/ppermute | solution.py:383
  49.0 5.4 %collective-permute-start.15 = (bf16[400,128]{1,0:T(8,128)(2,1)S(1)}, bf16[400,128]{1,0:T(8,128)(2,1)S(1)}, u32[]{:S(2)}, u32[]{:S(2)}) collective-permute-start(bf16[400,128]{1,0:T(8,128)(2,1)S(1)} %pad_maximum_fusion.6), channel_id=1, source_target_pairs={{0,2},{1,3},{2,0},{3,1},{4,6},{5,7},{6,4},{7,5},{8,10},{9,11},{10,... | collective-permute-start | bytes 307208 | tf_op jit(solution)/shard_map/ppermute | solution.py:383
  51.5 7.1 %collective-permute-start.21 = (bf16[256,128]{1,0:T(8,128)(2,1)S(1)}, bf16[256,128]{1,0:T(8,128)(2,1)S(1)}, u32[]{:S(2)}, u32[]{:S(2)}) collective-permute-start(bf16[256,128]{1,0:T(8,128)(2,1)S(1)} %add_convert_fusion.9), channel_id=1, source_target_pairs={{0,4},{1,5},{2,6},{3,7},{4,0},{5,1},{6,2},{7,3},{8,12},{9,13},{10,... | collective-permute-start | bytes 196616 | tf_op jit(solution)/shard_map/ppermute | solution.py:383
  54.5 6.4 %collective-permute-start.16 = (bf16[272,128]{1,0:T(8,128)(2,1)S(1)}, bf16[272,128]{1,0:T(8,128)(2,1)S(1)}, u32[]{:S(2)}, u32[]{:S(2)}) collective-permute-start(bf16[272,128]{1,0:T(8,128)(2,1)S(1)} %add_convert_fusion.5), channel_id=1, source_target_pairs={{0,4},{1,5},{2,6},{3,7},{4,0},{5,1},{6,2},{7,3},{8,12},{9,13},{10,... | collective-permute-start | bytes 208904 | tf_op jit(solution)/shard_map/ppermute | solution.py:383
  59.6 4.3 %collective-permute-start.22 = (bf16[256,128]{1,0:T(8,128)(2,1)S(1)}, bf16[256,128]{1,0:T(8,128)(2,1)S(1)}, u32[]{:S(2)}, u32[]{:S(2)}) collective-permute-start(bf16[256,128]{1,0:T(8,128)(2,1)S(1)} %add_convert_fusion.8), channel_id=1, source_target_pairs={{0,16},{1,17},{2,18},{3,19},{4,20},{5,21},{6,22},{7,23},{8,24},{9,... | collective-permute-start | bytes 196616 | tf_op jit(solution)/shard_map/ppermute | solution.py:383
  60.9 4.5 %collective-permute-start.17 = (bf16[272,128]{1,0:T(8,128)(2,1)S(1)}, bf16[272,128]{1,0:T(8,128)(2,1)S(1)}, u32[]{:S(2)}, u32[]{:S(2)}) collective-permute-start(bf16[272,128]{1,0:T(8,128)(2,1)S(1)} %add_convert_fusion.4), channel_id=1, source_target_pairs={{0,2},{1,3},{2,0},{3,1},{4,6},{5,7},{6,4},{7,5},{8,10},{9,11},{10,... | collective-permute-start | bytes 208904 | tf_op jit(solution)/shard_map/ppermute | solution.py:383
  63.9 5.6 %collective-permute-start.23 = (bf16[256,128]{1,0:T(8,128)(2,1)S(1)}, bf16[256,128]{1,0:T(8,128)(2,1)S(1)}, u32[]{:S(2)}, u32[]{:S(2)}) collective-permute-start(bf16[256,128]{1,0:T(8,128)(2,1)S(1)} %add_convert_fusion.7), channel_id=1, source_target_pairs={{0,4},{1,5},{2,6},{3,7},{4,0},{5,1},{6,2},{7,3},{8,12},{9,13},{10,... | collective-permute-start | bytes 196616 | tf_op jit(solution)/shard_map/ppermute | solution.py:383
  64.8 4.7 %collective-permute-start.24 = (bf16[128,128]{1,0:T(8,128)(2,1)S(1)}, bf16[128,128]{1,0:T(8,128)(2,1)S(1)}, u32[]{:S(2)}, u32[]{:S(2)}) collective-permute-start(bf16[128,128]{1,0:T(8,128)(2,1)S(1)} %constant_dynamic-slice_fusion), channel_id=1, source_target_pairs={{2,4},{3,5},{10,12},{11,13},{18,20},{19,21},{26,28},{27,29},{4,2},... | collective-permute-start | bytes 98312 | tf_op jit(solution)/shard_map/ppermute | solution.py:383
  65.5 5.4 %collective-permute-start.18 = (bf16[544,128]{1,0:T(8,128)(2,1)S(1)}, bf16[544,128]{1,0:T(8,128)(2,1)S(1)}, u32[]{:S(2)}, u32[]{:S(2)}) collective-permute-start(bf16[544,128]{1,0:T(8,128)(2,1)S(1)} %pad_maximum_fusion.3), channel_id=1, source_target_pairs={{0,16},{1,17},{2,18},{3,19},{4,20},{5,21},{6,22},{7,23},{8,24},{9,... | collective-permute-start | bytes 417800 | tf_op jit(solution)/shard_map/ppermute | solution.py:383
  69.5 5.6 %collective-permute-start.25 = (bf16[512,128]{1,0:T(8,128)(2,1)S(1)}, bf16[512,128]{1,0:T(8,128)(2,1)S(1)}, u32[]{:S(2)}, u32[]{:S(2)}) collective-permute-start(bf16[512,128]{1,0:T(8,128)(2,1)S(1)} %pad_maximum_fusion.5), channel_id=1, source_target_pairs={{0,1},{1,0},{2,3},{3,2},{4,5},{5,4},{6,7},{7,6},{8,9},{9,8},{10,11... | collective-permute-start | bytes 393224 | tf_op jit(solution)/shard_map/ppermute | solution.py:383
  70.9 10.0 %collective-permute-start.27 = (bf16[1088,128]{1,0:T(8,128)(2,1)S(1)}, bf16[1088,128]{1,0:T(8,128)(2,1)S(1)}, u32[]{:S(2)}, u32[]{:S(2)}) collective-permute-start(bf16[1088,128]{1,0:T(8,128)(2,1)S(1)} %pad_maximum_fusion.1.refs_0_.refs_2_), channel_id=1, source_target_pairs={{0,8},{1,9},{2,10},{3,11},{4,12},{5,13},{6,14},{7,15},{8,0},{9,1},... | collective-permute-start | bytes 835592 | tf_op jit(solution)/shard_map/ppermute | solution.py:383
  71.0 14.0 %collective-permute-start.19 = (bf16[1088,128]{1,0:T(8,128)(2,1)S(1)}, bf16[1088,128]{1,0:T(8,128)(2,1)S(1)}, u32[]{:S(2)}, u32[]{:S(2)}) collective-permute-start(bf16[1088,128]{1,0:T(8,128)(2,1)S(1)} %pad_maximum_fusion.1.refs_0_.refs_2_), channel_id=1, source_target_pairs={{0,1},{1,0},{2,3},{3,2},{4,5},{5,4},{6,7},{7,6},{8,9},{9,8},{10,11... | collective-permute-start | bytes 835592 | tf_op jit(solution)/shard_map/ppermute | solution.py:383
  75.1 5.7 %collective-permute-start.28 = (bf16[1024,128]{1,0:T(8,128)(2,1)S(1)}, bf16[1024,128]{1,0:T(8,128)(2,1)S(1)}, u32[]{:S(2)}, u32[]{:S(2)}) collective-permute-start(bf16[1024,128]{1,0:T(8,128)(2,1)S(1)} %constant_dynamic-update-slice_fusion.refs_1_), channel_id=1, source_target_pairs={{0,8},{1,9},{2,10},{3,11},{4,12},{5,13},{6,14},{7,15},{8,0},{9,1},... | collective-permute-start | bytes 786440 | tf_op jit(solution)/shard_map/ppermute | solution.py:383
  75.2 9.7 %collective-permute-start.26 = (bf16[1024,128]{1,0:T(8,128)(2,1)S(1)}, bf16[1024,128]{1,0:T(8,128)(2,1)S(1)}, u32[]{:S(2)}, u32[]{:S(2)}) collective-permute-start(bf16[1024,128]{1,0:T(8,128)(2,1)S(1)} %constant_dynamic-update-slice_fusion.refs_1_), channel_id=1, source_target_pairs={{0,2},{1,3},{2,0},{3,1},{4,6},{5,7},{6,4},{7,5},{8,10},{9,11},{10,... | collective-permute-start | bytes 786440 | tf_op jit(solution)/shard_map/ppermute | solution.py:383
  84.9 2.1 %collective-permute-start.29 = (bf16[1088,128]{1,0:T(8,128)(2,1)S(1)}, bf16[1088,128]{1,0:T(8,128)(2,1)S(1)}, u32[]{:S(2)}, u32[]{:S(2)}) collective-permute-start(bf16[1088,128]{1,0:T(8,128)(2,1)S(1)} %collective-permute-done.19.refs_0_.refs_3_), channel_id=1, source_target_pairs={{0,8},{1,9},{2,10},{3,11},{4,12},{5,13},{6,14},{7,15},{8,0},{9,1},... | collective-permute-start | bytes 835592 | tf_op jit(solution)/shard_map/ppermute | solution.py:383
  84.9 2.1 %collective-permute-start.30 = (bf16[1024,128]{1,0:T(8,128)(2,1)S(1)}, bf16[1024,128]{1,0:T(8,128)(2,1)S(1)}, u32[]{:S(2)}, u32[]{:S(2)}) collective-permute-start(bf16[1024,128]{1,0:T(8,128)(2,1)S(1)} %collective-permute-done.26.refs_1_), channel_id=1, source_target_pairs={{0,8},{1,9},{2,10},{3,11},{4,12},{5,13},{6,14},{7,15},{8,0},{9,1},... | collective-permute-start | bytes 786440 | tf_op jit(solution)/shard_map/ppermute | solution.py:383

commit v15 on v14

--- a/solution.py
+++ b/solution.py
@@ -48,9 +48,9 @@
     return 0.5 * jnp.tanh(0.5 * v) + 0.5
 
 
-def edge_kernel(sub, bits, f0, pair, f2, f3, near, side):
+def edge_kernel(sub, bits, f0, f1, f2, f3, near, side):
     odd = bits[ODD]
-    for d, f in enumerate((f0, pair.at[0], f2, f3)):
+    for d, f in enumerate((f0, f1, f2, f3)):
         last = sub - HALO
         near[d] = f[:, pl.ds(pl.multiple_of((1 - odd) * last, HALO), HALO), :]
         side[d] = f[:, pl.ds(pl.multiple_of(odd * last, HALO), HALO), :]
@@ -70,11 +70,11 @@
     )
 
 
-def conv_kernel(plan, bits, f0, pair, f2, f3, near, side, kern, frames, conv_out, acted_out):
+def conv_kernel(plan, bits, f0, f1, f2, f3, near, side, kern, frames, conv_out, acted_out):
     groups, count, sub, width = plan
     mics = groups * count
     cuts = sub // HALO
-    for d, f in enumerate((f0, pair.at[0], f2, f3)):
+    for d, f in enumerate((f0, f1, f2, f3)):
         frames[d] = f[...]
 
     def conv_step(n, _):
@@ -94,7 +94,7 @@
 
 
 def main_kernel(
-    plan, bits, frames, conv_in, acted_in, c0, pair, c2, c3, near, side, weights,
+    plan, bits, frames, conv_in, acted_in, c0, c1, c2, c3, near, side, weights,
     a_keep, b_keep, a_send, b_send, back_keep, back_send,
     left_s, turned_s, right_s, q_s, k_s, v_s, u_s, dconv_s, tap_s,
 ):
@@ -107,7 +107,7 @@
 
     wq, wk, wv, wo = (weights.at[i] for i in range(4))
     left_s[0] = acted_in[...]
-    for d, cot in enumerate((c0, pair.at[1], c2, c3)):
+    for d, cot in enumerate((c0, c1, c2, c3)):
         for m in range(count):
             for c in range(cuts):
                 right_s[3, c, d, m] = cot[m, c * HALO : (c + 1) * HALO, :]
@@ -393,13 +393,15 @@
     def sub_block(x, d):
         return lax.dynamic_slice_in_dim(x, order(mic ^ d) * sub, sub, axis=1)
 
-    f, c = [[sub_block(x, d) for d in range(4)] for x in (frames, cotangent)]
-    f[2], f[3] = (swap(f[d], masks[d]) for d in (2, 3))
-    near_pair = swap(jnp.stack([f[1], c[1]]), masks[1])
-    c[2], c[3] = (swap(c[d], masks[d]) for d in (2, 3))
+    def scattered(x):
+        parts = [sub_block(x, d) for d in range(4)]
+        got = {d: swap(parts[d], masks[d]) for d in (2, 3, 1)}
+        return [parts[0], got[1], got[2], got[3]]
+
+    f, c = scattered(frames), scattered(cotangent)
     weights = jnp.stack([w_query, w_key, w_value, w_out])
     edge = shape((groups, count, HALO, width), BF)
-    near, side = call(functools.partial(edge_kernel, sub), (edge, edge), [], 8, bits, f[0], near_pair, f[2], f[3])
+    near, side = call(functools.partial(edge_kernel, sub), (edge, edge), [], 4, bits, *f)
     near, side, weights = lax.optimization_barrier((near, side, weights))
     near = swap(near, over_core)
     side = permute(
@@ -423,7 +425,7 @@
     placed, conv, acted = call(
         functools.partial(conv_kernel, (groups, count, sub, width)),
         (moved, shape((rows, width), F32), shape((rows, width), BF)),
-        [], 8, bits, f[0], near_pair, f[2], f[3], near, side, kernel,
+        [], 4, bits, *f, near, side, kernel,
     )
     a_keep, b_keep, a_send, b_send, back_keep, back_send = call(
         functools.partial(main_kernel, (groups, count, sub, width, factor)),
@@ -435,7 +437,7 @@
             big, big, big, big, wide,
             pltpu.VMEM((32 * cols + HALO, LANES), F32),
         ],
-        24, bits, placed, conv, acted, c[0], near_pair, c[2], c[3], near, side, weights,
+        14, bits, placed, conv, acted, *c, near, side, weights,
     )
 
     lines = [2**i for i in range(1, blocks.bit_length() - 1)]
@@ -462,12 +464,12 @@
     a = halved(a, over_x)
     b = halved(b, lines[0])
     y_got = swap(jnp.concatenate([back_keep[unit:], core_got[unit:]]), over_y)
-    y_got = after(y_got, (a[-1], b[-1]))
+    y_got = after(y_got, a[-1])
     edge = flat(count * cols * HALO)
     layer_out, dconv, *edges = call(
         functools.partial(home_kernel, (count, sub, cols)),
         (shape(frames.shape, BF), shape((count, cols, length, LANES), BF), edge, edge),
-        [], 8, bits, back_keep, core_got, y_got,
+        [], 4, bits, back_keep, core_got, y_got,
     )
     x_got = swap(jnp.concatenate(edges), over_x)
     n_edge = edge.shape[0]
@@ -502,7 +504,7 @@
             functools.partial(final_kernel, (kinds, not grads, bool(taps), width, norm)),
             (square,) * 4 + (shape((31, width), F32),) * bool(taps),
             scratch + [pltpu.VMEM((16, HALO, LANES), F32)] * bool(taps),
-            10, bits, *parts, *taps, *grads, hbm=range(first, first + len(grads)),
+            5, bits, *parts, *taps, *grads, hbm=range(first, first + len(grads)),
             hbm_outs=range(4), aliases={first + i: i for i in range(len(grads))},
         )
 
@@ -510,7 +512,7 @@
     a_other, b_other = swap(a, over_core), swap(b, over_core)
     (frame_grad,) = call(
         functools.partial(frame_kernel, (count, cols, length)),
-        (shape(frames.shape, BF),), [], 8,
+        (shape(frames.shape, BF),), [], 4,
         bits, after(dconv, a), x_got, z_got, other_got, cotangent, kernel,
     )
     grads = final(((1, 0, 0), (1, 1, 0), (0, 0, 0), (0, 1, 0)), (a, b, a_other, b_other), ())

time: 89.7 us -> 88 us (0.981)
  other arithmetic: 5.8 us -> 3.34 us
    convert_element_type x10, other arithmetic: 3.2 us -> 1.44 us  [total(): functools.reduce(lambda x, y: x + y, [x.astype(F32) for x in parts])]
    unnamed x7 -> x11, local copies, waits for them, and re-layouts: 0.02 us -> 1.61 us
    dynamic_slice x2, local copies, waits for them, and re-layouts: 1.94 us -> 1 us  [sub_block(): return lax.dynamic_slice_in_dim(x, order(mic ^ d) * sub, sub, axis=1)]
    ppermute x31 -> x32, starting transfers between devices: 34.2 us -> 33.9 us  [permute(): return lax.ppermute(x, ('mic', 'tm'), pairs)]
    ppermute x31 -> x32, waiting for transfers between devices: 24.8 us -> 24.7 us  [permute(): return lax.ppermute(x, ('mic', 'tm'), pairs)]
  transfers between devices with their start and end apart: 31 -> 32, of which waited for: 16 -> 16; matrix products, arithmetic and copies ran while one was open for 7% -> 4% of each run, Pallas kernels for 11% -> 12%
where the time goes in v15:
time: 88 us; the launch traced here: 87.8 us
  starting transfers between devices  33.9 us (39%)
  waiting for transfers between devices  24.7 us (28%)
  Pallas kernels  22 us (25%)
  other arithmetic  3.34 us (4%)
  local copies, waits for them, and re-layouts  2.74 us (3%)
  between operations  1.07 us (1%)
    ppermute x32, starting transfers between devices, permute(): return lax.ppermute(x, ('mic', 'tm'), pairs)  33.9 us
    ppermute x32, waiting for transfers between devices, permute(): return lax.ppermute(x, ('mic', 'tm'), pairs)  24.7 us
    pallas_call x8, Pallas kernels, call(): pl.pallas_call(body, out_shape=outs, in_specs=[pl.BlockSpec(memory_space=...  22 us
    another operation x1, other arithmetic, shards(): weights = jnp.stack([w_query, w_key, w_value, w_out])  1.82 us
  transfers between devices with their start and end apart: 32, of which 16 were waited for; matrix products, arithmetic and copies ran while one was open for 4% of the time, Pallas kernels for 12%

profile of v15, /device:TPU:0, one launch (start us, length us, event | category | flops | bytes accessed | tf_op | source)
XLA Modules:
  0.0 87.8 jit_solution(1107581187523925846)
XLA Ops:
  0.7 1.0 %constant_dynamic-slice_fusion.5 = (bf16[2,32,512]{2,1,0:T(8,128)(2,1)S(1)}, bf16[2,32,512]{2,1,0:T(8,128)(2,1)S(1)}, bf16[2,32,512]{2,1,0:T(8,128)(2,1)S(1)}, bf16[2,32,512]{2,1,0:T(8,128)(2,1)S(1)}) fusion(bf16[2,128,512]{2,1,0:T(8,128)(2,1)} %param.7, s32[]{:T(128)S(6)} %select_n.100, s32[]{:T(128)S(6)} %select_n.98, s32[]{:T(128)S(6)} %select_n.97, ...), kind=kLoop, calls=%fused_computation.24 | loop fusion | bytes 524304 | tf_op jit(solution)/shard_map/dynamic_slice | solution.py:394
  1.7 0.5 collective-permute-start
  2.2 2.6 %collective-permute-start.1 = (bf16[2,32,512]{2,1,0:T(8,128)(2,1)S(1)}, bf16[2,32,512]{2,1,0:T(8,128)(2,1)S(1)}, u32[]{:S(2)}, u32[]{:S(2)}) collective-permute-start(bf16[2,32,512]{2,1,0:T(8,128)(2,1)S(1)} %get-tuple-element.98), channel_id=1, source_target_pairs={{0,16},{1,17},{2,18},{3,19},{4,20},{5,21},{6,22},{7,23},{8,24},{9,... | collective-permute-start | bytes 196616 | tf_op jit(solution)/shard_map/ppermute | solution.py:383
  4.8 1.8 %pad_maximum_fusion.weights = bf16[4,512,512]{2,1,0:T(8,128)(2,1)S(1)} fusion(bf16[1,512,512]{2,1,0:T(8,128)(2,1)} %bitcast.15, bf16[1,512,512]{2,1,0:T(8,128)(2,1)} %bitcast.16, bf16[1,512,512]{2,1,0:T(8,128)(2,1)} %bitcast.17, bf16[1,512,512]{2,1,0:T(8,128)(2,1)} %bitcast.18), kind=kLoop, calls=%fused_computation | loop fusion | flops 3145728 | bytes 4194304 | tf_op jit(solution)/shard_map/stack | solution.py:402
  6.9 0.6 collective-permute-done.1.f2
  7.5 1.4 %collective-permute-done.2.f3 = bf16[2,32,512]{2,1,0:T(8,128)(2,1)S(1)} collective-permute-done((bf16[2,32,512]{2,1,0:T(8,128)(2,1)S(1)}, bf16[2,32,512]{2,1,0:T(8,128)(2,1)S(1)}, u32[]{:S(2)}, u32[]{:S(2)}) %collective-permute-start.2) | collective-permute-done | bytes 65568 | tf_op jit(solution)/shard_map/ppermute | solution.py:383
  8.8 0.6 shard_map.126
  9.6 0.7 collective-permute-start.4
  10.3 2.7 %collective-permute-start.5 = (bf16[2,32,512]{2,1,0:T(8,128)(2,1)S(1)}, bf16[2,32,512]{2,1,0:T(8,128)(2,1)S(1)}, u32[]{:S(2)}, u32[]{:S(2)}) collective-permute-start(bf16[2,32,512]{2,1,0:T(8,128)(2,1)S(1)} %get-tuple-element.93), channel_id=1, source_target_pairs={{0,8},{1,9},{2,10},{3,11},{4,12},{5,13},{6,14},{7,15},{8,0},{9,1},... | collective-permute-start | bytes 196616 | tf_op jit(solution)/shard_map/ppermute | solution.py:383
  13.0 1.6 %collective-permute-start.6 = (bf16[2,32,512]{2,1,0:T(8,128)(2,1)S(1)}, bf16[2,32,512]{2,1,0:T(8,128)(2,1)S(1)}, u32[]{:S(2)}, u32[]{:S(2)}) collective-permute-start(bf16[2,32,512]{2,1,0:T(8,128)(2,1)S(1)} %get-tuple-element.92), channel_id=1, source_target_pairs={{0,16},{1,17},{2,18},{3,19},{4,20},{5,21},{6,22},{7,23},{8,24},{9,... | collective-permute-start | bytes 196616 | tf_op jit(solution)/shard_map/ppermute | solution.py:383
  14.7 2.5 %shard_map.127 = (bf16[4,2,32,512]{3,2,1,0:T(8,128)(2,1)S(1)}, f32[256,512]{1,0:T(8,128)S(1)}, bf16[256,512]{1,0:T(8,128)(2,1)S(1)}) custom-call(s32[11]{0:T(128)S(1)} %stack.62.bits, bf16[2,32,512]{2,1,0:T(8,128)(2,1)S(1)} %get-tuple-element.97.f0, bf16[2,32,512]{2,1,0:T(8,128)(2,1)S(1)} %collective-permute-done.f1, ...), custom_call_target="tpu_custom_call" | custom-call | tf_op jit(solution)/shard_map/pallas_call | solution.py:344
  17.4 1.4 %collective-permute-done.7.c3 = bf16[2,32,512]{2,1,0:T(8,128)(2,1)S(1)} collective-permute-done((bf16[2,32,512]{2,1,0:T(8,128)(2,1)S(1)}, bf16[2,32,512]{2,1,0:T(8,128)(2,1)S(1)}, u32[]{:S(2)}, u32[]{:S(2)}) %collective-permute-start.7) | collective-permute-done | bytes 65568 | tf_op jit(solution)/shard_map/ppermute | solution.py:383
  18.7 9.1 %shard_map.128 = (bf16[2176,128]{1,0:T(8,128)(2,1)S(1)}, bf16[2048,128]{1,0:T(8,128)(2,1)S(1)}, bf16[2176,128]{1,0:T(8,128)(2,1)}, bf16[2048,128]{1,0:T(8,128)(2...) custom-call(s32[11]{0:T(128)S(1)} %stack.62.bits, ...), custom_call_target="tpu_custom_call" | custom-call | tf_op jit(solution)/shard_map/pallas_call | solution.py:344
  27.8 0.8 copy-done.1
  28.6 0.8 copy-done.4
  30.1 1.9 %collective-permute-done.8.core_got = bf16[1024,128]{1,0:T(8,128)(2,1)S(1)} collective-permute-done((bf16[1024,128]{1,0:T(8,128)(2,1)S(1)}, bf16[1024,128]{1,0:T(8,128)(2,1)S(1)}, u32[]{:S(2)}, u32[]{:S(2)}) %collective-permute-start.8) | collective-permute-done | bytes 262176 | tf_op jit(solution)/shard_map/ppermute | solution.py:383
  32.2 2.5 %collective-permute-start.11 = (bf16[1088,128]{1,0:T(8,128)(2,1)S(1)}, bf16[1088,128]{1,0:T(8,128)(2,1)S(1)}, u32[]{:S(2)}, u32[]{:S(2)}) collective-permute-start(bf16[1088,128]{1,0:T(8,128)(2,1)S(1)} %add_convert_fusion), channel_id=1, source_target_pairs={{0,1},{1,0},{2,3},{3,2},{4,5},{5,4},{6,7},{7,6},{8,9},{9,8},{10,11... | collective-permute-start | bytes 835592 | tf_op jit(solution)/shard_map/ppermute | solution.py:383
  34.7 0.6 collective-permute-start.9
  35.4 1.0 %add_convert_fusion.1 = bf16[1024,128]{1,0:T(8,128)(2,1)S(1)} fusion(bf16[2048,128]{1,0:T(8,128)(2,1)S(1)} %collective-permute-done.19, bf16[2048,128]{1,0:T(8,128)(2,1)} %copy-done.1), kind=kLoop, calls=%fused_computation.2 | loop fusion | flops 524288 | bytes 786432 | tf_op jit(solution)/shard_map/convert_element_type | solution.py:244
  36.4 1.7 %collective-permute-start.20 = (bf16[1024,128]{1,0:T(8,128)(2,1)S(1)}, bf16[1024,128]{1,0:T(8,128)(2,1)S(1)}, u32[]{:S(2)}, u32[]{:S(2)}) collective-permute-start(bf16[1024,128]{1,0:T(8,128)(2,1)S(1)} %add_convert_fusion.1), channel_id=1, source_target_pairs={{0,2},{1,3},{2,0},{3,1},{4,6},{5,7},{6,4},{7,5},{8,10},{9,11},{10,... | collective-permute-start | bytes 786440 | tf_op jit(solution)/shard_map/ppermute | solution.py:383
  38.1 3.7 %collective-permute-done.11 = bf16[1088,128]{1,0:T(8,128)(2,1)S(1)} collective-permute-done((bf16[1088,128]{1,0:T(8,128)(2,1)S(1)}, bf16[1088,128]{1,0:T(8,128)(2,1)S(1)}, u32[]{:S(2)}, u32[]{:S(2)}) %collective-permute-start.11) | collective-permute-done | bytes 278560 | tf_op jit(solution)/shard_map/ppermute | solution.py:383
  41.8 0.9 %collective-permute-start.12 = (bf16[544,128]{1,0:T(8,128)(2,1)S(1)}, bf16[544,128]{1,0:T(8,128)(2,1)S(1)}, u32[]{:S(2)}, u32[]{:S(2)}) collective-permute-start(bf16[544,128]{1,0:T(8,128)(2,1)S(1)} %add_convert_fusion.2), channel_id=1, source_target_pairs={{0,16},{1,17},{2,18},{3,19},{4,20},{5,21},{6,22},{7,23},{8,24},{9,... | collective-permute-start | bytes 417800 | tf_op jit(solution)/shard_map/ppermute | solution.py:383
  42.9 1.3 %shard_map.129 = (bf16[2,128,512]{2,1,0:T(8,128)(2,1)}, bf16[2,4,128,128]{3,2,1,0:T(8,128)(2,1)S(1)}, bf16[128,128]{1,0:T(8,128)(2,1)S(1)}, bf16[128,128]{1,0:T(8,128)(2,1)S(1)}) custom-call(s32[11]{0:T(128)S(1)} %stack.62.bits, bf16[1024,128]{1,0:T(8,128)(2,1)S(1)} %get-tuple-element.57.own, bf16[1024,128]{1,0:T(8,128)(2,1)S(1)} %collective-permute-done.8.core_got, ...), custom_call_target="tpu_custom_call" | custom-call | tf_op jit(solution)/shard_map/pallas_call | solution.py:344
  44.2 1.2 %collective-permute-start.13 = (bf16[256,128]{1,0:T(8,128)(2,1)S(1)}, bf16[256,128]{1,0:T(8,128)(2,1)S(1)}, u32[]{:S(2)}, u32[]{:S(2)}) collective-permute-start(bf16[256,128]{1,0:T(8,128)(2,1)S(1)} %pad_maximum_fusion.6), channel_id=1, source_target_pairs={{0,1},{1,0},{2,3},{3,2},{4,5},{5,4},{6,7},{7,6},{8,9},{9,8},{10,11... | collective-permute-start | bytes 196616 | tf_op jit(solution)/shard_map/ppermute | solution.py:383
  45.5 0.9 collective-permute-start.21
  46.4 2.7 %collective-permute-done.13.x_got = bf16[256,128]{1,0:T(8,128)(2,1)S(1)} collective-permute-done((bf16[256,128]{1,0:T(8,128)(2,1)S(1)}, bf16[256,128]{1,0:T(8,128)(2,1)S(1)}, u32[]{:S(2)}, u32[]{:S(2)}) %collective-permute-start.13) | collective-permute-done | bytes 65568 | tf_op jit(solution)/shard_map/ppermute | solution.py:383
  49.2 1.7 %collective-permute-start.14 = (bf16[400,128]{1,0:T(8,128)(2,1)S(1)}, bf16[400,128]{1,0:T(8,128)(2,1)S(1)}, u32[]{:S(2)}, u32[]{:S(2)}) collective-permute-start(bf16[400,128]{1,0:T(8,128)(2,1)S(1)} %pad_maximum_fusion.5), channel_id=1, source_target_pairs={{0,2},{1,3},{2,0},{3,1},{4,6},{5,7},{6,4},{7,5},{8,10},{9,11},{10,... | collective-permute-start | bytes 307208 | tf_op jit(solution)/shard_map/ppermute | solution.py:383
  50.9 2.4 %collective-permute-start.22 = (bf16[256,128]{1,0:T(8,128)(2,1)S(1)}, bf16[256,128]{1,0:T(8,128)(2,1)S(1)}, u32[]{:S(2)}, u32[]{:S(2)}) collective-permute-start(bf16[256,128]{1,0:T(8,128)(2,1)S(1)} %add_convert_fusion.9), channel_id=1, source_target_pairs={{0,4},{1,5},{2,6},{3,7},{4,0},{5,1},{6,2},{7,3},{8,12},{9,13},{10,... | collective-permute-start | bytes 196616 | tf_op jit(solution)/shard_map/ppermute | solution.py:383
  53.3 1.3 %collective-permute-done.14 = bf16[400,128]{1,0:T(8,128)(2,1)S(1)} collective-permute-done((bf16[400,128]{1,0:T(8,128)(2,1)S(1)}, bf16[400,128]{1,0:T(8,128)(2,1)S(1)}, u32[]{:S(2)}, u32[]{:S(2)}) %collective-permute-start.14) | collective-permute-done | bytes 102432 | tf_op jit(solution)/shard_map/ppermute | solution.py:383
  54.6 2.0 %collective-permute-start.15 = (bf16[272,128]{1,0:T(8,128)(2,1)S(1)}, bf16[272,128]{1,0:T(8,128)(2,1)S(1)}, u32[]{:S(2)}, u32[]{:S(2)}) collective-permute-start(bf16[272,128]{1,0:T(8,128)(2,1)S(1)} %add_convert_fusion.5), channel_id=1, source_target_pairs={{0,4},{1,5},{2,6},{3,7},{4,0},{5,1},{6,2},{7,3},{8,12},{9,13},{10,... | collective-permute-start | bytes 208904 | tf_op jit(solution)/shard_map/ppermute | solution.py:383
  56.7 1.5 %collective-permute-done.22 = bf16[256,128]{1,0:T(8,128)(2,1)S(1)} collective-permute-done((bf16[256,128]{1,0:T(8,128)(2,1)S(1)}, bf16[256,128]{1,0:T(8,128)(2,1)S(1)}, u32[]{:S(2)}, u32[]{:S(2)}) %collective-permute-start.22) | collective-permute-done | bytes 65568 | tf_op jit(solution)/shard_map/ppermute | solution.py:383
  58.2 1.3 %collective-permute-start.23 = (bf16[256,128]{1,0:T(8,128)(2,1)S(1)}, bf16[256,128]{1,0:T(8,128)(2,1)S(1)}, u32[]{:S(2)}, u32[]{:S(2)}) collective-permute-start(bf16[256,128]{1,0:T(8,128)(2,1)S(1)} %add_convert_fusion.8), channel_id=1, source_target_pairs={{0,16},{1,17},{2,18},{3,19},{4,20},{5,21},{6,22},{7,23},{8,24},{9,... | collective-permute-start | bytes 196616 | tf_op jit(solution)/shard_map/ppermute | solution.py:383
  59.5 0.4 collective-permute-done.15
  59.9 1.9 %collective-permute-start.16 = (bf16[272,128]{1,0:T(8,128)(2,1)S(1)}, bf16[272,128]{1,0:T(8,128)(2,1)S(1)}, u32[]{:S(2)}, u32[]{:S(2)}) collective-permute-start(bf16[272,128]{1,0:T(8,128)(2,1)S(1)} %add_convert_fusion.4), channel_id=1, source_target_pairs={{0,2},{1,3},{2,0},{3,1},{4,6},{5,7},{6,4},{7,5},{8,10},{9,11},{10,... | collective-permute-start | bytes 208904 | tf_op jit(solution)/shard_map/ppermute | solution.py:383
  61.8 0.7 collective-permute-done.23
  62.6 2.0 %collective-permute-start.24 = (bf16[256,128]{1,0:T(8,128)(2,1)S(1)}, bf16[256,128]{1,0:T(8,128)(2,1)S(1)}, u32[]{:S(2)}, u32[]{:S(2)}) collective-permute-start(bf16[256,128]{1,0:T(8,128)(2,1)S(1)} %add_convert_fusion.7), channel_id=1, source_target_pairs={{0,4},{1,5},{2,6},{3,7},{4,0},{5,1},{6,2},{7,3},{8,12},{9,13},{10,... | collective-permute-start | bytes 196616 | tf_op jit(solution)/shard_map/ppermute | solution.py:383
  64.6 0.7 collective-permute-start.25
  65.5 3.0 %collective-permute-done.24 = bf16[256,128]{1,0:T(8,128)(2,1)S(1)} collective-permute-done((bf16[256,128]{1,0:T(8,128)(2,1)S(1)}, bf16[256,128]{1,0:T(8,128)(2,1)S(1)}, u32[]{:S(2)}, u32[]{:S(2)}) %collective-permute-start.24) | collective-permute-done | bytes 65568 | tf_op jit(solution)/shard_map/ppermute | solution.py:383
  68.6 1.8 %collective-permute-done.17 = bf16[544,128]{1,0:T(8,128)(2,1)S(1)} collective-permute-done((bf16[544,128]{1,0:T(8,128)(2,1)S(1)}, bf16[544,128]{1,0:T(8,128)(2,1)S(1)}, u32[]{:S(2)}, u32[]{:S(2)}) %collective-permute-start.17) | collective-permute-done | bytes 139296 | tf_op jit(solution)/shard_map/ppermute | solution.py:383
  70.5 1.1 %collective-permute-start.18 = (bf16[1088,128]{1,0:T(8,128)(2,1)S(1)}, bf16[1088,128]{1,0:T(8,128)(2,1)S(1)}, u32[]{:S(2)}, u32[]{:S(2)}) collective-permute-start(bf16[1088,128]{1,0:T(8,128)(2,1)S(1)} %pad_maximum_fusion.1.refs_0_.refs_2_), channel_id=1, source_target_pairs={{0,1},{1,0},{2,3},{3,2},{4,5},{5,4},{6,7},{7,6},{8,9},{9,8},{10,11... | collective-permute-start | bytes 835592 | tf_op jit(solution)/shard_map/ppermute | solution.py:383
  71.6 2.0 %collective-permute-done.26 = bf16[512,128]{1,0:T(8,128)(2,1)S(1)} collective-permute-done((bf16[512,128]{1,0:T(8,128)(2,1)S(1)}, bf16[512,128]{1,0:T(8,128)(2,1)S(1)}, u32[]{:S(2)}, u32[]{:S(2)}) %collective-permute-start.26) | collective-permute-done | bytes 131104 | tf_op jit(solution)/shard_map/ppermute | solution.py:383
  73.7 2.9 %collective-permute-start.27 = (bf16[1024,128]{1,0:T(8,128)(2,1)S(1)}, bf16[1024,128]{1,0:T(8,128)(2,1)S(1)}, u32[]{:S(2)}, u32[]{:S(2)}) collective-permute-start(bf16[1024,128]{1,0:T(8,128)(2,1)S(1)} %constant_dynamic-update-slice_fusion.refs_1_), channel_id=1, source_target_pairs={{0,2},{1,3},{2,0},{3,1},{4,6},{5,7},{6,4},{7,5},{8,10},{9,11},{10,... | collective-permute-start | bytes 786440 | tf_op jit(solution)/shard_map/ppermute | solution.py:383
  76.5 2.8 %shard_map.130 = bf16[2,128,512]{2,1,0:T(8,128)(2,1)} custom-call(s32[11]{0:T(128)S(1)} %stack.62.bits, bf16[2,4,128,128]{3,2,1,0:T(8,128)(2,1)S(1)} %get-tuple-element.70.dconv, bf16[256,128]{1,0:T(8,128)(2,1)S(1)} %collective-permute-done.13.x_got, bf16[128,128]{1,0:T(8,128)(2,1)S(1)} %slice.170.z_got, ...), custom_call_target="tpu_custom_call" | custom-call | tf_op jit(solution)/shard_map/pallas_call | solution.py:344
  79.4 2.0 %shard_map.131 = (f32[512,512]{1,0:T(8,128)}, f32[512,512]{1,0:T(8,128)}, f32[512,512]{1,0:T(8,128)}, f32[512,512]{1,0:T(8,128)}) custom-call(s32[11]{0:T(128)S(1)} %stack.62.bits, bf16[1088,128]{1,0:T(8,128)(2,1)S(1)} %pad_maximum_fusion.1.refs_0_.refs_2_, bf16[1024,128]{1,0:T(8,128)(2,1)S(1)} %constant_dynamic-update-slice_fusion.refs_1_, ...), custom_call_target="tpu_custom_call" | custom-call | tf_op jit(solution)/shard_map/pallas_call | solution.py:344
  81.4 2.1 %collective-permute-done.27.refs_1_ = bf16[1024,128]{1,0:T(8,128)(2,1)S(1)} collective-permute-done((bf16[1024,128]{1,0:T(8,128)(2,1)S(1)}, bf16[1024,128]{1,0:T(8,128)(2,1)S(1)}, u32[]{:S(2)}, u32[]{:S(2)}) %collective-permute-start.27) | collective-permute-done | bytes 262176 | tf_op jit(solution)/shard_map/ppermute | solution.py:383
  83.5 0.5 collective-permute-start.31
  84.0 1.6 %shard_map.132 = (f32[512,512]{1,0:T(8,128)}, f32[512,512]{1,0:T(8,128)}, f32[512,512]{1,0:T(8,128)}, f32[512,512]{1,0:T(8,128)}) custom-call(s32[11]{0:T(128)S(1)} %stack.62.bits, bf16[1088,128]{1,0:T(8,128)(2,1)S(1)} %collective-permute-done.18.refs_0_.refs_3_, ...), custom_call_target="tpu_custom_call", output_to_operand_aliasing={{0}: (3, {}), {1}: (4, {}), {2}: (5, {}), {3}: (6, {})} | custom-call | tf_op jit(solution)/shard_map/pallas_call | solution.py:344
  85.6 2.2 %shard_map.133 = (f32[512,512]{1,0:T(8,128)}, f32[512,512]{1,0:T(8,128)}, f32[512,512]{1,0:T(8,128)}, f32[512,512]{1,0:T(8,128)}, f32[31,512]{1,0:T(8,128)}) custom-call(s32[11]{0:T(128)S(1)} %stack.62.bits, bf16[1088,128]{1,0:T(8,128)(2,1)S(1)} %collective-permute-done.30.refs_0_.refs_5_, ...), custom_call_target="tpu_custom_call", output_to_operand_aliasing={{0}: (7, {}), {1}: (8, {}), {2}: (9, {}), {3}: (10, {})} | custom-call | tf_op jit(solution)/shard_map/pallas_call | solution.py:344
  (60 shorter events, 2.6 us)
Async XLA Ops:
  1.7 5.2 %collective-permute-start = (bf16[2,32,512]{2,1,0:T(8,128)(2,1)S(1)}, bf16[2,32,512]{2,1,0:T(8,128)(2,1)S(1)}, u32[]{:S(2)}, u32[]{:S(2)}) collective-permute-start(bf16[2,32,512]{2,1,0:T(8,128)(2,1)S(1)} %get-tuple-element.96), channel_id=1, source_target_pairs={{0,8},{1,9},{2,10},{3,11},{4,12},{5,13},{6,14},{7,15},{8,0},{9,1},... | collective-permute-start | bytes 196616 | tf_op jit(solution)/shard_map/ppermute | solution.py:383
  2.2 5.3 %collective-permute-start.1 = (bf16[2,32,512]{2,1,0:T(8,128)(2,1)S(1)}, bf16[2,32,512]{2,1,0:T(8,128)(2,1)S(1)}, u32[]{:S(2)}, u32[]{:S(2)}) collective-permute-start(bf16[2,32,512]{2,1,0:T(8,128)(2,1)S(1)} %get-tuple-element.98), channel_id=1, source_target_pairs={{0,16},{1,17},{2,18},{3,19},{4,20},{5,21},{6,22},{7,23},{8,24},{9,... | collective-permute-start | bytes 196616 | tf_op jit(solution)/shard_map/ppermute | solution.py:383
  4.8 4.0 %collective-permute-start.2 = (bf16[2,32,512]{2,1,0:T(8,128)(2,1)S(1)}, bf16[2,32,512]{2,1,0:T(8,128)(2,1)S(1)}, u32[]{:S(2)}, u32[]{:S(2)}) collective-permute-start(bf16[2,32,512]{2,1,0:T(8,128)(2,1)S(1)} %get-tuple-element.95), channel_id=1, source_target_pairs={{0,24},{1,25},{2,26},{3,27},{4,28},{5,29},{6,30},{7,31},{8,16},{9,... | collective-permute-start | bytes 196616 | tf_op jit(solution)/shard_map/ppermute | solution.py:383
  4.8 5.4 %copy-start = (bf16[2,128,512]{2,1,0:T(8,128)(2,1)S(1)}, bf16[2,128,512]{2,1,0:T(8,128)(2,1)}, u32[]{:S(2)}) copy-start(bf16[2,128,512]{2,1,0:T(8,128)(2,1)} %cot.1) | copy-start | bytes 786436
  4.8 9.9 %copy-start.3 = (f32[31,512]{1,0:T(8,128)S(1)}, f32[31,512]{1,0:T(8,128)}, u32[]{:S(2)}) copy-start(f32[31,512]{1,0:T(8,128)} %kern.3) | copy-start | bytes 190468
  9.4 5.3 %collective-permute-start.3 = (bf16[4,2,16,512]{3,2,1,0:T(8,128)(2,1)S(1)}, bf16[4,2,16,512]{3,2,1,0:T(8,128)(2,1)S(1)}, u32[]{:S(2)}, u32[]{:S(2)}) collective-permute-start(bf16[4,2,16,512]{3,2,1,0:T(8,128)(2,1)S(1)} %get-tuple-element.51), channel_id=1, source_target_pairs={{0,8},{1,9},{2,10},{3,11},{4,12},{5,13},{6,14},{7,15},{8,0},{9,1},... | collective-permute-start | bytes 393224 | tf_op jit(solution)/shard_map/ppermute | solution.py:383
  9.6 5.1 %collective-permute-start.4 = (bf16[4,2,16,512]{3,2,1,0:T(8,128)(2,1)S(1)}, bf16[4,2,16,512]{3,2,1,0:T(8,128)(2,1)S(1)}, u32[]{:S(2)}, u32[]{:S(2)}) collective-permute-start(bf16[4,2,16,512]{3,2,1,0:T(8,128)(2,1)S(1)} %get-tuple-element.52), channel_id=1, source_target_pairs={{8,24},{9,25},{10,26},{11,27},{12,28},{13,29},{14,30},{15,31},{24,... | collective-permute-start | bytes 393224 | tf_op jit(solution)/shard_map/ppermute | solution.py:383
  10.3 6.9 %collective-permute-start.5 = (bf16[2,32,512]{2,1,0:T(8,128)(2,1)S(1)}, bf16[2,32,512]{2,1,0:T(8,128)(2,1)S(1)}, u32[]{:S(2)}, u32[]{:S(2)}) collective-permute-start(bf16[2,32,512]{2,1,0:T(8,128)(2,1)S(1)} %get-tuple-element.93), channel_id=1, source_target_pairs={{0,8},{1,9},{2,10},{3,11},{4,12},{5,13},{6,14},{7,15},{8,0},{9,1},... | collective-permute-start | bytes 196616 | tf_op jit(solution)/shard_map/ppermute | solution.py:383
  13.0 4.3 %collective-permute-start.6 = (bf16[2,32,512]{2,1,0:T(8,128)(2,1)S(1)}, bf16[2,32,512]{2,1,0:T(8,128)(2,1)S(1)}, u32[]{:S(2)}, u32[]{:S(2)}) collective-permute-start(bf16[2,32,512]{2,1,0:T(8,128)(2,1)S(1)} %get-tuple-element.92), channel_id=1, source_target_pairs={{0,16},{1,17},{2,18},{3,19},{4,20},{5,21},{6,22},{7,23},{8,24},{9,... | collective-permute-start | bytes 196616 | tf_op jit(solution)/shard_map/ppermute | solution.py:383
  14.7 4.0 %collective-permute-start.7 = (bf16[2,32,512]{2,1,0:T(8,128)(2,1)S(1)}, bf16[2,32,512]{2,1,0:T(8,128)(2,1)S(1)}, u32[]{:S(2)}, u32[]{:S(2)}) collective-permute-start(bf16[2,32,512]{2,1,0:T(8,128)(2,1)S(1)} %get-tuple-element.91), channel_id=1, source_target_pairs={{0,24},{1,25},{2,26},{3,27},{4,28},{5,29},{6,30},{7,31},{8,16},{9,... | collective-permute-start | bytes 196616 | tf_op jit(solution)/shard_map/ppermute | solution.py:383
  27.8 0.8 copy-start.1
  28.6 0.8 copy-start.4
  29.4 16.1 %copy-start.2 = (bf16[2048,128]{1,0:T(8,128)(2,1)S(1)}, bf16[2048,128]{1,0:T(8,128)(2,1)}, u32[]{:S(2)}) copy-start(bf16[2048,128]{1,0:T(8,128)(2,1)} %copy-done.1) | copy-start | bytes 1572868
  29.4 2.7 %collective-permute-start.10 = (bf16[2176,128]{1,0:T(8,128)(2,1)}, bf16[2176,128]{1,0:T(8,128)(2,1)S(1)}, u32[]{:S(2)}, u32[]{:S(2)}) collective-permute-start(bf16[2176,128]{1,0:T(8,128)(2,1)} %get-tuple-element.60), channel_id=1, source_target_pairs={{0,8},{1,9},{2,10},{3,11},{4,12},{5,13},{6,14},{7,15},{8,0},{9,1},... | collective-permute-start | bytes 1671176 | tf_op jit(solution)/shard_map/ppermute | solution.py:383
  29.5 2.5 %collective-permute-start.8 = (bf16[1024,128]{1,0:T(8,128)(2,1)S(1)}, bf16[1024,128]{1,0:T(8,128)(2,1)S(1)}, u32[]{:S(2)}, u32[]{:S(2)}) collective-permute-start(bf16[1024,128]{1,0:T(8,128)(2,1)S(1)} %get-tuple-element.58), channel_id=1, source_target_pairs={{0,8},{1,9},{2,10},{3,11},{4,12},{5,13},{6,14},{7,15},{8,0},{9,1},... | collective-permute-start | bytes 786440 | tf_op jit(solution)/shard_map/ppermute | solution.py:383
  29.9 5.5 %collective-permute-start.19 = (bf16[2048,128]{1,0:T(8,128)(2,1)}, bf16[2048,128]{1,0:T(8,128)(2,1)S(1)}, u32[]{:S(2)}, u32[]{:S(2)}) collective-permute-start(bf16[2048,128]{1,0:T(8,128)(2,1)} %copy-done.4), channel_id=1, source_target_pairs={{0,8},{1,9},{2,10},{3,11},{4,12},{5,13},{6,14},{7,15},{8,0},{9,1},... | collective-permute-start | bytes 1572872 | tf_op jit(solution)/shard_map/ppermute | solution.py:383
  32.2 9.5 %collective-permute-start.11 = (bf16[1088,128]{1,0:T(8,128)(2,1)S(1)}, bf16[1088,128]{1,0:T(8,128)(2,1)S(1)}, u32[]{:S(2)}, u32[]{:S(2)}) collective-permute-start(bf16[1088,128]{1,0:T(8,128)(2,1)S(1)} %add_convert_fusion), channel_id=1, source_target_pairs={{0,1},{1,0},{2,3},{3,2},{4,5},{5,4},{6,7},{7,6},{8,9},{9,8},{10,11... | collective-permute-start | bytes 835592 | tf_op jit(solution)/shard_map/ppermute | solution.py:383
  34.7 8.2 %collective-permute-start.9 = (bf16[1024,128]{1,0:T(8,128)(2,1)S(1)}, bf16[1024,128]{1,0:T(8,128)(2,1)S(1)}, u32[]{:S(2)}, u32[]{:S(2)}) collective-permute-start(bf16[1024,128]{1,0:T(8,128)(2,1)S(1)} %pad_maximum_fusion.2), channel_id=1, source_target_pairs={{0,16},{1,17},{2,18},{3,19},{4,20},{5,21},{6,22},{7,23},{8,24},{9,... | collective-permute-start | bytes 786440 | tf_op jit(solution)/shard_map/ppermute | solution.py:383
  36.4 9.1 %collective-permute-start.20 = (bf16[1024,128]{1,0:T(8,128)(2,1)S(1)}, bf16[1024,128]{1,0:T(8,128)(2,1)S(1)}, u32[]{:S(2)}, u32[]{:S(2)}) collective-permute-start(bf16[1024,128]{1,0:T(8,128)(2,1)S(1)} %add_convert_fusion.1), channel_id=1, source_target_pairs={{0,2},{1,3},{2,0},{3,1},{4,6},{5,7},{6,4},{7,5},{8,10},{9,11},{10,... | collective-permute-start | bytes 786440 | tf_op jit(solution)/shard_map/ppermute | solution.py:383
  41.8 7.3 %collective-permute-start.12 = (bf16[544,128]{1,0:T(8,128)(2,1)S(1)}, bf16[544,128]{1,0:T(8,128)(2,1)S(1)}, u32[]{:S(2)}, u32[]{:S(2)}) collective-permute-start(bf16[544,128]{1,0:T(8,128)(2,1)S(1)} %add_convert_fusion.2), channel_id=1, source_target_pairs={{0,16},{1,17},{2,18},{3,19},{4,20},{5,21},{6,22},{7,23},{8,24},{9,... | collective-permute-start | bytes 417800 | tf_op jit(solution)/shard_map/ppermute | solution.py:383
  44.2 4.9 %collective-permute-start.13 = (bf16[256,128]{1,0:T(8,128)(2,1)S(1)}, bf16[256,128]{1,0:T(8,128)(2,1)S(1)}, u32[]{:S(2)}, u32[]{:S(2)}) collective-permute-start(bf16[256,128]{1,0:T(8,128)(2,1)S(1)} %pad_maximum_fusion.6), channel_id=1, source_target_pairs={{0,1},{1,0},{2,3},{3,2},{4,5},{5,4},{6,7},{7,6},{8,9},{9,8},{10,11... | collective-permute-start | bytes 196616 | tf_op jit(solution)/shard_map/ppermute | solution.py:383
  45.5 5.3 %collective-permute-start.21 = (bf16[512,128]{1,0:T(8,128)(2,1)S(1)}, bf16[512,128]{1,0:T(8,128)(2,1)S(1)}, u32[]{:S(2)}, u32[]{:S(2)}) collective-permute-start(bf16[512,128]{1,0:T(8,128)(2,1)S(1)} %add_convert_fusion.3), channel_id=1, source_target_pairs={{0,1},{1,0},{2,3},{3,2},{4,5},{5,4},{6,7},{7,6},{8,9},{9,8},{10,11... | collective-permute-start | bytes 393224 | tf_op jit(solution)/shard_map/ppermute | solution.py:383
  49.2 5.4 %collective-permute-start.14 = (bf16[400,128]{1,0:T(8,128)(2,1)S(1)}, bf16[400,128]{1,0:T(8,128)(2,1)S(1)}, u32[]{:S(2)}, u32[]{:S(2)}) collective-permute-start(bf16[400,128]{1,0:T(8,128)(2,1)S(1)} %pad_maximum_fusion.5), channel_id=1, source_target_pairs={{0,2},{1,3},{2,0},{3,1},{4,6},{5,7},{6,4},{7,5},{8,10},{9,11},{10,... | collective-permute-start | bytes 307208 | tf_op jit(solution)/shard_map/ppermute | solution.py:383
  50.9 7.3 %collective-permute-start.22 = (bf16[256,128]{1,0:T(8,128)(2,1)S(1)}, bf16[256,128]{1,0:T(8,128)(2,1)S(1)}, u32[]{:S(2)}, u32[]{:S(2)}) collective-permute-start(bf16[256,128]{1,0:T(8,128)(2,1)S(1)} %add_convert_fusion.9), channel_id=1, source_target_pairs={{0,4},{1,5},{2,6},{3,7},{4,0},{5,1},{6,2},{7,3},{8,12},{9,13},{10,... | collective-permute-start | bytes 196616 | tf_op jit(solution)/shard_map/ppermute | solution.py:383
  54.6 5.3 %collective-permute-start.15 = (bf16[272,128]{1,0:T(8,128)(2,1)S(1)}, bf16[272,128]{1,0:T(8,128)(2,1)S(1)}, u32[]{:S(2)}, u32[]{:S(2)}) collective-permute-start(bf16[272,128]{1,0:T(8,128)(2,1)S(1)} %add_convert_fusion.5), channel_id=1, source_target_pairs={{0,4},{1,5},{2,6},{3,7},{4,0},{5,1},{6,2},{7,3},{8,12},{9,13},{10,... | collective-permute-start | bytes 208904 | tf_op jit(solution)/shard_map/ppermute | solution.py:383
  58.2 4.3 %collective-permute-start.23 = (bf16[256,128]{1,0:T(8,128)(2,1)S(1)}, bf16[256,128]{1,0:T(8,128)(2,1)S(1)}, u32[]{:S(2)}, u32[]{:S(2)}) collective-permute-start(bf16[256,128]{1,0:T(8,128)(2,1)S(1)} %add_convert_fusion.8), channel_id=1, source_target_pairs={{0,16},{1,17},{2,18},{3,19},{4,20},{5,21},{6,22},{7,23},{8,24},{9,... | collective-permute-start | bytes 196616 | tf_op jit(solution)/shard_map/ppermute | solution.py:383
  59.9 5.3 %collective-permute-start.16 = (bf16[272,128]{1,0:T(8,128)(2,1)S(1)}, bf16[272,128]{1,0:T(8,128)(2,1)S(1)}, u32[]{:S(2)}, u32[]{:S(2)}) collective-permute-start(bf16[272,128]{1,0:T(8,128)(2,1)S(1)} %add_convert_fusion.4), channel_id=1, source_target_pairs={{0,2},{1,3},{2,0},{3,1},{4,6},{5,7},{6,4},{7,5},{8,10},{9,11},{10,... | collective-permute-start | bytes 208904 | tf_op jit(solution)/shard_map/ppermute | solution.py:383
  62.6 5.9 %collective-permute-start.24 = (bf16[256,128]{1,0:T(8,128)(2,1)S(1)}, bf16[256,128]{1,0:T(8,128)(2,1)S(1)}, u32[]{:S(2)}, u32[]{:S(2)}) collective-permute-start(bf16[256,128]{1,0:T(8,128)(2,1)S(1)} %add_convert_fusion.7), channel_id=1, source_target_pairs={{0,4},{1,5},{2,6},{3,7},{4,0},{5,1},{6,2},{7,3},{8,12},{9,13},{10,... | collective-permute-start | bytes 196616 | tf_op jit(solution)/shard_map/ppermute | solution.py:383
  64.6 3.9 %collective-permute-start.25 = (bf16[128,128]{1,0:T(8,128)(2,1)S(1)}, bf16[128,128]{1,0:T(8,128)(2,1)S(1)}, u32[]{:S(2)}, u32[]{:S(2)}) collective-permute-start(bf16[128,128]{1,0:T(8,128)(2,1)S(1)} %constant_dynamic-slice_fusion), channel_id=1, source_target_pairs={{2,4},{3,5},{10,12},{11,13},{18,20},{19,21},{26,28},{27,29},{4,2},... | collective-permute-start | bytes 98312 | tf_op jit(solution)/shard_map/ppermute | solution.py:383
  65.3 5.1 %collective-permute-start.17 = (bf16[544,128]{1,0:T(8,128)(2,1)S(1)}, bf16[544,128]{1,0:T(8,128)(2,1)S(1)}, u32[]{:S(2)}, u32[]{:S(2)}) collective-permute-start(bf16[544,128]{1,0:T(8,128)(2,1)S(1)} %pad_maximum_fusion.3), channel_id=1, source_target_pairs={{0,16},{1,17},{2,18},{3,19},{4,20},{5,21},{6,22},{7,23},{8,24},{9,... | collective-permute-start | bytes 417800 | tf_op jit(solution)/shard_map/ppermute | solution.py:383
  68.5 5.0 %collective-permute-start.26 = (bf16[512,128]{1,0:T(8,128)(2,1)S(1)}, bf16[512,128]{1,0:T(8,128)(2,1)S(1)}, u32[]{:S(2)}, u32[]{:S(2)}) collective-permute-start(bf16[512,128]{1,0:T(8,128)(2,1)S(1)} %pad_maximum_fusion.4), channel_id=1, source_target_pairs={{0,1},{1,0},{2,3},{3,2},{4,5},{5,4},{6,7},{7,6},{8,9},{9,8},{10,11... | collective-permute-start | bytes 393224 | tf_op jit(solution)/shard_map/ppermute | solution.py:383
  70.4 8.9 %collective-permute-start.28 = (bf16[1088,128]{1,0:T(8,128)(2,1)S(1)}, bf16[1088,128]{1,0:T(8,128)(2,1)S(1)}, u32[]{:S(2)}, u32[]{:S(2)}) collective-permute-start(bf16[1088,128]{1,0:T(8,128)(2,1)S(1)} %pad_maximum_fusion.1.refs_0_.refs_2_), channel_id=1, source_target_pairs={{0,8},{1,9},{2,10},{3,11},{4,12},{5,13},{6,14},{7,15},{8,0},{9,1},... | collective-permute-start | bytes 835592 | tf_op jit(solution)/shard_map/ppermute | solution.py:383
  70.5 12.9 %collective-permute-start.18 = (bf16[1088,128]{1,0:T(8,128)(2,1)S(1)}, bf16[1088,128]{1,0:T(8,128)(2,1)S(1)}, u32[]{:S(2)}, u32[]{:S(2)}) collective-permute-start(bf16[1088,128]{1,0:T(8,128)(2,1)S(1)} %pad_maximum_fusion.1.refs_0_.refs_2_), channel_id=1, source_target_pairs={{0,1},{1,0},{2,3},{3,2},{4,5},{5,4},{6,7},{7,6},{8,9},{9,8},{10,11... | collective-permute-start | bytes 835592 | tf_op jit(solution)/shard_map/ppermute | solution.py:383
  73.6 5.8 %collective-permute-start.29 = (bf16[1024,128]{1,0:T(8,128)(2,1)S(1)}, bf16[1024,128]{1,0:T(8,128)(2,1)S(1)}, u32[]{:S(2)}, u32[]{:S(2)}) collective-permute-start(bf16[1024,128]{1,0:T(8,128)(2,1)S(1)} %constant_dynamic-update-slice_fusion.refs_1_), channel_id=1, source_target_pairs={{0,8},{1,9},{2,10},{3,11},{4,12},{5,13},{6,14},{7,15},{8,0},{9,1},... | collective-permute-start | bytes 786440 | tf_op jit(solution)/shard_map/ppermute | solution.py:383
  73.7 9.8 %collective-permute-start.27 = (bf16[1024,128]{1,0:T(8,128)(2,1)S(1)}, bf16[1024,128]{1,0:T(8,128)(2,1)S(1)}, u32[]{:S(2)}, u32[]{:S(2)}) collective-permute-start(bf16[1024,128]{1,0:T(8,128)(2,1)S(1)} %constant_dynamic-update-slice_fusion.refs_1_), channel_id=1, source_target_pairs={{0,2},{1,3},{2,0},{3,1},{4,6},{5,7},{6,4},{7,5},{8,10},{9,11},{10,... | collective-permute-start | bytes 786440 | tf_op jit(solution)/shard_map/ppermute | solution.py:383
  83.4 2.1 %collective-permute-start.30 = (bf16[1088,128]{1,0:T(8,128)(2,1)S(1)}, bf16[1088,128]{1,0:T(8,128)(2,1)S(1)}, u32[]{:S(2)}, u32[]{:S(2)}) collective-permute-start(bf16[1088,128]{1,0:T(8,128)(2,1)S(1)} %collective-permute-done.18.refs_0_.refs_3_), channel_id=1, source_target_pairs={{0,8},{1,9},{2,10},{3,11},{4,12},{5,13},{6,14},{7,15},{8,0},{9,1},... | collective-permute-start | bytes 835592 | tf_op jit(solution)/shard_map/ppermute | solution.py:383
  83.5 2.1 %collective-permute-start.31 = (bf16[1024,128]{1,0:T(8,128)(2,1)S(1)}, bf16[1024,128]{1,0:T(8,128)(2,1)S(1)}, u32[]{:S(2)}, u32[]{:S(2)}) collective-permute-start(bf16[1024,128]{1,0:T(8,128)(2,1)S(1)} %collective-permute-done.27.refs_1_), channel_id=1, source_target_pairs={{0,8},{1,9},{2,10},{3,11},{4,12},{5,13},{6,14},{7,15},{8,0},{9,1},... | collective-permute-start | bytes 786440 | tf_op jit(solution)/shard_map/ppermute | solution.py:383

commit v16 on v15

--- a/solution.py
+++ b/solution.py
@@ -401,7 +401,7 @@
     f, c = scattered(frames), scattered(cotangent)
     weights = jnp.stack([w_query, w_key, w_value, w_out])
     edge = shape((groups, count, HALO, width), BF)
-    near, side = call(functools.partial(edge_kernel, sub), (edge, edge), [], 4, bits, *f)
+    near, side = call(functools.partial(edge_kernel, sub), (edge, edge), [], 8, bits, *f)
     near, side, weights = lax.optimization_barrier((near, side, weights))
     near = swap(near, over_core)
     side = permute(
@@ -425,7 +425,7 @@
     placed, conv, acted = call(
         functools.partial(conv_kernel, (groups, count, sub, width)),
         (moved, shape((rows, width), F32), shape((rows, width), BF)),
-        [], 4, bits, *f, near, side, kernel,
+        [], 8, bits, *f, near, side, kernel,
     )
     a_keep, b_keep, a_send, b_send, back_keep, back_send = call(
         functools.partial(main_kernel, (groups, count, sub, width, factor)),
@@ -437,7 +437,7 @@
             big, big, big, big, wide,
             pltpu.VMEM((32 * cols + HALO, LANES), F32),
         ],
-        14, bits, placed, conv, acted, *c, near, side, weights,
+        24, bits, placed, conv, acted, *c, near, side, weights,
     )
 
     lines = [2**i for i in range(1, blocks.bit_length() - 1)]
@@ -445,9 +445,12 @@
     def after(x, y):
         return lax.optimization_barrier((x, y))[0]
 
+    def kept(parts, n):
+        return lax.optimization_barrier(total(*(t[:n] for t in parts)))
+
     def halved(parts, mask):
         n = parts[0].shape[0] // 2
-        return [t[:n] for t in parts] + [swap(total(*(t[n:] for t in parts)), mask)]
+        return [kept(parts, n), swap(total(*(t[n:] for t in parts)), mask)]
 
     def exchanged(parts, masks):
         mine = total(*parts)
@@ -464,12 +467,12 @@
     a = halved(a, over_x)
     b = halved(b, lines[0])
     y_got = swap(jnp.concatenate([back_keep[unit:], core_got[unit:]]), over_y)
-    y_got = after(y_got, a[-1])
+    y_got = after(y_got, b[-1])
     edge = flat(count * cols * HALO)
     layer_out, dconv, *edges = call(
         functools.partial(home_kernel, (count, sub, cols)),
         (shape(frames.shape, BF), shape((count, cols, length, LANES), BF), edge, edge),
-        [], 4, bits, back_keep, core_got, y_got,
+        [], 8, bits, back_keep, core_got, y_got,
     )
     x_got = swap(jnp.concatenate(edges), over_x)
     n_edge = edge.shape[0]
@@ -477,7 +480,7 @@
     a = halved(a, over_y)
     b = halved(b, over_x)
     got = swap(jnp.concatenate([total(*(t[span:] for t in a)), passed]), lines[0])
-    a, z_got = [t[:span] for t in a] + [got[:span]], got[span:]
+    a, z_got = [kept(a, span), got[:span]], got[span:]
     b = halved(b, lines[1])
     a = exchanged(a, lines[1:])
     b = exchanged(b, [over_y] + lines[2:])
@@ -504,7 +507,7 @@
             functools.partial(final_kernel, (kinds, not grads, bool(taps), width, norm)),
             (square,) * 4 + (shape((31, width), F32),) * bool(taps),
             scratch + [pltpu.VMEM((16, HALO, LANES), F32)] * bool(taps),
-            5, bits, *parts, *taps, *grads, hbm=range(first, first + len(grads)),
+            10, bits, *parts, *taps, *grads, hbm=range(first, first + len(grads)),
             hbm_outs=range(4), aliases={first + i: i for i in range(len(grads))},
         )
 
@@ -512,7 +515,7 @@
     a_other, b_other = swap(a, over_core), swap(b, over_core)
     (frame_grad,) = call(
         functools.partial(frame_kernel, (count, cols, length)),
-        (shape(frames.shape, BF),), [], 4,
+        (shape(frames.shape, BF),), [], 8,
         bits, after(dconv, a), x_got, z_got, other_got, cotangent, kernel,
     )
     grads = final(((1, 0, 0), (1, 1, 0), (0, 0, 0), (0, 1, 0)), (a, b, a_other, b_other), ())

time: 88 us -> 87.1 us (0.990)
  starting transfers between devices: 33.9 us -> 39 us
  waiting for transfers between devices: 24.7 us -> 21.8 us
  local copies, waits for them, and re-layouts: 2.74 us -> 1.15 us
    ppermute x32, starting transfers between devices: 33.9 us -> 39 us  [permute(): return lax.ppermute(x, ('mic', 'tm'), pairs)]
    ppermute x32, waiting for transfers between devices: 24.7 us -> 21.8 us  [permute(): return lax.ppermute(x, ('mic', 'tm'), pairs)]
    unnamed x11 -> x5, local copies, waits for them, and re-layouts: 1.61 us -> 0.02 us
  transfers between devices with their start and end apart: 32 -> 32, of which waited for: 16 -> 17; matrix products, arithmetic and copies ran while one was open for 4% -> 3% of each run, Pallas kernels for 12% -> 12%
where the time goes in v16:
time: 87.1 us; the launch traced here: 86.8 us
  starting transfers between devices  39 us (45%)
  waiting for transfers between devices  21.8 us (25%)
  Pallas kernels  21.4 us (25%)
  other arithmetic  2.5 us (3%)
  local copies, waits for them, and re-layouts  1.15 us (1%)
  between operations  1.04 us (1%)
    ppermute x32, starting transfers between devices, permute(): return lax.ppermute(x, ('mic', 'tm'), pairs)  39 us
    ppermute x32, waiting for transfers between devices, permute(): return lax.ppermute(x, ('mic', 'tm'), pairs)  21.8 us
    pallas_call x8, Pallas kernels, call(): pl.pallas_call(body, out_shape=outs, in_specs=[pl.BlockSpec(memory_space=...  21.4 us
    another operation x1, other arithmetic, shards(): weights = jnp.stack([w_query, w_key, w_value, w_out])  1.82 us
  transfers between devices with their start and end apart: 32, of which 17 were waited for; matrix products, arithmetic and copies ran while one was open for 3% of the time, Pallas kernels for 12%

profile of v16, /device:TPU:0, one launch (start us, length us, event | category | flops | bytes accessed | tf_op | source)
XLA Modules:
  0.0 86.8 jit_solution(14273355996627693930)
XLA Ops:
  0.7 1.0 %constant_dynamic-slice_fusion.5 = (bf16[2,32,512]{2,1,0:T(8,128)(2,1)S(1)}, bf16[2,32,512]{2,1,0:T(8,128)(2,1)S(1)}, bf16[2,32,512]{2,1,0:T(8,128)(2,1)S(1)}, bf16[2,32,512]{2,1,0:T(8,128)(2,1)S(1)}) fusion(bf16[2,128,512]{2,1,0:T(8,128)(2,1)} %param.7, s32[]{:T(128)S(6)} %select_n.100, s32[]{:T(128)S(6)} %select_n.98, s32[]{:T(128)S(6)} %select_n.97, ...), kind=kLoop, calls=%fused_computation.30 | loop fusion | bytes 524304 | tf_op jit(solution)/shard_map/dynamic_slice | solution.py:394
  1.7 0.5 collective-permute-start
  2.2 2.6 %collective-permute-start.1 = (bf16[2,32,512]{2,1,0:T(8,128)(2,1)S(1)}, bf16[2,32,512]{2,1,0:T(8,128)(2,1)S(1)}, u32[]{:S(2)}, u32[]{:S(2)}) collective-permute-start(bf16[2,32,512]{2,1,0:T(8,128)(2,1)S(1)} %get-tuple-element.110), channel_id=1, source_target_pairs={{0,16},{1,17},{2,18},{3,19},{4,20},{5,21},{6,22},{7,23},{8,24},{9,... | collective-permute-start | bytes 196616 | tf_op jit(solution)/shard_map/ppermute | solution.py:383
  4.8 1.8 %pad_maximum_fusion.weights = bf16[4,512,512]{2,1,0:T(8,128)(2,1)S(1)} fusion(bf16[1,512,512]{2,1,0:T(8,128)(2,1)} %bitcast.15, bf16[1,512,512]{2,1,0:T(8,128)(2,1)} %bitcast.16, bf16[1,512,512]{2,1,0:T(8,128)(2,1)} %bitcast.17, bf16[1,512,512]{2,1,0:T(8,128)(2,1)} %bitcast.18), kind=kLoop, calls=%fused_computation | loop fusion | flops 3145728 | bytes 4194304 | tf_op jit(solution)/shard_map/stack | solution.py:402
  6.9 0.6 collective-permute-done.1.f2
  7.5 1.4 %collective-permute-done.2.f3 = bf16[2,32,512]{2,1,0:T(8,128)(2,1)S(1)} collective-permute-done((bf16[2,32,512]{2,1,0:T(8,128)(2,1)S(1)}, bf16[2,32,512]{2,1,0:T(8,128)(2,1)S(1)}, u32[]{:S(2)}, u32[]{:S(2)}) %collective-permute-start.2) | collective-permute-done | bytes 65568 | tf_op jit(solution)/shard_map/ppermute | solution.py:383
  8.8 0.6 shard_map.126
  9.6 0.7 collective-permute-start.4
  10.3 2.7 %collective-permute-start.5 = (bf16[2,32,512]{2,1,0:T(8,128)(2,1)S(1)}, bf16[2,32,512]{2,1,0:T(8,128)(2,1)S(1)}, u32[]{:S(2)}, u32[]{:S(2)}) collective-permute-start(bf16[2,32,512]{2,1,0:T(8,128)(2,1)S(1)} %get-tuple-element.105), channel_id=1, source_target_pairs={{0,8},{1,9},{2,10},{3,11},{4,12},{5,13},{6,14},{7,15},{8,0},{9,1},... | collective-permute-start | bytes 196616 | tf_op jit(solution)/shard_map/ppermute | solution.py:383
  13.0 1.6 %collective-permute-start.6 = (bf16[2,32,512]{2,1,0:T(8,128)(2,1)S(1)}, bf16[2,32,512]{2,1,0:T(8,128)(2,1)S(1)}, u32[]{:S(2)}, u32[]{:S(2)}) collective-permute-start(bf16[2,32,512]{2,1,0:T(8,128)(2,1)S(1)} %get-tuple-element.104), channel_id=1, source_target_pairs={{0,16},{1,17},{2,18},{3,19},{4,20},{5,21},{6,22},{7,23},{8,24},{9,... | collective-permute-start | bytes 196616 | tf_op jit(solution)/shard_map/ppermute | solution.py:383
  14.7 2.5 %shard_map.127 = (bf16[4,2,32,512]{3,2,1,0:T(8,128)(2,1)S(1)}, f32[256,512]{1,0:T(8,128)S(1)}, bf16[256,512]{1,0:T(8,128)(2,1)S(1)}) custom-call(s32[11]{0:T(128)S(1)} %stack.62.bits, bf16[2,32,512]{2,1,0:T(8,128)(2,1)S(1)} %get-tuple-element.109.f0, bf16[2,32,512]{2,1,0:T(8,128)(2,1)S(1)} %collective-permute-done.f1, ...), custom_call_target="tpu_custom_call" | custom-call | tf_op jit(solution)/shard_map/pallas_call | solution.py:344
  17.3 1.4 %collective-permute-done.7.c3 = bf16[2,32,512]{2,1,0:T(8,128)(2,1)S(1)} collective-permute-done((bf16[2,32,512]{2,1,0:T(8,128)(2,1)S(1)}, bf16[2,32,512]{2,1,0:T(8,128)(2,1)S(1)}, u32[]{:S(2)}, u32[]{:S(2)}) %collective-permute-start.7) | collective-permute-done | bytes 65568 | tf_op jit(solution)/shard_map/ppermute | solution.py:383
  18.7 8.4 %shard_map.128 = (bf16[2176,128]{1,0:T(8,128)(2,1)S(1)}, bf16[2048,128]{1,0:T(8,128)(2,1)S(1)}, bf16[2176,128]{1,0:T(8,128)(2,1)S(1)}, bf16[2048,128]{1,0:T(8,12...) custom-call(s32[11]{0:T(128)S(1)} %stack.62.bits, ...), custom_call_target="tpu_custom_call" | custom-call | tf_op jit(solution)/shard_map/pallas_call | solution.py:344
  27.8 1.6 %collective-permute-done.8.core_got = bf16[1024,128]{1,0:T(8,128)(2,1)S(1)} collective-permute-done((bf16[1024,128]{1,0:T(8,128)(2,1)S(1)}, bf16[1024,128]{1,0:T(8,128)(2,1)S(1)}, u32[]{:S(2)}, u32[]{:S(2)}) %collective-permute-start.8) | collective-permute-done | bytes 262176 | tf_op jit(solution)/shard_map/ppermute | solution.py:383
  29.5 1.8 %collective-permute-start.9 = (bf16[1024,128]{1,0:T(8,128)(2,1)S(1)}, bf16[1024,128]{1,0:T(8,128)(2,1)S(1)}, u32[]{:S(2)}, u32[]{:S(2)}) collective-permute-start(bf16[1024,128]{1,0:T(8,128)(2,1)S(1)} %pad_maximum_fusion.2), channel_id=1, source_target_pairs={{0,16},{1,17},{2,18},{3,19},{4,20},{5,21},{6,22},{7,23},{8,24},{9,... | collective-permute-start | bytes 786440 | tf_op jit(solution)/shard_map/ppermute | solution.py:383
  31.4 1.7 %collective-permute-start.11 = (bf16[1024,128]{1,0:T(8,128)(2,1)S(1)}, bf16[1024,128]{1,0:T(8,128)(2,1)S(1)}, u32[]{:S(2)}, u32[]{:S(2)}) collective-permute-start(bf16[1024,128]{1,0:T(8,128)(2,1)S(1)} %get-tuple-element.94), channel_id=1, source_target_pairs={{0,2},{1,3},{2,0},{3,1},{4,6},{5,7},{6,4},{7,5},{8,10},{9,11},{10,... | collective-permute-start | bytes 786440 | tf_op jit(solution)/shard_map/ppermute | solution.py:383
  33.2 1.5 %collective-permute-start.13 = (bf16[1088,128]{1,0:T(8,128)(2,1)S(1)}, bf16[1088,128]{1,0:T(8,128)(2,1)S(1)}, u32[]{:S(2)}, u32[]{:S(2)}) collective-permute-start(bf16[1088,128]{1,0:T(8,128)(2,1)S(1)} %get-tuple-element.92), channel_id=1, source_target_pairs={{0,1},{1,0},{2,3},{3,2},{4,5},{5,4},{6,7},{7,6},{8,9},{9,8},{10,11... | collective-permute-start | bytes 835592 | tf_op jit(solution)/shard_map/ppermute | solution.py:383
  34.8 3.1 %collective-permute-done.9.y_got = bf16[1024,128]{1,0:T(8,128)(2,1)S(1)} collective-permute-done((bf16[1024,128]{1,0:T(8,128)(2,1)S(1)}, bf16[1024,128]{1,0:T(8,128)(2,1)S(1)}, u32[]{:S(2)}, u32[]{:S(2)}) %collective-permute-start.9) | collective-permute-done | bytes 262176 | tf_op jit(solution)/shard_map/ppermute | solution.py:383
  37.9 1.6 %collective-permute-done.11 = bf16[1024,128]{1,0:T(8,128)(2,1)S(1)} collective-permute-done((bf16[1024,128]{1,0:T(8,128)(2,1)S(1)}, bf16[1024,128]{1,0:T(8,128)(2,1)S(1)}, u32[]{:S(2)}, u32[]{:S(2)}) %collective-permute-start.11) | collective-permute-done | bytes 262176 | tf_op jit(solution)/shard_map/ppermute | solution.py:383
  39.6 1.3 %shard_map.129 = (bf16[2,128,512]{2,1,0:T(8,128)(2,1)}, bf16[2,4,128,128]{3,2,1,0:T(8,128)(2,1)S(1)}, bf16[128,128]{1,0:T(8,128)(2,1)S(1)}, bf16[128,128]{1,0:T(8,128)(2,1)S(1)}) custom-call(s32[11]{0:T(128)S(1)} %stack.62.bits, bf16[1024,128]{1,0:T(8,128)(2,1)S(1)} %get-tuple-element.57.own, bf16[1024,128]{1,0:T(8,128)(2,1)S(1)} %collective-permute-done.8.core_got, ...), custom_call_target="tpu_custom_call" | custom-call | tf_op jit(solution)/shard_map/pallas_call | solution.py:344
  40.9 1.5 %collective-permute-start.15 = (bf16[256,128]{1,0:T(8,128)(2,1)S(1)}, bf16[256,128]{1,0:T(8,128)(2,1)S(1)}, u32[]{:S(2)}, u32[]{:S(2)}) collective-permute-start(bf16[256,128]{1,0:T(8,128)(2,1)S(1)} %pad_maximum_fusion.6), channel_id=1, source_target_pairs={{0,1},{1,0},{2,3},{3,2},{4,5},{5,4},{6,7},{7,6},{8,9},{9,8},{10,11... | collective-permute-start | bytes 196616 | tf_op jit(solution)/shard_map/ppermute | solution.py:383
  42.5 1.5 %collective-permute-start.14 = (bf16[544,128]{1,0:T(8,128)(2,1)S(1)}, bf16[544,128]{1,0:T(8,128)(2,1)S(1)}, u32[]{:S(2)}, u32[]{:S(2)}) collective-permute-start(bf16[544,128]{1,0:T(8,128)(2,1)S(1)} %get-tuple-element.96), channel_id=1, source_target_pairs={{0,16},{1,17},{2,18},{3,19},{4,20},{5,21},{6,22},{7,23},{8,24},{9,... | collective-permute-start | bytes 417800 | tf_op jit(solution)/shard_map/ppermute | solution.py:383
  44.1 0.6 collective-permute-start.21
  44.7 0.4 collective-permute-done.15.x_got
  45.1 2.4 %collective-permute-done.14 = bf16[544,128]{1,0:T(8,128)(2,1)S(1)} collective-permute-done((bf16[544,128]{1,0:T(8,128)(2,1)S(1)}, bf16[544,128]{1,0:T(8,128)(2,1)S(1)}, u32[]{:S(2)}, u32[]{:S(2)}) %collective-permute-start.14) | collective-permute-done | bytes 139296 | tf_op jit(solution)/shard_map/ppermute | solution.py:383
  47.6 1.6 %collective-permute-start.16 = (bf16[400,128]{1,0:T(8,128)(2,1)S(1)}, bf16[400,128]{1,0:T(8,128)(2,1)S(1)}, u32[]{:S(2)}, u32[]{:S(2)}) collective-permute-start(bf16[400,128]{1,0:T(8,128)(2,1)S(1)} %pad_maximum_fusion.5), channel_id=1, source_target_pairs={{0,2},{1,3},{2,0},{3,1},{4,6},{5,7},{6,4},{7,5},{8,10},{9,11},{10,... | collective-permute-start | bytes 307208 | tf_op jit(solution)/shard_map/ppermute | solution.py:383
  49.3 2.7 %collective-permute-start.22 = (bf16[256,128]{1,0:T(8,128)(2,1)S(1)}, bf16[256,128]{1,0:T(8,128)(2,1)S(1)}, u32[]{:S(2)}, u32[]{:S(2)}) collective-permute-start(bf16[256,128]{1,0:T(8,128)(2,1)S(1)} %get-tuple-element.102), channel_id=1, source_target_pairs={{0,4},{1,5},{2,6},{3,7},{4,0},{5,1},{6,2},{7,3},{8,12},{9,13},{10,... | collective-permute-start | bytes 196616 | tf_op jit(solution)/shard_map/ppermute | solution.py:383
  52.0 0.4 collective-permute-done.16
  52.4 3.3 %collective-permute-start.17 = (bf16[272,128]{1,0:T(8,128)(2,1)S(1)}, bf16[272,128]{1,0:T(8,128)(2,1)S(1)}, u32[]{:S(2)}, u32[]{:S(2)}) collective-permute-start(bf16[272,128]{1,0:T(8,128)(2,1)S(1)} %add_convert_fusion.9), channel_id=1, source_target_pairs={{0,4},{1,5},{2,6},{3,7},{4,0},{5,1},{6,2},{7,3},{8,12},{9,13},{10,... | collective-permute-start | bytes 208904 | tf_op jit(solution)/shard_map/ppermute | solution.py:383
  56.0 1.4 %collective-permute-start.23 = (bf16[256,128]{1,0:T(8,128)(2,1)S(1)}, bf16[256,128]{1,0:T(8,128)(2,1)S(1)}, u32[]{:S(2)}, u32[]{:S(2)}) collective-permute-start(bf16[256,128]{1,0:T(8,128)(2,1)S(1)} %add_convert_fusion.13), channel_id=1, source_target_pairs={{0,16},{1,17},{2,18},{3,19},{4,20},{5,21},{6,22},{7,23},{8,24},{9,... | collective-permute-start | bytes 196616 | tf_op jit(solution)/shard_map/ppermute | solution.py:383
  57.4 0.8 collective-permute-done.17
  58.2 1.2 %collective-permute-start.18 = (bf16[272,128]{1,0:T(8,128)(2,1)S(1)}, bf16[272,128]{1,0:T(8,128)(2,1)S(1)}, u32[]{:S(2)}, u32[]{:S(2)}) collective-permute-start(bf16[272,128]{1,0:T(8,128)(2,1)S(1)} %add_convert_fusion.8), channel_id=1, source_target_pairs={{0,2},{1,3},{2,0},{3,1},{4,6},{5,7},{6,4},{7,5},{8,10},{9,11},{10,... | collective-permute-start | bytes 208904 | tf_op jit(solution)/shard_map/ppermute | solution.py:383
  59.3 1.0 %collective-permute-done.23 = bf16[256,128]{1,0:T(8,128)(2,1)S(1)} collective-permute-done((bf16[256,128]{1,0:T(8,128)(2,1)S(1)}, bf16[256,128]{1,0:T(8,128)(2,1)S(1)}, u32[]{:S(2)}, u32[]{:S(2)}) %collective-permute-start.23) | collective-permute-done | bytes 65568 | tf_op jit(solution)/shard_map/ppermute | solution.py:383
  60.3 2.5 %collective-permute-start.24 = (bf16[256,128]{1,0:T(8,128)(2,1)S(1)}, bf16[256,128]{1,0:T(8,128)(2,1)S(1)}, u32[]{:S(2)}, u32[]{:S(2)}) collective-permute-start(bf16[256,128]{1,0:T(8,128)(2,1)S(1)} %add_convert_fusion.12), channel_id=1, source_target_pairs={{0,4},{1,5},{2,6},{3,7},{4,0},{5,1},{6,2},{7,3},{8,12},{9,13},{10,... | collective-permute-start | bytes 196616 | tf_op jit(solution)/shard_map/ppermute | solution.py:383
  62.8 0.7 collective-permute-start.25
  63.5 1.3 %collective-permute-start.19 = (bf16[544,128]{1,0:T(8,128)(2,1)S(1)}, bf16[544,128]{1,0:T(8,128)(2,1)S(1)}, u32[]{:S(2)}, u32[]{:S(2)}) collective-permute-start(bf16[544,128]{1,0:T(8,128)(2,1)S(1)} %pad_maximum_fusion.3), channel_id=1, source_target_pairs={{0,16},{1,17},{2,18},{3,19},{4,20},{5,21},{6,22},{7,23},{8,24},{9,... | collective-permute-start | bytes 417800 | tf_op jit(solution)/shard_map/ppermute | solution.py:383
  64.8 1.5 %collective-permute-done.24 = bf16[256,128]{1,0:T(8,128)(2,1)S(1)} collective-permute-done((bf16[256,128]{1,0:T(8,128)(2,1)S(1)}, bf16[256,128]{1,0:T(8,128)(2,1)S(1)}, u32[]{:S(2)}, u32[]{:S(2)}) %collective-permute-start.24) | collective-permute-done | bytes 65568 | tf_op jit(solution)/shard_map/ppermute | solution.py:383
  66.3 0.9 %collective-permute-start.26 = (bf16[512,128]{1,0:T(8,128)(2,1)S(1)}, bf16[512,128]{1,0:T(8,128)(2,1)S(1)}, u32[]{:S(2)}, u32[]{:S(2)}) collective-permute-start(bf16[512,128]{1,0:T(8,128)(2,1)S(1)} %pad_maximum_fusion.4), channel_id=1, source_target_pairs={{0,1},{1,0},{2,3},{3,2},{4,5},{5,4},{6,7},{7,6},{8,9},{9,8},{10,11... | collective-permute-start | bytes 393224 | tf_op jit(solution)/shard_map/ppermute | solution.py:383
  67.2 1.4 %collective-permute-done.19 = bf16[544,128]{1,0:T(8,128)(2,1)S(1)} collective-permute-done((bf16[544,128]{1,0:T(8,128)(2,1)S(1)}, bf16[544,128]{1,0:T(8,128)(2,1)S(1)}, u32[]{:S(2)}, u32[]{:S(2)}) %collective-permute-start.19) | collective-permute-done | bytes 139296 | tf_op jit(solution)/shard_map/ppermute | solution.py:383
  68.7 0.8 collective-permute-start.20
  69.6 1.7 %collective-permute-done.26 = bf16[512,128]{1,0:T(8,128)(2,1)S(1)} collective-permute-done((bf16[512,128]{1,0:T(8,128)(2,1)S(1)}, bf16[512,128]{1,0:T(8,128)(2,1)S(1)}, u32[]{:S(2)}, u32[]{:S(2)}) %collective-permute-start.26) | collective-permute-done | bytes 131104 | tf_op jit(solution)/shard_map/ppermute | solution.py:383
  71.4 4.2 %collective-permute-start.27 = (bf16[1024,128]{1,0:T(8,128)(2,1)S(1)}, bf16[1024,128]{1,0:T(8,128)(2,1)S(1)}, u32[]{:S(2)}, u32[]{:S(2)}) collective-permute-start(bf16[1024,128]{1,0:T(8,128)(2,1)S(1)} %constant_dynamic-update-slice_fusion.refs_1_), channel_id=1, source_target_pairs={{0,2},{1,3},{2,0},{3,1},{4,6},{5,7},{6,4},{7,5},{8,10},{9,11},{10,... | collective-permute-start | bytes 786440 | tf_op jit(solution)/shard_map/ppermute | solution.py:383
  75.6 2.8 %shard_map.130 = bf16[2,128,512]{2,1,0:T(8,128)(2,1)} custom-call(s32[11]{0:T(128)S(1)} %stack.62.bits, bf16[2,4,128,128]{3,2,1,0:T(8,128)(2,1)S(1)} %get-tuple-element.70.dconv, bf16[256,128]{1,0:T(8,128)(2,1)S(1)} %collective-permute-done.15.x_got, bf16[128,128]{1,0:T(8,128)(2,1)S(1)} %slice.134.z_got, ...), custom_call_target="tpu_custom_call" | custom-call | tf_op jit(solution)/shard_map/pallas_call | solution.py:344
  78.4 2.0 %shard_map.131 = (f32[512,512]{1,0:T(8,128)}, f32[512,512]{1,0:T(8,128)}, f32[512,512]{1,0:T(8,128)}, f32[512,512]{1,0:T(8,128)}) custom-call(s32[11]{0:T(128)S(1)} %stack.62.bits, bf16[1088,128]{1,0:T(8,128)(2,1)S(1)} %pad_maximum_fusion.1.refs_0_.refs_2_, bf16[1024,128]{1,0:T(8,128)(2,1)S(1)} %constant_dynamic-update-slice_fusion.refs_1_, ...), custom_call_target="tpu_custom_call" | custom-call | tf_op jit(solution)/shard_map/pallas_call | solution.py:344
  80.4 2.1 %collective-permute-done.27.refs_1_ = bf16[1024,128]{1,0:T(8,128)(2,1)S(1)} collective-permute-done((bf16[1024,128]{1,0:T(8,128)(2,1)S(1)}, bf16[1024,128]{1,0:T(8,128)(2,1)S(1)}, u32[]{:S(2)}, u32[]{:S(2)}) %collective-permute-start.27) | collective-permute-done | bytes 262176 | tf_op jit(solution)/shard_map/ppermute | solution.py:383
  82.5 0.5 collective-permute-start.31
  83.0 1.6 %shard_map.132 = (f32[512,512]{1,0:T(8,128)}, f32[512,512]{1,0:T(8,128)}, f32[512,512]{1,0:T(8,128)}, f32[512,512]{1,0:T(8,128)}) custom-call(s32[11]{0:T(128)S(1)} %stack.62.bits, bf16[1088,128]{1,0:T(8,128)(2,1)S(1)} %collective-permute-done.20.refs_0_.refs_3_, ...), custom_call_target="tpu_custom_call", output_to_operand_aliasing={{0}: (3, {}), {1}: (4, {}), {2}: (5, {}), {3}: (6, {})} | custom-call | tf_op jit(solution)/shard_map/pallas_call | solution.py:344
  84.6 2.2 %shard_map.133 = (f32[512,512]{1,0:T(8,128)}, f32[512,512]{1,0:T(8,128)}, f32[512,512]{1,0:T(8,128)}, f32[512,512]{1,0:T(8,128)}, f32[31,512]{1,0:T(8,128)}) custom-call(s32[11]{0:T(128)S(1)} %stack.62.bits, bf16[1088,128]{1,0:T(8,128)(2,1)S(1)} %collective-permute-done.30.refs_0_.refs_5_, ...), custom_call_target="tpu_custom_call", output_to_operand_aliasing={{0}: (7, {}), {1}: (8, {}), {2}: (9, {}), {3}: (10, {})} | custom-call | tf_op jit(solution)/shard_map/pallas_call | solution.py:344
  (54 shorter events, 2.5 us)
Async XLA Ops:
  1.7 5.2 %collective-permute-start = (bf16[2,32,512]{2,1,0:T(8,128)(2,1)S(1)}, bf16[2,32,512]{2,1,0:T(8,128)(2,1)S(1)}, u32[]{:S(2)}, u32[]{:S(2)}) collective-permute-start(bf16[2,32,512]{2,1,0:T(8,128)(2,1)S(1)} %get-tuple-element.108), channel_id=1, source_target_pairs={{0,8},{1,9},{2,10},{3,11},{4,12},{5,13},{6,14},{7,15},{8,0},{9,1},... | collective-permute-start | bytes 196616 | tf_op jit(solution)/shard_map/ppermute | solution.py:383
  2.2 5.3 %collective-permute-start.1 = (bf16[2,32,512]{2,1,0:T(8,128)(2,1)S(1)}, bf16[2,32,512]{2,1,0:T(8,128)(2,1)S(1)}, u32[]{:S(2)}, u32[]{:S(2)}) collective-permute-start(bf16[2,32,512]{2,1,0:T(8,128)(2,1)S(1)} %get-tuple-element.110), channel_id=1, source_target_pairs={{0,16},{1,17},{2,18},{3,19},{4,20},{5,21},{6,22},{7,23},{8,24},{9,... | collective-permute-start | bytes 196616 | tf_op jit(solution)/shard_map/ppermute | solution.py:383
  4.8 4.0 %collective-permute-start.2 = (bf16[2,32,512]{2,1,0:T(8,128)(2,1)S(1)}, bf16[2,32,512]{2,1,0:T(8,128)(2,1)S(1)}, u32[]{:S(2)}, u32[]{:S(2)}) collective-permute-start(bf16[2,32,512]{2,1,0:T(8,128)(2,1)S(1)} %get-tuple-element.107), channel_id=1, source_target_pairs={{0,24},{1,25},{2,26},{3,27},{4,28},{5,29},{6,30},{7,31},{8,16},{9,... | collective-permute-start | bytes 196616 | tf_op jit(solution)/shard_map/ppermute | solution.py:383
  4.8 5.4 %copy-start = (bf16[2,128,512]{2,1,0:T(8,128)(2,1)S(1)}, bf16[2,128,512]{2,1,0:T(8,128)(2,1)}, u32[]{:S(2)}) copy-start(bf16[2,128,512]{2,1,0:T(8,128)(2,1)} %cot.1) | copy-start | bytes 786436
  4.8 9.9 %copy-start.1 = (f32[31,512]{1,0:T(8,128)S(1)}, f32[31,512]{1,0:T(8,128)}, u32[]{:S(2)}) copy-start(f32[31,512]{1,0:T(8,128)} %kern.3) | copy-start | bytes 190468
  9.4 5.3 %collective-permute-start.3 = (bf16[4,2,16,512]{3,2,1,0:T(8,128)(2,1)S(1)}, bf16[4,2,16,512]{3,2,1,0:T(8,128)(2,1)S(1)}, u32[]{:S(2)}, u32[]{:S(2)}) collective-permute-start(bf16[4,2,16,512]{3,2,1,0:T(8,128)(2,1)S(1)} %get-tuple-element.51), channel_id=1, source_target_pairs={{0,8},{1,9},{2,10},{3,11},{4,12},{5,13},{6,14},{7,15},{8,0},{9,1},... | collective-permute-start | bytes 393224 | tf_op jit(solution)/shard_map/ppermute | solution.py:383
  9.6 5.1 %collective-permute-start.4 = (bf16[4,2,16,512]{3,2,1,0:T(8,128)(2,1)S(1)}, bf16[4,2,16,512]{3,2,1,0:T(8,128)(2,1)S(1)}, u32[]{:S(2)}, u32[]{:S(2)}) collective-permute-start(bf16[4,2,16,512]{3,2,1,0:T(8,128)(2,1)S(1)} %get-tuple-element.52), channel_id=1, source_target_pairs={{8,24},{9,25},{10,26},{11,27},{12,28},{13,29},{14,30},{15,31},{24,... | collective-permute-start | bytes 393224 | tf_op jit(solution)/shard_map/ppermute | solution.py:383
  10.3 6.9 %collective-permute-start.5 = (bf16[2,32,512]{2,1,0:T(8,128)(2,1)S(1)}, bf16[2,32,512]{2,1,0:T(8,128)(2,1)S(1)}, u32[]{:S(2)}, u32[]{:S(2)}) collective-permute-start(bf16[2,32,512]{2,1,0:T(8,128)(2,1)S(1)} %get-tuple-element.105), channel_id=1, source_target_pairs={{0,8},{1,9},{2,10},{3,11},{4,12},{5,13},{6,14},{7,15},{8,0},{9,1},... | collective-permute-start | bytes 196616 | tf_op jit(solution)/shard_map/ppermute | solution.py:383
  13.0 4.3 %collective-permute-start.6 = (bf16[2,32,512]{2,1,0:T(8,128)(2,1)S(1)}, bf16[2,32,512]{2,1,0:T(8,128)(2,1)S(1)}, u32[]{:S(2)}, u32[]{:S(2)}) collective-permute-start(bf16[2,32,512]{2,1,0:T(8,128)(2,1)S(1)} %get-tuple-element.104), channel_id=1, source_target_pairs={{0,16},{1,17},{2,18},{3,19},{4,20},{5,21},{6,22},{7,23},{8,24},{9,... | collective-permute-start | bytes 196616 | tf_op jit(solution)/shard_map/ppermute | solution.py:383
  14.7 4.0 %collective-permute-start.7 = (bf16[2,32,512]{2,1,0:T(8,128)(2,1)S(1)}, bf16[2,32,512]{2,1,0:T(8,128)(2,1)S(1)}, u32[]{:S(2)}, u32[]{:S(2)}) collective-permute-start(bf16[2,32,512]{2,1,0:T(8,128)(2,1)S(1)} %get-tuple-element.103), channel_id=1, source_target_pairs={{0,24},{1,25},{2,26},{3,27},{4,28},{5,29},{6,30},{7,31},{8,16},{9,... | collective-permute-start | bytes 196616 | tf_op jit(solution)/shard_map/ppermute | solution.py:383
  27.1 4.2 %collective-permute-start.10 = (bf16[2048,128]{1,0:T(8,128)(2,1)S(1)}, bf16[2048,128]{1,0:T(8,128)(2,1)S(1)}, u32[]{:S(2)}, u32[]{:S(2)}) collective-permute-start(bf16[2048,128]{1,0:T(8,128)(2,1)S(1)} %get-tuple-element.60), channel_id=1, source_target_pairs={{0,8},{1,9},{2,10},{3,11},{4,12},{5,13},{6,14},{7,15},{8,0},{9,1},... | collective-permute-start | bytes 1572872 | tf_op jit(solution)/shard_map/ppermute | solution.py:383
  27.3 2.1 %collective-permute-start.8 = (bf16[1024,128]{1,0:T(8,128)(2,1)S(1)}, bf16[1024,128]{1,0:T(8,128)(2,1)S(1)}, u32[]{:S(2)}, u32[]{:S(2)}) collective-permute-start(bf16[1024,128]{1,0:T(8,128)(2,1)S(1)} %get-tuple-element.58), channel_id=1, source_target_pairs={{0,8},{1,9},{2,10},{3,11},{4,12},{5,13},{6,14},{7,15},{8,0},{9,1},... | collective-permute-start | bytes 786440 | tf_op jit(solution)/shard_map/ppermute | solution.py:383
  27.7 5.4 %collective-permute-start.12 = (bf16[2176,128]{1,0:T(8,128)(2,1)S(1)}, bf16[2176,128]{1,0:T(8,128)(2,1)S(1)}, u32[]{:S(2)}, u32[]{:S(2)}) collective-permute-start(bf16[2176,128]{1,0:T(8,128)(2,1)S(1)} %get-tuple-element.64), channel_id=1, source_target_pairs={{0,8},{1,9},{2,10},{3,11},{4,12},{5,13},{6,14},{7,15},{8,0},{9,1},... | collective-permute-start | bytes 1671176 | tf_op jit(solution)/shard_map/ppermute | solution.py:383
  29.5 8.4 %collective-permute-start.9 = (bf16[1024,128]{1,0:T(8,128)(2,1)S(1)}, bf16[1024,128]{1,0:T(8,128)(2,1)S(1)}, u32[]{:S(2)}, u32[]{:S(2)}) collective-permute-start(bf16[1024,128]{1,0:T(8,128)(2,1)S(1)} %pad_maximum_fusion.2), channel_id=1, source_target_pairs={{0,16},{1,17},{2,18},{3,19},{4,20},{5,21},{6,22},{7,23},{8,24},{9,... | collective-permute-start | bytes 786440 | tf_op jit(solution)/shard_map/ppermute | solution.py:383
  31.4 8.1 %collective-permute-start.11 = (bf16[1024,128]{1,0:T(8,128)(2,1)S(1)}, bf16[1024,128]{1,0:T(8,128)(2,1)S(1)}, u32[]{:S(2)}, u32[]{:S(2)}) collective-permute-start(bf16[1024,128]{1,0:T(8,128)(2,1)S(1)} %get-tuple-element.94), channel_id=1, source_target_pairs={{0,2},{1,3},{2,0},{3,1},{4,6},{5,7},{6,4},{7,5},{8,10},{9,11},{10,... | collective-permute-start | bytes 786440 | tf_op jit(solution)/shard_map/ppermute | solution.py:383
  33.2 9.1 %collective-permute-start.13 = (bf16[1088,128]{1,0:T(8,128)(2,1)S(1)}, bf16[1088,128]{1,0:T(8,128)(2,1)S(1)}, u32[]{:S(2)}, u32[]{:S(2)}) collective-permute-start(bf16[1088,128]{1,0:T(8,128)(2,1)S(1)} %get-tuple-element.92), channel_id=1, source_target_pairs={{0,1},{1,0},{2,3},{3,2},{4,5},{5,4},{6,7},{7,6},{8,9},{9,8},{10,11... | collective-permute-start | bytes 835592 | tf_op jit(solution)/shard_map/ppermute | solution.py:383
  40.9 4.3 %collective-permute-start.15 = (bf16[256,128]{1,0:T(8,128)(2,1)S(1)}, bf16[256,128]{1,0:T(8,128)(2,1)S(1)}, u32[]{:S(2)}, u32[]{:S(2)}) collective-permute-start(bf16[256,128]{1,0:T(8,128)(2,1)S(1)} %pad_maximum_fusion.6), channel_id=1, source_target_pairs={{0,1},{1,0},{2,3},{3,2},{4,5},{5,4},{6,7},{7,6},{8,9},{9,8},{10,11... | collective-permute-start | bytes 196616 | tf_op jit(solution)/shard_map/ppermute | solution.py:383
  42.5 5.1 %collective-permute-start.14 = (bf16[544,128]{1,0:T(8,128)(2,1)S(1)}, bf16[544,128]{1,0:T(8,128)(2,1)S(1)}, u32[]{:S(2)}, u32[]{:S(2)}) collective-permute-start(bf16[544,128]{1,0:T(8,128)(2,1)S(1)} %get-tuple-element.96), channel_id=1, source_target_pairs={{0,16},{1,17},{2,18},{3,19},{4,20},{5,21},{6,22},{7,23},{8,24},{9,... | collective-permute-start | bytes 417800 | tf_op jit(solution)/shard_map/ppermute | solution.py:383
  44.1 5.2 %collective-permute-start.21 = (bf16[512,128]{1,0:T(8,128)(2,1)S(1)}, bf16[512,128]{1,0:T(8,128)(2,1)S(1)}, u32[]{:S(2)}, u32[]{:S(2)}) collective-permute-start(bf16[512,128]{1,0:T(8,128)(2,1)S(1)} %get-tuple-element.98), channel_id=1, source_target_pairs={{0,1},{1,0},{2,3},{3,2},{4,5},{5,4},{6,7},{7,6},{8,9},{9,8},{10,11... | collective-permute-start | bytes 393224 | tf_op jit(solution)/shard_map/ppermute | solution.py:383
  47.6 4.7 %collective-permute-start.16 = (bf16[400,128]{1,0:T(8,128)(2,1)S(1)}, bf16[400,128]{1,0:T(8,128)(2,1)S(1)}, u32[]{:S(2)}, u32[]{:S(2)}) collective-permute-start(bf16[400,128]{1,0:T(8,128)(2,1)S(1)} %pad_maximum_fusion.5), channel_id=1, source_target_pairs={{0,2},{1,3},{2,0},{3,1},{4,6},{5,7},{6,4},{7,5},{8,10},{9,11},{10,... | collective-permute-start | bytes 307208 | tf_op jit(solution)/shard_map/ppermute | solution.py:383
  49.3 6.6 %collective-permute-start.22 = (bf16[256,128]{1,0:T(8,128)(2,1)S(1)}, bf16[256,128]{1,0:T(8,128)(2,1)S(1)}, u32[]{:S(2)}, u32[]{:S(2)}) collective-permute-start(bf16[256,128]{1,0:T(8,128)(2,1)S(1)} %get-tuple-element.102), channel_id=1, source_target_pairs={{0,4},{1,5},{2,6},{3,7},{4,0},{5,1},{6,2},{7,3},{8,12},{9,13},{10,... | collective-permute-start | bytes 196616 | tf_op jit(solution)/shard_map/ppermute | solution.py:383
  52.4 5.8 %collective-permute-start.17 = (bf16[272,128]{1,0:T(8,128)(2,1)S(1)}, bf16[272,128]{1,0:T(8,128)(2,1)S(1)}, u32[]{:S(2)}, u32[]{:S(2)}) collective-permute-start(bf16[272,128]{1,0:T(8,128)(2,1)S(1)} %add_convert_fusion.9), channel_id=1, source_target_pairs={{0,4},{1,5},{2,6},{3,7},{4,0},{5,1},{6,2},{7,3},{8,12},{9,13},{10,... | collective-permute-start | bytes 208904 | tf_op jit(solution)/shard_map/ppermute | solution.py:383
  56.0 4.3 %collective-permute-start.23 = (bf16[256,128]{1,0:T(8,128)(2,1)S(1)}, bf16[256,128]{1,0:T(8,128)(2,1)S(1)}, u32[]{:S(2)}, u32[]{:S(2)}) collective-permute-start(bf16[256,128]{1,0:T(8,128)(2,1)S(1)} %add_convert_fusion.13), channel_id=1, source_target_pairs={{0,16},{1,17},{2,18},{3,19},{4,20},{5,21},{6,22},{7,23},{8,24},{9,... | collective-permute-start | bytes 196616 | tf_op jit(solution)/shard_map/ppermute | solution.py:383
  58.2 5.3 %collective-permute-start.18 = (bf16[272,128]{1,0:T(8,128)(2,1)S(1)}, bf16[272,128]{1,0:T(8,128)(2,1)S(1)}, u32[]{:S(2)}, u32[]{:S(2)}) collective-permute-start(bf16[272,128]{1,0:T(8,128)(2,1)S(1)} %add_convert_fusion.8), channel_id=1, source_target_pairs={{0,2},{1,3},{2,0},{3,1},{4,6},{5,7},{6,4},{7,5},{8,10},{9,11},{10,... | collective-permute-start | bytes 208904 | tf_op jit(solution)/shard_map/ppermute | solution.py:383
  60.3 5.9 %collective-permute-start.24 = (bf16[256,128]{1,0:T(8,128)(2,1)S(1)}, bf16[256,128]{1,0:T(8,128)(2,1)S(1)}, u32[]{:S(2)}, u32[]{:S(2)}) collective-permute-start(bf16[256,128]{1,0:T(8,128)(2,1)S(1)} %add_convert_fusion.12), channel_id=1, source_target_pairs={{0,4},{1,5},{2,6},{3,7},{4,0},{5,1},{6,2},{7,3},{8,12},{9,13},{10,... | collective-permute-start | bytes 196616 | tf_op jit(solution)/shard_map/ppermute | solution.py:383
  62.8 3.5 %collective-permute-start.25 = (bf16[128,128]{1,0:T(8,128)(2,1)S(1)}, bf16[128,128]{1,0:T(8,128)(2,1)S(1)}, u32[]{:S(2)}, u32[]{:S(2)}) collective-permute-start(bf16[128,128]{1,0:T(8,128)(2,1)S(1)} %constant_dynamic-slice_fusion), channel_id=1, source_target_pairs={{2,4},{3,5},{10,12},{11,13},{18,20},{19,21},{26,28},{27,29},{4,2},... | collective-permute-start | bytes 98312 | tf_op jit(solution)/shard_map/ppermute | solution.py:383
  63.5 5.1 %collective-permute-start.19 = (bf16[544,128]{1,0:T(8,128)(2,1)S(1)}, bf16[544,128]{1,0:T(8,128)(2,1)S(1)}, u32[]{:S(2)}, u32[]{:S(2)}) collective-permute-start(bf16[544,128]{1,0:T(8,128)(2,1)S(1)} %pad_maximum_fusion.3), channel_id=1, source_target_pairs={{0,16},{1,17},{2,18},{3,19},{4,20},{5,21},{6,22},{7,23},{8,24},{9,... | collective-permute-start | bytes 417800 | tf_op jit(solution)/shard_map/ppermute | solution.py:383
  66.3 5.0 %collective-permute-start.26 = (bf16[512,128]{1,0:T(8,128)(2,1)S(1)}, bf16[512,128]{1,0:T(8,128)(2,1)S(1)}, u32[]{:S(2)}, u32[]{:S(2)}) collective-permute-start(bf16[512,128]{1,0:T(8,128)(2,1)S(1)} %pad_maximum_fusion.4), channel_id=1, source_target_pairs={{0,1},{1,0},{2,3},{3,2},{4,5},{5,4},{6,7},{7,6},{8,9},{9,8},{10,11... | collective-permute-start | bytes 393224 | tf_op jit(solution)/shard_map/ppermute | solution.py:383
  68.7 9.8 %collective-permute-start.28 = (bf16[1088,128]{1,0:T(8,128)(2,1)S(1)}, bf16[1088,128]{1,0:T(8,128)(2,1)S(1)}, u32[]{:S(2)}, u32[]{:S(2)}) collective-permute-start(bf16[1088,128]{1,0:T(8,128)(2,1)S(1)} %pad_maximum_fusion.1.refs_0_.refs_2_), channel_id=1, source_target_pairs={{0,8},{1,9},{2,10},{3,11},{4,12},{5,13},{6,14},{7,15},{8,0},{9,1},... | collective-permute-start | bytes 835592 | tf_op jit(solution)/shard_map/ppermute | solution.py:383
  68.7 13.8 %collective-permute-start.20 = (bf16[1088,128]{1,0:T(8,128)(2,1)S(1)}, bf16[1088,128]{1,0:T(8,128)(2,1)S(1)}, u32[]{:S(2)}, u32[]{:S(2)}) collective-permute-start(bf16[1088,128]{1,0:T(8,128)(2,1)S(1)} %pad_maximum_fusion.1.refs_0_.refs_2_), channel_id=1, source_target_pairs={{0,1},{1,0},{2,3},{3,2},{4,5},{5,4},{6,7},{7,6},{8,9},{9,8},{10,11... | collective-permute-start | bytes 835592 | tf_op jit(solution)/shard_map/ppermute | solution.py:383
  71.3 7.1 %collective-permute-start.29 = (bf16[1024,128]{1,0:T(8,128)(2,1)S(1)}, bf16[1024,128]{1,0:T(8,128)(2,1)S(1)}, u32[]{:S(2)}, u32[]{:S(2)}) collective-permute-start(bf16[1024,128]{1,0:T(8,128)(2,1)S(1)} %constant_dynamic-update-slice_fusion.refs_1_), channel_id=1, source_target_pairs={{0,8},{1,9},{2,10},{3,11},{4,12},{5,13},{6,14},{7,15},{8,0},{9,1},... | collective-permute-start | bytes 786440 | tf_op jit(solution)/shard_map/ppermute | solution.py:383
  71.4 11.1 %collective-permute-start.27 = (bf16[1024,128]{1,0:T(8,128)(2,1)S(1)}, bf16[1024,128]{1,0:T(8,128)(2,1)S(1)}, u32[]{:S(2)}, u32[]{:S(2)}) collective-permute-start(bf16[1024,128]{1,0:T(8,128)(2,1)S(1)} %constant_dynamic-update-slice_fusion.refs_1_), channel_id=1, source_target_pairs={{0,2},{1,3},{2,0},{3,1},{4,6},{5,7},{6,4},{7,5},{8,10},{9,11},{10,... | collective-permute-start | bytes 786440 | tf_op jit(solution)/shard_map/ppermute | solution.py:383
  82.5 2.1 %collective-permute-start.30 = (bf16[1088,128]{1,0:T(8,128)(2,1)S(1)}, bf16[1088,128]{1,0:T(8,128)(2,1)S(1)}, u32[]{:S(2)}, u32[]{:S(2)}) collective-permute-start(bf16[1088,128]{1,0:T(8,128)(2,1)S(1)} %collective-permute-done.20.refs_0_.refs_3_), channel_id=1, source_target_pairs={{0,8},{1,9},{2,10},{3,11},{4,12},{5,13},{6,14},{7,15},{8,0},{9,1},... | collective-permute-start | bytes 835592 | tf_op jit(solution)/shard_map/ppermute | solution.py:383
  82.5 2.1 %collective-permute-start.31 = (bf16[1024,128]{1,0:T(8,128)(2,1)S(1)}, bf16[1024,128]{1,0:T(8,128)(2,1)S(1)}, u32[]{:S(2)}, u32[]{:S(2)}) collective-permute-start(bf16[1024,128]{1,0:T(8,128)(2,1)S(1)} %collective-permute-done.27.refs_1_), channel_id=1, source_target_pairs={{0,8},{1,9},{2,10},{3,11},{4,12},{5,13},{6,14},{7,15},{8,0},{9,1},... | collective-permute-start | bytes 786440 | tf_op jit(solution)/shard_map/ppermute | solution.py:383

commit v17 on v16

--- a/solution.py
+++ b/solution.py
@@ -94,9 +94,9 @@
 
 
 def main_kernel(
-    plan, bits, frames, conv_in, acted_in, c0, c1, c2, c3, near, side, weights,
-    a_keep, b_keep, a_send, b_send, back_keep, back_send,
-    left_s, turned_s, right_s, q_s, k_s, v_s, u_s, dconv_s, tap_s,
+    plan, bits, frames, conv_in, acted_in, c0, c1, c2, c3, weights,
+    a_keep, b_keep, a_send, b_send, back_keep, back_send, dconv_s,
+    left_s, turned_s, right_s, q_s, k_s, v_s, u_s,
 ):
     groups, count, sub, width, factor = plan
     mics = groups * count
@@ -175,6 +175,50 @@
     sig = sigmoid(conv)
     dconv_s[...] = dacted * sig * (1.0 + conv * (1.0 - sig))
 
+    size = cols * width // 8
+    core = bits[CORE]
+    for out, owner, h in (
+        (a_send, 1 - core, 0), (b_send, 1 - core, 1), (a_keep, core, 0), (b_keep, core, 1)
+    ):
+        i = owner * 2 + h
+        span = size + HALO * (1 - h)
+        first, second, third = ways(bits, h)
+        grad = mm(turned_s[i // 3], flat(i)).astype(BF)
+        for piece in range(8):
+            cb, at = piece * size // width, piece * size % width
+            rel = ((piece // 4) ^ first) * 4 + ((piece // 2 % 2) ^ second) * 2 + ((piece % 2) ^ third)
+            start = pl.multiple_of(rel * span, HALO)
+            out[pl.ds(start, size), :] = grad[at : at + size, cb * LANES : (cb + 1) * LANES]
+            if h == 0:
+                out[pl.ds(pl.multiple_of(start + size, HALO), HALO), :] = jnp.zeros(
+                    (HALO, LANES), BF
+                )
+
+    proj = mm(left_s[1], wo[...])
+    unit = 2 * count * cols * sub
+    for d, (out, base) in enumerate(
+        ((back_keep, 0), (back_send, 0), (back_keep, unit), (back_send, unit))
+    ):
+        for m in range(count):
+            for c in range(cuts):
+                at = c * block + (d * count + m) * HALO
+                part = slice(c * HALO, (c + 1) * HALO)
+                layer = (frames[d, m, part, :].astype(F32) + proj[at : at + HALO]).astype(BF)
+                dconv = dconv_s[at : at + HALO, :].astype(BF)
+                for lc in range(cols):
+                    for kind, value in enumerate((layer, dconv)):
+                        to = base + ((kind * count + m) * cols + lc) * sub + c * HALO
+                        out[to : to + HALO, :] = value[:, lc * LANES : (lc + 1) * LANES]
+
+
+def tap_kernel(plan, bits, frames, near, side, dconv_s, keep_in, send_in, keep, send, tap_s):
+    groups, count, sub, width = plan
+    mics = groups * count
+    cuts = sub // HALO
+    block = mics * HALO
+    cols = width // LANES
+    keep[...] = keep_in[...]
+    send[...] = send_in[...]
     for lc in range(cols):
         lanes = slice(lc * LANES, (lc + 1) * LANES)
 
@@ -206,38 +250,15 @@
 
     tap_s[cols * 32 :, :] = jnp.zeros((HALO, LANES), F32)
     size = cols * width // 8
+    span = size + HALO
     core = bits[CORE]
-    for out, owner, h in (
-        (a_send, 1 - core, 0), (b_send, 1 - core, 1), (a_keep, core, 0), (b_keep, core, 1)
-    ):
-        i = owner * 2 + h
-        span = size + HALO * (1 - h)
-        first, second, third = ways(bits, h)
-        grad = mm(turned_s[i // 3], flat(i)).astype(BF)
+    first, second, third = ways(bits, 0)
+    for out, owner in ((send, 1 - core), (keep, core)):
         for piece in range(8):
-            cb, at = piece * size // width, piece * size % width
             rel = ((piece // 4) ^ first) * 4 + ((piece // 2 % 2) ^ second) * 2 + ((piece % 2) ^ third)
-            start = pl.multiple_of(rel * span, HALO)
-            out[pl.ds(start, size), :] = grad[at : at + size, cb * LANES : (cb + 1) * LANES]
-            if h == 0:
-                tail = tap_s[pl.ds(pl.multiple_of((owner * 8 + piece) * 8, 8), HALO), :]
-                out[pl.ds(pl.multiple_of(start + size, HALO), HALO), :] = tail.astype(BF)
-
-    proj = mm(left_s[1], wo[...])
-    unit = 2 * count * cols * sub
-    for d, (out, base) in enumerate(
-        ((back_keep, 0), (back_send, 0), (back_keep, unit), (back_send, unit))
-    ):
-        for m in range(count):
-            for c in range(cuts):
-                at = c * block + (d * count + m) * HALO
-                part = slice(c * HALO, (c + 1) * HALO)
-                layer = (frames[d, m, part, :].astype(F32) + proj[at : at + HALO]).astype(BF)
-                dconv = dconv_s[at : at + HALO, :].astype(BF)
-                for lc in range(cols):
-                    for kind, value in enumerate((layer, dconv)):
-                        to = base + ((kind * count + m) * cols + lc) * sub + c * HALO
-                        out[to : to + HALO, :] = value[:, lc * LANES : (lc + 1) * LANES]
+            tail = tap_s[pl.ds(pl.multiple_of((owner * 8 + piece) * 8, 8), HALO), :]
+            at = pl.multiple_of(rel * span + size, HALO)
+            out[pl.ds(at, HALO), :] = tail.astype(BF)
 
 
 def total(*parts):
@@ -427,17 +448,21 @@
         (moved, shape((rows, width), F32), shape((rows, width), BF)),
         [], 8, bits, *f, near, side, kernel,
     )
-    a_keep, b_keep, a_send, b_send, back_keep, back_send = call(
+    a_keep, b_keep, a_send, b_send, back_keep, back_send, dconv_here = call(
         functools.partial(main_kernel, (groups, count, sub, width, factor)),
-        (flat(8 * span), flat(8 * size)) * 2 + (flat(2 * unit),) * 2,
+        (flat(8 * span), flat(8 * size)) * 2 + (flat(2 * unit),) * 2 + (shape((rows, width), F32),),
         [
             pltpu.VMEM((2, rows, width), BF),
             pltpu.VMEM((2, width, rows), BF),
             pltpu.VMEM((4, cuts, groups, count, HALO, width), BF),
-            big, big, big, big, wide,
-            pltpu.VMEM((32 * cols + HALO, LANES), F32),
+            big, big, big, big,
         ],
-        24, bits, placed, conv, acted, *c, near, side, weights,
+        24, bits, placed, conv, acted, *c, weights,
+    )
+    a_keep, a_send = call(
+        functools.partial(tap_kernel, (groups, count, sub, width)), (flat(8 * span),) * 2,
+        [pltpu.VMEM((32 * cols + HALO, LANES), F32)],
+        8, bits, placed, near, side, dconv_here, a_keep, a_send,
     )
 
     lines = [2**i for i in range(1, blocks.bit_length() - 1)]

time: 87.1 us -> 87.1 us (level)
  starting transfers between devices: 39 us -> 37.7 us
    ppermute x32, starting transfers between devices: 39 us -> 37.7 us  [permute(): return lax.ppermute(x, ('mic', 'tm'), pairs)]
    pallas_call x8 -> x9, Pallas kernels: 21.4 us -> 21.9 us  [call(): pl.pallas_call(body, out_shape=outs, in_specs=[pl.BlockSpec(memory_space=...]
  transfers between devices with their start and end apart: 32 -> 32, of which waited for: 17 -> 16; matrix products, arithmetic and copies ran while one was open for 3% -> 4% of each run, Pallas kernels for 12% -> 15%
where the time goes in v17:
time: 87.1 us; the launch traced here: 86.9 us
  starting transfers between devices  37.7 us (43%)
  waiting for transfers between devices  21.9 us (25%)
  Pallas kernels  21.9 us (25%)
  other arithmetic  3.2 us (4%)
  local copies, waits for them, and re-layouts  1.15 us (1%)
  between operations  1.06 us (1%)
    ppermute x32, starting transfers between devices, permute(): return lax.ppermute(x, ('mic', 'tm'), pairs)  37.7 us
    ppermute x32, waiting for transfers between devices, permute(): return lax.ppermute(x, ('mic', 'tm'), pairs)  21.9 us
    pallas_call x9, Pallas kernels, call(): pl.pallas_call(body, out_shape=outs, in_specs=[pl.BlockSpec(memory_space=...  21.9 us
    another operation x1, other arithmetic, shards(): weights = jnp.stack([w_query, w_key, w_value, w_out])  1.82 us
  transfers between devices with their start and end apart: 32, of which 16 were waited for; matrix products, arithmetic and copies ran while one was open for 4% of the time, Pallas kernels for 15%

profile of v17, /device:TPU:0, one launch (start us, length us, event | category | flops | bytes accessed | tf_op | source)
XLA Modules:
  0.0 86.9 jit_solution(7786580163362258676)
XLA Ops:
  0.7 1.0 %constant_dynamic-slice_fusion.5 = (bf16[2,32,512]{2,1,0:T(8,128)(2,1)S(1)}, bf16[2,32,512]{2,1,0:T(8,128)(2,1)S(1)}, bf16[2,32,512]{2,1,0:T(8,128)(2,1)S(1)}, bf16[2,32,512]{2,1,0:T(8,128)(2,1)S(1)}) fusion(bf16[2,128,512]{2,1,0:T(8,128)(2,1)} %param.7, s32[]{:T(128)S(6)} %select_n.100, s32[]{:T(128)S(6)} %select_n.98, s32[]{:T(128)S(6)} %select_n.97, ...), kind=kLoop, calls=%fused_computation.30 | loop fusion | bytes 524304 | tf_op jit(solution)/shard_map/dynamic_slice | solution.py:415
  1.7 0.5 collective-permute-start
  2.2 2.6 %collective-permute-start.1 = (bf16[2,32,512]{2,1,0:T(8,128)(2,1)S(1)}, bf16[2,32,512]{2,1,0:T(8,128)(2,1)S(1)}, u32[]{:S(2)}, u32[]{:S(2)}) collective-permute-start(bf16[2,32,512]{2,1,0:T(8,128)(2,1)S(1)} %get-tuple-element.116), channel_id=1, source_target_pairs={{0,16},{1,17},{2,18},{3,19},{4,20},{5,21},{6,22},{7,23},{8,24},{9,... | collective-permute-start | bytes 196616 | tf_op jit(solution)/shard_map/ppermute | solution.py:404
  4.8 1.8 %pad_maximum_fusion.weights = bf16[4,512,512]{2,1,0:T(8,128)(2,1)S(1)} fusion(bf16[1,512,512]{2,1,0:T(8,128)(2,1)} %bitcast.15, bf16[1,512,512]{2,1,0:T(8,128)(2,1)} %bitcast.16, bf16[1,512,512]{2,1,0:T(8,128)(2,1)} %bitcast.17, bf16[1,512,512]{2,1,0:T(8,128)(2,1)} %bitcast.18), kind=kLoop, calls=%fused_computation | loop fusion | flops 3145728 | bytes 4194304 | tf_op jit(solution)/shard_map/stack | solution.py:423
  6.9 0.6 collective-permute-done.1.f2
  7.5 1.4 %collective-permute-done.2.f3 = bf16[2,32,512]{2,1,0:T(8,128)(2,1)S(1)} collective-permute-done((bf16[2,32,512]{2,1,0:T(8,128)(2,1)S(1)}, bf16[2,32,512]{2,1,0:T(8,128)(2,1)S(1)}, u32[]{:S(2)}, u32[]{:S(2)}) %collective-permute-start.2) | collective-permute-done | bytes 65568 | tf_op jit(solution)/shard_map/ppermute | solution.py:404
  8.8 0.6 shard_map.126
  9.6 0.7 collective-permute-start.4
  10.3 2.7 %collective-permute-start.5 = (bf16[2,32,512]{2,1,0:T(8,128)(2,1)S(1)}, bf16[2,32,512]{2,1,0:T(8,128)(2,1)S(1)}, u32[]{:S(2)}, u32[]{:S(2)}) collective-permute-start(bf16[2,32,512]{2,1,0:T(8,128)(2,1)S(1)} %get-tuple-element.111), channel_id=1, source_target_pairs={{0,8},{1,9},{2,10},{3,11},{4,12},{5,13},{6,14},{7,15},{8,0},{9,1},... | collective-permute-start | bytes 196616 | tf_op jit(solution)/shard_map/ppermute | solution.py:404
  13.0 1.6 %collective-permute-start.6 = (bf16[2,32,512]{2,1,0:T(8,128)(2,1)S(1)}, bf16[2,32,512]{2,1,0:T(8,128)(2,1)S(1)}, u32[]{:S(2)}, u32[]{:S(2)}) collective-permute-start(bf16[2,32,512]{2,1,0:T(8,128)(2,1)S(1)} %get-tuple-element.110), channel_id=1, source_target_pairs={{0,16},{1,17},{2,18},{3,19},{4,20},{5,21},{6,22},{7,23},{8,24},{9,... | collective-permute-start | bytes 196616 | tf_op jit(solution)/shard_map/ppermute | solution.py:404
  14.7 2.5 %shard_map.127 = (bf16[4,2,32,512]{3,2,1,0:T(8,128)(2,1)S(1)}, f32[256,512]{1,0:T(8,128)S(1)}, bf16[256,512]{1,0:T(8,128)(2,1)S(1)}) custom-call(s32[11]{0:T(128)S(1)} %stack.62.bits, bf16[2,32,512]{2,1,0:T(8,128)(2,1)S(1)} %get-tuple-element.115.f0, bf16[2,32,512]{2,1,0:T(8,128)(2,1)S(1)} %collective-permute-done.f1, ...), custom_call_target="tpu_custom_call" | custom-call | tf_op jit(solution)/shard_map/pallas_call | solution.py:365
  17.3 1.4 %collective-permute-done.7.c3 = bf16[2,32,512]{2,1,0:T(8,128)(2,1)S(1)} collective-permute-done((bf16[2,32,512]{2,1,0:T(8,128)(2,1)S(1)}, bf16[2,32,512]{2,1,0:T(8,128)(2,1)S(1)}, u32[]{:S(2)}, u32[]{:S(2)}) %collective-permute-start.7) | collective-permute-done | bytes 65568 | tf_op jit(solution)/shard_map/ppermute | solution.py:404
  18.7 6.0 %shard_map.128 = (bf16[2176,128]{1,0:T(8,128)(2,1)S(1)}, bf16[2048,128]{1,0:T(8,128)(2,1)S(1)}, bf16[2176,128]{1,0:T(8,128)(2,1)S(1)}, bf16[2048,128]{1,0:T(8,12...) custom-call(s32[11]{0:T(128)S(1)} %stack.62.bits, ...), custom_call_target="tpu_custom_call" | custom-call | tf_op jit(solution)/shard_map/pallas_call | solution.py:365
  25.3 2.9 %shard_map.130 = (bf16[2176,128]{1,0:T(8,128)(2,1)S(1)}, bf16[2176,128]{1,0:T(8,128)(2,1)S(1)}) custom-call(s32[11]{0:T(128)S(1)} %stack.62.bits, bf16[4,2,32,512]{3,2,1,0:T(8,128)(2,1)S(1)} %get-tuple-element.56.frames, bf16[4,2,16,512]{3,2,1,0:T(8,128)(2,1)S(1)} %collective-permute-done.3.near, bf16[4,2,16,512]{3,2,1,0:T(8,128)(2,1)S(1)} %collective-permute-done.4.side, ...), custom_call_target="tpu_custom_call" | custom-call | tf_op jit(solution)/shard_map/pallas_call | solution.py:365
  28.5 1.7 %collective-permute-start.9 = (bf16[1024,128]{1,0:T(8,128)(2,1)S(1)}, bf16[1024,128]{1,0:T(8,128)(2,1)S(1)}, u32[]{:S(2)}, u32[]{:S(2)}) collective-permute-start(bf16[1024,128]{1,0:T(8,128)(2,1)S(1)} %pad_maximum_fusion.2), channel_id=1, source_target_pairs={{0,16},{1,17},{2,18},{3,19},{4,20},{5,21},{6,22},{7,23},{8,24},{9,... | collective-permute-start | bytes 786440 | tf_op jit(solution)/shard_map/ppermute | solution.py:404
  30.2 0.8 add_convert_fusion.2
  31.0 1.6 %collective-permute-start.11 = (bf16[1024,128]{1,0:T(8,128)(2,1)}, bf16[1024,128]{1,0:T(8,128)(2,1)S(1)}, u32[]{:S(2)}, u32[]{:S(2)}) collective-permute-start(bf16[1024,128]{1,0:T(8,128)(2,1)} %get-tuple-element.100), channel_id=1, source_target_pairs={{0,2},{1,3},{2,0},{3,1},{4,6},{5,7},{6,4},{7,5},{8,10},{9,11},{10,... | collective-permute-start | bytes 786440 | tf_op jit(solution)/shard_map/ppermute | solution.py:404
  32.8 1.5 %collective-permute-start.13 = (bf16[1088,128]{1,0:T(8,128)(2,1)S(1)}, bf16[1088,128]{1,0:T(8,128)(2,1)S(1)}, u32[]{:S(2)}, u32[]{:S(2)}) collective-permute-start(bf16[1088,128]{1,0:T(8,128)(2,1)S(1)} %get-tuple-element.98), channel_id=1, source_target_pairs={{0,1},{1,0},{2,3},{3,2},{4,5},{5,4},{6,7},{7,6},{8,9},{9,8},{10,11... | collective-permute-start | bytes 835592 | tf_op jit(solution)/shard_map/ppermute | solution.py:404
  34.3 2.8 %collective-permute-done.9.y_got = bf16[1024,128]{1,0:T(8,128)(2,1)S(1)} collective-permute-done((bf16[1024,128]{1,0:T(8,128)(2,1)S(1)}, bf16[1024,128]{1,0:T(8,128)(2,1)S(1)}, u32[]{:S(2)}, u32[]{:S(2)}) %collective-permute-start.9) | collective-permute-done | bytes 262176 | tf_op jit(solution)/shard_map/ppermute | solution.py:404
  37.1 2.5 %collective-permute-done.11 = bf16[1024,128]{1,0:T(8,128)(2,1)S(1)} collective-permute-done((bf16[1024,128]{1,0:T(8,128)(2,1)}, bf16[1024,128]{1,0:T(8,128)(2,1)S(1)}, u32[]{:S(2)}, u32[]{:S(2)}) %collective-permute-start.11) | collective-permute-done | bytes 262176 | tf_op jit(solution)/shard_map/ppermute | solution.py:404
  39.6 1.3 %shard_map.129 = (bf16[2,128,512]{2,1,0:T(8,128)(2,1)}, bf16[2,4,128,128]{3,2,1,0:T(8,128)(2,1)S(1)}, bf16[128,128]{1,0:T(8,128)(2,1)S(1)}, bf16[128,128]{1,0:T(8,128)(2,1)S(1)}) custom-call(s32[11]{0:T(128)S(1)} %stack.62.bits, bf16[1024,128]{1,0:T(8,128)(2,1)S(1)} %get-tuple-element.60.own, bf16[1024,128]{1,0:T(8,128)(2,1)S(1)} %collective-permute-done.8.core_got, ...), custom_call_target="tpu_custom_call" | custom-call | tf_op jit(solution)/shard_map/pallas_call | solution.py:365
  40.9 1.5 %collective-permute-start.15 = (bf16[256,128]{1,0:T(8,128)(2,1)S(1)}, bf16[256,128]{1,0:T(8,128)(2,1)S(1)}, u32[]{:S(2)}, u32[]{:S(2)}) collective-permute-start(bf16[256,128]{1,0:T(8,128)(2,1)S(1)} %pad_maximum_fusion.6), channel_id=1, source_target_pairs={{0,1},{1,0},{2,3},{3,2},{4,5},{5,4},{6,7},{7,6},{8,9},{9,8},{10,11... | collective-permute-start | bytes 196616 | tf_op jit(solution)/shard_map/ppermute | solution.py:404
  42.5 1.5 %collective-permute-start.14 = (bf16[544,128]{1,0:T(8,128)(2,1)S(1)}, bf16[544,128]{1,0:T(8,128)(2,1)S(1)}, u32[]{:S(2)}, u32[]{:S(2)}) collective-permute-start(bf16[544,128]{1,0:T(8,128)(2,1)S(1)} %get-tuple-element.102), channel_id=1, source_target_pairs={{0,16},{1,17},{2,18},{3,19},{4,20},{5,21},{6,22},{7,23},{8,24},{9,... | collective-permute-start | bytes 417800 | tf_op jit(solution)/shard_map/ppermute | solution.py:404
  44.6 0.7 collective-permute-done.15.x_got
  45.2 2.4 %collective-permute-done.14 = bf16[544,128]{1,0:T(8,128)(2,1)S(1)} collective-permute-done((bf16[544,128]{1,0:T(8,128)(2,1)S(1)}, bf16[544,128]{1,0:T(8,128)(2,1)S(1)}, u32[]{:S(2)}, u32[]{:S(2)}) %collective-permute-start.14) | collective-permute-done | bytes 139296 | tf_op jit(solution)/shard_map/ppermute | solution.py:404
  47.7 1.6 %collective-permute-start.16 = (bf16[400,128]{1,0:T(8,128)(2,1)S(1)}, bf16[400,128]{1,0:T(8,128)(2,1)S(1)}, u32[]{:S(2)}, u32[]{:S(2)}) collective-permute-start(bf16[400,128]{1,0:T(8,128)(2,1)S(1)} %pad_maximum_fusion.5), channel_id=1, source_target_pairs={{0,2},{1,3},{2,0},{3,1},{4,6},{5,7},{6,4},{7,5},{8,10},{9,11},{10,... | collective-permute-start | bytes 307208 | tf_op jit(solution)/shard_map/ppermute | solution.py:404
  49.4 2.7 %collective-permute-start.22 = (bf16[256,128]{1,0:T(8,128)(2,1)S(1)}, bf16[256,128]{1,0:T(8,128)(2,1)S(1)}, u32[]{:S(2)}, u32[]{:S(2)}) collective-permute-start(bf16[256,128]{1,0:T(8,128)(2,1)S(1)} %get-tuple-element.108), channel_id=1, source_target_pairs={{0,4},{1,5},{2,6},{3,7},{4,0},{5,1},{6,2},{7,3},{8,12},{9,13},{10,... | collective-permute-start | bytes 196616 | tf_op jit(solution)/shard_map/ppermute | solution.py:404
  52.1 0.5 collective-permute-done.16
  52.6 3.0 %collective-permute-start.17 = (bf16[272,128]{1,0:T(8,128)(2,1)S(1)}, bf16[272,128]{1,0:T(8,128)(2,1)S(1)}, u32[]{:S(2)}, u32[]{:S(2)}) collective-permute-start(bf16[272,128]{1,0:T(8,128)(2,1)S(1)} %add_convert_fusion.9), channel_id=1, source_target_pairs={{0,4},{1,5},{2,6},{3,7},{4,0},{5,1},{6,2},{7,3},{8,12},{9,13},{10,... | collective-permute-start | bytes 208904 | tf_op jit(solution)/shard_map/ppermute | solution.py:404
  56.1 1.5 %collective-permute-start.23 = (bf16[256,128]{1,0:T(8,128)(2,1)S(1)}, bf16[256,128]{1,0:T(8,128)(2,1)S(1)}, u32[]{:S(2)}, u32[]{:S(2)}) collective-permute-start(bf16[256,128]{1,0:T(8,128)(2,1)S(1)} %add_convert_fusion.13), channel_id=1, source_target_pairs={{0,16},{1,17},{2,18},{3,19},{4,20},{5,21},{6,22},{7,23},{8,24},{9,... | collective-permute-start | bytes 196616 | tf_op jit(solution)/shard_map/ppermute | solution.py:404
  57.6 0.5 collective-permute-done.17
  58.2 1.5 %collective-permute-start.18 = (bf16[272,128]{1,0:T(8,128)(2,1)S(1)}, bf16[272,128]{1,0:T(8,128)(2,1)S(1)}, u32[]{:S(2)}, u32[]{:S(2)}) collective-permute-start(bf16[272,128]{1,0:T(8,128)(2,1)S(1)} %add_convert_fusion.8), channel_id=1, source_target_pairs={{0,2},{1,3},{2,0},{3,1},{4,6},{5,7},{6,4},{7,5},{8,10},{9,11},{10,... | collective-permute-start | bytes 208904 | tf_op jit(solution)/shard_map/ppermute | solution.py:404
  59.7 0.8 collective-permute-done.23
  60.5 2.3 %collective-permute-start.24 = (bf16[256,128]{1,0:T(8,128)(2,1)S(1)}, bf16[256,128]{1,0:T(8,128)(2,1)S(1)}, u32[]{:S(2)}, u32[]{:S(2)}) collective-permute-start(bf16[256,128]{1,0:T(8,128)(2,1)S(1)} %add_convert_fusion.12), channel_id=1, source_target_pairs={{0,4},{1,5},{2,6},{3,7},{4,0},{5,1},{6,2},{7,3},{8,12},{9,13},{10,... | collective-permute-start | bytes 196616 | tf_op jit(solution)/shard_map/ppermute | solution.py:404
  62.8 0.7 collective-permute-start.25
  63.5 0.5 collective-permute-start.19
  64.0 2.4 %collective-permute-done.24 = bf16[256,128]{1,0:T(8,128)(2,1)S(1)} collective-permute-done((bf16[256,128]{1,0:T(8,128)(2,1)S(1)}, bf16[256,128]{1,0:T(8,128)(2,1)S(1)}, u32[]{:S(2)}, u32[]{:S(2)}) %collective-permute-start.24) | collective-permute-done | bytes 65568 | tf_op jit(solution)/shard_map/ppermute | solution.py:404
  66.5 1.1 %collective-permute-start.26 = (bf16[512,128]{1,0:T(8,128)(2,1)S(1)}, bf16[512,128]{1,0:T(8,128)(2,1)S(1)}, u32[]{:S(2)}, u32[]{:S(2)}) collective-permute-start(bf16[512,128]{1,0:T(8,128)(2,1)S(1)} %pad_maximum_fusion.4), channel_id=1, source_target_pairs={{0,1},{1,0},{2,3},{3,2},{4,5},{5,4},{6,7},{7,6},{8,9},{9,8},{10,11... | collective-permute-start | bytes 393224 | tf_op jit(solution)/shard_map/ppermute | solution.py:404
  67.5 1.1 %collective-permute-done.19 = bf16[544,128]{1,0:T(8,128)(2,1)S(1)} collective-permute-done((bf16[544,128]{1,0:T(8,128)(2,1)S(1)}, bf16[544,128]{1,0:T(8,128)(2,1)S(1)}, u32[]{:S(2)}, u32[]{:S(2)}) %collective-permute-start.19) | collective-permute-done | bytes 139296 | tf_op jit(solution)/shard_map/ppermute | solution.py:404
  68.7 0.6 collective-permute-start.20
  69.3 2.2 %collective-permute-done.26 = bf16[512,128]{1,0:T(8,128)(2,1)S(1)} collective-permute-done((bf16[512,128]{1,0:T(8,128)(2,1)S(1)}, bf16[512,128]{1,0:T(8,128)(2,1)S(1)}, u32[]{:S(2)}, u32[]{:S(2)}) %collective-permute-start.26) | collective-permute-done | bytes 131104 | tf_op jit(solution)/shard_map/ppermute | solution.py:404
  71.6 4.0 %collective-permute-start.27 = (bf16[1024,128]{1,0:T(8,128)(2,1)S(1)}, bf16[1024,128]{1,0:T(8,128)(2,1)S(1)}, u32[]{:S(2)}, u32[]{:S(2)}) collective-permute-start(bf16[1024,128]{1,0:T(8,128)(2,1)S(1)} %constant_dynamic-update-slice_fusion.refs_1_), channel_id=1, source_target_pairs={{0,2},{1,3},{2,0},{3,1},{4,6},{5,7},{6,4},{7,5},{8,10},{9,11},{10,... | collective-permute-start | bytes 786440 | tf_op jit(solution)/shard_map/ppermute | solution.py:404
  75.6 2.8 %shard_map.131 = bf16[2,128,512]{2,1,0:T(8,128)(2,1)} custom-call(s32[11]{0:T(128)S(1)} %stack.62.bits, bf16[2,4,128,128]{3,2,1,0:T(8,128)(2,1)S(1)} %get-tuple-element.76.dconv, bf16[256,128]{1,0:T(8,128)(2,1)S(1)} %collective-permute-done.15.x_got, bf16[128,128]{1,0:T(8,128)(2,1)S(1)} %slice.134.z_got, ...), custom_call_target="tpu_custom_call" | custom-call | tf_op jit(solution)/shard_map/pallas_call | solution.py:365
  78.4 2.0 %shard_map.132 = (f32[512,512]{1,0:T(8,128)}, f32[512,512]{1,0:T(8,128)}, f32[512,512]{1,0:T(8,128)}, f32[512,512]{1,0:T(8,128)}) custom-call(s32[11]{0:T(128)S(1)} %stack.62.bits, bf16[1088,128]{1,0:T(8,128)(2,1)S(1)} %pad_maximum_fusion.1.refs_0_.refs_2_, bf16[1024,128]{1,0:T(8,128)(2,1)S(1)} %constant_dynamic-update-slice_fusion.refs_1_, ...), custom_call_target="tpu_custom_call" | custom-call | tf_op jit(solution)/shard_map/pallas_call | solution.py:365
  80.5 2.1 %collective-permute-done.27.refs_1_ = bf16[1024,128]{1,0:T(8,128)(2,1)S(1)} collective-permute-done((bf16[1024,128]{1,0:T(8,128)(2,1)S(1)}, bf16[1024,128]{1,0:T(8,128)(2,1)S(1)}, u32[]{:S(2)}, u32[]{:S(2)}) %collective-permute-start.27) | collective-permute-done | bytes 262176 | tf_op jit(solution)/shard_map/ppermute | solution.py:404
  82.5 0.5 collective-permute-start.31
  83.0 1.6 %shard_map.133 = (f32[512,512]{1,0:T(8,128)}, f32[512,512]{1,0:T(8,128)}, f32[512,512]{1,0:T(8,128)}, f32[512,512]{1,0:T(8,128)}) custom-call(s32[11]{0:T(128)S(1)} %stack.62.bits, bf16[1088,128]{1,0:T(8,128)(2,1)S(1)} %collective-permute-done.20.refs_0_.refs_3_, ...), custom_call_target="tpu_custom_call", output_to_operand_aliasing={{0}: (3, {}), {1}: (4, {}), {2}: (5, {}), {3}: (6, {})} | custom-call | tf_op jit(solution)/shard_map/pallas_call | solution.py:365
  84.6 2.2 %shard_map.134 = (f32[512,512]{1,0:T(8,128)}, f32[512,512]{1,0:T(8,128)}, f32[512,512]{1,0:T(8,128)}, f32[512,512]{1,0:T(8,128)}, f32[31,512]{1,0:T(8,128)}) custom-call(s32[11]{0:T(128)S(1)} %stack.62.bits, bf16[1088,128]{1,0:T(8,128)(2,1)S(1)} %collective-permute-done.30.refs_0_.refs_5_, ...), custom_call_target="tpu_custom_call", output_to_operand_aliasing={{0}: (7, {}), {1}: (8, {}), {2}: (9, {}), {3}: (10, {})} | custom-call | tf_op jit(solution)/shard_map/pallas_call | solution.py:365
  (55 shorter events, 3.1 us)
Async XLA Ops:
  1.7 5.2 %collective-permute-start = (bf16[2,32,512]{2,1,0:T(8,128)(2,1)S(1)}, bf16[2,32,512]{2,1,0:T(8,128)(2,1)S(1)}, u32[]{:S(2)}, u32[]{:S(2)}) collective-permute-start(bf16[2,32,512]{2,1,0:T(8,128)(2,1)S(1)} %get-tuple-element.114), channel_id=1, source_target_pairs={{0,8},{1,9},{2,10},{3,11},{4,12},{5,13},{6,14},{7,15},{8,0},{9,1},... | collective-permute-start | bytes 196616 | tf_op jit(solution)/shard_map/ppermute | solution.py:404
  2.2 5.3 %collective-permute-start.1 = (bf16[2,32,512]{2,1,0:T(8,128)(2,1)S(1)}, bf16[2,32,512]{2,1,0:T(8,128)(2,1)S(1)}, u32[]{:S(2)}, u32[]{:S(2)}) collective-permute-start(bf16[2,32,512]{2,1,0:T(8,128)(2,1)S(1)} %get-tuple-element.116), channel_id=1, source_target_pairs={{0,16},{1,17},{2,18},{3,19},{4,20},{5,21},{6,22},{7,23},{8,24},{9,... | collective-permute-start | bytes 196616 | tf_op jit(solution)/shard_map/ppermute | solution.py:404
  4.8 4.0 %collective-permute-start.2 = (bf16[2,32,512]{2,1,0:T(8,128)(2,1)S(1)}, bf16[2,32,512]{2,1,0:T(8,128)(2,1)S(1)}, u32[]{:S(2)}, u32[]{:S(2)}) collective-permute-start(bf16[2,32,512]{2,1,0:T(8,128)(2,1)S(1)} %get-tuple-element.113), channel_id=1, source_target_pairs={{0,24},{1,25},{2,26},{3,27},{4,28},{5,29},{6,30},{7,31},{8,16},{9,... | collective-permute-start | bytes 196616 | tf_op jit(solution)/shard_map/ppermute | solution.py:404
  4.8 5.4 %copy-start = (bf16[2,128,512]{2,1,0:T(8,128)(2,1)S(1)}, bf16[2,128,512]{2,1,0:T(8,128)(2,1)}, u32[]{:S(2)}) copy-start(bf16[2,128,512]{2,1,0:T(8,128)(2,1)} %cot.1) | copy-start | bytes 786436
  4.8 9.9 %copy-start.1 = (f32[31,512]{1,0:T(8,128)S(1)}, f32[31,512]{1,0:T(8,128)}, u32[]{:S(2)}) copy-start(f32[31,512]{1,0:T(8,128)} %kern.3) | copy-start | bytes 190468
  9.4 5.3 %collective-permute-start.3 = (bf16[4,2,16,512]{3,2,1,0:T(8,128)(2,1)S(1)}, bf16[4,2,16,512]{3,2,1,0:T(8,128)(2,1)S(1)}, u32[]{:S(2)}, u32[]{:S(2)}) collective-permute-start(bf16[4,2,16,512]{3,2,1,0:T(8,128)(2,1)S(1)} %get-tuple-element.54), channel_id=1, source_target_pairs={{0,8},{1,9},{2,10},{3,11},{4,12},{5,13},{6,14},{7,15},{8,0},{9,1},... | collective-permute-start | bytes 393224 | tf_op jit(solution)/shard_map/ppermute | solution.py:404
  9.6 5.1 %collective-permute-start.4 = (bf16[4,2,16,512]{3,2,1,0:T(8,128)(2,1)S(1)}, bf16[4,2,16,512]{3,2,1,0:T(8,128)(2,1)S(1)}, u32[]{:S(2)}, u32[]{:S(2)}) collective-permute-start(bf16[4,2,16,512]{3,2,1,0:T(8,128)(2,1)S(1)} %get-tuple-element.55), channel_id=1, source_target_pairs={{8,24},{9,25},{10,26},{11,27},{12,28},{13,29},{14,30},{15,31},{24,... | collective-permute-start | bytes 393224 | tf_op jit(solution)/shard_map/ppermute | solution.py:404
  10.3 6.9 %collective-permute-start.5 = (bf16[2,32,512]{2,1,0:T(8,128)(2,1)S(1)}, bf16[2,32,512]{2,1,0:T(8,128)(2,1)S(1)}, u32[]{:S(2)}, u32[]{:S(2)}) collective-permute-start(bf16[2,32,512]{2,1,0:T(8,128)(2,1)S(1)} %get-tuple-element.111), channel_id=1, source_target_pairs={{0,8},{1,9},{2,10},{3,11},{4,12},{5,13},{6,14},{7,15},{8,0},{9,1},... | collective-permute-start | bytes 196616 | tf_op jit(solution)/shard_map/ppermute | solution.py:404
  13.0 4.3 %collective-permute-start.6 = (bf16[2,32,512]{2,1,0:T(8,128)(2,1)S(1)}, bf16[2,32,512]{2,1,0:T(8,128)(2,1)S(1)}, u32[]{:S(2)}, u32[]{:S(2)}) collective-permute-start(bf16[2,32,512]{2,1,0:T(8,128)(2,1)S(1)} %get-tuple-element.110), channel_id=1, source_target_pairs={{0,16},{1,17},{2,18},{3,19},{4,20},{5,21},{6,22},{7,23},{8,24},{9,... | collective-permute-start | bytes 196616 | tf_op jit(solution)/shard_map/ppermute | solution.py:404
  14.7 4.0 %collective-permute-start.7 = (bf16[2,32,512]{2,1,0:T(8,128)(2,1)S(1)}, bf16[2,32,512]{2,1,0:T(8,128)(2,1)S(1)}, u32[]{:S(2)}, u32[]{:S(2)}) collective-permute-start(bf16[2,32,512]{2,1,0:T(8,128)(2,1)S(1)} %get-tuple-element.109), channel_id=1, source_target_pairs={{0,24},{1,25},{2,26},{3,27},{4,28},{5,29},{6,30},{7,31},{8,16},{9,... | collective-permute-start | bytes 196616 | tf_op jit(solution)/shard_map/ppermute | solution.py:404
  24.7 5.5 %collective-permute-start.10 = (bf16[2048,128]{1,0:T(8,128)(2,1)S(1)}, bf16[2048,128]{1,0:T(8,128)(2,1)S(1)}, u32[]{:S(2)}, u32[]{:S(2)}) collective-permute-start(bf16[2048,128]{1,0:T(8,128)(2,1)S(1)} %get-tuple-element.63), channel_id=1, source_target_pairs={{0,8},{1,9},{2,10},{3,11},{4,12},{5,13},{6,14},{7,15},{8,0},{9,1},... | collective-permute-start | bytes 1572872 | tf_op jit(solution)/shard_map/ppermute | solution.py:404
  25.0 3.5 %collective-permute-start.8 = (bf16[1024,128]{1,0:T(8,128)(2,1)S(1)}, bf16[1024,128]{1,0:T(8,128)(2,1)S(1)}, u32[]{:S(2)}, u32[]{:S(2)}) collective-permute-start(bf16[1024,128]{1,0:T(8,128)(2,1)S(1)} %get-tuple-element.61), channel_id=1, source_target_pairs={{0,8},{1,9},{2,10},{3,11},{4,12},{5,13},{6,14},{7,15},{8,0},{9,1},... | collective-permute-start | bytes 786440 | tf_op jit(solution)/shard_map/ppermute | solution.py:404
  28.2 4.4 %collective-permute-start.12 = (bf16[2176,128]{1,0:T(8,128)(2,1)S(1)}, bf16[2176,128]{1,0:T(8,128)(2,1)S(1)}, u32[]{:S(2)}, u32[]{:S(2)}) collective-permute-start(bf16[2176,128]{1,0:T(8,128)(2,1)S(1)} %get-tuple-element.70), channel_id=1, source_target_pairs={{0,8},{1,9},{2,10},{3,11},{4,12},{5,13},{6,14},{7,15},{8,0},{9,1},... | collective-permute-start | bytes 1671176 | tf_op jit(solution)/shard_map/ppermute | solution.py:404
  28.5 8.6 %collective-permute-start.9 = (bf16[1024,128]{1,0:T(8,128)(2,1)S(1)}, bf16[1024,128]{1,0:T(8,128)(2,1)S(1)}, u32[]{:S(2)}, u32[]{:S(2)}) collective-permute-start(bf16[1024,128]{1,0:T(8,128)(2,1)S(1)} %pad_maximum_fusion.2), channel_id=1, source_target_pairs={{0,16},{1,17},{2,18},{3,19},{4,20},{5,21},{6,22},{7,23},{8,24},{9,... | collective-permute-start | bytes 786440 | tf_op jit(solution)/shard_map/ppermute | solution.py:404
  31.0 8.6 %collective-permute-start.11 = (bf16[1024,128]{1,0:T(8,128)(2,1)}, bf16[1024,128]{1,0:T(8,128)(2,1)S(1)}, u32[]{:S(2)}, u32[]{:S(2)}) collective-permute-start(bf16[1024,128]{1,0:T(8,128)(2,1)} %get-tuple-element.100), channel_id=1, source_target_pairs={{0,2},{1,3},{2,0},{3,1},{4,6},{5,7},{6,4},{7,5},{8,10},{9,11},{10,... | collective-permute-start | bytes 786440 | tf_op jit(solution)/shard_map/ppermute | solution.py:404
  32.8 9.6 %collective-permute-start.13 = (bf16[1088,128]{1,0:T(8,128)(2,1)S(1)}, bf16[1088,128]{1,0:T(8,128)(2,1)S(1)}, u32[]{:S(2)}, u32[]{:S(2)}) collective-permute-start(bf16[1088,128]{1,0:T(8,128)(2,1)S(1)} %get-tuple-element.98), channel_id=1, source_target_pairs={{0,1},{1,0},{2,3},{3,2},{4,5},{5,4},{6,7},{7,6},{8,9},{9,8},{10,11... | collective-permute-start | bytes 835592 | tf_op jit(solution)/shard_map/ppermute | solution.py:404
  40.9 4.3 %collective-permute-start.15 = (bf16[256,128]{1,0:T(8,128)(2,1)S(1)}, bf16[256,128]{1,0:T(8,128)(2,1)S(1)}, u32[]{:S(2)}, u32[]{:S(2)}) collective-permute-start(bf16[256,128]{1,0:T(8,128)(2,1)S(1)} %pad_maximum_fusion.6), channel_id=1, source_target_pairs={{0,1},{1,0},{2,3},{3,2},{4,5},{5,4},{6,7},{7,6},{8,9},{9,8},{10,11... | collective-permute-start | bytes 196616 | tf_op jit(solution)/shard_map/ppermute | solution.py:404
  42.5 5.1 %collective-permute-start.14 = (bf16[544,128]{1,0:T(8,128)(2,1)S(1)}, bf16[544,128]{1,0:T(8,128)(2,1)S(1)}, u32[]{:S(2)}, u32[]{:S(2)}) collective-permute-start(bf16[544,128]{1,0:T(8,128)(2,1)S(1)} %get-tuple-element.102), channel_id=1, source_target_pairs={{0,16},{1,17},{2,18},{3,19},{4,20},{5,21},{6,22},{7,23},{8,24},{9,... | collective-permute-start | bytes 417800 | tf_op jit(solution)/shard_map/ppermute | solution.py:404
  44.1 5.2 %collective-permute-start.21 = (bf16[512,128]{1,0:T(8,128)(2,1)S(1)}, bf16[512,128]{1,0:T(8,128)(2,1)S(1)}, u32[]{:S(2)}, u32[]{:S(2)}) collective-permute-start(bf16[512,128]{1,0:T(8,128)(2,1)S(1)} %get-tuple-element.104), channel_id=1, source_target_pairs={{0,1},{1,0},{2,3},{3,2},{4,5},{5,4},{6,7},{7,6},{8,9},{9,8},{10,11... | collective-permute-start | bytes 393224 | tf_op jit(solution)/shard_map/ppermute | solution.py:404
  47.7 4.9 %collective-permute-start.16 = (bf16[400,128]{1,0:T(8,128)(2,1)S(1)}, bf16[400,128]{1,0:T(8,128)(2,1)S(1)}, u32[]{:S(2)}, u32[]{:S(2)}) collective-permute-start(bf16[400,128]{1,0:T(8,128)(2,1)S(1)} %pad_maximum_fusion.5), channel_id=1, source_target_pairs={{0,2},{1,3},{2,0},{3,1},{4,6},{5,7},{6,4},{7,5},{8,10},{9,11},{10,... | collective-permute-start | bytes 307208 | tf_op jit(solution)/shard_map/ppermute | solution.py:404
  49.4 6.7 %collective-permute-start.22 = (bf16[256,128]{1,0:T(8,128)(2,1)S(1)}, bf16[256,128]{1,0:T(8,128)(2,1)S(1)}, u32[]{:S(2)}, u32[]{:S(2)}) collective-permute-start(bf16[256,128]{1,0:T(8,128)(2,1)S(1)} %get-tuple-element.108), channel_id=1, source_target_pairs={{0,4},{1,5},{2,6},{3,7},{4,0},{5,1},{6,2},{7,3},{8,12},{9,13},{10,... | collective-permute-start | bytes 196616 | tf_op jit(solution)/shard_map/ppermute | solution.py:404
  52.6 5.6 %collective-permute-start.17 = (bf16[272,128]{1,0:T(8,128)(2,1)S(1)}, bf16[272,128]{1,0:T(8,128)(2,1)S(1)}, u32[]{:S(2)}, u32[]{:S(2)}) collective-permute-start(bf16[272,128]{1,0:T(8,128)(2,1)S(1)} %add_convert_fusion.9), channel_id=1, source_target_pairs={{0,4},{1,5},{2,6},{3,7},{4,0},{5,1},{6,2},{7,3},{8,12},{9,13},{10,... | collective-permute-start | bytes 208904 | tf_op jit(solution)/shard_map/ppermute | solution.py:404
  56.1 4.3 %collective-permute-start.23 = (bf16[256,128]{1,0:T(8,128)(2,1)S(1)}, bf16[256,128]{1,0:T(8,128)(2,1)S(1)}, u32[]{:S(2)}, u32[]{:S(2)}) collective-permute-start(bf16[256,128]{1,0:T(8,128)(2,1)S(1)} %add_convert_fusion.13), channel_id=1, source_target_pairs={{0,16},{1,17},{2,18},{3,19},{4,20},{5,21},{6,22},{7,23},{8,24},{9,... | collective-permute-start | bytes 196616 | tf_op jit(solution)/shard_map/ppermute | solution.py:404
  58.2 5.3 %collective-permute-start.18 = (bf16[272,128]{1,0:T(8,128)(2,1)S(1)}, bf16[272,128]{1,0:T(8,128)(2,1)S(1)}, u32[]{:S(2)}, u32[]{:S(2)}) collective-permute-start(bf16[272,128]{1,0:T(8,128)(2,1)S(1)} %add_convert_fusion.8), channel_id=1, source_target_pairs={{0,2},{1,3},{2,0},{3,1},{4,6},{5,7},{6,4},{7,5},{8,10},{9,11},{10,... | collective-permute-start | bytes 208904 | tf_op jit(solution)/shard_map/ppermute | solution.py:404
  60.5 5.9 %collective-permute-start.24 = (bf16[256,128]{1,0:T(8,128)(2,1)S(1)}, bf16[256,128]{1,0:T(8,128)(2,1)S(1)}, u32[]{:S(2)}, u32[]{:S(2)}) collective-permute-start(bf16[256,128]{1,0:T(8,128)(2,1)S(1)} %add_convert_fusion.12), channel_id=1, source_target_pairs={{0,4},{1,5},{2,6},{3,7},{4,0},{5,1},{6,2},{7,3},{8,12},{9,13},{10,... | collective-permute-start | bytes 196616 | tf_op jit(solution)/shard_map/ppermute | solution.py:404
  62.8 3.7 %collective-permute-start.25 = (bf16[128,128]{1,0:T(8,128)(2,1)S(1)}, bf16[128,128]{1,0:T(8,128)(2,1)S(1)}, u32[]{:S(2)}, u32[]{:S(2)}) collective-permute-start(bf16[128,128]{1,0:T(8,128)(2,1)S(1)} %constant_dynamic-slice_fusion), channel_id=1, source_target_pairs={{2,4},{3,5},{10,12},{11,13},{18,20},{19,21},{26,28},{27,29},{4,2},... | collective-permute-start | bytes 98312 | tf_op jit(solution)/shard_map/ppermute | solution.py:404
  63.5 5.1 %collective-permute-start.19 = (bf16[544,128]{1,0:T(8,128)(2,1)S(1)}, bf16[544,128]{1,0:T(8,128)(2,1)S(1)}, u32[]{:S(2)}, u32[]{:S(2)}) collective-permute-start(bf16[544,128]{1,0:T(8,128)(2,1)S(1)} %pad_maximum_fusion.3), channel_id=1, source_target_pairs={{0,16},{1,17},{2,18},{3,19},{4,20},{5,21},{6,22},{7,23},{8,24},{9,... | collective-permute-start | bytes 417800 | tf_op jit(solution)/shard_map/ppermute | solution.py:404
  66.5 5.0 %collective-permute-start.26 = (bf16[512,128]{1,0:T(8,128)(2,1)S(1)}, bf16[512,128]{1,0:T(8,128)(2,1)S(1)}, u32[]{:S(2)}, u32[]{:S(2)}) collective-permute-start(bf16[512,128]{1,0:T(8,128)(2,1)S(1)} %pad_maximum_fusion.4), channel_id=1, source_target_pairs={{0,1},{1,0},{2,3},{3,2},{4,5},{5,4},{6,7},{7,6},{8,9},{9,8},{10,11... | collective-permute-start | bytes 393224 | tf_op jit(solution)/shard_map/ppermute | solution.py:404
  68.6 9.8 %collective-permute-start.28 = (bf16[1088,128]{1,0:T(8,128)(2,1)S(1)}, bf16[1088,128]{1,0:T(8,128)(2,1)S(1)}, u32[]{:S(2)}, u32[]{:S(2)}) collective-permute-start(bf16[1088,128]{1,0:T(8,128)(2,1)S(1)} %pad_maximum_fusion.1.refs_0_.refs_2_), channel_id=1, source_target_pairs={{0,8},{1,9},{2,10},{3,11},{4,12},{5,13},{6,14},{7,15},{8,0},{9,1},... | collective-permute-start | bytes 835592 | tf_op jit(solution)/shard_map/ppermute | solution.py:404
  68.7 13.8 %collective-permute-start.20 = (bf16[1088,128]{1,0:T(8,128)(2,1)S(1)}, bf16[1088,128]{1,0:T(8,128)(2,1)S(1)}, u32[]{:S(2)}, u32[]{:S(2)}) collective-permute-start(bf16[1088,128]{1,0:T(8,128)(2,1)S(1)} %pad_maximum_fusion.1.refs_0_.refs_2_), channel_id=1, source_target_pairs={{0,1},{1,0},{2,3},{3,2},{4,5},{5,4},{6,7},{7,6},{8,9},{9,8},{10,11... | collective-permute-start | bytes 835592 | tf_op jit(solution)/shard_map/ppermute | solution.py:404
  71.5 6.9 %collective-permute-start.29 = (bf16[1024,128]{1,0:T(8,128)(2,1)S(1)}, bf16[1024,128]{1,0:T(8,128)(2,1)S(1)}, u32[]{:S(2)}, u32[]{:S(2)}) collective-permute-start(bf16[1024,128]{1,0:T(8,128)(2,1)S(1)} %constant_dynamic-update-slice_fusion.refs_1_), channel_id=1, source_target_pairs={{0,8},{1,9},{2,10},{3,11},{4,12},{5,13},{6,14},{7,15},{8,0},{9,1},... | collective-permute-start | bytes 786440 | tf_op jit(solution)/shard_map/ppermute | solution.py:404
  71.6 10.9 %collective-permute-start.27 = (bf16[1024,128]{1,0:T(8,128)(2,1)S(1)}, bf16[1024,128]{1,0:T(8,128)(2,1)S(1)}, u32[]{:S(2)}, u32[]{:S(2)}) collective-permute-start(bf16[1024,128]{1,0:T(8,128)(2,1)S(1)} %constant_dynamic-update-slice_fusion.refs_1_), channel_id=1, source_target_pairs={{0,2},{1,3},{2,0},{3,1},{4,6},{5,7},{6,4},{7,5},{8,10},{9,11},{10,... | collective-permute-start | bytes 786440 | tf_op jit(solution)/shard_map/ppermute | solution.py:404
  82.5 2.1 %collective-permute-start.30 = (bf16[1088,128]{1,0:T(8,128)(2,1)S(1)}, bf16[1088,128]{1,0:T(8,128)(2,1)S(1)}, u32[]{:S(2)}, u32[]{:S(2)}) collective-permute-start(bf16[1088,128]{1,0:T(8,128)(2,1)S(1)} %collective-permute-done.20.refs_0_.refs_3_), channel_id=1, source_target_pairs={{0,8},{1,9},{2,10},{3,11},{4,12},{5,13},{6,14},{7,15},{8,0},{9,1},... | collective-permute-start | bytes 835592 | tf_op jit(solution)/shard_map/ppermute | solution.py:404
  82.5 2.1 %collective-permute-start.31 = (bf16[1024,128]{1,0:T(8,128)(2,1)S(1)}, bf16[1024,128]{1,0:T(8,128)(2,1)S(1)}, u32[]{:S(2)}, u32[]{:S(2)}) collective-permute-start(bf16[1024,128]{1,0:T(8,128)(2,1)S(1)} %collective-permute-done.27.refs_1_), channel_id=1, source_target_pairs={{0,8},{1,9},{2,10},{3,11},{4,12},{5,13},{6,14},{7,15},{8,0},{9,1},... | collective-permute-start | bytes 786440 | tf_op jit(solution)/shard_map/ppermute | solution.py:404

commit v18 on v17

--- a/solution.py
+++ b/solution.py
@@ -489,8 +489,10 @@
     a = [a_keep, swap(a_send, over_core)]
     b = [b_keep, swap(b_send, over_core)]
     core_got = swap(back_send, over_core)
-    a = halved(a, over_x)
+    a_sent = total(*(t[4 * span :] for t in a))
+    a = [kept(a, 4 * span), swap(a_sent, over_x)]
     b = halved(b, lines[0])
+    core_got = after(core_got, a_sent)
     y_got = swap(jnp.concatenate([back_keep[unit:], core_got[unit:]]), over_y)
     y_got = after(y_got, b[-1])
     edge = flat(count * cols * HALO)
@@ -509,15 +511,10 @@
     b = halved(b, lines[1])
     a = exchanged(a, lines[1:])
     b = exchanged(b, [over_y] + lines[2:])
-    other_got = permute(
-        after(passed, a),
-        both([(m * blocks + t, m * blocks + t + 2)
-              for m in range(groups) for t in range(2, blocks - 2) if t // 2 % 2]),
-    )
     a = doubled(a, lines[0])
     b = doubled(b, lines[1])
     a = doubled(a, over_y)
-    b = doubled(after(b, other_got), over_x)
+    b = doubled(b, over_x)
 
     norm = 1.0 / math.sqrt(groups * count * blocks * length)
     square = shape((width, width), F32)
@@ -537,6 +534,11 @@
         )
 
     a_far, b_far = swap(a, over_x), swap(b, lines[0])
+    other_got = permute(
+        after(passed, (a, b)),
+        both([(m * blocks + t, m * blocks + t + 2)
+              for m in range(groups) for t in range(2, blocks - 2) if t // 2 % 2]),
+    )
     a_other, b_other = swap(a, over_core), swap(b, over_core)
     (frame_grad,) = call(
         functools.partial(frame_kernel, (count, cols, length)),

time: 87.1 us -> 87.2 us (level); the launches traced: 86.9 us -> 85.7 us
  starting transfers between devices: 37.7 us -> 30.7 us
  waiting for transfers between devices: 21.9 us -> 28.4 us
    ppermute x32, starting transfers between devices: 37.7 us -> 30.7 us  [permute(): return lax.ppermute(x, ('mic', 'tm'), pairs)]
    ppermute x32, waiting for transfers between devices: 21.9 us -> 28.4 us  [permute(): return lax.ppermute(x, ('mic', 'tm'), pairs)]
  transfers between devices with their start and end apart: 32 -> 32, of which waited for: 16 -> 17; matrix products, arithmetic and copies ran while one was open for 4% -> 3% of each run, Pallas kernels for 15% -> 15%
where the time goes in v18:
time: 87.2 us; the launch traced here: 85.7 us
  starting transfers between devices  30.7 us (35%)
  waiting for transfers between devices  28.4 us (33%)
  Pallas kernels  21.9 us (25%)
  other arithmetic  2.51 us (3%)
  local copies, waits for them, and re-layouts  1.12 us (1%)
  between operations  1.08 us (1%)
    ppermute x32, starting transfers between devices, permute(): return lax.ppermute(x, ('mic', 'tm'), pairs)  30.7 us
    ppermute x32, waiting for transfers between devices, permute(): return lax.ppermute(x, ('mic', 'tm'), pairs)  28.4 us
    pallas_call x9, Pallas kernels, call(): pl.pallas_call(body, out_shape=outs, in_specs=[pl.BlockSpec(memory_space=...  21.9 us
    another operation x1, other arithmetic, shards(): weights = jnp.stack([w_query, w_key, w_value, w_out])  1.82 us
  transfers between devices with their start and end apart: 32, of which 17 were waited for; matrix products, arithmetic and copies ran while one was open for 3% of the time, Pallas kernels for 15%

profile of v18, /device:TPU:0, one launch (start us, length us, event | category | flops | bytes accessed | tf_op | source)
XLA Modules:
  0.0 85.7 jit_solution(4082116391212997171)
XLA Ops:
  0.7 1.0 %constant_dynamic-slice_fusion.5 = (bf16[2,32,512]{2,1,0:T(8,128)(2,1)S(1)}, bf16[2,32,512]{2,1,0:T(8,128)(2,1)S(1)}, bf16[2,32,512]{2,1,0:T(8,128)(2,1)S(1)}, bf16[2,32,512]{2,1,0:T(8,128)(2,1)S(1)}) fusion(bf16[2,128,512]{2,1,0:T(8,128)(2,1)} %param.7, s32[]{:T(128)S(6)} %select_n.100, s32[]{:T(128)S(6)} %select_n.98, s32[]{:T(128)S(6)} %select_n.97, ...), kind=kLoop, calls=%fused_computation.29 | loop fusion | bytes 524304 | tf_op jit(solution)/shard_map/dynamic_slice | solution.py:415
  1.7 0.5 collective-permute-start
  2.2 2.6 %collective-permute-start.1 = (bf16[2,32,512]{2,1,0:T(8,128)(2,1)S(1)}, bf16[2,32,512]{2,1,0:T(8,128)(2,1)S(1)}, u32[]{:S(2)}, u32[]{:S(2)}) collective-permute-start(bf16[2,32,512]{2,1,0:T(8,128)(2,1)S(1)} %get-tuple-element.116), channel_id=1, source_target_pairs={{0,16},{1,17},{2,18},{3,19},{4,20},{5,21},{6,22},{7,23},{8,24},{9,... | collective-permute-start | bytes 196616 | tf_op jit(solution)/shard_map/ppermute | solution.py:404
  4.8 1.8 %pad_maximum_fusion.weights = bf16[4,512,512]{2,1,0:T(8,128)(2,1)S(1)} fusion(bf16[1,512,512]{2,1,0:T(8,128)(2,1)} %bitcast.15, bf16[1,512,512]{2,1,0:T(8,128)(2,1)} %bitcast.16, bf16[1,512,512]{2,1,0:T(8,128)(2,1)} %bitcast.17, bf16[1,512,512]{2,1,0:T(8,128)(2,1)} %bitcast.18), kind=kLoop, calls=%fused_computation | loop fusion | flops 3145728 | bytes 4194304 | tf_op jit(solution)/shard_map/stack | solution.py:423
  6.9 0.6 collective-permute-done.1.f2
  7.5 1.4 %collective-permute-done.2.f3 = bf16[2,32,512]{2,1,0:T(8,128)(2,1)S(1)} collective-permute-done((bf16[2,32,512]{2,1,0:T(8,128)(2,1)S(1)}, bf16[2,32,512]{2,1,0:T(8,128)(2,1)S(1)}, u32[]{:S(2)}, u32[]{:S(2)}) %collective-permute-start.2) | collective-permute-done | bytes 65568 | tf_op jit(solution)/shard_map/ppermute | solution.py:404
  8.8 0.6 shard_map.126
  9.6 0.7 collective-permute-start.4
  10.3 2.7 %collective-permute-start.5 = (bf16[2,32,512]{2,1,0:T(8,128)(2,1)S(1)}, bf16[2,32,512]{2,1,0:T(8,128)(2,1)S(1)}, u32[]{:S(2)}, u32[]{:S(2)}) collective-permute-start(bf16[2,32,512]{2,1,0:T(8,128)(2,1)S(1)} %get-tuple-element.111), channel_id=1, source_target_pairs={{0,8},{1,9},{2,10},{3,11},{4,12},{5,13},{6,14},{7,15},{8,0},{9,1},... | collective-permute-start | bytes 196616 | tf_op jit(solution)/shard_map/ppermute | solution.py:404
  13.0 1.6 %collective-permute-start.6 = (bf16[2,32,512]{2,1,0:T(8,128)(2,1)S(1)}, bf16[2,32,512]{2,1,0:T(8,128)(2,1)S(1)}, u32[]{:S(2)}, u32[]{:S(2)}) collective-permute-start(bf16[2,32,512]{2,1,0:T(8,128)(2,1)S(1)} %get-tuple-element.110), channel_id=1, source_target_pairs={{0,16},{1,17},{2,18},{3,19},{4,20},{5,21},{6,22},{7,23},{8,24},{9,... | collective-permute-start | bytes 196616 | tf_op jit(solution)/shard_map/ppermute | solution.py:404
  14.7 2.5 %shard_map.127 = (bf16[4,2,32,512]{3,2,1,0:T(8,128)(2,1)S(1)}, f32[256,512]{1,0:T(8,128)S(1)}, bf16[256,512]{1,0:T(8,128)(2,1)S(1)}) custom-call(s32[11]{0:T(128)S(1)} %stack.62.bits, bf16[2,32,512]{2,1,0:T(8,128)(2,1)S(1)} %get-tuple-element.115.f0, bf16[2,32,512]{2,1,0:T(8,128)(2,1)S(1)} %collective-permute-done.f1, ...), custom_call_target="tpu_custom_call" | custom-call | tf_op jit(solution)/shard_map/pallas_call | solution.py:365
  17.3 1.4 %collective-permute-done.7.c3 = bf16[2,32,512]{2,1,0:T(8,128)(2,1)S(1)} collective-permute-done((bf16[2,32,512]{2,1,0:T(8,128)(2,1)S(1)}, bf16[2,32,512]{2,1,0:T(8,128)(2,1)S(1)}, u32[]{:S(2)}, u32[]{:S(2)}) %collective-permute-start.7) | collective-permute-done | bytes 65568 | tf_op jit(solution)/shard_map/ppermute | solution.py:404
  18.7 6.0 %shard_map.128 = (bf16[2176,128]{1,0:T(8,128)(2,1)S(1)}, bf16[2048,128]{1,0:T(8,128)(2,1)S(1)}, bf16[2176,128]{1,0:T(8,128)(2,1)S(1)}, bf16[2048,128]{1,0:T(8,12...) custom-call(s32[11]{0:T(128)S(1)} %stack.62.bits, ...), custom_call_target="tpu_custom_call" | custom-call | tf_op jit(solution)/shard_map/pallas_call | solution.py:365
  25.0 2.9 %shard_map.129 = (bf16[2176,128]{1,0:T(8,128)(2,1)S(1)}, bf16[2176,128]{1,0:T(8,128)(2,1)S(1)}) custom-call(s32[11]{0:T(128)S(1)} %stack.62.bits, bf16[4,2,32,512]{3,2,1,0:T(8,128)(2,1)S(1)} %get-tuple-element.56.frames, bf16[4,2,16,512]{3,2,1,0:T(8,128)(2,1)S(1)} %collective-permute-done.3.near, bf16[4,2,16,512]{3,2,1,0:T(8,128)(2,1)S(1)} %collective-permute-done.4.side, ...), custom_call_target="tpu_custom_call" | custom-call | tf_op jit(solution)/shard_map/pallas_call | solution.py:365
  28.6 2.7 %collective-permute-start.12 = (bf16[1024,128]{1,0:T(8,128)(2,1)S(1)}, bf16[1024,128]{1,0:T(8,128)(2,1)S(1)}, u32[]{:S(2)}, u32[]{:S(2)}) collective-permute-start(bf16[1024,128]{1,0:T(8,128)(2,1)S(1)} %get-tuple-element.100), channel_id=1, source_target_pairs={{0,2},{1,3},{2,0},{3,1},{4,6},{5,7},{6,4},{7,5},{8,10},{9,11},{10,... | collective-permute-start | bytes 786440 | tf_op jit(solution)/shard_map/ppermute | solution.py:404
  31.5 0.6 collective-permute-start.10
  32.2 1.5 %collective-permute-start.13 = (bf16[1088,128]{1,0:T(8,128)(2,1)S(1)}, bf16[1088,128]{1,0:T(8,128)(2,1)S(1)}, u32[]{:S(2)}, u32[]{:S(2)}) collective-permute-start(bf16[1088,128]{1,0:T(8,128)(2,1)S(1)} %get-tuple-element.98), channel_id=1, source_target_pairs={{0,1},{1,0},{2,3},{3,2},{4,5},{5,4},{6,7},{7,6},{8,9},{9,8},{10,11... | collective-permute-start | bytes 835592 | tf_op jit(solution)/shard_map/ppermute | solution.py:404
  33.6 4.6 %collective-permute-done.12 = bf16[1024,128]{1,0:T(8,128)(2,1)S(1)} collective-permute-done((bf16[1024,128]{1,0:T(8,128)(2,1)S(1)}, bf16[1024,128]{1,0:T(8,128)(2,1)S(1)}, u32[]{:S(2)}, u32[]{:S(2)}) %collective-permute-start.12) | collective-permute-done | bytes 262176 | tf_op jit(solution)/shard_map/ppermute | solution.py:404
  38.2 1.8 %collective-permute-done.10.y_got = bf16[1024,128]{1,0:T(8,128)(2,1)S(1)} collective-permute-done((bf16[1024,128]{1,0:T(8,128)(2,1)S(1)}, bf16[1024,128]{1,0:T(8,128)(2,1)S(1)}, u32[]{:S(2)}, u32[]{:S(2)}) %collective-permute-start.10) | collective-permute-done | bytes 262176 | tf_op jit(solution)/shard_map/ppermute | solution.py:404
  40.0 1.3 %shard_map.130 = (bf16[2,128,512]{2,1,0:T(8,128)(2,1)}, bf16[2,4,128,128]{3,2,1,0:T(8,128)(2,1)S(1)}, bf16[128,128]{1,0:T(8,128)(2,1)S(1)}, bf16[128,128]{1,0:T(8,128)(2,1)S(1)}) custom-call(s32[11]{0:T(128)S(1)} %stack.62.bits, bf16[1024,128]{1,0:T(8,128)(2,1)S(1)} %get-tuple-element.60.own, bf16[1024,128]{1,0:T(8,128)(2,1)S(1)} %collective-permute-done.8.core_got, ...), custom_call_target="tpu_custom_call" | custom-call | tf_op jit(solution)/shard_map/pallas_call | solution.py:365
  41.3 1.6 %collective-permute-start.15 = (bf16[256,128]{1,0:T(8,128)(2,1)S(1)}, bf16[256,128]{1,0:T(8,128)(2,1)S(1)}, u32[]{:S(2)}, u32[]{:S(2)}) collective-permute-start(bf16[256,128]{1,0:T(8,128)(2,1)S(1)} %pad_maximum_fusion.7), channel_id=1, source_target_pairs={{0,1},{1,0},{2,3},{3,2},{4,5},{5,4},{6,7},{7,6},{8,9},{9,8},{10,11... | collective-permute-start | bytes 196616 | tf_op jit(solution)/shard_map/ppermute | solution.py:404
  42.9 0.6 collective-permute-start.14
  43.6 0.6 collective-permute-start.21
  44.3 1.7 %collective-permute-done.15.x_got = bf16[256,128]{1,0:T(8,128)(2,1)S(1)} collective-permute-done((bf16[256,128]{1,0:T(8,128)(2,1)S(1)}, bf16[256,128]{1,0:T(8,128)(2,1)S(1)}, u32[]{:S(2)}, u32[]{:S(2)}) %collective-permute-start.15) | collective-permute-done | bytes 65568 | tf_op jit(solution)/shard_map/ppermute | solution.py:404
  46.0 2.1 %collective-permute-done.14 = bf16[544,128]{1,0:T(8,128)(2,1)S(1)} collective-permute-done((bf16[544,128]{1,0:T(8,128)(2,1)S(1)}, bf16[544,128]{1,0:T(8,128)(2,1)S(1)}, u32[]{:S(2)}, u32[]{:S(2)}) %collective-permute-start.14) | collective-permute-done | bytes 139296 | tf_op jit(solution)/shard_map/ppermute | solution.py:404
  48.1 1.6 %collective-permute-start.16 = (bf16[400,128]{1,0:T(8,128)(2,1)S(1)}, bf16[400,128]{1,0:T(8,128)(2,1)S(1)}, u32[]{:S(2)}, u32[]{:S(2)}) collective-permute-start(bf16[400,128]{1,0:T(8,128)(2,1)S(1)} %pad_maximum_fusion.6), channel_id=1, source_target_pairs={{0,2},{1,3},{2,0},{3,1},{4,6},{5,7},{6,4},{7,5},{8,10},{9,11},{10,... | collective-permute-start | bytes 307208 | tf_op jit(solution)/shard_map/ppermute | solution.py:404
  49.8 1.6 %collective-permute-start.22 = (bf16[256,128]{1,0:T(8,128)(2,1)S(1)}, bf16[256,128]{1,0:T(8,128)(2,1)S(1)}, u32[]{:S(2)}, u32[]{:S(2)}) collective-permute-start(bf16[256,128]{1,0:T(8,128)(2,1)S(1)} %get-tuple-element.108), channel_id=1, source_target_pairs={{0,4},{1,5},{2,6},{3,7},{4,0},{5,1},{6,2},{7,3},{8,12},{9,13},{10,... | collective-permute-start | bytes 196616 | tf_op jit(solution)/shard_map/ppermute | solution.py:404
  51.4 1.6 %collective-permute-done.16 = bf16[400,128]{1,0:T(8,128)(2,1)S(1)} collective-permute-done((bf16[400,128]{1,0:T(8,128)(2,1)S(1)}, bf16[400,128]{1,0:T(8,128)(2,1)S(1)}, u32[]{:S(2)}, u32[]{:S(2)}) %collective-permute-start.16) | collective-permute-done | bytes 102432 | tf_op jit(solution)/shard_map/ppermute | solution.py:404
  53.0 3.0 %collective-permute-start.17 = (bf16[272,128]{1,0:T(8,128)(2,1)S(1)}, bf16[272,128]{1,0:T(8,128)(2,1)S(1)}, u32[]{:S(2)}, u32[]{:S(2)}) collective-permute-start(bf16[272,128]{1,0:T(8,128)(2,1)S(1)} %add_convert_fusion.9), channel_id=1, source_target_pairs={{0,4},{1,5},{2,6},{3,7},{4,0},{5,1},{6,2},{7,3},{8,12},{9,13},{10,... | collective-permute-start | bytes 208904 | tf_op jit(solution)/shard_map/ppermute | solution.py:404
  56.5 0.8 collective-permute-start.23
  57.3 1.2 %collective-permute-done.17 = bf16[272,128]{1,0:T(8,128)(2,1)S(1)} collective-permute-done((bf16[272,128]{1,0:T(8,128)(2,1)S(1)}, bf16[272,128]{1,0:T(8,128)(2,1)S(1)}, u32[]{:S(2)}, u32[]{:S(2)}) %collective-permute-start.17) | collective-permute-done | bytes 69664 | tf_op jit(solution)/shard_map/ppermute | solution.py:404
  58.5 1.3 %collective-permute-start.18 = (bf16[272,128]{1,0:T(8,128)(2,1)S(1)}, bf16[272,128]{1,0:T(8,128)(2,1)S(1)}, u32[]{:S(2)}, u32[]{:S(2)}) collective-permute-start(bf16[272,128]{1,0:T(8,128)(2,1)S(1)} %add_convert_fusion.8), channel_id=1, source_target_pairs={{0,2},{1,3},{2,0},{3,1},{4,6},{5,7},{6,4},{7,5},{8,10},{9,11},{10,... | collective-permute-start | bytes 208904 | tf_op jit(solution)/shard_map/ppermute | solution.py:404
  59.8 1.0 %collective-permute-done.23 = bf16[256,128]{1,0:T(8,128)(2,1)S(1)} collective-permute-done((bf16[256,128]{1,0:T(8,128)(2,1)S(1)}, bf16[256,128]{1,0:T(8,128)(2,1)S(1)}, u32[]{:S(2)}, u32[]{:S(2)}) %collective-permute-start.23) | collective-permute-done | bytes 65568 | tf_op jit(solution)/shard_map/ppermute | solution.py:404
  60.9 1.2 %collective-permute-start.24 = (bf16[256,128]{1,0:T(8,128)(2,1)S(1)}, bf16[256,128]{1,0:T(8,128)(2,1)S(1)}, u32[]{:S(2)}, u32[]{:S(2)}) collective-permute-start(bf16[256,128]{1,0:T(8,128)(2,1)S(1)} %add_convert_fusion.12), channel_id=1, source_target_pairs={{0,4},{1,5},{2,6},{3,7},{4,0},{5,1},{6,2},{7,3},{8,12},{9,13},{10,... | collective-permute-start | bytes 196616 | tf_op jit(solution)/shard_map/ppermute | solution.py:404
  62.0 0.8 collective-permute-done.18
  62.9 1.1 %collective-permute-start.19 = (bf16[544,128]{1,0:T(8,128)(2,1)S(1)}, bf16[544,128]{1,0:T(8,128)(2,1)S(1)}, u32[]{:S(2)}, u32[]{:S(2)}) collective-permute-start(bf16[544,128]{1,0:T(8,128)(2,1)S(1)} %pad_maximum_fusion.4), channel_id=1, source_target_pairs={{0,16},{1,17},{2,18},{3,19},{4,20},{5,21},{6,22},{7,23},{8,24},{9,... | collective-permute-start | bytes 417800 | tf_op jit(solution)/shard_map/ppermute | solution.py:404
  64.0 2.8 %collective-permute-done.24 = bf16[256,128]{1,0:T(8,128)(2,1)S(1)} collective-permute-done((bf16[256,128]{1,0:T(8,128)(2,1)S(1)}, bf16[256,128]{1,0:T(8,128)(2,1)S(1)}, u32[]{:S(2)}, u32[]{:S(2)}) %collective-permute-start.24) | collective-permute-done | bytes 65568 | tf_op jit(solution)/shard_map/ppermute | solution.py:404
  66.8 0.7 collective-permute-start.25
  67.5 0.5 collective-permute-done.19
  68.1 1.1 %collective-permute-start.20 = (bf16[1088,128]{1,0:T(8,128)(2,1)S(1)}, bf16[1088,128]{1,0:T(8,128)(2,1)S(1)}, u32[]{:S(2)}, u32[]{:S(2)}) collective-permute-start(bf16[1088,128]{1,0:T(8,128)(2,1)S(1)} %pad_maximum_fusion.1.refs_0_.refs_2_), channel_id=1, source_target_pairs={{0,1},{1,0},{2,3},{3,2},{4,5},{5,4},{6,7},{7,6},{8,9},{9,8},{10,11... | collective-permute-start | bytes 835592 | tf_op jit(solution)/shard_map/ppermute | solution.py:404
  69.1 3.4 %collective-permute-done.25 = bf16[512,128]{1,0:T(8,128)(2,1)S(1)} collective-permute-done((bf16[512,128]{1,0:T(8,128)(2,1)S(1)}, bf16[512,128]{1,0:T(8,128)(2,1)S(1)}, u32[]{:S(2)}, u32[]{:S(2)}) %collective-permute-start.25) | collective-permute-done | bytes 131104 | tf_op jit(solution)/shard_map/ppermute | solution.py:404
  72.7 0.7 collective-permute-start.27
  73.4 2.8 %shard_map.131 = bf16[2,128,512]{2,1,0:T(8,128)(2,1)} custom-call(s32[11]{0:T(128)S(1)} %stack.62.bits, bf16[2,4,128,128]{3,2,1,0:T(8,128)(2,1)S(1)} %get-tuple-element.75.dconv, bf16[256,128]{1,0:T(8,128)(2,1)S(1)} %collective-permute-done.15.x_got, bf16[128,128]{1,0:T(8,128)(2,1)S(1)} %slice.133.z_got, ...), custom_call_target="tpu_custom_call" | custom-call | tf_op jit(solution)/shard_map/pallas_call | solution.py:365
  76.2 2.0 %shard_map.132 = (f32[512,512]{1,0:T(8,128)}, f32[512,512]{1,0:T(8,128)}, f32[512,512]{1,0:T(8,128)}, f32[512,512]{1,0:T(8,128)}) custom-call(s32[11]{0:T(128)S(1)} %stack.62.bits, bf16[1088,128]{1,0:T(8,128)(2,1)S(1)} %pad_maximum_fusion.1.refs_0_.refs_2_, bf16[1024,128]{1,0:T(8,128)(2,1)S(1)} %pad_maximum_fusion.3.refs_1_, ...), custom_call_target="tpu_custom_call" | custom-call | tf_op jit(solution)/shard_map/pallas_call | solution.py:365
  78.3 3.1 %collective-permute-done.26.refs_1_ = bf16[1024,128]{1,0:T(8,128)(2,1)S(1)} collective-permute-done((bf16[1024,128]{1,0:T(8,128)(2,1)S(1)}, bf16[1024,128]{1,0:T(8,128)(2,1)S(1)}, u32[]{:S(2)}, u32[]{:S(2)}) %collective-permute-start.26) | collective-permute-done | bytes 262176 | tf_op jit(solution)/shard_map/ppermute | solution.py:404
  81.4 0.5 collective-permute-start.31
  81.9 1.6 %shard_map.133 = (f32[512,512]{1,0:T(8,128)}, f32[512,512]{1,0:T(8,128)}, f32[512,512]{1,0:T(8,128)}, f32[512,512]{1,0:T(8,128)}) custom-call(s32[11]{0:T(128)S(1)} %stack.62.bits, bf16[1088,128]{1,0:T(8,128)(2,1)S(1)} %collective-permute-done.20.refs_0_.refs_3_, ...), custom_call_target="tpu_custom_call", output_to_operand_aliasing={{0}: (3, {}), {1}: (4, {}), {2}: (5, {}), {3}: (6, {})} | custom-call | tf_op jit(solution)/shard_map/pallas_call | solution.py:365
  83.5 2.2 %shard_map.134 = (f32[512,512]{1,0:T(8,128)}, f32[512,512]{1,0:T(8,128)}, f32[512,512]{1,0:T(8,128)}, f32[512,512]{1,0:T(8,128)}, f32[31,512]{1,0:T(8,128)}) custom-call(s32[11]{0:T(128)S(1)} %stack.62.bits, bf16[1088,128]{1,0:T(8,128)(2,1)S(1)} %collective-permute-done.30.refs_0_.refs_5_, ...), custom_call_target="tpu_custom_call", output_to_operand_aliasing={{0}: (7, {}), {1}: (8, {}), {2}: (9, {}), {3}: (10, {})} | custom-call | tf_op jit(solution)/shard_map/pallas_call | solution.py:365
  (54 shorter events, 2.8 us)
Async XLA Ops:
  1.7 5.2 %collective-permute-start = (bf16[2,32,512]{2,1,0:T(8,128)(2,1)S(1)}, bf16[2,32,512]{2,1,0:T(8,128)(2,1)S(1)}, u32[]{:S(2)}, u32[]{:S(2)}) collective-permute-start(bf16[2,32,512]{2,1,0:T(8,128)(2,1)S(1)} %get-tuple-element.114), channel_id=1, source_target_pairs={{0,8},{1,9},{2,10},{3,11},{4,12},{5,13},{6,14},{7,15},{8,0},{9,1},... | collective-permute-start | bytes 196616 | tf_op jit(solution)/shard_map/ppermute | solution.py:404
  2.2 5.3 %collective-permute-start.1 = (bf16[2,32,512]{2,1,0:T(8,128)(2,1)S(1)}, bf16[2,32,512]{2,1,0:T(8,128)(2,1)S(1)}, u32[]{:S(2)}, u32[]{:S(2)}) collective-permute-start(bf16[2,32,512]{2,1,0:T(8,128)(2,1)S(1)} %get-tuple-element.116), channel_id=1, source_target_pairs={{0,16},{1,17},{2,18},{3,19},{4,20},{5,21},{6,22},{7,23},{8,24},{9,... | collective-permute-start | bytes 196616 | tf_op jit(solution)/shard_map/ppermute | solution.py:404
  4.8 4.0 %collective-permute-start.2 = (bf16[2,32,512]{2,1,0:T(8,128)(2,1)S(1)}, bf16[2,32,512]{2,1,0:T(8,128)(2,1)S(1)}, u32[]{:S(2)}, u32[]{:S(2)}) collective-permute-start(bf16[2,32,512]{2,1,0:T(8,128)(2,1)S(1)} %get-tuple-element.113), channel_id=1, source_target_pairs={{0,24},{1,25},{2,26},{3,27},{4,28},{5,29},{6,30},{7,31},{8,16},{9,... | collective-permute-start | bytes 196616 | tf_op jit(solution)/shard_map/ppermute | solution.py:404
  4.8 5.4 %copy-start = (bf16[2,128,512]{2,1,0:T(8,128)(2,1)S(1)}, bf16[2,128,512]{2,1,0:T(8,128)(2,1)}, u32[]{:S(2)}) copy-start(bf16[2,128,512]{2,1,0:T(8,128)(2,1)} %cot.1) | copy-start | bytes 786436
  4.8 9.9 %copy-start.1 = (f32[31,512]{1,0:T(8,128)S(1)}, f32[31,512]{1,0:T(8,128)}, u32[]{:S(2)}) copy-start(f32[31,512]{1,0:T(8,128)} %kern.3) | copy-start | bytes 190468
  9.4 5.3 %collective-permute-start.3 = (bf16[4,2,16,512]{3,2,1,0:T(8,128)(2,1)S(1)}, bf16[4,2,16,512]{3,2,1,0:T(8,128)(2,1)S(1)}, u32[]{:S(2)}, u32[]{:S(2)}) collective-permute-start(bf16[4,2,16,512]{3,2,1,0:T(8,128)(2,1)S(1)} %get-tuple-element.54), channel_id=1, source_target_pairs={{0,8},{1,9},{2,10},{3,11},{4,12},{5,13},{6,14},{7,15},{8,0},{9,1},... | collective-permute-start | bytes 393224 | tf_op jit(solution)/shard_map/ppermute | solution.py:404
  9.6 5.1 %collective-permute-start.4 = (bf16[4,2,16,512]{3,2,1,0:T(8,128)(2,1)S(1)}, bf16[4,2,16,512]{3,2,1,0:T(8,128)(2,1)S(1)}, u32[]{:S(2)}, u32[]{:S(2)}) collective-permute-start(bf16[4,2,16,512]{3,2,1,0:T(8,128)(2,1)S(1)} %get-tuple-element.55), channel_id=1, source_target_pairs={{8,24},{9,25},{10,26},{11,27},{12,28},{13,29},{14,30},{15,31},{24,... | collective-permute-start | bytes 393224 | tf_op jit(solution)/shard_map/ppermute | solution.py:404
  10.3 6.9 %collective-permute-start.5 = (bf16[2,32,512]{2,1,0:T(8,128)(2,1)S(1)}, bf16[2,32,512]{2,1,0:T(8,128)(2,1)S(1)}, u32[]{:S(2)}, u32[]{:S(2)}) collective-permute-start(bf16[2,32,512]{2,1,0:T(8,128)(2,1)S(1)} %get-tuple-element.111), channel_id=1, source_target_pairs={{0,8},{1,9},{2,10},{3,11},{4,12},{5,13},{6,14},{7,15},{8,0},{9,1},... | collective-permute-start | bytes 196616 | tf_op jit(solution)/shard_map/ppermute | solution.py:404
  13.0 4.3 %collective-permute-start.6 = (bf16[2,32,512]{2,1,0:T(8,128)(2,1)S(1)}, bf16[2,32,512]{2,1,0:T(8,128)(2,1)S(1)}, u32[]{:S(2)}, u32[]{:S(2)}) collective-permute-start(bf16[2,32,512]{2,1,0:T(8,128)(2,1)S(1)} %get-tuple-element.110), channel_id=1, source_target_pairs={{0,16},{1,17},{2,18},{3,19},{4,20},{5,21},{6,22},{7,23},{8,24},{9,... | collective-permute-start | bytes 196616 | tf_op jit(solution)/shard_map/ppermute | solution.py:404
  14.7 4.0 %collective-permute-start.7 = (bf16[2,32,512]{2,1,0:T(8,128)(2,1)S(1)}, bf16[2,32,512]{2,1,0:T(8,128)(2,1)S(1)}, u32[]{:S(2)}, u32[]{:S(2)}) collective-permute-start(bf16[2,32,512]{2,1,0:T(8,128)(2,1)S(1)} %get-tuple-element.109), channel_id=1, source_target_pairs={{0,24},{1,25},{2,26},{3,27},{4,28},{5,29},{6,30},{7,31},{8,16},{9,... | collective-permute-start | bytes 196616 | tf_op jit(solution)/shard_map/ppermute | solution.py:404
  24.7 3.7 %collective-permute-start.11 = (bf16[2048,128]{1,0:T(8,128)(2,1)S(1)}, bf16[2048,128]{1,0:T(8,128)(2,1)S(1)}, u32[]{:S(2)}, u32[]{:S(2)}) collective-permute-start(bf16[2048,128]{1,0:T(8,128)(2,1)S(1)} %get-tuple-element.69), channel_id=1, source_target_pairs={{0,8},{1,9},{2,10},{3,11},{4,12},{5,13},{6,14},{7,15},{8,0},{9,1},... | collective-permute-start | bytes 1572872 | tf_op jit(solution)/shard_map/ppermute | solution.py:404
  27.8 3.5 %collective-permute-start.9 = (bf16[2176,128]{1,0:T(8,128)(2,1)S(1)}, bf16[2176,128]{1,0:T(8,128)(2,1)S(1)}, u32[]{:S(2)}, u32[]{:S(2)}) collective-permute-start(bf16[2176,128]{1,0:T(8,128)(2,1)S(1)} %get-tuple-element.66), channel_id=1, source_target_pairs={{0,8},{1,9},{2,10},{3,11},{4,12},{5,13},{6,14},{7,15},{8,0},{9,1},... | collective-permute-start | bytes 1671176 | tf_op jit(solution)/shard_map/ppermute | solution.py:404
  28.2 3.2 %collective-permute-start.8 = (bf16[1024,128]{1,0:T(8,128)(2,1)S(1)}, bf16[1024,128]{1,0:T(8,128)(2,1)S(1)}, u32[]{:S(2)}, u32[]{:S(2)}) collective-permute-start(bf16[1024,128]{1,0:T(8,128)(2,1)S(1)} %get-tuple-element.61), channel_id=1, source_target_pairs={{0,8},{1,9},{2,10},{3,11},{4,12},{5,13},{6,14},{7,15},{8,0},{9,1},... | collective-permute-start | bytes 786440 | tf_op jit(solution)/shard_map/ppermute | solution.py:404
  28.6 9.6 %collective-permute-start.12 = (bf16[1024,128]{1,0:T(8,128)(2,1)S(1)}, bf16[1024,128]{1,0:T(8,128)(2,1)S(1)}, u32[]{:S(2)}, u32[]{:S(2)}) collective-permute-start(bf16[1024,128]{1,0:T(8,128)(2,1)S(1)} %get-tuple-element.100), channel_id=1, source_target_pairs={{0,2},{1,3},{2,0},{3,1},{4,6},{5,7},{6,4},{7,5},{8,10},{9,11},{10,... | collective-permute-start | bytes 786440 | tf_op jit(solution)/shard_map/ppermute | solution.py:404
  31.5 8.4 %collective-permute-start.10 = (bf16[1024,128]{1,0:T(8,128)(2,1)S(1)}, bf16[1024,128]{1,0:T(8,128)(2,1)S(1)}, u32[]{:S(2)}, u32[]{:S(2)}) collective-permute-start(bf16[1024,128]{1,0:T(8,128)(2,1)S(1)} %pad_maximum_fusion.2), channel_id=1, source_target_pairs={{0,16},{1,17},{2,18},{3,19},{4,20},{5,21},{6,22},{7,23},{8,24},{9,... | collective-permute-start | bytes 786440 | tf_op jit(solution)/shard_map/ppermute | solution.py:404
  32.2 10.7 %collective-permute-start.13 = (bf16[1088,128]{1,0:T(8,128)(2,1)S(1)}, bf16[1088,128]{1,0:T(8,128)(2,1)S(1)}, u32[]{:S(2)}, u32[]{:S(2)}) collective-permute-start(bf16[1088,128]{1,0:T(8,128)(2,1)S(1)} %get-tuple-element.98), channel_id=1, source_target_pairs={{0,1},{1,0},{2,3},{3,2},{4,5},{5,4},{6,7},{7,6},{8,9},{9,8},{10,11... | collective-permute-start | bytes 835592 | tf_op jit(solution)/shard_map/ppermute | solution.py:404
  41.3 4.7 %collective-permute-start.15 = (bf16[256,128]{1,0:T(8,128)(2,1)S(1)}, bf16[256,128]{1,0:T(8,128)(2,1)S(1)}, u32[]{:S(2)}, u32[]{:S(2)}) collective-permute-start(bf16[256,128]{1,0:T(8,128)(2,1)S(1)} %pad_maximum_fusion.7), channel_id=1, source_target_pairs={{0,1},{1,0},{2,3},{3,2},{4,5},{5,4},{6,7},{7,6},{8,9},{9,8},{10,11... | collective-permute-start | bytes 196616 | tf_op jit(solution)/shard_map/ppermute | solution.py:404
  42.9 5.1 %collective-permute-start.14 = (bf16[544,128]{1,0:T(8,128)(2,1)S(1)}, bf16[544,128]{1,0:T(8,128)(2,1)S(1)}, u32[]{:S(2)}, u32[]{:S(2)}) collective-permute-start(bf16[544,128]{1,0:T(8,128)(2,1)S(1)} %get-tuple-element.102), channel_id=1, source_target_pairs={{0,16},{1,17},{2,18},{3,19},{4,20},{5,21},{6,22},{7,23},{8,24},{9,... | collective-permute-start | bytes 417800 | tf_op jit(solution)/shard_map/ppermute | solution.py:404
  43.6 6.1 %collective-permute-start.21 = (bf16[512,128]{1,0:T(8,128)(2,1)S(1)}, bf16[512,128]{1,0:T(8,128)(2,1)S(1)}, u32[]{:S(2)}, u32[]{:S(2)}) collective-permute-start(bf16[512,128]{1,0:T(8,128)(2,1)S(1)} %get-tuple-element.104), channel_id=1, source_target_pairs={{0,1},{1,0},{2,3},{3,2},{4,5},{5,4},{6,7},{7,6},{8,9},{9,8},{10,11... | collective-permute-start | bytes 393224 | tf_op jit(solution)/shard_map/ppermute | solution.py:404
  48.1 4.9 %collective-permute-start.16 = (bf16[400,128]{1,0:T(8,128)(2,1)S(1)}, bf16[400,128]{1,0:T(8,128)(2,1)S(1)}, u32[]{:S(2)}, u32[]{:S(2)}) collective-permute-start(bf16[400,128]{1,0:T(8,128)(2,1)S(1)} %pad_maximum_fusion.6), channel_id=1, source_target_pairs={{0,2},{1,3},{2,0},{3,1},{4,6},{5,7},{6,4},{7,5},{8,10},{9,11},{10,... | collective-permute-start | bytes 307208 | tf_op jit(solution)/shard_map/ppermute | solution.py:404
  49.8 6.7 %collective-permute-start.22 = (bf16[256,128]{1,0:T(8,128)(2,1)S(1)}, bf16[256,128]{1,0:T(8,128)(2,1)S(1)}, u32[]{:S(2)}, u32[]{:S(2)}) collective-permute-start(bf16[256,128]{1,0:T(8,128)(2,1)S(1)} %get-tuple-element.108), channel_id=1, source_target_pairs={{0,4},{1,5},{2,6},{3,7},{4,0},{5,1},{6,2},{7,3},{8,12},{9,13},{10,... | collective-permute-start | bytes 196616 | tf_op jit(solution)/shard_map/ppermute | solution.py:404
  53.0 5.4 %collective-permute-start.17 = (bf16[272,128]{1,0:T(8,128)(2,1)S(1)}, bf16[272,128]{1,0:T(8,128)(2,1)S(1)}, u32[]{:S(2)}, u32[]{:S(2)}) collective-permute-start(bf16[272,128]{1,0:T(8,128)(2,1)S(1)} %add_convert_fusion.9), channel_id=1, source_target_pairs={{0,4},{1,5},{2,6},{3,7},{4,0},{5,1},{6,2},{7,3},{8,12},{9,13},{10,... | collective-permute-start | bytes 208904 | tf_op jit(solution)/shard_map/ppermute | solution.py:404
  56.5 4.3 %collective-permute-start.23 = (bf16[256,128]{1,0:T(8,128)(2,1)S(1)}, bf16[256,128]{1,0:T(8,128)(2,1)S(1)}, u32[]{:S(2)}, u32[]{:S(2)}) collective-permute-start(bf16[256,128]{1,0:T(8,128)(2,1)S(1)} %add_convert_fusion.13), channel_id=1, source_target_pairs={{0,16},{1,17},{2,18},{3,19},{4,20},{5,21},{6,22},{7,23},{8,24},{9,... | collective-permute-start | bytes 196616 | tf_op jit(solution)/shard_map/ppermute | solution.py:404
  58.5 4.4 %collective-permute-start.18 = (bf16[272,128]{1,0:T(8,128)(2,1)S(1)}, bf16[272,128]{1,0:T(8,128)(2,1)S(1)}, u32[]{:S(2)}, u32[]{:S(2)}) collective-permute-start(bf16[272,128]{1,0:T(8,128)(2,1)S(1)} %add_convert_fusion.8), channel_id=1, source_target_pairs={{0,2},{1,3},{2,0},{3,1},{4,6},{5,7},{6,4},{7,5},{8,10},{9,11},{10,... | collective-permute-start | bytes 208904 | tf_op jit(solution)/shard_map/ppermute | solution.py:404
  60.9 5.9 %collective-permute-start.24 = (bf16[256,128]{1,0:T(8,128)(2,1)S(1)}, bf16[256,128]{1,0:T(8,128)(2,1)S(1)}, u32[]{:S(2)}, u32[]{:S(2)}) collective-permute-start(bf16[256,128]{1,0:T(8,128)(2,1)S(1)} %add_convert_fusion.12), channel_id=1, source_target_pairs={{0,4},{1,5},{2,6},{3,7},{4,0},{5,1},{6,2},{7,3},{8,12},{9,13},{10,... | collective-permute-start | bytes 196616 | tf_op jit(solution)/shard_map/ppermute | solution.py:404
  62.9 5.1 %collective-permute-start.19 = (bf16[544,128]{1,0:T(8,128)(2,1)S(1)}, bf16[544,128]{1,0:T(8,128)(2,1)S(1)}, u32[]{:S(2)}, u32[]{:S(2)}) collective-permute-start(bf16[544,128]{1,0:T(8,128)(2,1)S(1)} %pad_maximum_fusion.4), channel_id=1, source_target_pairs={{0,16},{1,17},{2,18},{3,19},{4,20},{5,21},{6,22},{7,23},{8,24},{9,... | collective-permute-start | bytes 417800 | tf_op jit(solution)/shard_map/ppermute | solution.py:404
  66.8 5.7 %collective-permute-start.25 = (bf16[512,128]{1,0:T(8,128)(2,1)S(1)}, bf16[512,128]{1,0:T(8,128)(2,1)S(1)}, u32[]{:S(2)}, u32[]{:S(2)}) collective-permute-start(bf16[512,128]{1,0:T(8,128)(2,1)S(1)} %pad_maximum_fusion.5), channel_id=1, source_target_pairs={{0,1},{1,0},{2,3},{3,2},{4,5},{5,4},{6,7},{7,6},{8,9},{9,8},{10,11... | collective-permute-start | bytes 393224 | tf_op jit(solution)/shard_map/ppermute | solution.py:404
  68.0 8.2 %collective-permute-start.28 = (bf16[1088,128]{1,0:T(8,128)(2,1)S(1)}, bf16[1088,128]{1,0:T(8,128)(2,1)S(1)}, u32[]{:S(2)}, u32[]{:S(2)}) collective-permute-start(bf16[1088,128]{1,0:T(8,128)(2,1)S(1)} %pad_maximum_fusion.1.refs_0_.refs_2_), channel_id=1, source_target_pairs={{0,8},{1,9},{2,10},{3,11},{4,12},{5,13},{6,14},{7,15},{8,0},{9,1},... | collective-permute-start | bytes 835592 | tf_op jit(solution)/shard_map/ppermute | solution.py:404
  68.1 13.3 %collective-permute-start.20 = (bf16[1088,128]{1,0:T(8,128)(2,1)S(1)}, bf16[1088,128]{1,0:T(8,128)(2,1)S(1)}, u32[]{:S(2)}, u32[]{:S(2)}) collective-permute-start(bf16[1088,128]{1,0:T(8,128)(2,1)S(1)} %pad_maximum_fusion.1.refs_0_.refs_2_), channel_id=1, source_target_pairs={{0,1},{1,0},{2,3},{3,2},{4,5},{5,4},{6,7},{7,6},{8,9},{9,8},{10,11... | collective-permute-start | bytes 835592 | tf_op jit(solution)/shard_map/ppermute | solution.py:404
  72.6 3.7 %collective-permute-start.29 = (bf16[1024,128]{1,0:T(8,128)(2,1)S(1)}, bf16[1024,128]{1,0:T(8,128)(2,1)S(1)}, u32[]{:S(2)}, u32[]{:S(2)}) collective-permute-start(bf16[1024,128]{1,0:T(8,128)(2,1)S(1)} %pad_maximum_fusion.3.refs_1_), channel_id=1, source_target_pairs={{0,8},{1,9},{2,10},{3,11},{4,12},{5,13},{6,14},{7,15},{8,0},{9,1},... | collective-permute-start | bytes 786440 | tf_op jit(solution)/shard_map/ppermute | solution.py:404
  72.6 8.7 %collective-permute-start.26 = (bf16[1024,128]{1,0:T(8,128)(2,1)S(1)}, bf16[1024,128]{1,0:T(8,128)(2,1)S(1)}, u32[]{:S(2)}, u32[]{:S(2)}) collective-permute-start(bf16[1024,128]{1,0:T(8,128)(2,1)S(1)} %pad_maximum_fusion.3.refs_1_), channel_id=1, source_target_pairs={{0,2},{1,3},{2,0},{3,1},{4,6},{5,7},{6,4},{7,5},{8,10},{9,11},{10,... | collective-permute-start | bytes 786440 | tf_op jit(solution)/shard_map/ppermute | solution.py:404
  72.7 0.7 collective-permute-start.27
  81.4 2.1 %collective-permute-start.30 = (bf16[1088,128]{1,0:T(8,128)(2,1)S(1)}, bf16[1088,128]{1,0:T(8,128)(2,1)S(1)}, u32[]{:S(2)}, u32[]{:S(2)}) collective-permute-start(bf16[1088,128]{1,0:T(8,128)(2,1)S(1)} %collective-permute-done.20.refs_0_.refs_3_), channel_id=1, source_target_pairs={{0,8},{1,9},{2,10},{3,11},{4,12},{5,13},{6,14},{7,15},{8,0},{9,1},... | collective-permute-start | bytes 835592 | tf_op jit(solution)/shard_map/ppermute | solution.py:404
  81.4 2.1 %collective-permute-start.31 = (bf16[1024,128]{1,0:T(8,128)(2,1)S(1)}, bf16[1024,128]{1,0:T(8,128)(2,1)S(1)}, u32[]{:S(2)}, u32[]{:S(2)}) collective-permute-start(bf16[1024,128]{1,0:T(8,128)(2,1)S(1)} %collective-permute-done.26.refs_1_), channel_id=1, source_target_pairs={{0,8},{1,9},{2,10},{3,11},{4,12},{5,13},{6,14},{7,15},{8,0},{9,1},... | collective-permute-start | bytes 786440 | tf_op jit(solution)/shard_map/ppermute | solution.py:404

commit v19 on v16

--- a/solution.py
+++ b/solution.py
@@ -482,17 +482,17 @@
     got = swap(jnp.concatenate([total(*(t[span:] for t in a)), passed]), lines[0])
     a, z_got = [kept(a, span), got[:span]], got[span:]
     b = halved(b, lines[1])
-    a = exchanged(a, lines[1:])
-    b = exchanged(b, [over_y] + lines[2:])
     other_got = permute(
-        after(passed, a),
+        passed,
         both([(m * blocks + t, m * blocks + t + 2)
               for m in range(groups) for t in range(2, blocks - 2) if t // 2 % 2]),
     )
+    a = exchanged([after(a[0], other_got), a[1]], lines[1:])
+    b = exchanged(b, [over_y] + lines[2:])
     a = doubled(a, lines[0])
     b = doubled(b, lines[1])
     a = doubled(a, over_y)
-    b = doubled(after(b, other_got), over_x)
+    b = doubled(b, over_x)
 
     norm = 1.0 / math.sqrt(groups * count * blocks * length)
     square = shape((width, width), F32)

time: 87.1 us -> 85.9 us (0.986)
  starting transfers between devices: 39 us -> 35.4 us
  waiting for transfers between devices: 21.8 us -> 24.3 us
    ppermute x32, starting transfers between devices: 39 us -> 35.4 us  [permute(): return lax.ppermute(x, ('mic', 'tm'), pairs)]
    ppermute x32, waiting for transfers between devices: 21.8 us -> 24.3 us  [permute(): return lax.ppermute(x, ('mic', 'tm'), pairs)]
  transfers between devices with their start and end apart: 32 -> 32, of which waited for: 17 -> 16; matrix products, arithmetic and copies ran while one was open for 3% -> 3% of each run, Pallas kernels for 12% -> 12%
where the time goes in v19:
time: 85.9 us; the launch traced here: 85.7 us
  starting transfers between devices  35.4 us (41%)
  waiting for transfers between devices  24.3 us (28%)
  Pallas kernels  21.4 us (25%)
  other arithmetic  2.51 us (3%)
  local copies, waits for them, and re-layouts  1.12 us (1%)
  between operations  1.02 us (1%)
    ppermute x32, starting transfers between devices, permute(): return lax.ppermute(x, ('mic', 'tm'), pairs)  35.4 us
    ppermute x32, waiting for transfers between devices, permute(): return lax.ppermute(x, ('mic', 'tm'), pairs)  24.3 us
    pallas_call x8, Pallas kernels, call(): pl.pallas_call(body, out_shape=outs, in_specs=[pl.BlockSpec(memory_space=...  21.4 us
    another operation x1, other arithmetic, shards(): weights = jnp.stack([w_query, w_key, w_value, w_out])  1.82 us
  transfers between devices with their start and end apart: 32, of which 16 were waited for; matrix products, arithmetic and copies ran while one was open for 3% of the time, Pallas kernels for 12%

profile of v19, /device:TPU:0, one launch (start us, length us, event | category | flops | bytes accessed | tf_op | source)
XLA Modules:
  0.0 85.7 jit_solution(8952575643474074371)
XLA Ops:
  0.7 1.0 %constant_dynamic-slice_fusion.5 = (bf16[2,32,512]{2,1,0:T(8,128)(2,1)S(1)}, bf16[2,32,512]{2,1,0:T(8,128)(2,1)S(1)}, bf16[2,32,512]{2,1,0:T(8,128)(2,1)S(1)}, bf16[2,32,512]{2,1,0:T(8,128)(2,1)S(1)}) fusion(bf16[2,128,512]{2,1,0:T(8,128)(2,1)} %param.7, s32[]{:T(128)S(6)} %select_n.100, s32[]{:T(128)S(6)} %select_n.98, s32[]{:T(128)S(6)} %select_n.97, ...), kind=kLoop, calls=%fused_computation.29 | loop fusion | bytes 524304 | tf_op jit(solution)/shard_map/dynamic_slice | solution.py:394
  1.7 0.5 collective-permute-start
  2.2 2.6 %collective-permute-start.1 = (bf16[2,32,512]{2,1,0:T(8,128)(2,1)S(1)}, bf16[2,32,512]{2,1,0:T(8,128)(2,1)S(1)}, u32[]{:S(2)}, u32[]{:S(2)}) collective-permute-start(bf16[2,32,512]{2,1,0:T(8,128)(2,1)S(1)} %get-tuple-element.108), channel_id=1, source_target_pairs={{0,16},{1,17},{2,18},{3,19},{4,20},{5,21},{6,22},{7,23},{8,24},{9,... | collective-permute-start | bytes 196616 | tf_op jit(solution)/shard_map/ppermute | solution.py:383
  4.8 1.8 %pad_maximum_fusion.weights = bf16[4,512,512]{2,1,0:T(8,128)(2,1)S(1)} fusion(bf16[1,512,512]{2,1,0:T(8,128)(2,1)} %bitcast.15, bf16[1,512,512]{2,1,0:T(8,128)(2,1)} %bitcast.16, bf16[1,512,512]{2,1,0:T(8,128)(2,1)} %bitcast.17, bf16[1,512,512]{2,1,0:T(8,128)(2,1)} %bitcast.18), kind=kLoop, calls=%fused_computation | loop fusion | flops 3145728 | bytes 4194304 | tf_op jit(solution)/shard_map/stack | solution.py:402
  6.9 0.6 collective-permute-done.1.f2
  7.5 1.4 %collective-permute-done.2.f3 = bf16[2,32,512]{2,1,0:T(8,128)(2,1)S(1)} collective-permute-done((bf16[2,32,512]{2,1,0:T(8,128)(2,1)S(1)}, bf16[2,32,512]{2,1,0:T(8,128)(2,1)S(1)}, u32[]{:S(2)}, u32[]{:S(2)}) %collective-permute-start.2) | collective-permute-done | bytes 65568 | tf_op jit(solution)/shard_map/ppermute | solution.py:383
  8.8 0.6 shard_map.126
  9.6 0.7 collective-permute-start.4
  10.3 2.7 %collective-permute-start.5 = (bf16[2,32,512]{2,1,0:T(8,128)(2,1)S(1)}, bf16[2,32,512]{2,1,0:T(8,128)(2,1)S(1)}, u32[]{:S(2)}, u32[]{:S(2)}) collective-permute-start(bf16[2,32,512]{2,1,0:T(8,128)(2,1)S(1)} %get-tuple-element.103), channel_id=1, source_target_pairs={{0,8},{1,9},{2,10},{3,11},{4,12},{5,13},{6,14},{7,15},{8,0},{9,1},... | collective-permute-start | bytes 196616 | tf_op jit(solution)/shard_map/ppermute | solution.py:383
  13.0 1.6 %collective-permute-start.6 = (bf16[2,32,512]{2,1,0:T(8,128)(2,1)S(1)}, bf16[2,32,512]{2,1,0:T(8,128)(2,1)S(1)}, u32[]{:S(2)}, u32[]{:S(2)}) collective-permute-start(bf16[2,32,512]{2,1,0:T(8,128)(2,1)S(1)} %get-tuple-element.102), channel_id=1, source_target_pairs={{0,16},{1,17},{2,18},{3,19},{4,20},{5,21},{6,22},{7,23},{8,24},{9,... | collective-permute-start | bytes 196616 | tf_op jit(solution)/shard_map/ppermute | solution.py:383
  14.7 2.5 %shard_map.127 = (bf16[4,2,32,512]{3,2,1,0:T(8,128)(2,1)S(1)}, f32[256,512]{1,0:T(8,128)S(1)}, bf16[256,512]{1,0:T(8,128)(2,1)S(1)}) custom-call(s32[11]{0:T(128)S(1)} %stack.62.bits, bf16[2,32,512]{2,1,0:T(8,128)(2,1)S(1)} %get-tuple-element.107.f0, bf16[2,32,512]{2,1,0:T(8,128)(2,1)S(1)} %collective-permute-done.f1, ...), custom_call_target="tpu_custom_call" | custom-call | tf_op jit(solution)/shard_map/pallas_call | solution.py:344
  17.3 1.4 %collective-permute-done.7.c3 = bf16[2,32,512]{2,1,0:T(8,128)(2,1)S(1)} collective-permute-done((bf16[2,32,512]{2,1,0:T(8,128)(2,1)S(1)}, bf16[2,32,512]{2,1,0:T(8,128)(2,1)S(1)}, u32[]{:S(2)}, u32[]{:S(2)}) %collective-permute-start.7) | collective-permute-done | bytes 65568 | tf_op jit(solution)/shard_map/ppermute | solution.py:383
  18.7 8.4 %shard_map.128 = (bf16[2176,128]{1,0:T(8,128)(2,1)S(1)}, bf16[2048,128]{1,0:T(8,128)(2,1)S(1)}, bf16[2176,128]{1,0:T(8,128)(2,1)S(1)}, bf16[2048,128]{1,0:T(8,12...) custom-call(s32[11]{0:T(128)S(1)} %stack.62.bits, ...), custom_call_target="tpu_custom_call" | custom-call | tf_op jit(solution)/shard_map/pallas_call | solution.py:344
  27.3 0.4 collective-permute-start.8
  27.8 1.6 %collective-permute-done.8.core_got = bf16[1024,128]{1,0:T(8,128)(2,1)S(1)} collective-permute-done((bf16[1024,128]{1,0:T(8,128)(2,1)S(1)}, bf16[1024,128]{1,0:T(8,128)(2,1)S(1)}, u32[]{:S(2)}, u32[]{:S(2)}) %collective-permute-start.8) | collective-permute-done | bytes 262176 | tf_op jit(solution)/shard_map/ppermute | solution.py:383
  29.5 1.8 %collective-permute-start.9 = (bf16[1024,128]{1,0:T(8,128)(2,1)S(1)}, bf16[1024,128]{1,0:T(8,128)(2,1)S(1)}, u32[]{:S(2)}, u32[]{:S(2)}) collective-permute-start(bf16[1024,128]{1,0:T(8,128)(2,1)S(1)} %pad_maximum_fusion.2), channel_id=1, source_target_pairs={{0,16},{1,17},{2,18},{3,19},{4,20},{5,21},{6,22},{7,23},{8,24},{9,... | collective-permute-start | bytes 786440 | tf_op jit(solution)/shard_map/ppermute | solution.py:383
  31.4 1.7 %collective-permute-start.11 = (bf16[1024,128]{1,0:T(8,128)(2,1)S(1)}, bf16[1024,128]{1,0:T(8,128)(2,1)S(1)}, u32[]{:S(2)}, u32[]{:S(2)}) collective-permute-start(bf16[1024,128]{1,0:T(8,128)(2,1)S(1)} %get-tuple-element.92), channel_id=1, source_target_pairs={{0,2},{1,3},{2,0},{3,1},{4,6},{5,7},{6,4},{7,5},{8,10},{9,11},{10,... | collective-permute-start | bytes 786440 | tf_op jit(solution)/shard_map/ppermute | solution.py:383
  33.2 1.5 %collective-permute-start.13 = (bf16[1088,128]{1,0:T(8,128)(2,1)S(1)}, bf16[1088,128]{1,0:T(8,128)(2,1)S(1)}, u32[]{:S(2)}, u32[]{:S(2)}) collective-permute-start(bf16[1088,128]{1,0:T(8,128)(2,1)S(1)} %get-tuple-element.90), channel_id=1, source_target_pairs={{0,1},{1,0},{2,3},{3,2},{4,5},{5,4},{6,7},{7,6},{8,9},{9,8},{10,11... | collective-permute-start | bytes 835592 | tf_op jit(solution)/shard_map/ppermute | solution.py:383
  34.8 3.1 %collective-permute-done.9.y_got = bf16[1024,128]{1,0:T(8,128)(2,1)S(1)} collective-permute-done((bf16[1024,128]{1,0:T(8,128)(2,1)S(1)}, bf16[1024,128]{1,0:T(8,128)(2,1)S(1)}, u32[]{:S(2)}, u32[]{:S(2)}) %collective-permute-start.9) | collective-permute-done | bytes 262176 | tf_op jit(solution)/shard_map/ppermute | solution.py:383
  37.9 1.6 %collective-permute-done.11 = bf16[1024,128]{1,0:T(8,128)(2,1)S(1)} collective-permute-done((bf16[1024,128]{1,0:T(8,128)(2,1)S(1)}, bf16[1024,128]{1,0:T(8,128)(2,1)S(1)}, u32[]{:S(2)}, u32[]{:S(2)}) %collective-permute-start.11) | collective-permute-done | bytes 262176 | tf_op jit(solution)/shard_map/ppermute | solution.py:383
  39.6 1.3 %shard_map.129 = (bf16[2,128,512]{2,1,0:T(8,128)(2,1)}, bf16[2,4,128,128]{3,2,1,0:T(8,128)(2,1)S(1)}, bf16[128,128]{1,0:T(8,128)(2,1)S(1)}, bf16[128,128]{1,0:T(8,128)(2,1)S(1)}) custom-call(s32[11]{0:T(128)S(1)} %stack.62.bits, bf16[1024,128]{1,0:T(8,128)(2,1)S(1)} %get-tuple-element.56.own, bf16[1024,128]{1,0:T(8,128)(2,1)S(1)} %collective-permute-done.8.core_got, ...), custom_call_target="tpu_custom_call" | custom-call | tf_op jit(solution)/shard_map/pallas_call | solution.py:344
  40.9 1.5 %collective-permute-start.15 = (bf16[256,128]{1,0:T(8,128)(2,1)S(1)}, bf16[256,128]{1,0:T(8,128)(2,1)S(1)}, u32[]{:S(2)}, u32[]{:S(2)}) collective-permute-start(bf16[256,128]{1,0:T(8,128)(2,1)S(1)} %pad_maximum_fusion.7), channel_id=1, source_target_pairs={{0,1},{1,0},{2,3},{3,2},{4,5},{5,4},{6,7},{7,6},{8,9},{9,8},{10,11... | collective-permute-start | bytes 196616 | tf_op jit(solution)/shard_map/ppermute | solution.py:383
  42.5 1.5 %collective-permute-start.14 = (bf16[544,128]{1,0:T(8,128)(2,1)S(1)}, bf16[544,128]{1,0:T(8,128)(2,1)S(1)}, u32[]{:S(2)}, u32[]{:S(2)}) collective-permute-start(bf16[544,128]{1,0:T(8,128)(2,1)S(1)} %get-tuple-element.94), channel_id=1, source_target_pairs={{0,16},{1,17},{2,18},{3,19},{4,20},{5,21},{6,22},{7,23},{8,24},{9,... | collective-permute-start | bytes 417800 | tf_op jit(solution)/shard_map/ppermute | solution.py:383
  44.1 0.6 collective-permute-start.22
  44.7 0.4 collective-permute-done.15.x_got
  45.1 0.7 collective-permute-start.16
  45.8 1.8 %collective-permute-done.14 = bf16[544,128]{1,0:T(8,128)(2,1)S(1)} collective-permute-done((bf16[544,128]{1,0:T(8,128)(2,1)S(1)}, bf16[544,128]{1,0:T(8,128)(2,1)S(1)}, u32[]{:S(2)}, u32[]{:S(2)}) %collective-permute-start.14) | collective-permute-done | bytes 139296 | tf_op jit(solution)/shard_map/ppermute | solution.py:383
  47.6 2.7 %collective-permute-start.17 = (bf16[400,128]{1,0:T(8,128)(2,1)S(1)}, bf16[400,128]{1,0:T(8,128)(2,1)S(1)}, u32[]{:S(2)}, u32[]{:S(2)}) collective-permute-start(bf16[400,128]{1,0:T(8,128)(2,1)S(1)} %pad_maximum_fusion.6), channel_id=1, source_target_pairs={{0,2},{1,3},{2,0},{3,1},{4,6},{5,7},{6,4},{7,5},{8,10},{9,11},{10,... | collective-permute-start | bytes 307208 | tf_op jit(solution)/shard_map/ppermute | solution.py:383
  50.4 1.6 %collective-permute-start.23 = (bf16[256,128]{1,0:T(8,128)(2,1)S(1)}, bf16[256,128]{1,0:T(8,128)(2,1)S(1)}, u32[]{:S(2)}, u32[]{:S(2)}) collective-permute-start(bf16[256,128]{1,0:T(8,128)(2,1)S(1)} %get-tuple-element.100), channel_id=1, source_target_pairs={{0,4},{1,5},{2,6},{3,7},{4,0},{5,1},{6,2},{7,3},{8,12},{9,13},{10,... | collective-permute-start | bytes 196616 | tf_op jit(solution)/shard_map/ppermute | solution.py:383
  52.0 2.3 %collective-permute-done.17 = bf16[400,128]{1,0:T(8,128)(2,1)S(1)} collective-permute-done((bf16[400,128]{1,0:T(8,128)(2,1)S(1)}, bf16[400,128]{1,0:T(8,128)(2,1)S(1)}, u32[]{:S(2)}, u32[]{:S(2)}) %collective-permute-start.17) | collective-permute-done | bytes 102432 | tf_op jit(solution)/shard_map/ppermute | solution.py:383
  54.3 0.7 collective-permute-start.18
  55.0 1.6 %collective-permute-done.23 = bf16[256,128]{1,0:T(8,128)(2,1)S(1)} collective-permute-done((bf16[256,128]{1,0:T(8,128)(2,1)S(1)}, bf16[256,128]{1,0:T(8,128)(2,1)S(1)}, u32[]{:S(2)}, u32[]{:S(2)}) %collective-permute-start.23) | collective-permute-done | bytes 65568 | tf_op jit(solution)/shard_map/ppermute | solution.py:383
  56.6 2.1 %collective-permute-start.24 = (bf16[256,128]{1,0:T(8,128)(2,1)S(1)}, bf16[256,128]{1,0:T(8,128)(2,1)S(1)}, u32[]{:S(2)}, u32[]{:S(2)}) collective-permute-start(bf16[256,128]{1,0:T(8,128)(2,1)S(1)} %add_convert_fusion.13), channel_id=1, source_target_pairs={{0,16},{1,17},{2,18},{3,19},{4,20},{5,21},{6,22},{7,23},{8,24},{9,... | collective-permute-start | bytes 196616 | tf_op jit(solution)/shard_map/ppermute | solution.py:383
  58.7 0.9 %collective-permute-done.18 = bf16[272,128]{1,0:T(8,128)(2,1)S(1)} collective-permute-done((bf16[272,128]{1,0:T(8,128)(2,1)S(1)}, bf16[272,128]{1,0:T(8,128)(2,1)S(1)}, u32[]{:S(2)}, u32[]{:S(2)}) %collective-permute-start.18) | collective-permute-done | bytes 69664 | tf_op jit(solution)/shard_map/ppermute | solution.py:383
  59.6 1.6 %collective-permute-start.19 = (bf16[272,128]{1,0:T(8,128)(2,1)S(1)}, bf16[272,128]{1,0:T(8,128)(2,1)S(1)}, u32[]{:S(2)}, u32[]{:S(2)}) collective-permute-start(bf16[272,128]{1,0:T(8,128)(2,1)S(1)} %add_convert_fusion.8), channel_id=1, source_target_pairs={{0,2},{1,3},{2,0},{3,1},{4,6},{5,7},{6,4},{7,5},{8,10},{9,11},{10,... | collective-permute-start | bytes 208904 | tf_op jit(solution)/shard_map/ppermute | solution.py:383
  61.2 1.4 %collective-permute-start.25 = (bf16[256,128]{1,0:T(8,128)(2,1)S(1)}, bf16[256,128]{1,0:T(8,128)(2,1)S(1)}, u32[]{:S(2)}, u32[]{:S(2)}) collective-permute-start(bf16[256,128]{1,0:T(8,128)(2,1)S(1)} %add_convert_fusion.12), channel_id=1, source_target_pairs={{0,4},{1,5},{2,6},{3,7},{4,0},{5,1},{6,2},{7,3},{8,12},{9,13},{10,... | collective-permute-start | bytes 196616 | tf_op jit(solution)/shard_map/ppermute | solution.py:383
  62.6 1.3 %collective-permute-done.19 = bf16[272,128]{1,0:T(8,128)(2,1)S(1)} collective-permute-done((bf16[272,128]{1,0:T(8,128)(2,1)S(1)}, bf16[272,128]{1,0:T(8,128)(2,1)S(1)}, u32[]{:S(2)}, u32[]{:S(2)}) %collective-permute-start.19) | collective-permute-done | bytes 69664 | tf_op jit(solution)/shard_map/ppermute | solution.py:383
  64.0 3.5 %collective-permute-start.20 = (bf16[544,128]{1,0:T(8,128)(2,1)S(1)}, bf16[544,128]{1,0:T(8,128)(2,1)S(1)}, u32[]{:S(2)}, u32[]{:S(2)}) collective-permute-start(bf16[544,128]{1,0:T(8,128)(2,1)S(1)} %pad_maximum_fusion.4), channel_id=1, source_target_pairs={{0,16},{1,17},{2,18},{3,19},{4,20},{5,21},{6,22},{7,23},{8,24},{9,... | collective-permute-start | bytes 417800 | tf_op jit(solution)/shard_map/ppermute | solution.py:383
  67.5 1.6 %collective-permute-start.26 = (bf16[512,128]{1,0:T(8,128)(2,1)S(1)}, bf16[512,128]{1,0:T(8,128)(2,1)S(1)}, u32[]{:S(2)}, u32[]{:S(2)}) collective-permute-start(bf16[512,128]{1,0:T(8,128)(2,1)S(1)} %pad_maximum_fusion.5), channel_id=1, source_target_pairs={{0,1},{1,0},{2,3},{3,2},{4,5},{5,4},{6,7},{7,6},{8,9},{9,8},{10,11... | collective-permute-start | bytes 393224 | tf_op jit(solution)/shard_map/ppermute | solution.py:383
  69.1 1.4 %collective-permute-done.20 = bf16[544,128]{1,0:T(8,128)(2,1)S(1)} collective-permute-done((bf16[544,128]{1,0:T(8,128)(2,1)S(1)}, bf16[544,128]{1,0:T(8,128)(2,1)S(1)}, u32[]{:S(2)}, u32[]{:S(2)}) %collective-permute-start.20) | collective-permute-done | bytes 139296 | tf_op jit(solution)/shard_map/ppermute | solution.py:383
  70.9 1.6 %collective-permute-done.26 = bf16[512,128]{1,0:T(8,128)(2,1)S(1)} collective-permute-done((bf16[512,128]{1,0:T(8,128)(2,1)S(1)}, bf16[512,128]{1,0:T(8,128)(2,1)S(1)}, u32[]{:S(2)}, u32[]{:S(2)}) %collective-permute-start.26) | collective-permute-done | bytes 131104 | tf_op jit(solution)/shard_map/ppermute | solution.py:383
  72.6 0.6 collective-permute-start.27
  73.2 2.8 %shard_map.130 = bf16[2,128,512]{2,1,0:T(8,128)(2,1)} custom-call(s32[11]{0:T(128)S(1)} %stack.62.bits, bf16[2,4,128,128]{3,2,1,0:T(8,128)(2,1)S(1)} %get-tuple-element.68.dconv, bf16[256,128]{1,0:T(8,128)(2,1)S(1)} %collective-permute-done.15.x_got, bf16[128,128]{1,0:T(8,128)(2,1)S(1)} %slice.134.z_got, ...), custom_call_target="tpu_custom_call" | custom-call | tf_op jit(solution)/shard_map/pallas_call | solution.py:344
  76.1 2.0 %shard_map.131 = (f32[512,512]{1,0:T(8,128)}, f32[512,512]{1,0:T(8,128)}, f32[512,512]{1,0:T(8,128)}, f32[512,512]{1,0:T(8,128)}) custom-call(s32[11]{0:T(128)S(1)} %stack.62.bits, bf16[1088,128]{1,0:T(8,128)(2,1)S(1)} %pad_maximum_fusion.1.refs_0_.refs_2_, bf16[1024,128]{1,0:T(8,128)(2,1)S(1)} %pad_maximum_fusion.3.refs_1_, ...), custom_call_target="tpu_custom_call" | custom-call | tf_op jit(solution)/shard_map/pallas_call | solution.py:344
  78.1 3.3 %collective-permute-done.27.refs_1_ = bf16[1024,128]{1,0:T(8,128)(2,1)S(1)} collective-permute-done((bf16[1024,128]{1,0:T(8,128)(2,1)S(1)}, bf16[1024,128]{1,0:T(8,128)(2,1)S(1)}, u32[]{:S(2)}, u32[]{:S(2)}) %collective-permute-start.27) | collective-permute-done | bytes 262176 | tf_op jit(solution)/shard_map/ppermute | solution.py:383
  81.3 0.5 collective-permute-start.31
  81.8 1.6 %shard_map.132 = (f32[512,512]{1,0:T(8,128)}, f32[512,512]{1,0:T(8,128)}, f32[512,512]{1,0:T(8,128)}, f32[512,512]{1,0:T(8,128)}) custom-call(s32[11]{0:T(128)S(1)} %stack.62.bits, bf16[1088,128]{1,0:T(8,128)(2,1)S(1)} %collective-permute-done.21.refs_0_.refs_3_, ...), custom_call_target="tpu_custom_call", output_to_operand_aliasing={{0}: (3, {}), {1}: (4, {}), {2}: (5, {}), {3}: (6, {})} | custom-call | tf_op jit(solution)/shard_map/pallas_call | solution.py:344
  83.5 2.2 %shard_map.133 = (f32[512,512]{1,0:T(8,128)}, f32[512,512]{1,0:T(8,128)}, f32[512,512]{1,0:T(8,128)}, f32[512,512]{1,0:T(8,128)}, f32[31,512]{1,0:T(8,128)}) custom-call(s32[11]{0:T(128)S(1)} %stack.62.bits, bf16[1088,128]{1,0:T(8,128)(2,1)S(1)} %collective-permute-done.30.refs_0_.refs_5_, ...), custom_call_target="tpu_custom_call", output_to_operand_aliasing={{0}: (7, {}), {1}: (8, {}), {2}: (9, {}), {3}: (10, {})} | custom-call | tf_op jit(solution)/shard_map/pallas_call | solution.py:344
  (53 shorter events, 2.2 us)
Async XLA Ops:
  1.7 5.2 %collective-permute-start = (bf16[2,32,512]{2,1,0:T(8,128)(2,1)S(1)}, bf16[2,32,512]{2,1,0:T(8,128)(2,1)S(1)}, u32[]{:S(2)}, u32[]{:S(2)}) collective-permute-start(bf16[2,32,512]{2,1,0:T(8,128)(2,1)S(1)} %get-tuple-element.106), channel_id=1, source_target_pairs={{0,8},{1,9},{2,10},{3,11},{4,12},{5,13},{6,14},{7,15},{8,0},{9,1},... | collective-permute-start | bytes 196616 | tf_op jit(solution)/shard_map/ppermute | solution.py:383
  2.2 5.3 %collective-permute-start.1 = (bf16[2,32,512]{2,1,0:T(8,128)(2,1)S(1)}, bf16[2,32,512]{2,1,0:T(8,128)(2,1)S(1)}, u32[]{:S(2)}, u32[]{:S(2)}) collective-permute-start(bf16[2,32,512]{2,1,0:T(8,128)(2,1)S(1)} %get-tuple-element.108), channel_id=1, source_target_pairs={{0,16},{1,17},{2,18},{3,19},{4,20},{5,21},{6,22},{7,23},{8,24},{9,... | collective-permute-start | bytes 196616 | tf_op jit(solution)/shard_map/ppermute | solution.py:383
  4.8 4.0 %collective-permute-start.2 = (bf16[2,32,512]{2,1,0:T(8,128)(2,1)S(1)}, bf16[2,32,512]{2,1,0:T(8,128)(2,1)S(1)}, u32[]{:S(2)}, u32[]{:S(2)}) collective-permute-start(bf16[2,32,512]{2,1,0:T(8,128)(2,1)S(1)} %get-tuple-element.105), channel_id=1, source_target_pairs={{0,24},{1,25},{2,26},{3,27},{4,28},{5,29},{6,30},{7,31},{8,16},{9,... | collective-permute-start | bytes 196616 | tf_op jit(solution)/shard_map/ppermute | solution.py:383
  4.8 5.4 %copy-start = (bf16[2,128,512]{2,1,0:T(8,128)(2,1)S(1)}, bf16[2,128,512]{2,1,0:T(8,128)(2,1)}, u32[]{:S(2)}) copy-start(bf16[2,128,512]{2,1,0:T(8,128)(2,1)} %cot.1) | copy-start | bytes 786436
  4.8 9.9 %copy-start.1 = (f32[31,512]{1,0:T(8,128)S(1)}, f32[31,512]{1,0:T(8,128)}, u32[]{:S(2)}) copy-start(f32[31,512]{1,0:T(8,128)} %kern.3) | copy-start | bytes 190468
  9.4 5.3 %collective-permute-start.3 = (bf16[4,2,16,512]{3,2,1,0:T(8,128)(2,1)S(1)}, bf16[4,2,16,512]{3,2,1,0:T(8,128)(2,1)S(1)}, u32[]{:S(2)}, u32[]{:S(2)}) collective-permute-start(bf16[4,2,16,512]{3,2,1,0:T(8,128)(2,1)S(1)} %get-tuple-element.50), channel_id=1, source_target_pairs={{0,8},{1,9},{2,10},{3,11},{4,12},{5,13},{6,14},{7,15},{8,0},{9,1},... | collective-permute-start | bytes 393224 | tf_op jit(solution)/shard_map/ppermute | solution.py:383
  9.6 5.1 %collective-permute-start.4 = (bf16[4,2,16,512]{3,2,1,0:T(8,128)(2,1)S(1)}, bf16[4,2,16,512]{3,2,1,0:T(8,128)(2,1)S(1)}, u32[]{:S(2)}, u32[]{:S(2)}) collective-permute-start(bf16[4,2,16,512]{3,2,1,0:T(8,128)(2,1)S(1)} %get-tuple-element.51), channel_id=1, source_target_pairs={{8,24},{9,25},{10,26},{11,27},{12,28},{13,29},{14,30},{15,31},{24,... | collective-permute-start | bytes 393224 | tf_op jit(solution)/shard_map/ppermute | solution.py:383
  10.3 6.9 %collective-permute-start.5 = (bf16[2,32,512]{2,1,0:T(8,128)(2,1)S(1)}, bf16[2,32,512]{2,1,0:T(8,128)(2,1)S(1)}, u32[]{:S(2)}, u32[]{:S(2)}) collective-permute-start(bf16[2,32,512]{2,1,0:T(8,128)(2,1)S(1)} %get-tuple-element.103), channel_id=1, source_target_pairs={{0,8},{1,9},{2,10},{3,11},{4,12},{5,13},{6,14},{7,15},{8,0},{9,1},... | collective-permute-start | bytes 196616 | tf_op jit(solution)/shard_map/ppermute | solution.py:383
  13.0 4.3 %collective-permute-start.6 = (bf16[2,32,512]{2,1,0:T(8,128)(2,1)S(1)}, bf16[2,32,512]{2,1,0:T(8,128)(2,1)S(1)}, u32[]{:S(2)}, u32[]{:S(2)}) collective-permute-start(bf16[2,32,512]{2,1,0:T(8,128)(2,1)S(1)} %get-tuple-element.102), channel_id=1, source_target_pairs={{0,16},{1,17},{2,18},{3,19},{4,20},{5,21},{6,22},{7,23},{8,24},{9,... | collective-permute-start | bytes 196616 | tf_op jit(solution)/shard_map/ppermute | solution.py:383
  14.7 4.0 %collective-permute-start.7 = (bf16[2,32,512]{2,1,0:T(8,128)(2,1)S(1)}, bf16[2,32,512]{2,1,0:T(8,128)(2,1)S(1)}, u32[]{:S(2)}, u32[]{:S(2)}) collective-permute-start(bf16[2,32,512]{2,1,0:T(8,128)(2,1)S(1)} %get-tuple-element.101), channel_id=1, source_target_pairs={{0,24},{1,25},{2,26},{3,27},{4,28},{5,29},{6,30},{7,31},{8,16},{9,... | collective-permute-start | bytes 196616 | tf_op jit(solution)/shard_map/ppermute | solution.py:383
  27.1 4.2 %collective-permute-start.10 = (bf16[2048,128]{1,0:T(8,128)(2,1)S(1)}, bf16[2048,128]{1,0:T(8,128)(2,1)S(1)}, u32[]{:S(2)}, u32[]{:S(2)}) collective-permute-start(bf16[2048,128]{1,0:T(8,128)(2,1)S(1)} %get-tuple-element.59), channel_id=1, source_target_pairs={{0,8},{1,9},{2,10},{3,11},{4,12},{5,13},{6,14},{7,15},{8,0},{9,1},... | collective-permute-start | bytes 1572872 | tf_op jit(solution)/shard_map/ppermute | solution.py:383
  27.3 2.1 %collective-permute-start.8 = (bf16[1024,128]{1,0:T(8,128)(2,1)S(1)}, bf16[1024,128]{1,0:T(8,128)(2,1)S(1)}, u32[]{:S(2)}, u32[]{:S(2)}) collective-permute-start(bf16[1024,128]{1,0:T(8,128)(2,1)S(1)} %get-tuple-element.57), channel_id=1, source_target_pairs={{0,8},{1,9},{2,10},{3,11},{4,12},{5,13},{6,14},{7,15},{8,0},{9,1},... | collective-permute-start | bytes 786440 | tf_op jit(solution)/shard_map/ppermute | solution.py:383
  27.7 5.4 %collective-permute-start.12 = (bf16[2176,128]{1,0:T(8,128)(2,1)S(1)}, bf16[2176,128]{1,0:T(8,128)(2,1)S(1)}, u32[]{:S(2)}, u32[]{:S(2)}) collective-permute-start(bf16[2176,128]{1,0:T(8,128)(2,1)S(1)} %get-tuple-element.63), channel_id=1, source_target_pairs={{0,8},{1,9},{2,10},{3,11},{4,12},{5,13},{6,14},{7,15},{8,0},{9,1},... | collective-permute-start | bytes 1671176 | tf_op jit(solution)/shard_map/ppermute | solution.py:383
  29.5 8.4 %collective-permute-start.9 = (bf16[1024,128]{1,0:T(8,128)(2,1)S(1)}, bf16[1024,128]{1,0:T(8,128)(2,1)S(1)}, u32[]{:S(2)}, u32[]{:S(2)}) collective-permute-start(bf16[1024,128]{1,0:T(8,128)(2,1)S(1)} %pad_maximum_fusion.2), channel_id=1, source_target_pairs={{0,16},{1,17},{2,18},{3,19},{4,20},{5,21},{6,22},{7,23},{8,24},{9,... | collective-permute-start | bytes 786440 | tf_op jit(solution)/shard_map/ppermute | solution.py:383
  31.4 8.1 %collective-permute-start.11 = (bf16[1024,128]{1,0:T(8,128)(2,1)S(1)}, bf16[1024,128]{1,0:T(8,128)(2,1)S(1)}, u32[]{:S(2)}, u32[]{:S(2)}) collective-permute-start(bf16[1024,128]{1,0:T(8,128)(2,1)S(1)} %get-tuple-element.92), channel_id=1, source_target_pairs={{0,2},{1,3},{2,0},{3,1},{4,6},{5,7},{6,4},{7,5},{8,10},{9,11},{10,... | collective-permute-start | bytes 786440 | tf_op jit(solution)/shard_map/ppermute | solution.py:383
  33.2 9.1 %collective-permute-start.13 = (bf16[1088,128]{1,0:T(8,128)(2,1)S(1)}, bf16[1088,128]{1,0:T(8,128)(2,1)S(1)}, u32[]{:S(2)}, u32[]{:S(2)}) collective-permute-start(bf16[1088,128]{1,0:T(8,128)(2,1)S(1)} %get-tuple-element.90), channel_id=1, source_target_pairs={{0,1},{1,0},{2,3},{3,2},{4,5},{5,4},{6,7},{7,6},{8,9},{9,8},{10,11... | collective-permute-start | bytes 835592 | tf_op jit(solution)/shard_map/ppermute | solution.py:383
  40.9 4.3 %collective-permute-start.15 = (bf16[256,128]{1,0:T(8,128)(2,1)S(1)}, bf16[256,128]{1,0:T(8,128)(2,1)S(1)}, u32[]{:S(2)}, u32[]{:S(2)}) collective-permute-start(bf16[256,128]{1,0:T(8,128)(2,1)S(1)} %pad_maximum_fusion.7), channel_id=1, source_target_pairs={{0,1},{1,0},{2,3},{3,2},{4,5},{5,4},{6,7},{7,6},{8,9},{9,8},{10,11... | collective-permute-start | bytes 196616 | tf_op jit(solution)/shard_map/ppermute | solution.py:383
  42.5 5.1 %collective-permute-start.14 = (bf16[544,128]{1,0:T(8,128)(2,1)S(1)}, bf16[544,128]{1,0:T(8,128)(2,1)S(1)}, u32[]{:S(2)}, u32[]{:S(2)}) collective-permute-start(bf16[544,128]{1,0:T(8,128)(2,1)S(1)} %get-tuple-element.94), channel_id=1, source_target_pairs={{0,16},{1,17},{2,18},{3,19},{4,20},{5,21},{6,22},{7,23},{8,24},{9,... | collective-permute-start | bytes 417800 | tf_op jit(solution)/shard_map/ppermute | solution.py:383
  44.1 6.3 %collective-permute-start.22 = (bf16[512,128]{1,0:T(8,128)(2,1)S(1)}, bf16[512,128]{1,0:T(8,128)(2,1)S(1)}, u32[]{:S(2)}, u32[]{:S(2)}) collective-permute-start(bf16[512,128]{1,0:T(8,128)(2,1)S(1)} %get-tuple-element.96), channel_id=1, source_target_pairs={{0,1},{1,0},{2,3},{3,2},{4,5},{5,4},{6,7},{7,6},{8,9},{9,8},{10,11... | collective-permute-start | bytes 393224 | tf_op jit(solution)/shard_map/ppermute | solution.py:383
  45.1 6.9 %collective-permute-start.16 = (bf16[128,128]{1,0:T(8,128)(2,1)S(1)}, bf16[128,128]{1,0:T(8,128)(2,1)S(1)}, u32[]{:S(2)}, u32[]{:S(2)}) collective-permute-start(bf16[128,128]{1,0:T(8,128)(2,1)S(1)} %constant_dynamic-slice_fusion), channel_id=1, source_target_pairs={{2,4},{3,5},{10,12},{11,13},{18,20},{19,21},{26,28},{27,29},{4,2},... | collective-permute-start | bytes 98312 | tf_op jit(solution)/shard_map/ppermute | solution.py:383
  47.6 6.6 %collective-permute-start.17 = (bf16[400,128]{1,0:T(8,128)(2,1)S(1)}, bf16[400,128]{1,0:T(8,128)(2,1)S(1)}, u32[]{:S(2)}, u32[]{:S(2)}) collective-permute-start(bf16[400,128]{1,0:T(8,128)(2,1)S(1)} %pad_maximum_fusion.6), channel_id=1, source_target_pairs={{0,2},{1,3},{2,0},{3,1},{4,6},{5,7},{6,4},{7,5},{8,10},{9,11},{10,... | collective-permute-start | bytes 307208 | tf_op jit(solution)/shard_map/ppermute | solution.py:383
  50.4 6.2 %collective-permute-start.23 = (bf16[256,128]{1,0:T(8,128)(2,1)S(1)}, bf16[256,128]{1,0:T(8,128)(2,1)S(1)}, u32[]{:S(2)}, u32[]{:S(2)}) collective-permute-start(bf16[256,128]{1,0:T(8,128)(2,1)S(1)} %get-tuple-element.100), channel_id=1, source_target_pairs={{0,4},{1,5},{2,6},{3,7},{4,0},{5,1},{6,2},{7,3},{8,12},{9,13},{10,... | collective-permute-start | bytes 196616 | tf_op jit(solution)/shard_map/ppermute | solution.py:383
  54.3 5.3 %collective-permute-start.18 = (bf16[272,128]{1,0:T(8,128)(2,1)S(1)}, bf16[272,128]{1,0:T(8,128)(2,1)S(1)}, u32[]{:S(2)}, u32[]{:S(2)}) collective-permute-start(bf16[272,128]{1,0:T(8,128)(2,1)S(1)} %add_convert_fusion.9), channel_id=1, source_target_pairs={{0,4},{1,5},{2,6},{3,7},{4,0},{5,1},{6,2},{7,3},{8,12},{9,13},{10,... | collective-permute-start | bytes 208904 | tf_op jit(solution)/shard_map/ppermute | solution.py:383
  56.6 4.6 %collective-permute-start.24 = (bf16[256,128]{1,0:T(8,128)(2,1)S(1)}, bf16[256,128]{1,0:T(8,128)(2,1)S(1)}, u32[]{:S(2)}, u32[]{:S(2)}) collective-permute-start(bf16[256,128]{1,0:T(8,128)(2,1)S(1)} %add_convert_fusion.13), channel_id=1, source_target_pairs={{0,16},{1,17},{2,18},{3,19},{4,20},{5,21},{6,22},{7,23},{8,24},{9,... | collective-permute-start | bytes 196616 | tf_op jit(solution)/shard_map/ppermute | solution.py:383
  59.6 4.4 %collective-permute-start.19 = (bf16[272,128]{1,0:T(8,128)(2,1)S(1)}, bf16[272,128]{1,0:T(8,128)(2,1)S(1)}, u32[]{:S(2)}, u32[]{:S(2)}) collective-permute-start(bf16[272,128]{1,0:T(8,128)(2,1)S(1)} %add_convert_fusion.8), channel_id=1, source_target_pairs={{0,2},{1,3},{2,0},{3,1},{4,6},{5,7},{6,4},{7,5},{8,10},{9,11},{10,... | collective-permute-start | bytes 208904 | tf_op jit(solution)/shard_map/ppermute | solution.py:383
  61.2 6.2 %collective-permute-start.25 = (bf16[256,128]{1,0:T(8,128)(2,1)S(1)}, bf16[256,128]{1,0:T(8,128)(2,1)S(1)}, u32[]{:S(2)}, u32[]{:S(2)}) collective-permute-start(bf16[256,128]{1,0:T(8,128)(2,1)S(1)} %add_convert_fusion.12), channel_id=1, source_target_pairs={{0,4},{1,5},{2,6},{3,7},{4,0},{5,1},{6,2},{7,3},{8,12},{9,13},{10,... | collective-permute-start | bytes 196616 | tf_op jit(solution)/shard_map/ppermute | solution.py:383
  64.0 6.5 %collective-permute-start.20 = (bf16[544,128]{1,0:T(8,128)(2,1)S(1)}, bf16[544,128]{1,0:T(8,128)(2,1)S(1)}, u32[]{:S(2)}, u32[]{:S(2)}) collective-permute-start(bf16[544,128]{1,0:T(8,128)(2,1)S(1)} %pad_maximum_fusion.4), channel_id=1, source_target_pairs={{0,16},{1,17},{2,18},{3,19},{4,20},{5,21},{6,22},{7,23},{8,24},{9,... | collective-permute-start | bytes 417800 | tf_op jit(solution)/shard_map/ppermute | solution.py:383
  67.5 5.0 %collective-permute-start.26 = (bf16[512,128]{1,0:T(8,128)(2,1)S(1)}, bf16[512,128]{1,0:T(8,128)(2,1)S(1)}, u32[]{:S(2)}, u32[]{:S(2)}) collective-permute-start(bf16[512,128]{1,0:T(8,128)(2,1)S(1)} %pad_maximum_fusion.5), channel_id=1, source_target_pairs={{0,1},{1,0},{2,3},{3,2},{4,5},{5,4},{6,7},{7,6},{8,9},{9,8},{10,11... | collective-permute-start | bytes 393224 | tf_op jit(solution)/shard_map/ppermute | solution.py:383
  70.5 5.5 %collective-permute-start.28 = (bf16[1088,128]{1,0:T(8,128)(2,1)S(1)}, bf16[1088,128]{1,0:T(8,128)(2,1)S(1)}, u32[]{:S(2)}, u32[]{:S(2)}) collective-permute-start(bf16[1088,128]{1,0:T(8,128)(2,1)S(1)} %pad_maximum_fusion.1.refs_0_.refs_2_), channel_id=1, source_target_pairs={{0,8},{1,9},{2,10},{3,11},{4,12},{5,13},{6,14},{7,15},{8,0},{9,1},... | collective-permute-start | bytes 835592 | tf_op jit(solution)/shard_map/ppermute | solution.py:383
  70.6 10.7 %collective-permute-start.21 = (bf16[1088,128]{1,0:T(8,128)(2,1)S(1)}, bf16[1088,128]{1,0:T(8,128)(2,1)S(1)}, u32[]{:S(2)}, u32[]{:S(2)}) collective-permute-start(bf16[1088,128]{1,0:T(8,128)(2,1)S(1)} %pad_maximum_fusion.1.refs_0_.refs_2_), channel_id=1, source_target_pairs={{0,1},{1,0},{2,3},{3,2},{4,5},{5,4},{6,7},{7,6},{8,9},{9,8},{10,11... | collective-permute-start | bytes 835592 | tf_op jit(solution)/shard_map/ppermute | solution.py:383
  72.5 3.5 %collective-permute-start.29 = (bf16[1024,128]{1,0:T(8,128)(2,1)S(1)}, bf16[1024,128]{1,0:T(8,128)(2,1)S(1)}, u32[]{:S(2)}, u32[]{:S(2)}) collective-permute-start(bf16[1024,128]{1,0:T(8,128)(2,1)S(1)} %pad_maximum_fusion.3.refs_1_), channel_id=1, source_target_pairs={{0,8},{1,9},{2,10},{3,11},{4,12},{5,13},{6,14},{7,15},{8,0},{9,1},... | collective-permute-start | bytes 786440 | tf_op jit(solution)/shard_map/ppermute | solution.py:383
  72.6 8.7 %collective-permute-start.27 = (bf16[1024,128]{1,0:T(8,128)(2,1)S(1)}, bf16[1024,128]{1,0:T(8,128)(2,1)S(1)}, u32[]{:S(2)}, u32[]{:S(2)}) collective-permute-start(bf16[1024,128]{1,0:T(8,128)(2,1)S(1)} %pad_maximum_fusion.3.refs_1_), channel_id=1, source_target_pairs={{0,2},{1,3},{2,0},{3,1},{4,6},{5,7},{6,4},{7,5},{8,10},{9,11},{10,... | collective-permute-start | bytes 786440 | tf_op jit(solution)/shard_map/ppermute | solution.py:383
  81.3 2.1 %collective-permute-start.30 = (bf16[1088,128]{1,0:T(8,128)(2,1)S(1)}, bf16[1088,128]{1,0:T(8,128)(2,1)S(1)}, u32[]{:S(2)}, u32[]{:S(2)}) collective-permute-start(bf16[1088,128]{1,0:T(8,128)(2,1)S(1)} %collective-permute-done.21.refs_0_.refs_3_), channel_id=1, source_target_pairs={{0,8},{1,9},{2,10},{3,11},{4,12},{5,13},{6,14},{7,15},{8,0},{9,1},... | collective-permute-start | bytes 835592 | tf_op jit(solution)/shard_map/ppermute | solution.py:383
  81.3 2.1 %collective-permute-start.31 = (bf16[1024,128]{1,0:T(8,128)(2,1)S(1)}, bf16[1024,128]{1,0:T(8,128)(2,1)S(1)}, u32[]{:S(2)}, u32[]{:S(2)}) collective-permute-start(bf16[1024,128]{1,0:T(8,128)(2,1)S(1)} %collective-permute-done.27.refs_1_), channel_id=1, source_target_pairs={{0,8},{1,9},{2,10},{3,11},{4,12},{5,13},{6,14},{7,15},{8,0},{9,1},... | collective-permute-start | bytes 786440 | tf_op jit(solution)/shard_map/ppermute | solution.py:383
